TPU v7x, 32 devices: a whole 2x2x4 slice. The times are simulated.
32 devices in a mesh: gx: 8 (over y, x, core), gy: 4 (over z).
Axes of the slice: x: 2, y: 2, z: 4, core: 2. Of those that a mesh axis runs over, the one named last changes fastest.
Arguments:
- fields: float32 [3, 16, 256, 512], P(None, None, 'gx', 'gy'), may hold values from -5 to 5
- levels: int32 [8], replicated, may hold values from 0 to 15, as said below
- cuts: int32 [3, 8], replicated, may hold values from 8 to 32
- parent_modes: float32 [32, 2, 24, 4096], P(('gx', 'gy')), may hold values from -24 to 24
- owners: int32 [2], replicated, may hold values from 0 to 31
- plume: float32 [16, 256, 512], P(None, 'gx', 'gy'), may hold values from 0 to 2
- source: float32 [16, 256, 512], P(None, 'gx', 'gy'), may hold values from 0 to 1
Outputs:
- fields_out: float32 [3, 16, 256, 512], P(None, None, 'gx', 'gy')
- plume_out: float32 [16, 256, 512], P(None, 'gx', 'gy')
Inputs may be any that keep to these rules, and one draw needn't show every extreme that they name: 8 distinct level indices; the first and last model levels are always among them.
All inputs are finite; a program needn't handle non-finite values.
Results may differ from a plain program's by a relative error of at most 0.0001.
Values sent between devices are 32-bit elements; how exact they have to be, the bound alone decides.
No kernel may reach another device: no remote copies, remote signals or barrier semaphores. Data moves between devices by JAX's collectives and lax.ppermute only.
A program may use at most 64 MiB of HBM per device.

v0:
```python
import math

import jax
import jax.numpy as jnp
from jax import lax
from jax.sharding import PartitionSpec as P

KX = 32
STEPS = 2


def broadcast(value, axis, source):
    kept = jnp.where(lax.axis_index(axis) == source, value, 0).astype(value.dtype)
    return lax.psum(kept, axis)


def with_halo(block, sides, width):
    for axis, dim in sides:
        count = lax.axis_size(axis)
        forward = [(i, i + 1) for i in range(count - 1)]
        backward = [(target, source) for source, target in forward]
        low = lax.ppermute(
            lax.slice_in_dim(block, block.shape[dim] - width, None, axis=dim), axis, forward
        )
        high = lax.ppermute(lax.slice_in_dim(block, 0, width, axis=dim), axis, backward)
        block = jnp.concatenate([low, block, high], axis=dim)
    return block


def tables(length_cells, first_cell, period):
    wavenum = jnp.arange(KX, dtype=jnp.int32)[:, None]
    position = first_cell + jnp.arange(length_cells, dtype=jnp.int32)[None, :]
    phase = (wavenum * position % period).astype(jnp.float32) * (2.0 * math.pi / period)
    return jnp.concatenate([jnp.cos(phase), jnp.sin(phase)], axis=0)


def spectral_weights(cuts, period_x, period_y):
    rows = jnp.arange(2 * KX, dtype=jnp.int32)
    wavenum = rows % KX
    factor = jnp.where(rows == 0, 1.0, 2.0).astype(jnp.float32)
    weighting = factor[:, None] * factor[None, :] / math.sqrt(period_x * period_y)
    limit = cuts.reshape(-1)[:, None, None]
    keep_mask = ((wavenum[None, :, None] < limit) & (wavenum[None, None, :] < limit)).astype(
        jnp.float32
    )
    return keep_mask * weighting[None]


def transport(values, padded, east_wind, north_wind):
    per_group = east_wind.shape[0]
    groups = values.shape[0] // per_group

    def split(array):
        return array.reshape((groups, per_group) + array.shape[1:])

    centre = split(values)
    west_side = split(padded[:, :-2, 1:-1])
    east_side = split(padded[:, 2:, 1:-1])
    south_side = split(padded[:, 1:-1, :-2])
    north_side = split(padded[:, 1:-1, 2:])
    upwind = (
        jnp.maximum(east_wind, 0.0) * (centre - west_side)
        + jnp.minimum(east_wind, 0.0) * (east_side - centre)
        + jnp.maximum(north_wind, 0.0) * (centre - south_side)
        + jnp.minimum(north_wind, 0.0) * (north_side - centre)
    )
    laplace = east_side + west_side + north_side + south_side - 4.0 * centre
    return (0.1 * laplace - 0.1 * upwind).reshape(values.shape)


def settle(concentration, moved, source):
    above = jnp.concatenate([concentration[1:], jnp.zeros_like(concentration[:1])], axis=0)
    return concentration + moved - 0.3 * concentration + 0.3 * above + source


def reduce_modes(partial_terms):
    return lax.psum(partial_terms, ("gx", "gy"))


def local(fields, levels, cuts, parent_modes, owners, plume, source):
    hi = lax.Precision.HIGHEST
    level_total = fields.shape[1]
    cells_x = fields.shape[2]
    cells_y = fields.shape[3]
    period_x = cells_x * lax.axis_size("gx")
    period_y = cells_y * lax.axis_size("gy")
    x_table = tables(cells_x, lax.axis_index("gx") * cells_x, period_x)
    y_table = tables(cells_y, lax.axis_index("gy") * cells_y, period_y)
    scaling = 1.0 / math.sqrt(period_x * period_y)
    weighted = spectral_weights(cuts, period_x, period_y)
    level_count = levels.shape[0]
    nudged = 3 * level_count
    field_rows = 3 * level_total
    for step_index in range(STEPS):
        chosen = jnp.take(fields, levels, axis=1).reshape(nudged, cells_x, cells_y)
        halfway = jnp.einsum("kx,cxy->cky", x_table, chosen, precision=hi)
        partial_modes = (
            jnp.einsum("cky,jy->ckj", halfway, y_table, precision=hi) * scaling
        ).reshape(nudged, -1)
        parent_here = parent_modes[0, step_index]
        parent = broadcast(parent_here, ("gx", "gy"), owners[step_index])
        difference = parent - reduce_modes(partial_modes)
        mismatch = difference.reshape(nudged, 2 * KX, 2 * KX) * weighted
        back = jnp.einsum("ckj,jy->cky", mismatch, y_table, precision=hi)
        update = jnp.einsum("kx,cky->cxy", x_table, back, precision=hi)
        fields = fields.at[:, levels].add(update.reshape(3, level_count, cells_x, cells_y))
        east_wind = fields[0]
        north_wind = fields[1]
        state = jnp.concatenate([fields.reshape(field_rows, cells_x, cells_y), plume], axis=0)
        padded = with_halo(state, (("gx", 1), ("gy", 2)), 1)
        moved = transport(state, padded, east_wind, north_wind)
        plume = settle(plume, moved[field_rows:], source)
        fields = (state[:field_rows] + moved[:field_rows]).reshape(3, level_total, cells_x, cells_y)
    return (fields, plume)


def solution(mesh):
    in_specs = (
        P(None, None, "gx", "gy"),
        P(),
        P(),
        P(("gx", "gy"), None, None, None),
        P(),
        P(None, "gx", "gy"),
        P(None, "gx", "gy"),
    )
    out_specs = (P(None, None, "gx", "gy"), P(None, "gx", "gy"))
    return jax.shard_map(local, mesh=mesh, in_specs=in_specs, out_specs=out_specs, check_vma=False)
```

profile of v0, /device:TPU:0, one launch (start us, length us, event | category | flops | bytes accessed | tf_op | source)
XLA Modules:
  0.0 390.0 jit_solution(10901568139343369147)
XLA Ops:
  17.2 131.4 %all-reduce.9.cloned.1.call-done = (f32[24,4096]{1,0:T(8,128)}, f32[24,4096]{1,0:T(8,128)}) async-done(((f32[24,4096]{1,0:T(8,128)}, f32[24,4096]{1,0:T(8,128)}), (f32[24,4096]{1,0:T(8,128)}, f32[24,4096]{1,0:T(8,128)})) %all-reduce.9.cloned.1.call-update) | async-done | bytes 786448 | tf_op jit(solution)/shard_map/psum | solution.py:14
  149.8 1.2 reshape.218
  151.0 2.0 fusion
  153.6 1.3 scatter_fusion
  154.8 2.0 copy.20
  158.0 1.3 collective-permute-start
  159.3 3.0 collective-permute-start.1
  163.4 1.3 collective-permute-start.2
  164.7 4.7 %collective-permute-start.3 = (f32[64,34,1]{0,2,1:T(1,128)S(1)}, f32[64,34,1]{0,2,1:T(1,128)S(1)}, u32[]{:S(2)}, u32[]{:S(2)}) collective-permute-start(f32[64,34,1]{0,2,1:T(1,128)S(1)} %get-tuple-element.13), channel_id=1, source_target_pairs={{0,1},{1,2},{2,3},{4,5},{5,6},{6,7},{8,9},{9,10},{10,11},{12,13},{... | collective-permute-start | bytes 26120 | tf_op jit(solution)/shard_map/ppermute | solution.py:22
  170.7 8.5 %pad_maximum_fusion.12 = (f32[64,32,128]{0,2,1:T(8,128)}, f32[64,32,128]{0,2,1:T(8,128)}, f32[64,32,128]{0,2,1:T(8,128)}, f32[64,32,128]{0,2,1:T(8,128)}, f32[64,32,128]{0,2,1:T(8,128)}) fusion(f32[64,34,1]{0,2,1:T(1,128)S(1)} %collective-permute-done.3, f32[64,1,128]{0,2,1:T(8,128)S(1)} %collective-permute-done, ...), kind=kLoop, calls=%fused_computation.16 | loop fusion | flops 3407872 | bytes 6374400 | tf_op jit(solution)/shard_map/concatenate | solution.py:26
  179.2 3.3 copy.22
  182.5 3.5 copy.23
  186.0 1.8 copy.24
  187.8 3.5 copy.25
  191.4 1.8 copy.26
  193.2 3.4 multiply_subtract_fusion.1
  200.9 131.8 %all-reduce.7.cloned.1.call-done = (f32[24,4096]{1,0:T(8,128)}, f32[24,4096]{1,0:T(8,128)}) async-done(((f32[24,4096]{1,0:T(8,128)}, f32[24,4096]{1,0:T(8,128)}), (f32[24,4096]{1,0:T(8,128)}, f32[24,4096]{1,0:T(8,128)})) %all-reduce.7.cloned.1.call-update) | async-done | bytes 786448 | tf_op jit(solution)/shard_map/psum | solution.py:14
  333.9 1.2 reshape.228
  335.1 2.1 fusion.1
  337.8 1.5 scatter_fusion.1
  339.3 2.0 copy.29
  342.4 1.3 collective-permute-start.4
  343.7 3.0 collective-permute-start.5
  347.8 1.3 collective-permute-start.6
  349.1 4.5 %collective-permute-start.7 = (f32[64,34,1]{0,2,1:T(1,128)S(1)}, f32[64,34,1]{0,2,1:T(1,128)S(1)}, u32[]{:S(2)}, u32[]{:S(2)}) collective-permute-start(f32[64,34,1]{0,2,1:T(1,128)S(1)} %get-tuple-element.9), channel_id=1, source_target_pairs={{0,1},{1,2},{2,3},{4,5},{5,6},{6,7},{8,9},{9,10},{10,11},{12,13},{... | collective-permute-start | bytes 26120 | tf_op jit(solution)/shard_map/ppermute | solution.py:22
  355.1 8.5 %pad_maximum_fusion = (f32[64,32,128]{0,2,1:T(8,128)}, f32[64,32,128]{0,2,1:T(8,128)}, f32[64,32,128]{0,2,1:T(8,128)}, f32[64,32,128]{0,2,1:T(8,128)}, f32[64,32,128]{0,2,1:T(8,128)}) fusion(f32[64,34,1]{0,2,1:T(1,128)S(1)} %collective-permute-done.7, f32[64,1,128]{0,2,1:T(8,128)S(1)} %collective-permute-done.4, f32[64,1,128]{0,2,1:T(8,128)S(1)} %collective-permute-done.5, ...), kind=kLoop, calls=%fused_computation.4 | loop fusion | flops 3407872 | bytes 6374400 | tf_op jit(solution)/shard_map/concatenate | solution.py:26
  363.6 3.3 copy.31
  366.9 3.5 copy.32
  370.5 1.8 copy.33
  372.3 3.5 copy.34
  375.8 1.8 copy.35
  377.6 3.4 multiply_subtract_fusion
  (96 shorter events, 25.4 us)
Async XLA Ops:
  7.2 141.5 %all-reduce.9.cloned.1.call-start = ((), (), s32[]{:S(2)}) async-start(), calls=%async_computation.1 | async-start | bytes 1572864 | tf_op jit(solution)/shard_map/psum | solution.py:14
  10.6 2.9 copy-start.16
  10.6 4.7 %copy-start.14 = (f32[1,2,24,4096]{3,2,1,0:T(8,128)S(1)}, f32[1,2,24,4096]{3,2,1,0:T(8,128)}, u32[]{:S(2)}) copy-start(f32[1,2,24,4096]{3,2,1,0:T(8,128)} %param.12) | copy-start | bytes 2359300
  12.4 4.0 %copy-start.15 = (s32[3,8]{1,0:T(4,128)S(1)}, s32[3,8]{1,0:T(4,128)}, u32[]{:S(2)}) copy-start(s32[3,8]{1,0:T(4,128)} %param.11) | copy-start | bytes 292
  12.4 4.1 %copy-start.10 = (f32[16,32,128]{2,1,0:T(8,128)S(1)}, f32[16,32,128]{2,1,0:T(8,128)}, u32[]{:S(2)}) copy-start(f32[16,32,128]{2,1,0:T(8,128)} %param.14) | copy-start | bytes 786436
  16.3 316.5 %all-reduce.7.cloned.1.call-start = ((), (), s32[]{:S(2)}) async-start(), calls=%async_computation | async-start | bytes 1572864 | tf_op jit(solution)/shard_map/psum | solution.py:14
  156.9 6.4 %copy-start.1 = (f32[48,32,128]{0,2,1:T(8,128)S(1)}, f32[48,32,128]{0,2,1:T(8,128)}, u32[]{:S(2)}) copy-start(f32[48,32,128]{0,2,1:T(8,128)} %copy.20) | copy-start | bytes 2359300
  158.0 4.3 %collective-permute-start = (f32[64,1,128]{0,2,1:T(8,128)S(1)}, f32[64,1,128]{0,2,1:T(8,128)S(1)}, u32[]{:S(2)}, u32[]{:S(2)}) collective-permute-start(f32[64,1,128]{0,2,1:T(8,128)S(1)} %get-tuple-element.24), channel_id=1, source_target_pairs={{4,0},{8,4},{12,8},{16,12},{20,16},{24,20},{28,24},{5,1},{9,5},{13... | collective-permute-start | bytes 98312 | tf_op jit(solution)/shard_map/ppermute | solution.py:25
  159.3 3.9 %collective-permute-start.1 = (f32[64,1,128]{0,2,1:T(8,128)S(1)}, f32[64,1,128]{0,2,1:T(8,128)S(1)}, u32[]{:S(2)}, u32[]{:S(2)}) collective-permute-start(f32[64,1,128]{0,2,1:T(8,128)S(1)} %get-tuple-element.23), channel_id=1, source_target_pairs={{0,4},{4,8},{8,12},{12,16},{16,20},{20,24},{24,28},{1,5},{5,9},{9,... | collective-permute-start | bytes 98312 | tf_op jit(solution)/shard_map/ppermute | solution.py:22
  163.4 7.0 %collective-permute-start.2 = (f32[64,34,1]{0,2,1:T(1,128)S(1)}, f32[64,34,1]{0,2,1:T(1,128)S(1)}, u32[]{:S(2)}, u32[]{:S(2)}) collective-permute-start(f32[64,34,1]{0,2,1:T(1,128)S(1)} %get-tuple-element.14), channel_id=1, source_target_pairs={{1,0},{2,1},{3,2},{5,4},{6,5},{7,6},{9,8},{10,9},{11,10},{13,12},{... | collective-permute-start | bytes 26120 | tf_op jit(solution)/shard_map/ppermute | solution.py:25
  164.7 6.0 %collective-permute-start.3 = (f32[64,34,1]{0,2,1:T(1,128)S(1)}, f32[64,34,1]{0,2,1:T(1,128)S(1)}, u32[]{:S(2)}, u32[]{:S(2)}) collective-permute-start(f32[64,34,1]{0,2,1:T(1,128)S(1)} %get-tuple-element.13), channel_id=1, source_target_pairs={{0,1},{1,2},{2,3},{4,5},{5,6},{6,7},{8,9},{9,10},{10,11},{12,13},{... | collective-permute-start | bytes 26120 | tf_op jit(solution)/shard_map/ppermute | solution.py:22
  182.5 3.5 copy-start.6
  187.8 3.5 copy-start.4
  196.7 2.3 copy-start.2
  199.1 1.1 copy-start.11
  199.1 1.1 slice-start.1
  199.1 1.1 copy-start.12
  200.3 146.5 %copy-start.8 = (f32[16,32,128]{2,1,0:T(8,128)}, f32[16,32,128]{2,1,0:T(8,128)S(1)}, u32[]{:S(2)}) copy-start(f32[16,32,128]{2,1,0:T(8,128)S(1)} %fusion.17) | copy-start | bytes 786436
  335.1 2.7 copy-start.3
  341.3 6.4 %copy-start = (f32[48,32,128]{0,2,1:T(8,128)S(1)}, f32[48,32,128]{0,2,1:T(8,128)}, u32[]{:S(2)}) copy-start(f32[48,32,128]{0,2,1:T(8,128)} %copy.29) | copy-start | bytes 2359300
  342.4 4.4 %collective-permute-start.4 = (f32[64,1,128]{0,2,1:T(8,128)S(1)}, f32[64,1,128]{0,2,1:T(8,128)S(1)}, u32[]{:S(2)}, u32[]{:S(2)}) collective-permute-start(f32[64,1,128]{0,2,1:T(8,128)S(1)} %get-tuple-element.22), channel_id=1, source_target_pairs={{4,0},{8,4},{12,8},{16,12},{20,16},{24,20},{28,24},{5,1},{9,5},{13... | collective-permute-start | bytes 98312 | tf_op jit(solution)/shard_map/ppermute | solution.py:25
  343.7 3.9 %collective-permute-start.5 = (f32[64,1,128]{0,2,1:T(8,128)S(1)}, f32[64,1,128]{0,2,1:T(8,128)S(1)}, u32[]{:S(2)}, u32[]{:S(2)}) collective-permute-start(f32[64,1,128]{0,2,1:T(8,128)S(1)} %get-tuple-element.21), channel_id=1, source_target_pairs={{0,4},{4,8},{8,12},{12,16},{16,20},{20,24},{24,28},{1,5},{5,9},{9,... | collective-permute-start | bytes 98312 | tf_op jit(solution)/shard_map/ppermute | solution.py:22
  347.8 6.8 %collective-permute-start.6 = (f32[64,34,1]{0,2,1:T(1,128)S(1)}, f32[64,34,1]{0,2,1:T(1,128)S(1)}, u32[]{:S(2)}, u32[]{:S(2)}) collective-permute-start(f32[64,34,1]{0,2,1:T(1,128)S(1)} %get-tuple-element.10), channel_id=1, source_target_pairs={{1,0},{2,1},{3,2},{5,4},{6,5},{7,6},{9,8},{10,9},{11,10},{13,12},{... | collective-permute-start | bytes 26120 | tf_op jit(solution)/shard_map/ppermute | solution.py:25
  349.1 6.0 %collective-permute-start.7 = (f32[64,34,1]{0,2,1:T(1,128)S(1)}, f32[64,34,1]{0,2,1:T(1,128)S(1)}, u32[]{:S(2)}, u32[]{:S(2)}) collective-permute-start(f32[64,34,1]{0,2,1:T(1,128)S(1)} %get-tuple-element.9), channel_id=1, source_target_pairs={{0,1},{1,2},{2,3},{4,5},{5,6},{6,7},{8,9},{9,10},{10,11},{12,13},{... | collective-permute-start | bytes 26120 | tf_op jit(solution)/shard_map/ppermute | solution.py:22
  366.9 3.5 copy-start.7
  372.3 3.5 copy-start.5
  381.0 1.1 copy-start.9
  381.0 1.0 slice-start
  381.0 1.3 copy-start.13
Sparse Core Ops, SparseCore 0:
  16.4 132.1 all-reduce.8
  200.3 132.3 all-reduce.6
where the time goes:
time: 393 us; the launch traced here: 390 us
  waiting for transfers between devices  266 us (68%)
  local copies, waits for them, and re-layouts  41.3 us (11%)
  other arithmetic  38.2 us (10%)
  starting transfers between devices  20.6 us (5%)
  between operations  15.8 us (4%)
  matrix products  8.35 us (2%)
    psum x2, waiting for transfers between devices, broadcast(): return lax.psum(kept, axis)  263 us
    concatenate x4, other arithmetic, with_halo(): block = jnp.concatenate([low, block, high], axis=dim)  17.3 us
    ppermute x4, starting transfers between devices, with_halo(): lax.ppermute(lax.slice_in_dim(block, block.shape[dim] - width, None, axis...  15.3 us
  transfers between devices with their start and end apart: 10, of which 6 were waited for; matrix products, arithmetic and copies ran while one was open for 1% of the time, Pallas kernels for 0%

commit v1 on v0

v1 whole, which is shorter than its diff:
```python
import functools
import math

import jax
import jax.numpy as jnp
import numpy as np
from jax import lax
from jax.experimental import pallas as pl
from jax.experimental.pallas import tpu as pltpu
from jax.sharding import PartitionSpec as P

KX = 32
STEPS = 2
HI = lax.Precision.HIGHEST
VMEM = pl.BlockSpec(memory_space=pltpu.VMEM)
SMEM = pl.BlockSpec(memory_space=pltpu.SMEM)
AXES = ("gx", "gy")


def wave_table(positions, period):
    wavenum = np.arange(KX)[:, None]
    phase = (wavenum * positions[None, :] % period) * (2.0 * math.pi / period)
    inside = (positions >= 0) & (positions < period)
    return np.concatenate([np.cos(phase), np.sin(phase)], axis=0) * inside[None, :]


def build_tables(n_gx, n_gy, cells_x, cells_y):
    period_x, period_y = n_gx * cells_x, n_gy * cells_y
    order = np.concatenate([np.arange(0, 2 * KX, 2), np.arange(1, 2 * KX, 2)])
    scaling = 1.0 / math.sqrt(period_x * period_y)
    x_fwd, x_back, y_fwd, y_back = [], [], [], []
    for g in range(n_gx):
        first = g * cells_x
        x_fwd.append(wave_table(first + np.arange(cells_x), period_x)[order])
        rows = np.concatenate([first + np.arange(cells_x), [first - 1, first + cells_x]])
        back = np.zeros((cells_x + 8, 2 * KX))
        back[: cells_x + 2] = wave_table(rows, period_x)[order].T
        x_back.append(back)
    for g in range(n_gy):
        first = g * cells_y
        table = wave_table(first + np.arange(cells_y), period_y)
        edge = np.zeros((2 * KX, cells_y))
        edge[:, [0, -1]] = wave_table(np.array([first - 1, first + cells_y]), period_y)
        y_fwd.append(np.concatenate([table.T, table.T], axis=1) * scaling)
        none = np.zeros_like(table)
        y_back.append(
            np.concatenate(
                [
                    np.concatenate([table, edge, none, none], axis=1),
                    np.concatenate([none, none, table, edge], axis=1),
                ],
                axis=0,
            )
        )
    return [np.stack(t).astype(np.float32) for t in (x_fwd, x_back, y_fwd, y_back)]


def dot(a, b):
    return jnp.dot(a, b, precision=HI, preferred_element_type=jnp.float32)


def emit_modes(read, parent_ref, x_fwd, y_fwd, is_owner, sel_ref, half_ref, modes_ref, nudged):
    cells_x = x_fwd.shape[1]
    for c in range(nudged):
        sel_ref[c] = read(c)
    flat = sel_ref[...].reshape(nudged * cells_x, -1)
    half_ref[...] = dot(flat, y_fwd).reshape(half_ref.shape)
    lane = lax.broadcasted_iota(jnp.int32, (KX, 4 * KX), 1)

    def body(c, carry):
        both = dot(x_fwd, half_ref[c])
        modes_ref[c] = -jnp.where(lane < 2 * KX, both[:KX], both[KX:])
        return carry

    lax.fori_loop(0, nudged, body, 0, unroll=4)

    @pl.when(is_owner)
    def _():
        for i in range(KX):
            tile = parent_ref[:, i * 4 * KX : (i + 1) * 4 * KX]
            modes_ref[:, i, :] = modes_ref[:, i, :] + tile


def emit_edges(read, total, west_ref, east_ref, cols_ref):
    cells_x = cols_ref.shape[0]
    lane = lax.broadcasted_iota(jnp.int32, cols_ref.shape, 1)
    acc = jnp.zeros(cols_ref.shape, jnp.float32)
    for c in range(total):
        a = read(c)
        west_ref[c : c + 1, :] = a[:1]
        east_ref[c : c + 1, :] = a[cells_x - 1 :]
        acc = jnp.where(lane == c, a[:, :1], acc)
        acc = jnp.where(lane == total + c, a[:, a.shape[1] - 1 :], acc)
    cols_ref[...] = acc


def first_kernel(n_gy, levels, owners, fields, plume, parent, x_fwd, y_fwd,
                 modes, west, east, cols, sel, half, parent_here, parent_sem):
    fetch = pltpu.make_async_copy(parent.at[0, 0], parent_here, parent_sem)
    fetch.start()
    level_total = plume.shape[0]
    nudged = sel.shape[0]
    level_count = nudged // 3
    me = lax.axis_index("gx") * n_gy + lax.axis_index("gy")
    fetch.wait()
    emit_modes(
        lambda c: fields[(c // level_count) * level_total + levels[c % level_count]],
        parent_here, x_fwd[0], y_fwd[0], owners[0] == me, sel, half, modes, nudged,
    )
    field_rows = fields.shape[0]
    emit_edges(
        lambda c: fields[c] if c < field_rows else plume[c - field_rows],
        field_rows + level_total, west, east, cols,
    )


def share_kernel(n_gy, period, copies, cuts, parts, out):
    count, rows, lanes = parts.shape
    me = lax.axis_index("gx") * n_gy + lax.axis_index("gy")
    total = parts[0]
    for p in range(1, count):
        total = total + parts[p]
    row = me * rows + lax.broadcasted_iota(jnp.int32, (rows, lanes), 0)
    lane = lax.broadcasted_iota(jnp.int32, (rows, lanes), 1)
    slab, pair = row // KX, row % KX
    r = 2 * pair + lane // (2 * KX)
    s = lane % (2 * KX)
    limit = jnp.zeros((rows, lanes), jnp.int32)
    for c in range(cuts.shape[0]):
        limit = jnp.where(slab == c, cuts[c], limit)
    keep = ((r % KX) < limit) & ((s % KX) < limit)
    factor = jnp.where(r == 0, 1.0, 2.0) * jnp.where(s == 0, 1.0, 2.0) * (1.0 / math.sqrt(period))
    result = jnp.where(keep, total * factor, 0.0)
    if copies:
        for p in range(count):
            out[p] = result
    else:
        out[...] = result


def step_kernel(n_gy, step, last, levels, owners, mismatch, fields, plume, source, west, east,
                south, north, parent, x_fwd, y_fwd, x_back, y_back, *rest):
    if last:
        fields_out, plume_out, back, nudged_ref, rows_ref, cols_ref = rest
    else:
        (fields_out, plume_out, modes, west_out, east_out, cols_out,
         back, nudged_ref, rows_ref, cols_ref, sel, half, parent_here, parent_sem) = rest
        fetch = pltpu.make_async_copy(parent.at[0, step + 1], parent_here, parent_sem)
        fetch.start()
    level_total, cells_x, cells_y = plume.shape
    field_rows = fields.shape[0]
    total = field_rows + level_total
    nudged = mismatch.shape[0] // KX
    level_count = nudged // 3
    back[...] = dot(mismatch[...], y_back[0])
    for c in range(field_rows):
        nudged_ref[c] = fields[c]
    rows_ref[...] = jnp.zeros_like(rows_ref)
    cols_ref[...] = jnp.zeros_like(cols_ref)
    x_table = x_back[0]
    for c in range(nudged):
        pair = back[c * KX : (c + 1) * KX]
        stacked = jnp.concatenate([pair[:, : 2 * cells_y], pair[:, 2 * cells_y :]], axis=0)
        update = dot(x_table, stacked)
        spot = (c // level_count) * level_total + levels[c % level_count]
        nudged_ref[spot] = nudged_ref[spot] + update[:cells_x, :cells_y]
        rows_ref[spot] = update[cells_x:, :cells_y]
        cols_ref[spot] = update[:cells_x, cells_y:]

    row = lax.broadcasted_iota(jnp.int32, (cells_x, cells_y), 0)
    lane = lax.broadcasted_iota(jnp.int32, (cells_x, cells_y), 1)

    def move(a, c, spot, up, um, vp, vm):
        west_row, east_row = west[c : c + 1, :], east[c : c + 1, :]
        south_col, north_col = south[:, total + c : total + c + 1], north[:, c : c + 1]
        if spot is not None:
            west_row = west_row + rows_ref[spot, 0:1]
            east_row = east_row + rows_ref[spot, 1:2]
            south_col = south_col + cols_ref[spot]
            north_col = north_col + cols_ref[spot]
        a_west = jnp.where(row == 0, west_row, pltpu.roll(a, 1, 0))
        a_east = jnp.where(row == cells_x - 1, east_row, pltpu.roll(a, cells_x - 1, 0))
        a_south = jnp.where(lane == 0, south_col, pltpu.roll(a, 1, 1))
        a_north = jnp.where(lane == cells_y - 1, north_col, pltpu.roll(a, cells_y - 1, 1))
        upwind = up * (a - a_west) + um * (a_east - a) + vp * (a - a_south) + vm * (a_north - a)
        laplace = a_east + a_west + a_north + a_south - 4.0 * a
        return 0.1 * laplace - 0.1 * upwind

    for l in range(level_total):
        u, v = nudged_ref[l], nudged_ref[level_total + l]
        up, um = jnp.maximum(u, 0.0), jnp.minimum(u, 0.0)
        vp, vm = jnp.maximum(v, 0.0), jnp.minimum(v, 0.0)
        for f in range(3):
            c = f * level_total + l
            a = nudged_ref[c]
            fields_out[c] = a + move(a, c, c, up, um, vp, vm)
        q = plume[l]
        above = plume[l + 1] if l + 1 < level_total else jnp.zeros_like(q)
        moved = move(q, field_rows + l, None, up, um, vp, vm)
        plume_out[l] = q + moved - 0.3 * q + 0.3 * above + source[l]

    if last:
        return
    fetch.wait()
    me = lax.axis_index("gx") * n_gy + lax.axis_index("gy")
    emit_modes(
        lambda c: fields_out[(c // level_count) * level_total + levels[c % level_count]],
        parent_here, x_fwd[0], y_fwd[0], owners[step + 1] == me, sel, half, modes, nudged,
    )
    emit_edges(
        lambda c: fields_out[c] if c < field_rows else plume_out[c - field_rows],
        total, west_out, east_out, cols_out,
    )


def swap_edges(west, east, cols):
    n_gx, n_gy = lax.axis_size("gx"), lax.axis_size("gy")
    up_x = [(i, i + 1) for i in range(n_gx - 1)]
    up_y = [(i, i + 1) for i in range(n_gy - 1)]
    down_x = [(b, a) for a, b in up_x]
    down_y = [(b, a) for a, b in up_y]
    return (
        lax.ppermute(east, "gx", up_x),
        lax.ppermute(west, "gx", down_x),
        lax.ppermute(cols, "gy", up_y),
        lax.ppermute(cols, "gy", down_y),
    )


def local(tables, fields, levels, cuts, parent_modes, owners, plume, source):
    n_gx, n_gy = lax.axis_size("gx"), lax.axis_size("gy")
    devices = n_gx * n_gy
    level_total, cells_x, cells_y = plume.shape
    period = n_gx * cells_x * n_gy * cells_y
    level_count = levels.shape[0]
    nudged = 3 * level_count
    field_rows = 3 * level_total
    total = field_rows + level_total
    lanes = 4 * KX
    flat = fields.reshape(field_rows, cells_x, cells_y)
    cuts = cuts.reshape(-1)
    gx, gy = lax.axis_index("gx"), lax.axis_index("gy")
    f32 = functools.partial(jax.ShapeDtypeStruct, dtype=jnp.float32)
    params = pltpu.CompilerParams(vmem_limit_bytes=40 * 1024 * 1024)
    x_fwd, x_back, y_fwd, y_back = (
        lax.dynamic_slice_in_dim(jnp.asarray(t), g, 1) for t, g in zip(tables, (gx, gx, gy, gy))
    )
    edge_shapes = [f32((total, cells_y)), f32((total, cells_y)), f32((cells_x, 2 * total))]
    mode_shape = f32((nudged, KX, lanes))
    mode_scratch = [pltpu.VMEM((nudged, cells_x, cells_y), jnp.float32),
                    pltpu.VMEM((nudged, cells_x, lanes), jnp.float32),
                    pltpu.VMEM((nudged, 4 * KX * KX), jnp.float32),
                    pltpu.SemaphoreType.DMA]
    step_scratch = [pltpu.VMEM((nudged * KX, 4 * cells_y), jnp.float32),
                    pltpu.VMEM((field_rows, cells_x, cells_y), jnp.float32),
                    pltpu.VMEM((field_rows, 8, cells_y), jnp.float32),
                    pltpu.VMEM((field_rows, cells_x, cells_y), jnp.float32)]
    parent_spec = pl.BlockSpec(memory_space=pl.ANY)

    modes, west, east, cols = pl.pallas_call(
        functools.partial(first_kernel, n_gy),
        out_shape=[mode_shape] + edge_shapes,
        in_specs=[SMEM, SMEM, VMEM, VMEM, parent_spec, VMEM, VMEM],
        out_specs=[VMEM] * 4,
        scratch_shapes=mode_scratch,
        compiler_params=params,
        name="first_modes",
    )(levels, owners, flat, plume, parent_modes, x_fwd, y_fwd)
    for step in range(STEPS):
        last = step == STEPS - 1
        halo = swap_edges(west, east, cols)
        rows = nudged * KX // devices
        parts = lax.all_to_all(modes.reshape(devices, rows, lanes), AXES, 0, 0, tiled=True)
        direct = step == 0
        share = pl.pallas_call(
            functools.partial(share_kernel, n_gy, period, direct),
            out_shape=f32((devices, rows, lanes) if direct else (rows, lanes)),
            in_specs=[SMEM, VMEM],
            out_specs=VMEM,
            compiler_params=params,
            name="share_sum",
        )(cuts, parts)
        if direct:
            mismatch = lax.all_to_all(share, AXES, 0, 0, tiled=True)
        else:
            mismatch = lax.all_gather(share, AXES, axis=0, tiled=True)
        out_shape = [f32(flat.shape), f32(plume.shape)]
        if not last:
            out_shape += [mode_shape] + edge_shapes
        results = pl.pallas_call(
            functools.partial(step_kernel, n_gy, step, last),
            out_shape=out_shape,
            in_specs=[SMEM, SMEM] + [VMEM] * 8 + [parent_spec] + [VMEM] * 4,
            out_specs=[VMEM] * len(out_shape),
            scratch_shapes=step_scratch + ([] if last else mode_scratch),
            compiler_params=params,
            name="final_step" if last else "inner_step",
        )(levels, owners, mismatch.reshape(nudged * KX, lanes), flat, plume, source, *halo,
          parent_modes, x_fwd, y_fwd, x_back, y_back)
        if last:
            flat, plume = results
        else:
            flat, plume, modes, west, east, cols = results
    return flat.reshape(fields.shape), plume


def solution(mesh):
    in_specs = (
        P(None, None, "gx", "gy"),
        P(),
        P(),
        P(("gx", "gy"), None, None, None),
        P(),
        P(None, "gx", "gy"),
        P(None, "gx", "gy"),
    )
    out_specs = (P(None, None, "gx", "gy"), P(None, "gx", "gy"))
    n_gx, n_gy = mesh.shape["gx"], mesh.shape["gy"]

    def whole(fields, levels, cuts, parent_modes, owners, plume, source):
        tables = build_tables(n_gx, n_gy, plume.shape[1] // n_gx, plume.shape[2] // n_gy)
        return jax.shard_map(
            functools.partial(local, tables), mesh=mesh, in_specs=in_specs, out_specs=out_specs,
            check_vma=False,
        )(fields, levels, cuts, parent_modes, owners, plume, source)

    return whole
```

time: 393 us -> 151 us (0.38)
  waiting for transfers between devices: 266 us -> 16.8 us
  blocking collectives: 0 us -> 69 us
  other arithmetic: 38.2 us -> 0 us
  local copies, waits for them, and re-layouts: 41.3 us -> 9.32 us
  Pallas kernels: 0 us -> 18.4 us
  between operations: 15.8 us -> 0.84 us
  starting transfers between devices: 20.6 us -> 35.5 us
  matrix products: 8.35 us -> 0 us
    psum x2 -> x0, waiting for transfers between devices: 263 us -> none  [broadcast(): return lax.psum(kept, axis)]
    all_gather x0 -> x1, blocking collectives: none -> 69 us  [local(): mismatch = lax.all_gather(share, AXES, axis=0, tiled=True)]
    slice x13 -> x0, local copies, waits for them, and re-layouts: 25 us -> none  [the longest x2 7.09 us: transport(): south_side = split(padded[:, 1:-1, :-2])]
    concatenate x7 -> x0, other arithmetic: 19.6 us -> none  [the longest x4 17.3 us: with_halo(): block = jnp.concatenate([low, block, high], axis=dim)]
    pallas_call x0 -> x5, Pallas kernels: none -> 18.4 us  [the longest x2 12.9 us: local(): pl.pallas_call(functools.partial(step_kernel, n_gy, step, last), out_shap...]
    all_to_all x0 -> x3, starting transfers between devices: none -> 17.9 us  [the longest x2 14.1 us: local(): lax.all_to_all(modes.reshape(devices, rows, lanes), AXES, 0, 0, tiled=True)]
    all_to_all x0 -> x3, waiting for transfers between devices: none -> 15 us  [the longest x2 15 us: local(): lax.all_to_all(modes.reshape(devices, rows, lanes), AXES, 0, 0, tiled=True)]
    sub x4 -> x0, other arithmetic: 9.11 us -> none  [the longest x2 6.8 us: transport(): return (0.1 * laplace - 0.1 * upwind).reshape(values.shape)]
  transfers between devices with their start and end apart: 10 -> 11, of which waited for: 6 -> 3; matrix products, arithmetic and copies ran while one was open for 1% -> 1% of each run, Pallas kernels for 0% -> 0%
where the time goes in v1:
time: 151 us; the launch traced here: 150 us
  blocking collectives  69 us (46%)
  starting transfers between devices  35.5 us (24%)
  Pallas kernels  18.4 us (12%)
  waiting for transfers between devices  16.8 us (11%)
  local copies, waits for them, and re-layouts  9.32 us (6%)
    all_gather x1, blocking collectives, local(): mismatch = lax.all_gather(share, AXES, axis=0, tiled=True)  69 us
    all_to_all x2, waiting for transfers between devices, local(): lax.all_to_all(modes.reshape(devices, rows, lanes), AXES, 0, 0, tiled=True)  15 us
    all_to_all x2, starting transfers between devices, local(): lax.all_to_all(modes.reshape(devices, rows, lanes), AXES, 0, 0, tiled=True)  14.1 us
    pallas_call x2, Pallas kernels, local(): pl.pallas_call(functools.partial(step_kernel, n_gy, step, last), out_shap...  12.9 us
    ppermute x2, starting transfers between devices, swap_edges(): lax.ppermute(cols, 'gy', up_y)  9.09 us
    unnamed x24, local copies, waits for them, and re-layouts  5.91 us
    all_to_all x1, starting transfers between devices, local(): mismatch = lax.all_to_all(share, AXES, 0, 0, tiled=True)  3.86 us
    pallas_call x1, Pallas kernels, local(): pl.pallas_call(functools.partial(first_kernel, n_gy), out_shape=[mode_sha...  3.54 us
  transfers between devices with their start and end apart: 11, of which 3 were waited for; matrix products, arithmetic and copies ran while one was open for 1% of the time, Pallas kernels for 0%

profile of v1, /device:TPU:0, one launch (start us, length us, event | category | flops | bytes accessed | tf_op | source)
XLA Modules:
  0.0 149.9 jit_solution(719944010396016193)
XLA Ops:
  0.6 0.8 constant_dynamic-slice_fusion.3.x_fwd
  1.4 0.8 constant_dynamic-slice_fusion.2.y_fwd
  2.3 0.6 copy-done.9
  2.9 0.0 copy-done.10
  2.9 1.1 copy-done
  4.1 1.1 copy-done.2
  5.2 0.9 copy-done.4
  6.1 3.5 %first_modes.1 = (f32[24,32,128]{2,1,0:T(8,128)}, f32[64,128]{1,0:T(8,128)S(1)}, f32[64,128]{1,0:T(8,128)S(1)}, f32[32,128]{1,0:T(8,128)S(1)}) custom-call(s32[8]{0:T(128)S(1)} %copy-done.9, s32[2]{0:T(128)S(1)} %copy-done.10, f32[48,32,128]{2,1,0:T(8,128)S(1)} %bitcast.5, f32[16,32,128]{2,1,0:T(8,128)S(1)} %copy-done.4, f32[1,2,24,4096]{3,2,1,0:T(8,128)S(1)} %copy-done, ...), custom_call_target="tpu_custom_call" | custom-call | tf_op jit(solution)/shard_map/first_modes/pallas_call | solution.py:260
  9.7 7.3 %all-to-all-start = ((f32[32,24,128]{2,1,0:T(8,128)}), f32[32,24,128]{2,1,0:T(8,128)S(1)}, u32[]{:S(2)}, u32[]{:S(2)}) async-start(f32[32,24,128]{2,1,0:T(8,128)} %bitcast.1), calls=%async_computation | async-start | bytes 786432 | tf_op jit(solution)/shard_map/all_to_all | solution.py:273
  17.0 0.1 reshape.22.cuts
  17.1 11.7 %all-to-all-done.parts = f32[32,24,128]{2,1,0:T(8,128)S(1)} async-done(((f32[32,24,128]{2,1,0:T(8,128)}), f32[32,24,128]{2,1,0:T(8,128)S(1)}, u32[]{:S(2)}, u32[]{:S(2)}) %all-to-all-start) | async-done | bytes 393248 | tf_op jit(solution)/shard_map/all_to_all | solution.py:273
  28.8 1.4 share_sum.2
  30.2 3.9 %all-to-all-start.1 = ((f32[32,24,128]{2,1,0:T(8,128)}), f32[32,24,128]{2,1,0:T(8,128)S(1)}, u32[]{:S(2)}, u32[]{:S(2)}) async-start(f32[32,24,128]{2,1,0:T(8,128)} %share_sum.2), calls=%async_computation.1 | async-start | bytes 786432 | tf_op jit(solution)/shard_map/all_to_all | solution.py:284
  34.1 1.3 collective-permute-start.3
  35.4 4.5 %collective-permute-start.2 = (f32[32,128]{1,0:T(8,128)S(1)}, f32[32,128]{1,0:T(8,128)S(1)}, u32[]{:S(2)}, u32[]{:S(2)}) collective-permute-start(f32[32,128]{1,0:T(8,128)S(1)} %get-tuple-element.17), channel_id=1, source_target_pairs={{0,1},{1,2},{2,3},{4,5},{5,6},{6,7},{8,9},{9,10},{10,11},{12,13},{... | collective-permute-start | bytes 49160 | tf_op jit(solution)/shard_map/ppermute | solution.py:225
  39.9 1.6 %collective-permute-start = (f32[64,128]{1,0:T(8,128)S(1)}, f32[64,128]{1,0:T(8,128)S(1)}, u32[]{:S(2)}, u32[]{:S(2)}) collective-permute-start(f32[64,128]{1,0:T(8,128)S(1)} %get-tuple-element.15), channel_id=1, source_target_pairs={{0,4},{4,8},{8,12},{12,16},{16,20},{20,24},{24,28},{1,5},{5,9},{9,... | collective-permute-start | bytes 98312 | tf_op jit(solution)/shard_map/ppermute | solution.py:223
  41.6 1.4 collective-permute-start.1
  43.0 1.0 constant_dynamic-slice_fusion.y_back
  44.0 0.7 constant_dynamic-slice_fusion.1.x_back
  44.7 1.8 %collective-permute-done.1.east = f32[64,128]{1,0:T(8,128)S(1)} collective-permute-done((f32[64,128]{1,0:T(8,128)S(1)}, f32[64,128]{1,0:T(8,128)S(1)}, u32[]{:S(2)}, u32[]{:S(2)}) %collective-permute-start.1) | collective-permute-done | bytes 32800 | tf_op jit(solution)/shard_map/ppermute | solution.py:224
  46.5 7.6 %inner_step.1 = (f32[48,32,128]{2,1,0:T(8,128)S(1)}, f32[16,32,128]{2,1,0:T(8,128)S(1)}, f32[24,32,128]{2,1,0:T(8,128)}, f32[64,128]{1,0:T(8,128)S(1)}, f32[64,128]{1,0:T(8,128)S(1)}, /*index=5*/f32[32,128]{1,0:T(8,128)S(1)}) custom-call(s32[8]{0:T(128)S(1)} %copy-done.9, s32[2]{0:T(128)S(1)} %copy-done.10, f32[768,128]{1,0:T(8,128)S(1)} %bitcast.7, ...), custom_call_target="tpu_custom_call" | custom-call | tf_op jit(solution)/shard_map/inner_step/pallas_call | solution.py:290
  54.2 0.9 copy-done.7
  55.0 6.8 %all-to-all-start.2 = ((f32[32,24,128]{2,1,0:T(8,128)}), f32[32,24,128]{2,1,0:T(8,128)S(1)}, u32[]{:S(2)}, u32[]{:S(2)}) async-start(f32[32,24,128]{2,1,0:T(8,128)} %bitcast.3), calls=%async_computation.2 | async-start | bytes 786432 | tf_op jit(solution)/shard_map/all_to_all | solution.py:273
  61.8 1.3 collective-permute-start.7
  63.1 4.5 %collective-permute-start.6 = (f32[32,128]{1,0:T(8,128)S(1)}, f32[32,128]{1,0:T(8,128)S(1)}, u32[]{:S(2)}, u32[]{:S(2)}) collective-permute-start(f32[32,128]{1,0:T(8,128)S(1)} %get-tuple-element.23), channel_id=1, source_target_pairs={{0,1},{1,2},{2,3},{4,5},{5,6},{6,7},{8,9},{9,10},{10,11},{12,13},{... | collective-permute-start | bytes 49160 | tf_op jit(solution)/shard_map/ppermute | solution.py:225
  67.7 1.6 %collective-permute-start.4 = (f32[64,128]{1,0:T(8,128)S(1)}, f32[64,128]{1,0:T(8,128)S(1)}, u32[]{:S(2)}, u32[]{:S(2)}) collective-permute-start(f32[64,128]{1,0:T(8,128)S(1)} %get-tuple-element.21), channel_id=1, source_target_pairs={{0,4},{4,8},{8,12},{12,16},{16,20},{20,24},{24,28},{1,5},{5,9},{9,... | collective-permute-start | bytes 98312 | tf_op jit(solution)/shard_map/ppermute | solution.py:223
  69.3 1.3 collective-permute-start.5
  70.6 3.2 %all-to-all-done.2.parts = f32[32,24,128]{2,1,0:T(8,128)S(1)} async-done(((f32[32,24,128]{2,1,0:T(8,128)}), f32[32,24,128]{2,1,0:T(8,128)S(1)}, u32[]{:S(2)}, u32[]{:S(2)}) %all-to-all-start.2) | async-done | bytes 393248 | tf_op jit(solution)/shard_map/all_to_all | solution.py:273
  73.8 0.6 share_sum.3
  74.4 69.0 %all_gather.3.mismatch = f32[768,128]{1,0:T(8,128)S(1)} all-gather(f32[24,128]{1,0:T(8,128)S(1)} %share_sum.3), channel_id=1, replica_groups=mesh['gx'=8,'gy'=4] {'gx','gy'}, dimensions={0}, use_global_device_ids=true | all-gather | bytes 405504 | tf_op jit(solution)/shard_map/all_gather | solution.py:286
  143.5 1.1 copy-done.8
  144.6 5.3 %final_step.1 = (f32[48,32,128]{2,1,0:T(8,128)}, f32[16,32,128]{2,1,0:T(8,128)}) custom-call(s32[8]{0:T(128)S(1)} %copy-done.9, s32[2]{0:T(128)S(1)} %copy-done.10, f32[768,128]{1,0:T(8,128)S(1)} %all_gather.3.mismatch, f32[48,32,128]{2,1,0:T(8,128)S(1)} %copy-done.8, f32[16,32,128]{2,1,0:T(8,128)S(1)} %get-tuple-element.20.plume, ...), custom_call_target="tpu_custom_call" | custom-call | tf_op jit(solution)/shard_map/final_step/pallas_call | solution.py:290
  (25 shorter events, 0.1 us)
Async XLA Ops:
  2.2 0.7 copy-start.9
  2.2 0.7 copy-start.10
  2.9 1.1 copy-start
  4.1 1.1 copy-start.2
  5.2 0.9 copy-start.4
  9.7 7.3 %copy-start.11 = (s32[3,8]{1,0:T(4,128)S(1)}, s32[3,8]{1,0:T(4,128)}, u32[]{:S(2)}) copy-start(s32[3,8]{1,0:T(4,128)} %param.13) | copy-start | bytes 292
  9.7 19.1 %all-to-all-start = ((f32[32,24,128]{2,1,0:T(8,128)}), f32[32,24,128]{2,1,0:T(8,128)S(1)}, u32[]{:S(2)}, u32[]{:S(2)}) async-start(f32[32,24,128]{2,1,0:T(8,128)} %bitcast.1), calls=%async_computation | async-start | bytes 786432 | tf_op jit(solution)/shard_map/all_to_all | solution.py:273
  28.8 17.7 %copy-start.3 = (f32[3,16,32,128]{3,2,1,0:T(8,128)S(1)}, f32[3,16,32,128]{3,2,1,0:T(8,128)}, u32[]{:S(2)}) copy-start(f32[3,16,32,128]{3,2,1,0:T(8,128)} %param.11) | copy-start | bytes 2359300
  30.2 16.3 %copy-start.1 = (f32[1,2,24,4096]{3,2,1,0:T(8,128)S(1)}, f32[1,2,24,4096]{3,2,1,0:T(8,128)}, u32[]{:S(2)}) copy-start(f32[1,2,24,4096]{3,2,1,0:T(8,128)} %parent.5) | copy-start | bytes 2359300
  30.2 16.3 %all-to-all-start.1 = ((f32[32,24,128]{2,1,0:T(8,128)}), f32[32,24,128]{2,1,0:T(8,128)S(1)}, u32[]{:S(2)}, u32[]{:S(2)}) async-start(f32[32,24,128]{2,1,0:T(8,128)} %share_sum.2), calls=%async_computation.1 | async-start | bytes 786432 | tf_op jit(solution)/shard_map/all_to_all | solution.py:284
  34.1 10.6 %collective-permute-start.3 = (f32[32,128]{1,0:T(8,128)S(1)}, f32[32,128]{1,0:T(8,128)S(1)}, u32[]{:S(2)}, u32[]{:S(2)}) collective-permute-start(f32[32,128]{1,0:T(8,128)S(1)} %get-tuple-element.17), channel_id=1, source_target_pairs={{1,0},{2,1},{3,2},{5,4},{6,5},{7,6},{9,8},{10,9},{11,10},{13,12},{... | collective-permute-start | bytes 49160 | tf_op jit(solution)/shard_map/ppermute | solution.py:226
  35.4 9.3 %collective-permute-start.2 = (f32[32,128]{1,0:T(8,128)S(1)}, f32[32,128]{1,0:T(8,128)S(1)}, u32[]{:S(2)}, u32[]{:S(2)}) collective-permute-start(f32[32,128]{1,0:T(8,128)S(1)} %get-tuple-element.17), channel_id=1, source_target_pairs={{0,1},{1,2},{2,3},{4,5},{5,6},{6,7},{8,9},{9,10},{10,11},{12,13},{... | collective-permute-start | bytes 49160 | tf_op jit(solution)/shard_map/ppermute | solution.py:225
  39.9 4.8 %collective-permute-start = (f32[64,128]{1,0:T(8,128)S(1)}, f32[64,128]{1,0:T(8,128)S(1)}, u32[]{:S(2)}, u32[]{:S(2)}) collective-permute-start(f32[64,128]{1,0:T(8,128)S(1)} %get-tuple-element.15), channel_id=1, source_target_pairs={{0,4},{4,8},{8,12},{12,16},{16,20},{20,24},{24,28},{1,5},{5,9},{9,... | collective-permute-start | bytes 98312 | tf_op jit(solution)/shard_map/ppermute | solution.py:223
  41.5 5.0 %copy-start.5 = (f32[16,32,128]{2,1,0:T(8,128)S(1)}, f32[16,32,128]{2,1,0:T(8,128)}, u32[]{:S(2)}) copy-start(f32[16,32,128]{2,1,0:T(8,128)} %plume.3) | copy-start | bytes 786436
  41.6 5.0 %copy-start.6 = (f32[16,32,128]{2,1,0:T(8,128)S(1)}, f32[16,32,128]{2,1,0:T(8,128)}, u32[]{:S(2)}) copy-start(f32[16,32,128]{2,1,0:T(8,128)} %source.3) | copy-start | bytes 786436
  41.6 4.9 %collective-permute-start.1 = (f32[64,128]{1,0:T(8,128)S(1)}, f32[64,128]{1,0:T(8,128)S(1)}, u32[]{:S(2)}, u32[]{:S(2)}) collective-permute-start(f32[64,128]{1,0:T(8,128)S(1)} %get-tuple-element.16), channel_id=1, source_target_pairs={{4,0},{8,4},{12,8},{16,12},{20,16},{24,20},{28,24},{5,1},{9,5},{13... | collective-permute-start | bytes 98312 | tf_op jit(solution)/shard_map/ppermute | solution.py:224
  54.2 0.9 copy-start.7
  55.0 18.8 %all-to-all-start.2 = ((f32[32,24,128]{2,1,0:T(8,128)}), f32[32,24,128]{2,1,0:T(8,128)S(1)}, u32[]{:S(2)}, u32[]{:S(2)}) async-start(f32[32,24,128]{2,1,0:T(8,128)} %bitcast.3), calls=%async_computation.2 | async-start | bytes 786432 | tf_op jit(solution)/shard_map/all_to_all | solution.py:273
  61.8 81.6 %collective-permute-start.7 = (f32[32,128]{1,0:T(8,128)S(1)}, f32[32,128]{1,0:T(8,128)S(1)}, u32[]{:S(2)}, u32[]{:S(2)}) collective-permute-start(f32[32,128]{1,0:T(8,128)S(1)} %get-tuple-element.23), channel_id=1, source_target_pairs={{1,0},{2,1},{3,2},{5,4},{6,5},{7,6},{9,8},{10,9},{11,10},{13,12},{... | collective-permute-start | bytes 49160 | tf_op jit(solution)/shard_map/ppermute | solution.py:226
  63.1 80.3 %collective-permute-start.6 = (f32[32,128]{1,0:T(8,128)S(1)}, f32[32,128]{1,0:T(8,128)S(1)}, u32[]{:S(2)}, u32[]{:S(2)}) collective-permute-start(f32[32,128]{1,0:T(8,128)S(1)} %get-tuple-element.23), channel_id=1, source_target_pairs={{0,1},{1,2},{2,3},{4,5},{5,6},{6,7},{8,9},{9,10},{10,11},{12,13},{... | collective-permute-start | bytes 49160 | tf_op jit(solution)/shard_map/ppermute | solution.py:225
  67.7 75.8 %collective-permute-start.4 = (f32[64,128]{1,0:T(8,128)S(1)}, f32[64,128]{1,0:T(8,128)S(1)}, u32[]{:S(2)}, u32[]{:S(2)}) collective-permute-start(f32[64,128]{1,0:T(8,128)S(1)} %get-tuple-element.21), channel_id=1, source_target_pairs={{0,4},{4,8},{8,12},{12,16},{16,20},{20,24},{24,28},{1,5},{5,9},{9,... | collective-permute-start | bytes 98312 | tf_op jit(solution)/shard_map/ppermute | solution.py:223
  69.3 74.2 %collective-permute-start.5 = (f32[64,128]{1,0:T(8,128)S(1)}, f32[64,128]{1,0:T(8,128)S(1)}, u32[]{:S(2)}, u32[]{:S(2)}) collective-permute-start(f32[64,128]{1,0:T(8,128)S(1)} %get-tuple-element.22), channel_id=1, source_target_pairs={{4,0},{8,4},{12,8},{16,12},{20,16},{24,20},{28,24},{5,1},{9,5},{13... | collective-permute-start | bytes 98312 | tf_op jit(solution)/shard_map/ppermute | solution.py:224
  143.5 1.1 copy-start.8

commit v2 on v1

--- a/solution.py
+++ b/solution.py
@@ -11,9 +11,11 @@
 
 KX = 32
 STEPS = 2
+FIRST_VMEM = 60 * 1024 * 1024
 HI = lax.Precision.HIGHEST
 VMEM = pl.BlockSpec(memory_space=pltpu.VMEM)
 SMEM = pl.BlockSpec(memory_space=pltpu.SMEM)
+HBM = pl.BlockSpec(memory_space=pltpu.HBM)
 AXES = ("gx", "gy")
 
 
@@ -94,15 +96,26 @@
     cols_ref[...] = acc
 
 
-def first_kernel(n_gy, levels, owners, fields, plume, parent, x_fwd, y_fwd,
-                 modes, west, east, cols, sel, half, parent_here, parent_sem):
-    fetch = pltpu.make_async_copy(parent.at[0, 0], parent_here, parent_sem)
-    fetch.start()
+def fetch_all(sems, pairs):
+    copies = [pltpu.make_async_copy(a, b, sems.at[i]) for i, (a, b) in enumerate(pairs)]
+    for copy in copies:
+        copy.start()
+    return copies
+
+
+def first_kernel(n_gy, levels, owners, fields_all, plume_all, parent, x_fwd_all, y_fwd_all,
+                 modes, west, east, cols, sel, half, parent_here, x_fwd, y_fwd, fields, plume,
+                 sems):
+    gx, gy = lax.axis_index("gx"), lax.axis_index("gy")
+    copies = fetch_all(sems, [
+        (x_fwd_all.at[gx], x_fwd.at[0]), (y_fwd_all.at[gy], y_fwd.at[0]), (fields_all, fields),
+        (parent.at[0, 0], parent_here), (plume_all, plume)])
     level_total = plume.shape[0]
     nudged = sel.shape[0]
     level_count = nudged // 3
     me = lax.axis_index("gx") * n_gy + lax.axis_index("gy")
-    fetch.wait()
+    for copy in copies:
+        copy.wait()
     emit_modes(
         lambda c: fields[(c // level_count) * level_total + levels[c % level_count]],
         parent_here, x_fwd[0], y_fwd[0], owners[0] == me, sel, half, modes, nudged,
@@ -138,15 +151,26 @@
         out[...] = result
 
 
-def step_kernel(n_gy, step, last, levels, owners, mismatch, fields, plume, source, west, east,
-                south, north, parent, x_fwd, y_fwd, x_back, y_back, *rest):
+def step_kernel(n_gy, step, last, levels, owners, mismatch, fields_all, plume_all, source_all,
+                west, east, south, north, parent, x_fwd_all, y_fwd_all, x_back_all, y_back_all,
+                *rest):
+    gx, gy = lax.axis_index("gx"), lax.axis_index("gy")
     if last:
-        fields_out, plume_out, back, nudged_ref, rows_ref, cols_ref = rest
+        (fields_out, plume_out, x_back, y_back, back, nudged_ref, rows_ref, cols_ref, source,
+         sems) = rest
+        fields, plume = fields_all, plume_all
+        extra = []
     else:
         (fields_out, plume_out, modes, west_out, east_out, cols_out,
-         back, nudged_ref, rows_ref, cols_ref, sel, half, parent_here, parent_sem) = rest
-        fetch = pltpu.make_async_copy(parent.at[0, step + 1], parent_here, parent_sem)
-        fetch.start()
+         x_back, y_back, back, nudged_ref, rows_ref, cols_ref, source, sems,
+         sel, half, parent_here, x_fwd, y_fwd, fields, plume) = rest
+        extra = [(fields_all, fields), (plume_all, plume), (x_fwd_all.at[gx], x_fwd.at[0]),
+                 (y_fwd_all.at[gy], y_fwd.at[0]), (parent.at[0, step + 1], parent_here)]
+    copies = fetch_all(sems, [
+        (y_back_all.at[gy], y_back.at[0]), (x_back_all.at[gx], x_back.at[0]),
+        (source_all, source)] + extra)
+    for copy in copies:
+        copy.wait()
     level_total, cells_x, cells_y = plume.shape
     field_rows = fields.shape[0]
     total = field_rows + level_total
@@ -201,7 +225,6 @@
 
     if last:
         return
-    fetch.wait()
     me = lax.axis_index("gx") * n_gy + lax.axis_index("gy")
     emit_modes(
         lambda c: fields_out[(c // level_count) * level_total + levels[c % level_count]],
@@ -239,31 +262,27 @@
     lanes = 4 * KX
     flat = fields.reshape(field_rows, cells_x, cells_y)
     cuts = cuts.reshape(-1)
-    gx, gy = lax.axis_index("gx"), lax.axis_index("gy")
     f32 = functools.partial(jax.ShapeDtypeStruct, dtype=jnp.float32)
     params = pltpu.CompilerParams(vmem_limit_bytes=40 * 1024 * 1024)
-    x_fwd, x_back, y_fwd, y_back = (
-        lax.dynamic_slice_in_dim(jnp.asarray(t), g, 1) for t, g in zip(tables, (gx, gx, gy, gy))
-    )
+    x_fwd, x_back, y_fwd, y_back = (jnp.asarray(t) for t in tables)
     edge_shapes = [f32((total, cells_y)), f32((total, cells_y)), f32((cells_x, 2 * total))]
     mode_shape = f32((nudged, KX, lanes))
-    mode_scratch = [pltpu.VMEM((nudged, cells_x, cells_y), jnp.float32),
-                    pltpu.VMEM((nudged, cells_x, lanes), jnp.float32),
-                    pltpu.VMEM((nudged, 4 * KX * KX), jnp.float32),
-                    pltpu.SemaphoreType.DMA]
-    step_scratch = [pltpu.VMEM((nudged * KX, 4 * cells_y), jnp.float32),
-                    pltpu.VMEM((field_rows, cells_x, cells_y), jnp.float32),
-                    pltpu.VMEM((field_rows, 8, cells_y), jnp.float32),
-                    pltpu.VMEM((field_rows, cells_x, cells_y), jnp.float32)]
-    parent_spec = pl.BlockSpec(memory_space=pl.ANY)
+    vmem = lambda *shape: pltpu.VMEM(shape, jnp.float32)
+    slabs, ash = vmem(field_rows, cells_x, cells_y), vmem(level_total, cells_x, cells_y)
+    mode_scratch = [vmem(nudged, cells_x, cells_y), vmem(nudged, cells_x, lanes),
+                    vmem(nudged, 4 * KX * KX), vmem(1, *x_fwd.shape[1:]), vmem(1, *y_fwd.shape[1:]),
+                    slabs, ash]
+    step_scratch = [vmem(1, *x_back.shape[1:]), vmem(1, *y_back.shape[1:]),
+                    vmem(nudged * KX, 4 * cells_y), slabs, vmem(field_rows, 8, cells_y), slabs,
+                    ash, pltpu.SemaphoreType.DMA((8,))]
 
     modes, west, east, cols = pl.pallas_call(
         functools.partial(first_kernel, n_gy),
         out_shape=[mode_shape] + edge_shapes,
-        in_specs=[SMEM, SMEM, VMEM, VMEM, parent_spec, VMEM, VMEM],
+        in_specs=[SMEM, SMEM] + [HBM] * 5,
         out_specs=[VMEM] * 4,
-        scratch_shapes=mode_scratch,
-        compiler_params=params,
+        scratch_shapes=mode_scratch + [pltpu.SemaphoreType.DMA((5,))],
+        compiler_params=pltpu.CompilerParams(vmem_limit_bytes=FIRST_VMEM),
         name="first_modes",
     )(levels, owners, flat, plume, parent_modes, x_fwd, y_fwd)
     for step in range(STEPS):
@@ -283,14 +302,19 @@
         if direct:
             mismatch = lax.all_to_all(share, AXES, 0, 0, tiled=True)
         else:
-            mismatch = lax.all_gather(share, AXES, axis=0, tiled=True)
+            line = lax.all_to_all(
+                jnp.broadcast_to(share[None], (n_gy, rows, lanes)), "gy", 0, 0, tiled=True
+            ).reshape(n_gy * rows, lanes)
+            mismatch = lax.all_to_all(
+                jnp.broadcast_to(line[None], (n_gx, n_gy * rows, lanes)), "gx", 0, 0, tiled=True
+            )
         out_shape = [f32(flat.shape), f32(plume.shape)]
         if not last:
             out_shape += [mode_shape] + edge_shapes
         results = pl.pallas_call(
             functools.partial(step_kernel, n_gy, step, last),
             out_shape=out_shape,
-            in_specs=[SMEM, SMEM] + [VMEM] * 8 + [parent_spec] + [VMEM] * 4,
+            in_specs=[SMEM, SMEM, VMEM] + [VMEM if last else HBM] * 2 + [HBM] + [VMEM] * 4 + [HBM] * 5,
             out_specs=[VMEM] * len(out_shape),
             scratch_shapes=step_scratch + ([] if last else mode_scratch),
             compiler_params=params,

time: 151 us -> 116 us (0.77)
  the two profiles are of different devices: /device:TPU:0 before, /device:TPU:12 now
where the time goes in v2:
time: 116 us; the launch traced here: 115 us
  starting transfers between devices  39.1 us (34%)
  blocking collectives  24.9 us (21%)
  Pallas kernels  20.7 us (18%)
  waiting for transfers between devices  16.5 us (14%)
  local copies, waits for them, and re-layouts  12.3 us (11%)
    all_to_all x1, blocking collectives, local(): lax.all_to_all(modes.reshape(devices, rows, lanes), AXES, 0, 0, tiled=True)  16.1 us
    pallas_call x2, Pallas kernels, local(): pl.pallas_call(functools.partial(step_kernel, n_gy, step, last), out_shap...  13.9 us
    unnamed x60, local copies, waits for them, and re-layouts  11.4 us
    all_to_all x1, waiting for transfers between devices, local(): lax.all_to_all(modes.reshape(devices, rows, lanes), AXES, 0, 0, tiled=True)  11.3 us
    all_to_all x1, blocking collectives, local(): lax.all_to_all(jnp.broadcast_to(share[None], (n_gy, rows, lanes)), 'gy',...  8.84 us
    ppermute x2, starting transfers between devices, swap_edges(): lax.ppermute(west, 'gx', down_x)  8.81 us
    ppermute x2, starting transfers between devices, swap_edges(): lax.ppermute(cols, 'gy', up_y)  6.29 us
    all_to_all x1, starting transfers between devices, local(): lax.all_to_all(modes.reshape(devices, rows, lanes), AXES, 0, 0, tiled=True)  6 us
  transfers between devices with their start and end apart: 11, of which 3 were waited for; matrix products, arithmetic and copies ran while one was open for 0% of the time, Pallas kernels for 0%

profile of v2, /device:TPU:12, one launch (start us, length us, event | category | flops | bytes accessed | tf_op | source)
XLA Modules:
  0.0 114.6 jit_solution(11937787102464856853)
XLA Ops:
  0.6 5.6 %first_modes.1 = (f32[24,32,128]{2,1,0:T(8,128)}, f32[64,128]{1,0:T(8,128)}, f32[64,128]{1,0:T(8,128)}, f32[32,128]{1,0:T(8,128)}) custom-call(s32[8]{0:T(128)} %levels.5, s32[2]{0:T(128)} %owners.5, f32[48,32,128]{2,1,0:T(8,128)} %bitcast.7, f32[16,32,128]{2,1,0:T(8,128)} %plume_all.3, f32[1,2,24,4096]{3,2,1,0:T(8,128)} %parent.5, ...), custom_call_target="tpu_custom_call" | custom-call | tf_op jit(solution)/shard_map/first_modes/pallas_call | solution.py:279
  6.3 6.0 %all-to-all-start = ((f32[32,24,128]{2,1,0:T(8,128)}), f32[32,24,128]{2,1,0:T(8,128)S(1)}, u32[]{:S(2)}, u32[]{:S(2)}) async-start(f32[32,24,128]{2,1,0:T(8,128)} %bitcast.12), calls=%async_computation | async-start | bytes 786432 | tf_op jit(solution)/shard_map/all_to_all | solution.py:292
  12.4 11.3 %all-to-all-done.parts = f32[32,24,128]{2,1,0:T(8,128)S(1)} async-done(((f32[32,24,128]{2,1,0:T(8,128)}), f32[32,24,128]{2,1,0:T(8,128)S(1)}, u32[]{:S(2)}, u32[]{:S(2)}) %all-to-all-start) | async-done | bytes 393248 | tf_op jit(solution)/shard_map/all_to_all | solution.py:292
  23.7 0.6 share_sum.2
  24.3 0.7 copy-done.5
  25.6 4.3 %all-to-all-start.1 = ((f32[32,24,128]{2,1,0:T(8,128)}), f32[32,24,128]{2,1,0:T(8,128)S(1)}, u32[]{:S(2)}, u32[]{:S(2)}) async-start(f32[32,24,128]{2,1,0:T(8,128)} %copy-done.5), calls=%async_computation.1 | async-start | bytes 786432 | tf_op jit(solution)/shard_map/all_to_all | solution.py:303
  29.9 2.1 %collective-permute-start = (f32[64,128]{1,0:T(8,128)}, f32[64,128]{1,0:T(8,128)S(1)}, u32[]{:S(2)}, u32[]{:S(2)}) collective-permute-start(f32[64,128]{1,0:T(8,128)} %get-tuple-element.15), channel_id=1, source_target_pairs={{0,4},{4,8},{8,12},{12,16},{16,20},{20,24},{24,28},{1,5},{5,9},{9,... | collective-permute-start | bytes 98312 | tf_op jit(solution)/shard_map/ppermute | solution.py:246
  32.0 4.4 %collective-permute-start.1 = (f32[64,128]{1,0:T(8,128)}, f32[64,128]{1,0:T(8,128)S(1)}, u32[]{:S(2)}, u32[]{:S(2)}) collective-permute-start(f32[64,128]{1,0:T(8,128)} %get-tuple-element.16), channel_id=1, source_target_pairs={{4,0},{8,4},{12,8},{16,12},{20,16},{24,20},{28,24},{5,1},{9,5},{13... | collective-permute-start | bytes 98312 | tf_op jit(solution)/shard_map/ppermute | solution.py:247
  36.4 2.5 %collective-permute-start.3 = (f32[32,128]{1,0:T(8,128)}, f32[32,128]{1,0:T(8,128)S(1)}, u32[]{:S(2)}, u32[]{:S(2)}) collective-permute-start(f32[32,128]{1,0:T(8,128)} %get-tuple-element.17), channel_id=1, source_target_pairs={{1,0},{2,1},{3,2},{5,4},{6,5},{7,6},{9,8},{10,9},{11,10},{13,12},{... | collective-permute-start | bytes 49160 | tf_op jit(solution)/shard_map/ppermute | solution.py:249
  38.8 3.4 %collective-permute-start.2 = (f32[32,128]{1,0:T(8,128)}, f32[32,128]{1,0:T(8,128)S(1)}, u32[]{:S(2)}, u32[]{:S(2)}) collective-permute-start(f32[32,128]{1,0:T(8,128)} %get-tuple-element.17), channel_id=1, source_target_pairs={{0,1},{1,2},{2,3},{4,5},{5,6},{6,7},{8,9},{9,10},{10,11},{12,13},{... | collective-permute-start | bytes 49160 | tf_op jit(solution)/shard_map/ppermute | solution.py:248
  42.2 2.4 %collective-permute-done.2.south = f32[32,128]{1,0:T(8,128)S(1)} collective-permute-done((f32[32,128]{1,0:T(8,128)}, f32[32,128]{1,0:T(8,128)S(1)}, u32[]{:S(2)}, u32[]{:S(2)}) %collective-permute-start.2) | collective-permute-done | bytes 16416 | tf_op jit(solution)/shard_map/ppermute | solution.py:248
  45.9 0.6 copy-done.17
  47.2 0.9 copy-done.6
  48.1 0.9 copy-done.7
  49.1 0.9 copy-done.11
  50.0 0.8 copy-done.16
  50.8 0.8 copy-done.18
  51.5 0.7 copy-done.20
  52.2 8.5 %inner_step.1 = (f32[48,32,128]{2,1,0:T(8,128)S(1)}, f32[16,32,128]{2,1,0:T(8,128)S(1)}, f32[24,32,128]{2,1,0:T(8,128)S(1)}, f32[64,128]{1,0:T(8,128)}, f32[64,128]{1,0:T(8,128)}, /*index=5*/f32[32,128]{1,0:T(8,128)S(1)}) custom-call(s32[8]{0:T(128)S(1)} %copy-done.23, s32[2]{0:T(128)S(1)} %copy-done.25, f32[768,128]{1,0:T(8,128)S(1)} %bitcast.10, ...), custom_call_target="tpu_custom_call" | custom-call | tf_op jit(solution)/shard_map/inner_step/pallas_call | solution.py:314
  60.7 0.9 copy-done.9
  61.6 16.1 %all_to_all.25.parts = f32[32,24,128]{2,1,0:T(8,128)S(1)} all-to-all(f32[32,24,128]{2,1,0:T(8,128)S(1)} %bitcast.11), channel_id=1, replica_groups=mesh['gx'=8,'gy'=4] {'gx','gy'}, dimensions={0} | all-to-all | bytes 786432 | tf_op jit(solution)/shard_map/all_to_all | solution.py:292
  77.7 0.6 share_sum.3
  78.3 8.8 %all_to_all.26 = f32[4,24,128]{2,1,0:T(8,128)S(1)} all-to-all(f32[4,24,128]{2,1,0:T(8,128)S(1)} %broadcast_in_dim.6), channel_id=1, replica_groups=mesh['gx'=8,'gy'=4] {'gy'}, dimensions={0} | all-to-all | bytes 98304 | tf_op jit(solution)/shard_map/all_to_all | solution.py:305
  87.2 0.8 broadcast_in_dim.15
  87.9 4.1 %all-to-all-start.4 = ((f32[8,96,128]{2,1,0:T(8,128)}), f32[8,96,128]{2,1,0:T(8,128)S(1)}, u32[]{:S(2)}, u32[]{:S(2)}) async-start(f32[8,96,128]{2,1,0:T(8,128)} %broadcast_in_dim.15), calls=%async_computation.4 | async-start | bytes 786432 | tf_op jit(solution)/shard_map/all_to_all | solution.py:308
  92.0 2.0 %collective-permute-start.4 = (f32[64,128]{1,0:T(8,128)}, f32[64,128]{1,0:T(8,128)S(1)}, u32[]{:S(2)}, u32[]{:S(2)}) collective-permute-start(f32[64,128]{1,0:T(8,128)} %get-tuple-element.21), channel_id=1, source_target_pairs={{0,4},{4,8},{8,12},{12,16},{16,20},{20,24},{24,28},{1,5},{5,9},{9,... | collective-permute-start | bytes 98312 | tf_op jit(solution)/shard_map/ppermute | solution.py:246
  94.1 4.4 %collective-permute-start.5 = (f32[64,128]{1,0:T(8,128)}, f32[64,128]{1,0:T(8,128)S(1)}, u32[]{:S(2)}, u32[]{:S(2)}) collective-permute-start(f32[64,128]{1,0:T(8,128)} %get-tuple-element.22), channel_id=1, source_target_pairs={{4,0},{8,4},{12,8},{16,12},{20,16},{24,20},{28,24},{5,1},{9,5},{13... | collective-permute-start | bytes 98312 | tf_op jit(solution)/shard_map/ppermute | solution.py:247
  98.5 3.1 %collective-permute-start.7 = (f32[32,128]{1,0:T(8,128)S(1)}, f32[32,128]{1,0:T(8,128)S(1)}, u32[]{:S(2)}, u32[]{:S(2)}) collective-permute-start(f32[32,128]{1,0:T(8,128)S(1)} %copy-done.28), channel_id=1, source_target_pairs={{1,0},{2,1},{3,2},{5,4},{6,5},{7,6},{9,8},{10,9},{11,10},{13,12},{... | collective-permute-start | bytes 49160 | tf_op jit(solution)/shard_map/ppermute | solution.py:249
  101.6 2.9 %collective-permute-start.6 = (f32[32,128]{1,0:T(8,128)S(1)}, f32[32,128]{1,0:T(8,128)S(1)}, u32[]{:S(2)}, u32[]{:S(2)}) collective-permute-start(f32[32,128]{1,0:T(8,128)S(1)} %copy-done.28), channel_id=1, source_target_pairs={{0,1},{1,2},{2,3},{4,5},{5,6},{6,7},{8,9},{9,10},{10,11},{12,13},{... | collective-permute-start | bytes 49160 | tf_op jit(solution)/shard_map/ppermute | solution.py:248
  104.5 2.7 %collective-permute-done.6.south = f32[32,128]{1,0:T(8,128)S(1)} collective-permute-done((f32[32,128]{1,0:T(8,128)S(1)}, f32[32,128]{1,0:T(8,128)S(1)}, u32[]{:S(2)}, u32[]{:S(2)}) %collective-permute-start.6) | collective-permute-done | bytes 16416 | tf_op jit(solution)/shard_map/ppermute | solution.py:248
  107.9 1.1 copy-done.10
  109.1 5.4 %final_step.1 = (f32[48,32,128]{2,1,0:T(8,128)}, f32[16,32,128]{2,1,0:T(8,128)}) custom-call(s32[8]{0:T(128)S(1)} %copy-done.24, s32[2]{0:T(128)S(1)} %copy-done.26, f32[768,128]{1,0:T(8,128)S(1)} %bitcast.9, f32[48,32,128]{2,1,0:T(8,128)S(1)} %copy-done.10, f32[16,32,128]{2,1,0:T(8,128)S(1)} %copy-done.14, f32[16,32,128]{2,1,0:T(8,128)S(1)} %copy-done.8, ...), custom_call_target="tpu_custom_call" | custom-call | tf_op jit(solution)/shard_map/final_step/pallas_call | solution.py:314
  (60 shorter events, 3.2 us)
Async XLA Ops:
  0.6 11.7 %copy-start.29 = (s32[3,8]{1,0:T(4,128)S(1)}, s32[3,8]{1,0:T(4,128)}, u32[]{:S(2)}) copy-start(s32[3,8]{1,0:T(4,128)} %param.13) | copy-start | bytes 292
  0.6 45.9 %copy-start.2 = (f32[3,16,32,128]{3,2,1,0:T(8,128)S(1)}, f32[3,16,32,128]{3,2,1,0:T(8,128)}, u32[]{:S(2)}) copy-start(f32[3,16,32,128]{3,2,1,0:T(8,128)} %param.11) | copy-start | bytes 2359300
  6.3 40.3 %copy-start.1 = (f32[4,128,512]{2,1,0:T(8,128)S(1)}, f32[4,128,512]{2,1,0:T(8,128)}, u32[]{:S(2)}) copy-start(f32[4,128,512]{2,1,0:T(8,128)} %constant.11.clone.y_back_all) | copy-start | bytes 3145732
  6.3 17.4 %all-to-all-start = ((f32[32,24,128]{2,1,0:T(8,128)}), f32[32,24,128]{2,1,0:T(8,128)S(1)}, u32[]{:S(2)}, u32[]{:S(2)}) async-start(f32[32,24,128]{2,1,0:T(8,128)} %bitcast.12), calls=%async_computation | async-start | bytes 786432 | tf_op jit(solution)/shard_map/all_to_all | solution.py:292
  12.4 34.2 %copy-start = (f32[1,2,24,4096]{3,2,1,0:T(8,128)S(1)}, f32[1,2,24,4096]{3,2,1,0:T(8,128)}, u32[]{:S(2)}) copy-start(f32[1,2,24,4096]{3,2,1,0:T(8,128)} %parent.5) | copy-start | bytes 2359300
  24.3 0.7 copy-start.5
  25.6 20.9 %copy-start.3 = (f32[4,128,128]{2,1,0:T(8,128)S(1)}, f32[4,128,128]{2,1,0:T(8,128)}, u32[]{:S(2)}) copy-start(f32[4,128,128]{2,1,0:T(8,128)} %constant.10.clone.y_fwd_all) | copy-start | bytes 786436
  25.6 21.0 %copy-start.4 = (f32[8,64,32]{2,1,0:T(8,128)S(1)}, f32[8,64,32]{2,1,0:T(8,128)}, u32[]{:S(2)}) copy-start(f32[8,64,32]{2,1,0:T(8,128)} %constant.8.clone.x_fwd_all) | copy-start | bytes 196612
  25.6 20.9 %all-to-all-start.1 = ((f32[32,24,128]{2,1,0:T(8,128)}), f32[32,24,128]{2,1,0:T(8,128)S(1)}, u32[]{:S(2)}, u32[]{:S(2)}) async-start(f32[32,24,128]{2,1,0:T(8,128)} %copy-done.5), calls=%async_computation.1 | async-start | bytes 786432 | tf_op jit(solution)/shard_map/all_to_all | solution.py:303
  29.9 15.4 %collective-permute-start = (f32[64,128]{1,0:T(8,128)}, f32[64,128]{1,0:T(8,128)S(1)}, u32[]{:S(2)}, u32[]{:S(2)}) collective-permute-start(f32[64,128]{1,0:T(8,128)} %get-tuple-element.15), channel_id=1, source_target_pairs={{0,4},{4,8},{8,12},{12,16},{16,20},{20,24},{24,28},{1,5},{5,9},{9,... | collective-permute-start | bytes 98312 | tf_op jit(solution)/shard_map/ppermute | solution.py:246
  32.0 13.9 %collective-permute-start.1 = (f32[64,128]{1,0:T(8,128)}, f32[64,128]{1,0:T(8,128)S(1)}, u32[]{:S(2)}, u32[]{:S(2)}) collective-permute-start(f32[64,128]{1,0:T(8,128)} %get-tuple-element.16), channel_id=1, source_target_pairs={{4,0},{8,4},{12,8},{16,12},{20,16},{24,20},{28,24},{5,1},{9,5},{13... | collective-permute-start | bytes 98312 | tf_op jit(solution)/shard_map/ppermute | solution.py:247
  36.4 5.9 %collective-permute-start.3 = (f32[32,128]{1,0:T(8,128)}, f32[32,128]{1,0:T(8,128)S(1)}, u32[]{:S(2)}, u32[]{:S(2)}) collective-permute-start(f32[32,128]{1,0:T(8,128)} %get-tuple-element.17), channel_id=1, source_target_pairs={{1,0},{2,1},{3,2},{5,4},{6,5},{7,6},{9,8},{10,9},{11,10},{13,12},{... | collective-permute-start | bytes 49160 | tf_op jit(solution)/shard_map/ppermute | solution.py:249
  38.8 5.8 %collective-permute-start.2 = (f32[32,128]{1,0:T(8,128)}, f32[32,128]{1,0:T(8,128)S(1)}, u32[]{:S(2)}, u32[]{:S(2)}) collective-permute-start(f32[32,128]{1,0:T(8,128)} %get-tuple-element.17), channel_id=1, source_target_pairs={{0,1},{1,2},{2,3},{4,5},{5,6},{6,7},{8,9},{9,10},{10,11},{12,13},{... | collective-permute-start | bytes 49160 | tf_op jit(solution)/shard_map/ppermute | solution.py:248
  47.2 0.9 copy-start.6
  48.1 0.9 copy-start.7
  49.1 0.9 copy-start.11
  50.0 0.8 copy-start.16
  50.8 0.8 copy-start.18
  60.7 0.9 copy-start.9
  61.6 16.1 %copy-start.13 = (f32[16,32,128]{2,1,0:T(8,128)}, f32[16,32,128]{2,1,0:T(8,128)S(1)}, u32[]{:S(2)}) copy-start(f32[16,32,128]{2,1,0:T(8,128)S(1)} %get-tuple-element.20.plume_all) | copy-start | bytes 786436
  61.6 16.1 %copy-start.27 = (f32[32,128]{1,0:T(8,128)}, f32[32,128]{1,0:T(8,128)S(1)}, u32[]{:S(2)}) copy-start(f32[32,128]{1,0:T(8,128)S(1)} %get-tuple-element.23) | copy-start | bytes 49156
  61.6 16.1 %copy-start.22 = (s32[24]{0:T(128)S(1)}, s32[24]{0:T(128)}, u32[]{:S(2)}) copy-start(s32[24]{0:T(128)} %copy-done.21) | copy-start | bytes 292
  87.9 10.6 %copy-start.28 = (f32[32,128]{1,0:T(8,128)S(1)}, f32[32,128]{1,0:T(8,128)}, u32[]{:S(2)}) copy-start(f32[32,128]{1,0:T(8,128)} %copy-done.27) | copy-start | bytes 49156
  87.9 19.3 %copy-start.8 = (f32[16,32,128]{2,1,0:T(8,128)S(1)}, f32[16,32,128]{2,1,0:T(8,128)}, u32[]{:S(2)}) copy-start(f32[16,32,128]{2,1,0:T(8,128)} %source_all.3) | copy-start | bytes 786436
  87.9 19.4 %copy-start.12 = (f32[8,40,64]{2,1,0:T(8,128)S(1)}, f32[8,40,64]{2,1,0:T(8,128)}, u32[]{:S(2)}) copy-start(f32[8,40,64]{2,1,0:T(8,128)} %constant.9.clone.x_back_all) | copy-start | bytes 245764
  87.9 19.4 %copy-start.14 = (f32[16,32,128]{2,1,0:T(8,128)S(1)}, f32[16,32,128]{2,1,0:T(8,128)}, u32[]{:S(2)}) copy-start(f32[16,32,128]{2,1,0:T(8,128)} %copy-done.13) | copy-start | bytes 786436
  87.9 19.3 %all-to-all-start.4 = ((f32[8,96,128]{2,1,0:T(8,128)}), f32[8,96,128]{2,1,0:T(8,128)S(1)}, u32[]{:S(2)}, u32[]{:S(2)}) async-start(f32[8,96,128]{2,1,0:T(8,128)} %broadcast_in_dim.15), calls=%async_computation.4 | async-start | bytes 786432 | tf_op jit(solution)/shard_map/all_to_all | solution.py:308
  92.0 15.2 %collective-permute-start.4 = (f32[64,128]{1,0:T(8,128)}, f32[64,128]{1,0:T(8,128)S(1)}, u32[]{:S(2)}, u32[]{:S(2)}) collective-permute-start(f32[64,128]{1,0:T(8,128)} %get-tuple-element.21), channel_id=1, source_target_pairs={{0,4},{4,8},{8,12},{12,16},{16,20},{20,24},{24,28},{1,5},{5,9},{9,... | collective-permute-start | bytes 98312 | tf_op jit(solution)/shard_map/ppermute | solution.py:246
  94.1 13.2 %collective-permute-start.5 = (f32[64,128]{1,0:T(8,128)}, f32[64,128]{1,0:T(8,128)S(1)}, u32[]{:S(2)}, u32[]{:S(2)}) collective-permute-start(f32[64,128]{1,0:T(8,128)} %get-tuple-element.22), channel_id=1, source_target_pairs={{4,0},{8,4},{12,8},{16,12},{20,16},{24,20},{28,24},{5,1},{9,5},{13... | collective-permute-start | bytes 98312 | tf_op jit(solution)/shard_map/ppermute | solution.py:247
  98.5 6.0 %collective-permute-start.7 = (f32[32,128]{1,0:T(8,128)S(1)}, f32[32,128]{1,0:T(8,128)S(1)}, u32[]{:S(2)}, u32[]{:S(2)}) collective-permute-start(f32[32,128]{1,0:T(8,128)S(1)} %copy-done.28), channel_id=1, source_target_pairs={{1,0},{2,1},{3,2},{5,4},{6,5},{7,6},{9,8},{10,9},{11,10},{13,12},{... | collective-permute-start | bytes 49160 | tf_op jit(solution)/shard_map/ppermute | solution.py:249
  101.6 5.6 %collective-permute-start.6 = (f32[32,128]{1,0:T(8,128)S(1)}, f32[32,128]{1,0:T(8,128)S(1)}, u32[]{:S(2)}, u32[]{:S(2)}) collective-permute-start(f32[32,128]{1,0:T(8,128)S(1)} %copy-done.28), channel_id=1, source_target_pairs={{0,1},{1,2},{2,3},{4,5},{5,6},{6,7},{8,9},{9,10},{10,11},{12,13},{... | collective-permute-start | bytes 49160 | tf_op jit(solution)/shard_map/ppermute | solution.py:248
  107.9 1.1 copy-start.10
  (9 other events, 5.7 us)

commit v3 on v2

v3 whole, which is shorter than its diff:
```python
import functools
import math

import jax
import jax.numpy as jnp
import ml_dtypes
import numpy as np
from jax import lax
from jax.experimental import pallas as pl
from jax.experimental.pallas import tpu as pltpu
from jax.sharding import PartitionSpec as P

KX = 32
STEPS = 2
FIRST_MIB = 60
PAD = 8
VMEM = pl.BlockSpec(memory_space=pltpu.VMEM)
SMEM = pl.BlockSpec(memory_space=pltpu.SMEM)
HBM = pl.BlockSpec(memory_space=pltpu.HBM)
AXES = ("gx", "gy")


def wave_table(positions, period):
    wavenum = np.arange(KX)[:, None]
    phase = (wavenum * positions[None, :] % period) * (2.0 * math.pi / period)
    inside = (positions >= 0) & (positions < period)
    return np.concatenate([np.cos(phase), np.sin(phase)], axis=0) * inside[None, :]


def split(a):
    head = a.astype(jnp.bfloat16)
    return head, (a - head.astype(jnp.float32)).astype(jnp.bfloat16)


def split_table(table, axis, order):
    head = table.astype(ml_dtypes.bfloat16)
    rest = (table - head.astype(np.float64)).astype(ml_dtypes.bfloat16)
    return np.concatenate([head if part == "h" else rest for part in order], axis=axis)


def build_tables(n_gx, n_gy, cells_x, cells_y):
    period_x, period_y = n_gx * cells_x, n_gy * cells_y
    order = np.concatenate([np.arange(0, 2 * KX, 2), np.arange(1, 2 * KX, 2)])
    scaling = 1.0 / math.sqrt(period_x * period_y)
    x_fwd, x_back, y_fwd, y_back = [], [], [], []
    for g in range(n_gx):
        first = g * cells_x
        forward = wave_table(first + np.arange(cells_x), period_x)[order]
        x_fwd.append(split_table(forward, 1, "hlh"))
        rows = np.concatenate([first + np.arange(cells_x), [first - 1, first + cells_x]])
        back = np.zeros((cells_x + 16, 2 * KX))
        back[: cells_x + 2] = wave_table(rows, period_x)[order].T
        x_back.append(split_table(back, 1, "hlh"))
    for g in range(n_gy):
        first = g * cells_y
        table = wave_table(first + np.arange(cells_y), period_y)
        edge = np.zeros((2 * KX, cells_y))
        edge[:, [0, -1]] = wave_table(np.array([first - 1, first + cells_y]), period_y)
        forward = np.concatenate([table.T, table.T], axis=1) * scaling
        y_fwd.append(split_table(forward, 0, "hhl"))
        none = np.zeros_like(table)
        back = np.concatenate(
            [
                np.concatenate([table, edge, none, none], axis=1),
                np.concatenate([none, none, table, edge], axis=1),
            ],
            axis=0,
        )
        y_back.append(split_table(back, 0, "hhl"))
    return [np.stack(t) for t in (x_fwd, x_back, y_fwd, y_back)]


def data_dot(a, table):
    head, rest = split(a)
    return jnp.dot(
        jnp.concatenate([head, rest, head], axis=1), table, preferred_element_type=jnp.float32
    )


def table_dot(table, a):
    head, rest = split(a)
    return jnp.dot(
        table, jnp.concatenate([head, head, rest], axis=0), preferred_element_type=jnp.float32
    )


def emit_modes(read, x_fwd, y_fwd, modes_ref):
    nudged = modes_ref.shape[0]
    slabs = [read(c) for c in range(nudged)]
    cells_x = slabs[0].shape[0]
    half = data_dot(jnp.concatenate(slabs, axis=0), y_fwd)
    lane = lax.broadcasted_iota(jnp.int32, (KX, 4 * KX), 1)
    for c in range(nudged):
        both = table_dot(x_fwd, half[c * cells_x : (c + 1) * cells_x])
        modes_ref[c] = -jnp.where(lane < 2 * KX, both[:KX], both[KX:])


def add_parent(parent, is_owner, modes_ref):
    @pl.when(is_owner)
    def _():
        for i in range(KX):
            tile = parent[:, i * 4 * KX : (i + 1) * 4 * KX]
            modes_ref[:, i, :] = modes_ref[:, i, :] + tile


def fetch_all(sems, pairs):
    copies = [pltpu.make_async_copy(a, b, sems.at[i]) for i, (a, b) in enumerate(pairs)]
    for copy in copies:
        copy.start()
    return copies


def slab_of(levels, c, level_count, level_total):
    return (c // level_count) * level_total + levels[c % level_count]


def first_kernel(n_gy, level_total, levels, owners, fields_all, parent_all, x_fwd_all, y_fwd_all,
                 modes, x_fwd, y_fwd, fields, parent, sems):
    gx, gy = lax.axis_index("gx"), lax.axis_index("gy")
    copies = fetch_all(sems, [
        (fields_all, fields), (x_fwd_all.at[gx], x_fwd), (y_fwd_all.at[gy], y_fwd),
        (parent_all.at[0, 0], parent)])
    for copy in copies[:3]:
        copy.wait()
    level_count = modes.shape[0] // 3
    emit_modes(
        lambda c: fields[slab_of(levels, c, level_count, level_total)], x_fwd[...], y_fwd[...],
        modes,
    )
    copies[3].wait()
    add_parent(parent, owners[0] == gx * n_gy + gy, modes)


def edge_kernel(fields, plume, west, east, cols):
    cells_x, cells_y = plume.shape[1:]
    field_rows = fields.shape[0]
    lane = lax.broadcasted_iota(jnp.int32, cols.shape, 1)
    acc = jnp.zeros(cols.shape, jnp.float32)
    for c in range(field_rows + plume.shape[0]):
        a = fields[c] if c < field_rows else plume[c - field_rows]
        west[c : c + 1, :] = a[:1]
        east[c : c + 1, :] = a[cells_x - 1 :]
        acc = jnp.where(lane // 2 == c, pltpu.roll(a, 2 * c + 1, 1), acc)
    cols[...] = acc


def share_kernel(n_gy, period, cuts, parts, out):
    count, rows, lanes = parts.shape
    me = lax.axis_index("gx") * n_gy + lax.axis_index("gy")
    total = parts[0]
    for p in range(1, count):
        total = total + parts[p]
    row = me * rows + lax.broadcasted_iota(jnp.int32, (rows, lanes), 0)
    lane = lax.broadcasted_iota(jnp.int32, (rows, lanes), 1)
    slab, pair = row // KX, row % KX
    r = 2 * pair + lane // (2 * KX)
    s = lane % (2 * KX)
    limit = jnp.zeros((rows, lanes), jnp.int32)
    for c in range(cuts.shape[0]):
        limit = jnp.where(slab == c, cuts[c], limit)
    keep = ((r % KX) < limit) & ((s % KX) < limit)
    factor = jnp.where(r == 0, 1.0, 2.0) * jnp.where(s == 0, 1.0, 2.0) * (1.0 / math.sqrt(period))
    result = jnp.where(keep, total * factor, 0.0)
    for p in range(count):
        out[p] = result


def step_kernel(n_gy, step, last, levels, owners, mismatch, fields, plume, source,
                west, east, south, north, x_back_all, y_back_all, *rest):
    gx, gy = lax.axis_index("gx"), lax.axis_index("gy")
    extra = []
    if last:
        fields_out, plume_out, x_back, y_back, slabs, beside, sems = rest
    else:
        (parent_all, x_fwd_all, y_fwd_all, fields_out, plume_out, modes,
         x_back, y_back, slabs, beside, sems, parent, x_fwd, y_fwd) = rest
        extra = [(x_fwd_all.at[gx], x_fwd), (y_fwd_all.at[gy], y_fwd),
                 (parent_all.at[0, step + 1], parent)]
    copies = fetch_all(
        sems, [(y_back_all.at[gy], y_back), (x_back_all.at[gx], x_back)] + extra)
    level_total, cells_x, cells_y = plume.shape
    field_rows = fields.shape[0]
    total = field_rows + level_total
    nudged = mismatch.shape[0] // KX
    level_count = nudged // 3
    inner = slice(PAD, PAD + cells_x)
    for c in range(total):
        slabs[c, inner] = fields[c] if c < field_rows else plume[c - field_rows]
        slabs[c, PAD - 1 : PAD] = west[c : c + 1, :]
        slabs[c, PAD + cells_x : PAD + cells_x + 1] = east[c : c + 1, :]
    beside[...] = jnp.zeros_like(beside)
    for copy in copies:
        copy.wait()
    back = data_dot(mismatch[...], y_back[...])
    x_table = x_back[...]
    for c in range(nudged):
        pair = back[c * KX : (c + 1) * KX]
        update = table_dot(
            x_table, jnp.concatenate([pair[:, : 2 * cells_y], pair[:, 2 * cells_y :]], axis=0))
        spot = slab_of(levels, c, level_count, level_total)
        slabs[spot, inner] += update[:cells_x, :cells_y]
        slabs[spot, PAD - 1 : PAD] += update[cells_x : cells_x + 1, :cells_y]
        slabs[spot, PAD + cells_x : PAD + cells_x + 1] += update[cells_x + 1 : cells_x + 2, :cells_y]
        beside[spot] = update[:cells_x, cells_y:]

    lane = lax.broadcasted_iota(jnp.int32, (cells_x, cells_y), 1)
    first, final = lane == 0, lane == cells_y - 1
    columns = jnp.where(
        lane % 2 == 0, pltpu.roll(north[...], cells_y - 1, 1), pltpu.roll(south[...], 1, 1))

    def advance(c, parts):
        centre, to_west, to_east, to_south, to_north = parts
        a = slabs[c, inner]
        column = pltpu.roll(columns, cells_y - 1 - 2 * c, 1)
        if c < field_rows:
            column = column + beside[c]
        return (
            centre * a
            + to_west * slabs[c, PAD - 1 : PAD - 1 + cells_x]
            + to_east * slabs[c, PAD + 1 : PAD + 1 + cells_x]
            + to_south * jnp.where(first, column, pltpu.roll(a, 1, 1))
            + to_north * jnp.where(final, column, pltpu.roll(a, cells_y - 1, 1))
        )

    for l in range(level_total):
        u, v = slabs[l, inner], slabs[level_total + l, inner]
        beside_parts = (
            0.1 + 0.1 * jnp.maximum(u, 0.0), 0.1 - 0.1 * jnp.minimum(u, 0.0),
            0.1 + 0.1 * jnp.maximum(v, 0.0), 0.1 - 0.1 * jnp.minimum(v, 0.0),
        )
        centre = 1.0 - (beside_parts[0] + beside_parts[1] + beside_parts[2] + beside_parts[3])
        for f in range(3):
            fields_out[f * level_total + l] = advance(
                f * level_total + l, (centre,) + beside_parts)
        settled = advance(field_rows + l, (centre - 0.3,) + beside_parts) + source[l]
        if l + 1 < level_total:
            settled = settled + 0.3 * plume[l + 1]
        plume_out[l] = settled

    if last:
        return
    emit_modes(
        lambda c: fields_out[slab_of(levels, c, level_count, level_total)], x_fwd[...], y_fwd[...],
        modes,
    )
    add_parent(parent, owners[step + 1] == gx * n_gy + gy, modes)


def swap_edges(west, east, cols):
    n_gx, n_gy = lax.axis_size("gx"), lax.axis_size("gy")
    up_x = [(i, i + 1) for i in range(n_gx - 1)]
    up_y = [(i, i + 1) for i in range(n_gy - 1)]
    down_x = [(b, a) for a, b in up_x]
    down_y = [(b, a) for a, b in up_y]
    return (
        lax.ppermute(east, "gx", up_x),
        lax.ppermute(west, "gx", down_x),
        lax.ppermute(cols, "gy", up_y),
        lax.ppermute(cols, "gy", down_y),
    )


def local(tables, fields, levels, cuts, parent_modes, owners, plume, source):
    n_gx, n_gy = lax.axis_size("gx"), lax.axis_size("gy")
    devices = n_gx * n_gy
    level_total, cells_x, cells_y = plume.shape
    period = n_gx * cells_x * n_gy * cells_y
    nudged = 3 * levels.shape[0]
    field_rows = 3 * level_total
    total = field_rows + level_total
    lanes = 4 * KX
    rows = nudged * KX // devices
    flat = fields.reshape(field_rows, cells_x, cells_y)
    cuts = cuts.reshape(-1)
    f32 = functools.partial(jax.ShapeDtypeStruct, dtype=jnp.float32)
    x_fwd, x_back, y_fwd, y_back = (jnp.asarray(t) for t in tables)

    def vmem(*shape):
        return pltpu.VMEM(shape, jnp.float32)

    def table_space(table):
        return pltpu.VMEM(table.shape[1:], table.dtype)

    def limit(mib):
        return pltpu.CompilerParams(vmem_limit_bytes=mib * 1024 * 1024)

    mode_shape = f32((nudged, KX, lanes))
    parent_space = vmem(nudged, 4 * KX * KX)
    step_scratch = [table_space(x_back), table_space(y_back),
                    vmem(total, cells_x + 2 * PAD, cells_y), vmem(field_rows, cells_x, cells_y),
                    pltpu.SemaphoreType.DMA((5,))]
    mode_scratch = [parent_space, table_space(x_fwd), table_space(y_fwd)]

    modes = pl.pallas_call(
        functools.partial(first_kernel, n_gy, level_total),
        out_shape=mode_shape,
        in_specs=[SMEM, SMEM] + [HBM] * 4,
        out_specs=VMEM,
        scratch_shapes=[table_space(x_fwd), table_space(y_fwd),
                        vmem(field_rows, cells_x, cells_y), parent_space,
                        pltpu.SemaphoreType.DMA((4,))],
        compiler_params=limit(FIRST_MIB),
        name="first_modes",
    )(levels, owners, flat, parent_modes, x_fwd, y_fwd)
    for step in range(STEPS):
        last = step == STEPS - 1
        edges = pl.pallas_call(
            edge_kernel,
            out_shape=[f32((total, cells_y)), f32((total, cells_y)), f32((cells_x, 2 * total))],
            in_specs=[VMEM, VMEM],
            out_specs=[VMEM] * 3,
            compiler_params=limit(8),
            name="edges",
        )(flat, plume)
        halo = swap_edges(*edges)
        parts = lax.all_to_all(modes.reshape(devices, rows, lanes), AXES, 0, 0, tiled=True)
        share = pl.pallas_call(
            functools.partial(share_kernel, n_gy, period),
            out_shape=f32((devices, rows, lanes)),
            in_specs=[SMEM, VMEM],
            out_specs=VMEM,
            compiler_params=limit(4),
            name="share_sum",
        )(cuts, parts)
        mismatch = lax.all_to_all(share, AXES, 0, 0, tiled=True)
        out_shape = [f32(flat.shape), f32(plume.shape)]
        operands = [levels, owners, mismatch.reshape(nudged * KX, lanes), flat, plume, source,
                    *halo, x_back, y_back]
        if not last:
            out_shape.append(mode_shape)
            operands += [parent_modes, x_fwd, y_fwd]
        results = pl.pallas_call(
            functools.partial(step_kernel, n_gy, step, last),
            out_shape=out_shape,
            in_specs=[SMEM, SMEM] + [VMEM] * 8 + [HBM] * (len(operands) - 10),
            out_specs=[VMEM] * len(out_shape),
            scratch_shapes=step_scratch + ([] if last else mode_scratch),
            compiler_params=limit(20),
            name="final_step" if last else "inner_step",
        )(*operands)
        if last:
            flat, plume = results
        else:
            flat, plume, modes = results
    return flat.reshape(fields.shape), plume


def solution(mesh):
    in_specs = (
        P(None, None, "gx", "gy"),
        P(),
        P(),
        P(("gx", "gy"), None, None, None),
        P(),
        P(None, "gx", "gy"),
        P(None, "gx", "gy"),
    )
    out_specs = (P(None, None, "gx", "gy"), P(None, "gx", "gy"))
    n_gx, n_gy = mesh.shape["gx"], mesh.shape["gy"]

    def whole(fields, levels, cuts, parent_modes, owners, plume, source):
        tables = build_tables(n_gx, n_gy, plume.shape[1] // n_gx, plume.shape[2] // n_gy)
        return jax.shard_map(
            functools.partial(local, tables), mesh=mesh, in_specs=in_specs, out_specs=out_specs,
            check_vma=False,
        )(fields, levels, cuts, parent_modes, owners, plume, source)

    return whole
```

time: 116 us -> 102 us (0.88)
  blocking collectives: 24.9 us -> 16.1 us
  Pallas kernels: 20.7 us -> 13.7 us
  local copies, waits for them, and re-layouts: 12.3 us -> 15.3 us
    all_to_all x1 -> x0, blocking collectives: 8.84 us -> none  [local(): lax.all_to_all(jnp.broadcast_to(share[None], (n_gy, rows, lanes)), 'gy',...]
    pallas_call x2, Pallas kernels: 13.9 us -> 7.02 us  [local(): pl.pallas_call(functools.partial(step_kernel, n_gy, step, last), out_shap...]
    all_to_all x1 -> x2, starting transfers between devices: 4.28 us -> 8.56 us  [local(): mismatch = lax.all_to_all(share, AXES, 0, 0, tiled=True)]
    all_to_all x1 -> x0, starting transfers between devices: 4.08 us -> none  [local(): lax.all_to_all(jnp.broadcast_to(line[None], (n_gx, n_gy * rows, lanes)),...]
    unnamed x60, local copies, waits for them, and re-layouts: 11.4 us -> 15.3 us
    pallas_call x3 -> x5, Pallas kernels: 6.85 us -> 6.64 us  [the longest x1 3.23 us: local(): pl.pallas_call(functools.partial(first_kernel, n_gy, level_total), out_sh...]
  transfers between devices with their start and end apart: 11 -> 11, of which waited for: 3 -> 3; matrix products, arithmetic and copies ran while one was open for 0% -> 0% of each run, Pallas kernels for 0% -> 1%
where the time goes in v3:
time: 102 us; the launch traced here: 101 us
  starting transfers between devices  39.2 us (38%)
  blocking collectives  16.1 us (16%)
  waiting for transfers between devices  15.8 us (15%)
  local copies, waits for them, and re-layouts  15.3 us (15%)
  Pallas kernels  13.7 us (13%)
    all_to_all x1, blocking collectives, local(): lax.all_to_all(modes.reshape(devices, rows, lanes), AXES, 0, 0, tiled=True)  16.1 us
    unnamed x60, local copies, waits for them, and re-layouts  15.3 us
    all_to_all x1, waiting for transfers between devices, local(): lax.all_to_all(modes.reshape(devices, rows, lanes), AXES, 0, 0, tiled=True)  11.3 us
    ppermute x2, starting transfers between devices, swap_edges(): lax.ppermute(west, 'gx', down_x)  8.81 us
    all_to_all x2, starting transfers between devices, local(): mismatch = lax.all_to_all(share, AXES, 0, 0, tiled=True)  8.56 us
    pallas_call x2, Pallas kernels, local(): pl.pallas_call(functools.partial(step_kernel, n_gy, step, last), out_shap...  7.02 us
    ppermute x2, starting transfers between devices, swap_edges(): lax.ppermute(cols, 'gy', up_y)  6.75 us
    all_to_all x1, starting transfers between devices, local(): lax.all_to_all(modes.reshape(devices, rows, lanes), AXES, 0, 0, tiled=True)  6 us
  transfers between devices with their start and end apart: 11, of which 3 were waited for; matrix products, arithmetic and copies ran while one was open for 0% of the time, Pallas kernels for 1%

profile of v3, /device:TPU:12, one launch (start us, length us, event | category | flops | bytes accessed | tf_op | source)
XLA Modules:
  0.0 101.0 jit_solution(13503827436592235829)
XLA Ops:
  0.6 3.2 %first_modes.1 = f32[24,32,128]{2,1,0:T(8,128)} custom-call(s32[8]{0:T(128)} %levels.5, s32[2]{0:T(128)} %owners.5, f32[48,32,128]{2,1,0:T(8,128)} %bitcast.6, f32[1,2,24,4096]{3,2,1,0:T(8,128)} %rest_0_.1, bf16[8,64,96]{2,1,0:T(8,128)(2,1)} %constant.8.clone.x_fwd_all.rest_1_, bf16[4,384,128]{2,1,0:T(8,128)(2,1)} %constant.10.clone.y_fwd_all.rest_2_), custom_call_target="tpu_custom_call" | custom-call | tf_op jit(solution)/shard_map/first_modes/pallas_call | solution.py:294
  3.9 6.0 %all-to-all-start = ((f32[32,24,128]{2,1,0:T(8,128)}), f32[32,24,128]{2,1,0:T(8,128)S(1)}, u32[]{:S(2)}, u32[]{:S(2)}) async-start(f32[32,24,128]{2,1,0:T(8,128)} %bitcast.12), calls=%async_computation | async-start | bytes 786432 | tf_op jit(solution)/shard_map/all_to_all | solution.py:316
  10.0 11.3 %all-to-all-done.parts = f32[32,24,128]{2,1,0:T(8,128)S(1)} async-done(((f32[32,24,128]{2,1,0:T(8,128)}), f32[32,24,128]{2,1,0:T(8,128)S(1)}, u32[]{:S(2)}, u32[]{:S(2)}) %all-to-all-start) | async-done | bytes 393248 | tf_op jit(solution)/shard_map/all_to_all | solution.py:316
  21.3 1.4 %share_sum.2 = f32[32,24,128]{2,1,0:T(8,128)} custom-call(s32[24]{0:T(128)S(1)} %reshape.25.cuts, f32[32,24,128]{2,1,0:T(8,128)S(1)} %all-to-all-done.parts), custom_call_target="tpu_custom_call" | custom-call | tf_op jit(solution)/shard_map/share_sum/pallas_call | solution.py:317
  22.7 4.3 %all-to-all-start.1 = ((f32[32,24,128]{2,1,0:T(8,128)}), f32[32,24,128]{2,1,0:T(8,128)S(1)}, u32[]{:S(2)}, u32[]{:S(2)}) async-start(f32[32,24,128]{2,1,0:T(8,128)} %share_sum.2), calls=%async_computation.1 | async-start | bytes 786432 | tf_op jit(solution)/shard_map/all_to_all | solution.py:325
  27.0 0.9 copy-done.8
  28.3 2.1 %collective-permute-start = (f32[64,128]{1,0:T(8,128)S(1)}, f32[64,128]{1,0:T(8,128)S(1)}, u32[]{:S(2)}, u32[]{:S(2)}) collective-permute-start(f32[64,128]{1,0:T(8,128)S(1)} %get-tuple-element.13), channel_id=1, source_target_pairs={{0,4},{4,8},{8,12},{12,16},{16,20},{20,24},{24,28},{1,5},{5,9},{9,... | collective-permute-start | bytes 98312 | tf_op jit(solution)/shard_map/ppermute | solution.py:256
  30.3 4.4 %collective-permute-start.1 = (f32[64,128]{1,0:T(8,128)S(1)}, f32[64,128]{1,0:T(8,128)S(1)}, u32[]{:S(2)}, u32[]{:S(2)}) collective-permute-start(f32[64,128]{1,0:T(8,128)S(1)} %get-tuple-element.14), channel_id=1, source_target_pairs={{4,0},{8,4},{12,8},{16,12},{20,16},{24,20},{28,24},{5,1},{9,5},{13... | collective-permute-start | bytes 98312 | tf_op jit(solution)/shard_map/ppermute | solution.py:257
  34.8 2.5 %collective-permute-start.3 = (f32[32,128]{1,0:T(8,128)S(1)}, f32[32,128]{1,0:T(8,128)S(1)}, u32[]{:S(2)}, u32[]{:S(2)}) collective-permute-start(f32[32,128]{1,0:T(8,128)S(1)} %get-tuple-element.15), channel_id=1, source_target_pairs={{1,0},{2,1},{3,2},{5,4},{6,5},{7,6},{9,8},{10,9},{11,10},{13,12},{... | collective-permute-start | bytes 49160 | tf_op jit(solution)/shard_map/ppermute | solution.py:259
  37.2 3.4 %collective-permute-start.2 = (f32[32,128]{1,0:T(8,128)S(1)}, f32[32,128]{1,0:T(8,128)S(1)}, u32[]{:S(2)}, u32[]{:S(2)}) collective-permute-start(f32[32,128]{1,0:T(8,128)S(1)} %get-tuple-element.15), channel_id=1, source_target_pairs={{0,1},{1,2},{2,3},{4,5},{5,6},{6,7},{8,9},{9,10},{10,11},{12,13},{... | collective-permute-start | bytes 49160 | tf_op jit(solution)/shard_map/ppermute | solution.py:258
  40.6 2.2 %collective-permute-done.2.south = f32[32,128]{1,0:T(8,128)S(1)} collective-permute-done((f32[32,128]{1,0:T(8,128)S(1)}, f32[32,128]{1,0:T(8,128)S(1)}, u32[]{:S(2)}, u32[]{:S(2)}) %collective-permute-start.2) | collective-permute-done | bytes 16416 | tf_op jit(solution)/shard_map/ppermute | solution.py:258
  44.7 1.0 copy-done.5
  45.7 0.9 copy-done.9
  46.7 0.9 copy-done.10
  47.6 0.9 copy-done.12
  48.5 0.9 copy-done.14
  49.4 0.8 copy-done.16
  50.2 0.8 copy-done.18
  51.0 0.7 copy-done.22
  53.0 3.5 %inner_step.1 = (f32[48,32,128]{2,1,0:T(8,128)S(1)}, f32[16,32,128]{2,1,0:T(8,128)S(1)}, f32[24,32,128]{2,1,0:T(8,128)S(1)}) custom-call(s32[8]{0:T(128)S(1)} %copy-done.25, s32[2]{0:T(128)S(1)} %copy-done.27, f32[768,128]{1,0:T(8,128)S(1)} %bitcast.10, f32[48,32,128]{2,1,0:T(8,128)S(1)} %bitcast.8, f32[16,32,128]{2,1,0:T(8,128)S(1)} %copy-done.9, ...), custom_call_target="tpu_custom_call" | custom-call | tf_op jit(solution)/shard_map/inner_step/pallas_call | solution.py:332
  56.5 0.9 copy-done.3
  57.3 0.7 copy-done.6
  58.1 16.1 %all_to_all.20.parts = f32[32,24,128]{2,1,0:T(8,128)S(1)} all-to-all(f32[32,24,128]{2,1,0:T(8,128)S(1)} %bitcast.11), channel_id=1, replica_groups=mesh['gx'=8,'gy'=4] {'gx','gy'}, dimensions={0} | all-to-all | bytes 786432 | tf_op jit(solution)/shard_map/all_to_all | solution.py:316
  74.1 1.4 %share_sum.3 = f32[32,24,128]{2,1,0:T(8,128)} custom-call(s32[24]{0:T(128)S(1)} %copy-done.24, f32[32,24,128]{2,1,0:T(8,128)S(1)} %all_to_all.20.parts), custom_call_target="tpu_custom_call" | custom-call | tf_op jit(solution)/shard_map/share_sum/pallas_call | solution.py:317
  75.5 4.3 %all-to-all-start.3 = ((f32[32,24,128]{2,1,0:T(8,128)}), f32[32,24,128]{2,1,0:T(8,128)S(1)}, u32[]{:S(2)}, u32[]{:S(2)}) async-start(f32[32,24,128]{2,1,0:T(8,128)} %share_sum.3), calls=%async_computation.3 | async-start | bytes 786432 | tf_op jit(solution)/shard_map/all_to_all | solution.py:325
  80.2 2.1 %collective-permute-start.4 = (f32[64,128]{1,0:T(8,128)S(1)}, f32[64,128]{1,0:T(8,128)S(1)}, u32[]{:S(2)}, u32[]{:S(2)}) collective-permute-start(f32[64,128]{1,0:T(8,128)S(1)} %get-tuple-element.19), channel_id=1, source_target_pairs={{0,4},{4,8},{8,12},{12,16},{16,20},{20,24},{24,28},{1,5},{5,9},{9,... | collective-permute-start | bytes 98312 | tf_op jit(solution)/shard_map/ppermute | solution.py:256
  82.2 4.4 %collective-permute-start.5 = (f32[64,128]{1,0:T(8,128)S(1)}, f32[64,128]{1,0:T(8,128)S(1)}, u32[]{:S(2)}, u32[]{:S(2)}) collective-permute-start(f32[64,128]{1,0:T(8,128)S(1)} %get-tuple-element.20), channel_id=1, source_target_pairs={{4,0},{8,4},{12,8},{16,12},{20,16},{24,20},{28,24},{5,1},{9,5},{13... | collective-permute-start | bytes 98312 | tf_op jit(solution)/shard_map/ppermute | solution.py:257
  86.6 2.5 %collective-permute-start.7 = (f32[32,128]{1,0:T(8,128)S(1)}, f32[32,128]{1,0:T(8,128)S(1)}, u32[]{:S(2)}, u32[]{:S(2)}) collective-permute-start(f32[32,128]{1,0:T(8,128)S(1)} %get-tuple-element.21), channel_id=1, source_target_pairs={{1,0},{2,1},{3,2},{5,4},{6,5},{7,6},{9,8},{10,9},{11,10},{13,12},{... | collective-permute-start | bytes 49160 | tf_op jit(solution)/shard_map/ppermute | solution.py:259
  89.1 3.4 %collective-permute-start.6 = (f32[32,128]{1,0:T(8,128)S(1)}, f32[32,128]{1,0:T(8,128)S(1)}, u32[]{:S(2)}, u32[]{:S(2)}) collective-permute-start(f32[32,128]{1,0:T(8,128)S(1)} %get-tuple-element.21), channel_id=1, source_target_pairs={{0,1},{1,2},{2,3},{4,5},{5,6},{6,7},{8,9},{9,10},{10,11},{12,13},{... | collective-permute-start | bytes 49160 | tf_op jit(solution)/shard_map/ppermute | solution.py:258
  92.5 2.2 %collective-permute-done.6.south = f32[32,128]{1,0:T(8,128)S(1)} collective-permute-done((f32[32,128]{1,0:T(8,128)S(1)}, f32[32,128]{1,0:T(8,128)S(1)}, u32[]{:S(2)}, u32[]{:S(2)}) %collective-permute-start.6) | collective-permute-done | bytes 16416 | tf_op jit(solution)/shard_map/ppermute | solution.py:258
  95.4 0.7 copy-done.20
  97.4 3.6 %final_step.1 = (f32[48,32,128]{2,1,0:T(8,128)}, f32[16,32,128]{2,1,0:T(8,128)}) custom-call(s32[8]{0:T(128)S(1)} %copy-done.26, s32[2]{0:T(128)S(1)} %copy-done.28, f32[768,128]{1,0:T(8,128)S(1)} %bitcast.9, f32[48,32,128]{2,1,0:T(8,128)S(1)} %copy-done.4, f32[16,32,128]{2,1,0:T(8,128)S(1)} %copy-done.7, f32[16,32,128]{2,1,0:T(8,128)S(1)} %copy-done.11, ...), custom_call_target="tpu_custom_call" | custom-call | tf_op jit(solution)/shard_map/final_step/pallas_call | solution.py:332
  (59 shorter events, 5.9 us)
Async XLA Ops:
  0.6 9.3 %copy-start.29 = (s32[3,8]{1,0:T(4,128)S(1)}, s32[3,8]{1,0:T(4,128)}, u32[]{:S(2)}) copy-start(s32[3,8]{1,0:T(4,128)} %param.13) | copy-start | bytes 292
  3.9 23.1 %copy-start = (f32[3,16,32,128]{3,2,1,0:T(8,128)S(1)}, f32[3,16,32,128]{3,2,1,0:T(8,128)}, u32[]{:S(2)}) copy-start(f32[3,16,32,128]{3,2,1,0:T(8,128)} %param.11) | copy-start | bytes 2359300
  3.9 40.8 %copy-start.1 = (bf16[4,384,512]{2,1,0:T(8,128)(2,1)S(1)}, bf16[4,384,512]{2,1,0:T(8,128)(2,1)}, u32[]{:S(2)}) copy-start(bf16[4,384,512]{2,1,0:T(8,128)(2,1)} %constant.11.clone.y_back_all) | copy-start | bytes 4718596
  3.9 40.8 %copy-start.2 = (f32[1,2,24,4096]{3,2,1,0:T(8,128)S(1)}, f32[1,2,24,4096]{3,2,1,0:T(8,128)}, u32[]{:S(2)}) copy-start(f32[1,2,24,4096]{3,2,1,0:T(8,128)} %rest_0_.1) | copy-start | bytes 2359300
  3.9 17.4 %all-to-all-start = ((f32[32,24,128]{2,1,0:T(8,128)}), f32[32,24,128]{2,1,0:T(8,128)S(1)}, u32[]{:S(2)}, u32[]{:S(2)}) async-start(f32[32,24,128]{2,1,0:T(8,128)} %bitcast.12), calls=%async_computation | async-start | bytes 786432 | tf_op jit(solution)/shard_map/all_to_all | solution.py:316
  10.0 24.7 %copy-start.23 = (s32[24]{0:T(128)}, s32[24]{0:T(128)S(1)}, u32[]{:S(2)}) copy-start(s32[24]{0:T(128)S(1)} %reshape.25.cuts) | copy-start | bytes 292
  22.7 22.0 %all-to-all-start.1 = ((f32[32,24,128]{2,1,0:T(8,128)}), f32[32,24,128]{2,1,0:T(8,128)S(1)}, u32[]{:S(2)}, u32[]{:S(2)}) async-start(f32[32,24,128]{2,1,0:T(8,128)} %share_sum.2), calls=%async_computation.1 | async-start | bytes 786432 | tf_op jit(solution)/shard_map/all_to_all | solution.py:325
  27.0 1.0 copy-start.8
  28.3 15.2 %collective-permute-start = (f32[64,128]{1,0:T(8,128)S(1)}, f32[64,128]{1,0:T(8,128)S(1)}, u32[]{:S(2)}, u32[]{:S(2)}) collective-permute-start(f32[64,128]{1,0:T(8,128)S(1)} %get-tuple-element.13), channel_id=1, source_target_pairs={{0,4},{4,8},{8,12},{12,16},{16,20},{20,24},{24,28},{1,5},{5,9},{9,... | collective-permute-start | bytes 98312 | tf_op jit(solution)/shard_map/ppermute | solution.py:256
  30.3 13.7 %collective-permute-start.1 = (f32[64,128]{1,0:T(8,128)S(1)}, f32[64,128]{1,0:T(8,128)S(1)}, u32[]{:S(2)}, u32[]{:S(2)}) collective-permute-start(f32[64,128]{1,0:T(8,128)S(1)} %get-tuple-element.14), channel_id=1, source_target_pairs={{4,0},{8,4},{12,8},{16,12},{20,16},{24,20},{28,24},{5,1},{9,5},{13... | collective-permute-start | bytes 98312 | tf_op jit(solution)/shard_map/ppermute | solution.py:257
  34.8 5.9 %collective-permute-start.3 = (f32[32,128]{1,0:T(8,128)S(1)}, f32[32,128]{1,0:T(8,128)S(1)}, u32[]{:S(2)}, u32[]{:S(2)}) collective-permute-start(f32[32,128]{1,0:T(8,128)S(1)} %get-tuple-element.15), channel_id=1, source_target_pairs={{1,0},{2,1},{3,2},{5,4},{6,5},{7,6},{9,8},{10,9},{11,10},{13,12},{... | collective-permute-start | bytes 49160 | tf_op jit(solution)/shard_map/ppermute | solution.py:259
  37.2 5.6 %collective-permute-start.2 = (f32[32,128]{1,0:T(8,128)S(1)}, f32[32,128]{1,0:T(8,128)S(1)}, u32[]{:S(2)}, u32[]{:S(2)}) collective-permute-start(f32[32,128]{1,0:T(8,128)S(1)} %get-tuple-element.15), channel_id=1, source_target_pairs={{0,1},{1,2},{2,3},{4,5},{5,6},{6,7},{8,9},{9,10},{10,11},{12,13},{... | collective-permute-start | bytes 49160 | tf_op jit(solution)/shard_map/ppermute | solution.py:258
  44.7 1.0 copy-start.5
  45.7 0.9 copy-start.9
  46.7 0.9 copy-start.10
  47.6 0.9 copy-start.12
  48.5 0.9 copy-start.14
  49.4 0.8 copy-start.16
  50.2 0.8 copy-start.18
  51.0 0.7 copy-start.22
  53.0 21.2 %copy-start.24 = (s32[24]{0:T(128)S(1)}, s32[24]{0:T(128)}, u32[]{:S(2)}) copy-start(s32[24]{0:T(128)} %copy-done.23) | copy-start | bytes 292
  56.5 0.9 copy-start.3
  58.0 21.8 %copy-start.4 = (f32[48,32,128]{2,1,0:T(8,128)S(1)}, f32[48,32,128]{2,1,0:T(8,128)}, u32[]{:S(2)}) copy-start(f32[48,32,128]{2,1,0:T(8,128)} %copy-done.3) | copy-start | bytes 2359300
  58.1 21.8 %copy-start.7 = (f32[16,32,128]{2,1,0:T(8,128)S(1)}, f32[16,32,128]{2,1,0:T(8,128)}, u32[]{:S(2)}) copy-start(f32[16,32,128]{2,1,0:T(8,128)} %copy-done.6) | copy-start | bytes 786436
  58.1 37.3 %copy-start.11 = (f32[16,32,128]{2,1,0:T(8,128)S(1)}, f32[16,32,128]{2,1,0:T(8,128)}, u32[]{:S(2)}) copy-start(f32[16,32,128]{2,1,0:T(8,128)} %source.3) | copy-start | bytes 786436
  58.1 37.3 %copy-start.13 = (bf16[8,48,192]{2,1,0:T(8,128)(2,1)S(1)}, bf16[8,48,192]{2,1,0:T(8,128)(2,1)}, u32[]{:S(2)}) copy-start(bf16[8,48,192]{2,1,0:T(8,128)(2,1)} %constant.9.clone.x_back_all) | copy-start | bytes 442372
  75.5 19.8 %all-to-all-start.3 = ((f32[32,24,128]{2,1,0:T(8,128)}), f32[32,24,128]{2,1,0:T(8,128)S(1)}, u32[]{:S(2)}, u32[]{:S(2)}) async-start(f32[32,24,128]{2,1,0:T(8,128)} %share_sum.3), calls=%async_computation.3 | async-start | bytes 786432 | tf_op jit(solution)/shard_map/all_to_all | solution.py:325
  80.2 15.2 %collective-permute-start.4 = (f32[64,128]{1,0:T(8,128)S(1)}, f32[64,128]{1,0:T(8,128)S(1)}, u32[]{:S(2)}, u32[]{:S(2)}) collective-permute-start(f32[64,128]{1,0:T(8,128)S(1)} %get-tuple-element.19), channel_id=1, source_target_pairs={{0,4},{4,8},{8,12},{12,16},{16,20},{20,24},{24,28},{1,5},{5,9},{9,... | collective-permute-start | bytes 98312 | tf_op jit(solution)/shard_map/ppermute | solution.py:256
  82.2 13.1 %collective-permute-start.5 = (f32[64,128]{1,0:T(8,128)S(1)}, f32[64,128]{1,0:T(8,128)S(1)}, u32[]{:S(2)}, u32[]{:S(2)}) collective-permute-start(f32[64,128]{1,0:T(8,128)S(1)} %get-tuple-element.20), channel_id=1, source_target_pairs={{4,0},{8,4},{12,8},{16,12},{20,16},{24,20},{28,24},{5,1},{9,5},{13... | collective-permute-start | bytes 98312 | tf_op jit(solution)/shard_map/ppermute | solution.py:257
  86.6 5.9 %collective-permute-start.7 = (f32[32,128]{1,0:T(8,128)S(1)}, f32[32,128]{1,0:T(8,128)S(1)}, u32[]{:S(2)}, u32[]{:S(2)}) collective-permute-start(f32[32,128]{1,0:T(8,128)S(1)} %get-tuple-element.21), channel_id=1, source_target_pairs={{1,0},{2,1},{3,2},{5,4},{6,5},{7,6},{9,8},{10,9},{11,10},{13,12},{... | collective-permute-start | bytes 49160 | tf_op jit(solution)/shard_map/ppermute | solution.py:259
  89.1 5.6 %collective-permute-start.6 = (f32[32,128]{1,0:T(8,128)S(1)}, f32[32,128]{1,0:T(8,128)S(1)}, u32[]{:S(2)}, u32[]{:S(2)}) collective-permute-start(f32[32,128]{1,0:T(8,128)S(1)} %get-tuple-element.21), channel_id=1, source_target_pairs={{0,1},{1,2},{2,3},{4,5},{5,6},{6,7},{8,9},{9,10},{10,11},{12,13},{... | collective-permute-start | bytes 49160 | tf_op jit(solution)/shard_map/ppermute | solution.py:258
  95.4 0.7 copy-start.20
  (9 other events, 5.7 us)

commit v4 on v3

--- a/solution.py
+++ b/solution.py
@@ -12,12 +12,15 @@
 
 KX = 32
 STEPS = 2
-FIRST_MIB = 60
 PAD = 8
 VMEM = pl.BlockSpec(memory_space=pltpu.VMEM)
 SMEM = pl.BlockSpec(memory_space=pltpu.SMEM)
 HBM = pl.BlockSpec(memory_space=pltpu.HBM)
 AXES = ("gx", "gy")
+
+
+def in_hbm(array):
+    return pltpu.with_memory_space_constraint(array, pltpu.HBM)
 
 
 def wave_table(positions, period):
@@ -299,9 +302,9 @@
         scratch_shapes=[table_space(x_fwd), table_space(y_fwd),
                         vmem(field_rows, cells_x, cells_y), parent_space,
                         pltpu.SemaphoreType.DMA((4,))],
-        compiler_params=limit(FIRST_MIB),
+        compiler_params=limit(8),
         name="first_modes",
-    )(levels, owners, flat, parent_modes, x_fwd, y_fwd)
+    )(levels, owners, in_hbm(flat), in_hbm(parent_modes), in_hbm(x_fwd), in_hbm(y_fwd))
     for step in range(STEPS):
         last = step == STEPS - 1
         edges = pl.pallas_call(
@@ -314,6 +317,7 @@
         )(flat, plume)
         halo = swap_edges(*edges)
         parts = lax.all_to_all(modes.reshape(devices, rows, lanes), AXES, 0, 0, tiled=True)
+        parts, *halo = lax.optimization_barrier((parts, *halo))
         share = pl.pallas_call(
             functools.partial(share_kernel, n_gy, period),
             out_shape=f32((devices, rows, lanes)),
@@ -325,10 +329,10 @@
         mismatch = lax.all_to_all(share, AXES, 0, 0, tiled=True)
         out_shape = [f32(flat.shape), f32(plume.shape)]
         operands = [levels, owners, mismatch.reshape(nudged * KX, lanes), flat, plume, source,
-                    *halo, x_back, y_back]
+                    *halo, in_hbm(x_back), in_hbm(y_back)]
         if not last:
             out_shape.append(mode_shape)
-            operands += [parent_modes, x_fwd, y_fwd]
+            operands += [in_hbm(parent_modes), in_hbm(x_fwd), in_hbm(y_fwd)]
         results = pl.pallas_call(
             functools.partial(step_kernel, n_gy, step, last),
             out_shape=out_shape,

time: 102 us -> 90.4 us (0.89)
  the two profiles are of different devices: /device:TPU:12 before, /device:TPU:0 now
where the time goes in v4:
time: 90.4 us; the launch traced here: 89.2 us
  blocking collectives  39.2 us (43%)
  starting transfers between devices  29.7 us (33%)
  Pallas kernels  13.7 us (15%)
  waiting for transfers between devices  4.24 us (5%)
  local copies, waits for them, and re-layouts  1.42 us (2%)
    all_to_all x2, blocking collectives, local(): mismatch = lax.all_to_all(share, AXES, 0, 0, tiled=True)  39.2 us
    all_to_all x2, starting transfers between devices, local(): lax.all_to_all(modes.reshape(devices, rows, lanes), AXES, 0, 0, tiled=True)  11.2 us
    ppermute x2, starting transfers between devices, swap_edges(): lax.ppermute(cols, 'gy', up_y)  9.09 us
    pallas_call x2, Pallas kernels, local(): pl.pallas_call(functools.partial(step_kernel, n_gy, step, last), out_shap...  8.84 us
    ppermute x2, starting transfers between devices, swap_edges(): lax.ppermute(east, 'gx', up_x)  4.31 us
    pallas_call x1, Pallas kernels, local(): pl.pallas_call(functools.partial(first_kernel, n_gy, level_total), out_sh...  2.97 us
    ppermute x2, waiting for transfers between devices, swap_edges(): lax.ppermute(cols, 'gy', up_y)  2.74 us
    ppermute x2, starting transfers between devices, swap_edges(): lax.ppermute(west, 'gx', down_x)  2.58 us
  transfers between devices with their start and end apart: 10, of which 4 were waited for; matrix products, arithmetic and copies ran while one was open for 0% of the time, Pallas kernels for 1%

profile of v4, /device:TPU:0, one launch (start us, length us, event | category | flops | bytes accessed | tf_op | source)
XLA Modules:
  0.0 89.2 jit_solution(894135045377646787)
XLA Ops:
  0.6 0.0 copy-start.3
  0.6 0.6 copy-done.3
  1.3 0.7 copy-done.5
  2.0 3.0 %first_modes.1 = f32[24,32,128]{2,1,0:T(8,128)} custom-call(s32[8]{0:T(128)S(1)} %copy-done.3, s32[2]{0:T(128)S(1)} %copy-done.5, f32[48,32,128]{2,1,0:T(8,128)} %bitcast.6, f32[1,2,24,4096]{3,2,1,0:T(8,128)} %rest_0_.1, bf16[8,64,96]{2,1,0:T(8,128)(2,1)} %constant.8.clone.x_fwd_all.rest_1_, bf16[4,384,128]{2,1,0:T(8,128)(2,1)} %constant.10.clone.y_fwd_all.rest_2_), custom_call_target="tpu_custom_call" | custom-call | tf_op jit(solution)/shard_map/first_modes/pallas_call | solution.py:297
  4.9 0.0 copy-start.2
  4.9 0.0 copy-start.4
  5.0 0.0 copy-start.6
  5.0 7.3 %all-to-all-start = ((f32[32,24,128]{2,1,0:T(8,128)}), f32[32,24,128]{2,1,0:T(8,128)S(1)}, u32[]{:S(2)}, u32[]{:S(2)}) async-start(f32[32,24,128]{2,1,0:T(8,128)} %bitcast.1), calls=%async_computation | async-start | bytes 786432 | tf_op jit(solution)/shard_map/all_to_all | solution.py:319
  12.3 0.3 edges.2
  12.6 2.2 %collective-permute-start = (f32[64,128]{1,0:T(8,128)S(1)}, f32[64,128]{1,0:T(8,128)S(1)}, u32[]{:S(2)}, u32[]{:S(2)}) collective-permute-start(f32[64,128]{1,0:T(8,128)S(1)} %get-tuple-element.23), channel_id=1, source_target_pairs={{0,4},{4,8},{8,12},{12,16},{16,20},{20,24},{24,28},{1,5},{5,9},{9,... | collective-permute-start | bytes 98312 | tf_op jit(solution)/shard_map/ppermute | solution.py:259
  14.8 1.3 %collective-permute-start.1 = (f32[64,128]{1,0:T(8,128)S(1)}, f32[64,128]{1,0:T(8,128)S(1)}, u32[]{:S(2)}, u32[]{:S(2)}) collective-permute-start(f32[64,128]{1,0:T(8,128)S(1)} %get-tuple-element.24), channel_id=1, source_target_pairs={{4,0},{8,4},{12,8},{16,12},{20,16},{24,20},{28,24},{5,1},{9,5},{13... | collective-permute-start | bytes 98312 | tf_op jit(solution)/shard_map/ppermute | solution.py:260
  16.1 1.3 %collective-permute-start.3 = (f32[32,128]{1,0:T(8,128)S(1)}, f32[32,128]{1,0:T(8,128)S(1)}, u32[]{:S(2)}, u32[]{:S(2)}) collective-permute-start(f32[32,128]{1,0:T(8,128)S(1)} %get-tuple-element.25), channel_id=1, source_target_pairs={{1,0},{2,1},{3,2},{5,4},{6,5},{7,6},{9,8},{10,9},{11,10},{13,12},{... | collective-permute-start | bytes 49160 | tf_op jit(solution)/shard_map/ppermute | solution.py:262
  17.4 4.5 %collective-permute-start.2 = (f32[32,128]{1,0:T(8,128)S(1)}, f32[32,128]{1,0:T(8,128)S(1)}, u32[]{:S(2)}, u32[]{:S(2)}) collective-permute-start(f32[32,128]{1,0:T(8,128)S(1)} %get-tuple-element.25), channel_id=1, source_target_pairs={{0,1},{1,2},{2,3},{4,5},{5,6},{6,7},{8,9},{9,10},{10,11},{12,13},{... | collective-permute-start | bytes 49160 | tf_op jit(solution)/shard_map/ppermute | solution.py:261
  22.0 0.1 reshape.25.cuts
  22.0 1.3 %collective-permute-done.2.south = f32[32,128]{1,0:T(8,128)S(1)} collective-permute-done((f32[32,128]{1,0:T(8,128)S(1)}, f32[32,128]{1,0:T(8,128)S(1)}, u32[]{:S(2)}, u32[]{:S(2)}) %collective-permute-start.2) | collective-permute-done | bytes 16416 | tf_op jit(solution)/shard_map/ppermute | solution.py:261
  23.4 0.0 collective-permute-done.1.east
  23.4 0.7 all-to-all-done.parts
  24.1 0.6 share_sum.2
  24.7 19.6 %all_to_all.20 = f32[32,24,128]{2,1,0:T(8,128)S(1)} all-to-all(f32[32,24,128]{2,1,0:T(8,128)S(1)} %share_sum.2), channel_id=1, replica_groups=mesh['gx'=8,'gy'=4] {'gx','gy'}, dimensions={0} | all-to-all | bytes 786432 | tf_op jit(solution)/shard_map/all_to_all | solution.py:329
  44.4 4.7 %inner_step.1 = (f32[48,32,128]{2,1,0:T(8,128)S(1)}, f32[16,32,128]{2,1,0:T(8,128)S(1)}, f32[24,32,128]{2,1,0:T(8,128)}) custom-call(s32[8]{0:T(128)S(1)} %copy-done.4, s32[2]{0:T(128)S(1)} %copy-done.6, f32[768,128]{1,0:T(8,128)S(1)} %bitcast.10, f32[48,32,128]{2,1,0:T(8,128)S(1)} %bitcast.8, f32[16,32,128]{2,1,0:T(8,128)S(1)} %copy-done.1, ...), custom_call_target="tpu_custom_call" | custom-call | tf_op jit(solution)/shard_map/inner_step/pallas_call | solution.py:336
  49.0 3.9 %all-to-all-start.2 = ((f32[32,24,128]{2,1,0:T(8,128)}), f32[32,24,128]{2,1,0:T(8,128)S(1)}, u32[]{:S(2)}, u32[]{:S(2)}) async-start(f32[32,24,128]{2,1,0:T(8,128)} %bitcast.3), calls=%async_computation.2 | async-start | bytes 786432 | tf_op jit(solution)/shard_map/all_to_all | solution.py:319
  52.9 0.3 edges.3
  53.2 2.2 %collective-permute-start.4 = (f32[64,128]{1,0:T(8,128)S(1)}, f32[64,128]{1,0:T(8,128)S(1)}, u32[]{:S(2)}, u32[]{:S(2)}) collective-permute-start(f32[64,128]{1,0:T(8,128)S(1)} %get-tuple-element.34), channel_id=1, source_target_pairs={{0,4},{4,8},{8,12},{12,16},{16,20},{20,24},{24,28},{1,5},{5,9},{9,... | collective-permute-start | bytes 98312 | tf_op jit(solution)/shard_map/ppermute | solution.py:259
  55.4 1.3 %collective-permute-start.5 = (f32[64,128]{1,0:T(8,128)S(1)}, f32[64,128]{1,0:T(8,128)S(1)}, u32[]{:S(2)}, u32[]{:S(2)}) collective-permute-start(f32[64,128]{1,0:T(8,128)S(1)} %get-tuple-element.35), channel_id=1, source_target_pairs={{4,0},{8,4},{12,8},{16,12},{20,16},{24,20},{28,24},{5,1},{9,5},{13... | collective-permute-start | bytes 98312 | tf_op jit(solution)/shard_map/ppermute | solution.py:260
  56.7 1.3 %collective-permute-start.7 = (f32[32,128]{1,0:T(8,128)S(1)}, f32[32,128]{1,0:T(8,128)S(1)}, u32[]{:S(2)}, u32[]{:S(2)}) collective-permute-start(f32[32,128]{1,0:T(8,128)S(1)} %get-tuple-element.36), channel_id=1, source_target_pairs={{1,0},{2,1},{3,2},{5,4},{6,5},{7,6},{9,8},{10,9},{11,10},{13,12},{... | collective-permute-start | bytes 49160 | tf_op jit(solution)/shard_map/ppermute | solution.py:262
  58.0 4.5 %collective-permute-start.6 = (f32[32,128]{1,0:T(8,128)S(1)}, f32[32,128]{1,0:T(8,128)S(1)}, u32[]{:S(2)}, u32[]{:S(2)}) collective-permute-start(f32[32,128]{1,0:T(8,128)S(1)} %get-tuple-element.36), channel_id=1, source_target_pairs={{0,1},{1,2},{2,3},{4,5},{5,6},{6,7},{8,9},{9,10},{10,11},{12,13},{... | collective-permute-start | bytes 49160 | tf_op jit(solution)/shard_map/ppermute | solution.py:261
  62.6 0.0 collective-permute-done.7.north
  62.6 1.4 %collective-permute-done.6.south = f32[32,128]{1,0:T(8,128)S(1)} collective-permute-done((f32[32,128]{1,0:T(8,128)S(1)}, f32[32,128]{1,0:T(8,128)S(1)}, u32[]{:S(2)}, u32[]{:S(2)}) %collective-permute-start.6) | collective-permute-done | bytes 16416 | tf_op jit(solution)/shard_map/ppermute | solution.py:261
  64.0 0.8 all-to-all-done.2.parts
  64.7 0.6 share_sum.3
  65.4 19.6 %all_to_all.21 = f32[32,24,128]{2,1,0:T(8,128)S(1)} all-to-all(f32[32,24,128]{2,1,0:T(8,128)S(1)} %share_sum.3), channel_id=1, replica_groups=mesh['gx'=8,'gy'=4] {'gx','gy'}, dimensions={0} | all-to-all | bytes 786432 | tf_op jit(solution)/shard_map/all_to_all | solution.py:329
  85.0 4.2 %final_step.1 = (f32[48,32,128]{2,1,0:T(8,128)}, f32[16,32,128]{2,1,0:T(8,128)}) custom-call(s32[8]{0:T(128)S(1)} %copy-done.4, s32[2]{0:T(128)S(1)} %copy-done.6, f32[768,128]{1,0:T(8,128)S(1)} %bitcast.9, f32[48,32,128]{2,1,0:T(8,128)S(1)} %get-tuple-element.32.fields, f32[16,32,128]{2,1,0:T(8,128)S(1)} %get-tuple-element.33.plume, ...), custom_call_target="tpu_custom_call" | custom-call | tf_op jit(solution)/shard_map/final_step/pallas_call | solution.py:336
  (14 shorter events, 0.0 us)
Async XLA Ops:
  0.6 0.7 copy-start.3
  1.3 0.7 copy-start.5
  1.9 10.3 %copy-start = (f32[3,16,32,128]{3,2,1,0:T(8,128)S(1)}, f32[3,16,32,128]{3,2,1,0:T(8,128)}, u32[]{:S(2)}) copy-start(f32[3,16,32,128]{3,2,1,0:T(8,128)} %param.11) | copy-start | bytes 2359300
  1.9 10.3 %copy-start.1 = (f32[16,32,128]{2,1,0:T(8,128)S(1)}, f32[16,32,128]{2,1,0:T(8,128)}, u32[]{:S(2)}) copy-start(f32[16,32,128]{2,1,0:T(8,128)} %plume.3) | copy-start | bytes 786436
  1.9 20.0 %copy-start.7 = (s32[3,8]{1,0:T(4,128)S(1)}, s32[3,8]{1,0:T(4,128)}, u32[]{:S(2)}) copy-start(s32[3,8]{1,0:T(4,128)} %param.13) | copy-start | bytes 292
  4.9 39.4 %copy-start.2 = (f32[16,32,128]{2,1,0:T(8,128)S(1)}, f32[16,32,128]{2,1,0:T(8,128)}, u32[]{:S(2)}) copy-start(f32[16,32,128]{2,1,0:T(8,128)} %source.3) | copy-start | bytes 786436
  4.9 39.4 %copy-start.4 = (s32[8]{0:T(128)S(1)}, s32[8]{0:T(128)}, u32[]{:S(2)}) copy-start(s32[8]{0:T(128)} %levels.5) | copy-start | bytes 100
  5.0 39.4 %copy-start.6 = (s32[2]{0:T(128)S(1)}, s32[2]{0:T(128)}, u32[]{:S(2)}) copy-start(s32[2]{0:T(128)} %owners.5) | copy-start | bytes 28
  5.0 19.1 %all-to-all-start = ((f32[32,24,128]{2,1,0:T(8,128)}), f32[32,24,128]{2,1,0:T(8,128)S(1)}, u32[]{:S(2)}, u32[]{:S(2)}) async-start(f32[32,24,128]{2,1,0:T(8,128)} %bitcast.1), calls=%async_computation | async-start | bytes 786432 | tf_op jit(solution)/shard_map/all_to_all | solution.py:319
  12.6 10.7 %collective-permute-start = (f32[64,128]{1,0:T(8,128)S(1)}, f32[64,128]{1,0:T(8,128)S(1)}, u32[]{:S(2)}, u32[]{:S(2)}) collective-permute-start(f32[64,128]{1,0:T(8,128)S(1)} %get-tuple-element.23), channel_id=1, source_target_pairs={{0,4},{4,8},{8,12},{12,16},{16,20},{20,24},{24,28},{1,5},{5,9},{9,... | collective-permute-start | bytes 98312 | tf_op jit(solution)/shard_map/ppermute | solution.py:259
  14.8 8.6 %collective-permute-start.1 = (f32[64,128]{1,0:T(8,128)S(1)}, f32[64,128]{1,0:T(8,128)S(1)}, u32[]{:S(2)}, u32[]{:S(2)}) collective-permute-start(f32[64,128]{1,0:T(8,128)S(1)} %get-tuple-element.24), channel_id=1, source_target_pairs={{4,0},{8,4},{12,8},{16,12},{20,16},{24,20},{28,24},{5,1},{9,5},{13... | collective-permute-start | bytes 98312 | tf_op jit(solution)/shard_map/ppermute | solution.py:260
  16.1 6.0 %collective-permute-start.3 = (f32[32,128]{1,0:T(8,128)S(1)}, f32[32,128]{1,0:T(8,128)S(1)}, u32[]{:S(2)}, u32[]{:S(2)}) collective-permute-start(f32[32,128]{1,0:T(8,128)S(1)} %get-tuple-element.25), channel_id=1, source_target_pairs={{1,0},{2,1},{3,2},{5,4},{6,5},{7,6},{9,8},{10,9},{11,10},{13,12},{... | collective-permute-start | bytes 49160 | tf_op jit(solution)/shard_map/ppermute | solution.py:262
  17.4 6.0 %collective-permute-start.2 = (f32[32,128]{1,0:T(8,128)S(1)}, f32[32,128]{1,0:T(8,128)S(1)}, u32[]{:S(2)}, u32[]{:S(2)}) collective-permute-start(f32[32,128]{1,0:T(8,128)S(1)} %get-tuple-element.25), channel_id=1, source_target_pairs={{0,1},{1,2},{2,3},{4,5},{5,6},{6,7},{8,9},{9,10},{10,11},{12,13},{... | collective-permute-start | bytes 49160 | tf_op jit(solution)/shard_map/ppermute | solution.py:261
  49.0 15.7 %all-to-all-start.2 = ((f32[32,24,128]{2,1,0:T(8,128)}), f32[32,24,128]{2,1,0:T(8,128)S(1)}, u32[]{:S(2)}, u32[]{:S(2)}) async-start(f32[32,24,128]{2,1,0:T(8,128)} %bitcast.3), calls=%async_computation.2 | async-start | bytes 786432 | tf_op jit(solution)/shard_map/all_to_all | solution.py:319
  53.2 10.7 %collective-permute-start.4 = (f32[64,128]{1,0:T(8,128)S(1)}, f32[64,128]{1,0:T(8,128)S(1)}, u32[]{:S(2)}, u32[]{:S(2)}) collective-permute-start(f32[64,128]{1,0:T(8,128)S(1)} %get-tuple-element.34), channel_id=1, source_target_pairs={{0,4},{4,8},{8,12},{12,16},{16,20},{20,24},{24,28},{1,5},{5,9},{9,... | collective-permute-start | bytes 98312 | tf_op jit(solution)/shard_map/ppermute | solution.py:259
  55.4 8.6 %collective-permute-start.5 = (f32[64,128]{1,0:T(8,128)S(1)}, f32[64,128]{1,0:T(8,128)S(1)}, u32[]{:S(2)}, u32[]{:S(2)}) collective-permute-start(f32[64,128]{1,0:T(8,128)S(1)} %get-tuple-element.35), channel_id=1, source_target_pairs={{4,0},{8,4},{12,8},{16,12},{20,16},{24,20},{28,24},{5,1},{9,5},{13... | collective-permute-start | bytes 98312 | tf_op jit(solution)/shard_map/ppermute | solution.py:260
  56.7 5.9 %collective-permute-start.7 = (f32[32,128]{1,0:T(8,128)S(1)}, f32[32,128]{1,0:T(8,128)S(1)}, u32[]{:S(2)}, u32[]{:S(2)}) collective-permute-start(f32[32,128]{1,0:T(8,128)S(1)} %get-tuple-element.36), channel_id=1, source_target_pairs={{1,0},{2,1},{3,2},{5,4},{6,5},{7,6},{9,8},{10,9},{11,10},{13,12},{... | collective-permute-start | bytes 49160 | tf_op jit(solution)/shard_map/ppermute | solution.py:262
  58.0 6.0 %collective-permute-start.6 = (f32[32,128]{1,0:T(8,128)S(1)}, f32[32,128]{1,0:T(8,128)S(1)}, u32[]{:S(2)}, u32[]{:S(2)}) collective-permute-start(f32[32,128]{1,0:T(8,128)S(1)} %get-tuple-element.36), channel_id=1, source_target_pairs={{0,1},{1,2},{2,3},{4,5},{5,6},{6,7},{8,9},{9,10},{10,11},{12,13},{... | collective-permute-start | bytes 49160 | tf_op jit(solution)/shard_map/ppermute | solution.py:261

commit v5 on v4

--- a/solution.py
+++ b/solution.py
@@ -87,23 +87,29 @@
     )
 
 
-def emit_modes(read, x_fwd, y_fwd, modes_ref):
-    nudged = modes_ref.shape[0]
+def emit_modes(read, x_fwd, y_fwd, winds, heat):
+    wind_slabs = winds.shape[0]
+    nudged = wind_slabs + heat.shape[0]
     slabs = [read(c) for c in range(nudged)]
     cells_x = slabs[0].shape[0]
     half = data_dot(jnp.concatenate(slabs, axis=0), y_fwd)
     lane = lax.broadcasted_iota(jnp.int32, (KX, 4 * KX), 1)
     for c in range(nudged):
         both = table_dot(x_fwd, half[c * cells_x : (c + 1) * cells_x])
-        modes_ref[c] = -jnp.where(lane < 2 * KX, both[:KX], both[KX:])
-
-
-def add_parent(parent, is_owner, modes_ref):
+        modes = -jnp.where(lane < 2 * KX, both[:KX], both[KX:])
+        if c < wind_slabs:
+            winds[c] = modes
+        else:
+            heat[c - wind_slabs] = modes
+
+
+def add_parent(parent, is_owner, winds, heat):
     @pl.when(is_owner)
     def _():
         for i in range(KX):
             tile = parent[:, i * 4 * KX : (i + 1) * 4 * KX]
-            modes_ref[:, i, :] = modes_ref[:, i, :] + tile
+            winds[:, i, :] = winds[:, i, :] + tile[: winds.shape[0]]
+            heat[:, i, :] = heat[:, i, :] + tile[winds.shape[0] :]
 
 
 def fetch_all(sems, pairs):
@@ -118,20 +124,20 @@
 
 
 def first_kernel(n_gy, level_total, levels, owners, fields_all, parent_all, x_fwd_all, y_fwd_all,
-                 modes, x_fwd, y_fwd, fields, parent, sems):
+                 winds, heat, x_fwd, y_fwd, fields, parent, sems):
     gx, gy = lax.axis_index("gx"), lax.axis_index("gy")
     copies = fetch_all(sems, [
         (fields_all, fields), (x_fwd_all.at[gx], x_fwd), (y_fwd_all.at[gy], y_fwd),
         (parent_all.at[0, 0], parent)])
     for copy in copies[:3]:
         copy.wait()
-    level_count = modes.shape[0] // 3
+    level_count = heat.shape[0]
     emit_modes(
         lambda c: fields[slab_of(levels, c, level_count, level_total)], x_fwd[...], y_fwd[...],
-        modes,
+        winds, heat,
     )
     copies[3].wait()
-    add_parent(parent, owners[0] == gx * n_gy + gy, modes)
+    add_parent(parent, owners[0] == gx * n_gy + gy, winds, heat)
 
 
 def edge_kernel(fields, plume, west, east, cols):
@@ -147,7 +153,7 @@
     cols[...] = acc
 
 
-def share_kernel(n_gy, period, cuts, parts, out):
+def share_kernel(n_gy, period, first_slab, cuts, parts, out):
     count, rows, lanes = parts.shape
     me = lax.axis_index("gx") * n_gy + lax.axis_index("gy")
     total = parts[0]
@@ -159,8 +165,8 @@
     r = 2 * pair + lane // (2 * KX)
     s = lane % (2 * KX)
     limit = jnp.zeros((rows, lanes), jnp.int32)
-    for c in range(cuts.shape[0]):
-        limit = jnp.where(slab == c, cuts[c], limit)
+    for c in range(first_slab, cuts.shape[0]):
+        limit = jnp.where(slab == c - first_slab, cuts[c], limit)
     keep = ((r % KX) < limit) & ((s % KX) < limit)
     factor = jnp.where(r == 0, 1.0, 2.0) * jnp.where(s == 0, 1.0, 2.0) * (1.0 / math.sqrt(period))
     result = jnp.where(keep, total * factor, 0.0)
@@ -168,14 +174,14 @@
         out[p] = result
 
 
-def step_kernel(n_gy, step, last, levels, owners, mismatch, fields, plume, source,
+def step_kernel(n_gy, step, last, levels, owners, winds_in, heat_in, fields, plume, source,
                 west, east, south, north, x_back_all, y_back_all, *rest):
     gx, gy = lax.axis_index("gx"), lax.axis_index("gy")
     extra = []
     if last:
         fields_out, plume_out, x_back, y_back, slabs, beside, sems = rest
     else:
-        (parent_all, x_fwd_all, y_fwd_all, fields_out, plume_out, modes,
+        (parent_all, x_fwd_all, y_fwd_all, fields_out, plume_out, winds, heat,
          x_back, y_back, slabs, beside, sems, parent, x_fwd, y_fwd) = rest
         extra = [(x_fwd_all.at[gx], x_fwd), (y_fwd_all.at[gy], y_fwd),
                  (parent_all.at[0, step + 1], parent)]
@@ -184,8 +190,8 @@
     level_total, cells_x, cells_y = plume.shape
     field_rows = fields.shape[0]
     total = field_rows + level_total
-    nudged = mismatch.shape[0] // KX
-    level_count = nudged // 3
+    level_count = heat_in.shape[0] // KX
+    nudged = 3 * level_count
     inner = slice(PAD, PAD + cells_x)
     for c in range(total):
         slabs[c, inner] = fields[c] if c < field_rows else plume[c - field_rows]
@@ -194,7 +200,7 @@
     beside[...] = jnp.zeros_like(beside)
     for copy in copies:
         copy.wait()
-    back = data_dot(mismatch[...], y_back[...])
+    back = data_dot(jnp.concatenate([winds_in[...], heat_in[...]], axis=0), y_back[...])
     x_table = x_back[...]
     for c in range(nudged):
         pair = back[c * KX : (c + 1) * KX]
@@ -244,9 +250,9 @@
         return
     emit_modes(
         lambda c: fields_out[slab_of(levels, c, level_count, level_total)], x_fwd[...], y_fwd[...],
-        modes,
-    )
-    add_parent(parent, owners[step + 1] == gx * n_gy + gy, modes)
+        winds, heat,
+    )
+    add_parent(parent, owners[step + 1] == gx * n_gy + gy, winds, heat)
 
 
 def swap_edges(west, east, cols):
@@ -272,7 +278,6 @@
     field_rows = 3 * level_total
     total = field_rows + level_total
     lanes = 4 * KX
-    rows = nudged * KX // devices
     flat = fields.reshape(field_rows, cells_x, cells_y)
     cuts = cuts.reshape(-1)
     f32 = functools.partial(jax.ShapeDtypeStruct, dtype=jnp.float32)
@@ -287,7 +292,8 @@
     def limit(mib):
         return pltpu.CompilerParams(vmem_limit_bytes=mib * 1024 * 1024)
 
-    mode_shape = f32((nudged, KX, lanes))
+    level_count = levels.shape[0]
+    mode_shapes = [f32((2 * level_count, KX, lanes)), f32((level_count, KX, lanes))]
     parent_space = vmem(nudged, 4 * KX * KX)
     step_scratch = [table_space(x_back), table_space(y_back),
                     vmem(total, cells_x + 2 * PAD, cells_y), vmem(field_rows, cells_x, cells_y),
@@ -296,9 +302,9 @@
 
     modes = pl.pallas_call(
         functools.partial(first_kernel, n_gy, level_total),
-        out_shape=mode_shape,
+        out_shape=mode_shapes,
         in_specs=[SMEM, SMEM] + [HBM] * 4,
-        out_specs=VMEM,
+        out_specs=[VMEM] * 2,
         scratch_shapes=[table_space(x_fwd), table_space(y_fwd),
                         vmem(field_rows, cells_x, cells_y), parent_space,
                         pltpu.SemaphoreType.DMA((4,))],
@@ -315,28 +321,33 @@
             compiler_params=limit(8),
             name="edges",
         )(flat, plume)
-        halo = swap_edges(*edges)
-        parts = lax.all_to_all(modes.reshape(devices, rows, lanes), AXES, 0, 0, tiled=True)
-        parts, *halo = lax.optimization_barrier((parts, *halo))
-        share = pl.pallas_call(
-            functools.partial(share_kernel, n_gy, period),
-            out_shape=f32((devices, rows, lanes)),
-            in_specs=[SMEM, VMEM],
-            out_specs=VMEM,
-            compiler_params=limit(4),
-            name="share_sum",
-        )(cuts, parts)
-        mismatch = lax.all_to_all(share, AXES, 0, 0, tiled=True)
+        west, east, south, north = swap_edges(*edges)
+        parts = [
+            lax.all_to_all(m.reshape(devices, -1, lanes), AXES, 0, 0, tiled=True) for m in modes
+        ]
+        parts[1], west, east = lax.optimization_barrier((parts[1], west, east))
+        halo = west, east, south, north
+        mismatch = []
+        for part, first_slab in zip(parts, (0, 2 * level_count)):
+            share = pl.pallas_call(
+                functools.partial(share_kernel, n_gy, period, first_slab),
+                out_shape=f32(part.shape),
+                in_specs=[SMEM, VMEM],
+                out_specs=VMEM,
+                compiler_params=limit(4),
+                name="share_heat" if first_slab else "share_winds",
+            )(cuts, part)
+            mismatch.append(lax.all_to_all(share, AXES, 0, 0, tiled=True).reshape(-1, lanes))
         out_shape = [f32(flat.shape), f32(plume.shape)]
-        operands = [levels, owners, mismatch.reshape(nudged * KX, lanes), flat, plume, source,
+        operands = [levels, owners, *mismatch, flat, plume, source,
                     *halo, in_hbm(x_back), in_hbm(y_back)]
         if not last:
-            out_shape.append(mode_shape)
+            out_shape += mode_shapes
             operands += [in_hbm(parent_modes), in_hbm(x_fwd), in_hbm(y_fwd)]
         results = pl.pallas_call(
             functools.partial(step_kernel, n_gy, step, last),
             out_shape=out_shape,
-            in_specs=[SMEM, SMEM] + [VMEM] * 8 + [HBM] * (len(operands) - 10),
+            in_specs=[SMEM, SMEM] + [VMEM] * 9 + [HBM] * (len(operands) - 11),
             out_specs=[VMEM] * len(out_shape),
             scratch_shapes=step_scratch + ([] if last else mode_scratch),
             compiler_params=limit(20),
@@ -345,7 +356,7 @@
         if last:
             flat, plume = results
         else:
-            flat, plume, modes = results
+            flat, plume, *modes = results
     return flat.reshape(fields.shape), plume
 
 

time: 90.4 us -> 121 us (1.34)
  waiting for transfers between devices: 4.24 us -> 33.5 us
  blocking collectives: 39.2 us -> 27.4 us
  starting transfers between devices: 29.7 us -> 39.7 us
  Pallas kernels: 13.7 us -> 17.5 us
    all_to_all x2 -> x6, waiting for transfers between devices: 1.48 us -> 24.9 us  [the longest x4 20.1 us: local(): lax.all_to_all(share, AXES, 0, 0, tiled=True).reshape(-1, lanes)]
    all_to_all x2, blocking collectives: 39.2 us -> 27.4 us  [local(): lax.all_to_all(m.reshape(devices, -1, lanes), AXES, 0, 0, tiled=True)]
    all_to_all x2 -> x6, starting transfers between devices: 11.2 us -> 21.4 us  [the longest x4 16.1 us: local(): lax.all_to_all(share, AXES, 0, 0, tiled=True).reshape(-1, lanes)]
    ppermute x2, waiting for transfers between devices: 0.01 us -> 5.79 us  [swap_edges(): lax.ppermute(west, 'gx', down_x)]
    pallas_call x2 -> x4, Pallas kernels: 1.25 us -> 5.09 us  [local(): pl.pallas_call(functools.partial(share_kernel, n_gy, period, first_slab),...]
  transfers between devices with their start and end apart: 10 -> 14, of which waited for: 4 -> 10; matrix products, arithmetic and copies ran while one was open for 0% -> 0% of each run, Pallas kernels for 1% -> 5%
where the time goes in v5:
time: 121 us; the launch traced here: 120 us
  starting transfers between devices  39.7 us (33%)
  waiting for transfers between devices  33.5 us (28%)
  blocking collectives  27.4 us (23%)
  Pallas kernels  17.5 us (14%)
  local copies, waits for them, and re-layouts  1.5 us (1%)
    all_to_all x2, blocking collectives, local(): lax.all_to_all(m.reshape(devices, -1, lanes), AXES, 0, 0, tiled=True)  27.4 us
    all_to_all x4, waiting for transfers between devices, local(): lax.all_to_all(share, AXES, 0, 0, tiled=True).reshape(-1, lanes)  20.1 us
    all_to_all x4, starting transfers between devices, local(): lax.all_to_all(share, AXES, 0, 0, tiled=True).reshape(-1, lanes)  16.1 us
    ppermute x2, starting transfers between devices, swap_edges(): lax.ppermute(cols, 'gy', up_y)  9.09 us
    pallas_call x2, Pallas kernels, local(): pl.pallas_call(functools.partial(step_kernel, n_gy, step, last), out_shap...  8.78 us
    ppermute x2, waiting for transfers between devices, swap_edges(): lax.ppermute(west, 'gx', down_x)  5.79 us
    all_to_all x2, starting transfers between devices, local(): lax.all_to_all(m.reshape(devices, -1, lanes), AXES, 0, 0, tiled=True)  5.3 us
    pallas_call x4, Pallas kernels, local(): pl.pallas_call(functools.partial(share_kernel, n_gy, period, first_slab),...  5.09 us
  transfers between devices with their start and end apart: 14, of which 10 were waited for; matrix products, arithmetic and copies ran while one was open for 0% of the time, Pallas kernels for 5%

profile of v5, /device:TPU:0, one launch (start us, length us, event | category | flops | bytes accessed | tf_op | source)
XLA Modules:
  0.0 120.4 jit_solution(7424906691354619924)
XLA Ops:
  2.1 2.9 %first_modes.1 = (f32[16,32,128]{2,1,0:T(8,128)}, f32[8,32,128]{2,1,0:T(8,128)S(1)}) custom-call(s32[8]{0:T(128)S(1)} %copy-done.3, s32[2]{0:T(128)S(1)} %copy-done.5, f32[48,32,128]{2,1,0:T(8,128)} %bitcast.10, f32[1,2,24,4096]{3,2,1,0:T(8,128)} %rest_0_.1, bf16[8,64,96]{2,1,0:T(8,128)(2,1)} %constant.8.clone.x_fwd_all.rest_1_, ...), custom_call_target="tpu_custom_call" | custom-call | tf_op jit(solution)/shard_map/first_modes/pallas_call | solution.py:303
  5.0 15.5 %all_to_all.40.parts = f32[32,8,128]{2,1,0:T(8,128)S(1)} all-to-all(f32[32,8,128]{2,1,0:T(8,128)S(1)} %bitcast.18), channel_id=1, replica_groups=mesh['gx'=8,'gy'=4] {'gx','gy'}, dimensions={0} | all-to-all | bytes 262144 | tf_op jit(solution)/shard_map/all_to_all | solution.py:326
  20.5 2.7 %all-to-all-start = ((f32[32,16,128]{2,1,0:T(8,128)}), f32[32,16,128]{2,1,0:T(8,128)S(1)}, u32[]{:S(2)}, u32[]{:S(2)}) async-start(f32[32,16,128]{2,1,0:T(8,128)} %bitcast.1), calls=%async_computation | async-start | bytes 524288 | tf_op jit(solution)/shard_map/all_to_all | solution.py:326
  23.6 2.0 %collective-permute-start = (f32[64,128]{1,0:T(8,128)S(1)}, f32[64,128]{1,0:T(8,128)S(1)}, u32[]{:S(2)}, u32[]{:S(2)}) collective-permute-start(f32[64,128]{1,0:T(8,128)S(1)} %get-tuple-element.24), channel_id=1, source_target_pairs={{0,4},{4,8},{8,12},{12,16},{16,20},{20,24},{24,28},{1,5},{5,9},{9,... | collective-permute-start | bytes 98312 | tf_op jit(solution)/shard_map/ppermute | solution.py:265
  25.6 1.3 %collective-permute-start.1 = (f32[64,128]{1,0:T(8,128)S(1)}, f32[64,128]{1,0:T(8,128)S(1)}, u32[]{:S(2)}, u32[]{:S(2)}) collective-permute-start(f32[64,128]{1,0:T(8,128)S(1)} %get-tuple-element.25), channel_id=1, source_target_pairs={{4,0},{8,4},{12,8},{16,12},{20,16},{24,20},{28,24},{5,1},{9,5},{13... | collective-permute-start | bytes 98312 | tf_op jit(solution)/shard_map/ppermute | solution.py:266
  27.0 2.9 %collective-permute-done.1.east = f32[64,128]{1,0:T(8,128)S(1)} collective-permute-done((f32[64,128]{1,0:T(8,128)S(1)}, f32[64,128]{1,0:T(8,128)S(1)}, u32[]{:S(2)}, u32[]{:S(2)}) %collective-permute-start.1) | collective-permute-done | bytes 32800 | tf_op jit(solution)/shard_map/ppermute | solution.py:266
  29.9 1.2 %share_heat.2 = f32[32,8,128]{2,1,0:T(8,128)} custom-call(s32[24]{0:T(128)S(1)} %reshape.37.cuts, f32[32,8,128]{2,1,0:T(8,128)S(1)} %all_to_all.40.parts), custom_call_target="tpu_custom_call" | custom-call | tf_op jit(solution)/shard_map/share_heat/pallas_call | solution.py:332
  31.1 2.4 %all-to-all-done.parts = f32[32,16,128]{2,1,0:T(8,128)S(1)} async-done(((f32[32,16,128]{2,1,0:T(8,128)}), f32[32,16,128]{2,1,0:T(8,128)S(1)}, u32[]{:S(2)}, u32[]{:S(2)}) %all-to-all-start) | async-done | bytes 262176 | tf_op jit(solution)/shard_map/all_to_all | solution.py:326
  33.5 5.5 %all-to-all-start.3 = ((f32[32,8,128]{2,1,0:T(8,128)}), f32[32,8,128]{2,1,0:T(8,128)S(1)}, u32[]{:S(2)}, u32[]{:S(2)}) async-start(f32[32,8,128]{2,1,0:T(8,128)} %share_heat.2), calls=%async_computation.3 | async-start | bytes 262144 | tf_op jit(solution)/shard_map/all_to_all | solution.py:340
  39.0 1.3 %share_winds.2 = f32[32,16,128]{2,1,0:T(8,128)} custom-call(s32[24]{0:T(128)S(1)} %reshape.37.cuts, f32[32,16,128]{2,1,0:T(8,128)S(1)} %all-to-all-done.parts), custom_call_target="tpu_custom_call" | custom-call | tf_op jit(solution)/shard_map/share_winds/pallas_call | solution.py:332
  40.3 7.1 %all-to-all-done.3 = f32[32,8,128]{2,1,0:T(8,128)S(1)} async-done(((f32[32,8,128]{2,1,0:T(8,128)}), f32[32,8,128]{2,1,0:T(8,128)S(1)}, u32[]{:S(2)}, u32[]{:S(2)}) %all-to-all-start.3) | async-done | bytes 131104 | tf_op jit(solution)/shard_map/all_to_all | solution.py:340
  47.4 2.6 %all-to-all-start.1 = ((f32[32,16,128]{2,1,0:T(8,128)}), f32[32,16,128]{2,1,0:T(8,128)S(1)}, u32[]{:S(2)}, u32[]{:S(2)}) async-start(f32[32,16,128]{2,1,0:T(8,128)} %share_winds.2), calls=%async_computation.1 | async-start | bytes 524288 | tf_op jit(solution)/shard_map/all_to_all | solution.py:340
  50.0 1.3 %collective-permute-start.3 = (f32[32,128]{1,0:T(8,128)S(1)}, f32[32,128]{1,0:T(8,128)S(1)}, u32[]{:S(2)}, u32[]{:S(2)}) collective-permute-start(f32[32,128]{1,0:T(8,128)S(1)} %get-tuple-element.29), channel_id=1, source_target_pairs={{1,0},{2,1},{3,2},{5,4},{6,5},{7,6},{9,8},{10,9},{11,10},{13,12},{... | collective-permute-start | bytes 49160 | tf_op jit(solution)/shard_map/ppermute | solution.py:268
  51.3 4.5 %collective-permute-start.2 = (f32[32,128]{1,0:T(8,128)S(1)}, f32[32,128]{1,0:T(8,128)S(1)}, u32[]{:S(2)}, u32[]{:S(2)}) collective-permute-start(f32[32,128]{1,0:T(8,128)S(1)} %get-tuple-element.29), channel_id=1, source_target_pairs={{0,1},{1,2},{2,3},{4,5},{5,6},{6,7},{8,9},{9,10},{10,11},{12,13},{... | collective-permute-start | bytes 49160 | tf_op jit(solution)/shard_map/ppermute | solution.py:267
  55.8 1.4 %collective-permute-done.2.south = f32[32,128]{1,0:T(8,128)S(1)} collective-permute-done((f32[32,128]{1,0:T(8,128)S(1)}, f32[32,128]{1,0:T(8,128)S(1)}, u32[]{:S(2)}, u32[]{:S(2)}) %collective-permute-start.2) | collective-permute-done | bytes 16416 | tf_op jit(solution)/shard_map/ppermute | solution.py:267
  57.3 2.9 %all-to-all-done.1 = f32[32,16,128]{2,1,0:T(8,128)S(1)} async-done(((f32[32,16,128]{2,1,0:T(8,128)}), f32[32,16,128]{2,1,0:T(8,128)S(1)}, u32[]{:S(2)}, u32[]{:S(2)}) %all-to-all-start.1) | async-done | bytes 262176 | tf_op jit(solution)/shard_map/all_to_all | solution.py:340
  60.2 4.6 %inner_step.1 = (f32[48,32,128]{2,1,0:T(8,128)S(1)}, f32[16,32,128]{2,1,0:T(8,128)S(1)}, f32[16,32,128]{2,1,0:T(8,128)}, f32[8,32,128]{2,1,0:T(8,128)S(1)}) custom-call(s32[8]{0:T(128)S(1)} %copy-done.4, s32[2]{0:T(128)S(1)} %copy-done.6, f32[512,128]{1,0:T(8,128)S(1)} %bitcast.14, f32[256,128]{1,0:T(8,128)S(1)} %bitcast.15, f32[48,32,128]{2,1,0:T(8,128)S(1)} %bitcast.12, ...), custom_call_target="tpu_custom_call" | custom-call | tf_op jit(solution)/shard_map/inner_step/pallas_call | solution.py:347
  64.8 11.9 %all_to_all.41.parts = f32[32,8,128]{2,1,0:T(8,128)S(1)} all-to-all(f32[32,8,128]{2,1,0:T(8,128)S(1)} %bitcast.17), channel_id=1, replica_groups=mesh['gx'=8,'gy'=4] {'gx','gy'}, dimensions={0} | all-to-all | bytes 262144 | tf_op jit(solution)/shard_map/all_to_all | solution.py:326
  76.7 2.6 %all-to-all-start.4 = ((f32[32,16,128]{2,1,0:T(8,128)}), f32[32,16,128]{2,1,0:T(8,128)S(1)}, u32[]{:S(2)}, u32[]{:S(2)}) async-start(f32[32,16,128]{2,1,0:T(8,128)} %bitcast.5), calls=%async_computation.4 | async-start | bytes 524288 | tf_op jit(solution)/shard_map/all_to_all | solution.py:326
  79.6 2.0 %collective-permute-start.4 = (f32[64,128]{1,0:T(8,128)S(1)}, f32[64,128]{1,0:T(8,128)S(1)}, u32[]{:S(2)}, u32[]{:S(2)}) collective-permute-start(f32[64,128]{1,0:T(8,128)S(1)} %get-tuple-element.34), channel_id=1, source_target_pairs={{0,4},{4,8},{8,12},{12,16},{16,20},{20,24},{24,28},{1,5},{5,9},{9,... | collective-permute-start | bytes 98312 | tf_op jit(solution)/shard_map/ppermute | solution.py:265
  81.7 1.3 %collective-permute-start.5 = (f32[64,128]{1,0:T(8,128)S(1)}, f32[64,128]{1,0:T(8,128)S(1)}, u32[]{:S(2)}, u32[]{:S(2)}) collective-permute-start(f32[64,128]{1,0:T(8,128)S(1)} %get-tuple-element.35), channel_id=1, source_target_pairs={{4,0},{8,4},{12,8},{16,12},{20,16},{24,20},{28,24},{5,1},{9,5},{13... | collective-permute-start | bytes 98312 | tf_op jit(solution)/shard_map/ppermute | solution.py:266
  83.0 2.9 %collective-permute-done.5.east = f32[64,128]{1,0:T(8,128)S(1)} collective-permute-done((f32[64,128]{1,0:T(8,128)S(1)}, f32[64,128]{1,0:T(8,128)S(1)}, u32[]{:S(2)}, u32[]{:S(2)}) %collective-permute-start.5) | collective-permute-done | bytes 32800 | tf_op jit(solution)/shard_map/ppermute | solution.py:266
  87.1 2.4 %all-to-all-done.4.parts = f32[32,16,128]{2,1,0:T(8,128)S(1)} async-done(((f32[32,16,128]{2,1,0:T(8,128)}), f32[32,16,128]{2,1,0:T(8,128)S(1)}, u32[]{:S(2)}, u32[]{:S(2)}) %all-to-all-start.4) | async-done | bytes 262176 | tf_op jit(solution)/shard_map/all_to_all | solution.py:326
  89.6 5.5 %all-to-all-start.7 = ((f32[32,8,128]{2,1,0:T(8,128)}), f32[32,8,128]{2,1,0:T(8,128)S(1)}, u32[]{:S(2)}, u32[]{:S(2)}) async-start(f32[32,8,128]{2,1,0:T(8,128)} %share_heat.3), calls=%async_computation.7 | async-start | bytes 262144 | tf_op jit(solution)/shard_map/all_to_all | solution.py:340
  95.0 1.3 %share_winds.3 = f32[32,16,128]{2,1,0:T(8,128)} custom-call(s32[24]{0:T(128)S(1)} %reshape.37.cuts, f32[32,16,128]{2,1,0:T(8,128)S(1)} %all-to-all-done.4.parts), custom_call_target="tpu_custom_call" | custom-call | tf_op jit(solution)/shard_map/share_winds/pallas_call | solution.py:332
  96.3 7.1 %all-to-all-done.7 = f32[32,8,128]{2,1,0:T(8,128)S(1)} async-done(((f32[32,8,128]{2,1,0:T(8,128)}), f32[32,8,128]{2,1,0:T(8,128)S(1)}, u32[]{:S(2)}, u32[]{:S(2)}) %all-to-all-start.7) | async-done | bytes 131104 | tf_op jit(solution)/shard_map/all_to_all | solution.py:340
  103.4 2.6 %all-to-all-start.5 = ((f32[32,16,128]{2,1,0:T(8,128)}), f32[32,16,128]{2,1,0:T(8,128)S(1)}, u32[]{:S(2)}, u32[]{:S(2)}) async-start(f32[32,16,128]{2,1,0:T(8,128)} %share_winds.3), calls=%async_computation.5 | async-start | bytes 524288 | tf_op jit(solution)/shard_map/all_to_all | solution.py:340
  106.0 1.3 %collective-permute-start.7 = (f32[32,128]{1,0:T(8,128)S(1)}, f32[32,128]{1,0:T(8,128)S(1)}, u32[]{:S(2)}, u32[]{:S(2)}) collective-permute-start(f32[32,128]{1,0:T(8,128)S(1)} %get-tuple-element.39), channel_id=1, source_target_pairs={{1,0},{2,1},{3,2},{5,4},{6,5},{7,6},{9,8},{10,9},{11,10},{13,12},{... | collective-permute-start | bytes 49160 | tf_op jit(solution)/shard_map/ppermute | solution.py:268
  107.3 4.5 %collective-permute-start.6 = (f32[32,128]{1,0:T(8,128)S(1)}, f32[32,128]{1,0:T(8,128)S(1)}, u32[]{:S(2)}, u32[]{:S(2)}) collective-permute-start(f32[32,128]{1,0:T(8,128)S(1)} %get-tuple-element.39), channel_id=1, source_target_pairs={{0,1},{1,2},{2,3},{4,5},{5,6},{6,7},{8,9},{9,10},{10,11},{12,13},{... | collective-permute-start | bytes 49160 | tf_op jit(solution)/shard_map/ppermute | solution.py:267
  111.9 1.4 %collective-permute-done.6.south = f32[32,128]{1,0:T(8,128)S(1)} collective-permute-done((f32[32,128]{1,0:T(8,128)S(1)}, f32[32,128]{1,0:T(8,128)S(1)}, u32[]{:S(2)}, u32[]{:S(2)}) %collective-permute-start.6) | collective-permute-done | bytes 16416 | tf_op jit(solution)/shard_map/ppermute | solution.py:267
  113.3 2.9 %all-to-all-done.5 = f32[32,16,128]{2,1,0:T(8,128)S(1)} async-done(((f32[32,16,128]{2,1,0:T(8,128)}), f32[32,16,128]{2,1,0:T(8,128)S(1)}, u32[]{:S(2)}, u32[]{:S(2)}) %all-to-all-start.5) | async-done | bytes 262176 | tf_op jit(solution)/shard_map/all_to_all | solution.py:340
  116.2 4.2 %final_step.1 = (f32[48,32,128]{2,1,0:T(8,128)}, f32[16,32,128]{2,1,0:T(8,128)}) custom-call(s32[8]{0:T(128)S(1)} %copy-done.4, s32[2]{0:T(128)S(1)} %copy-done.6, f32[512,128]{1,0:T(8,128)S(1)} %bitcast.13, f32[256,128]{1,0:T(8,128)S(1)} %bitcast.16, f32[48,32,128]{2,1,0:T(8,128)S(1)} %get-tuple-element.32.fields, ...), custom_call_target="tpu_custom_call" | custom-call | tf_op jit(solution)/shard_map/final_step/pallas_call | solution.py:347
  (24 shorter events, 3.4 us)
Async XLA Ops:
  0.6 22.6 %copy-start = (f32[3,16,32,128]{3,2,1,0:T(8,128)S(1)}, f32[3,16,32,128]{3,2,1,0:T(8,128)}, u32[]{:S(2)}) copy-start(f32[3,16,32,128]{3,2,1,0:T(8,128)} %param.11) | copy-start | bytes 2359300
  0.6 22.6 %copy-start.1 = (f32[16,32,128]{2,1,0:T(8,128)S(1)}, f32[16,32,128]{2,1,0:T(8,128)}, u32[]{:S(2)}) copy-start(f32[16,32,128]{2,1,0:T(8,128)} %plume.3) | copy-start | bytes 786436
  0.7 0.7 copy-start.3
  1.4 0.7 copy-start.5
  2.0 24.9 %copy-start.7 = (s32[3,8]{1,0:T(4,128)S(1)}, s32[3,8]{1,0:T(4,128)}, u32[]{:S(2)}) copy-start(s32[3,8]{1,0:T(4,128)} %param.13) | copy-start | bytes 292
  20.5 39.7 %copy-start.2 = (f32[16,32,128]{2,1,0:T(8,128)S(1)}, f32[16,32,128]{2,1,0:T(8,128)}, u32[]{:S(2)}) copy-start(f32[16,32,128]{2,1,0:T(8,128)} %source.3) | copy-start | bytes 786436
  20.5 39.7 %copy-start.4 = (s32[8]{0:T(128)S(1)}, s32[8]{0:T(128)}, u32[]{:S(2)}) copy-start(s32[8]{0:T(128)} %levels.5) | copy-start | bytes 100
  20.5 39.7 %copy-start.6 = (s32[2]{0:T(128)S(1)}, s32[2]{0:T(128)}, u32[]{:S(2)}) copy-start(s32[2]{0:T(128)} %owners.5) | copy-start | bytes 28
  20.5 13.0 %all-to-all-start = ((f32[32,16,128]{2,1,0:T(8,128)}), f32[32,16,128]{2,1,0:T(8,128)S(1)}, u32[]{:S(2)}, u32[]{:S(2)}) async-start(f32[32,16,128]{2,1,0:T(8,128)} %bitcast.1), calls=%async_computation | async-start | bytes 524288 | tf_op jit(solution)/shard_map/all_to_all | solution.py:326
  23.6 3.4 %collective-permute-start = (f32[64,128]{1,0:T(8,128)S(1)}, f32[64,128]{1,0:T(8,128)S(1)}, u32[]{:S(2)}, u32[]{:S(2)}) collective-permute-start(f32[64,128]{1,0:T(8,128)S(1)} %get-tuple-element.24), channel_id=1, source_target_pairs={{0,4},{4,8},{8,12},{12,16},{16,20},{20,24},{24,28},{1,5},{5,9},{9,... | collective-permute-start | bytes 98312 | tf_op jit(solution)/shard_map/ppermute | solution.py:265
  25.6 4.2 %collective-permute-start.1 = (f32[64,128]{1,0:T(8,128)S(1)}, f32[64,128]{1,0:T(8,128)S(1)}, u32[]{:S(2)}, u32[]{:S(2)}) collective-permute-start(f32[64,128]{1,0:T(8,128)S(1)} %get-tuple-element.25), channel_id=1, source_target_pairs={{4,0},{8,4},{12,8},{16,12},{20,16},{24,20},{28,24},{5,1},{9,5},{13... | collective-permute-start | bytes 98312 | tf_op jit(solution)/shard_map/ppermute | solution.py:266
  33.5 13.9 %all-to-all-start.3 = ((f32[32,8,128]{2,1,0:T(8,128)}), f32[32,8,128]{2,1,0:T(8,128)S(1)}, u32[]{:S(2)}, u32[]{:S(2)}) async-start(f32[32,8,128]{2,1,0:T(8,128)} %share_heat.2), calls=%async_computation.3 | async-start | bytes 262144 | tf_op jit(solution)/shard_map/all_to_all | solution.py:340
  47.4 12.8 %all-to-all-start.1 = ((f32[32,16,128]{2,1,0:T(8,128)}), f32[32,16,128]{2,1,0:T(8,128)S(1)}, u32[]{:S(2)}, u32[]{:S(2)}) async-start(f32[32,16,128]{2,1,0:T(8,128)} %share_winds.2), calls=%async_computation.1 | async-start | bytes 524288 | tf_op jit(solution)/shard_map/all_to_all | solution.py:340
  50.0 5.9 %collective-permute-start.3 = (f32[32,128]{1,0:T(8,128)S(1)}, f32[32,128]{1,0:T(8,128)S(1)}, u32[]{:S(2)}, u32[]{:S(2)}) collective-permute-start(f32[32,128]{1,0:T(8,128)S(1)} %get-tuple-element.29), channel_id=1, source_target_pairs={{1,0},{2,1},{3,2},{5,4},{6,5},{7,6},{9,8},{10,9},{11,10},{13,12},{... | collective-permute-start | bytes 49160 | tf_op jit(solution)/shard_map/ppermute | solution.py:268
  51.3 6.0 %collective-permute-start.2 = (f32[32,128]{1,0:T(8,128)S(1)}, f32[32,128]{1,0:T(8,128)S(1)}, u32[]{:S(2)}, u32[]{:S(2)}) collective-permute-start(f32[32,128]{1,0:T(8,128)S(1)} %get-tuple-element.29), channel_id=1, source_target_pairs={{0,1},{1,2},{2,3},{4,5},{5,6},{6,7},{8,9},{9,10},{10,11},{12,13},{... | collective-permute-start | bytes 49160 | tf_op jit(solution)/shard_map/ppermute | solution.py:267
  76.7 12.9 %all-to-all-start.4 = ((f32[32,16,128]{2,1,0:T(8,128)}), f32[32,16,128]{2,1,0:T(8,128)S(1)}, u32[]{:S(2)}, u32[]{:S(2)}) async-start(f32[32,16,128]{2,1,0:T(8,128)} %bitcast.5), calls=%async_computation.4 | async-start | bytes 524288 | tf_op jit(solution)/shard_map/all_to_all | solution.py:326
  79.6 3.3 %collective-permute-start.4 = (f32[64,128]{1,0:T(8,128)S(1)}, f32[64,128]{1,0:T(8,128)S(1)}, u32[]{:S(2)}, u32[]{:S(2)}) collective-permute-start(f32[64,128]{1,0:T(8,128)S(1)} %get-tuple-element.34), channel_id=1, source_target_pairs={{0,4},{4,8},{8,12},{12,16},{16,20},{20,24},{24,28},{1,5},{5,9},{9,... | collective-permute-start | bytes 98312 | tf_op jit(solution)/shard_map/ppermute | solution.py:265
  81.7 4.2 %collective-permute-start.5 = (f32[64,128]{1,0:T(8,128)S(1)}, f32[64,128]{1,0:T(8,128)S(1)}, u32[]{:S(2)}, u32[]{:S(2)}) collective-permute-start(f32[64,128]{1,0:T(8,128)S(1)} %get-tuple-element.35), channel_id=1, source_target_pairs={{4,0},{8,4},{12,8},{16,12},{20,16},{24,20},{28,24},{5,1},{9,5},{13... | collective-permute-start | bytes 98312 | tf_op jit(solution)/shard_map/ppermute | solution.py:266
  89.6 13.9 %all-to-all-start.7 = ((f32[32,8,128]{2,1,0:T(8,128)}), f32[32,8,128]{2,1,0:T(8,128)S(1)}, u32[]{:S(2)}, u32[]{:S(2)}) async-start(f32[32,8,128]{2,1,0:T(8,128)} %share_heat.3), calls=%async_computation.7 | async-start | bytes 262144 | tf_op jit(solution)/shard_map/all_to_all | solution.py:340
  103.4 12.8 %all-to-all-start.5 = ((f32[32,16,128]{2,1,0:T(8,128)}), f32[32,16,128]{2,1,0:T(8,128)S(1)}, u32[]{:S(2)}, u32[]{:S(2)}) async-start(f32[32,16,128]{2,1,0:T(8,128)} %share_winds.3), calls=%async_computation.5 | async-start | bytes 524288 | tf_op jit(solution)/shard_map/all_to_all | solution.py:340
  106.0 5.9 %collective-permute-start.7 = (f32[32,128]{1,0:T(8,128)S(1)}, f32[32,128]{1,0:T(8,128)S(1)}, u32[]{:S(2)}, u32[]{:S(2)}) collective-permute-start(f32[32,128]{1,0:T(8,128)S(1)} %get-tuple-element.39), channel_id=1, source_target_pairs={{1,0},{2,1},{3,2},{5,4},{6,5},{7,6},{9,8},{10,9},{11,10},{13,12},{... | collective-permute-start | bytes 49160 | tf_op jit(solution)/shard_map/ppermute | solution.py:268
  107.3 6.0 %collective-permute-start.6 = (f32[32,128]{1,0:T(8,128)S(1)}, f32[32,128]{1,0:T(8,128)S(1)}, u32[]{:S(2)}, u32[]{:S(2)}) collective-permute-start(f32[32,128]{1,0:T(8,128)S(1)} %get-tuple-element.39), channel_id=1, source_target_pairs={{0,1},{1,2},{2,3},{4,5},{5,6},{6,7},{8,9},{9,10},{10,11},{12,13},{... | collective-permute-start | bytes 49160 | tf_op jit(solution)/shard_map/ppermute | solution.py:267

commit v6 on v4

--- a/solution.py
+++ b/solution.py
@@ -134,7 +134,14 @@
     add_parent(parent, owners[0] == gx * n_gy + gy, modes)
 
 
-def edge_kernel(fields, plume, west, east, cols):
+def edge_kernel(fields, plume, *rest):
+    copies = []
+    if len(rest) > 3:
+        x_back_all, y_back_all, west, east, cols, x_back, y_back, sems = rest
+        copies = fetch_all(sems, [(x_back_all.at[lax.axis_index("gx")], x_back),
+                                  (y_back_all.at[lax.axis_index("gy")], y_back)])
+    else:
+        west, east, cols = rest
     cells_x, cells_y = plume.shape[1:]
     field_rows = fields.shape[0]
     lane = lax.broadcasted_iota(jnp.int32, cols.shape, 1)
@@ -145,6 +152,8 @@
         east[c : c + 1, :] = a[cells_x - 1 :]
         acc = jnp.where(lane // 2 == c, pltpu.roll(a, 2 * c + 1, 1), acc)
     cols[...] = acc
+    for copy in copies:
+        copy.wait()
 
 
 def share_kernel(n_gy, period, cuts, parts, out):
@@ -169,18 +178,16 @@
 
 
 def step_kernel(n_gy, step, last, levels, owners, mismatch, fields, plume, source,
-                west, east, south, north, x_back_all, y_back_all, *rest):
+                west, east, south, north, x_back, y_back, *rest):
     gx, gy = lax.axis_index("gx"), lax.axis_index("gy")
-    extra = []
+    copies = []
     if last:
-        fields_out, plume_out, x_back, y_back, slabs, beside, sems = rest
+        fields_out, plume_out, slabs, beside = rest
     else:
         (parent_all, x_fwd_all, y_fwd_all, fields_out, plume_out, modes,
-         x_back, y_back, slabs, beside, sems, parent, x_fwd, y_fwd) = rest
-        extra = [(x_fwd_all.at[gx], x_fwd), (y_fwd_all.at[gy], y_fwd),
-                 (parent_all.at[0, step + 1], parent)]
-    copies = fetch_all(
-        sems, [(y_back_all.at[gy], y_back), (x_back_all.at[gx], x_back)] + extra)
+         slabs, beside, sems, parent, x_fwd, y_fwd) = rest
+        copies = fetch_all(sems, [(x_fwd_all.at[gx], x_fwd), (y_fwd_all.at[gy], y_fwd),
+                                  (parent_all.at[0, step + 1], parent)])
     level_total, cells_x, cells_y = plume.shape
     field_rows = fields.shape[0]
     total = field_rows + level_total
@@ -192,8 +199,6 @@
         slabs[c, PAD - 1 : PAD] = west[c : c + 1, :]
         slabs[c, PAD + cells_x : PAD + cells_x + 1] = east[c : c + 1, :]
     beside[...] = jnp.zeros_like(beside)
-    for copy in copies:
-        copy.wait()
     back = data_dot(mismatch[...], y_back[...])
     x_table = x_back[...]
     for c in range(nudged):
@@ -242,6 +247,8 @@
 
     if last:
         return
+    for copy in copies:
+        copy.wait()
     emit_modes(
         lambda c: fields_out[slab_of(levels, c, level_count, level_total)], x_fwd[...], y_fwd[...],
         modes,
@@ -249,18 +256,11 @@
     add_parent(parent, owners[step + 1] == gx * n_gy + gy, modes)
 
 
-def swap_edges(west, east, cols):
-    n_gx, n_gy = lax.axis_size("gx"), lax.axis_size("gy")
-    up_x = [(i, i + 1) for i in range(n_gx - 1)]
-    up_y = [(i, i + 1) for i in range(n_gy - 1)]
-    down_x = [(b, a) for a, b in up_x]
-    down_y = [(b, a) for a, b in up_y]
-    return (
-        lax.ppermute(east, "gx", up_x),
-        lax.ppermute(west, "gx", down_x),
-        lax.ppermute(cols, "gy", up_y),
-        lax.ppermute(cols, "gy", down_y),
-    )
+def swap(axis, to_next, to_previous):
+    count = lax.axis_size(axis)
+    up = [(i, i + 1) for i in range(count - 1)]
+    down = [(b, a) for a, b in up]
+    return lax.ppermute(to_next, axis, up), lax.ppermute(to_previous, axis, down)
 
 
 def local(tables, fields, levels, cuts, parent_modes, owners, plume, source):
@@ -289,10 +289,10 @@
 
     mode_shape = f32((nudged, KX, lanes))
     parent_space = vmem(nudged, 4 * KX * KX)
-    step_scratch = [table_space(x_back), table_space(y_back),
-                    vmem(total, cells_x + 2 * PAD, cells_y), vmem(field_rows, cells_x, cells_y),
-                    pltpu.SemaphoreType.DMA((5,))]
-    mode_scratch = [parent_space, table_space(x_fwd), table_space(y_fwd)]
+    step_scratch = [vmem(total, cells_x + 2 * PAD, cells_y), vmem(field_rows, cells_x, cells_y)]
+    mode_scratch = [pltpu.SemaphoreType.DMA((3,)), parent_space, table_space(x_fwd),
+                    table_space(y_fwd)]
+    levels, owners = in_hbm(levels), in_hbm(owners)
 
     modes = pl.pallas_call(
         functools.partial(first_kernel, n_gy, level_total),
@@ -307,17 +307,26 @@
     )(levels, owners, in_hbm(flat), in_hbm(parent_modes), in_hbm(x_fwd), in_hbm(y_fwd))
     for step in range(STEPS):
         last = step == STEPS - 1
+        edge_shapes = [f32((total, cells_y)), f32((total, cells_y)), f32((cells_x, 2 * total))]
+        edge_operands = [flat, plume]
+        if step == 0:
+            edge_shapes += [jax.ShapeDtypeStruct(t.shape[1:], t.dtype) for t in (x_back, y_back)]
+            edge_operands += [in_hbm(x_back), in_hbm(y_back)]
         edges = pl.pallas_call(
             edge_kernel,
-            out_shape=[f32((total, cells_y)), f32((total, cells_y)), f32((cells_x, 2 * total))],
-            in_specs=[VMEM, VMEM],
-            out_specs=[VMEM] * 3,
+            out_shape=edge_shapes,
+            in_specs=[VMEM, VMEM] + [HBM] * (len(edge_operands) - 2),
+            out_specs=[VMEM] * len(edge_shapes),
+            scratch_shapes=[pltpu.SemaphoreType.DMA((2,))] if step == 0 else [],
             compiler_params=limit(8),
             name="edges",
-        )(flat, plume)
-        halo = swap_edges(*edges)
+        )(*edge_operands)
+        if step == 0:
+            back_tables = edges[3:]
+        to_west, to_east, cols = edges[:3]
+        west, east = swap("gx", to_east, to_west)
         parts = lax.all_to_all(modes.reshape(devices, rows, lanes), AXES, 0, 0, tiled=True)
-        parts, *halo = lax.optimization_barrier((parts, *halo))
+        parts, west, east = lax.optimization_barrier((parts, west, east))
         share = pl.pallas_call(
             functools.partial(share_kernel, n_gy, period),
             out_shape=f32((devices, rows, lanes)),
@@ -326,17 +335,19 @@
             compiler_params=limit(4),
             name="share_sum",
         )(cuts, parts)
+        share, cols = lax.optimization_barrier((share, cols))
+        south, north = swap("gy", cols, cols)
         mismatch = lax.all_to_all(share, AXES, 0, 0, tiled=True)
         out_shape = [f32(flat.shape), f32(plume.shape)]
         operands = [levels, owners, mismatch.reshape(nudged * KX, lanes), flat, plume, source,
-                    *halo, in_hbm(x_back), in_hbm(y_back)]
+                    west, east, south, north, *back_tables]
         if not last:
             out_shape.append(mode_shape)
             operands += [in_hbm(parent_modes), in_hbm(x_fwd), in_hbm(y_fwd)]
         results = pl.pallas_call(
             functools.partial(step_kernel, n_gy, step, last),
             out_shape=out_shape,
-            in_specs=[SMEM, SMEM] + [VMEM] * 8 + [HBM] * (len(operands) - 10),
+            in_specs=[SMEM, SMEM] + [VMEM] * 10 + [HBM] * (len(operands) - 12),
             out_specs=[VMEM] * len(out_shape),
             scratch_shapes=step_scratch + ([] if last else mode_scratch),
             compiler_params=limit(20),

time: 90.4 us -> 82.6 us (0.914)
  blocking collectives: 39.2 us -> 0 us
  waiting for transfers between devices: 4.24 us -> 27.2 us
  starting transfers between devices: 29.7 us -> 37.4 us
  Pallas kernels: 13.7 us -> 15.7 us
  local copies, waits for them, and re-layouts: 1.42 us -> 0.1 us
    all_to_all x2 -> x0, blocking collectives: 39.2 us -> none  [local(): mismatch = lax.all_to_all(share, AXES, 0, 0, tiled=True)]
    all_to_all x0 -> x2, waiting for transfers between devices: none -> 9.17 us  [local(): mismatch = lax.all_to_all(share, AXES, 0, 0, tiled=True)]
    all_to_all x0 -> x2, starting transfers between devices: none -> 7.72 us  [local(): mismatch = lax.all_to_all(share, AXES, 0, 0, tiled=True)]
    all_to_all x2, waiting for transfers between devices: 1.48 us -> 9.17 us  [local(): lax.all_to_all(modes.reshape(devices, rows, lanes), AXES, 0, 0, tiled=True)]
    ppermute x8, waiting for transfers between devices: 2.76 us -> 8.88 us  [the longest x4 7.92 us: swap(): lax.ppermute(to_previous, axis, down)]
    pallas_call x2, Pallas kernels: 1.25 us -> 2.74 us  [local(): pl.pallas_call(functools.partial(share_kernel, n_gy, period), out_shape=f...]
    unnamed x16 -> x8, local copies, waits for them, and re-layouts: 1.34 us -> 0.02 us
    pallas_call x2, Pallas kernels: 0.67 us -> 1.63 us  [local(): pl.pallas_call(edge_kernel, out_shape=edge_shapes, in_specs=[VMEM, VMEM]...]
  transfers between devices with their start and end apart: 10 -> 12, of which waited for: 4 -> 10; matrix products, arithmetic and copies ran while one was open for 0% -> 0% of each run, Pallas kernels for 1% -> 2%
where the time goes in v6:
time: 82.6 us; the launch traced here: 81.2 us
  starting transfers between devices  37.4 us (45%)
  waiting for transfers between devices  27.2 us (33%)
  Pallas kernels  15.7 us (19%)
    ppermute x4, starting transfers between devices, swap(): lax.ppermute(to_next, axis, up)  13.4 us
    all_to_all x2, starting transfers between devices, local(): lax.all_to_all(modes.reshape(devices, rows, lanes), AXES, 0, 0, tiled=True)  11.1 us
    all_to_all x2, waiting for transfers between devices, local(): mismatch = lax.all_to_all(share, AXES, 0, 0, tiled=True)  9.17 us
    all_to_all x2, waiting for transfers between devices, local(): lax.all_to_all(modes.reshape(devices, rows, lanes), AXES, 0, 0, tiled=True)  9.17 us
    pallas_call x2, Pallas kernels, local(): pl.pallas_call(functools.partial(step_kernel, n_gy, step, last), out_shap...  8.11 us
    ppermute x4, waiting for transfers between devices, swap(): lax.ppermute(to_previous, axis, down)  7.92 us
    all_to_all x2, starting transfers between devices, local(): mismatch = lax.all_to_all(share, AXES, 0, 0, tiled=True)  7.72 us
    ppermute x4, starting transfers between devices, swap(): lax.ppermute(to_previous, axis, down)  5.17 us
  transfers between devices with their start and end apart: 12, of which 10 were waited for; matrix products, arithmetic and copies ran while one was open for 0% of the time, Pallas kernels for 2%

profile of v6, /device:TPU:0, one launch (start us, length us, event | category | flops | bytes accessed | tf_op | source)
XLA Modules:
  0.0 81.2 jit_solution(13286061792181690564)
XLA Ops:
  0.6 3.2 %first_modes.1 = f32[24,32,128]{2,1,0:T(8,128)} custom-call(s32[8]{0:T(128)} %levels.5, s32[2]{0:T(128)} %owners.5, f32[48,32,128]{2,1,0:T(8,128)} %bitcast.6, f32[1,2,24,4096]{3,2,1,0:T(8,128)} %rest_0_.2, bf16[8,64,96]{2,1,0:T(8,128)(2,1)} %constant.8.clone.x_fwd_all.rest_1_, bf16[4,384,128]{2,1,0:T(8,128)(2,1)} %constant.10.clone.y_fwd_all.rest_2_), custom_call_target="tpu_custom_call" | custom-call | tf_op jit(solution)/shard_map/first_modes/pallas_call | solution.py:297
  3.9 7.3 %all-to-all-start = ((f32[32,24,128]{2,1,0:T(8,128)}), f32[32,24,128]{2,1,0:T(8,128)S(1)}, u32[]{:S(2)}, u32[]{:S(2)}) async-start(f32[32,24,128]{2,1,0:T(8,128)} %bitcast.1), calls=%async_computation | async-start | bytes 786432 | tf_op jit(solution)/shard_map/all_to_all | solution.py:328
  11.2 0.0 copy-start.3
  11.2 0.0 copy-start.2
  11.2 1.3 %edges.2 = (f32[64,128]{1,0:T(8,128)S(1)}, f32[64,128]{1,0:T(8,128)S(1)}, f32[32,128]{1,0:T(8,128)S(1)}, bf16[48,192]{1,0:T(8,128)(2,1)S(1)}, bf16[384,512]{1,0:T(8,128)(2,1)S(1)}) custom-call(f32[48,32,128]{2,1,0:T(8,128)S(1)} %bitcast.7, f32[16,32,128]{2,1,0:T(8,128)S(1)} %copy-done.1, bf16[8,48,192]{2,1,0:T(8,128)(2,1)} %constant.9.clone.rest_0_, ...), custom_call_target="tpu_custom_call" | custom-call | tf_op jit(solution)/shard_map/edges/pallas_call | solution.py:315
  12.5 2.2 %collective-permute-start = (f32[64,128]{1,0:T(8,128)S(1)}, f32[64,128]{1,0:T(8,128)S(1)}, u32[]{:S(2)}, u32[]{:S(2)}) collective-permute-start(f32[64,128]{1,0:T(8,128)S(1)} %get-tuple-element.25), channel_id=1, source_target_pairs={{0,4},{4,8},{8,12},{12,16},{16,20},{20,24},{24,28},{1,5},{5,9},{9,... | collective-permute-start | bytes 98312 | tf_op jit(solution)/shard_map/ppermute | solution.py:263
  14.7 1.3 %collective-permute-start.1 = (f32[64,128]{1,0:T(8,128)S(1)}, f32[64,128]{1,0:T(8,128)S(1)}, u32[]{:S(2)}, u32[]{:S(2)}) collective-permute-start(f32[64,128]{1,0:T(8,128)S(1)} %get-tuple-element.26), channel_id=1, source_target_pairs={{4,0},{8,4},{12,8},{16,12},{20,16},{24,20},{28,24},{5,1},{9,5},{13... | collective-permute-start | bytes 98312 | tf_op jit(solution)/shard_map/ppermute | solution.py:263
  16.0 0.1 reshape.25.cuts
  16.1 2.8 %collective-permute-done.1.east = f32[64,128]{1,0:T(8,128)S(1)} collective-permute-done((f32[64,128]{1,0:T(8,128)S(1)}, f32[64,128]{1,0:T(8,128)S(1)}, u32[]{:S(2)}, u32[]{:S(2)}) %collective-permute-start.1) | collective-permute-done | bytes 32800 | tf_op jit(solution)/shard_map/ppermute | solution.py:263
  19.0 4.1 %all-to-all-done.parts = f32[32,24,128]{2,1,0:T(8,128)S(1)} async-done(((f32[32,24,128]{2,1,0:T(8,128)}), f32[32,24,128]{2,1,0:T(8,128)S(1)}, u32[]{:S(2)}, u32[]{:S(2)}) %all-to-all-start) | async-done | bytes 393248 | tf_op jit(solution)/shard_map/all_to_all | solution.py:328
  23.0 1.4 %share_sum.2 = f32[32,24,128]{2,1,0:T(8,128)} custom-call(s32[24]{0:T(128)S(1)} %reshape.25.cuts, f32[32,24,128]{2,1,0:T(8,128)S(1)} %all-to-all-done.parts), custom_call_target="tpu_custom_call" | custom-call | tf_op jit(solution)/shard_map/share_sum/pallas_call | solution.py:330
  24.4 3.9 %all-to-all-start.1 = ((f32[32,24,128]{2,1,0:T(8,128)}), f32[32,24,128]{2,1,0:T(8,128)S(1)}, u32[]{:S(2)}, u32[]{:S(2)}) async-start(f32[32,24,128]{2,1,0:T(8,128)} %share_sum.2), calls=%async_computation.1 | async-start | bytes 786432 | tf_op jit(solution)/shard_map/all_to_all | solution.py:340
  28.3 1.3 %collective-permute-start.3 = (f32[32,128]{1,0:T(8,128)S(1)}, f32[32,128]{1,0:T(8,128)S(1)}, u32[]{:S(2)}, u32[]{:S(2)}) collective-permute-start(f32[32,128]{1,0:T(8,128)S(1)} %get-tuple-element.32), channel_id=1, source_target_pairs={{1,0},{2,1},{3,2},{5,4},{6,5},{7,6},{9,8},{10,9},{11,10},{13,12},{... | collective-permute-start | bytes 49160 | tf_op jit(solution)/shard_map/ppermute | solution.py:263
  29.6 4.5 %collective-permute-start.2 = (f32[32,128]{1,0:T(8,128)S(1)}, f32[32,128]{1,0:T(8,128)S(1)}, u32[]{:S(2)}, u32[]{:S(2)}) collective-permute-start(f32[32,128]{1,0:T(8,128)S(1)} %get-tuple-element.32), channel_id=1, source_target_pairs={{0,1},{1,2},{2,3},{4,5},{5,6},{6,7},{8,9},{9,10},{10,11},{12,13},{... | collective-permute-start | bytes 49160 | tf_op jit(solution)/shard_map/ppermute | solution.py:263
  34.1 1.1 %collective-permute-done.3.north = f32[32,128]{1,0:T(8,128)S(1)} collective-permute-done((f32[32,128]{1,0:T(8,128)S(1)}, f32[32,128]{1,0:T(8,128)S(1)}, u32[]{:S(2)}, u32[]{:S(2)}) %collective-permute-start.3) | collective-permute-done | bytes 16416 | tf_op jit(solution)/shard_map/ppermute | solution.py:263
  35.2 0.5 collective-permute-done.2.south
  35.7 4.6 %all-to-all-done.1 = f32[32,24,128]{2,1,0:T(8,128)S(1)} async-done(((f32[32,24,128]{2,1,0:T(8,128)}), f32[32,24,128]{2,1,0:T(8,128)S(1)}, u32[]{:S(2)}, u32[]{:S(2)}) %all-to-all-start.1) | async-done | bytes 393248 | tf_op jit(solution)/shard_map/all_to_all | solution.py:340
  40.3 4.7 %inner_step.1 = (f32[48,32,128]{2,1,0:T(8,128)S(1)}, f32[16,32,128]{2,1,0:T(8,128)S(1)}, f32[24,32,128]{2,1,0:T(8,128)}) custom-call(s32[8]{0:T(128)} %levels.5, s32[2]{0:T(128)} %owners.5, f32[768,128]{1,0:T(8,128)S(1)} %bitcast.9, f32[48,32,128]{2,1,0:T(8,128)S(1)} %bitcast.8, f32[16,32,128]{2,1,0:T(8,128)S(1)} %copy-done.1, f32[16,32,128]{2,1,0:T(8,128)S(1)} %copy-done.2, ...), custom_call_target="tpu_custom_call" | custom-call | tf_op jit(solution)/shard_map/inner_step/pallas_call | solution.py:347
  45.0 3.8 %all-to-all-start.2 = ((f32[32,24,128]{2,1,0:T(8,128)}), f32[32,24,128]{2,1,0:T(8,128)S(1)}, u32[]{:S(2)}, u32[]{:S(2)}) async-start(f32[32,24,128]{2,1,0:T(8,128)} %bitcast.3), calls=%async_computation.2 | async-start | bytes 786432 | tf_op jit(solution)/shard_map/all_to_all | solution.py:328
  48.8 0.3 edges.3
  49.1 2.2 %collective-permute-start.4 = (f32[64,128]{1,0:T(8,128)S(1)}, f32[64,128]{1,0:T(8,128)S(1)}, u32[]{:S(2)}, u32[]{:S(2)}) collective-permute-start(f32[64,128]{1,0:T(8,128)S(1)} %get-tuple-element.38), channel_id=1, source_target_pairs={{0,4},{4,8},{8,12},{12,16},{16,20},{20,24},{24,28},{1,5},{5,9},{9,... | collective-permute-start | bytes 98312 | tf_op jit(solution)/shard_map/ppermute | solution.py:263
  51.3 1.3 %collective-permute-start.5 = (f32[64,128]{1,0:T(8,128)S(1)}, f32[64,128]{1,0:T(8,128)S(1)}, u32[]{:S(2)}, u32[]{:S(2)}) collective-permute-start(f32[64,128]{1,0:T(8,128)S(1)} %get-tuple-element.39), channel_id=1, source_target_pairs={{4,0},{8,4},{12,8},{16,12},{20,16},{24,20},{28,24},{5,1},{9,5},{13... | collective-permute-start | bytes 98312 | tf_op jit(solution)/shard_map/ppermute | solution.py:263
  52.6 2.9 %collective-permute-done.5.east = f32[64,128]{1,0:T(8,128)S(1)} collective-permute-done((f32[64,128]{1,0:T(8,128)S(1)}, f32[64,128]{1,0:T(8,128)S(1)}, u32[]{:S(2)}, u32[]{:S(2)}) %collective-permute-start.5) | collective-permute-done | bytes 32800 | tf_op jit(solution)/shard_map/ppermute | solution.py:263
  55.5 5.1 %all-to-all-done.2.parts = f32[32,24,128]{2,1,0:T(8,128)S(1)} async-done(((f32[32,24,128]{2,1,0:T(8,128)}), f32[32,24,128]{2,1,0:T(8,128)S(1)}, u32[]{:S(2)}, u32[]{:S(2)}) %all-to-all-start.2) | async-done | bytes 393248 | tf_op jit(solution)/shard_map/all_to_all | solution.py:328
  60.6 1.4 %share_sum.3 = f32[32,24,128]{2,1,0:T(8,128)} custom-call(s32[24]{0:T(128)S(1)} %reshape.25.cuts, f32[32,24,128]{2,1,0:T(8,128)S(1)} %all-to-all-done.2.parts), custom_call_target="tpu_custom_call" | custom-call | tf_op jit(solution)/shard_map/share_sum/pallas_call | solution.py:330
  62.0 3.9 %all-to-all-start.3 = ((f32[32,24,128]{2,1,0:T(8,128)}), f32[32,24,128]{2,1,0:T(8,128)S(1)}, u32[]{:S(2)}, u32[]{:S(2)}) async-start(f32[32,24,128]{2,1,0:T(8,128)} %share_sum.3), calls=%async_computation.3 | async-start | bytes 786432 | tf_op jit(solution)/shard_map/all_to_all | solution.py:340
  65.8 1.3 %collective-permute-start.7 = (f32[32,128]{1,0:T(8,128)S(1)}, f32[32,128]{1,0:T(8,128)S(1)}, u32[]{:S(2)}, u32[]{:S(2)}) collective-permute-start(f32[32,128]{1,0:T(8,128)S(1)} %get-tuple-element.45), channel_id=1, source_target_pairs={{1,0},{2,1},{3,2},{5,4},{6,5},{7,6},{9,8},{10,9},{11,10},{13,12},{... | collective-permute-start | bytes 49160 | tf_op jit(solution)/shard_map/ppermute | solution.py:263
  67.1 4.5 %collective-permute-start.6 = (f32[32,128]{1,0:T(8,128)S(1)}, f32[32,128]{1,0:T(8,128)S(1)}, u32[]{:S(2)}, u32[]{:S(2)}) collective-permute-start(f32[32,128]{1,0:T(8,128)S(1)} %get-tuple-element.45), channel_id=1, source_target_pairs={{0,1},{1,2},{2,3},{4,5},{5,6},{6,7},{8,9},{9,10},{10,11},{12,13},{... | collective-permute-start | bytes 49160 | tf_op jit(solution)/shard_map/ppermute | solution.py:263
  71.7 1.1 %collective-permute-done.7.north = f32[32,128]{1,0:T(8,128)S(1)} collective-permute-done((f32[32,128]{1,0:T(8,128)S(1)}, f32[32,128]{1,0:T(8,128)S(1)}, u32[]{:S(2)}, u32[]{:S(2)}) %collective-permute-start.7) | collective-permute-done | bytes 16416 | tf_op jit(solution)/shard_map/ppermute | solution.py:263
  72.8 0.5 collective-permute-done.6.south
  73.2 4.6 %all-to-all-done.3 = f32[32,24,128]{2,1,0:T(8,128)S(1)} async-done(((f32[32,24,128]{2,1,0:T(8,128)}), f32[32,24,128]{2,1,0:T(8,128)S(1)}, u32[]{:S(2)}, u32[]{:S(2)}) %all-to-all-start.3) | async-done | bytes 393248 | tf_op jit(solution)/shard_map/all_to_all | solution.py:340
  77.8 3.4 %final_step.1 = (f32[48,32,128]{2,1,0:T(8,128)}, f32[16,32,128]{2,1,0:T(8,128)}) custom-call(s32[8]{0:T(128)} %levels.5, s32[2]{0:T(128)} %owners.5, f32[768,128]{1,0:T(8,128)S(1)} %bitcast.10, f32[48,32,128]{2,1,0:T(8,128)S(1)} %get-tuple-element.36.fields, f32[16,32,128]{2,1,0:T(8,128)S(1)} %get-tuple-element.37.plume, f32[16,32,128]{2,1,0:T(8,128)S(1)} %copy-done.2, ...), custom_call_target="tpu_custom_call" | custom-call | tf_op jit(solution)/shard_map/final_step/pallas_call | solution.py:347
  (8 shorter events, 0.0 us)
Async XLA Ops:
  0.6 10.6 %copy-start = (f32[3,16,32,128]{3,2,1,0:T(8,128)S(1)}, f32[3,16,32,128]{3,2,1,0:T(8,128)}, u32[]{:S(2)}) copy-start(f32[3,16,32,128]{3,2,1,0:T(8,128)} %param.11) | copy-start | bytes 2359300
  0.6 10.6 %copy-start.1 = (f32[16,32,128]{2,1,0:T(8,128)S(1)}, f32[16,32,128]{2,1,0:T(8,128)}, u32[]{:S(2)}) copy-start(f32[16,32,128]{2,1,0:T(8,128)} %plume.3) | copy-start | bytes 786436
  3.9 19.1 %all-to-all-start = ((f32[32,24,128]{2,1,0:T(8,128)}), f32[32,24,128]{2,1,0:T(8,128)S(1)}, u32[]{:S(2)}, u32[]{:S(2)}) async-start(f32[32,24,128]{2,1,0:T(8,128)} %bitcast.1), calls=%async_computation | async-start | bytes 786432 | tf_op jit(solution)/shard_map/all_to_all | solution.py:328
  11.2 4.8 %copy-start.3 = (s32[3,8]{1,0:T(4,128)S(1)}, s32[3,8]{1,0:T(4,128)}, u32[]{:S(2)}) copy-start(s32[3,8]{1,0:T(4,128)} %param.13) | copy-start | bytes 292
  11.2 29.0 %copy-start.2 = (f32[16,32,128]{2,1,0:T(8,128)S(1)}, f32[16,32,128]{2,1,0:T(8,128)}, u32[]{:S(2)}) copy-start(f32[16,32,128]{2,1,0:T(8,128)} %source.3) | copy-start | bytes 786436
  12.5 3.6 %collective-permute-start = (f32[64,128]{1,0:T(8,128)S(1)}, f32[64,128]{1,0:T(8,128)S(1)}, u32[]{:S(2)}, u32[]{:S(2)}) collective-permute-start(f32[64,128]{1,0:T(8,128)S(1)} %get-tuple-element.25), channel_id=1, source_target_pairs={{0,4},{4,8},{8,12},{12,16},{16,20},{20,24},{24,28},{1,5},{5,9},{9,... | collective-permute-start | bytes 98312 | tf_op jit(solution)/shard_map/ppermute | solution.py:263
  14.7 4.2 %collective-permute-start.1 = (f32[64,128]{1,0:T(8,128)S(1)}, f32[64,128]{1,0:T(8,128)S(1)}, u32[]{:S(2)}, u32[]{:S(2)}) collective-permute-start(f32[64,128]{1,0:T(8,128)S(1)} %get-tuple-element.26), channel_id=1, source_target_pairs={{4,0},{8,4},{12,8},{16,12},{20,16},{24,20},{28,24},{5,1},{9,5},{13... | collective-permute-start | bytes 98312 | tf_op jit(solution)/shard_map/ppermute | solution.py:263
  24.4 15.9 %all-to-all-start.1 = ((f32[32,24,128]{2,1,0:T(8,128)}), f32[32,24,128]{2,1,0:T(8,128)S(1)}, u32[]{:S(2)}, u32[]{:S(2)}) async-start(f32[32,24,128]{2,1,0:T(8,128)} %share_sum.2), calls=%async_computation.1 | async-start | bytes 786432 | tf_op jit(solution)/shard_map/all_to_all | solution.py:340
  28.3 6.9 %collective-permute-start.3 = (f32[32,128]{1,0:T(8,128)S(1)}, f32[32,128]{1,0:T(8,128)S(1)}, u32[]{:S(2)}, u32[]{:S(2)}) collective-permute-start(f32[32,128]{1,0:T(8,128)S(1)} %get-tuple-element.32), channel_id=1, source_target_pairs={{1,0},{2,1},{3,2},{5,4},{6,5},{7,6},{9,8},{10,9},{11,10},{13,12},{... | collective-permute-start | bytes 49160 | tf_op jit(solution)/shard_map/ppermute | solution.py:263
  29.6 6.1 %collective-permute-start.2 = (f32[32,128]{1,0:T(8,128)S(1)}, f32[32,128]{1,0:T(8,128)S(1)}, u32[]{:S(2)}, u32[]{:S(2)}) collective-permute-start(f32[32,128]{1,0:T(8,128)S(1)} %get-tuple-element.32), channel_id=1, source_target_pairs={{0,1},{1,2},{2,3},{4,5},{5,6},{6,7},{8,9},{9,10},{10,11},{12,13},{... | collective-permute-start | bytes 49160 | tf_op jit(solution)/shard_map/ppermute | solution.py:263
  45.0 15.6 %all-to-all-start.2 = ((f32[32,24,128]{2,1,0:T(8,128)}), f32[32,24,128]{2,1,0:T(8,128)S(1)}, u32[]{:S(2)}, u32[]{:S(2)}) async-start(f32[32,24,128]{2,1,0:T(8,128)} %bitcast.3), calls=%async_computation.2 | async-start | bytes 786432 | tf_op jit(solution)/shard_map/all_to_all | solution.py:328
  49.1 3.5 %collective-permute-start.4 = (f32[64,128]{1,0:T(8,128)S(1)}, f32[64,128]{1,0:T(8,128)S(1)}, u32[]{:S(2)}, u32[]{:S(2)}) collective-permute-start(f32[64,128]{1,0:T(8,128)S(1)} %get-tuple-element.38), channel_id=1, source_target_pairs={{0,4},{4,8},{8,12},{12,16},{16,20},{20,24},{24,28},{1,5},{5,9},{9,... | collective-permute-start | bytes 98312 | tf_op jit(solution)/shard_map/ppermute | solution.py:263
  51.3 4.2 %collective-permute-start.5 = (f32[64,128]{1,0:T(8,128)S(1)}, f32[64,128]{1,0:T(8,128)S(1)}, u32[]{:S(2)}, u32[]{:S(2)}) collective-permute-start(f32[64,128]{1,0:T(8,128)S(1)} %get-tuple-element.39), channel_id=1, source_target_pairs={{4,0},{8,4},{12,8},{16,12},{20,16},{24,20},{28,24},{5,1},{9,5},{13... | collective-permute-start | bytes 98312 | tf_op jit(solution)/shard_map/ppermute | solution.py:263
  62.0 15.9 %all-to-all-start.3 = ((f32[32,24,128]{2,1,0:T(8,128)}), f32[32,24,128]{2,1,0:T(8,128)S(1)}, u32[]{:S(2)}, u32[]{:S(2)}) async-start(f32[32,24,128]{2,1,0:T(8,128)} %share_sum.3), calls=%async_computation.3 | async-start | bytes 786432 | tf_op jit(solution)/shard_map/all_to_all | solution.py:340
  65.8 6.9 %collective-permute-start.7 = (f32[32,128]{1,0:T(8,128)S(1)}, f32[32,128]{1,0:T(8,128)S(1)}, u32[]{:S(2)}, u32[]{:S(2)}) collective-permute-start(f32[32,128]{1,0:T(8,128)S(1)} %get-tuple-element.45), channel_id=1, source_target_pairs={{1,0},{2,1},{3,2},{5,4},{6,5},{7,6},{9,8},{10,9},{11,10},{13,12},{... | collective-permute-start | bytes 49160 | tf_op jit(solution)/shard_map/ppermute | solution.py:263
  67.1 6.1 %collective-permute-start.6 = (f32[32,128]{1,0:T(8,128)S(1)}, f32[32,128]{1,0:T(8,128)S(1)}, u32[]{:S(2)}, u32[]{:S(2)}) collective-permute-start(f32[32,128]{1,0:T(8,128)S(1)} %get-tuple-element.45), channel_id=1, source_target_pairs={{0,1},{1,2},{2,3},{4,5},{5,6},{6,7},{8,9},{9,10},{10,11},{12,13},{... | collective-permute-start | bytes 49160 | tf_op jit(solution)/shard_map/ppermute | solution.py:263

commit v7 on v6

--- a/solution.py
+++ b/solution.py
@@ -287,7 +287,7 @@
     def limit(mib):
         return pltpu.CompilerParams(vmem_limit_bytes=mib * 1024 * 1024)
 
-    mode_shape = f32((nudged, KX, lanes))
+    mode_shape = vmem(nudged, KX, lanes)
     parent_space = vmem(nudged, 4 * KX * KX)
     step_scratch = [vmem(total, cells_x + 2 * PAD, cells_y), vmem(field_rows, cells_x, cells_y)]
     mode_scratch = [pltpu.SemaphoreType.DMA((3,)), parent_space, table_space(x_fwd),
@@ -329,7 +329,7 @@
         parts, west, east = lax.optimization_barrier((parts, west, east))
         share = pl.pallas_call(
             functools.partial(share_kernel, n_gy, period),
-            out_shape=f32((devices, rows, lanes)),
+            out_shape=vmem(devices, rows, lanes),
             in_specs=[SMEM, VMEM],
             out_specs=VMEM,
             compiler_params=limit(4),

time: 82.6 us -> 82.6 us (level)
  no operation moved by 1% of the time
where the time goes in v7:
time: 82.6 us; the launch traced here: 81.2 us
  starting transfers between devices  37.4 us (45%)
  waiting for transfers between devices  27.2 us (33%)
  Pallas kernels  15.7 us (19%)
    ppermute x4, starting transfers between devices, swap(): lax.ppermute(to_next, axis, up)  13.4 us
    all_to_all x2, starting transfers between devices, local(): lax.all_to_all(modes.reshape(devices, rows, lanes), AXES, 0, 0, tiled=True)  11.1 us
    all_to_all x2, waiting for transfers between devices, local(): mismatch = lax.all_to_all(share, AXES, 0, 0, tiled=True)  9.17 us
    all_to_all x2, waiting for transfers between devices, local(): lax.all_to_all(modes.reshape(devices, rows, lanes), AXES, 0, 0, tiled=True)  9.17 us
    pallas_call x2, Pallas kernels, local(): pl.pallas_call(functools.partial(step_kernel, n_gy, step, last), out_shap...  8.12 us
    ppermute x4, waiting for transfers between devices, swap(): lax.ppermute(to_previous, axis, down)  7.92 us
    all_to_all x2, starting transfers between devices, local(): mismatch = lax.all_to_all(share, AXES, 0, 0, tiled=True)  7.72 us
    ppermute x4, starting transfers between devices, swap(): lax.ppermute(to_previous, axis, down)  5.17 us
  transfers between devices with their start and end apart: 12, of which 10 were waited for; matrix products, arithmetic and copies ran while one was open for 0% of the time, Pallas kernels for 2%

profile of v7, /device:TPU:0, one launch (start us, length us, event | category | flops | bytes accessed | tf_op | source)
XLA Modules:
  0.0 81.2 jit_solution(13286061792181690564)
XLA Ops:
  0.6 3.2 %first_modes.1 = f32[24,32,128]{2,1,0:T(8,128)} custom-call(s32[8]{0:T(128)} %levels.5, s32[2]{0:T(128)} %owners.5, f32[48,32,128]{2,1,0:T(8,128)} %bitcast.6, f32[1,2,24,4096]{3,2,1,0:T(8,128)} %rest_0_.2, bf16[8,64,96]{2,1,0:T(8,128)(2,1)} %constant.8.clone.x_fwd_all.rest_1_, bf16[4,384,128]{2,1,0:T(8,128)(2,1)} %constant.10.clone.y_fwd_all.rest_2_), custom_call_target="tpu_custom_call" | custom-call | tf_op jit(solution)/shard_map/first_modes/pallas_call | solution.py:297
  3.9 7.3 %all-to-all-start = ((f32[32,24,128]{2,1,0:T(8,128)}), f32[32,24,128]{2,1,0:T(8,128)S(1)}, u32[]{:S(2)}, u32[]{:S(2)}) async-start(f32[32,24,128]{2,1,0:T(8,128)} %bitcast.1), calls=%async_computation | async-start | bytes 786432 | tf_op jit(solution)/shard_map/all_to_all | solution.py:328
  11.2 0.0 copy-start.3
  11.2 0.0 copy-start.2
  11.2 1.3 %edges.2 = (f32[64,128]{1,0:T(8,128)S(1)}, f32[64,128]{1,0:T(8,128)S(1)}, f32[32,128]{1,0:T(8,128)S(1)}, bf16[48,192]{1,0:T(8,128)(2,1)S(1)}, bf16[384,512]{1,0:T(8,128)(2,1)S(1)}) custom-call(f32[48,32,128]{2,1,0:T(8,128)S(1)} %bitcast.7, f32[16,32,128]{2,1,0:T(8,128)S(1)} %copy-done.1, bf16[8,48,192]{2,1,0:T(8,128)(2,1)} %constant.9.clone.rest_0_, ...), custom_call_target="tpu_custom_call" | custom-call | tf_op jit(solution)/shard_map/edges/pallas_call | solution.py:315
  12.5 2.2 %collective-permute-start = (f32[64,128]{1,0:T(8,128)S(1)}, f32[64,128]{1,0:T(8,128)S(1)}, u32[]{:S(2)}, u32[]{:S(2)}) collective-permute-start(f32[64,128]{1,0:T(8,128)S(1)} %get-tuple-element.25), channel_id=1, source_target_pairs={{0,4},{4,8},{8,12},{12,16},{16,20},{20,24},{24,28},{1,5},{5,9},{9,... | collective-permute-start | bytes 98312 | tf_op jit(solution)/shard_map/ppermute | solution.py:263
  14.7 1.3 %collective-permute-start.1 = (f32[64,128]{1,0:T(8,128)S(1)}, f32[64,128]{1,0:T(8,128)S(1)}, u32[]{:S(2)}, u32[]{:S(2)}) collective-permute-start(f32[64,128]{1,0:T(8,128)S(1)} %get-tuple-element.26), channel_id=1, source_target_pairs={{4,0},{8,4},{12,8},{16,12},{20,16},{24,20},{28,24},{5,1},{9,5},{13... | collective-permute-start | bytes 98312 | tf_op jit(solution)/shard_map/ppermute | solution.py:263
  16.0 0.1 reshape.25.cuts
  16.1 2.8 %collective-permute-done.1.east = f32[64,128]{1,0:T(8,128)S(1)} collective-permute-done((f32[64,128]{1,0:T(8,128)S(1)}, f32[64,128]{1,0:T(8,128)S(1)}, u32[]{:S(2)}, u32[]{:S(2)}) %collective-permute-start.1) | collective-permute-done | bytes 32800 | tf_op jit(solution)/shard_map/ppermute | solution.py:263
  19.0 4.1 %all-to-all-done.parts = f32[32,24,128]{2,1,0:T(8,128)S(1)} async-done(((f32[32,24,128]{2,1,0:T(8,128)}), f32[32,24,128]{2,1,0:T(8,128)S(1)}, u32[]{:S(2)}, u32[]{:S(2)}) %all-to-all-start) | async-done | bytes 393248 | tf_op jit(solution)/shard_map/all_to_all | solution.py:328
  23.0 1.4 %share_sum.2 = f32[32,24,128]{2,1,0:T(8,128)} custom-call(s32[24]{0:T(128)S(1)} %reshape.25.cuts, f32[32,24,128]{2,1,0:T(8,128)S(1)} %all-to-all-done.parts), custom_call_target="tpu_custom_call" | custom-call | tf_op jit(solution)/shard_map/share_sum/pallas_call | solution.py:330
  24.4 3.9 %all-to-all-start.1 = ((f32[32,24,128]{2,1,0:T(8,128)}), f32[32,24,128]{2,1,0:T(8,128)S(1)}, u32[]{:S(2)}, u32[]{:S(2)}) async-start(f32[32,24,128]{2,1,0:T(8,128)} %share_sum.2), calls=%async_computation.1 | async-start | bytes 786432 | tf_op jit(solution)/shard_map/all_to_all | solution.py:340
  28.3 1.3 %collective-permute-start.3 = (f32[32,128]{1,0:T(8,128)S(1)}, f32[32,128]{1,0:T(8,128)S(1)}, u32[]{:S(2)}, u32[]{:S(2)}) collective-permute-start(f32[32,128]{1,0:T(8,128)S(1)} %get-tuple-element.32), channel_id=1, source_target_pairs={{1,0},{2,1},{3,2},{5,4},{6,5},{7,6},{9,8},{10,9},{11,10},{13,12},{... | collective-permute-start | bytes 49160 | tf_op jit(solution)/shard_map/ppermute | solution.py:263
  29.6 4.5 %collective-permute-start.2 = (f32[32,128]{1,0:T(8,128)S(1)}, f32[32,128]{1,0:T(8,128)S(1)}, u32[]{:S(2)}, u32[]{:S(2)}) collective-permute-start(f32[32,128]{1,0:T(8,128)S(1)} %get-tuple-element.32), channel_id=1, source_target_pairs={{0,1},{1,2},{2,3},{4,5},{5,6},{6,7},{8,9},{9,10},{10,11},{12,13},{... | collective-permute-start | bytes 49160 | tf_op jit(solution)/shard_map/ppermute | solution.py:263
  34.1 1.1 %collective-permute-done.3.north = f32[32,128]{1,0:T(8,128)S(1)} collective-permute-done((f32[32,128]{1,0:T(8,128)S(1)}, f32[32,128]{1,0:T(8,128)S(1)}, u32[]{:S(2)}, u32[]{:S(2)}) %collective-permute-start.3) | collective-permute-done | bytes 16416 | tf_op jit(solution)/shard_map/ppermute | solution.py:263
  35.2 0.5 collective-permute-done.2.south
  35.7 4.6 %all-to-all-done.1 = f32[32,24,128]{2,1,0:T(8,128)S(1)} async-done(((f32[32,24,128]{2,1,0:T(8,128)}), f32[32,24,128]{2,1,0:T(8,128)S(1)}, u32[]{:S(2)}, u32[]{:S(2)}) %all-to-all-start.1) | async-done | bytes 393248 | tf_op jit(solution)/shard_map/all_to_all | solution.py:340
  40.3 4.7 %inner_step.1 = (f32[48,32,128]{2,1,0:T(8,128)S(1)}, f32[16,32,128]{2,1,0:T(8,128)S(1)}, f32[24,32,128]{2,1,0:T(8,128)}) custom-call(s32[8]{0:T(128)} %levels.5, s32[2]{0:T(128)} %owners.5, f32[768,128]{1,0:T(8,128)S(1)} %bitcast.9, f32[48,32,128]{2,1,0:T(8,128)S(1)} %bitcast.8, f32[16,32,128]{2,1,0:T(8,128)S(1)} %copy-done.1, f32[16,32,128]{2,1,0:T(8,128)S(1)} %copy-done.2, ...), custom_call_target="tpu_custom_call" | custom-call | tf_op jit(solution)/shard_map/inner_step/pallas_call | solution.py:347
  45.0 3.8 %all-to-all-start.2 = ((f32[32,24,128]{2,1,0:T(8,128)}), f32[32,24,128]{2,1,0:T(8,128)S(1)}, u32[]{:S(2)}, u32[]{:S(2)}) async-start(f32[32,24,128]{2,1,0:T(8,128)} %bitcast.3), calls=%async_computation.2 | async-start | bytes 786432 | tf_op jit(solution)/shard_map/all_to_all | solution.py:328
  48.8 0.3 edges.3
  49.1 2.2 %collective-permute-start.4 = (f32[64,128]{1,0:T(8,128)S(1)}, f32[64,128]{1,0:T(8,128)S(1)}, u32[]{:S(2)}, u32[]{:S(2)}) collective-permute-start(f32[64,128]{1,0:T(8,128)S(1)} %get-tuple-element.38), channel_id=1, source_target_pairs={{0,4},{4,8},{8,12},{12,16},{16,20},{20,24},{24,28},{1,5},{5,9},{9,... | collective-permute-start | bytes 98312 | tf_op jit(solution)/shard_map/ppermute | solution.py:263
  51.3 1.3 %collective-permute-start.5 = (f32[64,128]{1,0:T(8,128)S(1)}, f32[64,128]{1,0:T(8,128)S(1)}, u32[]{:S(2)}, u32[]{:S(2)}) collective-permute-start(f32[64,128]{1,0:T(8,128)S(1)} %get-tuple-element.39), channel_id=1, source_target_pairs={{4,0},{8,4},{12,8},{16,12},{20,16},{24,20},{28,24},{5,1},{9,5},{13... | collective-permute-start | bytes 98312 | tf_op jit(solution)/shard_map/ppermute | solution.py:263
  52.6 2.9 %collective-permute-done.5.east = f32[64,128]{1,0:T(8,128)S(1)} collective-permute-done((f32[64,128]{1,0:T(8,128)S(1)}, f32[64,128]{1,0:T(8,128)S(1)}, u32[]{:S(2)}, u32[]{:S(2)}) %collective-permute-start.5) | collective-permute-done | bytes 32800 | tf_op jit(solution)/shard_map/ppermute | solution.py:263
  55.5 5.1 %all-to-all-done.2.parts = f32[32,24,128]{2,1,0:T(8,128)S(1)} async-done(((f32[32,24,128]{2,1,0:T(8,128)}), f32[32,24,128]{2,1,0:T(8,128)S(1)}, u32[]{:S(2)}, u32[]{:S(2)}) %all-to-all-start.2) | async-done | bytes 393248 | tf_op jit(solution)/shard_map/all_to_all | solution.py:328
  60.6 1.4 %share_sum.3 = f32[32,24,128]{2,1,0:T(8,128)} custom-call(s32[24]{0:T(128)S(1)} %reshape.25.cuts, f32[32,24,128]{2,1,0:T(8,128)S(1)} %all-to-all-done.2.parts), custom_call_target="tpu_custom_call" | custom-call | tf_op jit(solution)/shard_map/share_sum/pallas_call | solution.py:330
  62.0 3.9 %all-to-all-start.3 = ((f32[32,24,128]{2,1,0:T(8,128)}), f32[32,24,128]{2,1,0:T(8,128)S(1)}, u32[]{:S(2)}, u32[]{:S(2)}) async-start(f32[32,24,128]{2,1,0:T(8,128)} %share_sum.3), calls=%async_computation.3 | async-start | bytes 786432 | tf_op jit(solution)/shard_map/all_to_all | solution.py:340
  65.8 1.3 %collective-permute-start.7 = (f32[32,128]{1,0:T(8,128)S(1)}, f32[32,128]{1,0:T(8,128)S(1)}, u32[]{:S(2)}, u32[]{:S(2)}) collective-permute-start(f32[32,128]{1,0:T(8,128)S(1)} %get-tuple-element.45), channel_id=1, source_target_pairs={{1,0},{2,1},{3,2},{5,4},{6,5},{7,6},{9,8},{10,9},{11,10},{13,12},{... | collective-permute-start | bytes 49160 | tf_op jit(solution)/shard_map/ppermute | solution.py:263
  67.1 4.5 %collective-permute-start.6 = (f32[32,128]{1,0:T(8,128)S(1)}, f32[32,128]{1,0:T(8,128)S(1)}, u32[]{:S(2)}, u32[]{:S(2)}) collective-permute-start(f32[32,128]{1,0:T(8,128)S(1)} %get-tuple-element.45), channel_id=1, source_target_pairs={{0,1},{1,2},{2,3},{4,5},{5,6},{6,7},{8,9},{9,10},{10,11},{12,13},{... | collective-permute-start | bytes 49160 | tf_op jit(solution)/shard_map/ppermute | solution.py:263
  71.7 1.1 %collective-permute-done.7.north = f32[32,128]{1,0:T(8,128)S(1)} collective-permute-done((f32[32,128]{1,0:T(8,128)S(1)}, f32[32,128]{1,0:T(8,128)S(1)}, u32[]{:S(2)}, u32[]{:S(2)}) %collective-permute-start.7) | collective-permute-done | bytes 16416 | tf_op jit(solution)/shard_map/ppermute | solution.py:263
  72.8 0.5 collective-permute-done.6.south
  73.2 4.6 %all-to-all-done.3 = f32[32,24,128]{2,1,0:T(8,128)S(1)} async-done(((f32[32,24,128]{2,1,0:T(8,128)}), f32[32,24,128]{2,1,0:T(8,128)S(1)}, u32[]{:S(2)}, u32[]{:S(2)}) %all-to-all-start.3) | async-done | bytes 393248 | tf_op jit(solution)/shard_map/all_to_all | solution.py:340
  77.8 3.4 %final_step.1 = (f32[48,32,128]{2,1,0:T(8,128)}, f32[16,32,128]{2,1,0:T(8,128)}) custom-call(s32[8]{0:T(128)} %levels.5, s32[2]{0:T(128)} %owners.5, f32[768,128]{1,0:T(8,128)S(1)} %bitcast.10, f32[48,32,128]{2,1,0:T(8,128)S(1)} %get-tuple-element.36.fields, f32[16,32,128]{2,1,0:T(8,128)S(1)} %get-tuple-element.37.plume, f32[16,32,128]{2,1,0:T(8,128)S(1)} %copy-done.2, ...), custom_call_target="tpu_custom_call" | custom-call | tf_op jit(solution)/shard_map/final_step/pallas_call | solution.py:347
  (8 shorter events, 0.0 us)
Async XLA Ops:
  0.6 10.6 %copy-start = (f32[3,16,32,128]{3,2,1,0:T(8,128)S(1)}, f32[3,16,32,128]{3,2,1,0:T(8,128)}, u32[]{:S(2)}) copy-start(f32[3,16,32,128]{3,2,1,0:T(8,128)} %param.11) | copy-start | bytes 2359300
  0.6 10.6 %copy-start.1 = (f32[16,32,128]{2,1,0:T(8,128)S(1)}, f32[16,32,128]{2,1,0:T(8,128)}, u32[]{:S(2)}) copy-start(f32[16,32,128]{2,1,0:T(8,128)} %plume.3) | copy-start | bytes 786436
  3.9 19.1 %all-to-all-start = ((f32[32,24,128]{2,1,0:T(8,128)}), f32[32,24,128]{2,1,0:T(8,128)S(1)}, u32[]{:S(2)}, u32[]{:S(2)}) async-start(f32[32,24,128]{2,1,0:T(8,128)} %bitcast.1), calls=%async_computation | async-start | bytes 786432 | tf_op jit(solution)/shard_map/all_to_all | solution.py:328
  11.2 4.8 %copy-start.3 = (s32[3,8]{1,0:T(4,128)S(1)}, s32[3,8]{1,0:T(4,128)}, u32[]{:S(2)}) copy-start(s32[3,8]{1,0:T(4,128)} %param.13) | copy-start | bytes 292
  11.2 29.0 %copy-start.2 = (f32[16,32,128]{2,1,0:T(8,128)S(1)}, f32[16,32,128]{2,1,0:T(8,128)}, u32[]{:S(2)}) copy-start(f32[16,32,128]{2,1,0:T(8,128)} %source.3) | copy-start | bytes 786436
  12.5 3.6 %collective-permute-start = (f32[64,128]{1,0:T(8,128)S(1)}, f32[64,128]{1,0:T(8,128)S(1)}, u32[]{:S(2)}, u32[]{:S(2)}) collective-permute-start(f32[64,128]{1,0:T(8,128)S(1)} %get-tuple-element.25), channel_id=1, source_target_pairs={{0,4},{4,8},{8,12},{12,16},{16,20},{20,24},{24,28},{1,5},{5,9},{9,... | collective-permute-start | bytes 98312 | tf_op jit(solution)/shard_map/ppermute | solution.py:263
  14.7 4.2 %collective-permute-start.1 = (f32[64,128]{1,0:T(8,128)S(1)}, f32[64,128]{1,0:T(8,128)S(1)}, u32[]{:S(2)}, u32[]{:S(2)}) collective-permute-start(f32[64,128]{1,0:T(8,128)S(1)} %get-tuple-element.26), channel_id=1, source_target_pairs={{4,0},{8,4},{12,8},{16,12},{20,16},{24,20},{28,24},{5,1},{9,5},{13... | collective-permute-start | bytes 98312 | tf_op jit(solution)/shard_map/ppermute | solution.py:263
  24.4 15.9 %all-to-all-start.1 = ((f32[32,24,128]{2,1,0:T(8,128)}), f32[32,24,128]{2,1,0:T(8,128)S(1)}, u32[]{:S(2)}, u32[]{:S(2)}) async-start(f32[32,24,128]{2,1,0:T(8,128)} %share_sum.2), calls=%async_computation.1 | async-start | bytes 786432 | tf_op jit(solution)/shard_map/all_to_all | solution.py:340
  28.3 6.9 %collective-permute-start.3 = (f32[32,128]{1,0:T(8,128)S(1)}, f32[32,128]{1,0:T(8,128)S(1)}, u32[]{:S(2)}, u32[]{:S(2)}) collective-permute-start(f32[32,128]{1,0:T(8,128)S(1)} %get-tuple-element.32), channel_id=1, source_target_pairs={{1,0},{2,1},{3,2},{5,4},{6,5},{7,6},{9,8},{10,9},{11,10},{13,12},{... | collective-permute-start | bytes 49160 | tf_op jit(solution)/shard_map/ppermute | solution.py:263
  29.6 6.1 %collective-permute-start.2 = (f32[32,128]{1,0:T(8,128)S(1)}, f32[32,128]{1,0:T(8,128)S(1)}, u32[]{:S(2)}, u32[]{:S(2)}) collective-permute-start(f32[32,128]{1,0:T(8,128)S(1)} %get-tuple-element.32), channel_id=1, source_target_pairs={{0,1},{1,2},{2,3},{4,5},{5,6},{6,7},{8,9},{9,10},{10,11},{12,13},{... | collective-permute-start | bytes 49160 | tf_op jit(solution)/shard_map/ppermute | solution.py:263
  45.0 15.6 %all-to-all-start.2 = ((f32[32,24,128]{2,1,0:T(8,128)}), f32[32,24,128]{2,1,0:T(8,128)S(1)}, u32[]{:S(2)}, u32[]{:S(2)}) async-start(f32[32,24,128]{2,1,0:T(8,128)} %bitcast.3), calls=%async_computation.2 | async-start | bytes 786432 | tf_op jit(solution)/shard_map/all_to_all | solution.py:328
  49.1 3.5 %collective-permute-start.4 = (f32[64,128]{1,0:T(8,128)S(1)}, f32[64,128]{1,0:T(8,128)S(1)}, u32[]{:S(2)}, u32[]{:S(2)}) collective-permute-start(f32[64,128]{1,0:T(8,128)S(1)} %get-tuple-element.38), channel_id=1, source_target_pairs={{0,4},{4,8},{8,12},{12,16},{16,20},{20,24},{24,28},{1,5},{5,9},{9,... | collective-permute-start | bytes 98312 | tf_op jit(solution)/shard_map/ppermute | solution.py:263
  51.3 4.2 %collective-permute-start.5 = (f32[64,128]{1,0:T(8,128)S(1)}, f32[64,128]{1,0:T(8,128)S(1)}, u32[]{:S(2)}, u32[]{:S(2)}) collective-permute-start(f32[64,128]{1,0:T(8,128)S(1)} %get-tuple-element.39), channel_id=1, source_target_pairs={{4,0},{8,4},{12,8},{16,12},{20,16},{24,20},{28,24},{5,1},{9,5},{13... | collective-permute-start | bytes 98312 | tf_op jit(solution)/shard_map/ppermute | solution.py:263
  62.0 15.9 %all-to-all-start.3 = ((f32[32,24,128]{2,1,0:T(8,128)}), f32[32,24,128]{2,1,0:T(8,128)S(1)}, u32[]{:S(2)}, u32[]{:S(2)}) async-start(f32[32,24,128]{2,1,0:T(8,128)} %share_sum.3), calls=%async_computation.3 | async-start | bytes 786432 | tf_op jit(solution)/shard_map/all_to_all | solution.py:340
  65.8 6.9 %collective-permute-start.7 = (f32[32,128]{1,0:T(8,128)S(1)}, f32[32,128]{1,0:T(8,128)S(1)}, u32[]{:S(2)}, u32[]{:S(2)}) collective-permute-start(f32[32,128]{1,0:T(8,128)S(1)} %get-tuple-element.45), channel_id=1, source_target_pairs={{1,0},{2,1},{3,2},{5,4},{6,5},{7,6},{9,8},{10,9},{11,10},{13,12},{... | collective-permute-start | bytes 49160 | tf_op jit(solution)/shard_map/ppermute | solution.py:263
  67.1 6.1 %collective-permute-start.6 = (f32[32,128]{1,0:T(8,128)S(1)}, f32[32,128]{1,0:T(8,128)S(1)}, u32[]{:S(2)}, u32[]{:S(2)}) collective-permute-start(f32[32,128]{1,0:T(8,128)S(1)} %get-tuple-element.45), channel_id=1, source_target_pairs={{0,1},{1,2},{2,3},{4,5},{5,6},{6,7},{8,9},{9,10},{10,11},{12,13},{... | collective-permute-start | bytes 49160 | tf_op jit(solution)/shard_map/ppermute | solution.py:263

commit v8 on v7

v8 whole, which is shorter than its diff:
```python
import functools
import math

import jax
import jax.numpy as jnp
import ml_dtypes
import numpy as np
from jax import lax
from jax.experimental import pallas as pl
from jax.experimental.pallas import tpu as pltpu
from jax.sharding import PartitionSpec as P

KX = 32
STEPS = 2
GROUP = 4
LANES = GROUP * KX
PAD = 8
VMEM = pl.BlockSpec(memory_space=pltpu.VMEM)
SMEM = pl.BlockSpec(memory_space=pltpu.SMEM)
HBM = pl.BlockSpec(memory_space=pltpu.HBM)
AXES = ("gx", "gy")


def in_hbm(array):
    return pltpu.with_memory_space_constraint(array, pltpu.HBM)


def wave_table(positions, period):
    wavenum = np.arange(KX)[:, None]
    phase = (wavenum * positions[None, :] % period) * (2.0 * math.pi / period)
    inside = (positions >= 0) & (positions < period)
    return np.concatenate([np.cos(phase), np.sin(phase)], axis=0) * inside[None, :]


def split(a):
    head = a.astype(jnp.bfloat16)
    return head, (a - head.astype(jnp.float32)).astype(jnp.bfloat16)


def split_table(table, axis, order):
    head = table.astype(ml_dtypes.bfloat16)
    rest = (table - head.astype(np.float64)).astype(ml_dtypes.bfloat16)
    return np.concatenate([head if part == "h" else rest for part in order], axis=axis)


def per_slab(table):
    return np.kron(np.eye(GROUP), table)


def build_tables(n_gx, n_gy, cells_x, cells_y):
    period_x, period_y = n_gx * cells_x, n_gy * cells_y
    scaling = 1.0 / math.sqrt(period_x * period_y)
    parity = [np.arange(p, 2 * KX, 2) for p in range(2)]
    x_fwd, y_fwd, y_back, inner, outer = [], [], [], [], []
    for g in range(n_gx):
        first = g * cells_x
        table = wave_table(first + np.arange(cells_x), period_x)
        x_fwd.append(split_table(
            np.concatenate([per_slab(table[rows].T) for rows in parity], axis=1), 0, "hhl"))
        beside = wave_table(np.array([first - 1, first + cells_x]), period_x)
        inner.append(np.concatenate([per_slab(table[rows]) for rows in parity], axis=0))
        outer.append(np.concatenate([per_slab(beside[rows]) for rows in parity], axis=0))
    spare = -(2 * GROUP * n_gx) % LANES
    x_back = np.concatenate(inner + outer + [np.zeros((2 * LANES, spare))], axis=1)
    for g in range(n_gy):
        first = g * cells_y
        table = wave_table(first + np.arange(cells_y), period_y)
        edge = np.zeros((2 * KX, cells_y))
        edge[:, [0, -1]] = wave_table(np.array([first - 1, first + cells_y]), period_y)
        y_fwd.append(split_table(table * scaling, 1, "hlh"))
        y_back.append(split_table(np.concatenate([table, edge], axis=1), 0, "hhl"))
    return [np.stack(x_fwd), np.stack(y_fwd), np.stack(y_back), split_table(x_back, 0, "hhl")]


def data_dot(a, table):
    head, rest = split(a)
    return jnp.dot(
        jnp.concatenate([head, rest, head], axis=1), table, preferred_element_type=jnp.float32
    )


def columns_dot(a, table):
    head, rest = split(a)
    stacked = jnp.concatenate([head, rest, head], axis=0)
    return lax.dot_general(
        stacked, table, (((0,), (0,)), ((), ())), preferred_element_type=jnp.float32)


def emit_modes(read, parent, is_owner, x_fwd, y_fwd, modes, turned, work):
    devices, rows = modes.shape[0], modes.shape[1] // 2
    slabs = parent.shape[0]
    groups = slabs // GROUP
    head, rest = split(jnp.concatenate([read(c) for c in range(slabs)], axis=0))
    half = lax.dot_general(
        y_fwd, jnp.concatenate([head, head, rest], axis=1), (((1,), (1,)), ((), ())),
        preferred_element_type=jnp.float32)
    half = jnp.concatenate([half[:, t * LANES : (t + 1) * LANES] for t in range(groups)], axis=0)
    count = groups * 2 * KX
    work[0:count] = -data_dot(half, x_fwd)
    if count < devices * rows:
        work[count:] = jnp.zeros((devices * rows - count, 2 * LANES), jnp.float32)

    @pl.when(is_owner)
    def _():
        for i in range(KX):
            turned[:, i, :] = parent[:, i * LANES : (i + 1) * LANES]
        for t in range(groups):
            block = turned[t * GROUP : (t + 1) * GROUP].reshape(LANES, LANES).T
            span = slice(t * 2 * KX, (t + 1) * 2 * KX)
            for p in range(2):
                work[span, p * LANES : (p + 1) * LANES] += block[p * 2 * KX : (p + 1) * 2 * KX]

    for d in range(devices):
        for p in range(2):
            modes[d, p * rows : (p + 1) * rows, :] = work[
                d * rows : (d + 1) * rows, p * LANES : (p + 1) * LANES]


def fetch_all(sems, pairs):
    copies = [pltpu.make_async_copy(a, b, sems.at[i]) for i, (a, b) in enumerate(pairs)]
    for copy in copies:
        copy.start()
    return copies


def slab_of(levels, c, level_count, level_total):
    return (c // level_count) * level_total + levels[c % level_count]


def first_kernel(n_gy, level_total, levels, owners, fields_all, parent_all, x_fwd_all, y_fwd_all,
                 modes, fields, sems, parent, x_fwd, y_fwd, turned, work):
    gx, gy = lax.axis_index("gx"), lax.axis_index("gy")
    copies = fetch_all(sems, [
        (fields_all, fields), (x_fwd_all.at[gx], x_fwd), (y_fwd_all.at[gy], y_fwd),
        (parent_all.at[0, 0], parent)])
    for copy in copies:
        copy.wait()
    level_count = parent.shape[0] // 3
    emit_modes(
        lambda c: fields[slab_of(levels, c, level_count, level_total)],
        parent, owners[0] == gx * n_gy + gy, x_fwd[...], y_fwd[...], modes, turned, work,
    )


def edge_kernel(fields, plume, *rest):
    copies = []
    if len(rest) > 3:
        y_back_all, west, east, cols, y_back, sems = rest
        copies = fetch_all(sems, [(y_back_all.at[lax.axis_index("gy")], y_back)])
    else:
        west, east, cols = rest
    cells_x, cells_y = plume.shape[1:]
    field_rows = fields.shape[0]
    lane = lax.broadcasted_iota(jnp.int32, cols.shape, 1)
    acc = jnp.zeros(cols.shape, jnp.float32)
    for c in range(field_rows + plume.shape[0]):
        a = fields[c] if c < field_rows else plume[c - field_rows]
        west[c : c + 1, :] = a[:1]
        east[c : c + 1, :] = a[cells_x - 1 :]
        acc = jnp.where(lane // 2 == c, pltpu.roll(a, 2 * c + 1, 1), acc)
    cols[...] = acc
    for copy in copies:
        copy.wait()


def beside_rows(rows):
    return -(-rows // 3)


def share_kernel(n_gx, n_gy, period, cuts, parts, x_back, out):
    devices = parts.shape[0]
    rows = parts.shape[1] // 2
    me = lax.axis_index("gx") * n_gy + lax.axis_index("gy")
    total = parts[0]
    for d in range(1, devices):
        total = total + parts[d]
    shape = total.shape
    place = lax.broadcasted_iota(jnp.int32, shape, 0)
    lane = lax.broadcasted_iota(jnp.int32, shape, 1)
    p = (place >= rows).astype(jnp.int32)
    row = me * rows + place - p * rows
    k = 2 * (lane % KX) + p
    j = row % (2 * KX)
    slab = GROUP * (row // (2 * KX)) + lane // KX
    limit = jnp.zeros(shape, jnp.int32)
    for c in range(cuts.shape[0]):
        limit = jnp.where(slab == c, cuts[c], limit)
    keep = ((k % KX) < limit) & ((j % KX) < limit)
    factor = jnp.where(k == 0, 1.0, 2.0) * jnp.where(j == 0, 1.0, 2.0) * (1.0 / math.sqrt(period))
    mismatch = jnp.where(keep, total * factor, 0.0)
    both = jnp.concatenate([mismatch[:rows], mismatch[rows:]], axis=1)
    spare = -rows % 16
    if spare:
        both = jnp.concatenate([both, jnp.zeros((spare, 2 * LANES), jnp.float32)], axis=0)
    half = data_dot(both, x_back[...])
    packed = beside_rows(rows)
    width = 2 * GROUP
    spot = lax.broadcasted_iota(jnp.int32, (packed, LANES), 1) // width
    for g in range(n_gx):
        first = (n_gx + g * width // LANES) * LANES
        edge = half[:, first : first + LANES]
        beside = jnp.zeros((packed, LANES), jnp.float32)
        for m in range(3):
            piece = edge[m * packed : (m + 1) * packed]
            beside = jnp.where(
                spot == m, pltpu.roll(piece, (m - g) * width % LANES, 1), beside)
        for h in range(n_gy):
            out[g * n_gy + h, :rows, :] = half[:rows, g * LANES : (g + 1) * LANES]
            out[g * n_gy + h, rows:, :] = beside


def step_kernel(n_gy, step, last, levels, owners, shares, fields, plume, source,
                west, east, south, north, y_back, *rest):
    gx, gy = lax.axis_index("gx"), lax.axis_index("gy")
    copies = []
    if last:
        fields_out, plume_out, slabs, beside, spread, spread_edges = rest
    else:
        (parent_all, x_fwd_all, y_fwd_all, fields_out, plume_out, modes,
         slabs, beside, spread, spread_edges, sems, parent, x_fwd, y_fwd, turned, work) = rest
        copies = fetch_all(sems, [(x_fwd_all.at[gx], x_fwd), (y_fwd_all.at[gy], y_fwd),
                                  (parent_all.at[0, step + 1], parent)])
    level_total, cells_x, cells_y = plume.shape
    field_rows = fields.shape[0]
    total = field_rows + level_total
    level_count = levels.shape[0]
    nudged = 3 * level_count
    inner = slice(PAD, PAD + cells_x)
    for c in range(total):
        slabs[c, inner] = fields[c] if c < field_rows else plume[c - field_rows]
        slabs[c, PAD - 1 : PAD] = west[c : c + 1, :]
        slabs[c, PAD + cells_x : PAD + cells_x + 1] = east[c : c + 1, :]
    beside[...] = jnp.zeros_like(beside)
    devices = shares.shape[0]
    rows = spread.shape[0] // devices
    packed = beside_rows(rows)
    width = 2 * GROUP
    for d in range(devices):
        spread[d * rows : (d + 1) * rows] = shares[d, :rows, :]
        edge = shares[d, rows:, :]
        for m in range(3):
            count = min(packed, rows - m * packed)
            if count > 0:
                moved = pltpu.roll(edge, -m * width % LANES, 1) if m else edge
                start = d * rows + m * packed
                spread_edges[start : start + count] = moved[:count]
    y_table = y_back[...]
    groups = nudged // GROUP
    spot_of = lax.broadcasted_iota(jnp.int32, (2 * KX, LANES), 1) // width
    edges = jnp.zeros((2 * KX, LANES), jnp.float32)
    for t in range(groups):
        piece = spread_edges[t * 2 * KX : (t + 1) * 2 * KX]
        edges = jnp.where(spot_of == t, pltpu.roll(piece, t * width, 1) if t else piece, edges)
    update_rows = columns_dot(edges, y_table)
    for t in range(groups):
        update = columns_dot(spread[t * 2 * KX : (t + 1) * 2 * KX], y_table)
        for n in range(GROUP):
            c = t * GROUP + n
            part = update[n * cells_x : (n + 1) * cells_x]
            spot = slab_of(levels, c, level_count, level_total)
            slabs[spot, inner] += part[:, :cells_y]
            slabs[spot, PAD - 1 : PAD] += update_rows[2 * c : 2 * c + 1, :cells_y]
            slabs[spot, PAD + cells_x : PAD + cells_x + 1] += update_rows[
                2 * c + 1 : 2 * c + 2, :cells_y]
            beside[spot] = part[:, cells_y:]

    lane = lax.broadcasted_iota(jnp.int32, (cells_x, cells_y), 1)
    first, final = lane == 0, lane == cells_y - 1
    columns = jnp.where(
        lane % 2 == 0, pltpu.roll(north[...], cells_y - 1, 1), pltpu.roll(south[...], 1, 1))

    def advance(c, parts):
        centre, to_west, to_east, to_south, to_north = parts
        a = slabs[c, inner]
        column = pltpu.roll(columns, cells_y - 1 - 2 * c, 1)
        if c < field_rows:
            column = column + beside[c]
        return (
            centre * a
            + to_west * slabs[c, PAD - 1 : PAD - 1 + cells_x]
            + to_east * slabs[c, PAD + 1 : PAD + 1 + cells_x]
            + to_south * jnp.where(first, column, pltpu.roll(a, 1, 1))
            + to_north * jnp.where(final, column, pltpu.roll(a, cells_y - 1, 1))
        )

    for l in range(level_total):
        u, v = slabs[l, inner], slabs[level_total + l, inner]
        beside_parts = (
            0.1 + 0.1 * jnp.maximum(u, 0.0), 0.1 - 0.1 * jnp.minimum(u, 0.0),
            0.1 + 0.1 * jnp.maximum(v, 0.0), 0.1 - 0.1 * jnp.minimum(v, 0.0),
        )
        centre = 1.0 - (beside_parts[0] + beside_parts[1] + beside_parts[2] + beside_parts[3])
        for f in range(3):
            fields_out[f * level_total + l] = advance(
                f * level_total + l, (centre,) + beside_parts)
        settled = advance(field_rows + l, (centre - 0.3,) + beside_parts) + source[l]
        if l + 1 < level_total:
            settled = settled + 0.3 * plume[l + 1]
        plume_out[l] = settled

    if last:
        return
    for copy in copies:
        copy.wait()
    emit_modes(
        lambda c: fields_out[slab_of(levels, c, level_count, level_total)],
        parent, owners[step + 1] == gx * n_gy + gy, x_fwd[...], y_fwd[...], modes, turned, work,
    )


def swap(axis, to_next, to_previous):
    count = lax.axis_size(axis)
    up = [(i, i + 1) for i in range(count - 1)]
    down = [(b, a) for a, b in up]
    return lax.ppermute(to_next, axis, up), lax.ppermute(to_previous, axis, down)


def local(tables, fields, levels, cuts, parent_modes, owners, plume, source):
    n_gx, n_gy = lax.axis_size("gx"), lax.axis_size("gy")
    devices = n_gx * n_gy
    level_total, cells_x, cells_y = plume.shape
    period = n_gx * cells_x * n_gy * cells_y
    nudged = 3 * levels.shape[0]
    field_rows = 3 * level_total
    total = field_rows + level_total
    rows = -(-(nudged // GROUP * 2 * KX) // devices)
    flat = fields.reshape(field_rows, cells_x, cells_y)
    cuts = cuts.reshape(-1)
    f32 = functools.partial(jax.ShapeDtypeStruct, dtype=jnp.float32)
    x_fwd, y_fwd, y_back, x_back = (jnp.asarray(t) for t in tables)

    def vmem(*shape):
        return pltpu.VMEM(shape, jnp.float32)

    def table_space(table):
        return pltpu.VMEM(table.shape[1:], table.dtype)

    def limit(mib):
        return pltpu.CompilerParams(vmem_limit_bytes=mib * 1024 * 1024)

    mode_shape = f32((devices, 2 * rows, LANES))
    step_scratch = [vmem(total, cells_x + 2 * PAD, cells_y), vmem(field_rows, cells_x, cells_y),
                    vmem(devices * rows, LANES), vmem(devices * rows, LANES)]
    mode_scratch = [pltpu.SemaphoreType.DMA((4,)), vmem(nudged, 4 * KX * KX), table_space(x_fwd),
                    table_space(y_fwd), vmem(nudged, KX, LANES),
                    vmem(devices * rows, 2 * LANES)]
    levels, owners = in_hbm(levels), in_hbm(owners)

    modes = pl.pallas_call(
        functools.partial(first_kernel, n_gy, level_total),
        out_shape=mode_shape,
        in_specs=[SMEM, SMEM] + [HBM] * 4,
        out_specs=VMEM,
        scratch_shapes=[vmem(field_rows, cells_x, cells_y)] + mode_scratch,
        compiler_params=limit(8),
        name="first_modes",
    )(levels, owners, in_hbm(flat), in_hbm(parent_modes), in_hbm(x_fwd), in_hbm(y_fwd))
    for step in range(STEPS):
        last = step == STEPS - 1
        edge_shapes = [f32((total, cells_y)), f32((total, cells_y)), f32((cells_x, 2 * total))]
        edge_operands = [flat, plume]
        if step == 0:
            edge_shapes.append(jax.ShapeDtypeStruct(y_back.shape[1:], y_back.dtype))
            edge_operands.append(in_hbm(y_back))
        edges = pl.pallas_call(
            edge_kernel,
            out_shape=edge_shapes,
            in_specs=[VMEM, VMEM] + [HBM] * (len(edge_operands) - 2),
            out_specs=[VMEM] * len(edge_shapes),
            scratch_shapes=[pltpu.SemaphoreType.DMA((1,))] if step == 0 else [],
            compiler_params=limit(8),
            name="edges",
        )(*edge_operands)
        if step == 0:
            back_table = edges[3]
        to_west, to_east, cols = edges[:3]
        west, east = swap("gx", to_east, to_west)
        parts = lax.all_to_all(modes, AXES, 0, 0, tiled=True)
        parts, west, east = lax.optimization_barrier((parts, west, east))
        share = pl.pallas_call(
            functools.partial(share_kernel, n_gx, n_gy, period),
            out_shape=f32((devices, rows + beside_rows(rows), LANES)),
            in_specs=[SMEM, VMEM, VMEM],
            out_specs=VMEM,
            compiler_params=limit(12),
            name="share_sum",
        )(cuts, parts, x_back)
        share, cols = lax.optimization_barrier((share, cols))
        south, north = swap("gy", cols, cols)
        shares = lax.all_to_all(share, AXES, 0, 0, tiled=True)
        out_shape = [f32(flat.shape), f32(plume.shape)]
        operands = [levels, owners, shares, flat, plume, source, west, east, south, north,
                    back_table]
        if not last:
            out_shape.append(mode_shape)
            operands += [in_hbm(parent_modes), in_hbm(x_fwd), in_hbm(y_fwd)]
        results = pl.pallas_call(
            functools.partial(step_kernel, n_gy, step, last),
            out_shape=out_shape,
            in_specs=[SMEM, SMEM] + [VMEM] * 9 + [HBM] * (len(operands) - 11),
            out_specs=[VMEM] * len(out_shape),
            scratch_shapes=step_scratch + ([] if last else mode_scratch),
            compiler_params=limit(20),
            name="final_step" if last else "inner_step",
        )(*operands)
        if last:
            flat, plume = results
        else:
            flat, plume, modes = results
    return flat.reshape(fields.shape), plume


def solution(mesh):
    in_specs = (
        P(None, None, "gx", "gy"),
        P(),
        P(),
        P(("gx", "gy"), None, None, None),
        P(),
        P(None, "gx", "gy"),
        P(None, "gx", "gy"),
    )
    out_specs = (P(None, None, "gx", "gy"), P(None, "gx", "gy"))
    n_gx, n_gy = mesh.shape["gx"], mesh.shape["gy"]

    def whole(fields, levels, cuts, parent_modes, owners, plume, source):
        tables = build_tables(n_gx, n_gy, plume.shape[1] // n_gx, plume.shape[2] // n_gy)
        return jax.shard_map(
            functools.partial(local, tables), mesh=mesh, in_specs=in_specs, out_specs=out_specs,
            check_vma=False,
        )(fields, levels, cuts, parent_modes, owners, plume, source)

    return whole
```

time: 82.6 us -> 84.2 us (1.019)
  local copies, waits for them, and re-layouts: 0.1 us -> 6.99 us
  waiting for transfers between devices: 27.2 us -> 22.8 us
    unnamed x8 -> x26, local copies, waits for them, and re-layouts: 0.02 us -> 6.9 us
    all_to_all x4, waiting for transfers between devices: 18.3 us -> 14.2 us  [the longest x2 8.37 us: local(): parts = lax.all_to_all(modes, AXES, 0, 0, tiled=True)]
    ppermute x4, waiting for transfers between devices: 7.92 us -> 5.77 us  [swap(): lax.ppermute(to_previous, axis, down)]
    ppermute x4, waiting for transfers between devices: 0.97 us -> 2.83 us  [swap(): lax.ppermute(to_next, axis, up)]
    pallas_call x2, Pallas kernels: 8.12 us -> 6.89 us  [local(): pl.pallas_call(functools.partial(step_kernel, n_gy, step, last), out_shap...]
  transfers between devices with their start and end apart: 12 -> 12, of which waited for: 10 -> 8; matrix products, arithmetic and copies ran while one was open for 0% -> 0% of each run, Pallas kernels for 2% -> 2%
where the time goes in v8:
time: 84.2 us; the launch traced here: 83.4 us
  starting transfers between devices  37.4 us (44%)
  waiting for transfers between devices  22.8 us (27%)
  Pallas kernels  15.3 us (18%)
  local copies, waits for them, and re-layouts  6.99 us (8%)
  between operations  0.86 us (1%)
    ppermute x4, starting transfers between devices, swap(): lax.ppermute(to_next, axis, up)  13.4 us
    all_to_all x2, starting transfers between devices, local(): parts = lax.all_to_all(modes, AXES, 0, 0, tiled=True)  11 us
    all_to_all x2, waiting for transfers between devices, local(): parts = lax.all_to_all(modes, AXES, 0, 0, tiled=True)  8.37 us
    all_to_all x2, starting transfers between devices, local(): shares = lax.all_to_all(share, AXES, 0, 0, tiled=True)  7.82 us
    unnamed x26, local copies, waits for them, and re-layouts  6.9 us
    pallas_call x2, Pallas kernels, local(): pl.pallas_call(functools.partial(step_kernel, n_gy, step, last), out_shap...  6.89 us
    all_to_all x2, waiting for transfers between devices, local(): shares = lax.all_to_all(share, AXES, 0, 0, tiled=True)  5.86 us
    ppermute x4, waiting for transfers between devices, swap(): lax.ppermute(to_previous, axis, down)  5.77 us
  transfers between devices with their start and end apart: 12, of which 8 were waited for; matrix products, arithmetic and copies ran while one was open for 0% of the time, Pallas kernels for 2%

profile of v8, /device:TPU:0, one launch (start us, length us, event | category | flops | bytes accessed | tf_op | source)
XLA Modules:
  0.0 83.4 jit_solution(15713587673045555230)
XLA Ops:
  0.7 3.5 %first_modes.1 = f32[32,24,128]{2,1,0:T(8,128)} custom-call(s32[8]{0:T(128)} %levels.5, s32[2]{0:T(128)} %owners.5, f32[48,32,128]{2,1,0:T(8,128)} %bitcast.2, f32[1,2,24,4096]{3,2,1,0:T(8,128)} %rest_0_.2, bf16[8,384,256]{2,1,0:T(8,128)(2,1)} %constant.8.clone.x_fwd_all.rest_1_, bf16[4,64,384]{2,1,0:T(8,128)(2,1)} %constant.9.clone.y_fwd_all.rest_2_), custom_call_target="tpu_custom_call" | custom-call | tf_op jit(solution)/shard_map/first_modes/pallas_call | solution.py:349
  4.2 7.3 %all-to-all-start = ((f32[32,24,128]{2,1,0:T(8,128)}), f32[32,24,128]{2,1,0:T(8,128)S(1)}, u32[]{:S(2)}, u32[]{:S(2)}) async-start(f32[32,24,128]{2,1,0:T(8,128)} %first_modes.1), calls=%async_computation | async-start | bytes 786432 | tf_op jit(solution)/shard_map/all_to_all | solution.py:378
  11.5 1.2 %edges.2 = (f32[64,128]{1,0:T(8,128)S(1)}, f32[64,128]{1,0:T(8,128)S(1)}, f32[32,128]{1,0:T(8,128)S(1)}, bf16[192,256]{1,0:T(8,128)(2,1)S(1)}) custom-call(f32[48,32,128]{2,1,0:T(8,128)S(1)} %bitcast.3, f32[16,32,128]{2,1,0:T(8,128)S(1)} %copy-done.4, bf16[4,192,256]{2,1,0:T(8,128)(2,1)} %constant.10.clone.rest_0_), custom_call_target="tpu_custom_call" | custom-call | tf_op jit(solution)/shard_map/edges/pallas_call | solution.py:365
  12.7 2.2 %collective-permute-start = (f32[64,128]{1,0:T(8,128)S(1)}, f32[64,128]{1,0:T(8,128)S(1)}, u32[]{:S(2)}, u32[]{:S(2)}) collective-permute-start(f32[64,128]{1,0:T(8,128)S(1)} %get-tuple-element.24), channel_id=1, source_target_pairs={{0,4},{4,8},{8,12},{12,16},{16,20},{20,24},{24,28},{1,5},{5,9},{9,... | collective-permute-start | bytes 98312 | tf_op jit(solution)/shard_map/ppermute | solution.py:315
  14.8 1.3 %collective-permute-start.1 = (f32[64,128]{1,0:T(8,128)S(1)}, f32[64,128]{1,0:T(8,128)S(1)}, u32[]{:S(2)}, u32[]{:S(2)}) collective-permute-start(f32[64,128]{1,0:T(8,128)S(1)} %get-tuple-element.25), channel_id=1, source_target_pairs={{4,0},{8,4},{12,8},{16,12},{20,16},{24,20},{28,24},{5,1},{9,5},{13... | collective-permute-start | bytes 98312 | tf_op jit(solution)/shard_map/ppermute | solution.py:315
  16.2 2.8 %collective-permute-done.1.east = f32[64,128]{1,0:T(8,128)S(1)} collective-permute-done((f32[64,128]{1,0:T(8,128)S(1)}, f32[64,128]{1,0:T(8,128)S(1)}, u32[]{:S(2)}, u32[]{:S(2)}) %collective-permute-start.1) | collective-permute-done | bytes 32800 | tf_op jit(solution)/shard_map/ppermute | solution.py:315
  19.1 4.2 %all-to-all-done.parts = f32[32,24,128]{2,1,0:T(8,128)S(1)} async-done(((f32[32,24,128]{2,1,0:T(8,128)}), f32[32,24,128]{2,1,0:T(8,128)S(1)}, u32[]{:S(2)}, u32[]{:S(2)}) %all-to-all-start) | async-done | bytes 393248 | tf_op jit(solution)/shard_map/all_to_all | solution.py:378
  23.3 1.7 %share_sum.2 = f32[32,16,128]{2,1,0:T(8,128)} custom-call(s32[24]{0:T(128)S(1)} %reshape.13.cuts, f32[32,24,128]{2,1,0:T(8,128)S(1)} %all-to-all-done.parts, bf16[768,1152]{1,0:T(8,128)(2,1)S(1)} %copy-done.1), custom_call_target="tpu_custom_call" | custom-call | tf_op jit(solution)/shard_map/share_sum/pallas_call | solution.py:380
  25.0 4.0 %all-to-all-start.1 = ((f32[32,16,128]{2,1,0:T(8,128)}), f32[32,16,128]{2,1,0:T(8,128)S(1)}, u32[]{:S(2)}, u32[]{:S(2)}) async-start(f32[32,16,128]{2,1,0:T(8,128)} %share_sum.2), calls=%async_computation.1 | async-start | bytes 524288 | tf_op jit(solution)/shard_map/all_to_all | solution.py:390
  29.0 1.3 %collective-permute-start.3 = (f32[32,128]{1,0:T(8,128)S(1)}, f32[32,128]{1,0:T(8,128)S(1)}, u32[]{:S(2)}, u32[]{:S(2)}) collective-permute-start(f32[32,128]{1,0:T(8,128)S(1)} %get-tuple-element.31), channel_id=1, source_target_pairs={{1,0},{2,1},{3,2},{5,4},{6,5},{7,6},{9,8},{10,9},{11,10},{13,12},{... | collective-permute-start | bytes 49160 | tf_op jit(solution)/shard_map/ppermute | solution.py:315
  30.3 4.5 %collective-permute-start.2 = (f32[32,128]{1,0:T(8,128)S(1)}, f32[32,128]{1,0:T(8,128)S(1)}, u32[]{:S(2)}, u32[]{:S(2)}) collective-permute-start(f32[32,128]{1,0:T(8,128)S(1)} %get-tuple-element.31), channel_id=1, source_target_pairs={{0,1},{1,2},{2,3},{4,5},{5,6},{6,7},{8,9},{9,10},{10,11},{12,13},{... | collective-permute-start | bytes 49160 | tf_op jit(solution)/shard_map/ppermute | solution.py:315
  34.9 1.4 %collective-permute-done.2.south = f32[32,128]{1,0:T(8,128)S(1)} collective-permute-done((f32[32,128]{1,0:T(8,128)S(1)}, f32[32,128]{1,0:T(8,128)S(1)}, u32[]{:S(2)}, u32[]{:S(2)}) %collective-permute-start.2) | collective-permute-done | bytes 16416 | tf_op jit(solution)/shard_map/ppermute | solution.py:315
  36.3 2.9 %all-to-all-done.1.shares = f32[32,16,128]{2,1,0:T(8,128)S(1)} async-done(((f32[32,16,128]{2,1,0:T(8,128)}), f32[32,16,128]{2,1,0:T(8,128)S(1)}, u32[]{:S(2)}, u32[]{:S(2)}) %all-to-all-start.1) | async-done | bytes 262176 | tf_op jit(solution)/shard_map/all_to_all | solution.py:390
  39.9 0.9 %copy-done.3 = f32[32,16,128]{2,1,0:T(8,128)S(1)} copy-done((f32[32,16,128]{2,1,0:T(8,128)S(1)}, f32[32,16,128]{2,1,0:T(8,128)}, u32[]{:S(2)}) %copy-start.3) | copy-done | bytes 262168
  40.9 0.9 %copy-done.5 = f32[16,32,128]{2,1,0:T(8,128)S(1)} copy-done((f32[16,32,128]{2,1,0:T(8,128)S(1)}, f32[16,32,128]{2,1,0:T(8,128)}, u32[]{:S(2)}) %copy-start.5) | copy-done | bytes 262168
  41.8 0.9 %copy-done.6 = f32[16,32,128]{2,1,0:T(8,128)S(1)} copy-done((f32[16,32,128]{2,1,0:T(8,128)S(1)}, f32[16,32,128]{2,1,0:T(8,128)}, u32[]{:S(2)}) %copy-start.6) | copy-done | bytes 262168
  42.8 3.8 %inner_step.1 = (f32[48,32,128]{2,1,0:T(8,128)S(1)}, f32[16,32,128]{2,1,0:T(8,128)S(1)}, f32[32,24,128]{2,1,0:T(8,128)S(1)}) custom-call(s32[8]{0:T(128)} %levels.5, s32[2]{0:T(128)} %owners.5, f32[32,16,128]{2,1,0:T(8,128)S(1)} %copy-done.3, f32[48,32,128]{2,1,0:T(8,128)S(1)} %bitcast.4, f32[16,32,128]{2,1,0:T(8,128)S(1)} %copy-done.5, ...), custom_call_target="tpu_custom_call" | custom-call | tf_op jit(solution)/shard_map/inner_step/pallas_call | solution.py:397
  47.3 0.7 copy-done.11
  48.0 3.7 %all-to-all-start.2 = ((f32[32,24,128]{2,1,0:T(8,128)}), f32[32,24,128]{2,1,0:T(8,128)S(1)}, u32[]{:S(2)}, u32[]{:S(2)}) async-start(f32[32,24,128]{2,1,0:T(8,128)} %copy-done.11), calls=%async_computation.2 | async-start | bytes 786432 | tf_op jit(solution)/shard_map/all_to_all | solution.py:378
  51.7 0.9 %copy-done.9 = f32[16,32,128]{2,1,0:T(8,128)S(1)} copy-done((f32[16,32,128]{2,1,0:T(8,128)S(1)}, f32[16,32,128]{2,1,0:T(8,128)}, u32[]{:S(2)}) %copy-start.9) | copy-done | bytes 262168
  53.0 2.2 %collective-permute-start.4 = (f32[64,128]{1,0:T(8,128)S(1)}, f32[64,128]{1,0:T(8,128)S(1)}, u32[]{:S(2)}, u32[]{:S(2)}) collective-permute-start(f32[64,128]{1,0:T(8,128)S(1)} %get-tuple-element.36), channel_id=1, source_target_pairs={{0,4},{4,8},{8,12},{12,16},{16,20},{20,24},{24,28},{1,5},{5,9},{9,... | collective-permute-start | bytes 98312 | tf_op jit(solution)/shard_map/ppermute | solution.py:315
  55.1 1.3 %collective-permute-start.5 = (f32[64,128]{1,0:T(8,128)S(1)}, f32[64,128]{1,0:T(8,128)S(1)}, u32[]{:S(2)}, u32[]{:S(2)}) collective-permute-start(f32[64,128]{1,0:T(8,128)S(1)} %get-tuple-element.37), channel_id=1, source_target_pairs={{4,0},{8,4},{12,8},{16,12},{20,16},{24,20},{28,24},{5,1},{9,5},{13... | collective-permute-start | bytes 98312 | tf_op jit(solution)/shard_map/ppermute | solution.py:315
  56.5 2.9 %collective-permute-done.5.east = f32[64,128]{1,0:T(8,128)S(1)} collective-permute-done((f32[64,128]{1,0:T(8,128)S(1)}, f32[64,128]{1,0:T(8,128)S(1)}, u32[]{:S(2)}, u32[]{:S(2)}) %collective-permute-start.5) | collective-permute-done | bytes 32800 | tf_op jit(solution)/shard_map/ppermute | solution.py:315
  59.4 4.1 %all-to-all-done.2.parts = f32[32,24,128]{2,1,0:T(8,128)S(1)} async-done(((f32[32,24,128]{2,1,0:T(8,128)}), f32[32,24,128]{2,1,0:T(8,128)S(1)}, u32[]{:S(2)}, u32[]{:S(2)}) %all-to-all-start.2) | async-done | bytes 393248 | tf_op jit(solution)/shard_map/all_to_all | solution.py:378
  63.5 1.7 %share_sum.3 = f32[32,16,128]{2,1,0:T(8,128)} custom-call(s32[24]{0:T(128)S(1)} %reshape.13.cuts, f32[32,24,128]{2,1,0:T(8,128)S(1)} %all-to-all-done.2.parts, bf16[768,1152]{1,0:T(8,128)(2,1)S(1)} %copy-done.1), custom_call_target="tpu_custom_call" | custom-call | tf_op jit(solution)/shard_map/share_sum/pallas_call | solution.py:380
  65.3 3.9 %all-to-all-start.3 = ((f32[32,16,128]{2,1,0:T(8,128)}), f32[32,16,128]{2,1,0:T(8,128)S(1)}, u32[]{:S(2)}, u32[]{:S(2)}) async-start(f32[32,16,128]{2,1,0:T(8,128)} %share_sum.3), calls=%async_computation.3 | async-start | bytes 524288 | tf_op jit(solution)/shard_map/all_to_all | solution.py:390
  69.1 1.3 %collective-permute-start.7 = (f32[32,128]{1,0:T(8,128)S(1)}, f32[32,128]{1,0:T(8,128)S(1)}, u32[]{:S(2)}, u32[]{:S(2)}) collective-permute-start(f32[32,128]{1,0:T(8,128)S(1)} %get-tuple-element.43), channel_id=1, source_target_pairs={{1,0},{2,1},{3,2},{5,4},{6,5},{7,6},{9,8},{10,9},{11,10},{13,12},{... | collective-permute-start | bytes 49160 | tf_op jit(solution)/shard_map/ppermute | solution.py:315
  70.4 4.5 %collective-permute-start.6 = (f32[32,128]{1,0:T(8,128)S(1)}, f32[32,128]{1,0:T(8,128)S(1)}, u32[]{:S(2)}, u32[]{:S(2)}) collective-permute-start(f32[32,128]{1,0:T(8,128)S(1)} %get-tuple-element.43), channel_id=1, source_target_pairs={{0,1},{1,2},{2,3},{4,5},{5,6},{6,7},{8,9},{9,10},{10,11},{12,13},{... | collective-permute-start | bytes 49160 | tf_op jit(solution)/shard_map/ppermute | solution.py:315
  75.0 1.4 %collective-permute-done.6.south = f32[32,128]{1,0:T(8,128)S(1)} collective-permute-done((f32[32,128]{1,0:T(8,128)S(1)}, f32[32,128]{1,0:T(8,128)S(1)}, u32[]{:S(2)}, u32[]{:S(2)}) %collective-permute-start.6) | collective-permute-done | bytes 16416 | tf_op jit(solution)/shard_map/ppermute | solution.py:315
  76.4 2.9 %all-to-all-done.3.shares = f32[32,16,128]{2,1,0:T(8,128)S(1)} async-done(((f32[32,16,128]{2,1,0:T(8,128)}), f32[32,16,128]{2,1,0:T(8,128)S(1)}, u32[]{:S(2)}, u32[]{:S(2)}) %all-to-all-start.3) | async-done | bytes 262176 | tf_op jit(solution)/shard_map/all_to_all | solution.py:390
  79.3 0.9 %copy-done.10 = f32[16,32,128]{2,1,0:T(8,128)S(1)} copy-done((f32[16,32,128]{2,1,0:T(8,128)S(1)}, f32[16,32,128]{2,1,0:T(8,128)}, u32[]{:S(2)}) %copy-start.10) | copy-done | bytes 262168
  80.3 3.1 %final_step.1 = (f32[48,32,128]{2,1,0:T(8,128)}, f32[16,32,128]{2,1,0:T(8,128)}) custom-call(s32[8]{0:T(128)} %levels.5, s32[2]{0:T(128)} %owners.5, f32[32,16,128]{2,1,0:T(8,128)S(1)} %all-to-all-done.3.shares, f32[48,32,128]{2,1,0:T(8,128)S(1)} %get-tuple-element.34.fields, f32[16,32,128]{2,1,0:T(8,128)S(1)} %copy-done.10, f32[16,32,128]{2,1,0:T(8,128)S(1)} %copy-done.7, ...), custom_call_target="tpu_custom_call" | custom-call | tf_op jit(solution)/shard_map/final_step/pallas_call | solution.py:397
  (26 shorter events, 1.9 us)
Async XLA Ops:
  0.6 10.8 %copy-start = (f32[3,16,32,128]{3,2,1,0:T(8,128)S(1)}, f32[3,16,32,128]{3,2,1,0:T(8,128)}, u32[]{:S(2)}) copy-start(f32[3,16,32,128]{3,2,1,0:T(8,128)} %param.11) | copy-start | bytes 2359300
  0.6 10.8 %copy-start.4 = (f32[16,32,128]{2,1,0:T(8,128)S(1)}, f32[16,32,128]{2,1,0:T(8,128)}, u32[]{:S(2)}) copy-start(f32[16,32,128]{2,1,0:T(8,128)} %plume.3) | copy-start | bytes 786436
  4.1 12.0 %copy-start.12 = (s32[3,8]{1,0:T(4,128)S(1)}, s32[3,8]{1,0:T(4,128)}, u32[]{:S(2)}) copy-start(s32[3,8]{1,0:T(4,128)} %param.13) | copy-start | bytes 292
  4.1 19.2 %copy-start.1 = (bf16[768,1152]{1,0:T(8,128)(2,1)S(1)}, bf16[768,1152]{1,0:T(8,128)(2,1)}, u32[]{:S(2)}) copy-start(bf16[768,1152]{1,0:T(8,128)(2,1)} %constant.11.clone.x_back) | copy-start | bytes 5308420
  4.2 19.1 %all-to-all-start = ((f32[32,24,128]{2,1,0:T(8,128)}), f32[32,24,128]{2,1,0:T(8,128)S(1)}, u32[]{:S(2)}, u32[]{:S(2)}) async-start(f32[32,24,128]{2,1,0:T(8,128)} %first_modes.1), calls=%async_computation | async-start | bytes 786432 | tf_op jit(solution)/shard_map/all_to_all | solution.py:378
  12.7 3.6 %collective-permute-start = (f32[64,128]{1,0:T(8,128)S(1)}, f32[64,128]{1,0:T(8,128)S(1)}, u32[]{:S(2)}, u32[]{:S(2)}) collective-permute-start(f32[64,128]{1,0:T(8,128)S(1)} %get-tuple-element.24), channel_id=1, source_target_pairs={{0,4},{4,8},{8,12},{12,16},{16,20},{20,24},{24,28},{1,5},{5,9},{9,... | collective-permute-start | bytes 98312 | tf_op jit(solution)/shard_map/ppermute | solution.py:315
  14.8 4.2 %collective-permute-start.1 = (f32[64,128]{1,0:T(8,128)S(1)}, f32[64,128]{1,0:T(8,128)S(1)}, u32[]{:S(2)}, u32[]{:S(2)}) collective-permute-start(f32[64,128]{1,0:T(8,128)S(1)} %get-tuple-element.25), channel_id=1, source_target_pairs={{4,0},{8,4},{12,8},{16,12},{20,16},{24,20},{28,24},{5,1},{9,5},{13... | collective-permute-start | bytes 98312 | tf_op jit(solution)/shard_map/ppermute | solution.py:315
  25.0 14.2 %all-to-all-start.1 = ((f32[32,16,128]{2,1,0:T(8,128)}), f32[32,16,128]{2,1,0:T(8,128)S(1)}, u32[]{:S(2)}, u32[]{:S(2)}) async-start(f32[32,16,128]{2,1,0:T(8,128)} %share_sum.2), calls=%async_computation.1 | async-start | bytes 524288 | tf_op jit(solution)/shard_map/all_to_all | solution.py:390
  29.0 5.9 %collective-permute-start.3 = (f32[32,128]{1,0:T(8,128)S(1)}, f32[32,128]{1,0:T(8,128)S(1)}, u32[]{:S(2)}, u32[]{:S(2)}) collective-permute-start(f32[32,128]{1,0:T(8,128)S(1)} %get-tuple-element.31), channel_id=1, source_target_pairs={{1,0},{2,1},{3,2},{5,4},{6,5},{7,6},{9,8},{10,9},{11,10},{13,12},{... | collective-permute-start | bytes 49160 | tf_op jit(solution)/shard_map/ppermute | solution.py:315
  30.3 6.0 %collective-permute-start.2 = (f32[32,128]{1,0:T(8,128)S(1)}, f32[32,128]{1,0:T(8,128)S(1)}, u32[]{:S(2)}, u32[]{:S(2)}) collective-permute-start(f32[32,128]{1,0:T(8,128)S(1)} %get-tuple-element.31), channel_id=1, source_target_pairs={{0,1},{1,2},{2,3},{4,5},{5,6},{6,7},{8,9},{9,10},{10,11},{12,13},{... | collective-permute-start | bytes 49160 | tf_op jit(solution)/shard_map/ppermute | solution.py:315
  39.2 0.7 copy-start.2
  39.9 0.9 %copy-start.3 = (f32[32,16,128]{2,1,0:T(8,128)S(1)}, f32[32,16,128]{2,1,0:T(8,128)}, u32[]{:S(2)}) copy-start(f32[32,16,128]{2,1,0:T(8,128)} %copy-done.2) | copy-start | bytes 786436
  40.9 0.9 %copy-start.5 = (f32[16,32,128]{2,1,0:T(8,128)S(1)}, f32[16,32,128]{2,1,0:T(8,128)}, u32[]{:S(2)}) copy-start(f32[16,32,128]{2,1,0:T(8,128)} %plume.3) | copy-start | bytes 786436
  41.8 0.9 %copy-start.6 = (f32[16,32,128]{2,1,0:T(8,128)S(1)}, f32[16,32,128]{2,1,0:T(8,128)}, u32[]{:S(2)}) copy-start(f32[16,32,128]{2,1,0:T(8,128)} %source.3) | copy-start | bytes 786436
  46.6 0.7 copy-start.8
  47.3 0.7 copy-start.11
  48.0 15.5 %all-to-all-start.2 = ((f32[32,24,128]{2,1,0:T(8,128)}), f32[32,24,128]{2,1,0:T(8,128)S(1)}, u32[]{:S(2)}, u32[]{:S(2)}) async-start(f32[32,24,128]{2,1,0:T(8,128)} %copy-done.11), calls=%async_computation.2 | async-start | bytes 786432 | tf_op jit(solution)/shard_map/all_to_all | solution.py:378
  51.7 1.0 %copy-start.9 = (f32[16,32,128]{2,1,0:T(8,128)S(1)}, f32[16,32,128]{2,1,0:T(8,128)}, u32[]{:S(2)}) copy-start(f32[16,32,128]{2,1,0:T(8,128)} %copy-done.8) | copy-start | bytes 786436
  52.7 26.7 %copy-start.7 = (f32[16,32,128]{2,1,0:T(8,128)S(1)}, f32[16,32,128]{2,1,0:T(8,128)}, u32[]{:S(2)}) copy-start(f32[16,32,128]{2,1,0:T(8,128)} %source.3) | copy-start | bytes 786436
  53.0 3.5 %collective-permute-start.4 = (f32[64,128]{1,0:T(8,128)S(1)}, f32[64,128]{1,0:T(8,128)S(1)}, u32[]{:S(2)}, u32[]{:S(2)}) collective-permute-start(f32[64,128]{1,0:T(8,128)S(1)} %get-tuple-element.36), channel_id=1, source_target_pairs={{0,4},{4,8},{8,12},{12,16},{16,20},{20,24},{24,28},{1,5},{5,9},{9,... | collective-permute-start | bytes 98312 | tf_op jit(solution)/shard_map/ppermute | solution.py:315
  55.1 4.2 %collective-permute-start.5 = (f32[64,128]{1,0:T(8,128)S(1)}, f32[64,128]{1,0:T(8,128)S(1)}, u32[]{:S(2)}, u32[]{:S(2)}) collective-permute-start(f32[64,128]{1,0:T(8,128)S(1)} %get-tuple-element.37), channel_id=1, source_target_pairs={{4,0},{8,4},{12,8},{16,12},{20,16},{24,20},{28,24},{5,1},{9,5},{13... | collective-permute-start | bytes 98312 | tf_op jit(solution)/shard_map/ppermute | solution.py:315
  65.3 14.1 %all-to-all-start.3 = ((f32[32,16,128]{2,1,0:T(8,128)}), f32[32,16,128]{2,1,0:T(8,128)S(1)}, u32[]{:S(2)}, u32[]{:S(2)}) async-start(f32[32,16,128]{2,1,0:T(8,128)} %share_sum.3), calls=%async_computation.3 | async-start | bytes 524288 | tf_op jit(solution)/shard_map/all_to_all | solution.py:390
  69.1 5.9 %collective-permute-start.7 = (f32[32,128]{1,0:T(8,128)S(1)}, f32[32,128]{1,0:T(8,128)S(1)}, u32[]{:S(2)}, u32[]{:S(2)}) collective-permute-start(f32[32,128]{1,0:T(8,128)S(1)} %get-tuple-element.43), channel_id=1, source_target_pairs={{1,0},{2,1},{3,2},{5,4},{6,5},{7,6},{9,8},{10,9},{11,10},{13,12},{... | collective-permute-start | bytes 49160 | tf_op jit(solution)/shard_map/ppermute | solution.py:315
  70.4 6.0 %collective-permute-start.6 = (f32[32,128]{1,0:T(8,128)S(1)}, f32[32,128]{1,0:T(8,128)S(1)}, u32[]{:S(2)}, u32[]{:S(2)}) collective-permute-start(f32[32,128]{1,0:T(8,128)S(1)} %get-tuple-element.43), channel_id=1, source_target_pairs={{0,1},{1,2},{2,3},{4,5},{5,6},{6,7},{8,9},{9,10},{10,11},{12,13},{... | collective-permute-start | bytes 49160 | tf_op jit(solution)/shard_map/ppermute | solution.py:315
  79.3 1.0 %copy-start.10 = (f32[16,32,128]{2,1,0:T(8,128)S(1)}, f32[16,32,128]{2,1,0:T(8,128)}, u32[]{:S(2)}) copy-start(f32[16,32,128]{2,1,0:T(8,128)} %copy-done.8) | copy-start | bytes 786436

commit v9 on v8

--- a/solution.py
+++ b/solution.py
@@ -69,7 +69,7 @@
         edge[:, [0, -1]] = wave_table(np.array([first - 1, first + cells_y]), period_y)
         y_fwd.append(split_table(table * scaling, 1, "hlh"))
         y_back.append(split_table(np.concatenate([table, edge], axis=1), 0, "hhl"))
-    return [np.stack(x_fwd), np.stack(y_fwd), np.stack(y_back), split_table(x_back, 0, "hhl")]
+    return [np.stack(x_fwd), np.stack(y_fwd), np.stack(y_back), split_table(x_back, 0, "hl")]
 
 
 def data_dot(a, table):
@@ -192,7 +192,12 @@
     spare = -rows % 16
     if spare:
         both = jnp.concatenate([both, jnp.zeros((spare, 2 * LANES), jnp.float32)], axis=0)
-    half = data_dot(both, x_back[...])
+    head, rest = split(both)
+    depth = 2 * LANES
+    heads = jnp.dot(
+        jnp.concatenate([head, rest], axis=0), x_back[:depth], preferred_element_type=jnp.float32)
+    half = heads[: rows + spare] + heads[rows + spare :] + jnp.dot(
+        head, x_back[depth:], preferred_element_type=jnp.float32)
     packed = beside_rows(rows)
     width = 2 * GROUP
     spot = lax.broadcasted_iota(jnp.int32, (packed, LANES), 1) // width
@@ -209,17 +214,19 @@
             out[g * n_gy + h, rows:, :] = beside
 
 
-def step_kernel(n_gy, step, last, levels, owners, shares, fields, plume, source,
-                west, east, south, north, y_back, *rest):
+def step_kernel(n_gy, step, last, levels, owners, shares, fields, plume,
+                west, east, south, north, y_back, source_all, *rest):
     gx, gy = lax.axis_index("gx"), lax.axis_index("gy")
-    copies = []
+    extra = []
     if last:
-        fields_out, plume_out, slabs, beside, spread, spread_edges = rest
+        fields_out, plume_out, slabs, beside, spread, spread_edges, source, sems = rest
     else:
         (parent_all, x_fwd_all, y_fwd_all, fields_out, plume_out, modes,
-         slabs, beside, spread, spread_edges, sems, parent, x_fwd, y_fwd, turned, work) = rest
-        copies = fetch_all(sems, [(x_fwd_all.at[gx], x_fwd), (y_fwd_all.at[gy], y_fwd),
-                                  (parent_all.at[0, step + 1], parent)])
+         slabs, beside, spread, spread_edges, source, sems, parent, x_fwd, y_fwd, turned,
+         work) = rest
+        extra = [(x_fwd_all.at[gx], x_fwd), (y_fwd_all.at[gy], y_fwd),
+                 (parent_all.at[0, step + 1], parent)]
+    copies = fetch_all(sems, [(source_all, source)] + extra)
     level_total, cells_x, cells_y = plume.shape
     field_rows = fields.shape[0]
     total = field_rows + level_total
@@ -269,6 +276,8 @@
     columns = jnp.where(
         lane % 2 == 0, pltpu.roll(north[...], cells_y - 1, 1), pltpu.roll(south[...], 1, 1))
 
+    copies[0].wait()
+
     def advance(c, parts):
         centre, to_west, to_east, to_south, to_north = parts
         a = slabs[c, inner]
@@ -300,7 +309,7 @@
 
     if last:
         return
-    for copy in copies:
+    for copy in copies[1:]:
         copy.wait()
     emit_modes(
         lambda c: fields_out[slab_of(levels, c, level_count, level_total)],
@@ -340,8 +349,9 @@
 
     mode_shape = f32((devices, 2 * rows, LANES))
     step_scratch = [vmem(total, cells_x + 2 * PAD, cells_y), vmem(field_rows, cells_x, cells_y),
-                    vmem(devices * rows, LANES), vmem(devices * rows, LANES)]
-    mode_scratch = [pltpu.SemaphoreType.DMA((4,)), vmem(nudged, 4 * KX * KX), table_space(x_fwd),
+                    vmem(devices * rows, LANES), vmem(devices * rows, LANES),
+                    vmem(level_total, cells_x, cells_y), pltpu.SemaphoreType.DMA((4,))]
+    mode_scratch = [vmem(nudged, 4 * KX * KX), table_space(x_fwd),
                     table_space(y_fwd), vmem(nudged, KX, LANES),
                     vmem(devices * rows, 2 * LANES)]
     levels, owners = in_hbm(levels), in_hbm(owners)
@@ -351,7 +361,8 @@
         out_shape=mode_shape,
         in_specs=[SMEM, SMEM] + [HBM] * 4,
         out_specs=VMEM,
-        scratch_shapes=[vmem(field_rows, cells_x, cells_y)] + mode_scratch,
+        scratch_shapes=[vmem(field_rows, cells_x, cells_y), pltpu.SemaphoreType.DMA((4,))]
+        + mode_scratch,
         compiler_params=limit(8),
         name="first_modes",
     )(levels, owners, in_hbm(flat), in_hbm(parent_modes), in_hbm(x_fwd), in_hbm(y_fwd))
@@ -382,22 +393,22 @@
             out_shape=f32((devices, rows + beside_rows(rows), LANES)),
             in_specs=[SMEM, VMEM, VMEM],
             out_specs=VMEM,
-            compiler_params=limit(12),
+            compiler_params=limit(8),
             name="share_sum",
         )(cuts, parts, x_back)
         share, cols = lax.optimization_barrier((share, cols))
         south, north = swap("gy", cols, cols)
         shares = lax.all_to_all(share, AXES, 0, 0, tiled=True)
         out_shape = [f32(flat.shape), f32(plume.shape)]
-        operands = [levels, owners, shares, flat, plume, source, west, east, south, north,
-                    back_table]
+        operands = [levels, owners, shares, flat, plume, west, east, south, north, back_table,
+                    in_hbm(source)]
         if not last:
             out_shape.append(mode_shape)
             operands += [in_hbm(parent_modes), in_hbm(x_fwd), in_hbm(y_fwd)]
         results = pl.pallas_call(
             functools.partial(step_kernel, n_gy, step, last),
             out_shape=out_shape,
-            in_specs=[SMEM, SMEM] + [VMEM] * 9 + [HBM] * (len(operands) - 11),
+            in_specs=[SMEM, SMEM] + [VMEM] * 8 + [HBM] * (len(operands) - 10),
             out_specs=[VMEM] * len(out_shape),
             scratch_shapes=step_scratch + ([] if last else mode_scratch),
             compiler_params=limit(20),

time: 84.2 us -> 84.8 us (level)
  waiting for transfers between devices: 22.8 us -> 21.3 us
  starting transfers between devices: 37.4 us -> 38.7 us
    unnamed x26 -> x32, local copies, waits for them, and re-layouts: 6.9 us -> 6.91 us
where the time goes in v9:
time: 84.8 us; the launch traced here: 83.9 us
  starting transfers between devices  38.7 us (46%)
  waiting for transfers between devices  21.3 us (25%)
  Pallas kernels  16 us (19%)
  local copies, waits for them, and re-layouts  6.99 us (8%)
  between operations  0.87 us (1%)
    ppermute x4, starting transfers between devices, swap(): lax.ppermute(to_next, axis, up)  13.4 us
    all_to_all x2, starting transfers between devices, local(): parts = lax.all_to_all(modes, AXES, 0, 0, tiled=True)  11.6 us
    all_to_all x2, starting transfers between devices, local(): shares = lax.all_to_all(share, AXES, 0, 0, tiled=True)  8.6 us
    all_to_all x2, waiting for transfers between devices, local(): parts = lax.all_to_all(modes, AXES, 0, 0, tiled=True)  8.09 us
    pallas_call x2, Pallas kernels, local(): pl.pallas_call(functools.partial(step_kernel, n_gy, step, last), out_shap...  7.67 us
    unnamed x32, local copies, waits for them, and re-layouts  6.91 us
    all_to_all x2, waiting for transfers between devices, local(): shares = lax.all_to_all(share, AXES, 0, 0, tiled=True)  5.25 us
    ppermute x4, starting transfers between devices, swap(): lax.ppermute(to_previous, axis, down)  5.17 us
  transfers between devices with their start and end apart: 12, of which 8 were waited for; matrix products, arithmetic and copies ran while one was open for 0% of the time, Pallas kernels for 2%

profile of v9, /device:TPU:0, one launch (start us, length us, event | category | flops | bytes accessed | tf_op | source)
XLA Modules:
  0.0 83.9 jit_solution(9358417463426474599)
XLA Ops:
  0.6 3.5 %first_modes.1 = f32[32,24,128]{2,1,0:T(8,128)} custom-call(s32[8]{0:T(128)} %levels.5, s32[2]{0:T(128)} %owners.5, f32[48,32,128]{2,1,0:T(8,128)} %bitcast.2, f32[1,2,24,4096]{3,2,1,0:T(8,128)} %rest_0_.2, bf16[8,384,256]{2,1,0:T(8,128)(2,1)} %constant.8.clone.x_fwd_all.rest_1_, bf16[4,64,384]{2,1,0:T(8,128)(2,1)} %constant.9.clone.y_fwd_all.rest_2_), custom_call_target="tpu_custom_call" | custom-call | tf_op jit(solution)/shard_map/first_modes/pallas_call | solution.py:359
  4.2 7.3 %all-to-all-start = ((f32[32,24,128]{2,1,0:T(8,128)}), f32[32,24,128]{2,1,0:T(8,128)S(1)}, u32[]{:S(2)}, u32[]{:S(2)}) async-start(f32[32,24,128]{2,1,0:T(8,128)} %first_modes.1), calls=%async_computation | async-start | bytes 786432 | tf_op jit(solution)/shard_map/all_to_all | solution.py:389
  11.5 1.2 %edges.2 = (f32[64,128]{1,0:T(8,128)S(1)}, f32[64,128]{1,0:T(8,128)S(1)}, f32[32,128]{1,0:T(8,128)S(1)}, bf16[192,256]{1,0:T(8,128)(2,1)S(1)}) custom-call(f32[48,32,128]{2,1,0:T(8,128)S(1)} %bitcast.3, f32[16,32,128]{2,1,0:T(8,128)S(1)} %copy-done.2, bf16[4,192,256]{2,1,0:T(8,128)(2,1)} %constant.10.clone.rest_0_), custom_call_target="tpu_custom_call" | custom-call | tf_op jit(solution)/shard_map/edges/pallas_call | solution.py:376
  12.7 0.6 copy-done.4
  13.3 2.1 %collective-permute-start = (f32[64,128]{1,0:T(8,128)S(1)}, f32[64,128]{1,0:T(8,128)S(1)}, u32[]{:S(2)}, u32[]{:S(2)}) collective-permute-start(f32[64,128]{1,0:T(8,128)S(1)} %get-tuple-element.24), channel_id=1, source_target_pairs={{0,4},{4,8},{8,12},{12,16},{16,20},{20,24},{24,28},{1,5},{5,9},{9,... | collective-permute-start | bytes 98312 | tf_op jit(solution)/shard_map/ppermute | solution.py:324
  15.4 1.3 %collective-permute-start.1 = (f32[64,128]{1,0:T(8,128)S(1)}, f32[64,128]{1,0:T(8,128)S(1)}, u32[]{:S(2)}, u32[]{:S(2)}) collective-permute-start(f32[64,128]{1,0:T(8,128)S(1)} %get-tuple-element.25), channel_id=1, source_target_pairs={{4,0},{8,4},{12,8},{16,12},{20,16},{24,20},{28,24},{5,1},{9,5},{13... | collective-permute-start | bytes 98312 | tf_op jit(solution)/shard_map/ppermute | solution.py:324
  17.5 2.2 %collective-permute-done.1.east = f32[64,128]{1,0:T(8,128)S(1)} collective-permute-done((f32[64,128]{1,0:T(8,128)S(1)}, f32[64,128]{1,0:T(8,128)S(1)}, u32[]{:S(2)}, u32[]{:S(2)}) %collective-permute-start.1) | collective-permute-done | bytes 32800 | tf_op jit(solution)/shard_map/ppermute | solution.py:324
  20.3 3.0 %all-to-all-done.parts = f32[32,24,128]{2,1,0:T(8,128)S(1)} async-done(((f32[32,24,128]{2,1,0:T(8,128)}), f32[32,24,128]{2,1,0:T(8,128)S(1)}, u32[]{:S(2)}, u32[]{:S(2)}) %all-to-all-start) | async-done | bytes 393248 | tf_op jit(solution)/shard_map/all_to_all | solution.py:389
  23.3 1.7 %share_sum.2 = f32[32,16,128]{2,1,0:T(8,128)} custom-call(s32[24]{0:T(128)S(1)} %reshape.13.cuts, f32[32,24,128]{2,1,0:T(8,128)S(1)} %all-to-all-done.parts, bf16[512,1152]{1,0:T(8,128)(2,1)S(1)} %copy-done.1), custom_call_target="tpu_custom_call" | custom-call | tf_op jit(solution)/shard_map/share_sum/pallas_call | solution.py:391
  25.5 4.7 %all-to-all-start.1 = ((f32[32,16,128]{2,1,0:T(8,128)}), f32[32,16,128]{2,1,0:T(8,128)S(1)}, u32[]{:S(2)}, u32[]{:S(2)}) async-start(f32[32,16,128]{2,1,0:T(8,128)} %share_sum.2), calls=%async_computation.1 | async-start | bytes 524288 | tf_op jit(solution)/shard_map/all_to_all | solution.py:401
  30.3 1.3 %collective-permute-start.3 = (f32[32,128]{1,0:T(8,128)S(1)}, f32[32,128]{1,0:T(8,128)S(1)}, u32[]{:S(2)}, u32[]{:S(2)}) collective-permute-start(f32[32,128]{1,0:T(8,128)S(1)} %get-tuple-element.31), channel_id=1, source_target_pairs={{1,0},{2,1},{3,2},{5,4},{6,5},{7,6},{9,8},{10,9},{11,10},{13,12},{... | collective-permute-start | bytes 49160 | tf_op jit(solution)/shard_map/ppermute | solution.py:324
  31.6 4.5 %collective-permute-start.2 = (f32[32,128]{1,0:T(8,128)S(1)}, f32[32,128]{1,0:T(8,128)S(1)}, u32[]{:S(2)}, u32[]{:S(2)}) collective-permute-start(f32[32,128]{1,0:T(8,128)S(1)} %get-tuple-element.31), channel_id=1, source_target_pairs={{0,1},{1,2},{2,3},{4,5},{5,6},{6,7},{8,9},{9,10},{10,11},{12,13},{... | collective-permute-start | bytes 49160 | tf_op jit(solution)/shard_map/ppermute | solution.py:324
  36.2 1.4 %collective-permute-done.2.south = f32[32,128]{1,0:T(8,128)S(1)} collective-permute-done((f32[32,128]{1,0:T(8,128)S(1)}, f32[32,128]{1,0:T(8,128)S(1)}, u32[]{:S(2)}, u32[]{:S(2)}) %collective-permute-start.2) | collective-permute-done | bytes 16416 | tf_op jit(solution)/shard_map/ppermute | solution.py:324
  38.2 2.3 %all-to-all-done.1.shares = f32[32,16,128]{2,1,0:T(8,128)S(1)} async-done(((f32[32,16,128]{2,1,0:T(8,128)}), f32[32,16,128]{2,1,0:T(8,128)S(1)}, u32[]{:S(2)}, u32[]{:S(2)}) %all-to-all-start.1) | async-done | bytes 262176 | tf_op jit(solution)/shard_map/all_to_all | solution.py:401
  40.5 0.9 %copy-done.5 = bf16[192,256]{1,0:T(8,128)(2,1)S(1)} copy-done((bf16[192,256]{1,0:T(8,128)(2,1)S(1)}, bf16[192,256]{1,0:T(8,128)(2,1)}, u32[]{:S(2)}) %copy-start.5) | copy-done | bytes 98328
  41.4 0.8 copy-done.8
  42.1 0.8 copy-done.10
  42.9 0.7 copy-done.12
  43.6 3.6 %inner_step.1 = (f32[48,32,128]{2,1,0:T(8,128)S(1)}, f32[16,32,128]{2,1,0:T(8,128)S(1)}, f32[32,24,128]{2,1,0:T(8,128)S(1)}) custom-call(s32[8]{0:T(128)} %levels.5, s32[2]{0:T(128)} %owners.5, f32[32,16,128]{2,1,0:T(8,128)S(1)} %all-to-all-done.1.shares, f32[48,32,128]{2,1,0:T(8,128)S(1)} %bitcast.4, f32[16,32,128]{2,1,0:T(8,128)S(1)} %copy-done.2, ...), custom_call_target="tpu_custom_call" | custom-call | tf_op jit(solution)/shard_map/inner_step/pallas_call | solution.py:408
  47.3 0.7 copy-done.3
  48.0 4.3 %all-to-all-start.2 = ((f32[32,24,128]{2,1,0:T(8,128)}), f32[32,24,128]{2,1,0:T(8,128)S(1)}, u32[]{:S(2)}, u32[]{:S(2)}) async-start(f32[32,24,128]{2,1,0:T(8,128)} %copy-done.3), calls=%async_computation.2 | async-start | bytes 786432 | tf_op jit(solution)/shard_map/all_to_all | solution.py:389
  52.7 2.2 %collective-permute-start.4 = (f32[64,128]{1,0:T(8,128)S(1)}, f32[64,128]{1,0:T(8,128)S(1)}, u32[]{:S(2)}, u32[]{:S(2)}) collective-permute-start(f32[64,128]{1,0:T(8,128)S(1)} %get-tuple-element.36), channel_id=1, source_target_pairs={{0,4},{4,8},{8,12},{12,16},{16,20},{20,24},{24,28},{1,5},{5,9},{9,... | collective-permute-start | bytes 98312 | tf_op jit(solution)/shard_map/ppermute | solution.py:324
  54.8 1.3 %collective-permute-start.5 = (f32[64,128]{1,0:T(8,128)S(1)}, f32[64,128]{1,0:T(8,128)S(1)}, u32[]{:S(2)}, u32[]{:S(2)}) collective-permute-start(f32[64,128]{1,0:T(8,128)S(1)} %get-tuple-element.37), channel_id=1, source_target_pairs={{4,0},{8,4},{12,8},{16,12},{20,16},{24,20},{28,24},{5,1},{9,5},{13... | collective-permute-start | bytes 98312 | tf_op jit(solution)/shard_map/ppermute | solution.py:324
  56.1 2.9 %collective-permute-done.5.east = f32[64,128]{1,0:T(8,128)S(1)} collective-permute-done((f32[64,128]{1,0:T(8,128)S(1)}, f32[64,128]{1,0:T(8,128)S(1)}, u32[]{:S(2)}, u32[]{:S(2)}) %collective-permute-start.5) | collective-permute-done | bytes 32800 | tf_op jit(solution)/shard_map/ppermute | solution.py:324
  59.1 5.1 %all-to-all-done.2.parts = f32[32,24,128]{2,1,0:T(8,128)S(1)} async-done(((f32[32,24,128]{2,1,0:T(8,128)}), f32[32,24,128]{2,1,0:T(8,128)S(1)}, u32[]{:S(2)}, u32[]{:S(2)}) %all-to-all-start.2) | async-done | bytes 393248 | tf_op jit(solution)/shard_map/all_to_all | solution.py:389
  64.1 1.7 %share_sum.3 = f32[32,16,128]{2,1,0:T(8,128)} custom-call(s32[24]{0:T(128)S(1)} %copy-done.14, f32[32,24,128]{2,1,0:T(8,128)S(1)} %all-to-all-done.2.parts, bf16[512,1152]{1,0:T(8,128)(2,1)S(1)} %copy-done.1), custom_call_target="tpu_custom_call" | custom-call | tf_op jit(solution)/shard_map/share_sum/pallas_call | solution.py:391
  65.8 3.9 %all-to-all-start.3 = ((f32[32,16,128]{2,1,0:T(8,128)}), f32[32,16,128]{2,1,0:T(8,128)S(1)}, u32[]{:S(2)}, u32[]{:S(2)}) async-start(f32[32,16,128]{2,1,0:T(8,128)} %share_sum.3), calls=%async_computation.3 | async-start | bytes 524288 | tf_op jit(solution)/shard_map/all_to_all | solution.py:401
  69.7 1.3 %collective-permute-start.7 = (f32[32,128]{1,0:T(8,128)S(1)}, f32[32,128]{1,0:T(8,128)S(1)}, u32[]{:S(2)}, u32[]{:S(2)}) collective-permute-start(f32[32,128]{1,0:T(8,128)S(1)} %get-tuple-element.43), channel_id=1, source_target_pairs={{1,0},{2,1},{3,2},{5,4},{6,5},{7,6},{9,8},{10,9},{11,10},{13,12},{... | collective-permute-start | bytes 49160 | tf_op jit(solution)/shard_map/ppermute | solution.py:324
  71.0 4.5 %collective-permute-start.6 = (f32[32,128]{1,0:T(8,128)S(1)}, f32[32,128]{1,0:T(8,128)S(1)}, u32[]{:S(2)}, u32[]{:S(2)}) collective-permute-start(f32[32,128]{1,0:T(8,128)S(1)} %get-tuple-element.43), channel_id=1, source_target_pairs={{0,1},{1,2},{2,3},{4,5},{5,6},{6,7},{8,9},{9,10},{10,11},{12,13},{... | collective-permute-start | bytes 49160 | tf_op jit(solution)/shard_map/ppermute | solution.py:324
  75.5 1.4 %collective-permute-done.6.south = f32[32,128]{1,0:T(8,128)S(1)} collective-permute-done((f32[32,128]{1,0:T(8,128)S(1)}, f32[32,128]{1,0:T(8,128)S(1)}, u32[]{:S(2)}, u32[]{:S(2)}) %collective-permute-start.6) | collective-permute-done | bytes 16416 | tf_op jit(solution)/shard_map/ppermute | solution.py:324
  77.0 2.9 %all-to-all-done.3.shares = f32[32,16,128]{2,1,0:T(8,128)S(1)} async-done(((f32[32,16,128]{2,1,0:T(8,128)}), f32[32,16,128]{2,1,0:T(8,128)S(1)}, u32[]{:S(2)}, u32[]{:S(2)}) %all-to-all-start.3) | async-done | bytes 262176 | tf_op jit(solution)/shard_map/all_to_all | solution.py:401
  79.9 4.0 %final_step.1 = (f32[48,32,128]{2,1,0:T(8,128)}, f32[16,32,128]{2,1,0:T(8,128)}) custom-call(s32[8]{0:T(128)} %levels.5, s32[2]{0:T(128)} %owners.5, f32[32,16,128]{2,1,0:T(8,128)S(1)} %all-to-all-done.3.shares, f32[48,32,128]{2,1,0:T(8,128)S(1)} %get-tuple-element.34.fields, f32[16,32,128]{2,1,0:T(8,128)S(1)} %get-tuple-element.35.plume, ...), custom_call_target="tpu_custom_call" | custom-call | tf_op jit(solution)/shard_map/final_step/pallas_call | solution.py:408
  (32 shorter events, 2.9 us)
Async XLA Ops:
  0.6 10.8 %copy-start = (f32[3,16,32,128]{3,2,1,0:T(8,128)S(1)}, f32[3,16,32,128]{3,2,1,0:T(8,128)}, u32[]{:S(2)}) copy-start(f32[3,16,32,128]{3,2,1,0:T(8,128)} %param.11) | copy-start | bytes 2359300
  0.6 10.8 %copy-start.2 = (f32[16,32,128]{2,1,0:T(8,128)S(1)}, f32[16,32,128]{2,1,0:T(8,128)}, u32[]{:S(2)}) copy-start(f32[16,32,128]{2,1,0:T(8,128)} %plume.3) | copy-start | bytes 786436
  4.1 12.6 %copy-start.15 = (s32[3,8]{1,0:T(4,128)S(1)}, s32[3,8]{1,0:T(4,128)}, u32[]{:S(2)}) copy-start(s32[3,8]{1,0:T(4,128)} %param.13) | copy-start | bytes 292
  4.1 19.2 %copy-start.1 = (bf16[512,1152]{1,0:T(8,128)(2,1)S(1)}, bf16[512,1152]{1,0:T(8,128)(2,1)}, u32[]{:S(2)}) copy-start(bf16[512,1152]{1,0:T(8,128)(2,1)} %constant.11.clone.x_back) | copy-start | bytes 3538948
  4.2 19.1 %all-to-all-start = ((f32[32,24,128]{2,1,0:T(8,128)}), f32[32,24,128]{2,1,0:T(8,128)S(1)}, u32[]{:S(2)}, u32[]{:S(2)}) async-start(f32[32,24,128]{2,1,0:T(8,128)} %first_modes.1), calls=%async_computation | async-start | bytes 786432 | tf_op jit(solution)/shard_map/all_to_all | solution.py:389
  12.7 0.6 copy-start.4
  13.3 3.5 %collective-permute-start = (f32[64,128]{1,0:T(8,128)S(1)}, f32[64,128]{1,0:T(8,128)S(1)}, u32[]{:S(2)}, u32[]{:S(2)}) collective-permute-start(f32[64,128]{1,0:T(8,128)S(1)} %get-tuple-element.24), channel_id=1, source_target_pairs={{0,4},{4,8},{8,12},{12,16},{16,20},{20,24},{24,28},{1,5},{5,9},{9,... | collective-permute-start | bytes 98312 | tf_op jit(solution)/shard_map/ppermute | solution.py:324
  15.4 4.2 %collective-permute-start.1 = (f32[64,128]{1,0:T(8,128)S(1)}, f32[64,128]{1,0:T(8,128)S(1)}, u32[]{:S(2)}, u32[]{:S(2)}) collective-permute-start(f32[64,128]{1,0:T(8,128)S(1)} %get-tuple-element.25), channel_id=1, source_target_pairs={{4,0},{8,4},{12,8},{16,12},{20,16},{24,20},{28,24},{5,1},{9,5},{13... | collective-permute-start | bytes 98312 | tf_op jit(solution)/shard_map/ppermute | solution.py:324
  16.8 0.6 copy-start.7
  19.7 0.6 copy-start.9
  25.0 0.6 copy-start.13
  25.5 15.0 %all-to-all-start.1 = ((f32[32,16,128]{2,1,0:T(8,128)}), f32[32,16,128]{2,1,0:T(8,128)S(1)}, u32[]{:S(2)}, u32[]{:S(2)}) async-start(f32[32,16,128]{2,1,0:T(8,128)} %share_sum.2), calls=%async_computation.1 | async-start | bytes 524288 | tf_op jit(solution)/shard_map/all_to_all | solution.py:401
  30.3 5.9 %collective-permute-start.3 = (f32[32,128]{1,0:T(8,128)S(1)}, f32[32,128]{1,0:T(8,128)S(1)}, u32[]{:S(2)}, u32[]{:S(2)}) collective-permute-start(f32[32,128]{1,0:T(8,128)S(1)} %get-tuple-element.31), channel_id=1, source_target_pairs={{1,0},{2,1},{3,2},{5,4},{6,5},{7,6},{9,8},{10,9},{11,10},{13,12},{... | collective-permute-start | bytes 49160 | tf_op jit(solution)/shard_map/ppermute | solution.py:324
  31.6 6.0 %collective-permute-start.2 = (f32[32,128]{1,0:T(8,128)S(1)}, f32[32,128]{1,0:T(8,128)S(1)}, u32[]{:S(2)}, u32[]{:S(2)}) collective-permute-start(f32[32,128]{1,0:T(8,128)S(1)} %get-tuple-element.31), channel_id=1, source_target_pairs={{0,1},{1,2},{2,3},{4,5},{5,6},{6,7},{8,9},{9,10},{10,11},{12,13},{... | collective-permute-start | bytes 49160 | tf_op jit(solution)/shard_map/ppermute | solution.py:324
  37.6 0.6 copy-start.11
  40.5 0.9 %copy-start.5 = (bf16[192,256]{1,0:T(8,128)(2,1)S(1)}, bf16[192,256]{1,0:T(8,128)(2,1)}, u32[]{:S(2)}) copy-start(bf16[192,256]{1,0:T(8,128)(2,1)} %copy-done.4) | copy-start | bytes 294916
  41.4 0.8 copy-start.8
  42.1 0.8 copy-start.10
  42.9 0.7 copy-start.12
  47.3 0.7 copy-start.3
  48.0 16.1 %copy-start.14 = (s32[24]{0:T(128)S(1)}, s32[24]{0:T(128)}, u32[]{:S(2)}) copy-start(s32[24]{0:T(128)} %copy-done.13) | copy-start | bytes 292
  48.0 16.1 %all-to-all-start.2 = ((f32[32,24,128]{2,1,0:T(8,128)}), f32[32,24,128]{2,1,0:T(8,128)S(1)}, u32[]{:S(2)}, u32[]{:S(2)}) async-start(f32[32,24,128]{2,1,0:T(8,128)} %copy-done.3), calls=%async_computation.2 | async-start | bytes 786432 | tf_op jit(solution)/shard_map/all_to_all | solution.py:389
  52.3 27.6 %copy-start.6 = (bf16[192,256]{1,0:T(8,128)(2,1)S(1)}, bf16[192,256]{1,0:T(8,128)(2,1)}, u32[]{:S(2)}) copy-start(bf16[192,256]{1,0:T(8,128)(2,1)} %copy-done.4) | copy-start | bytes 294916
  52.7 3.5 %collective-permute-start.4 = (f32[64,128]{1,0:T(8,128)S(1)}, f32[64,128]{1,0:T(8,128)S(1)}, u32[]{:S(2)}, u32[]{:S(2)}) collective-permute-start(f32[64,128]{1,0:T(8,128)S(1)} %get-tuple-element.36), channel_id=1, source_target_pairs={{0,4},{4,8},{8,12},{12,16},{16,20},{20,24},{24,28},{1,5},{5,9},{9,... | collective-permute-start | bytes 98312 | tf_op jit(solution)/shard_map/ppermute | solution.py:324
  54.8 4.2 %collective-permute-start.5 = (f32[64,128]{1,0:T(8,128)S(1)}, f32[64,128]{1,0:T(8,128)S(1)}, u32[]{:S(2)}, u32[]{:S(2)}) collective-permute-start(f32[64,128]{1,0:T(8,128)S(1)} %get-tuple-element.37), channel_id=1, source_target_pairs={{4,0},{8,4},{12,8},{16,12},{20,16},{24,20},{28,24},{5,1},{9,5},{13... | collective-permute-start | bytes 98312 | tf_op jit(solution)/shard_map/ppermute | solution.py:324
  65.8 14.1 %all-to-all-start.3 = ((f32[32,16,128]{2,1,0:T(8,128)}), f32[32,16,128]{2,1,0:T(8,128)S(1)}, u32[]{:S(2)}, u32[]{:S(2)}) async-start(f32[32,16,128]{2,1,0:T(8,128)} %share_sum.3), calls=%async_computation.3 | async-start | bytes 524288 | tf_op jit(solution)/shard_map/all_to_all | solution.py:401
  69.7 5.9 %collective-permute-start.7 = (f32[32,128]{1,0:T(8,128)S(1)}, f32[32,128]{1,0:T(8,128)S(1)}, u32[]{:S(2)}, u32[]{:S(2)}) collective-permute-start(f32[32,128]{1,0:T(8,128)S(1)} %get-tuple-element.43), channel_id=1, source_target_pairs={{1,0},{2,1},{3,2},{5,4},{6,5},{7,6},{9,8},{10,9},{11,10},{13,12},{... | collective-permute-start | bytes 49160 | tf_op jit(solution)/shard_map/ppermute | solution.py:324
  71.0 6.0 %collective-permute-start.6 = (f32[32,128]{1,0:T(8,128)S(1)}, f32[32,128]{1,0:T(8,128)S(1)}, u32[]{:S(2)}, u32[]{:S(2)}) collective-permute-start(f32[32,128]{1,0:T(8,128)S(1)} %get-tuple-element.43), channel_id=1, source_target_pairs={{0,1},{1,2},{2,3},{4,5},{5,6},{6,7},{8,9},{9,10},{10,11},{12,13},{... | collective-permute-start | bytes 49160 | tf_op jit(solution)/shard_map/ppermute | solution.py:324

commit v10 on v9

--- a/solution.py
+++ b/solution.py
@@ -58,10 +58,11 @@
         x_fwd.append(split_table(
             np.concatenate([per_slab(table[rows].T) for rows in parity], axis=1), 0, "hhl"))
         beside = wave_table(np.array([first - 1, first + cells_x]), period_x)
-        inner.append(np.concatenate([per_slab(table[rows]) for rows in parity], axis=0))
+        inner.append(np.concatenate([np.tile(table[rows], (GROUP, 1)) for rows in parity], axis=0))
         outer.append(np.concatenate([per_slab(beside[rows]) for rows in parity], axis=0))
     spare = -(2 * GROUP * n_gx) % LANES
-    x_back = np.concatenate(inner + outer + [np.zeros((2 * LANES, spare))], axis=1)
+    x_back = np.concatenate(inner, axis=1)
+    x_beside = np.concatenate(outer + [np.zeros((2 * LANES, spare))], axis=1)
     for g in range(n_gy):
         first = g * cells_y
         table = wave_table(first + np.arange(cells_y), period_y)
@@ -69,7 +70,8 @@
         edge[:, [0, -1]] = wave_table(np.array([first - 1, first + cells_y]), period_y)
         y_fwd.append(split_table(table * scaling, 1, "hlh"))
         y_back.append(split_table(np.concatenate([table, edge], axis=1), 0, "hhl"))
-    return [np.stack(x_fwd), np.stack(y_fwd), np.stack(y_back), split_table(x_back, 0, "hl")]
+    return [np.stack(x_fwd), np.stack(y_fwd), np.stack(y_back),
+            split_table(x_back, 0, "hl"), split_table(x_beside, 0, "hl")]
 
 
 def data_dot(a, table):
@@ -77,6 +79,15 @@
     return jnp.dot(
         jnp.concatenate([head, rest, head], axis=1), table, preferred_element_type=jnp.float32
     )
+
+
+def two_part_dot(a, table):
+    head, rest = split(a)
+    depth = a.shape[1]
+    heads = jnp.dot(
+        jnp.concatenate([head, rest], axis=0), table[:depth], preferred_element_type=jnp.float32)
+    rests = jnp.dot(head, table[depth:], preferred_element_type=jnp.float32)
+    return heads[: a.shape[0]] + heads[a.shape[0] :] + rests
 
 
 def columns_dot(a, table):
@@ -167,7 +178,7 @@
     return -(-rows // 3)
 
 
-def share_kernel(n_gx, n_gy, period, cuts, parts, x_back, out):
+def share_kernel(n_gx, n_gy, period, cuts, parts, x_back, x_beside, out):
     devices = parts.shape[0]
     rows = parts.shape[1] // 2
     me = lax.axis_index("gx") * n_gy + lax.axis_index("gy")
@@ -192,25 +203,30 @@
     spare = -rows % 16
     if spare:
         both = jnp.concatenate([both, jnp.zeros((spare, 2 * LANES), jnp.float32)], axis=0)
-    head, rest = split(both)
-    depth = 2 * LANES
-    heads = jnp.dot(
-        jnp.concatenate([head, rest], axis=0), x_back[:depth], preferred_element_type=jnp.float32)
-    half = heads[: rows + spare] + heads[rows + spare :] + jnp.dot(
-        head, x_back[depth:], preferred_element_type=jnp.float32)
+    slab_lane = lax.broadcasted_iota(jnp.int32, both.shape, 1) % LANES // KX
+    chosen = [jnp.where(slab_lane == n, both, 0.0) for n in range(GROUP)]
+    inner = two_part_dot(jnp.concatenate(chosen, axis=0), x_back)
+    edge_all = two_part_dot(both, x_beside)
+    height = rows + spare
     packed = beside_rows(rows)
     width = 2 * GROUP
+    cells_x = LANES // GROUP
+    slot = lax.broadcasted_iota(jnp.int32, (height, LANES), 1) // cells_x
     spot = lax.broadcasted_iota(jnp.int32, (packed, LANES), 1) // width
     for g in range(n_gx):
-        first = (n_gx + g * width // LANES) * LANES
-        edge = half[:, first : first + LANES]
+        first = g * cells_x // LANES * LANES
+        tile = jnp.zeros((height, LANES), jnp.float32)
+        for n in range(GROUP):
+            piece = inner[n * height : (n + 1) * height, first : first + LANES]
+            tile = jnp.where(slot == n, pltpu.roll(piece, (n - g) * cells_x % LANES, 1), tile)
+        first = g * width // LANES * LANES
         beside = jnp.zeros((packed, LANES), jnp.float32)
         for m in range(3):
-            piece = edge[m * packed : (m + 1) * packed]
+            piece = edge_all[m * packed : (m + 1) * packed, first : first + LANES]
             beside = jnp.where(
                 spot == m, pltpu.roll(piece, (m - g) * width % LANES, 1), beside)
         for h in range(n_gy):
-            out[g * n_gy + h, :rows, :] = half[:rows, g * LANES : (g + 1) * LANES]
+            out[g * n_gy + h, :rows, :] = tile[:rows]
             out[g * n_gy + h, rows:, :] = beside
 
 
@@ -336,7 +352,7 @@
     flat = fields.reshape(field_rows, cells_x, cells_y)
     cuts = cuts.reshape(-1)
     f32 = functools.partial(jax.ShapeDtypeStruct, dtype=jnp.float32)
-    x_fwd, y_fwd, y_back, x_back = (jnp.asarray(t) for t in tables)
+    x_fwd, y_fwd, y_back, x_back, x_beside = (jnp.asarray(t) for t in tables)
 
     def vmem(*shape):
         return pltpu.VMEM(shape, jnp.float32)
@@ -391,11 +407,11 @@
         share = pl.pallas_call(
             functools.partial(share_kernel, n_gx, n_gy, period),
             out_shape=f32((devices, rows + beside_rows(rows), LANES)),
-            in_specs=[SMEM, VMEM, VMEM],
+            in_specs=[SMEM, VMEM, VMEM, VMEM],
             out_specs=VMEM,
             compiler_params=limit(8),
             name="share_sum",
-        )(cuts, parts, x_back)
+        )(cuts, parts, x_back, x_beside)
         share, cols = lax.optimization_barrier((share, cols))
         south, north = swap("gy", cols, cols)
         shares = lax.all_to_all(share, AXES, 0, 0, tiled=True)

time: 84.8 us -> 79.6 us (0.939)
  local copies, waits for them, and re-layouts: 6.99 us -> 0.11 us
  waiting for transfers between devices: 21.3 us -> 23.8 us
  starting transfers between devices: 38.7 us -> 37.4 us
    unnamed x32 -> x10, local copies, waits for them, and re-layouts: 6.91 us -> 0.03 us
    all_to_all x2, waiting for transfers between devices: 8.09 us -> 9.32 us  [local(): parts = lax.all_to_all(modes, AXES, 0, 0, tiled=True)]
where the time goes in v10:
time: 79.6 us; the launch traced here: 78.7 us
  starting transfers between devices  37.4 us (47%)
  waiting for transfers between devices  23.8 us (30%)
  Pallas kernels  16.6 us (21%)
  between operations  0.84 us (1%)
    ppermute x4, starting transfers between devices, swap(): lax.ppermute(to_next, axis, up)  13.4 us
    all_to_all x2, starting transfers between devices, local(): parts = lax.all_to_all(modes, AXES, 0, 0, tiled=True)  11 us
    all_to_all x2, waiting for transfers between devices, local(): parts = lax.all_to_all(modes, AXES, 0, 0, tiled=True)  9.32 us
    pallas_call x2, Pallas kernels, local(): pl.pallas_call(functools.partial(step_kernel, n_gy, step, last), out_shap...  8.41 us
    all_to_all x2, starting transfers between devices, local(): shares = lax.all_to_all(share, AXES, 0, 0, tiled=True)  7.82 us
    all_to_all x2, waiting for transfers between devices, local(): shares = lax.all_to_all(share, AXES, 0, 0, tiled=True)  5.86 us
    ppermute x4, waiting for transfers between devices, swap(): lax.ppermute(to_previous, axis, down)  5.77 us
    ppermute x4, starting transfers between devices, swap(): lax.ppermute(to_previous, axis, down)  5.17 us
  transfers between devices with their start and end apart: 12, of which 8 were waited for; matrix products, arithmetic and copies ran while one was open for 0% of the time, Pallas kernels for 2%

profile of v10, /device:TPU:0, one launch (start us, length us, event | category | flops | bytes accessed | tf_op | source)
XLA Modules:
  0.0 78.7 jit_solution(10410764698699949974)
XLA Ops:
  0.6 3.5 %first_modes.1 = f32[32,24,128]{2,1,0:T(8,128)} custom-call(s32[8]{0:T(128)} %levels.5, s32[2]{0:T(128)} %owners.5, f32[48,32,128]{2,1,0:T(8,128)} %bitcast.2, f32[1,2,24,4096]{3,2,1,0:T(8,128)} %rest_0_.2, bf16[8,384,256]{2,1,0:T(8,128)(2,1)} %constant.10.clone.x_fwd_all.rest_1_, bf16[4,64,384]{2,1,0:T(8,128)(2,1)} %constant.11.clone.y_fwd_all.rest_2_), custom_call_target="tpu_custom_call" | custom-call | tf_op jit(solution)/shard_map/first_modes/pallas_call | solution.py:375
  4.1 0.0 copy-start.4
  4.1 0.0 copy-start.2
  4.2 0.0 copy-start.3
  4.2 7.3 %all-to-all-start = ((f32[32,24,128]{2,1,0:T(8,128)}), f32[32,24,128]{2,1,0:T(8,128)S(1)}, u32[]{:S(2)}, u32[]{:S(2)}) async-start(f32[32,24,128]{2,1,0:T(8,128)} %first_modes.1), calls=%async_computation | async-start | bytes 786432 | tf_op jit(solution)/shard_map/all_to_all | solution.py:405
  11.5 1.2 %edges.2 = (f32[64,128]{1,0:T(8,128)S(1)}, f32[64,128]{1,0:T(8,128)S(1)}, f32[32,128]{1,0:T(8,128)S(1)}, bf16[192,256]{1,0:T(8,128)(2,1)S(1)}) custom-call(f32[48,32,128]{2,1,0:T(8,128)S(1)} %bitcast.3, f32[16,32,128]{2,1,0:T(8,128)S(1)} %copy-done.1, bf16[4,192,256]{2,1,0:T(8,128)(2,1)} %constant.12.clone.rest_0_), custom_call_target="tpu_custom_call" | custom-call | tf_op jit(solution)/shard_map/edges/pallas_call | solution.py:392
  12.7 2.2 %collective-permute-start = (f32[64,128]{1,0:T(8,128)S(1)}, f32[64,128]{1,0:T(8,128)S(1)}, u32[]{:S(2)}, u32[]{:S(2)}) collective-permute-start(f32[64,128]{1,0:T(8,128)S(1)} %get-tuple-element.24), channel_id=1, source_target_pairs={{0,4},{4,8},{8,12},{12,16},{16,20},{20,24},{24,28},{1,5},{5,9},{9,... | collective-permute-start | bytes 98312 | tf_op jit(solution)/shard_map/ppermute | solution.py:340
  14.8 1.3 %collective-permute-start.1 = (f32[64,128]{1,0:T(8,128)S(1)}, f32[64,128]{1,0:T(8,128)S(1)}, u32[]{:S(2)}, u32[]{:S(2)}) collective-permute-start(f32[64,128]{1,0:T(8,128)S(1)} %get-tuple-element.25), channel_id=1, source_target_pairs={{4,0},{8,4},{12,8},{16,12},{20,16},{24,20},{28,24},{5,1},{9,5},{13... | collective-permute-start | bytes 98312 | tf_op jit(solution)/shard_map/ppermute | solution.py:340
  16.1 0.1 reshape.13.cuts
  16.2 2.8 %collective-permute-done.1.east = f32[64,128]{1,0:T(8,128)S(1)} collective-permute-done((f32[64,128]{1,0:T(8,128)S(1)}, f32[64,128]{1,0:T(8,128)S(1)}, u32[]{:S(2)}, u32[]{:S(2)}) %collective-permute-start.1) | collective-permute-done | bytes 32800 | tf_op jit(solution)/shard_map/ppermute | solution.py:340
  19.1 4.2 %all-to-all-done.parts = f32[32,24,128]{2,1,0:T(8,128)S(1)} async-done(((f32[32,24,128]{2,1,0:T(8,128)}), f32[32,24,128]{2,1,0:T(8,128)S(1)}, u32[]{:S(2)}, u32[]{:S(2)}) %all-to-all-start) | async-done | bytes 393248 | tf_op jit(solution)/shard_map/all_to_all | solution.py:405
  23.3 1.6 %share_sum.2 = f32[32,16,128]{2,1,0:T(8,128)} custom-call(s32[24]{0:T(128)S(1)} %reshape.13.cuts, f32[32,24,128]{2,1,0:T(8,128)S(1)} %all-to-all-done.parts, bf16[512,256]{1,0:T(8,128)(2,1)S(1)} %copy-done.2, bf16[512,128]{1,0:T(8,128)(2,1)S(1)} %copy-done.3), custom_call_target="tpu_custom_call" | custom-call | tf_op jit(solution)/shard_map/share_sum/pallas_call | solution.py:407
  24.9 4.0 %all-to-all-start.1 = ((f32[32,16,128]{2,1,0:T(8,128)}), f32[32,16,128]{2,1,0:T(8,128)S(1)}, u32[]{:S(2)}, u32[]{:S(2)}) async-start(f32[32,16,128]{2,1,0:T(8,128)} %share_sum.2), calls=%async_computation.1 | async-start | bytes 524288 | tf_op jit(solution)/shard_map/all_to_all | solution.py:417
  28.9 1.3 %collective-permute-start.3 = (f32[32,128]{1,0:T(8,128)S(1)}, f32[32,128]{1,0:T(8,128)S(1)}, u32[]{:S(2)}, u32[]{:S(2)}) collective-permute-start(f32[32,128]{1,0:T(8,128)S(1)} %get-tuple-element.31), channel_id=1, source_target_pairs={{1,0},{2,1},{3,2},{5,4},{6,5},{7,6},{9,8},{10,9},{11,10},{13,12},{... | collective-permute-start | bytes 49160 | tf_op jit(solution)/shard_map/ppermute | solution.py:340
  30.2 4.5 %collective-permute-start.2 = (f32[32,128]{1,0:T(8,128)S(1)}, f32[32,128]{1,0:T(8,128)S(1)}, u32[]{:S(2)}, u32[]{:S(2)}) collective-permute-start(f32[32,128]{1,0:T(8,128)S(1)} %get-tuple-element.31), channel_id=1, source_target_pairs={{0,1},{1,2},{2,3},{4,5},{5,6},{6,7},{8,9},{9,10},{10,11},{12,13},{... | collective-permute-start | bytes 49160 | tf_op jit(solution)/shard_map/ppermute | solution.py:340
  34.7 0.0 collective-permute-done.3.north
  34.7 1.4 %collective-permute-done.2.south = f32[32,128]{1,0:T(8,128)S(1)} collective-permute-done((f32[32,128]{1,0:T(8,128)S(1)}, f32[32,128]{1,0:T(8,128)S(1)}, u32[]{:S(2)}, u32[]{:S(2)}) %collective-permute-start.2) | collective-permute-done | bytes 16416 | tf_op jit(solution)/shard_map/ppermute | solution.py:340
  36.2 2.9 %all-to-all-done.1.shares = f32[32,16,128]{2,1,0:T(8,128)S(1)} async-done(((f32[32,16,128]{2,1,0:T(8,128)}), f32[32,16,128]{2,1,0:T(8,128)S(1)}, u32[]{:S(2)}, u32[]{:S(2)}) %all-to-all-start.1) | async-done | bytes 262176 | tf_op jit(solution)/shard_map/all_to_all | solution.py:417
  39.1 4.4 %inner_step.1 = (f32[48,32,128]{2,1,0:T(8,128)S(1)}, f32[16,32,128]{2,1,0:T(8,128)S(1)}, f32[32,24,128]{2,1,0:T(8,128)}) custom-call(s32[8]{0:T(128)} %levels.5, s32[2]{0:T(128)} %owners.5, f32[32,16,128]{2,1,0:T(8,128)S(1)} %all-to-all-done.1.shares, f32[48,32,128]{2,1,0:T(8,128)S(1)} %bitcast.4, f32[16,32,128]{2,1,0:T(8,128)S(1)} %copy-done.1, ...), custom_call_target="tpu_custom_call" | custom-call | tf_op jit(solution)/shard_map/inner_step/pallas_call | solution.py:424
  43.5 3.7 %all-to-all-start.2 = ((f32[32,24,128]{2,1,0:T(8,128)}), f32[32,24,128]{2,1,0:T(8,128)S(1)}, u32[]{:S(2)}, u32[]{:S(2)}) async-start(f32[32,24,128]{2,1,0:T(8,128)} %get-tuple-element.33), calls=%async_computation.2 | async-start | bytes 786432 | tf_op jit(solution)/shard_map/all_to_all | solution.py:405
  47.2 0.3 edges.3
  47.5 2.2 %collective-permute-start.4 = (f32[64,128]{1,0:T(8,128)S(1)}, f32[64,128]{1,0:T(8,128)S(1)}, u32[]{:S(2)}, u32[]{:S(2)}) collective-permute-start(f32[64,128]{1,0:T(8,128)S(1)} %get-tuple-element.36), channel_id=1, source_target_pairs={{0,4},{4,8},{8,12},{12,16},{16,20},{20,24},{24,28},{1,5},{5,9},{9,... | collective-permute-start | bytes 98312 | tf_op jit(solution)/shard_map/ppermute | solution.py:340
  49.7 1.3 %collective-permute-start.5 = (f32[64,128]{1,0:T(8,128)S(1)}, f32[64,128]{1,0:T(8,128)S(1)}, u32[]{:S(2)}, u32[]{:S(2)}) collective-permute-start(f32[64,128]{1,0:T(8,128)S(1)} %get-tuple-element.37), channel_id=1, source_target_pairs={{4,0},{8,4},{12,8},{16,12},{20,16},{24,20},{28,24},{5,1},{9,5},{13... | collective-permute-start | bytes 98312 | tf_op jit(solution)/shard_map/ppermute | solution.py:340
  51.0 2.9 %collective-permute-done.5.east = f32[64,128]{1,0:T(8,128)S(1)} collective-permute-done((f32[64,128]{1,0:T(8,128)S(1)}, f32[64,128]{1,0:T(8,128)S(1)}, u32[]{:S(2)}, u32[]{:S(2)}) %collective-permute-start.5) | collective-permute-done | bytes 32800 | tf_op jit(solution)/shard_map/ppermute | solution.py:340
  53.9 5.1 %all-to-all-done.2.parts = f32[32,24,128]{2,1,0:T(8,128)S(1)} async-done(((f32[32,24,128]{2,1,0:T(8,128)}), f32[32,24,128]{2,1,0:T(8,128)S(1)}, u32[]{:S(2)}, u32[]{:S(2)}) %all-to-all-start.2) | async-done | bytes 393248 | tf_op jit(solution)/shard_map/all_to_all | solution.py:405
  59.0 1.6 %share_sum.3 = f32[32,16,128]{2,1,0:T(8,128)} custom-call(s32[24]{0:T(128)S(1)} %reshape.13.cuts, f32[32,24,128]{2,1,0:T(8,128)S(1)} %all-to-all-done.2.parts, bf16[512,256]{1,0:T(8,128)(2,1)S(1)} %copy-done.2, bf16[512,128]{1,0:T(8,128)(2,1)S(1)} %copy-done.3), custom_call_target="tpu_custom_call" | custom-call | tf_op jit(solution)/shard_map/share_sum/pallas_call | solution.py:407
  60.6 3.9 %all-to-all-start.3 = ((f32[32,16,128]{2,1,0:T(8,128)}), f32[32,16,128]{2,1,0:T(8,128)S(1)}, u32[]{:S(2)}, u32[]{:S(2)}) async-start(f32[32,16,128]{2,1,0:T(8,128)} %share_sum.3), calls=%async_computation.3 | async-start | bytes 524288 | tf_op jit(solution)/shard_map/all_to_all | solution.py:417
  64.5 1.3 %collective-permute-start.7 = (f32[32,128]{1,0:T(8,128)S(1)}, f32[32,128]{1,0:T(8,128)S(1)}, u32[]{:S(2)}, u32[]{:S(2)}) collective-permute-start(f32[32,128]{1,0:T(8,128)S(1)} %get-tuple-element.43), channel_id=1, source_target_pairs={{1,0},{2,1},{3,2},{5,4},{6,5},{7,6},{9,8},{10,9},{11,10},{13,12},{... | collective-permute-start | bytes 49160 | tf_op jit(solution)/shard_map/ppermute | solution.py:340
  65.8 4.5 %collective-permute-start.6 = (f32[32,128]{1,0:T(8,128)S(1)}, f32[32,128]{1,0:T(8,128)S(1)}, u32[]{:S(2)}, u32[]{:S(2)}) collective-permute-start(f32[32,128]{1,0:T(8,128)S(1)} %get-tuple-element.43), channel_id=1, source_target_pairs={{0,1},{1,2},{2,3},{4,5},{5,6},{6,7},{8,9},{9,10},{10,11},{12,13},{... | collective-permute-start | bytes 49160 | tf_op jit(solution)/shard_map/ppermute | solution.py:340
  70.3 1.4 %collective-permute-done.6.south = f32[32,128]{1,0:T(8,128)S(1)} collective-permute-done((f32[32,128]{1,0:T(8,128)S(1)}, f32[32,128]{1,0:T(8,128)S(1)}, u32[]{:S(2)}, u32[]{:S(2)}) %collective-permute-start.6) | collective-permute-done | bytes 16416 | tf_op jit(solution)/shard_map/ppermute | solution.py:340
  71.7 2.9 %all-to-all-done.3.shares = f32[32,16,128]{2,1,0:T(8,128)S(1)} async-done(((f32[32,16,128]{2,1,0:T(8,128)}), f32[32,16,128]{2,1,0:T(8,128)S(1)}, u32[]{:S(2)}, u32[]{:S(2)}) %all-to-all-start.3) | async-done | bytes 262176 | tf_op jit(solution)/shard_map/all_to_all | solution.py:417
  74.7 4.0 %final_step.1 = (f32[48,32,128]{2,1,0:T(8,128)}, f32[16,32,128]{2,1,0:T(8,128)}) custom-call(s32[8]{0:T(128)} %levels.5, s32[2]{0:T(128)} %owners.5, f32[32,16,128]{2,1,0:T(8,128)S(1)} %all-to-all-done.3.shares, f32[48,32,128]{2,1,0:T(8,128)S(1)} %get-tuple-element.34.fields, f32[16,32,128]{2,1,0:T(8,128)S(1)} %get-tuple-element.35.plume, ...), custom_call_target="tpu_custom_call" | custom-call | tf_op jit(solution)/shard_map/final_step/pallas_call | solution.py:424
  (10 shorter events, 0.0 us)
Async XLA Ops:
  0.6 10.9 %copy-start = (f32[3,16,32,128]{3,2,1,0:T(8,128)S(1)}, f32[3,16,32,128]{3,2,1,0:T(8,128)}, u32[]{:S(2)}) copy-start(f32[3,16,32,128]{3,2,1,0:T(8,128)} %param.12) | copy-start | bytes 2359300
  0.6 10.9 %copy-start.1 = (f32[16,32,128]{2,1,0:T(8,128)S(1)}, f32[16,32,128]{2,1,0:T(8,128)}, u32[]{:S(2)}) copy-start(f32[16,32,128]{2,1,0:T(8,128)} %plume.3) | copy-start | bytes 786436
  4.1 12.0 %copy-start.4 = (s32[3,8]{1,0:T(4,128)S(1)}, s32[3,8]{1,0:T(4,128)}, u32[]{:S(2)}) copy-start(s32[3,8]{1,0:T(4,128)} %param.14) | copy-start | bytes 292
  4.1 19.2 %copy-start.2 = (bf16[512,256]{1,0:T(8,128)(2,1)S(1)}, bf16[512,256]{1,0:T(8,128)(2,1)}, u32[]{:S(2)}) copy-start(bf16[512,256]{1,0:T(8,128)(2,1)} %constant.13.clone.x_back) | copy-start | bytes 786436
  4.2 19.2 %copy-start.3 = (bf16[512,128]{1,0:T(8,128)(2,1)S(1)}, bf16[512,128]{1,0:T(8,128)(2,1)}, u32[]{:S(2)}) copy-start(bf16[512,128]{1,0:T(8,128)(2,1)} %constant.14.clone.x_beside) | copy-start | bytes 393220
  4.2 19.1 %all-to-all-start = ((f32[32,24,128]{2,1,0:T(8,128)}), f32[32,24,128]{2,1,0:T(8,128)S(1)}, u32[]{:S(2)}, u32[]{:S(2)}) async-start(f32[32,24,128]{2,1,0:T(8,128)} %first_modes.1), calls=%async_computation | async-start | bytes 786432 | tf_op jit(solution)/shard_map/all_to_all | solution.py:405
  12.7 3.6 %collective-permute-start = (f32[64,128]{1,0:T(8,128)S(1)}, f32[64,128]{1,0:T(8,128)S(1)}, u32[]{:S(2)}, u32[]{:S(2)}) collective-permute-start(f32[64,128]{1,0:T(8,128)S(1)} %get-tuple-element.24), channel_id=1, source_target_pairs={{0,4},{4,8},{8,12},{12,16},{16,20},{20,24},{24,28},{1,5},{5,9},{9,... | collective-permute-start | bytes 98312 | tf_op jit(solution)/shard_map/ppermute | solution.py:340
  14.8 4.2 %collective-permute-start.1 = (f32[64,128]{1,0:T(8,128)S(1)}, f32[64,128]{1,0:T(8,128)S(1)}, u32[]{:S(2)}, u32[]{:S(2)}) collective-permute-start(f32[64,128]{1,0:T(8,128)S(1)} %get-tuple-element.25), channel_id=1, source_target_pairs={{4,0},{8,4},{12,8},{16,12},{20,16},{24,20},{28,24},{5,1},{9,5},{13... | collective-permute-start | bytes 98312 | tf_op jit(solution)/shard_map/ppermute | solution.py:340
  24.9 14.2 %all-to-all-start.1 = ((f32[32,16,128]{2,1,0:T(8,128)}), f32[32,16,128]{2,1,0:T(8,128)S(1)}, u32[]{:S(2)}, u32[]{:S(2)}) async-start(f32[32,16,128]{2,1,0:T(8,128)} %share_sum.2), calls=%async_computation.1 | async-start | bytes 524288 | tf_op jit(solution)/shard_map/all_to_all | solution.py:417
  28.9 5.9 %collective-permute-start.3 = (f32[32,128]{1,0:T(8,128)S(1)}, f32[32,128]{1,0:T(8,128)S(1)}, u32[]{:S(2)}, u32[]{:S(2)}) collective-permute-start(f32[32,128]{1,0:T(8,128)S(1)} %get-tuple-element.31), channel_id=1, source_target_pairs={{1,0},{2,1},{3,2},{5,4},{6,5},{7,6},{9,8},{10,9},{11,10},{13,12},{... | collective-permute-start | bytes 49160 | tf_op jit(solution)/shard_map/ppermute | solution.py:340
  30.2 6.0 %collective-permute-start.2 = (f32[32,128]{1,0:T(8,128)S(1)}, f32[32,128]{1,0:T(8,128)S(1)}, u32[]{:S(2)}, u32[]{:S(2)}) collective-permute-start(f32[32,128]{1,0:T(8,128)S(1)} %get-tuple-element.31), channel_id=1, source_target_pairs={{0,1},{1,2},{2,3},{4,5},{5,6},{6,7},{8,9},{9,10},{10,11},{12,13},{... | collective-permute-start | bytes 49160 | tf_op jit(solution)/shard_map/ppermute | solution.py:340
  43.5 15.5 %all-to-all-start.2 = ((f32[32,24,128]{2,1,0:T(8,128)}), f32[32,24,128]{2,1,0:T(8,128)S(1)}, u32[]{:S(2)}, u32[]{:S(2)}) async-start(f32[32,24,128]{2,1,0:T(8,128)} %get-tuple-element.33), calls=%async_computation.2 | async-start | bytes 786432 | tf_op jit(solution)/shard_map/all_to_all | solution.py:405
  47.5 3.5 %collective-permute-start.4 = (f32[64,128]{1,0:T(8,128)S(1)}, f32[64,128]{1,0:T(8,128)S(1)}, u32[]{:S(2)}, u32[]{:S(2)}) collective-permute-start(f32[64,128]{1,0:T(8,128)S(1)} %get-tuple-element.36), channel_id=1, source_target_pairs={{0,4},{4,8},{8,12},{12,16},{16,20},{20,24},{24,28},{1,5},{5,9},{9,... | collective-permute-start | bytes 98312 | tf_op jit(solution)/shard_map/ppermute | solution.py:340
  49.7 4.2 %collective-permute-start.5 = (f32[64,128]{1,0:T(8,128)S(1)}, f32[64,128]{1,0:T(8,128)S(1)}, u32[]{:S(2)}, u32[]{:S(2)}) collective-permute-start(f32[64,128]{1,0:T(8,128)S(1)} %get-tuple-element.37), channel_id=1, source_target_pairs={{4,0},{8,4},{12,8},{16,12},{20,16},{24,20},{28,24},{5,1},{9,5},{13... | collective-permute-start | bytes 98312 | tf_op jit(solution)/shard_map/ppermute | solution.py:340
  60.6 14.1 %all-to-all-start.3 = ((f32[32,16,128]{2,1,0:T(8,128)}), f32[32,16,128]{2,1,0:T(8,128)S(1)}, u32[]{:S(2)}, u32[]{:S(2)}) async-start(f32[32,16,128]{2,1,0:T(8,128)} %share_sum.3), calls=%async_computation.3 | async-start | bytes 524288 | tf_op jit(solution)/shard_map/all_to_all | solution.py:417
  64.5 5.9 %collective-permute-start.7 = (f32[32,128]{1,0:T(8,128)S(1)}, f32[32,128]{1,0:T(8,128)S(1)}, u32[]{:S(2)}, u32[]{:S(2)}) collective-permute-start(f32[32,128]{1,0:T(8,128)S(1)} %get-tuple-element.43), channel_id=1, source_target_pairs={{1,0},{2,1},{3,2},{5,4},{6,5},{7,6},{9,8},{10,9},{11,10},{13,12},{... | collective-permute-start | bytes 49160 | tf_op jit(solution)/shard_map/ppermute | solution.py:340
  65.8 6.0 %collective-permute-start.6 = (f32[32,128]{1,0:T(8,128)S(1)}, f32[32,128]{1,0:T(8,128)S(1)}, u32[]{:S(2)}, u32[]{:S(2)}) collective-permute-start(f32[32,128]{1,0:T(8,128)S(1)} %get-tuple-element.43), channel_id=1, source_target_pairs={{0,1},{1,2},{2,3},{4,5},{5,6},{6,7},{8,9},{9,10},{10,11},{12,13},{... | collective-permute-start | bytes 49160 | tf_op jit(solution)/shard_map/ppermute | solution.py:340

commit v11 on v10

--- a/solution.py
+++ b/solution.py
@@ -138,12 +138,13 @@
     return (c // level_count) * level_total + levels[c % level_count]
 
 
-def first_kernel(n_gy, level_total, levels, owners, fields_all, parent_all, x_fwd_all, y_fwd_all,
-                 modes, fields, sems, parent, x_fwd, y_fwd, turned, work):
+def first_kernel(n_gy, level_total, levels_all, owners_all, fields_all, parent_all, x_fwd_all,
+                 y_fwd_all, modes, levels, owners, fields, sems, parent, x_fwd, y_fwd, turned,
+                 work):
     gx, gy = lax.axis_index("gx"), lax.axis_index("gy")
     copies = fetch_all(sems, [
-        (fields_all, fields), (x_fwd_all.at[gx], x_fwd), (y_fwd_all.at[gy], y_fwd),
-        (parent_all.at[0, 0], parent)])
+        (levels_all, levels), (owners_all, owners), (fields_all, fields),
+        (x_fwd_all.at[gx], x_fwd), (y_fwd_all.at[gy], y_fwd), (parent_all.at[0, 0], parent)])
     for copy in copies:
         copy.wait()
     level_count = parent.shape[0] // 3
@@ -230,19 +231,17 @@
             out[g * n_gy + h, rows:, :] = beside
 
 
-def step_kernel(n_gy, step, last, levels, owners, shares, fields, plume,
-                west, east, south, north, y_back, source_all, *rest):
+def step_kernel(n_gy, step, last, levels, owners, shares, fields, plume, source,
+                west, east, south, north, y_back, *rest):
     gx, gy = lax.axis_index("gx"), lax.axis_index("gy")
-    extra = []
+    copies = []
     if last:
-        fields_out, plume_out, slabs, beside, spread, spread_edges, source, sems = rest
+        fields_out, plume_out, slabs, beside, spread, spread_edges = rest
     else:
         (parent_all, x_fwd_all, y_fwd_all, fields_out, plume_out, modes,
-         slabs, beside, spread, spread_edges, source, sems, parent, x_fwd, y_fwd, turned,
-         work) = rest
-        extra = [(x_fwd_all.at[gx], x_fwd), (y_fwd_all.at[gy], y_fwd),
-                 (parent_all.at[0, step + 1], parent)]
-    copies = fetch_all(sems, [(source_all, source)] + extra)
+         slabs, beside, spread, spread_edges, sems, parent, x_fwd, y_fwd, turned, work) = rest
+        copies = fetch_all(sems, [(x_fwd_all.at[gx], x_fwd), (y_fwd_all.at[gy], y_fwd),
+                                  (parent_all.at[0, step + 1], parent)])
     level_total, cells_x, cells_y = plume.shape
     field_rows = fields.shape[0]
     total = field_rows + level_total
@@ -292,8 +291,6 @@
     columns = jnp.where(
         lane % 2 == 0, pltpu.roll(north[...], cells_y - 1, 1), pltpu.roll(south[...], 1, 1))
 
-    copies[0].wait()
-
     def advance(c, parts):
         centre, to_west, to_east, to_south, to_north = parts
         a = slabs[c, inner]
@@ -325,7 +322,7 @@
 
     if last:
         return
-    for copy in copies[1:]:
+    for copy in copies:
         copy.wait()
     emit_modes(
         lambda c: fields_out[slab_of(levels, c, level_count, level_total)],
@@ -365,23 +362,22 @@
 
     mode_shape = f32((devices, 2 * rows, LANES))
     step_scratch = [vmem(total, cells_x + 2 * PAD, cells_y), vmem(field_rows, cells_x, cells_y),
-                    vmem(devices * rows, LANES), vmem(devices * rows, LANES),
-                    vmem(level_total, cells_x, cells_y), pltpu.SemaphoreType.DMA((4,))]
+                    vmem(devices * rows, LANES), vmem(devices * rows, LANES)]
     mode_scratch = [vmem(nudged, 4 * KX * KX), table_space(x_fwd),
                     table_space(y_fwd), vmem(nudged, KX, LANES),
                     vmem(devices * rows, 2 * LANES)]
-    levels, owners = in_hbm(levels), in_hbm(owners)
 
     modes = pl.pallas_call(
         functools.partial(first_kernel, n_gy, level_total),
         out_shape=mode_shape,
-        in_specs=[SMEM, SMEM] + [HBM] * 4,
+        in_specs=[HBM] * 6,
         out_specs=VMEM,
-        scratch_shapes=[vmem(field_rows, cells_x, cells_y), pltpu.SemaphoreType.DMA((4,))]
+        scratch_shapes=[pltpu.SMEM(levels.shape, jnp.int32), pltpu.SMEM(owners.shape, jnp.int32),
+                        vmem(field_rows, cells_x, cells_y), pltpu.SemaphoreType.DMA((6,))]
         + mode_scratch,
         compiler_params=limit(8),
         name="first_modes",
-    )(levels, owners, in_hbm(flat), in_hbm(parent_modes), in_hbm(x_fwd), in_hbm(y_fwd))
+    )(*map(in_hbm, (levels, owners, flat, parent_modes, x_fwd, y_fwd)))
     for step in range(STEPS):
         last = step == STEPS - 1
         edge_shapes = [f32((total, cells_y)), f32((total, cells_y)), f32((cells_x, 2 * total))]
@@ -416,17 +412,18 @@
         south, north = swap("gy", cols, cols)
         shares = lax.all_to_all(share, AXES, 0, 0, tiled=True)
         out_shape = [f32(flat.shape), f32(plume.shape)]
-        operands = [levels, owners, shares, flat, plume, west, east, south, north, back_table,
-                    in_hbm(source)]
+        operands = [levels, owners, shares, flat, plume, source, west, east, south, north,
+                    back_table]
         if not last:
             out_shape.append(mode_shape)
             operands += [in_hbm(parent_modes), in_hbm(x_fwd), in_hbm(y_fwd)]
         results = pl.pallas_call(
             functools.partial(step_kernel, n_gy, step, last),
             out_shape=out_shape,
-            in_specs=[SMEM, SMEM] + [VMEM] * 8 + [HBM] * (len(operands) - 10),
+            in_specs=[SMEM, SMEM] + [VMEM] * 9 + [HBM] * (len(operands) - 11),
             out_specs=[VMEM] * len(out_shape),
-            scratch_shapes=step_scratch + ([] if last else mode_scratch),
+            scratch_shapes=step_scratch
+            + ([] if last else [pltpu.SemaphoreType.DMA((3,))] + mode_scratch),
             compiler_params=limit(20),
             name="final_step" if last else "inner_step",
         )(*operands)

time: 79.6 us -> 77.5 us (0.974)
  Pallas kernels: 16.6 us -> 14.8 us
    pallas_call x2, Pallas kernels: 8.41 us -> 7.37 us  [local(): pl.pallas_call(functools.partial(step_kernel, n_gy, step, last), out_shap...]
where the time goes in v11:
time: 77.5 us; the launch traced here: 76.9 us
  starting transfers between devices  37.3 us (48%)
  waiting for transfers between devices  23.8 us (31%)
  Pallas kernels  14.8 us (19%)
  between operations  0.87 us (1%)
    ppermute x4, starting transfers between devices, swap(): lax.ppermute(to_next, axis, up)  13.4 us
    all_to_all x2, starting transfers between devices, local(): parts = lax.all_to_all(modes, AXES, 0, 0, tiled=True)  11 us
    all_to_all x2, waiting for transfers between devices, local(): parts = lax.all_to_all(modes, AXES, 0, 0, tiled=True)  9.29 us
    all_to_all x2, starting transfers between devices, local(): shares = lax.all_to_all(share, AXES, 0, 0, tiled=True)  7.72 us
    pallas_call x2, Pallas kernels, local(): pl.pallas_call(functools.partial(step_kernel, n_gy, step, last), out_shap...  7.37 us
    all_to_all x2, waiting for transfers between devices, local(): shares = lax.all_to_all(share, AXES, 0, 0, tiled=True)  5.86 us
    ppermute x4, waiting for transfers between devices, swap(): lax.ppermute(to_previous, axis, down)  5.77 us
    ppermute x4, starting transfers between devices, swap(): lax.ppermute(to_previous, axis, down)  5.17 us
  transfers between devices with their start and end apart: 12, of which 8 were waited for; matrix products, arithmetic and copies ran while one was open for 0% of the time, Pallas kernels for 2%

profile of v11, /device:TPU:0, one launch (start us, length us, event | category | flops | bytes accessed | tf_op | source)
XLA Modules:
  0.0 76.9 jit_solution(526161418422010854)
XLA Ops:
  0.6 2.8 %first_modes.1 = f32[32,24,128]{2,1,0:T(8,128)} custom-call(s32[8]{0:T(128)} %levels.3, s32[2]{0:T(128)} %owners.3, f32[48,32,128]{2,1,0:T(8,128)} %bitcast.2, f32[1,2,24,4096]{3,2,1,0:T(8,128)} %rest_0_.2, bf16[8,384,256]{2,1,0:T(8,128)(2,1)} %constant.10.clone.x_fwd_all.rest_1_, bf16[4,64,384]{2,1,0:T(8,128)(2,1)} %constant.11.clone.y_fwd_all.rest_2_), custom_call_target="tpu_custom_call" | custom-call | tf_op jit(solution)/shard_map/first_modes/pallas_call | solution.py:370
  3.4 0.0 copy-start.7
  3.4 0.0 copy-start.3
  3.5 0.0 copy-start.4
  3.5 7.3 %all-to-all-start = ((f32[32,24,128]{2,1,0:T(8,128)}), f32[32,24,128]{2,1,0:T(8,128)S(1)}, u32[]{:S(2)}, u32[]{:S(2)}) async-start(f32[32,24,128]{2,1,0:T(8,128)} %first_modes.1), calls=%async_computation | async-start | bytes 786432 | tf_op jit(solution)/shard_map/all_to_all | solution.py:401
  10.8 0.0 copy-start.2
  10.8 1.2 %edges.2 = (f32[64,128]{1,0:T(8,128)S(1)}, f32[64,128]{1,0:T(8,128)S(1)}, f32[32,128]{1,0:T(8,128)S(1)}, bf16[192,256]{1,0:T(8,128)(2,1)S(1)}) custom-call(f32[48,32,128]{2,1,0:T(8,128)S(1)} %bitcast.3, f32[16,32,128]{2,1,0:T(8,128)S(1)} %copy-done.1, bf16[4,192,256]{2,1,0:T(8,128)(2,1)} %constant.12.clone.rest_0_), custom_call_target="tpu_custom_call" | custom-call | tf_op jit(solution)/shard_map/edges/pallas_call | solution.py:388
  12.0 2.2 %collective-permute-start = (f32[64,128]{1,0:T(8,128)S(1)}, f32[64,128]{1,0:T(8,128)S(1)}, u32[]{:S(2)}, u32[]{:S(2)}) collective-permute-start(f32[64,128]{1,0:T(8,128)S(1)} %get-tuple-element.24), channel_id=1, source_target_pairs={{0,4},{4,8},{8,12},{12,16},{16,20},{20,24},{24,28},{1,5},{5,9},{9,... | collective-permute-start | bytes 98312 | tf_op jit(solution)/shard_map/ppermute | solution.py:337
  14.2 1.3 %collective-permute-start.1 = (f32[64,128]{1,0:T(8,128)S(1)}, f32[64,128]{1,0:T(8,128)S(1)}, u32[]{:S(2)}, u32[]{:S(2)}) collective-permute-start(f32[64,128]{1,0:T(8,128)S(1)} %get-tuple-element.25), channel_id=1, source_target_pairs={{4,0},{8,4},{12,8},{16,12},{20,16},{24,20},{28,24},{5,1},{9,5},{13... | collective-permute-start | bytes 98312 | tf_op jit(solution)/shard_map/ppermute | solution.py:337
  15.5 0.1 reshape.13.cuts
  15.6 2.8 %collective-permute-done.1.east = f32[64,128]{1,0:T(8,128)S(1)} collective-permute-done((f32[64,128]{1,0:T(8,128)S(1)}, f32[64,128]{1,0:T(8,128)S(1)}, u32[]{:S(2)}, u32[]{:S(2)}) %collective-permute-start.1) | collective-permute-done | bytes 32800 | tf_op jit(solution)/shard_map/ppermute | solution.py:337
  18.4 4.2 %all-to-all-done.parts = f32[32,24,128]{2,1,0:T(8,128)S(1)} async-done(((f32[32,24,128]{2,1,0:T(8,128)}), f32[32,24,128]{2,1,0:T(8,128)S(1)}, u32[]{:S(2)}, u32[]{:S(2)}) %all-to-all-start) | async-done | bytes 393248 | tf_op jit(solution)/shard_map/all_to_all | solution.py:401
  22.6 1.6 %share_sum.2 = f32[32,16,128]{2,1,0:T(8,128)} custom-call(s32[24]{0:T(128)S(1)} %reshape.13.cuts, f32[32,24,128]{2,1,0:T(8,128)S(1)} %all-to-all-done.parts, bf16[512,256]{1,0:T(8,128)(2,1)S(1)} %copy-done.3, bf16[512,128]{1,0:T(8,128)(2,1)S(1)} %copy-done.4), custom_call_target="tpu_custom_call" | custom-call | tf_op jit(solution)/shard_map/share_sum/pallas_call | solution.py:403
  24.2 3.9 %all-to-all-start.1 = ((f32[32,16,128]{2,1,0:T(8,128)}), f32[32,16,128]{2,1,0:T(8,128)S(1)}, u32[]{:S(2)}, u32[]{:S(2)}) async-start(f32[32,16,128]{2,1,0:T(8,128)} %share_sum.2), calls=%async_computation.1 | async-start | bytes 524288 | tf_op jit(solution)/shard_map/all_to_all | solution.py:413
  28.1 1.3 %collective-permute-start.3 = (f32[32,128]{1,0:T(8,128)S(1)}, f32[32,128]{1,0:T(8,128)S(1)}, u32[]{:S(2)}, u32[]{:S(2)}) collective-permute-start(f32[32,128]{1,0:T(8,128)S(1)} %get-tuple-element.31), channel_id=1, source_target_pairs={{1,0},{2,1},{3,2},{5,4},{6,5},{7,6},{9,8},{10,9},{11,10},{13,12},{... | collective-permute-start | bytes 49160 | tf_op jit(solution)/shard_map/ppermute | solution.py:337
  29.4 4.5 %collective-permute-start.2 = (f32[32,128]{1,0:T(8,128)S(1)}, f32[32,128]{1,0:T(8,128)S(1)}, u32[]{:S(2)}, u32[]{:S(2)}) collective-permute-start(f32[32,128]{1,0:T(8,128)S(1)} %get-tuple-element.31), channel_id=1, source_target_pairs={{0,1},{1,2},{2,3},{4,5},{5,6},{6,7},{8,9},{9,10},{10,11},{12,13},{... | collective-permute-start | bytes 49160 | tf_op jit(solution)/shard_map/ppermute | solution.py:337
  34.0 1.4 %collective-permute-done.2.south = f32[32,128]{1,0:T(8,128)S(1)} collective-permute-done((f32[32,128]{1,0:T(8,128)S(1)}, f32[32,128]{1,0:T(8,128)S(1)}, u32[]{:S(2)}, u32[]{:S(2)}) %collective-permute-start.2) | collective-permute-done | bytes 16416 | tf_op jit(solution)/shard_map/ppermute | solution.py:337
  35.4 2.9 %all-to-all-done.1.shares = f32[32,16,128]{2,1,0:T(8,128)S(1)} async-done(((f32[32,16,128]{2,1,0:T(8,128)}), f32[32,16,128]{2,1,0:T(8,128)S(1)}, u32[]{:S(2)}, u32[]{:S(2)}) %all-to-all-start.1) | async-done | bytes 262176 | tf_op jit(solution)/shard_map/all_to_all | solution.py:413
  38.3 4.4 %inner_step.1 = (f32[48,32,128]{2,1,0:T(8,128)S(1)}, f32[16,32,128]{2,1,0:T(8,128)S(1)}, f32[32,24,128]{2,1,0:T(8,128)}) custom-call(s32[8]{0:T(128)S(1)} %copy-done.5, s32[2]{0:T(128)S(1)} %copy-done.6, f32[32,16,128]{2,1,0:T(8,128)S(1)} %all-to-all-done.1.shares, f32[48,32,128]{2,1,0:T(8,128)S(1)} %bitcast.4, f32[16,32,128]{2,1,0:T(8,128)S(1)} %copy-done.1, ...), custom_call_target="tpu_custom_call" | custom-call | tf_op jit(solution)/shard_map/inner_step/pallas_call | solution.py:420
  42.7 3.7 %all-to-all-start.2 = ((f32[32,24,128]{2,1,0:T(8,128)}), f32[32,24,128]{2,1,0:T(8,128)S(1)}, u32[]{:S(2)}, u32[]{:S(2)}) async-start(f32[32,24,128]{2,1,0:T(8,128)} %get-tuple-element.33), calls=%async_computation.2 | async-start | bytes 786432 | tf_op jit(solution)/shard_map/all_to_all | solution.py:401
  46.4 0.3 edges.3
  46.8 2.2 %collective-permute-start.4 = (f32[64,128]{1,0:T(8,128)S(1)}, f32[64,128]{1,0:T(8,128)S(1)}, u32[]{:S(2)}, u32[]{:S(2)}) collective-permute-start(f32[64,128]{1,0:T(8,128)S(1)} %get-tuple-element.36), channel_id=1, source_target_pairs={{0,4},{4,8},{8,12},{12,16},{16,20},{20,24},{24,28},{1,5},{5,9},{9,... | collective-permute-start | bytes 98312 | tf_op jit(solution)/shard_map/ppermute | solution.py:337
  48.9 1.3 %collective-permute-start.5 = (f32[64,128]{1,0:T(8,128)S(1)}, f32[64,128]{1,0:T(8,128)S(1)}, u32[]{:S(2)}, u32[]{:S(2)}) collective-permute-start(f32[64,128]{1,0:T(8,128)S(1)} %get-tuple-element.37), channel_id=1, source_target_pairs={{4,0},{8,4},{12,8},{16,12},{20,16},{24,20},{28,24},{5,1},{9,5},{13... | collective-permute-start | bytes 98312 | tf_op jit(solution)/shard_map/ppermute | solution.py:337
  50.2 2.9 %collective-permute-done.5.east = f32[64,128]{1,0:T(8,128)S(1)} collective-permute-done((f32[64,128]{1,0:T(8,128)S(1)}, f32[64,128]{1,0:T(8,128)S(1)}, u32[]{:S(2)}, u32[]{:S(2)}) %collective-permute-start.5) | collective-permute-done | bytes 32800 | tf_op jit(solution)/shard_map/ppermute | solution.py:337
  53.2 5.1 %all-to-all-done.2.parts = f32[32,24,128]{2,1,0:T(8,128)S(1)} async-done(((f32[32,24,128]{2,1,0:T(8,128)}), f32[32,24,128]{2,1,0:T(8,128)S(1)}, u32[]{:S(2)}, u32[]{:S(2)}) %all-to-all-start.2) | async-done | bytes 393248 | tf_op jit(solution)/shard_map/all_to_all | solution.py:401
  58.3 1.6 %share_sum.3 = f32[32,16,128]{2,1,0:T(8,128)} custom-call(s32[24]{0:T(128)S(1)} %reshape.13.cuts, f32[32,24,128]{2,1,0:T(8,128)S(1)} %all-to-all-done.2.parts, bf16[512,256]{1,0:T(8,128)(2,1)S(1)} %copy-done.3, bf16[512,128]{1,0:T(8,128)(2,1)S(1)} %copy-done.4), custom_call_target="tpu_custom_call" | custom-call | tf_op jit(solution)/shard_map/share_sum/pallas_call | solution.py:403
  59.9 3.9 %all-to-all-start.3 = ((f32[32,16,128]{2,1,0:T(8,128)}), f32[32,16,128]{2,1,0:T(8,128)S(1)}, u32[]{:S(2)}, u32[]{:S(2)}) async-start(f32[32,16,128]{2,1,0:T(8,128)} %share_sum.3), calls=%async_computation.3 | async-start | bytes 524288 | tf_op jit(solution)/shard_map/all_to_all | solution.py:413
  63.7 1.3 %collective-permute-start.7 = (f32[32,128]{1,0:T(8,128)S(1)}, f32[32,128]{1,0:T(8,128)S(1)}, u32[]{:S(2)}, u32[]{:S(2)}) collective-permute-start(f32[32,128]{1,0:T(8,128)S(1)} %get-tuple-element.43), channel_id=1, source_target_pairs={{1,0},{2,1},{3,2},{5,4},{6,5},{7,6},{9,8},{10,9},{11,10},{13,12},{... | collective-permute-start | bytes 49160 | tf_op jit(solution)/shard_map/ppermute | solution.py:337
  65.0 4.5 %collective-permute-start.6 = (f32[32,128]{1,0:T(8,128)S(1)}, f32[32,128]{1,0:T(8,128)S(1)}, u32[]{:S(2)}, u32[]{:S(2)}) collective-permute-start(f32[32,128]{1,0:T(8,128)S(1)} %get-tuple-element.43), channel_id=1, source_target_pairs={{0,1},{1,2},{2,3},{4,5},{5,6},{6,7},{8,9},{9,10},{10,11},{12,13},{... | collective-permute-start | bytes 49160 | tf_op jit(solution)/shard_map/ppermute | solution.py:337
  69.6 1.4 %collective-permute-done.6.south = f32[32,128]{1,0:T(8,128)S(1)} collective-permute-done((f32[32,128]{1,0:T(8,128)S(1)}, f32[32,128]{1,0:T(8,128)S(1)}, u32[]{:S(2)}, u32[]{:S(2)}) %collective-permute-start.6) | collective-permute-done | bytes 16416 | tf_op jit(solution)/shard_map/ppermute | solution.py:337
  71.0 2.9 %all-to-all-done.3.shares = f32[32,16,128]{2,1,0:T(8,128)S(1)} async-done(((f32[32,16,128]{2,1,0:T(8,128)}), f32[32,16,128]{2,1,0:T(8,128)S(1)}, u32[]{:S(2)}, u32[]{:S(2)}) %all-to-all-start.3) | async-done | bytes 262176 | tf_op jit(solution)/shard_map/all_to_all | solution.py:413
  73.9 3.0 %final_step.1 = (f32[48,32,128]{2,1,0:T(8,128)}, f32[16,32,128]{2,1,0:T(8,128)}) custom-call(s32[8]{0:T(128)S(1)} %copy-done.5, s32[2]{0:T(128)S(1)} %copy-done.6, f32[32,16,128]{2,1,0:T(8,128)S(1)} %all-to-all-done.3.shares, f32[48,32,128]{2,1,0:T(8,128)S(1)} %get-tuple-element.34.fields, f32[16,32,128]{2,1,0:T(8,128)S(1)} %get-tuple-element.35.plume, ...), custom_call_target="tpu_custom_call" | custom-call | tf_op jit(solution)/shard_map/final_step/pallas_call | solution.py:420
  (16 shorter events, 0.0 us)
Async XLA Ops:
  0.6 10.2 %copy-start = (f32[3,16,32,128]{3,2,1,0:T(8,128)S(1)}, f32[3,16,32,128]{3,2,1,0:T(8,128)}, u32[]{:S(2)}) copy-start(f32[3,16,32,128]{3,2,1,0:T(8,128)} %param.12) | copy-start | bytes 2359300
  0.6 10.2 %copy-start.1 = (f32[16,32,128]{2,1,0:T(8,128)S(1)}, f32[16,32,128]{2,1,0:T(8,128)}, u32[]{:S(2)}) copy-start(f32[16,32,128]{2,1,0:T(8,128)} %plume.3) | copy-start | bytes 786436
  3.4 12.0 %copy-start.7 = (s32[3,8]{1,0:T(4,128)S(1)}, s32[3,8]{1,0:T(4,128)}, u32[]{:S(2)}) copy-start(s32[3,8]{1,0:T(4,128)} %param.14) | copy-start | bytes 292
  3.4 19.2 %copy-start.3 = (bf16[512,256]{1,0:T(8,128)(2,1)S(1)}, bf16[512,256]{1,0:T(8,128)(2,1)}, u32[]{:S(2)}) copy-start(bf16[512,256]{1,0:T(8,128)(2,1)} %constant.13.clone.x_back) | copy-start | bytes 786436
  3.5 19.2 %copy-start.4 = (bf16[512,128]{1,0:T(8,128)(2,1)S(1)}, bf16[512,128]{1,0:T(8,128)(2,1)}, u32[]{:S(2)}) copy-start(bf16[512,128]{1,0:T(8,128)(2,1)} %constant.14.clone.x_beside) | copy-start | bytes 393220
  3.5 19.1 %all-to-all-start = ((f32[32,24,128]{2,1,0:T(8,128)}), f32[32,24,128]{2,1,0:T(8,128)S(1)}, u32[]{:S(2)}, u32[]{:S(2)}) async-start(f32[32,24,128]{2,1,0:T(8,128)} %first_modes.1), calls=%async_computation | async-start | bytes 786432 | tf_op jit(solution)/shard_map/all_to_all | solution.py:401
  10.8 27.5 %copy-start.2 = (f32[16,32,128]{2,1,0:T(8,128)S(1)}, f32[16,32,128]{2,1,0:T(8,128)}, u32[]{:S(2)}) copy-start(f32[16,32,128]{2,1,0:T(8,128)} %source.3) | copy-start | bytes 786436
  10.8 27.5 %copy-start.5 = (s32[8]{0:T(128)S(1)}, s32[8]{0:T(128)}, u32[]{:S(2)}) copy-start(s32[8]{0:T(128)} %levels.3) | copy-start | bytes 100
  10.8 27.5 %copy-start.6 = (s32[2]{0:T(128)S(1)}, s32[2]{0:T(128)}, u32[]{:S(2)}) copy-start(s32[2]{0:T(128)} %owners.3) | copy-start | bytes 28
  12.0 3.6 %collective-permute-start = (f32[64,128]{1,0:T(8,128)S(1)}, f32[64,128]{1,0:T(8,128)S(1)}, u32[]{:S(2)}, u32[]{:S(2)}) collective-permute-start(f32[64,128]{1,0:T(8,128)S(1)} %get-tuple-element.24), channel_id=1, source_target_pairs={{0,4},{4,8},{8,12},{12,16},{16,20},{20,24},{24,28},{1,5},{5,9},{9,... | collective-permute-start | bytes 98312 | tf_op jit(solution)/shard_map/ppermute | solution.py:337
  14.2 4.2 %collective-permute-start.1 = (f32[64,128]{1,0:T(8,128)S(1)}, f32[64,128]{1,0:T(8,128)S(1)}, u32[]{:S(2)}, u32[]{:S(2)}) collective-permute-start(f32[64,128]{1,0:T(8,128)S(1)} %get-tuple-element.25), channel_id=1, source_target_pairs={{4,0},{8,4},{12,8},{16,12},{20,16},{24,20},{28,24},{5,1},{9,5},{13... | collective-permute-start | bytes 98312 | tf_op jit(solution)/shard_map/ppermute | solution.py:337
  24.2 14.1 %all-to-all-start.1 = ((f32[32,16,128]{2,1,0:T(8,128)}), f32[32,16,128]{2,1,0:T(8,128)S(1)}, u32[]{:S(2)}, u32[]{:S(2)}) async-start(f32[32,16,128]{2,1,0:T(8,128)} %share_sum.2), calls=%async_computation.1 | async-start | bytes 524288 | tf_op jit(solution)/shard_map/all_to_all | solution.py:413
  28.1 5.9 %collective-permute-start.3 = (f32[32,128]{1,0:T(8,128)S(1)}, f32[32,128]{1,0:T(8,128)S(1)}, u32[]{:S(2)}, u32[]{:S(2)}) collective-permute-start(f32[32,128]{1,0:T(8,128)S(1)} %get-tuple-element.31), channel_id=1, source_target_pairs={{1,0},{2,1},{3,2},{5,4},{6,5},{7,6},{9,8},{10,9},{11,10},{13,12},{... | collective-permute-start | bytes 49160 | tf_op jit(solution)/shard_map/ppermute | solution.py:337
  29.4 6.0 %collective-permute-start.2 = (f32[32,128]{1,0:T(8,128)S(1)}, f32[32,128]{1,0:T(8,128)S(1)}, u32[]{:S(2)}, u32[]{:S(2)}) collective-permute-start(f32[32,128]{1,0:T(8,128)S(1)} %get-tuple-element.31), channel_id=1, source_target_pairs={{0,1},{1,2},{2,3},{4,5},{5,6},{6,7},{8,9},{9,10},{10,11},{12,13},{... | collective-permute-start | bytes 49160 | tf_op jit(solution)/shard_map/ppermute | solution.py:337
  42.7 15.5 %all-to-all-start.2 = ((f32[32,24,128]{2,1,0:T(8,128)}), f32[32,24,128]{2,1,0:T(8,128)S(1)}, u32[]{:S(2)}, u32[]{:S(2)}) async-start(f32[32,24,128]{2,1,0:T(8,128)} %get-tuple-element.33), calls=%async_computation.2 | async-start | bytes 786432 | tf_op jit(solution)/shard_map/all_to_all | solution.py:401
  46.8 3.5 %collective-permute-start.4 = (f32[64,128]{1,0:T(8,128)S(1)}, f32[64,128]{1,0:T(8,128)S(1)}, u32[]{:S(2)}, u32[]{:S(2)}) collective-permute-start(f32[64,128]{1,0:T(8,128)S(1)} %get-tuple-element.36), channel_id=1, source_target_pairs={{0,4},{4,8},{8,12},{12,16},{16,20},{20,24},{24,28},{1,5},{5,9},{9,... | collective-permute-start | bytes 98312 | tf_op jit(solution)/shard_map/ppermute | solution.py:337
  48.9 4.2 %collective-permute-start.5 = (f32[64,128]{1,0:T(8,128)S(1)}, f32[64,128]{1,0:T(8,128)S(1)}, u32[]{:S(2)}, u32[]{:S(2)}) collective-permute-start(f32[64,128]{1,0:T(8,128)S(1)} %get-tuple-element.37), channel_id=1, source_target_pairs={{4,0},{8,4},{12,8},{16,12},{20,16},{24,20},{28,24},{5,1},{9,5},{13... | collective-permute-start | bytes 98312 | tf_op jit(solution)/shard_map/ppermute | solution.py:337
  59.9 14.1 %all-to-all-start.3 = ((f32[32,16,128]{2,1,0:T(8,128)}), f32[32,16,128]{2,1,0:T(8,128)S(1)}, u32[]{:S(2)}, u32[]{:S(2)}) async-start(f32[32,16,128]{2,1,0:T(8,128)} %share_sum.3), calls=%async_computation.3 | async-start | bytes 524288 | tf_op jit(solution)/shard_map/all_to_all | solution.py:413
  63.7 5.9 %collective-permute-start.7 = (f32[32,128]{1,0:T(8,128)S(1)}, f32[32,128]{1,0:T(8,128)S(1)}, u32[]{:S(2)}, u32[]{:S(2)}) collective-permute-start(f32[32,128]{1,0:T(8,128)S(1)} %get-tuple-element.43), channel_id=1, source_target_pairs={{1,0},{2,1},{3,2},{5,4},{6,5},{7,6},{9,8},{10,9},{11,10},{13,12},{... | collective-permute-start | bytes 49160 | tf_op jit(solution)/shard_map/ppermute | solution.py:337
  65.0 6.0 %collective-permute-start.6 = (f32[32,128]{1,0:T(8,128)S(1)}, f32[32,128]{1,0:T(8,128)S(1)}, u32[]{:S(2)}, u32[]{:S(2)}) collective-permute-start(f32[32,128]{1,0:T(8,128)S(1)} %get-tuple-element.43), channel_id=1, source_target_pairs={{0,1},{1,2},{2,3},{4,5},{5,6},{6,7},{8,9},{9,10},{10,11},{12,13},{... | collective-permute-start | bytes 49160 | tf_op jit(solution)/shard_map/ppermute | solution.py:337

commit v12 on v11

--- a/solution.py
+++ b/solution.py
@@ -154,39 +154,33 @@
     )
 
 
-def edge_kernel(fields, plume, *rest):
-    copies = []
+def is_even(axis):
+    return lax.rem(lax.axis_index(axis), 2) == 0
+
+
+def edge_kernel(n_gy, period, fields, plume, *rest):
     if len(rest) > 3:
-        y_back_all, west, east, cols, y_back, sems = rest
-        copies = fetch_all(sems, [(y_back_all.at[lax.axis_index("gy")], y_back)])
+        cuts, first, second, cols, weights = rest
+        weights[...] = share_weights(n_gy, period, cuts, weights.shape)
     else:
-        west, east, cols = rest
+        first, second, cols = rest
+    even = is_even("gx")
     cells_x, cells_y = plume.shape[1:]
     field_rows = fields.shape[0]
     lane = lax.broadcasted_iota(jnp.int32, cols.shape, 1)
     acc = jnp.zeros(cols.shape, jnp.float32)
     for c in range(field_rows + plume.shape[0]):
         a = fields[c] if c < field_rows else plume[c - field_rows]
-        west[c : c + 1, :] = a[:1]
-        east[c : c + 1, :] = a[cells_x - 1 :]
+        west, east = a[:1], a[cells_x - 1 :]
+        first[c : c + 1, :] = jnp.where(even, east, west)
+        second[c : c + 1, :] = jnp.where(even, west, east)
         acc = jnp.where(lane // 2 == c, pltpu.roll(a, 2 * c + 1, 1), acc)
     cols[...] = acc
-    for copy in copies:
-        copy.wait()
-
-
-def beside_rows(rows):
-    return -(-rows // 3)
-
-
-def share_kernel(n_gx, n_gy, period, cuts, parts, x_back, x_beside, out):
-    devices = parts.shape[0]
-    rows = parts.shape[1] // 2
+
+
+def share_weights(n_gy, period, cuts, shape):
+    rows = shape[0] // 2
     me = lax.axis_index("gx") * n_gy + lax.axis_index("gy")
-    total = parts[0]
-    for d in range(1, devices):
-        total = total + parts[d]
-    shape = total.shape
     place = lax.broadcasted_iota(jnp.int32, shape, 0)
     lane = lax.broadcasted_iota(jnp.int32, shape, 1)
     p = (place >= rows).astype(jnp.int32)
@@ -199,7 +193,20 @@
         limit = jnp.where(slab == c, cuts[c], limit)
     keep = ((k % KX) < limit) & ((j % KX) < limit)
     factor = jnp.where(k == 0, 1.0, 2.0) * jnp.where(j == 0, 1.0, 2.0) * (1.0 / math.sqrt(period))
-    mismatch = jnp.where(keep, total * factor, 0.0)
+    return jnp.where(keep, factor, 0.0)
+
+
+def beside_rows(rows):
+    return -(-rows // 3)
+
+
+def share_kernel(n_gx, n_gy, weights, parts, x_back, x_beside, out):
+    devices = parts.shape[0]
+    rows = parts.shape[1] // 2
+    total = parts[0]
+    for d in range(1, devices):
+        total = total + parts[d]
+    mismatch = total * weights[...]
     both = jnp.concatenate([mismatch[:rows], mismatch[rows:]], axis=1)
     spare = -rows % 16
     if spare:
@@ -231,17 +238,23 @@
             out[g * n_gy + h, rows:, :] = beside
 
 
-def step_kernel(n_gy, step, last, levels, owners, shares, fields, plume, source,
-                west, east, south, north, y_back, *rest):
+def step_kernel(n_gy, step, last, shares, fields, plume, source, row_first, row_second,
+                col_first, col_second, y_back, levels_all, *rest):
     gx, gy = lax.axis_index("gx"), lax.axis_index("gy")
-    copies = []
+    extra = []
     if last:
-        fields_out, plume_out, slabs, beside, spread, spread_edges = rest
+        (fields_out, plume_out, levels, slabs, beside, spread, spread_edges, west, east,
+         sems) = rest
     else:
-        (parent_all, x_fwd_all, y_fwd_all, fields_out, plume_out, modes,
-         slabs, beside, spread, spread_edges, sems, parent, x_fwd, y_fwd, turned, work) = rest
-        copies = fetch_all(sems, [(x_fwd_all.at[gx], x_fwd), (y_fwd_all.at[gy], y_fwd),
-                                  (parent_all.at[0, step + 1], parent)])
+        (owners_all, parent_all, x_fwd_all, y_fwd_all, fields_out, plume_out, modes,
+         levels, slabs, beside, spread, spread_edges, west, east, sems,
+         owners, parent, x_fwd, y_fwd, turned, work) = rest
+        extra = [(owners_all, owners), (x_fwd_all.at[gx], x_fwd), (y_fwd_all.at[gy], y_fwd),
+                 (parent_all.at[0, step + 1], parent)]
+    copies = fetch_all(sems, [(levels_all, levels)] + extra)
+    even = is_even("gx")
+    west[...] = jnp.where(even, row_second[...], row_first[...])
+    east[...] = jnp.where(even, row_first[...], row_second[...])
     level_total, cells_x, cells_y = plume.shape
     field_rows = fields.shape[0]
     total = field_rows + level_total
@@ -266,7 +279,7 @@
                 moved = pltpu.roll(edge, -m * width % LANES, 1) if m else edge
                 start = d * rows + m * packed
                 spread_edges[start : start + count] = moved[:count]
-    y_table = y_back[...]
+    y_table = y_back[gy]
     groups = nudged // GROUP
     spot_of = lax.broadcasted_iota(jnp.int32, (2 * KX, LANES), 1) // width
     edges = jnp.zeros((2 * KX, LANES), jnp.float32)
@@ -274,6 +287,7 @@
         piece = spread_edges[t * 2 * KX : (t + 1) * 2 * KX]
         edges = jnp.where(spot_of == t, pltpu.roll(piece, t * width, 1) if t else piece, edges)
     update_rows = columns_dot(edges, y_table)
+    copies[0].wait()
     for t in range(groups):
         update = columns_dot(spread[t * 2 * KX : (t + 1) * 2 * KX], y_table)
         for n in range(GROUP):
@@ -288,8 +302,11 @@
 
     lane = lax.broadcasted_iota(jnp.int32, (cells_x, cells_y), 1)
     first, final = lane == 0, lane == cells_y - 1
+    even = is_even("gy")
+    north = jnp.where(even, col_first[...], col_second[...])
+    south = jnp.where(even, col_second[...], col_first[...])
     columns = jnp.where(
-        lane % 2 == 0, pltpu.roll(north[...], cells_y - 1, 1), pltpu.roll(south[...], 1, 1))
+        lane % 2 == 0, pltpu.roll(north, cells_y - 1, 1), pltpu.roll(south, 1, 1))
 
     def advance(c, parts):
         centre, to_west, to_east, to_south, to_north = parts
@@ -322,7 +339,7 @@
 
     if last:
         return
-    for copy in copies:
+    for copy in copies[1:]:
         copy.wait()
     emit_modes(
         lambda c: fields_out[slab_of(levels, c, level_count, level_total)],
@@ -330,11 +347,13 @@
     )
 
 
-def swap(axis, to_next, to_previous):
+def exchange(axis, first, second):
     count = lax.axis_size(axis)
-    up = [(i, i + 1) for i in range(count - 1)]
-    down = [(b, a) for a, b in up]
-    return lax.ppermute(to_next, axis, up), lax.ppermute(to_previous, axis, down)
+    received = []
+    for start, data in ((0, first), (1, second)):
+        pairs = [(i, i + 1) for i in range(start, count - 1, 2)]
+        received.append(lax.ppermute(data, axis, pairs + [(b, a) for a, b in pairs]))
+    return received
 
 
 def local(tables, fields, levels, cuts, parent_modes, owners, plume, source):
@@ -362,7 +381,11 @@
 
     mode_shape = f32((devices, 2 * rows, LANES))
     step_scratch = [vmem(total, cells_x + 2 * PAD, cells_y), vmem(field_rows, cells_x, cells_y),
-                    vmem(devices * rows, LANES), vmem(devices * rows, LANES)]
+                    vmem(devices * rows, LANES), vmem(devices * rows, LANES),
+                    vmem(total, cells_y), vmem(total, cells_y), pltpu.SemaphoreType.DMA((5,))]
+    levels_space = pltpu.SMEM(levels.shape, jnp.int32)
+    owners_space = pltpu.SMEM(owners.shape, jnp.int32)
+    levels, owners = in_hbm(levels), in_hbm(owners)
     mode_scratch = [vmem(nudged, 4 * KX * KX), table_space(x_fwd),
                     table_space(y_fwd), vmem(nudged, KX, LANES),
                     vmem(devices * rows, 2 * LANES)]
@@ -372,58 +395,56 @@
         out_shape=mode_shape,
         in_specs=[HBM] * 6,
         out_specs=VMEM,
-        scratch_shapes=[pltpu.SMEM(levels.shape, jnp.int32), pltpu.SMEM(owners.shape, jnp.int32),
-                        vmem(field_rows, cells_x, cells_y), pltpu.SemaphoreType.DMA((6,))]
+        scratch_shapes=[levels_space, owners_space, vmem(field_rows, cells_x, cells_y), pltpu.SemaphoreType.DMA((6,))]
         + mode_scratch,
         compiler_params=limit(8),
         name="first_modes",
-    )(*map(in_hbm, (levels, owners, flat, parent_modes, x_fwd, y_fwd)))
+    )(levels, owners, *map(in_hbm, (flat, parent_modes, x_fwd, y_fwd)))
     for step in range(STEPS):
         last = step == STEPS - 1
         edge_shapes = [f32((total, cells_y)), f32((total, cells_y)), f32((cells_x, 2 * total))]
         edge_operands = [flat, plume]
         if step == 0:
-            edge_shapes.append(jax.ShapeDtypeStruct(y_back.shape[1:], y_back.dtype))
-            edge_operands.append(in_hbm(y_back))
+            edge_shapes.append(f32((2 * rows, LANES)))
+            edge_operands.append(cuts)
         edges = pl.pallas_call(
-            edge_kernel,
+            functools.partial(edge_kernel, n_gy, period),
             out_shape=edge_shapes,
-            in_specs=[VMEM, VMEM] + [HBM] * (len(edge_operands) - 2),
+            in_specs=[VMEM, VMEM, SMEM][: len(edge_operands)],
             out_specs=[VMEM] * len(edge_shapes),
-            scratch_shapes=[pltpu.SemaphoreType.DMA((1,))] if step == 0 else [],
             compiler_params=limit(8),
             name="edges",
         )(*edge_operands)
         if step == 0:
-            back_table = edges[3]
-        to_west, to_east, cols = edges[:3]
-        west, east = swap("gx", to_east, to_west)
+            weights = edges[3]
+        cols = edges[2]
+        row_first, row_second = exchange("gx", *edges[:2])
         parts = lax.all_to_all(modes, AXES, 0, 0, tiled=True)
-        parts, west, east = lax.optimization_barrier((parts, west, east))
+        parts, row_first, row_second = lax.optimization_barrier((parts, row_first, row_second))
         share = pl.pallas_call(
-            functools.partial(share_kernel, n_gx, n_gy, period),
+            functools.partial(share_kernel, n_gx, n_gy),
             out_shape=f32((devices, rows + beside_rows(rows), LANES)),
-            in_specs=[SMEM, VMEM, VMEM, VMEM],
+            in_specs=[VMEM] * 4,
             out_specs=VMEM,
             compiler_params=limit(8),
             name="share_sum",
-        )(cuts, parts, x_back, x_beside)
+        )(weights, parts, x_back, x_beside)
         share, cols = lax.optimization_barrier((share, cols))
-        south, north = swap("gy", cols, cols)
+        col_first, col_second = exchange("gy", cols, cols)
         shares = lax.all_to_all(share, AXES, 0, 0, tiled=True)
         out_shape = [f32(flat.shape), f32(plume.shape)]
-        operands = [levels, owners, shares, flat, plume, source, west, east, south, north,
-                    back_table]
+        operands = [shares, flat, plume, source, row_first, row_second, col_first, col_second,
+                    y_back, levels]
         if not last:
             out_shape.append(mode_shape)
-            operands += [in_hbm(parent_modes), in_hbm(x_fwd), in_hbm(y_fwd)]
+            operands += [owners, in_hbm(parent_modes), in_hbm(x_fwd), in_hbm(y_fwd)]
         results = pl.pallas_call(
             functools.partial(step_kernel, n_gy, step, last),
             out_shape=out_shape,
-            in_specs=[SMEM, SMEM] + [VMEM] * 9 + [HBM] * (len(operands) - 11),
+            in_specs=[VMEM] * 9 + [HBM] * (len(operands) - 9),
             out_specs=[VMEM] * len(out_shape),
-            scratch_shapes=step_scratch
-            + ([] if last else [pltpu.SemaphoreType.DMA((3,))] + mode_scratch),
+            scratch_shapes=[levels_space] + step_scratch
+            + ([] if last else [owners_space] + mode_scratch),
             compiler_params=limit(20),
             name="final_step" if last else "inner_step",
         )(*operands)

time: 77.5 us -> 74.6 us (0.963)
  starting transfers between devices: 37.3 us -> 30.2 us
  waiting for transfers between devices: 23.8 us -> 30.3 us
  Pallas kernels: 14.8 us -> 11.8 us
    all_to_all x2, waiting for transfers between devices: 9.29 us -> 19.8 us  [local(): parts = lax.all_to_all(modes, AXES, 0, 0, tiled=True)]
    ppermute x8, starting transfers between devices: 18.6 us -> 12.4 us  [exchange(): lax.ppermute(data, axis, pairs + [(b, a) for a, b in pairs])]
    ppermute x8, waiting for transfers between devices: 8.61 us -> 4.31 us  [exchange(): lax.ppermute(data, axis, pairs + [(b, a) for a, b in pairs])]
    pallas_call x2, Pallas kernels: 7.37 us -> 5.76 us  [local(): pl.pallas_call(functools.partial(step_kernel, n_gy, step, last), out_shap...]
    pallas_call x4, Pallas kernels: 4.7 us -> 3.29 us  [the longest x2 2.08 us: local(): pl.pallas_call(functools.partial(share_kernel, n_gx, n_gy), out_shape=f32...]
    all_to_all x2, starting transfers between devices: 11 us -> 10.1 us  [local(): parts = lax.all_to_all(modes, AXES, 0, 0, tiled=True)]
where the time goes in v12:
time: 74.6 us; the launch traced here: 74 us
  waiting for transfers between devices  30.3 us (41%)
  starting transfers between devices  30.2 us (40%)
  Pallas kernels  11.8 us (16%)
  local copies, waits for them, and re-layouts  0.86 us (1%)
  between operations  0.81 us (1%)
    all_to_all x2, waiting for transfers between devices, local(): parts = lax.all_to_all(modes, AXES, 0, 0, tiled=True)  19.8 us
    ppermute x8, starting transfers between devices, exchange(): lax.ppermute(data, axis, pairs + [(b, a) for a, b in pairs])  12.4 us
    all_to_all x2, starting transfers between devices, local(): parts = lax.all_to_all(modes, AXES, 0, 0, tiled=True)  10.1 us
    all_to_all x2, starting transfers between devices, local(): shares = lax.all_to_all(share, AXES, 0, 0, tiled=True)  7.72 us
    all_to_all x2, waiting for transfers between devices, local(): shares = lax.all_to_all(share, AXES, 0, 0, tiled=True)  6.27 us
    pallas_call x2, Pallas kernels, local(): pl.pallas_call(functools.partial(step_kernel, n_gy, step, last), out_shap...  5.76 us
    ppermute x8, waiting for transfers between devices, exchange(): lax.ppermute(data, axis, pairs + [(b, a) for a, b in pairs])  4.31 us
    pallas_call x1, Pallas kernels, local(): pl.pallas_call(functools.partial(first_kernel, n_gy, level_total), out_sh...  2.78 us
  transfers between devices with their start and end apart: 12, of which 8 were waited for; matrix products, arithmetic and copies ran while one was open for 0% of the time, Pallas kernels for 2%

profile of v12, /device:TPU:0, one launch (start us, length us, event | category | flops | bytes accessed | tf_op | source)
XLA Modules:
  0.0 74.0 jit_solution(9689018643132809199)
XLA Ops:
  0.7 2.8 %first_modes.1 = f32[32,24,128]{2,1,0:T(8,128)} custom-call(s32[8]{0:T(128)} %levels_all.5, s32[2]{0:T(128)} %rest_0_.1, f32[48,32,128]{2,1,0:T(8,128)} %bitcast.2, f32[1,2,24,4096]{3,2,1,0:T(8,128)} %rest_1_.1, bf16[8,384,256]{2,1,0:T(8,128)(2,1)} %constant.10.clone.x_fwd_all.rest_2_, bf16[4,64,384]{2,1,0:T(8,128)(2,1)} %constant.11.clone.y_fwd_all.rest_3_), custom_call_target="tpu_custom_call" | custom-call | tf_op jit(solution)/shard_map/first_modes/pallas_call | solution.py:393
  3.4 0.0 copy-start.4
  3.5 0.0 copy-start.5
  3.5 0.0 copy-start.1
  3.5 7.3 %all-to-all-start = ((f32[32,24,128]{2,1,0:T(8,128)}), f32[32,24,128]{2,1,0:T(8,128)S(1)}, u32[]{:S(2)}, u32[]{:S(2)}) async-start(f32[32,24,128]{2,1,0:T(8,128)} %first_modes.1), calls=%async_computation | async-start | bytes 786432 | tf_op jit(solution)/shard_map/all_to_all | solution.py:422
  10.8 0.1 reshape.14.rest_0_
  10.9 0.9 %edges.2 = (f32[64,128]{1,0:T(8,128)S(1)}, f32[64,128]{1,0:T(8,128)S(1)}, f32[32,128]{1,0:T(8,128)S(1)}, f32[24,128]{1,0:T(8,128)S(1)}) custom-call(f32[48,32,128]{2,1,0:T(8,128)S(1)} %bitcast.3, f32[16,32,128]{2,1,0:T(8,128)S(1)} %copy-done.3, s32[24]{0:T(128)S(1)} %reshape.14.rest_0_), custom_call_target="tpu_custom_call" | custom-call | tf_op jit(solution)/shard_map/edges/pallas_call | solution.py:410
  11.8 0.3 collective-permute-start
  12.1 0.7 collective-permute-start.1
  12.8 0.3 collective-permute-done.row_first
  13.1 9.6 %all-to-all-done.parts = f32[32,24,128]{2,1,0:T(8,128)S(1)} async-done(((f32[32,24,128]{2,1,0:T(8,128)}), f32[32,24,128]{2,1,0:T(8,128)S(1)}, u32[]{:S(2)}, u32[]{:S(2)}) %all-to-all-start) | async-done | bytes 393248 | tf_op jit(solution)/shard_map/all_to_all | solution.py:422
  22.6 1.0 %share_sum.2 = f32[32,16,128]{2,1,0:T(8,128)} custom-call(f32[24,128]{1,0:T(8,128)S(1)} %get-tuple-element.24.weights, f32[32,24,128]{2,1,0:T(8,128)S(1)} %all-to-all-done.parts, bf16[512,256]{1,0:T(8,128)(2,1)S(1)} %copy-done.4, bf16[512,128]{1,0:T(8,128)(2,1)S(1)} %copy-done.5), custom_call_target="tpu_custom_call" | custom-call | tf_op jit(solution)/shard_map/share_sum/pallas_call | solution.py:424
  23.7 3.9 %all-to-all-start.1 = ((f32[32,16,128]{2,1,0:T(8,128)}), f32[32,16,128]{2,1,0:T(8,128)S(1)}, u32[]{:S(2)}, u32[]{:S(2)}) async-start(f32[32,16,128]{2,1,0:T(8,128)} %share_sum.2), calls=%async_computation.1 | async-start | bytes 524288 | tf_op jit(solution)/shard_map/all_to_all | solution.py:434
  27.5 0.7 collective-permute-start.3
  28.2 4.5 %collective-permute-start.2 = (f32[32,128]{1,0:T(8,128)S(1)}, f32[32,128]{1,0:T(8,128)S(1)}, u32[]{:S(2)}, u32[]{:S(2)}) collective-permute-start(f32[32,128]{1,0:T(8,128)S(1)} %get-tuple-element.32), channel_id=1, source_target_pairs={{0,1},{2,3},{1,0},{3,2},{4,5},{6,7},{5,4},{7,6},{8,9},{10,11},{9,8... | collective-permute-start | bytes 49160 | tf_op jit(solution)/shard_map/ppermute | solution.py:355
  32.8 1.9 %collective-permute-done.2.col_first = f32[32,128]{1,0:T(8,128)S(1)} collective-permute-done((f32[32,128]{1,0:T(8,128)S(1)}, f32[32,128]{1,0:T(8,128)S(1)}, u32[]{:S(2)}, u32[]{:S(2)}) %collective-permute-start.2) | collective-permute-done | bytes 16416 | tf_op jit(solution)/shard_map/ppermute | solution.py:355
  34.6 3.1 %all-to-all-done.1.shares = f32[32,16,128]{2,1,0:T(8,128)S(1)} async-done(((f32[32,16,128]{2,1,0:T(8,128)}), f32[32,16,128]{2,1,0:T(8,128)S(1)}, u32[]{:S(2)}, u32[]{:S(2)}) %all-to-all-start.1) | async-done | bytes 262176 | tf_op jit(solution)/shard_map/all_to_all | solution.py:434
  37.8 2.6 %inner_step.1 = (f32[48,32,128]{2,1,0:T(8,128)S(1)}, f32[16,32,128]{2,1,0:T(8,128)S(1)}, f32[32,24,128]{2,1,0:T(8,128)S(1)}) custom-call(f32[32,16,128]{2,1,0:T(8,128)S(1)} %all-to-all-done.1.shares, f32[48,32,128]{2,1,0:T(8,128)S(1)} %bitcast.4, f32[16,32,128]{2,1,0:T(8,128)S(1)} %copy-done.3, f32[16,32,128]{2,1,0:T(8,128)S(1)} %copy-done.2, ...), custom_call_target="tpu_custom_call" | custom-call | tf_op jit(solution)/shard_map/inner_step/pallas_call | solution.py:441
  40.4 0.7 copy-done.6
  41.2 2.8 %all-to-all-start.2 = ((f32[32,24,128]{2,1,0:T(8,128)}), f32[32,24,128]{2,1,0:T(8,128)S(1)}, u32[]{:S(2)}, u32[]{:S(2)}) async-start(f32[32,24,128]{2,1,0:T(8,128)} %copy-done.6), calls=%async_computation.2 | async-start | bytes 786432 | tf_op jit(solution)/shard_map/all_to_all | solution.py:422
  44.0 0.3 edges.3
  44.3 0.3 collective-permute-start.4
  44.6 0.7 collective-permute-start.5
  45.3 0.3 collective-permute-done.4.row_first
  45.6 10.2 %all-to-all-done.2.parts = f32[32,24,128]{2,1,0:T(8,128)S(1)} async-done(((f32[32,24,128]{2,1,0:T(8,128)}), f32[32,24,128]{2,1,0:T(8,128)S(1)}, u32[]{:S(2)}, u32[]{:S(2)}) %all-to-all-start.2) | async-done | bytes 393248 | tf_op jit(solution)/shard_map/all_to_all | solution.py:422
  55.8 1.0 %share_sum.3 = f32[32,16,128]{2,1,0:T(8,128)} custom-call(f32[24,128]{1,0:T(8,128)S(1)} %get-tuple-element.24.weights, f32[32,24,128]{2,1,0:T(8,128)S(1)} %all-to-all-done.2.parts, bf16[512,256]{1,0:T(8,128)(2,1)S(1)} %copy-done.4, bf16[512,128]{1,0:T(8,128)(2,1)S(1)} %copy-done.5), custom_call_target="tpu_custom_call" | custom-call | tf_op jit(solution)/shard_map/share_sum/pallas_call | solution.py:424
  56.8 3.9 %all-to-all-start.3 = ((f32[32,16,128]{2,1,0:T(8,128)}), f32[32,16,128]{2,1,0:T(8,128)S(1)}, u32[]{:S(2)}, u32[]{:S(2)}) async-start(f32[32,16,128]{2,1,0:T(8,128)} %share_sum.3), calls=%async_computation.3 | async-start | bytes 524288 | tf_op jit(solution)/shard_map/all_to_all | solution.py:434
  60.7 0.7 collective-permute-start.7
  61.4 4.5 %collective-permute-start.6 = (f32[32,128]{1,0:T(8,128)S(1)}, f32[32,128]{1,0:T(8,128)S(1)}, u32[]{:S(2)}, u32[]{:S(2)}) collective-permute-start(f32[32,128]{1,0:T(8,128)S(1)} %get-tuple-element.43), channel_id=1, source_target_pairs={{0,1},{2,3},{1,0},{3,2},{4,5},{6,7},{5,4},{7,6},{8,9},{10,11},{9,8... | collective-permute-start | bytes 49160 | tf_op jit(solution)/shard_map/ppermute | solution.py:355
  65.9 1.9 %collective-permute-done.6.col_first = f32[32,128]{1,0:T(8,128)S(1)} collective-permute-done((f32[32,128]{1,0:T(8,128)S(1)}, f32[32,128]{1,0:T(8,128)S(1)}, u32[]{:S(2)}, u32[]{:S(2)}) %collective-permute-start.6) | collective-permute-done | bytes 16416 | tf_op jit(solution)/shard_map/ppermute | solution.py:355
  67.8 3.1 %all-to-all-done.3.shares = f32[32,16,128]{2,1,0:T(8,128)S(1)} async-done(((f32[32,16,128]{2,1,0:T(8,128)}), f32[32,16,128]{2,1,0:T(8,128)S(1)}, u32[]{:S(2)}, u32[]{:S(2)}) %all-to-all-start.3) | async-done | bytes 262176 | tf_op jit(solution)/shard_map/all_to_all | solution.py:434
  70.9 3.1 %final_step.1 = (f32[48,32,128]{2,1,0:T(8,128)}, f32[16,32,128]{2,1,0:T(8,128)}) custom-call(f32[32,16,128]{2,1,0:T(8,128)S(1)} %all-to-all-done.3.shares, f32[48,32,128]{2,1,0:T(8,128)S(1)} %get-tuple-element.34.fields, f32[16,32,128]{2,1,0:T(8,128)S(1)} %get-tuple-element.35.plume, f32[16,32,128]{2,1,0:T(8,128)S(1)} %copy-done.2, ...), custom_call_target="tpu_custom_call" | custom-call | tf_op jit(solution)/shard_map/final_step/pallas_call | solution.py:441
  (16 shorter events, 0.0 us)
Async XLA Ops:
  0.6 10.2 %copy-start.7 = (s32[3,8]{1,0:T(4,128)S(1)}, s32[3,8]{1,0:T(4,128)}, u32[]{:S(2)}) copy-start(s32[3,8]{1,0:T(4,128)} %param.14) | copy-start | bytes 292
  0.6 10.3 %copy-start = (f32[3,16,32,128]{3,2,1,0:T(8,128)S(1)}, f32[3,16,32,128]{3,2,1,0:T(8,128)}, u32[]{:S(2)}) copy-start(f32[3,16,32,128]{3,2,1,0:T(8,128)} %param.12) | copy-start | bytes 2359300
  0.6 10.3 %copy-start.3 = (f32[16,32,128]{2,1,0:T(8,128)S(1)}, f32[16,32,128]{2,1,0:T(8,128)}, u32[]{:S(2)}) copy-start(f32[16,32,128]{2,1,0:T(8,128)} %plume.3) | copy-start | bytes 786436
  3.4 19.2 %copy-start.4 = (bf16[512,256]{1,0:T(8,128)(2,1)S(1)}, bf16[512,256]{1,0:T(8,128)(2,1)}, u32[]{:S(2)}) copy-start(bf16[512,256]{1,0:T(8,128)(2,1)} %constant.13.clone.x_back) | copy-start | bytes 786436
  3.5 19.2 %copy-start.5 = (bf16[512,128]{1,0:T(8,128)(2,1)S(1)}, bf16[512,128]{1,0:T(8,128)(2,1)}, u32[]{:S(2)}) copy-start(bf16[512,128]{1,0:T(8,128)(2,1)} %constant.14.clone.x_beside) | copy-start | bytes 393220
  3.5 34.3 %copy-start.1 = (bf16[4,192,256]{2,1,0:T(8,128)(2,1)S(1)}, bf16[4,192,256]{2,1,0:T(8,128)(2,1)}, u32[]{:S(2)}) copy-start(bf16[4,192,256]{2,1,0:T(8,128)(2,1)} %constant.12.clone.y_back) | copy-start | bytes 1179652
  3.5 34.3 %copy-start.2 = (f32[16,32,128]{2,1,0:T(8,128)S(1)}, f32[16,32,128]{2,1,0:T(8,128)}, u32[]{:S(2)}) copy-start(f32[16,32,128]{2,1,0:T(8,128)} %source.3) | copy-start | bytes 786436
  3.5 19.1 %all-to-all-start = ((f32[32,24,128]{2,1,0:T(8,128)}), f32[32,24,128]{2,1,0:T(8,128)S(1)}, u32[]{:S(2)}, u32[]{:S(2)}) async-start(f32[32,24,128]{2,1,0:T(8,128)} %first_modes.1), calls=%async_computation | async-start | bytes 786432 | tf_op jit(solution)/shard_map/all_to_all | solution.py:422
  11.8 1.3 %collective-permute-start = (f32[64,128]{1,0:T(8,128)S(1)}, f32[64,128]{1,0:T(8,128)S(1)}, u32[]{:S(2)}, u32[]{:S(2)}) collective-permute-start(f32[64,128]{1,0:T(8,128)S(1)} %get-tuple-element.25), channel_id=1, source_target_pairs={{0,4},{8,12},{16,20},{24,28},{4,0},{12,8},{20,16},{28,24},{1,5},{9... | collective-permute-start | bytes 98312 | tf_op jit(solution)/shard_map/ppermute | solution.py:355
  12.1 1.0 %collective-permute-start.1 = (f32[64,128]{1,0:T(8,128)S(1)}, f32[64,128]{1,0:T(8,128)S(1)}, u32[]{:S(2)}, u32[]{:S(2)}) collective-permute-start(f32[64,128]{1,0:T(8,128)S(1)} %get-tuple-element.26), channel_id=1, source_target_pairs={{4,8},{12,16},{20,24},{8,4},{16,12},{24,20},{5,9},{13,17},{21,25},... | collective-permute-start | bytes 98312 | tf_op jit(solution)/shard_map/ppermute | solution.py:355
  23.7 14.1 %all-to-all-start.1 = ((f32[32,16,128]{2,1,0:T(8,128)}), f32[32,16,128]{2,1,0:T(8,128)S(1)}, u32[]{:S(2)}, u32[]{:S(2)}) async-start(f32[32,16,128]{2,1,0:T(8,128)} %share_sum.2), calls=%async_computation.1 | async-start | bytes 524288 | tf_op jit(solution)/shard_map/all_to_all | solution.py:434
  27.5 5.2 %collective-permute-start.3 = (f32[32,128]{1,0:T(8,128)S(1)}, f32[32,128]{1,0:T(8,128)S(1)}, u32[]{:S(2)}, u32[]{:S(2)}) collective-permute-start(f32[32,128]{1,0:T(8,128)S(1)} %get-tuple-element.32), channel_id=1, source_target_pairs={{1,2},{2,1},{5,6},{6,5},{9,10},{10,9},{13,14},{14,13},{17,18},{18,... | collective-permute-start | bytes 49160 | tf_op jit(solution)/shard_map/ppermute | solution.py:355
  28.2 6.4 %collective-permute-start.2 = (f32[32,128]{1,0:T(8,128)S(1)}, f32[32,128]{1,0:T(8,128)S(1)}, u32[]{:S(2)}, u32[]{:S(2)}) collective-permute-start(f32[32,128]{1,0:T(8,128)S(1)} %get-tuple-element.32), channel_id=1, source_target_pairs={{0,1},{2,3},{1,0},{3,2},{4,5},{6,7},{5,4},{7,6},{8,9},{10,11},{9,8... | collective-permute-start | bytes 49160 | tf_op jit(solution)/shard_map/ppermute | solution.py:355
  40.4 0.7 %copy-start.6 = (f32[32,24,128]{2,1,0:T(8,128)}, f32[32,24,128]{2,1,0:T(8,128)S(1)}, u32[]{:S(2)}) copy-start(f32[32,24,128]{2,1,0:T(8,128)S(1)} %get-tuple-element.33) | copy-start | bytes 1179652
  41.2 14.7 %all-to-all-start.2 = ((f32[32,24,128]{2,1,0:T(8,128)}), f32[32,24,128]{2,1,0:T(8,128)S(1)}, u32[]{:S(2)}, u32[]{:S(2)}) async-start(f32[32,24,128]{2,1,0:T(8,128)} %copy-done.6), calls=%async_computation.2 | async-start | bytes 786432 | tf_op jit(solution)/shard_map/all_to_all | solution.py:422
  44.3 1.3 %collective-permute-start.4 = (f32[64,128]{1,0:T(8,128)S(1)}, f32[64,128]{1,0:T(8,128)S(1)}, u32[]{:S(2)}, u32[]{:S(2)}) collective-permute-start(f32[64,128]{1,0:T(8,128)S(1)} %get-tuple-element.36), channel_id=1, source_target_pairs={{0,4},{8,12},{16,20},{24,28},{4,0},{12,8},{20,16},{28,24},{1,5},{9... | collective-permute-start | bytes 98312 | tf_op jit(solution)/shard_map/ppermute | solution.py:355
  44.6 1.0 %collective-permute-start.5 = (f32[64,128]{1,0:T(8,128)S(1)}, f32[64,128]{1,0:T(8,128)S(1)}, u32[]{:S(2)}, u32[]{:S(2)}) collective-permute-start(f32[64,128]{1,0:T(8,128)S(1)} %get-tuple-element.37), channel_id=1, source_target_pairs={{4,8},{12,16},{20,24},{8,4},{16,12},{24,20},{5,9},{13,17},{21,25},... | collective-permute-start | bytes 98312 | tf_op jit(solution)/shard_map/ppermute | solution.py:355
  56.8 14.1 %all-to-all-start.3 = ((f32[32,16,128]{2,1,0:T(8,128)}), f32[32,16,128]{2,1,0:T(8,128)S(1)}, u32[]{:S(2)}, u32[]{:S(2)}) async-start(f32[32,16,128]{2,1,0:T(8,128)} %share_sum.3), calls=%async_computation.3 | async-start | bytes 524288 | tf_op jit(solution)/shard_map/all_to_all | solution.py:434
  60.7 5.2 %collective-permute-start.7 = (f32[32,128]{1,0:T(8,128)S(1)}, f32[32,128]{1,0:T(8,128)S(1)}, u32[]{:S(2)}, u32[]{:S(2)}) collective-permute-start(f32[32,128]{1,0:T(8,128)S(1)} %get-tuple-element.43), channel_id=1, source_target_pairs={{1,2},{2,1},{5,6},{6,5},{9,10},{10,9},{13,14},{14,13},{17,18},{18,... | collective-permute-start | bytes 49160 | tf_op jit(solution)/shard_map/ppermute | solution.py:355
  61.4 6.4 %collective-permute-start.6 = (f32[32,128]{1,0:T(8,128)S(1)}, f32[32,128]{1,0:T(8,128)S(1)}, u32[]{:S(2)}, u32[]{:S(2)}) collective-permute-start(f32[32,128]{1,0:T(8,128)S(1)} %get-tuple-element.43), channel_id=1, source_target_pairs={{0,1},{2,3},{1,0},{3,2},{4,5},{6,7},{5,4},{7,6},{8,9},{10,11},{9,8... | collective-permute-start | bytes 49160 | tf_op jit(solution)/shard_map/ppermute | solution.py:355

commit v13 on v12

--- a/solution.py
+++ b/solution.py
@@ -13,6 +13,7 @@
 KX = 32
 STEPS = 2
 GROUP = 4
+PIECES = 4
 LANES = GROUP * KX
 PAD = 8
 VMEM = pl.BlockSpec(memory_space=pltpu.VMEM)
@@ -97,11 +98,11 @@
         stacked, table, (((0,), (0,)), ((), ())), preferred_element_type=jnp.float32)
 
 
-def emit_modes(read, parent, is_owner, x_fwd, y_fwd, modes, turned, work):
+def emit_modes(chosen, parent, is_owner, x_fwd, y_fwd, modes, turned, work):
     devices, rows = modes.shape[0], modes.shape[1] // 2
     slabs = parent.shape[0]
     groups = slabs // GROUP
-    head, rest = split(jnp.concatenate([read(c) for c in range(slabs)], axis=0))
+    head, rest = split(jnp.concatenate(chosen, axis=0))
     half = lax.dot_general(
         y_fwd, jnp.concatenate([head, head, rest], axis=1), (((1,), (1,)), ((), ())),
         preferred_element_type=jnp.float32)
@@ -149,7 +150,7 @@
         copy.wait()
     level_count = parent.shape[0] // 3
     emit_modes(
-        lambda c: fields[slab_of(levels, c, level_count, level_total)],
+        [fields[slab_of(levels, c, level_count, level_total)] for c in range(parent.shape[0])],
         parent, owners[0] == gx * n_gy + gy, x_fwd[...], y_fwd[...], modes, turned, work,
     )
 
@@ -160,8 +161,20 @@
 
 def edge_kernel(n_gy, period, fields, plume, *rest):
     if len(rest) > 3:
-        cuts, first, second, cols, weights = rest
+        cuts, levels, first, second, cols, weights, order = rest
         weights[...] = share_weights(n_gy, period, cuts, weights.shape)
+        count = levels.shape[0]
+        for n in range(count):
+            order[n] = levels[n]
+        spot = jnp.int32(count)
+        for l in range(plume.shape[0]):
+            found = levels[0] == l
+            for n in range(1, count):
+                found = found | (levels[n] == l)
+            order[spot] = jnp.int32(l)
+            spot = spot + jnp.where(found, 0, 1)
+        for n in range(order.shape[0] - 1, plume.shape[0] - 1, -1):
+            order[n] = jnp.int32(0)
     else:
         first, second, cols = rest
     even = is_even("gx")
@@ -238,27 +251,26 @@
             out[g * n_gy + h, rows:, :] = beside
 
 
-def step_kernel(n_gy, step, last, shares, fields, plume, source, row_first, row_second,
-                col_first, col_second, y_back, levels_all, *rest):
+def step_kernel(n_gy, step, last, level_count, shares, fields, plume, source, row_first, row_second,
+                col_first, col_second, y_back, order_all, *rest):
     gx, gy = lax.axis_index("gx"), lax.axis_index("gy")
     extra = []
     if last:
-        (fields_out, plume_out, levels, slabs, beside, spread, spread_edges, west, east,
-         sems) = rest
+        (fields_all, plume_all, order, slabs, beside, spread, spread_edges, west, east, sems,
+         fields_out, plume_out, out_sems) = rest
     else:
-        (owners_all, parent_all, x_fwd_all, y_fwd_all, fields_out, plume_out, modes,
-         levels, slabs, beside, spread, spread_edges, west, east, sems,
-         owners, parent, x_fwd, y_fwd, turned, work) = rest
+        (owners_all, parent_all, x_fwd_all, y_fwd_all, fields_out, plume_out, modes_all,
+         order, slabs, beside, spread, spread_edges, west, east, sems,
+         owners, modes, out_sems, parent, x_fwd, y_fwd, turned, work) = rest
         extra = [(owners_all, owners), (x_fwd_all.at[gx], x_fwd), (y_fwd_all.at[gy], y_fwd),
                  (parent_all.at[0, step + 1], parent)]
-    copies = fetch_all(sems, [(levels_all, levels)] + extra)
+    copies = fetch_all(sems, [(order_all, order)] + extra)
     even = is_even("gx")
     west[...] = jnp.where(even, row_second[...], row_first[...])
     east[...] = jnp.where(even, row_first[...], row_second[...])
     level_total, cells_x, cells_y = plume.shape
     field_rows = fields.shape[0]
     total = field_rows + level_total
-    level_count = levels.shape[0]
     nudged = 3 * level_count
     inner = slice(PAD, PAD + cells_x)
     for c in range(total):
@@ -293,7 +305,7 @@
         for n in range(GROUP):
             c = t * GROUP + n
             part = update[n * cells_x : (n + 1) * cells_x]
-            spot = slab_of(levels, c, level_count, level_total)
+            spot = slab_of(order, c, level_count, level_total)
             slabs[spot, inner] += part[:, :cells_y]
             slabs[spot, PAD - 1 : PAD] += update_rows[2 * c : 2 * c + 1, :cells_y]
             slabs[spot, PAD + cells_x : PAD + cells_x + 1] += update_rows[
@@ -308,11 +320,11 @@
     columns = jnp.where(
         lane % 2 == 0, pltpu.roll(north, cells_y - 1, 1), pltpu.roll(south, 1, 1))
 
-    def advance(c, parts):
+    def advance(c, parts, is_field=True):
         centre, to_west, to_east, to_south, to_north = parts
         a = slabs[c, inner]
         column = pltpu.roll(columns, cells_y - 1 - 2 * c, 1)
-        if c < field_rows:
+        if is_field:
             column = column + beside[c]
         return (
             centre * a
@@ -322,29 +334,62 @@
             + to_north * jnp.where(final, column, pltpu.roll(a, cells_y - 1, 1))
         )
 
-    for l in range(level_total):
+    def weights_at(l):
         u, v = slabs[l, inner], slabs[level_total + l, inner]
-        beside_parts = (
+        neighbours = (
             0.1 + 0.1 * jnp.maximum(u, 0.0), 0.1 - 0.1 * jnp.minimum(u, 0.0),
             0.1 + 0.1 * jnp.maximum(v, 0.0), 0.1 - 0.1 * jnp.minimum(v, 0.0),
         )
-        centre = 1.0 - (beside_parts[0] + beside_parts[1] + beside_parts[2] + beside_parts[3])
+        centre = 1.0 - (neighbours[0] + neighbours[1] + neighbours[2] + neighbours[3])
+        return centre, neighbours
+
+    def advance_fields(l, parts):
+        results = []
         for f in range(3):
-            fields_out[f * level_total + l] = advance(
-                f * level_total + l, (centre,) + beside_parts)
-        settled = advance(field_rows + l, (centre - 0.3,) + beside_parts) + source[l]
+            c = f * level_total + l
+            results.append(advance(c, (parts[0],) + parts[1]))
+            fields_out[c] = results[f]
+        return results
+
+    def advance_ash(l, parts):
+        settled = advance(field_rows + l, (parts[0] - 0.3,) + parts[1], False) + source[l]
         if l + 1 < level_total:
             settled = settled + 0.3 * plume[l + 1]
         plume_out[l] = settled
 
     if last:
+        pieces = out_sems.shape[0] // 4
+        per_piece = level_total // pieces
+        for l in range(level_total):
+            parts = weights_at(l)
+            advance_fields(l, parts)
+            advance_ash(l, parts)
+            if (l + 1) % per_piece == 0:
+                start = l + 1 - per_piece
+                pairs = []
+                for f in range(3):
+                    span = pl.ds(f * level_total + start, per_piece)
+                    pairs.append((fields_out.at[span], fields_all.at[span]))
+                span = pl.ds(start, per_piece)
+                pairs.append((plume_out.at[span], plume_all.at[span]))
+                copies += fetch_all(out_sems.at[pl.ds(start // per_piece * 4, 4)], pairs)
+        for copy in copies[1:]:
+            copy.wait()
         return
+    results = [advance_fields(l, weights_at(l)) for l in (order[n] for n in range(level_count))]
     for copy in copies[1:]:
         copy.wait()
     emit_modes(
-        lambda c: fields_out[slab_of(levels, c, level_count, level_total)],
+        [results[n][f] for f in range(3) for n in range(level_count)],
         parent, owners[step + 1] == gx * n_gy + gy, x_fwd[...], y_fwd[...], modes, turned, work,
     )
+    sent = fetch_all(out_sems, [(modes, modes_all)])
+    for n in range(level_count, level_total):
+        l = order[n]
+        advance_fields(l, weights_at(l))
+    for l in range(level_total):
+        advance_ash(l, weights_at(l))
+    sent[0].wait()
 
 
 def exchange(axis, first, second):
@@ -385,18 +430,24 @@
                     vmem(total, cells_y), vmem(total, cells_y), pltpu.SemaphoreType.DMA((5,))]
     levels_space = pltpu.SMEM(levels.shape, jnp.int32)
     owners_space = pltpu.SMEM(owners.shape, jnp.int32)
+    order_space = pltpu.SMEM((2 * level_total,), jnp.int32)
+    raw_levels = levels
     levels, owners = in_hbm(levels), in_hbm(owners)
     mode_scratch = [vmem(nudged, 4 * KX * KX), table_space(x_fwd),
                     table_space(y_fwd), vmem(nudged, KX, LANES),
                     vmem(devices * rows, 2 * LANES)]
+    inner_scratch = [owners_space, vmem(*mode_shape.shape), pltpu.SemaphoreType.DMA((1,))]
+    inner_scratch += mode_scratch
+    last_scratch = [vmem(field_rows, cells_x, cells_y), vmem(level_total, cells_x, cells_y),
+                    pltpu.SemaphoreType.DMA((4 * PIECES,))]
 
     modes = pl.pallas_call(
         functools.partial(first_kernel, n_gy, level_total),
         out_shape=mode_shape,
         in_specs=[HBM] * 6,
         out_specs=VMEM,
-        scratch_shapes=[levels_space, owners_space, vmem(field_rows, cells_x, cells_y), pltpu.SemaphoreType.DMA((6,))]
-        + mode_scratch,
+        scratch_shapes=[levels_space, owners_space, vmem(field_rows, cells_x, cells_y),
+                        pltpu.SemaphoreType.DMA((6,))] + mode_scratch,
         compiler_params=limit(8),
         name="first_modes",
     )(levels, owners, *map(in_hbm, (flat, parent_modes, x_fwd, y_fwd)))
@@ -405,22 +456,23 @@
         edge_shapes = [f32((total, cells_y)), f32((total, cells_y)), f32((cells_x, 2 * total))]
         edge_operands = [flat, plume]
         if step == 0:
-            edge_shapes.append(f32((2 * rows, LANES)))
-            edge_operands.append(cuts)
+            edge_shapes += [f32((2 * rows, LANES)),
+                            jax.ShapeDtypeStruct((2 * level_total,), jnp.int32)]
+            edge_operands += [cuts, raw_levels]
         edges = pl.pallas_call(
             functools.partial(edge_kernel, n_gy, period),
             out_shape=edge_shapes,
-            in_specs=[VMEM, VMEM, SMEM][: len(edge_operands)],
-            out_specs=[VMEM] * len(edge_shapes),
+            in_specs=[VMEM, VMEM, SMEM, SMEM][: len(edge_operands)],
+            out_specs=[VMEM, VMEM, VMEM, VMEM, SMEM][: len(edge_shapes)],
             compiler_params=limit(8),
             name="edges",
         )(*edge_operands)
         if step == 0:
-            weights = edges[3]
-        cols = edges[2]
-        row_first, row_second = exchange("gx", *edges[:2])
+            weights, order = edges[3], in_hbm(edges[4])
+        to_first, to_second, cols = edges[:3]
+        col_first, col_second = exchange("gy", cols, cols)
         parts = lax.all_to_all(modes, AXES, 0, 0, tiled=True)
-        parts, row_first, row_second = lax.optimization_barrier((parts, row_first, row_second))
+        parts, col_first, col_second = lax.optimization_barrier((parts, col_first, col_second))
         share = pl.pallas_call(
             functools.partial(share_kernel, n_gx, n_gy),
             out_shape=f32((devices, rows + beside_rows(rows), LANES)),
@@ -429,22 +481,23 @@
             compiler_params=limit(8),
             name="share_sum",
         )(weights, parts, x_back, x_beside)
-        share, cols = lax.optimization_barrier((share, cols))
-        col_first, col_second = exchange("gy", cols, cols)
+        share, to_first, to_second = lax.optimization_barrier((share, to_first, to_second))
+        row_first, row_second = exchange("gx", to_first, to_second)
         shares = lax.all_to_all(share, AXES, 0, 0, tiled=True)
         out_shape = [f32(flat.shape), f32(plume.shape)]
+        out_specs = [HBM if last else VMEM] * 2
         operands = [shares, flat, plume, source, row_first, row_second, col_first, col_second,
-                    y_back, levels]
+                    y_back, order]
         if not last:
-            out_shape.append(mode_shape)
+            out_shape.append(pltpu.HBM(mode_shape.shape, jnp.float32))
+            out_specs.append(HBM)
             operands += [owners, in_hbm(parent_modes), in_hbm(x_fwd), in_hbm(y_fwd)]
         results = pl.pallas_call(
-            functools.partial(step_kernel, n_gy, step, last),
+            functools.partial(step_kernel, n_gy, step, last, levels.shape[0]),
             out_shape=out_shape,
             in_specs=[VMEM] * 9 + [HBM] * (len(operands) - 9),
-            out_specs=[VMEM] * len(out_shape),
-            scratch_shapes=[levels_space] + step_scratch
-            + ([] if last else [owners_space] + mode_scratch),
+            out_specs=out_specs,
+            scratch_shapes=[order_space] + step_scratch + (last_scratch if last else inner_scratch),
             compiler_params=limit(20),
             name="final_step" if last else "inner_step",
         )(*operands)

time: 74.6 us -> 74.8 us (level)
  Pallas kernels: 11.8 us -> 13.1 us
    all_to_all x2, waiting for transfers between devices: 19.8 us -> 7.7 us  [local(): parts = lax.all_to_all(modes, AXES, 0, 0, tiled=True)]
    all_to_all x2, waiting for transfers between devices: 6.27 us -> 17.8 us  [local(): shares = lax.all_to_all(share, AXES, 0, 0, tiled=True)]
where the time goes in v13:
time: 74.8 us; the launch traced here: 74.5 us
  starting transfers between devices  30.4 us (41%)
  waiting for transfers between devices  30 us (40%)
  Pallas kernels  13.1 us (18%)
  between operations  0.82 us (1%)
    all_to_all x2, waiting for transfers between devices, local(): shares = lax.all_to_all(share, AXES, 0, 0, tiled=True)  17.8 us
    ppermute x8, starting transfers between devices, exchange(): lax.ppermute(data, axis, pairs + [(b, a) for a, b in pairs])  12.4 us
    all_to_all x2, starting transfers between devices, local(): parts = lax.all_to_all(modes, AXES, 0, 0, tiled=True)  10.5 us
    all_to_all x2, waiting for transfers between devices, local(): parts = lax.all_to_all(modes, AXES, 0, 0, tiled=True)  7.7 us
    all_to_all x2, starting transfers between devices, local(): shares = lax.all_to_all(share, AXES, 0, 0, tiled=True)  7.57 us
    pallas_call x2, Pallas kernels, local(): pl.pallas_call(functools.partial(step_kernel, n_gy, step, last, levels.sh...  6.38 us
    ppermute x8, waiting for transfers between devices, exchange(): lax.ppermute(data, axis, pairs + [(b, a) for a, b in pairs])  4.5 us
    pallas_call x1, Pallas kernels, local(): pl.pallas_call(functools.partial(first_kernel, n_gy, level_total), out_sh...  2.78 us
  transfers between devices with their start and end apart: 12, of which 8 were waited for; matrix products, arithmetic and copies ran while one was open for 0% of the time, Pallas kernels for 2%

profile of v13, /device:TPU:0, one launch (start us, length us, event | category | flops | bytes accessed | tf_op | source)
XLA Modules:
  0.0 74.5 jit_solution(8742078820952143818)
XLA Ops:
  0.7 2.8 %first_modes.1 = f32[32,24,128]{2,1,0:T(8,128)} custom-call(s32[8]{0:T(128)} %levels_all.1, s32[2]{0:T(128)} %rest_0_.1, f32[48,32,128]{2,1,0:T(8,128)} %bitcast.2, f32[1,2,24,4096]{3,2,1,0:T(8,128)} %rest_1_.3, bf16[8,384,256]{2,1,0:T(8,128)(2,1)} %constant.10.clone.x_fwd_all.rest_2_, bf16[4,64,384]{2,1,0:T(8,128)(2,1)} %constant.11.clone.y_fwd_all.rest_3_), custom_call_target="tpu_custom_call" | custom-call | tf_op jit(solution)/shard_map/first_modes/pallas_call | solution.py:444
  3.5 0.0 copy-start.4
  3.5 0.0 copy-start.5
  3.5 0.0 copy-start.1
  3.5 0.0 copy-start.3
  3.5 7.8 %all-to-all-start = ((f32[32,24,128]{2,1,0:T(8,128)}), f32[32,24,128]{2,1,0:T(8,128)S(1)}, u32[]{:S(2)}, u32[]{:S(2)}) async-start(f32[32,24,128]{2,1,0:T(8,128)} %first_modes.1), calls=%async_computation | async-start | bytes 786432 | tf_op jit(solution)/shard_map/all_to_all | solution.py:474
  11.3 0.1 reshape.14.rest_0_
  11.4 1.5 %edges.2 = (f32[64,128]{1,0:T(8,128)S(1)}, f32[64,128]{1,0:T(8,128)S(1)}, f32[32,128]{1,0:T(8,128)S(1)}, f32[24,128]{1,0:T(8,128)S(1)}, s32[32]{0:T(128)S(1)}) custom-call(f32[48,32,128]{2,1,0:T(8,128)S(1)} %bitcast.3, f32[16,32,128]{2,1,0:T(8,128)S(1)} %copy-done.2, s32[24]{0:T(128)S(1)} %reshape.14.rest_0_, s32[8]{0:T(128)S(1)} %copy-done.6), custom_call_target="tpu_custom_call" | custom-call | tf_op jit(solution)/shard_map/edges/pallas_call | solution.py:462
  12.9 0.7 collective-permute-start.1
  13.6 4.5 %collective-permute-start = (f32[32,128]{1,0:T(8,128)S(1)}, f32[32,128]{1,0:T(8,128)S(1)}, u32[]{:S(2)}, u32[]{:S(2)}) collective-permute-start(f32[32,128]{1,0:T(8,128)S(1)} %get-tuple-element.28), channel_id=1, source_target_pairs={{0,1},{2,3},{1,0},{3,2},{4,5},{6,7},{5,4},{7,6},{8,9},{10,11},{9,8... | collective-permute-start | bytes 49160 | tf_op jit(solution)/shard_map/ppermute | solution.py:400
  18.1 1.9 %collective-permute-done.col_first = f32[32,128]{1,0:T(8,128)S(1)} collective-permute-done((f32[32,128]{1,0:T(8,128)S(1)}, f32[32,128]{1,0:T(8,128)S(1)}, u32[]{:S(2)}, u32[]{:S(2)}) %collective-permute-start) | collective-permute-done | bytes 16416 | tf_op jit(solution)/shard_map/ppermute | solution.py:400
  20.0 3.3 %all-to-all-done.parts = f32[32,24,128]{2,1,0:T(8,128)S(1)} async-done(((f32[32,24,128]{2,1,0:T(8,128)}), f32[32,24,128]{2,1,0:T(8,128)S(1)}, u32[]{:S(2)}, u32[]{:S(2)}) %all-to-all-start) | async-done | bytes 393248 | tf_op jit(solution)/shard_map/all_to_all | solution.py:474
  23.3 1.0 %share_sum.2 = f32[32,16,128]{2,1,0:T(8,128)} custom-call(f32[24,128]{1,0:T(8,128)S(1)} %get-tuple-element.27.weights, f32[32,24,128]{2,1,0:T(8,128)S(1)} %all-to-all-done.parts, bf16[512,256]{1,0:T(8,128)(2,1)S(1)} %copy-done.4, bf16[512,128]{1,0:T(8,128)(2,1)S(1)} %copy-done.5), custom_call_target="tpu_custom_call" | custom-call | tf_op jit(solution)/shard_map/share_sum/pallas_call | solution.py:476
  24.3 3.8 %all-to-all-start.1 = ((f32[32,16,128]{2,1,0:T(8,128)}), f32[32,16,128]{2,1,0:T(8,128)S(1)}, u32[]{:S(2)}, u32[]{:S(2)}) async-start(f32[32,16,128]{2,1,0:T(8,128)} %share_sum.2), calls=%async_computation.1 | async-start | bytes 524288 | tf_op jit(solution)/shard_map/all_to_all | solution.py:486
  28.1 0.3 collective-permute-start.2
  28.4 0.7 collective-permute-start.3
  29.1 0.3 collective-permute-done.2.row_first
  29.4 8.9 %all-to-all-done.1.shares = f32[32,16,128]{2,1,0:T(8,128)S(1)} async-done(((f32[32,16,128]{2,1,0:T(8,128)}), f32[32,16,128]{2,1,0:T(8,128)S(1)}, u32[]{:S(2)}, u32[]{:S(2)}) %all-to-all-start.1) | async-done | bytes 262176 | tf_op jit(solution)/shard_map/all_to_all | solution.py:486
  38.3 3.5 %inner_step.1 = (f32[48,32,128]{2,1,0:T(8,128)S(1)}, f32[16,32,128]{2,1,0:T(8,128)S(1)}, f32[32,24,128]{2,1,0:T(8,128)}) custom-call(f32[32,16,128]{2,1,0:T(8,128)S(1)} %all-to-all-done.1.shares, f32[48,32,128]{2,1,0:T(8,128)S(1)} %bitcast.4, f32[16,32,128]{2,1,0:T(8,128)S(1)} %copy-done.2, f32[16,32,128]{2,1,0:T(8,128)S(1)} %copy-done.3, ...), custom_call_target="tpu_custom_call" | custom-call | tf_op jit(solution)/shard_map/inner_step/pallas_call | solution.py:495
  41.9 2.7 %all-to-all-start.2 = ((f32[32,24,128]{2,1,0:T(8,128)}), f32[32,24,128]{2,1,0:T(8,128)S(1)}, u32[]{:S(2)}, u32[]{:S(2)}) async-start(f32[32,24,128]{2,1,0:T(8,128)} %get-tuple-element.38), calls=%async_computation.2 | async-start | bytes 786432 | tf_op jit(solution)/shard_map/all_to_all | solution.py:474
  44.6 0.3 edges.3
  44.9 0.7 collective-permute-start.5
  45.6 4.5 %collective-permute-start.4 = (f32[32,128]{1,0:T(8,128)S(1)}, f32[32,128]{1,0:T(8,128)S(1)}, u32[]{:S(2)}, u32[]{:S(2)}) collective-permute-start(f32[32,128]{1,0:T(8,128)S(1)} %get-tuple-element.41), channel_id=1, source_target_pairs={{0,1},{2,3},{1,0},{3,2},{4,5},{6,7},{5,4},{7,6},{8,9},{10,11},{9,8... | collective-permute-start | bytes 49160 | tf_op jit(solution)/shard_map/ppermute | solution.py:400
  50.2 2.0 %collective-permute-done.4.col_first = f32[32,128]{1,0:T(8,128)S(1)} collective-permute-done((f32[32,128]{1,0:T(8,128)S(1)}, f32[32,128]{1,0:T(8,128)S(1)}, u32[]{:S(2)}, u32[]{:S(2)}) %collective-permute-start.4) | collective-permute-done | bytes 16416 | tf_op jit(solution)/shard_map/ppermute | solution.py:400
  52.2 4.4 %all-to-all-done.2.parts = f32[32,24,128]{2,1,0:T(8,128)S(1)} async-done(((f32[32,24,128]{2,1,0:T(8,128)}), f32[32,24,128]{2,1,0:T(8,128)S(1)}, u32[]{:S(2)}, u32[]{:S(2)}) %all-to-all-start.2) | async-done | bytes 393248 | tf_op jit(solution)/shard_map/all_to_all | solution.py:474
  56.6 1.0 %share_sum.3 = f32[32,16,128]{2,1,0:T(8,128)} custom-call(f32[24,128]{1,0:T(8,128)S(1)} %get-tuple-element.27.weights, f32[32,24,128]{2,1,0:T(8,128)S(1)} %all-to-all-done.2.parts, bf16[512,256]{1,0:T(8,128)(2,1)S(1)} %copy-done.4, bf16[512,128]{1,0:T(8,128)(2,1)S(1)} %copy-done.5), custom_call_target="tpu_custom_call" | custom-call | tf_op jit(solution)/shard_map/share_sum/pallas_call | solution.py:476
  57.6 3.8 %all-to-all-start.3 = ((f32[32,16,128]{2,1,0:T(8,128)}), f32[32,16,128]{2,1,0:T(8,128)S(1)}, u32[]{:S(2)}, u32[]{:S(2)}) async-start(f32[32,16,128]{2,1,0:T(8,128)} %share_sum.3), calls=%async_computation.3 | async-start | bytes 524288 | tf_op jit(solution)/shard_map/all_to_all | solution.py:486
  61.4 0.3 collective-permute-start.6
  61.8 0.7 collective-permute-start.7
  62.4 0.3 collective-permute-done.6.row_first
  62.7 8.9 %all-to-all-done.3.shares = f32[32,16,128]{2,1,0:T(8,128)S(1)} async-done(((f32[32,16,128]{2,1,0:T(8,128)}), f32[32,16,128]{2,1,0:T(8,128)S(1)}, u32[]{:S(2)}, u32[]{:S(2)}) %all-to-all-start.3) | async-done | bytes 262176 | tf_op jit(solution)/shard_map/all_to_all | solution.py:486
  71.6 2.8 %final_step.1 = (f32[48,32,128]{2,1,0:T(8,128)}, f32[16,32,128]{2,1,0:T(8,128)}) custom-call(f32[32,16,128]{2,1,0:T(8,128)S(1)} %all-to-all-done.3.shares, f32[48,32,128]{2,1,0:T(8,128)S(1)} %get-tuple-element.39.fields, f32[16,32,128]{2,1,0:T(8,128)S(1)} %get-tuple-element.40.plume, f32[16,32,128]{2,1,0:T(8,128)S(1)} %copy-done.3, ...), custom_call_target="tpu_custom_call" | custom-call | tf_op jit(solution)/shard_map/final_step/pallas_call | solution.py:495
  (18 shorter events, 0.0 us)
Async XLA Ops:
  0.6 10.7 %copy-start.8 = (s32[3,8]{1,0:T(4,128)S(1)}, s32[3,8]{1,0:T(4,128)}, u32[]{:S(2)}) copy-start(s32[3,8]{1,0:T(4,128)} %param.14) | copy-start | bytes 292
  0.6 10.7 %copy-start = (f32[3,16,32,128]{3,2,1,0:T(8,128)S(1)}, f32[3,16,32,128]{3,2,1,0:T(8,128)}, u32[]{:S(2)}) copy-start(f32[3,16,32,128]{3,2,1,0:T(8,128)} %param.12) | copy-start | bytes 2359300
  0.7 10.7 %copy-start.2 = (f32[16,32,128]{2,1,0:T(8,128)S(1)}, f32[16,32,128]{2,1,0:T(8,128)}, u32[]{:S(2)}) copy-start(f32[16,32,128]{2,1,0:T(8,128)} %plume.3) | copy-start | bytes 786436
  0.7 10.7 %copy-start.6 = (s32[8]{0:T(128)S(1)}, s32[8]{0:T(128)}, u32[]{:S(2)}) copy-start(s32[8]{0:T(128)} %levels_all.1) | copy-start | bytes 100
  3.5 19.8 %copy-start.4 = (bf16[512,256]{1,0:T(8,128)(2,1)S(1)}, bf16[512,256]{1,0:T(8,128)(2,1)}, u32[]{:S(2)}) copy-start(bf16[512,256]{1,0:T(8,128)(2,1)} %constant.13.clone.x_back) | copy-start | bytes 786436
  3.5 19.8 %copy-start.5 = (bf16[512,128]{1,0:T(8,128)(2,1)S(1)}, bf16[512,128]{1,0:T(8,128)(2,1)}, u32[]{:S(2)}) copy-start(bf16[512,128]{1,0:T(8,128)(2,1)} %constant.14.clone.x_beside) | copy-start | bytes 393220
  3.5 34.8 %copy-start.1 = (bf16[4,192,256]{2,1,0:T(8,128)(2,1)S(1)}, bf16[4,192,256]{2,1,0:T(8,128)(2,1)}, u32[]{:S(2)}) copy-start(bf16[4,192,256]{2,1,0:T(8,128)(2,1)} %constant.12.clone.y_back) | copy-start | bytes 1179652
  3.5 34.8 %copy-start.3 = (f32[16,32,128]{2,1,0:T(8,128)S(1)}, f32[16,32,128]{2,1,0:T(8,128)}, u32[]{:S(2)}) copy-start(f32[16,32,128]{2,1,0:T(8,128)} %source.3) | copy-start | bytes 786436
  3.5 19.8 %all-to-all-start = ((f32[32,24,128]{2,1,0:T(8,128)}), f32[32,24,128]{2,1,0:T(8,128)S(1)}, u32[]{:S(2)}, u32[]{:S(2)}) async-start(f32[32,24,128]{2,1,0:T(8,128)} %first_modes.1), calls=%async_computation | async-start | bytes 786432 | tf_op jit(solution)/shard_map/all_to_all | solution.py:474
  12.9 25.4 %copy-start.7 = (s32[32]{0:T(128)}, s32[32]{0:T(128)S(1)}, u32[]{:S(2)}) copy-start(s32[32]{0:T(128)S(1)} %get-tuple-element.37.order_all) | copy-start | bytes 388
  12.9 5.2 %collective-permute-start.1 = (f32[32,128]{1,0:T(8,128)S(1)}, f32[32,128]{1,0:T(8,128)S(1)}, u32[]{:S(2)}, u32[]{:S(2)}) collective-permute-start(f32[32,128]{1,0:T(8,128)S(1)} %get-tuple-element.28), channel_id=1, source_target_pairs={{1,2},{2,1},{5,6},{6,5},{9,10},{10,9},{13,14},{14,13},{17,18},{18,... | collective-permute-start | bytes 49160 | tf_op jit(solution)/shard_map/ppermute | solution.py:400
  13.6 6.5 %collective-permute-start = (f32[32,128]{1,0:T(8,128)S(1)}, f32[32,128]{1,0:T(8,128)S(1)}, u32[]{:S(2)}, u32[]{:S(2)}) collective-permute-start(f32[32,128]{1,0:T(8,128)S(1)} %get-tuple-element.28), channel_id=1, source_target_pairs={{0,1},{2,3},{1,0},{3,2},{4,5},{6,7},{5,4},{7,6},{8,9},{10,11},{9,8... | collective-permute-start | bytes 49160 | tf_op jit(solution)/shard_map/ppermute | solution.py:400
  24.3 14.0 %all-to-all-start.1 = ((f32[32,16,128]{2,1,0:T(8,128)}), f32[32,16,128]{2,1,0:T(8,128)S(1)}, u32[]{:S(2)}, u32[]{:S(2)}) async-start(f32[32,16,128]{2,1,0:T(8,128)} %share_sum.2), calls=%async_computation.1 | async-start | bytes 524288 | tf_op jit(solution)/shard_map/all_to_all | solution.py:486
  28.1 1.3 %collective-permute-start.2 = (f32[64,128]{1,0:T(8,128)S(1)}, f32[64,128]{1,0:T(8,128)S(1)}, u32[]{:S(2)}, u32[]{:S(2)}) collective-permute-start(f32[64,128]{1,0:T(8,128)S(1)} %get-tuple-element.33), channel_id=1, source_target_pairs={{0,4},{8,12},{16,20},{24,28},{4,0},{12,8},{20,16},{28,24},{1,5},{9... | collective-permute-start | bytes 98312 | tf_op jit(solution)/shard_map/ppermute | solution.py:400
  28.4 1.0 %collective-permute-start.3 = (f32[64,128]{1,0:T(8,128)S(1)}, f32[64,128]{1,0:T(8,128)S(1)}, u32[]{:S(2)}, u32[]{:S(2)}) collective-permute-start(f32[64,128]{1,0:T(8,128)S(1)} %get-tuple-element.34), channel_id=1, source_target_pairs={{4,8},{12,16},{20,24},{8,4},{16,12},{24,20},{5,9},{13,17},{21,25},... | collective-permute-start | bytes 98312 | tf_op jit(solution)/shard_map/ppermute | solution.py:400
  41.9 14.7 %all-to-all-start.2 = ((f32[32,24,128]{2,1,0:T(8,128)}), f32[32,24,128]{2,1,0:T(8,128)S(1)}, u32[]{:S(2)}, u32[]{:S(2)}) async-start(f32[32,24,128]{2,1,0:T(8,128)} %get-tuple-element.38), calls=%async_computation.2 | async-start | bytes 786432 | tf_op jit(solution)/shard_map/all_to_all | solution.py:474
  44.9 5.2 %collective-permute-start.5 = (f32[32,128]{1,0:T(8,128)S(1)}, f32[32,128]{1,0:T(8,128)S(1)}, u32[]{:S(2)}, u32[]{:S(2)}) collective-permute-start(f32[32,128]{1,0:T(8,128)S(1)} %get-tuple-element.41), channel_id=1, source_target_pairs={{1,2},{2,1},{5,6},{6,5},{9,10},{10,9},{13,14},{14,13},{17,18},{18,... | collective-permute-start | bytes 49160 | tf_op jit(solution)/shard_map/ppermute | solution.py:400
  45.6 6.5 %collective-permute-start.4 = (f32[32,128]{1,0:T(8,128)S(1)}, f32[32,128]{1,0:T(8,128)S(1)}, u32[]{:S(2)}, u32[]{:S(2)}) collective-permute-start(f32[32,128]{1,0:T(8,128)S(1)} %get-tuple-element.41), channel_id=1, source_target_pairs={{0,1},{2,3},{1,0},{3,2},{4,5},{6,7},{5,4},{7,6},{8,9},{10,11},{9,8... | collective-permute-start | bytes 49160 | tf_op jit(solution)/shard_map/ppermute | solution.py:400
  57.6 14.0 %all-to-all-start.3 = ((f32[32,16,128]{2,1,0:T(8,128)}), f32[32,16,128]{2,1,0:T(8,128)S(1)}, u32[]{:S(2)}, u32[]{:S(2)}) async-start(f32[32,16,128]{2,1,0:T(8,128)} %share_sum.3), calls=%async_computation.3 | async-start | bytes 524288 | tf_op jit(solution)/shard_map/all_to_all | solution.py:486
  61.4 1.3 %collective-permute-start.6 = (f32[64,128]{1,0:T(8,128)S(1)}, f32[64,128]{1,0:T(8,128)S(1)}, u32[]{:S(2)}, u32[]{:S(2)}) collective-permute-start(f32[64,128]{1,0:T(8,128)S(1)} %get-tuple-element.46), channel_id=1, source_target_pairs={{0,4},{8,12},{16,20},{24,28},{4,0},{12,8},{20,16},{28,24},{1,5},{9... | collective-permute-start | bytes 98312 | tf_op jit(solution)/shard_map/ppermute | solution.py:400
  61.8 1.0 %collective-permute-start.7 = (f32[64,128]{1,0:T(8,128)S(1)}, f32[64,128]{1,0:T(8,128)S(1)}, u32[]{:S(2)}, u32[]{:S(2)}) collective-permute-start(f32[64,128]{1,0:T(8,128)S(1)} %get-tuple-element.47), channel_id=1, source_target_pairs={{4,8},{12,16},{20,24},{8,4},{16,12},{24,20},{5,9},{13,17},{21,25},... | collective-permute-start | bytes 98312 | tf_op jit(solution)/shard_map/ppermute | solution.py:400

commit v14 on v13

--- a/solution.py
+++ b/solution.py
@@ -13,7 +13,6 @@
 KX = 32
 STEPS = 2
 GROUP = 4
-PIECES = 4
 LANES = GROUP * KX
 PAD = 8
 VMEM = pl.BlockSpec(memory_space=pltpu.VMEM)
@@ -160,6 +159,7 @@
 
 
 def edge_kernel(n_gy, period, fields, plume, *rest):
+    level_total, cells_x, cells_y = plume.shape
     if len(rest) > 3:
         cuts, levels, first, second, cols, weights, order = rest
         weights[...] = share_weights(n_gy, period, cuts, weights.shape)
@@ -167,23 +167,26 @@
         for n in range(count):
             order[n] = levels[n]
         spot = jnp.int32(count)
-        for l in range(plume.shape[0]):
+        for l in range(level_total):
             found = levels[0] == l
             for n in range(1, count):
                 found = found | (levels[n] == l)
             order[spot] = jnp.int32(l)
             spot = spot + jnp.where(found, 0, 1)
-        for n in range(order.shape[0] - 1, plume.shape[0] - 1, -1):
+        chosen = [order[n] for n in range(level_total)]
+        for n in range(level_total, order.shape[0]):
             order[n] = jnp.int32(0)
+        for n in range(level_total):
+            order[level_total + chosen[n]] = jnp.int32(n)
     else:
         first, second, cols = rest
+        chosen = list(range(level_total))
     even = is_even("gx")
-    cells_x, cells_y = plume.shape[1:]
-    field_rows = fields.shape[0]
     lane = lax.broadcasted_iota(jnp.int32, cols.shape, 1)
     acc = jnp.zeros(cols.shape, jnp.float32)
-    for c in range(field_rows + plume.shape[0]):
-        a = fields[c] if c < field_rows else plume[c - field_rows]
+    for c in range(4 * level_total):
+        l = chosen[c % level_total]
+        a = plume[l] if c >= 3 * level_total else fields[c // level_total * level_total + l]
         west, east = a[:1], a[cells_x - 1 :]
         first[c : c + 1, :] = jnp.where(even, east, west)
         second[c : c + 1, :] = jnp.where(even, west, east)
@@ -256,11 +259,11 @@
     gx, gy = lax.axis_index("gx"), lax.axis_index("gy")
     extra = []
     if last:
-        (fields_all, plume_all, order, slabs, beside, spread, spread_edges, west, east, sems,
+        (fields_all, plume_all, order, slabs, spread, spread_edges, west, east, sems,
          fields_out, plume_out, out_sems) = rest
     else:
         (owners_all, parent_all, x_fwd_all, y_fwd_all, fields_out, plume_out, modes_all,
-         order, slabs, beside, spread, spread_edges, west, east, sems,
+         order, slabs, spread, spread_edges, west, east, sems,
          owners, modes, out_sems, parent, x_fwd, y_fwd, turned, work) = rest
         extra = [(owners_all, owners), (x_fwd_all.at[gx], x_fwd), (y_fwd_all.at[gy], y_fwd),
                  (parent_all.at[0, step + 1], parent)]
@@ -270,14 +273,7 @@
     east[...] = jnp.where(even, row_first[...], row_second[...])
     level_total, cells_x, cells_y = plume.shape
     field_rows = fields.shape[0]
-    total = field_rows + level_total
     nudged = 3 * level_count
-    inner = slice(PAD, PAD + cells_x)
-    for c in range(total):
-        slabs[c, inner] = fields[c] if c < field_rows else plume[c - field_rows]
-        slabs[c, PAD - 1 : PAD] = west[c : c + 1, :]
-        slabs[c, PAD + cells_x : PAD + cells_x + 1] = east[c : c + 1, :]
-    beside[...] = jnp.zeros_like(beside)
     devices = shares.shape[0]
     rows = spread.shape[0] // devices
     packed = beside_rows(rows)
@@ -299,18 +295,36 @@
         piece = spread_edges[t * 2 * KX : (t + 1) * 2 * KX]
         edges = jnp.where(spot_of == t, pltpu.roll(piece, t * width, 1) if t else piece, edges)
     update_rows = columns_dot(edges, y_table)
-    copies[0].wait()
+    updates = []
     for t in range(groups):
         update = columns_dot(spread[t * 2 * KX : (t + 1) * 2 * KX], y_table)
-        for n in range(GROUP):
-            c = t * GROUP + n
-            part = update[n * cells_x : (n + 1) * cells_x]
-            spot = slab_of(order, c, level_count, level_total)
-            slabs[spot, inner] += part[:, :cells_y]
-            slabs[spot, PAD - 1 : PAD] += update_rows[2 * c : 2 * c + 1, :cells_y]
-            slabs[spot, PAD + cells_x : PAD + cells_x + 1] += update_rows[
-                2 * c + 1 : 2 * c + 2, :cells_y]
-            beside[spot] = part[:, cells_y:]
+        updates += [update[n * cells_x : (n + 1) * cells_x] for n in range(GROUP)]
+    copies[0].wait()
+    level_at = [order[n] for n in range(level_total)]
+    source_at = [source[l] for l in level_at]
+    if step == 0:
+        field_at = [fields[f * level_total + l] for f in range(3) for l in level_at]
+        ash_at = [plume[l] for l in level_at]
+        above_at = [plume[jnp.minimum(l + 1, level_total - 1)] for l in level_at]
+    else:
+        field_at = [fields[c] for c in range(field_rows)]
+        ash_at = [plume[n] for n in range(level_total)]
+        above_at = [plume[order[level_total + l + 1]] for l in level_at]
+    falling = [jnp.where(l + 1 < level_total, 0.3, 0.0).astype(jnp.float32) for l in level_at]
+    inner = slice(PAD, PAD + cells_x)
+    beside = {}
+    for c, a in enumerate(field_at + ash_at):
+        n = c % level_total
+        before, after = west[c : c + 1, :], east[c : c + 1, :]
+        if c < field_rows and n < level_count:
+            k = c // level_total * level_count + n
+            a = a + updates[k][:, :cells_y]
+            before = before + update_rows[2 * k : 2 * k + 1, :cells_y]
+            after = after + update_rows[2 * k + 1 : 2 * k + 2, :cells_y]
+            beside[c] = updates[k][:, cells_y:]
+        slabs[c, inner] = a
+        slabs[c, PAD - 1 : PAD] = before
+        slabs[c, PAD + cells_x : PAD + cells_x + 1] = after
 
     lane = lax.broadcasted_iota(jnp.int32, (cells_x, cells_y), 1)
     first, final = lane == 0, lane == cells_y - 1
@@ -320,11 +334,11 @@
     columns = jnp.where(
         lane % 2 == 0, pltpu.roll(north, cells_y - 1, 1), pltpu.roll(south, 1, 1))
 
-    def advance(c, parts, is_field=True):
+    def advance(c, parts):
         centre, to_west, to_east, to_south, to_north = parts
         a = slabs[c, inner]
         column = pltpu.roll(columns, cells_y - 1 - 2 * c, 1)
-        if is_field:
+        if c in beside:
             column = column + beside[c]
         return (
             centre * a
@@ -334,8 +348,8 @@
             + to_north * jnp.where(final, column, pltpu.roll(a, cells_y - 1, 1))
         )
 
-    def weights_at(l):
-        u, v = slabs[l, inner], slabs[level_total + l, inner]
+    def weights_at(n):
+        u, v = slabs[n, inner], slabs[level_total + n, inner]
         neighbours = (
             0.1 + 0.1 * jnp.maximum(u, 0.0), 0.1 - 0.1 * jnp.minimum(u, 0.0),
             0.1 + 0.1 * jnp.maximum(v, 0.0), 0.1 - 0.1 * jnp.minimum(v, 0.0),
@@ -343,40 +357,32 @@
         centre = 1.0 - (neighbours[0] + neighbours[1] + neighbours[2] + neighbours[3])
         return centre, neighbours
 
-    def advance_fields(l, parts):
+    def advance_fields(n, parts):
         results = []
         for f in range(3):
-            c = f * level_total + l
+            c = f * level_total + n
             results.append(advance(c, (parts[0],) + parts[1]))
             fields_out[c] = results[f]
         return results
 
-    def advance_ash(l, parts):
-        settled = advance(field_rows + l, (parts[0] - 0.3,) + parts[1], False) + source[l]
-        if l + 1 < level_total:
-            settled = settled + 0.3 * plume[l + 1]
-        plume_out[l] = settled
+    def advance_ash(n, parts):
+        settled = advance(field_rows + n, (parts[0] - 0.3,) + parts[1])
+        plume_out[n] = settled + falling[n] * above_at[n] + source_at[n]
 
     if last:
-        pieces = out_sems.shape[0] // 4
-        per_piece = level_total // pieces
-        for l in range(level_total):
-            parts = weights_at(l)
-            advance_fields(l, parts)
-            advance_ash(l, parts)
-            if (l + 1) % per_piece == 0:
-                start = l + 1 - per_piece
-                pairs = []
-                for f in range(3):
-                    span = pl.ds(f * level_total + start, per_piece)
-                    pairs.append((fields_out.at[span], fields_all.at[span]))
-                span = pl.ds(start, per_piece)
-                pairs.append((plume_out.at[span], plume_all.at[span]))
-                copies += fetch_all(out_sems.at[pl.ds(start // per_piece * 4, 4)], pairs)
-        for copy in copies[1:]:
+        sent = []
+        for n in range(level_total):
+            parts = weights_at(n)
+            advance_fields(n, parts)
+            advance_ash(n, parts)
+            pairs = [(fields_out.at[f * level_total + n],
+                      fields_all.at[f * level_total + level_at[n]]) for f in range(3)]
+            pairs.append((plume_out.at[n], plume_all.at[level_at[n]]))
+            sent += fetch_all(out_sems.at[pl.ds(4 * n, 4)], pairs)
+        for copy in sent:
             copy.wait()
         return
-    results = [advance_fields(l, weights_at(l)) for l in (order[n] for n in range(level_count))]
+    results = [advance_fields(n, weights_at(n)) for n in range(level_count)]
     for copy in copies[1:]:
         copy.wait()
     emit_modes(
@@ -384,11 +390,11 @@
         parent, owners[step + 1] == gx * n_gy + gy, x_fwd[...], y_fwd[...], modes, turned, work,
     )
     sent = fetch_all(out_sems, [(modes, modes_all)])
-    for n in range(level_count, level_total):
-        l = order[n]
-        advance_fields(l, weights_at(l))
-    for l in range(level_total):
-        advance_ash(l, weights_at(l))
+    for n in range(level_total):
+        parts = weights_at(n)
+        if n >= level_count:
+            advance_fields(n, parts)
+        advance_ash(n, parts)
     sent[0].wait()
 
 
@@ -425,12 +431,12 @@
         return pltpu.CompilerParams(vmem_limit_bytes=mib * 1024 * 1024)
 
     mode_shape = f32((devices, 2 * rows, LANES))
-    step_scratch = [vmem(total, cells_x + 2 * PAD, cells_y), vmem(field_rows, cells_x, cells_y),
-                    vmem(devices * rows, LANES), vmem(devices * rows, LANES),
+    step_scratch = [vmem(total, cells_x + 2 * PAD, cells_y), vmem(devices * rows, LANES), vmem(devices * rows, LANES),
                     vmem(total, cells_y), vmem(total, cells_y), pltpu.SemaphoreType.DMA((5,))]
     levels_space = pltpu.SMEM(levels.shape, jnp.int32)
     owners_space = pltpu.SMEM(owners.shape, jnp.int32)
-    order_space = pltpu.SMEM((2 * level_total,), jnp.int32)
+    order_shape = (3 * level_total,)
+    order_space = pltpu.SMEM(order_shape, jnp.int32)
     raw_levels = levels
     levels, owners = in_hbm(levels), in_hbm(owners)
     mode_scratch = [vmem(nudged, 4 * KX * KX), table_space(x_fwd),
@@ -439,7 +445,7 @@
     inner_scratch = [owners_space, vmem(*mode_shape.shape), pltpu.SemaphoreType.DMA((1,))]
     inner_scratch += mode_scratch
     last_scratch = [vmem(field_rows, cells_x, cells_y), vmem(level_total, cells_x, cells_y),
-                    pltpu.SemaphoreType.DMA((4 * PIECES,))]
+                    pltpu.SemaphoreType.DMA((4 * level_total,))]
 
     modes = pl.pallas_call(
         functools.partial(first_kernel, n_gy, level_total),
@@ -457,7 +463,7 @@
         edge_operands = [flat, plume]
         if step == 0:
             edge_shapes += [f32((2 * rows, LANES)),
-                            jax.ShapeDtypeStruct((2 * level_total,), jnp.int32)]
+                            jax.ShapeDtypeStruct(order_shape, jnp.int32)]
             edge_operands += [cuts, raw_levels]
         edges = pl.pallas_call(
             functools.partial(edge_kernel, n_gy, period),
@@ -470,9 +476,9 @@
         if step == 0:
             weights, order = edges[3], in_hbm(edges[4])
         to_first, to_second, cols = edges[:3]
-        col_first, col_second = exchange("gy", cols, cols)
+        row_first, row_second = exchange("gx", to_first, to_second)
         parts = lax.all_to_all(modes, AXES, 0, 0, tiled=True)
-        parts, col_first, col_second = lax.optimization_barrier((parts, col_first, col_second))
+        parts, row_first, row_second = lax.optimization_barrier((parts, row_first, row_second))
         share = pl.pallas_call(
             functools.partial(share_kernel, n_gx, n_gy),
             out_shape=f32((devices, rows + beside_rows(rows), LANES)),
@@ -481,8 +487,8 @@
             compiler_params=limit(8),
             name="share_sum",
         )(weights, parts, x_back, x_beside)
-        share, to_first, to_second = lax.optimization_barrier((share, to_first, to_second))
-        row_first, row_second = exchange("gx", to_first, to_second)
+        share, cols = lax.optimization_barrier((share, cols))
+        col_first, col_second = exchange("gy", cols, cols)
         shares = lax.all_to_all(share, AXES, 0, 0, tiled=True)
         out_shape = [f32(flat.shape), f32(plume.shape)]
         out_specs = [HBM if last else VMEM] * 2

time: 74.8 us -> 75.1 us (level)
    all_to_all x2, waiting for transfers between devices: 17.8 us -> 6.27 us  [local(): shares = lax.all_to_all(share, AXES, 0, 0, tiled=True)]
    all_to_all x2, waiting for transfers between devices: 7.7 us -> 19.1 us  [local(): parts = lax.all_to_all(modes, AXES, 0, 0, tiled=True)]
where the time goes in v14:
time: 75.1 us; the launch traced here: 75 us
  starting transfers between devices  31.1 us (41%)
  waiting for transfers between devices  29.7 us (40%)
  Pallas kernels  13.2 us (18%)
  between operations  0.82 us (1%)
    all_to_all x2, waiting for transfers between devices, local(): parts = lax.all_to_all(modes, AXES, 0, 0, tiled=True)  19.1 us
    ppermute x8, starting transfers between devices, exchange(): lax.ppermute(data, axis, pairs + [(b, a) for a, b in pairs])  12.4 us
    all_to_all x2, starting transfers between devices, local(): parts = lax.all_to_all(modes, AXES, 0, 0, tiled=True)  11 us
    all_to_all x2, starting transfers between devices, local(): shares = lax.all_to_all(share, AXES, 0, 0, tiled=True)  7.72 us
    pallas_call x2, Pallas kernels, local(): pl.pallas_call(functools.partial(step_kernel, n_gy, step, last, levels.sh...  6.49 us
    all_to_all x2, waiting for transfers between devices, local(): shares = lax.all_to_all(share, AXES, 0, 0, tiled=True)  6.27 us
    ppermute x8, waiting for transfers between devices, exchange(): lax.ppermute(data, axis, pairs + [(b, a) for a, b in pairs])  4.31 us
    pallas_call x1, Pallas kernels, local(): pl.pallas_call(functools.partial(first_kernel, n_gy, level_total), out_sh...  2.78 us
  transfers between devices with their start and end apart: 12, of which 8 were waited for; matrix products, arithmetic and copies ran while one was open for 0% of the time, Pallas kernels for 2%

profile of v14, /device:TPU:0, one launch (start us, length us, event | category | flops | bytes accessed | tf_op | source)
XLA Modules:
  0.0 75.0 jit_solution(11528436758443213160)
XLA Ops:
  0.7 2.8 %first_modes.1 = f32[32,24,128]{2,1,0:T(8,128)} custom-call(s32[8]{0:T(128)} %levels_all.1, s32[2]{0:T(128)} %rest_0_.1, f32[48,32,128]{2,1,0:T(8,128)} %bitcast.2, f32[1,2,24,4096]{3,2,1,0:T(8,128)} %rest_1_.3, bf16[8,384,256]{2,1,0:T(8,128)(2,1)} %constant.10.clone.x_fwd_all.rest_2_, bf16[4,64,384]{2,1,0:T(8,128)(2,1)} %constant.11.clone.y_fwd_all.rest_3_), custom_call_target="tpu_custom_call" | custom-call | tf_op jit(solution)/shard_map/first_modes/pallas_call | solution.py:450
  3.5 0.0 copy-start.4
  3.5 0.0 copy-start.5
  3.5 0.0 copy-start.1
  3.5 0.0 copy-start.3
  3.5 7.8 %all-to-all-start = ((f32[32,24,128]{2,1,0:T(8,128)}), f32[32,24,128]{2,1,0:T(8,128)S(1)}, u32[]{:S(2)}, u32[]{:S(2)}) async-start(f32[32,24,128]{2,1,0:T(8,128)} %first_modes.1), calls=%async_computation | async-start | bytes 786432 | tf_op jit(solution)/shard_map/all_to_all | solution.py:480
  11.3 0.1 reshape.14.rest_0_
  11.4 1.5 %edges.2 = (f32[64,128]{1,0:T(8,128)S(1)}, f32[64,128]{1,0:T(8,128)S(1)}, f32[32,128]{1,0:T(8,128)S(1)}, f32[24,128]{1,0:T(8,128)S(1)}, s32[48]{0:T(128)S(1)}) custom-call(f32[48,32,128]{2,1,0:T(8,128)S(1)} %bitcast.3, f32[16,32,128]{2,1,0:T(8,128)S(1)} %copy-done.2, s32[24]{0:T(128)S(1)} %reshape.14.rest_0_, s32[8]{0:T(128)S(1)} %copy-done.6), custom_call_target="tpu_custom_call" | custom-call | tf_op jit(solution)/shard_map/edges/pallas_call | solution.py:468
  12.9 0.3 collective-permute-start
  13.2 0.7 collective-permute-start.1
  13.9 0.3 collective-permute-done.row_first
  14.2 8.9 %all-to-all-done.parts = f32[32,24,128]{2,1,0:T(8,128)S(1)} async-done(((f32[32,24,128]{2,1,0:T(8,128)}), f32[32,24,128]{2,1,0:T(8,128)S(1)}, u32[]{:S(2)}, u32[]{:S(2)}) %all-to-all-start) | async-done | bytes 393248 | tf_op jit(solution)/shard_map/all_to_all | solution.py:480
  23.1 1.0 %share_sum.2 = f32[32,16,128]{2,1,0:T(8,128)} custom-call(f32[24,128]{1,0:T(8,128)S(1)} %get-tuple-element.25.weights, f32[32,24,128]{2,1,0:T(8,128)S(1)} %all-to-all-done.parts, bf16[512,256]{1,0:T(8,128)(2,1)S(1)} %copy-done.4, bf16[512,128]{1,0:T(8,128)(2,1)S(1)} %copy-done.5), custom_call_target="tpu_custom_call" | custom-call | tf_op jit(solution)/shard_map/share_sum/pallas_call | solution.py:482
  24.1 3.9 %all-to-all-start.1 = ((f32[32,16,128]{2,1,0:T(8,128)}), f32[32,16,128]{2,1,0:T(8,128)S(1)}, u32[]{:S(2)}, u32[]{:S(2)}) async-start(f32[32,16,128]{2,1,0:T(8,128)} %share_sum.2), calls=%async_computation.1 | async-start | bytes 524288 | tf_op jit(solution)/shard_map/all_to_all | solution.py:492
  28.0 0.7 collective-permute-start.3
  28.7 4.5 %collective-permute-start.2 = (f32[32,128]{1,0:T(8,128)S(1)}, f32[32,128]{1,0:T(8,128)S(1)}, u32[]{:S(2)}, u32[]{:S(2)}) collective-permute-start(f32[32,128]{1,0:T(8,128)S(1)} %get-tuple-element.33), channel_id=1, source_target_pairs={{0,1},{2,3},{1,0},{3,2},{4,5},{6,7},{5,4},{7,6},{8,9},{10,11},{9,8... | collective-permute-start | bytes 49160 | tf_op jit(solution)/shard_map/ppermute | solution.py:406
  33.2 1.9 %collective-permute-done.2.col_first = f32[32,128]{1,0:T(8,128)S(1)} collective-permute-done((f32[32,128]{1,0:T(8,128)S(1)}, f32[32,128]{1,0:T(8,128)S(1)}, u32[]{:S(2)}, u32[]{:S(2)}) %collective-permute-start.2) | collective-permute-done | bytes 16416 | tf_op jit(solution)/shard_map/ppermute | solution.py:406
  35.1 3.1 %all-to-all-done.1.shares = f32[32,16,128]{2,1,0:T(8,128)S(1)} async-done(((f32[32,16,128]{2,1,0:T(8,128)}), f32[32,16,128]{2,1,0:T(8,128)S(1)}, u32[]{:S(2)}, u32[]{:S(2)}) %all-to-all-start.1) | async-done | bytes 262176 | tf_op jit(solution)/shard_map/all_to_all | solution.py:492
  38.2 3.4 %inner_step.1 = (f32[48,32,128]{2,1,0:T(8,128)S(1)}, f32[16,32,128]{2,1,0:T(8,128)S(1)}, f32[32,24,128]{2,1,0:T(8,128)}) custom-call(f32[32,16,128]{2,1,0:T(8,128)S(1)} %all-to-all-done.1.shares, f32[48,32,128]{2,1,0:T(8,128)S(1)} %bitcast.4, f32[16,32,128]{2,1,0:T(8,128)S(1)} %copy-done.2, f32[16,32,128]{2,1,0:T(8,128)S(1)} %copy-done.3, ...), custom_call_target="tpu_custom_call" | custom-call | tf_op jit(solution)/shard_map/inner_step/pallas_call | solution.py:501
  41.6 3.3 %all-to-all-start.2 = ((f32[32,24,128]{2,1,0:T(8,128)}), f32[32,24,128]{2,1,0:T(8,128)S(1)}, u32[]{:S(2)}, u32[]{:S(2)}) async-start(f32[32,24,128]{2,1,0:T(8,128)} %get-tuple-element.35), calls=%async_computation.2 | async-start | bytes 786432 | tf_op jit(solution)/shard_map/all_to_all | solution.py:480
  44.9 0.3 edges.3
  45.3 0.3 collective-permute-start.4
  45.6 0.7 collective-permute-start.5
  46.2 0.3 collective-permute-done.4.row_first
  46.5 10.2 %all-to-all-done.2.parts = f32[32,24,128]{2,1,0:T(8,128)S(1)} async-done(((f32[32,24,128]{2,1,0:T(8,128)}), f32[32,24,128]{2,1,0:T(8,128)S(1)}, u32[]{:S(2)}, u32[]{:S(2)}) %all-to-all-start.2) | async-done | bytes 393248 | tf_op jit(solution)/shard_map/all_to_all | solution.py:480
  56.7 1.0 %share_sum.3 = f32[32,16,128]{2,1,0:T(8,128)} custom-call(f32[24,128]{1,0:T(8,128)S(1)} %get-tuple-element.25.weights, f32[32,24,128]{2,1,0:T(8,128)S(1)} %all-to-all-done.2.parts, bf16[512,256]{1,0:T(8,128)(2,1)S(1)} %copy-done.4, bf16[512,128]{1,0:T(8,128)(2,1)S(1)} %copy-done.5), custom_call_target="tpu_custom_call" | custom-call | tf_op jit(solution)/shard_map/share_sum/pallas_call | solution.py:482
  57.8 3.9 %all-to-all-start.3 = ((f32[32,16,128]{2,1,0:T(8,128)}), f32[32,16,128]{2,1,0:T(8,128)S(1)}, u32[]{:S(2)}, u32[]{:S(2)}) async-start(f32[32,16,128]{2,1,0:T(8,128)} %share_sum.3), calls=%async_computation.3 | async-start | bytes 524288 | tf_op jit(solution)/shard_map/all_to_all | solution.py:492
  61.6 0.7 collective-permute-start.7
  62.3 4.5 %collective-permute-start.6 = (f32[32,128]{1,0:T(8,128)S(1)}, f32[32,128]{1,0:T(8,128)S(1)}, u32[]{:S(2)}, u32[]{:S(2)}) collective-permute-start(f32[32,128]{1,0:T(8,128)S(1)} %get-tuple-element.45), channel_id=1, source_target_pairs={{0,1},{2,3},{1,0},{3,2},{4,5},{6,7},{5,4},{7,6},{8,9},{10,11},{9,8... | collective-permute-start | bytes 49160 | tf_op jit(solution)/shard_map/ppermute | solution.py:406
  66.9 1.9 %collective-permute-done.6.col_first = f32[32,128]{1,0:T(8,128)S(1)} collective-permute-done((f32[32,128]{1,0:T(8,128)S(1)}, f32[32,128]{1,0:T(8,128)S(1)}, u32[]{:S(2)}, u32[]{:S(2)}) %collective-permute-start.6) | collective-permute-done | bytes 16416 | tf_op jit(solution)/shard_map/ppermute | solution.py:406
  68.7 3.1 %all-to-all-done.3.shares = f32[32,16,128]{2,1,0:T(8,128)S(1)} async-done(((f32[32,16,128]{2,1,0:T(8,128)}), f32[32,16,128]{2,1,0:T(8,128)S(1)}, u32[]{:S(2)}, u32[]{:S(2)}) %all-to-all-start.3) | async-done | bytes 262176 | tf_op jit(solution)/shard_map/all_to_all | solution.py:492
  71.9 3.1 %final_step.1 = (f32[48,32,128]{2,1,0:T(8,128)}, f32[16,32,128]{2,1,0:T(8,128)}) custom-call(f32[32,16,128]{2,1,0:T(8,128)S(1)} %all-to-all-done.3.shares, f32[48,32,128]{2,1,0:T(8,128)S(1)} %get-tuple-element.36.fields, f32[16,32,128]{2,1,0:T(8,128)S(1)} %get-tuple-element.37.plume, f32[16,32,128]{2,1,0:T(8,128)S(1)} %copy-done.3, ...), custom_call_target="tpu_custom_call" | custom-call | tf_op jit(solution)/shard_map/final_step/pallas_call | solution.py:501
  (18 shorter events, 0.0 us)
Async XLA Ops:
  0.6 10.7 %copy-start.8 = (s32[3,8]{1,0:T(4,128)S(1)}, s32[3,8]{1,0:T(4,128)}, u32[]{:S(2)}) copy-start(s32[3,8]{1,0:T(4,128)} %param.14) | copy-start | bytes 292
  0.6 10.7 %copy-start = (f32[3,16,32,128]{3,2,1,0:T(8,128)S(1)}, f32[3,16,32,128]{3,2,1,0:T(8,128)}, u32[]{:S(2)}) copy-start(f32[3,16,32,128]{3,2,1,0:T(8,128)} %param.12) | copy-start | bytes 2359300
  0.7 10.7 %copy-start.2 = (f32[16,32,128]{2,1,0:T(8,128)S(1)}, f32[16,32,128]{2,1,0:T(8,128)}, u32[]{:S(2)}) copy-start(f32[16,32,128]{2,1,0:T(8,128)} %plume.3) | copy-start | bytes 786436
  0.7 10.7 %copy-start.6 = (s32[8]{0:T(128)S(1)}, s32[8]{0:T(128)}, u32[]{:S(2)}) copy-start(s32[8]{0:T(128)} %levels_all.1) | copy-start | bytes 100
  3.5 19.7 %copy-start.4 = (bf16[512,256]{1,0:T(8,128)(2,1)S(1)}, bf16[512,256]{1,0:T(8,128)(2,1)}, u32[]{:S(2)}) copy-start(bf16[512,256]{1,0:T(8,128)(2,1)} %constant.13.clone.x_back) | copy-start | bytes 786436
  3.5 19.6 %copy-start.5 = (bf16[512,128]{1,0:T(8,128)(2,1)S(1)}, bf16[512,128]{1,0:T(8,128)(2,1)}, u32[]{:S(2)}) copy-start(bf16[512,128]{1,0:T(8,128)(2,1)} %constant.14.clone.x_beside) | copy-start | bytes 393220
  3.5 34.7 %copy-start.1 = (bf16[4,192,256]{2,1,0:T(8,128)(2,1)S(1)}, bf16[4,192,256]{2,1,0:T(8,128)(2,1)}, u32[]{:S(2)}) copy-start(bf16[4,192,256]{2,1,0:T(8,128)(2,1)} %constant.12.clone.y_back) | copy-start | bytes 1179652
  3.5 34.7 %copy-start.3 = (f32[16,32,128]{2,1,0:T(8,128)S(1)}, f32[16,32,128]{2,1,0:T(8,128)}, u32[]{:S(2)}) copy-start(f32[16,32,128]{2,1,0:T(8,128)} %source.3) | copy-start | bytes 786436
  3.5 19.6 %all-to-all-start = ((f32[32,24,128]{2,1,0:T(8,128)}), f32[32,24,128]{2,1,0:T(8,128)S(1)}, u32[]{:S(2)}, u32[]{:S(2)}) async-start(f32[32,24,128]{2,1,0:T(8,128)} %first_modes.1), calls=%async_computation | async-start | bytes 786432 | tf_op jit(solution)/shard_map/all_to_all | solution.py:480
  12.9 25.4 %copy-start.7 = (s32[48]{0:T(128)}, s32[48]{0:T(128)S(1)}, u32[]{:S(2)}) copy-start(s32[48]{0:T(128)S(1)} %get-tuple-element.34.order_all) | copy-start | bytes 580
  12.9 1.3 %collective-permute-start = (f32[64,128]{1,0:T(8,128)S(1)}, f32[64,128]{1,0:T(8,128)S(1)}, u32[]{:S(2)}, u32[]{:S(2)}) collective-permute-start(f32[64,128]{1,0:T(8,128)S(1)} %get-tuple-element.26), channel_id=1, source_target_pairs={{0,4},{8,12},{16,20},{24,28},{4,0},{12,8},{20,16},{28,24},{1,5},{9... | collective-permute-start | bytes 98312 | tf_op jit(solution)/shard_map/ppermute | solution.py:406
  13.2 1.0 %collective-permute-start.1 = (f32[64,128]{1,0:T(8,128)S(1)}, f32[64,128]{1,0:T(8,128)S(1)}, u32[]{:S(2)}, u32[]{:S(2)}) collective-permute-start(f32[64,128]{1,0:T(8,128)S(1)} %get-tuple-element.27), channel_id=1, source_target_pairs={{4,8},{12,16},{20,24},{8,4},{16,12},{24,20},{5,9},{13,17},{21,25},... | collective-permute-start | bytes 98312 | tf_op jit(solution)/shard_map/ppermute | solution.py:406
  24.1 14.1 %all-to-all-start.1 = ((f32[32,16,128]{2,1,0:T(8,128)}), f32[32,16,128]{2,1,0:T(8,128)S(1)}, u32[]{:S(2)}, u32[]{:S(2)}) async-start(f32[32,16,128]{2,1,0:T(8,128)} %share_sum.2), calls=%async_computation.1 | async-start | bytes 524288 | tf_op jit(solution)/shard_map/all_to_all | solution.py:492
  28.0 5.2 %collective-permute-start.3 = (f32[32,128]{1,0:T(8,128)S(1)}, f32[32,128]{1,0:T(8,128)S(1)}, u32[]{:S(2)}, u32[]{:S(2)}) collective-permute-start(f32[32,128]{1,0:T(8,128)S(1)} %get-tuple-element.33), channel_id=1, source_target_pairs={{1,2},{2,1},{5,6},{6,5},{9,10},{10,9},{13,14},{14,13},{17,18},{18,... | collective-permute-start | bytes 49160 | tf_op jit(solution)/shard_map/ppermute | solution.py:406
  28.7 6.4 %collective-permute-start.2 = (f32[32,128]{1,0:T(8,128)S(1)}, f32[32,128]{1,0:T(8,128)S(1)}, u32[]{:S(2)}, u32[]{:S(2)}) collective-permute-start(f32[32,128]{1,0:T(8,128)S(1)} %get-tuple-element.33), channel_id=1, source_target_pairs={{0,1},{2,3},{1,0},{3,2},{4,5},{6,7},{5,4},{7,6},{8,9},{10,11},{9,8... | collective-permute-start | bytes 49160 | tf_op jit(solution)/shard_map/ppermute | solution.py:406
  41.6 15.1 %all-to-all-start.2 = ((f32[32,24,128]{2,1,0:T(8,128)}), f32[32,24,128]{2,1,0:T(8,128)S(1)}, u32[]{:S(2)}, u32[]{:S(2)}) async-start(f32[32,24,128]{2,1,0:T(8,128)} %get-tuple-element.35), calls=%async_computation.2 | async-start | bytes 786432 | tf_op jit(solution)/shard_map/all_to_all | solution.py:480
  45.3 1.3 %collective-permute-start.4 = (f32[64,128]{1,0:T(8,128)S(1)}, f32[64,128]{1,0:T(8,128)S(1)}, u32[]{:S(2)}, u32[]{:S(2)}) collective-permute-start(f32[64,128]{1,0:T(8,128)S(1)} %get-tuple-element.38), channel_id=1, source_target_pairs={{0,4},{8,12},{16,20},{24,28},{4,0},{12,8},{20,16},{28,24},{1,5},{9... | collective-permute-start | bytes 98312 | tf_op jit(solution)/shard_map/ppermute | solution.py:406
  45.6 1.0 %collective-permute-start.5 = (f32[64,128]{1,0:T(8,128)S(1)}, f32[64,128]{1,0:T(8,128)S(1)}, u32[]{:S(2)}, u32[]{:S(2)}) collective-permute-start(f32[64,128]{1,0:T(8,128)S(1)} %get-tuple-element.39), channel_id=1, source_target_pairs={{4,8},{12,16},{20,24},{8,4},{16,12},{24,20},{5,9},{13,17},{21,25},... | collective-permute-start | bytes 98312 | tf_op jit(solution)/shard_map/ppermute | solution.py:406
  57.8 14.1 %all-to-all-start.3 = ((f32[32,16,128]{2,1,0:T(8,128)}), f32[32,16,128]{2,1,0:T(8,128)S(1)}, u32[]{:S(2)}, u32[]{:S(2)}) async-start(f32[32,16,128]{2,1,0:T(8,128)} %share_sum.3), calls=%async_computation.3 | async-start | bytes 524288 | tf_op jit(solution)/shard_map/all_to_all | solution.py:492
  61.6 5.2 %collective-permute-start.7 = (f32[32,128]{1,0:T(8,128)S(1)}, f32[32,128]{1,0:T(8,128)S(1)}, u32[]{:S(2)}, u32[]{:S(2)}) collective-permute-start(f32[32,128]{1,0:T(8,128)S(1)} %get-tuple-element.45), channel_id=1, source_target_pairs={{1,2},{2,1},{5,6},{6,5},{9,10},{10,9},{13,14},{14,13},{17,18},{18,... | collective-permute-start | bytes 49160 | tf_op jit(solution)/shard_map/ppermute | solution.py:406
  62.3 6.4 %collective-permute-start.6 = (f32[32,128]{1,0:T(8,128)S(1)}, f32[32,128]{1,0:T(8,128)S(1)}, u32[]{:S(2)}, u32[]{:S(2)}) collective-permute-start(f32[32,128]{1,0:T(8,128)S(1)} %get-tuple-element.45), channel_id=1, source_target_pairs={{0,1},{2,3},{1,0},{3,2},{4,5},{6,7},{5,4},{7,6},{8,9},{10,11},{9,8... | collective-permute-start | bytes 49160 | tf_op jit(solution)/shard_map/ppermute | solution.py:406

commit v15 on v12

--- a/solution.py
+++ b/solution.py
@@ -97,11 +97,11 @@
         stacked, table, (((0,), (0,)), ((), ())), preferred_element_type=jnp.float32)
 
 
-def emit_modes(read, parent, is_owner, x_fwd, y_fwd, modes, turned, work):
+def emit_modes(chosen, parent, is_owner, x_fwd, y_fwd, modes, turned, work):
     devices, rows = modes.shape[0], modes.shape[1] // 2
     slabs = parent.shape[0]
     groups = slabs // GROUP
-    head, rest = split(jnp.concatenate([read(c) for c in range(slabs)], axis=0))
+    head, rest = split(jnp.concatenate(chosen, axis=0))
     half = lax.dot_general(
         y_fwd, jnp.concatenate([head, head, rest], axis=1), (((1,), (1,)), ((), ())),
         preferred_element_type=jnp.float32)
@@ -149,7 +149,7 @@
         copy.wait()
     level_count = parent.shape[0] // 3
     emit_modes(
-        lambda c: fields[slab_of(levels, c, level_count, level_total)],
+        [fields[slab_of(levels, c, level_count, level_total)] for c in range(parent.shape[0])],
         parent, owners[0] == gx * n_gy + gy, x_fwd[...], y_fwd[...], modes, turned, work,
     )
 
@@ -158,20 +158,34 @@
     return lax.rem(lax.axis_index(axis), 2) == 0
 
 
-def edge_kernel(n_gy, period, fields, plume, *rest):
-    if len(rest) > 3:
-        cuts, first, second, cols, weights = rest
-        weights[...] = share_weights(n_gy, period, cuts, weights.shape)
-    else:
-        first, second, cols = rest
+def edge_kernel(n_gy, period, cuts, levels, fields, plume, first, second, cols, weights, order):
+    level_total = plume.shape[0]
+    weights[...] = share_weights(n_gy, period, cuts, weights.shape)
+    count = levels.shape[0]
+    for n in range(count):
+        order[n] = levels[n]
+    spot = jnp.int32(count)
+    for l in range(level_total):
+        found = levels[0] == l
+        for n in range(1, count):
+            found = found | (levels[n] == l)
+        order[spot] = jnp.int32(l)
+        spot = spot + jnp.where(found, 0, 1)
+    chosen = [order[n] for n in range(level_total)]
+    for n in range(level_total, order.shape[0]):
+        order[n] = jnp.int32(0)
+    for n in range(level_total):
+        order[level_total + chosen[n]] = jnp.int32(n)
+    slabs = [fields[f * level_total + l] for f in range(3) for l in chosen]
+    emit_edges(slabs + [plume[l] for l in chosen], first, second, cols)
+
+
+def emit_edges(slabs, first, second, cols):
     even = is_even("gx")
-    cells_x, cells_y = plume.shape[1:]
-    field_rows = fields.shape[0]
     lane = lax.broadcasted_iota(jnp.int32, cols.shape, 1)
     acc = jnp.zeros(cols.shape, jnp.float32)
-    for c in range(field_rows + plume.shape[0]):
-        a = fields[c] if c < field_rows else plume[c - field_rows]
-        west, east = a[:1], a[cells_x - 1 :]
+    for c, a in enumerate(slabs):
+        west, east = a[:1], a[a.shape[0] - 1 :]
         first[c : c + 1, :] = jnp.where(even, east, west)
         second[c : c + 1, :] = jnp.where(even, west, east)
         acc = jnp.where(lane // 2 == c, pltpu.roll(a, 2 * c + 1, 1), acc)
@@ -238,34 +252,66 @@
             out[g * n_gy + h, rows:, :] = beside
 
 
-def step_kernel(n_gy, step, last, shares, fields, plume, source, row_first, row_second,
-                col_first, col_second, y_back, levels_all, *rest):
-    gx, gy = lax.axis_index("gx"), lax.axis_index("gy")
-    extra = []
-    if last:
-        (fields_out, plume_out, levels, slabs, beside, spread, spread_edges, west, east,
-         sems) = rest
-    else:
-        (owners_all, parent_all, x_fwd_all, y_fwd_all, fields_out, plume_out, modes,
-         levels, slabs, beside, spread, spread_edges, west, east, sems,
-         owners, parent, x_fwd, y_fwd, turned, work) = rest
-        extra = [(owners_all, owners), (x_fwd_all.at[gx], x_fwd), (y_fwd_all.at[gy], y_fwd),
-                 (parent_all.at[0, step + 1], parent)]
-    copies = fetch_all(sems, [(levels_all, levels)] + extra)
-    even = is_even("gx")
-    west[...] = jnp.where(even, row_second[...], row_first[...])
-    east[...] = jnp.where(even, row_first[...], row_second[...])
-    level_total, cells_x, cells_y = plume.shape
-    field_rows = fields.shape[0]
-    total = field_rows + level_total
-    level_count = levels.shape[0]
-    nudged = 3 * level_count
-    inner = slice(PAD, PAD + cells_x)
-    for c in range(total):
-        slabs[c, inner] = fields[c] if c < field_rows else plume[c - field_rows]
-        slabs[c, PAD - 1 : PAD] = west[c : c + 1, :]
-        slabs[c, PAD + cells_x : PAD + cells_x + 1] = east[c : c + 1, :]
-    beside[...] = jnp.zeros_like(beside)
+class Halo:
+    def __init__(self, row_first, row_second, col_first, col_second, west, east):
+        even = is_even("gx")
+        west[...] = jnp.where(even, row_second[...], row_first[...])
+        east[...] = jnp.where(even, row_first[...], row_second[...])
+        self.west, self.east = west, east
+        even = is_even("gy")
+        north = jnp.where(even, col_first[...], col_second[...])
+        south = jnp.where(even, col_second[...], col_first[...])
+        shape = north.shape
+        lane = lax.broadcasted_iota(jnp.int32, shape, 1)
+        self.last = shape[1] - 1
+        self.at_first, self.at_last = lane == 0, lane == self.last
+        self.columns = jnp.where(
+            lane % 2 == 0, pltpu.roll(north, self.last, 1), pltpu.roll(south, 1, 1))
+
+    def rows(self, c):
+        return self.west[c : c + 1, :], self.east[c : c + 1, :]
+
+    def column(self, c):
+        return pltpu.roll(self.columns, self.last - 2 * c, 1)
+
+    def move(self, slab, column, parts):
+        centre, to_west, to_east, to_south, to_north = parts
+        cells_x = column.shape[0]
+        a = slab[PAD : PAD + cells_x]
+        return (
+            centre * a
+            + to_west * slab[PAD - 1 : PAD - 1 + cells_x]
+            + to_east * slab[PAD + 1 : PAD + 1 + cells_x]
+            + to_south * jnp.where(self.at_first, column, pltpu.roll(a, 1, 1))
+            + to_north * jnp.where(self.at_last, column, pltpu.roll(a, self.last, 1))
+        )
+
+
+def place(slab, a, rows):
+    cells_x = a.shape[0]
+    slab[PAD : PAD + cells_x] = a
+    slab[PAD - 1 : PAD] = rows[0]
+    slab[PAD + cells_x : PAD + cells_x + 1] = rows[1]
+
+
+def wind_weights(u, v):
+    neighbours = (
+        0.1 + 0.1 * jnp.maximum(u, 0.0), 0.1 - 0.1 * jnp.minimum(u, 0.0),
+        0.1 + 0.1 * jnp.maximum(v, 0.0), 0.1 - 0.1 * jnp.minimum(v, 0.0),
+    )
+    centre = 1.0 - (neighbours[0] + neighbours[1] + neighbours[2] + neighbours[3])
+    return (centre,) + neighbours
+
+
+def settling(parts):
+    return (parts[0] - 0.3,) + parts[1:]
+
+
+def above(l, level_total):
+    return jnp.where(l + 1 < level_total, 0.3, 0.0).astype(jnp.float32)
+
+
+def nudge_updates(shares, spread, spread_edges, y_table, nudged, cells_x):
     devices = shares.shape[0]
     rows = spread.shape[0] // devices
     packed = beside_rows(rows)
@@ -279,7 +325,6 @@
                 moved = pltpu.roll(edge, -m * width % LANES, 1) if m else edge
                 start = d * rows + m * packed
                 spread_edges[start : start + count] = moved[:count]
-    y_table = y_back[gy]
     groups = nudged // GROUP
     spot_of = lax.broadcasted_iota(jnp.int32, (2 * KX, LANES), 1) // width
     edges = jnp.zeros((2 * KX, LANES), jnp.float32)
@@ -287,64 +332,122 @@
         piece = spread_edges[t * 2 * KX : (t + 1) * 2 * KX]
         edges = jnp.where(spot_of == t, pltpu.roll(piece, t * width, 1) if t else piece, edges)
     update_rows = columns_dot(edges, y_table)
-    copies[0].wait()
+    updates = []
     for t in range(groups):
         update = columns_dot(spread[t * 2 * KX : (t + 1) * 2 * KX], y_table)
-        for n in range(GROUP):
-            c = t * GROUP + n
-            part = update[n * cells_x : (n + 1) * cells_x]
-            spot = slab_of(levels, c, level_count, level_total)
-            slabs[spot, inner] += part[:, :cells_y]
-            slabs[spot, PAD - 1 : PAD] += update_rows[2 * c : 2 * c + 1, :cells_y]
-            slabs[spot, PAD + cells_x : PAD + cells_x + 1] += update_rows[
-                2 * c + 1 : 2 * c + 2, :cells_y]
-            beside[spot] = part[:, cells_y:]
-
-    lane = lax.broadcasted_iota(jnp.int32, (cells_x, cells_y), 1)
-    first, final = lane == 0, lane == cells_y - 1
-    even = is_even("gy")
-    north = jnp.where(even, col_first[...], col_second[...])
-    south = jnp.where(even, col_second[...], col_first[...])
-    columns = jnp.where(
-        lane % 2 == 0, pltpu.roll(north, cells_y - 1, 1), pltpu.roll(south, 1, 1))
-
-    def advance(c, parts):
-        centre, to_west, to_east, to_south, to_north = parts
-        a = slabs[c, inner]
-        column = pltpu.roll(columns, cells_y - 1 - 2 * c, 1)
-        if c < field_rows:
-            column = column + beside[c]
-        return (
-            centre * a
-            + to_west * slabs[c, PAD - 1 : PAD - 1 + cells_x]
-            + to_east * slabs[c, PAD + 1 : PAD + 1 + cells_x]
-            + to_south * jnp.where(first, column, pltpu.roll(a, 1, 1))
-            + to_north * jnp.where(final, column, pltpu.roll(a, cells_y - 1, 1))
-        )
-
-    for l in range(level_total):
-        u, v = slabs[l, inner], slabs[level_total + l, inner]
-        beside_parts = (
-            0.1 + 0.1 * jnp.maximum(u, 0.0), 0.1 - 0.1 * jnp.minimum(u, 0.0),
-            0.1 + 0.1 * jnp.maximum(v, 0.0), 0.1 - 0.1 * jnp.minimum(v, 0.0),
-        )
-        centre = 1.0 - (beside_parts[0] + beside_parts[1] + beside_parts[2] + beside_parts[3])
+        updates += [update[n * cells_x : (n + 1) * cells_x] for n in range(GROUP)]
+    return updates, update_rows
+
+
+def nudged_kernel(n_gy, step, last, level_count, level_total, shares, fields, row_first, row_second,
+                  col_first, col_second, y_back, order_all, *rest):
+    gx, gy = lax.axis_index("gx"), lax.axis_index("gy")
+    cells_x, cells_y = fields.shape[1:]
+    nudged = 3 * level_count
+    if last:
+        (plume, source, _, _, fields_all, plume_all, order, slabs, spread, spread_edges, west, east,
+         sems, fields_out, plume_out, out_sems) = rest
+        extra = []
+    else:
+        (owners_all, parent_all, x_fwd_all, y_fwd_all, fields_out, winds_out, modes,
+         order, slabs, spread, spread_edges, west, east, sems,
+         owners, parent, x_fwd, y_fwd, turned, work) = rest
+        extra = [(owners_all, owners), (x_fwd_all.at[gx], x_fwd), (y_fwd_all.at[gy], y_fwd),
+                 (parent_all.at[0, step + 1], parent)]
+    copies = fetch_all(sems, [(order_all, order)] + extra)
+    halo = Halo(row_first, row_second, col_first, col_second, west, east)
+    updates, update_rows = nudge_updates(
+        shares, spread, spread_edges, y_back[gy], nudged, cells_x)
+    copies[0].wait()
+    level_at = [order[n] for n in range(level_count)]
+    beside = []
+    for k in range(nudged):
+        f, n = k // level_count, k % level_count
+        a = fields[f * level_total + level_at[n]] if step == 0 else fields[k]
+        before, after = halo.rows(f * level_total + n)
+        place(slabs.at[k], a + updates[k][:, :cells_y],
+              (before + update_rows[2 * k : 2 * k + 1, :cells_y],
+               after + update_rows[2 * k + 1 : 2 * k + 2, :cells_y]))
+        beside.append(updates[k][:, cells_y:])
+    inner = slice(PAD, PAD + cells_x)
+    results = [None] * nudged
+    sent = []
+    for n in range(level_count):
+        u, v = slabs[n, inner], slabs[level_count + n, inner]
+        parts = wind_weights(u, v)
         for f in range(3):
-            fields_out[f * level_total + l] = advance(
-                f * level_total + l, (centre,) + beside_parts)
-        settled = advance(field_rows + l, (centre - 0.3,) + beside_parts) + source[l]
-        if l + 1 < level_total:
-            settled = settled + 0.3 * plume[l + 1]
-        plume_out[l] = settled
-
+            k = f * level_count + n
+            column = halo.column(f * level_total + n) + beside[k]
+            results[k] = halo.move(slabs[k], column, parts)
+            fields_out[k] = results[k]
+        if not last:
+            winds_out[n] = u
+            winds_out[level_count + n] = v
+            continue
+        l = level_at[n]
+        c = 3 * level_total + n
+        place(slabs.at[nudged + n], plume[n], halo.rows(c))
+        settled = halo.move(slabs[nudged + n], halo.column(c), settling(parts))
+        plume_out[n] = settled + above(l, level_total) * plume[order[level_total + l + 1]] + source[l]
+        pairs = [(fields_out.at[f * level_count + n], fields_all.at[f * level_total + l])
+                 for f in range(3)] + [(plume_out.at[n], plume_all.at[l])]
+        sent += fetch_all(out_sems.at[pl.ds(4 * n, 4)], pairs)
     if last:
+        for copy in sent:
+            copy.wait()
         return
     for copy in copies[1:]:
         copy.wait()
-    emit_modes(
-        lambda c: fields_out[slab_of(levels, c, level_count, level_total)],
-        parent, owners[step + 1] == gx * n_gy + gy, x_fwd[...], y_fwd[...], modes, turned, work,
-    )
+    emit_modes(results, parent, owners[step + 1] == gx * n_gy + gy, x_fwd[...], y_fwd[...], modes,
+               turned, work)
+
+
+def others_kernel(step, last, level_count, fields, plume, source, row_first, row_second, col_first,
+                  col_second, order_all, *rest):
+    level_total, cells_x, cells_y = plume.shape
+    if last:
+        fields_all, plume_all, order, slab, west, east, sems, fields_out, plume_out, out_sems = rest
+    else:
+        (done, winds, fields_out, plume_out, first, second, cols, order, slab, west, east,
+         sems) = rest
+    copies = fetch_all(sems, [(order_all, order)])
+    halo = Halo(row_first, row_second, col_first, col_second, west, east)
+    copies[0].wait()
+    level_at = [order[n] for n in range(level_total)]
+    kept = level_total - level_count
+    sent = []
+    results = {}
+    for n in range(level_count if last else 0, level_total):
+        l = level_at[n]
+        m = n - level_count
+        if m < 0:
+            parts = wind_weights(winds[n], winds[level_count + n])
+        else:
+            given = [fields[f * level_total + l] if step == 0 else fields[f * kept + m]
+                     for f in range(3)]
+            parts = wind_weights(given[0], given[1])
+            for f in range(3):
+                c = f * level_total + n
+                place(slab.at[4 * n + f], given[f], halo.rows(c))
+                results[c] = halo.move(slab[4 * n + f], halo.column(c), parts)
+                fields_out[f * kept + m] = results[c]
+        c = 3 * level_total + n
+        place(slab.at[4 * n + 3], plume[l] if step == 0 else plume[n], halo.rows(c))
+        higher = (jnp.minimum(l + 1, level_total - 1) if step == 0 else order[level_total + l + 1])
+        results[c] = (halo.move(slab[4 * n + 3], halo.column(c), settling(parts))
+                      + above(l, level_total) * plume[higher] + source[l])
+        plume_out[m if last else n] = results[c]
+        if last:
+            pairs = [(fields_out.at[f * kept + m], fields_all.at[f * level_total + l])
+                     for f in range(3)] + [(plume_out.at[m], plume_all.at[l])]
+            sent += fetch_all(out_sems.at[pl.ds(4 * m, 4)], pairs)
+    for copy in sent:
+        copy.wait()
+    if not last:
+        for f in range(3):
+            for n in range(level_count):
+                results[f * level_total + n] = done[f * level_count + n]
+        emit_edges([results[c] for c in range(4 * level_total)], first, second, cols)
 
 
 def exchange(axis, first, second):
@@ -379,48 +482,55 @@
     def limit(mib):
         return pltpu.CompilerParams(vmem_limit_bytes=mib * 1024 * 1024)
 
+    count = levels.shape[0]
+    kept = level_total - count
     mode_shape = f32((devices, 2 * rows, LANES))
-    step_scratch = [vmem(total, cells_x + 2 * PAD, cells_y), vmem(field_rows, cells_x, cells_y),
-                    vmem(devices * rows, LANES), vmem(devices * rows, LANES),
-                    vmem(total, cells_y), vmem(total, cells_y), pltpu.SemaphoreType.DMA((5,))]
+    order_shape = (3 * level_total,)
+    edge_shapes = [f32((total, cells_y)), f32((total, cells_y)), f32((cells_x, 2 * total))]
     levels_space = pltpu.SMEM(levels.shape, jnp.int32)
     owners_space = pltpu.SMEM(owners.shape, jnp.int32)
-    levels, owners = in_hbm(levels), in_hbm(owners)
+    order_space = pltpu.SMEM(order_shape, jnp.int32)
+    rows_space = vmem(total, cells_y)
     mode_scratch = [vmem(nudged, 4 * KX * KX), table_space(x_fwd),
                     table_space(y_fwd), vmem(nudged, KX, LANES),
                     vmem(devices * rows, 2 * LANES)]
+    nudged_scratch = [order_space, vmem(nudged + count, cells_x + 2 * PAD, cells_y),
+                      vmem(devices * rows, LANES), vmem(devices * rows, LANES),
+                      rows_space, rows_space, pltpu.SemaphoreType.DMA((5,))]
+    others_scratch = [order_space, vmem(total, cells_x + 2 * PAD, cells_y), rows_space, rows_space,
+                      pltpu.SemaphoreType.DMA((1,))]
+
+    def out_scratch(slabs):
+        return [vmem(3 * slabs, cells_x, cells_y), vmem(slabs, cells_x, cells_y),
+                pltpu.SemaphoreType.DMA((4 * slabs,))]
 
     modes = pl.pallas_call(
         functools.partial(first_kernel, n_gy, level_total),
         out_shape=mode_shape,
         in_specs=[HBM] * 6,
         out_specs=VMEM,
-        scratch_shapes=[levels_space, owners_space, vmem(field_rows, cells_x, cells_y), pltpu.SemaphoreType.DMA((6,))]
-        + mode_scratch,
+        scratch_shapes=[levels_space, owners_space, vmem(field_rows, cells_x, cells_y),
+                        pltpu.SemaphoreType.DMA((6,))] + mode_scratch,
         compiler_params=limit(8),
         name="first_modes",
-    )(levels, owners, *map(in_hbm, (flat, parent_modes, x_fwd, y_fwd)))
+    )(*map(in_hbm, (levels, owners, flat, parent_modes, x_fwd, y_fwd)))
+    *edges, weights, order = pl.pallas_call(
+        functools.partial(edge_kernel, n_gy, period),
+        out_shape=edge_shapes
+        + [f32((2 * rows, LANES)), jax.ShapeDtypeStruct(order_shape, jnp.int32)],
+        in_specs=[SMEM, SMEM, VMEM, VMEM],
+        out_specs=[VMEM] * 4 + [SMEM],
+        compiler_params=limit(8),
+        name="edges",
+    )(cuts, levels, flat, plume)
+    order = in_hbm(order)
+    others = flat
     for step in range(STEPS):
         last = step == STEPS - 1
-        edge_shapes = [f32((total, cells_y)), f32((total, cells_y)), f32((cells_x, 2 * total))]
-        edge_operands = [flat, plume]
-        if step == 0:
-            edge_shapes.append(f32((2 * rows, LANES)))
-            edge_operands.append(cuts)
-        edges = pl.pallas_call(
-            functools.partial(edge_kernel, n_gy, period),
-            out_shape=edge_shapes,
-            in_specs=[VMEM, VMEM, SMEM][: len(edge_operands)],
-            out_specs=[VMEM] * len(edge_shapes),
-            compiler_params=limit(8),
-            name="edges",
-        )(*edge_operands)
-        if step == 0:
-            weights = edges[3]
-        cols = edges[2]
-        row_first, row_second = exchange("gx", *edges[:2])
+        to_first, to_second, cols = edges
+        col_first, col_second = exchange("gy", cols, cols)
         parts = lax.all_to_all(modes, AXES, 0, 0, tiled=True)
-        parts, row_first, row_second = lax.optimization_barrier((parts, row_first, row_second))
+        parts, col_first, col_second = lax.optimization_barrier((parts, col_first, col_second))
         share = pl.pallas_call(
             functools.partial(share_kernel, n_gx, n_gy),
             out_shape=f32((devices, rows + beside_rows(rows), LANES)),
@@ -429,29 +539,52 @@
             compiler_params=limit(8),
             name="share_sum",
         )(weights, parts, x_back, x_beside)
-        share, cols = lax.optimization_barrier((share, cols))
-        col_first, col_second = exchange("gy", cols, cols)
+        share, to_first, to_second = lax.optimization_barrier((share, to_first, to_second))
+        row_first, row_second = exchange("gx", to_first, to_second)
+        halo = [row_first, row_second, col_first, col_second]
         shares = lax.all_to_all(share, AXES, 0, 0, tiled=True)
-        out_shape = [f32(flat.shape), f32(plume.shape)]
-        operands = [shares, flat, plume, source, row_first, row_second, col_first, col_second,
-                    y_back, levels]
-        if not last:
-            out_shape.append(mode_shape)
-            operands += [owners, in_hbm(parent_modes), in_hbm(x_fwd), in_hbm(y_fwd)]
-        results = pl.pallas_call(
-            functools.partial(step_kernel, n_gy, step, last),
-            out_shape=out_shape,
-            in_specs=[VMEM] * 9 + [HBM] * (len(operands) - 9),
-            out_specs=[VMEM] * len(out_shape),
-            scratch_shapes=[levels_space] + step_scratch
-            + ([] if last else [owners_space] + mode_scratch),
-            compiler_params=limit(20),
-            name="final_step" if last else "inner_step",
-        )(*operands)
         if last:
-            flat, plume = results
+            final = pl.pallas_call(
+                functools.partial(others_kernel, step, True, count),
+                out_shape=[f32((field_rows, cells_x, cells_y)), f32(plume.shape)],
+                in_specs=[VMEM] * 7 + [HBM],
+                out_specs=[HBM] * 2,
+                scratch_shapes=others_scratch + out_scratch(kept),
+                compiler_params=limit(8),
+                name="last_others",
+            )(others, plume, source, *halo, order)
+            flat, plume = pl.pallas_call(
+                functools.partial(nudged_kernel, n_gy, step, True, count, level_total),
+                out_shape=[f32((field_rows, cells_x, cells_y)), f32(plume.shape)],
+                in_specs=[VMEM] * 7 + [HBM] + [VMEM] * 2 + [HBM] * 2,
+                out_specs=[HBM] * 2,
+                scratch_shapes=nudged_scratch + out_scratch(count),
+                input_output_aliases={10: 0, 11: 1},
+                compiler_params=limit(12),
+                name="last_nudged",
+            )(shares, flat, *halo, y_back, order, plume, source, *final)
         else:
-            flat, plume, modes = results
+            done, winds, modes = pl.pallas_call(
+                functools.partial(nudged_kernel, n_gy, step, False, count, level_total),
+                out_shape=[f32((nudged, cells_x, cells_y)), f32((2 * count, cells_x, cells_y)),
+                           mode_shape],
+                in_specs=[VMEM] * 7 + [HBM] * 5,
+                out_specs=[VMEM] * 3,
+                scratch_shapes=nudged_scratch + [owners_space] + mode_scratch,
+                compiler_params=limit(12),
+                name="inner_nudged",
+            )(shares, flat, *halo, y_back, order,
+              *map(in_hbm, (owners, parent_modes, x_fwd, y_fwd)))
+            others, plume, *edges = pl.pallas_call(
+                functools.partial(others_kernel, step, False, count),
+                out_shape=[f32((3 * kept, cells_x, cells_y)), f32(plume.shape)] + edge_shapes,
+                in_specs=[VMEM] * 7 + [HBM] + [VMEM] * 2,
+                out_specs=[VMEM] * 5,
+                scratch_shapes=others_scratch,
+                compiler_params=limit(8),
+                name="inner_others",
+            )(others, plume, source, *halo, order, done, winds)
+            flat = done
     return flat.reshape(fields.shape), plume
 
 

time: 74.6 us -> 76.1 us (1.020)
  waiting for transfers between devices: 30.3 us -> 23.2 us
  local copies, waits for them, and re-layouts: 0.86 us -> 5.26 us
  Pallas kernels: 11.8 us -> 15.3 us
    all_to_all x2, waiting for transfers between devices: 19.8 us -> 3.26 us  [local(): parts = lax.all_to_all(modes, AXES, 0, 0, tiled=True)]
    all_to_all x2, waiting for transfers between devices: 6.27 us -> 15.7 us  [local(): shares = lax.all_to_all(share, AXES, 0, 0, tiled=True)]
    unnamed x16 -> x46, local copies, waits for them, and re-layouts: 0.78 us -> 5.18 us
    pallas_call x2 -> x4, Pallas kernels: 5.76 us -> 9.01 us  [the longest x1 2.87 us: local(): pl.pallas_call(functools.partial(nudged_kernel, n_gy, step, False, count,...]
  transfers between devices with their start and end apart: 12 -> 12, of which waited for: 8 -> 7; matrix products, arithmetic and copies ran while one was open for 0% -> 0% of each run, Pallas kernels for 2% -> 7%
where the time goes in v15:
time: 76.1 us; the launch traced here: 75.6 us
  starting transfers between devices  30.8 us (40%)
  waiting for transfers between devices  23.2 us (30%)
  Pallas kernels  15.3 us (20%)
  local copies, waits for them, and re-layouts  5.26 us (7%)
  between operations  0.91 us (1%)
    all_to_all x2, waiting for transfers between devices, local(): shares = lax.all_to_all(share, AXES, 0, 0, tiled=True)  15.7 us
    ppermute x8, starting transfers between devices, exchange(): lax.ppermute(data, axis, pairs + [(b, a) for a, b in pairs])  12.3 us
    all_to_all x2, starting transfers between devices, local(): parts = lax.all_to_all(modes, AXES, 0, 0, tiled=True)  10.5 us
    all_to_all x2, starting transfers between devices, local(): shares = lax.all_to_all(share, AXES, 0, 0, tiled=True)  7.99 us
    unnamed x46, local copies, waits for them, and re-layouts  5.18 us
    ppermute x8, waiting for transfers between devices, exchange(): lax.ppermute(data, axis, pairs + [(b, a) for a, b in pairs])  4.22 us
    all_to_all x2, waiting for transfers between devices, local(): parts = lax.all_to_all(modes, AXES, 0, 0, tiled=True)  3.26 us
    pallas_call x1, Pallas kernels, local(): pl.pallas_call(functools.partial(nudged_kernel, n_gy, step, False, count,...  2.87 us
  transfers between devices with their start and end apart: 12, of which 7 were waited for; matrix products, arithmetic and copies ran while one was open for 0% of the time, Pallas kernels for 7%

profile of v15, /device:TPU:0, one launch (start us, length us, event | category | flops | bytes accessed | tf_op | source)
XLA Modules:
  0.0 75.6 jit_solution(11712718143571668475)
XLA Ops:
  0.7 2.8 %first_modes.1 = f32[32,24,128]{2,1,0:T(8,128)} custom-call(s32[8]{0:T(128)} %levels_all.1, s32[2]{0:T(128)} %rest_0_.1, f32[48,32,128]{2,1,0:T(8,128)} %bitcast.2, f32[1,2,24,4096]{3,2,1,0:T(8,128)} %rest_1_.2, bf16[8,384,256]{2,1,0:T(8,128)(2,1)} %constant.10.clone.x_fwd_all.rest_2_, bf16[4,64,384]{2,1,0:T(8,128)(2,1)} %constant.11.clone.y_fwd_all.rest_3_), custom_call_target="tpu_custom_call" | custom-call | tf_op jit(solution)/shard_map/first_modes/pallas_call | solution.py:507
  3.5 7.3 %all-to-all-start = ((f32[32,24,128]{2,1,0:T(8,128)}), f32[32,24,128]{2,1,0:T(8,128)S(1)}, u32[]{:S(2)}, u32[]{:S(2)}) async-start(f32[32,24,128]{2,1,0:T(8,128)} %first_modes.1), calls=%async_computation | async-start | bytes 786432 | tf_op jit(solution)/shard_map/all_to_all | solution.py:532
  10.9 1.5 %edges.1 = (f32[64,128]{1,0:T(8,128)S(1)}, f32[64,128]{1,0:T(8,128)S(1)}, f32[32,128]{1,0:T(8,128)S(1)}, f32[24,128]{1,0:T(8,128)S(1)}, s32[48]{0:T(128)S(1)}) custom-call(s32[24]{0:T(128)S(1)} %reshape.13.cuts, s32[8]{0:T(128)S(1)} %copy-done.17, f32[48,32,128]{2,1,0:T(8,128)S(1)} %bitcast.3, f32[16,32,128]{2,1,0:T(8,128)S(1)} %copy-done.3), custom_call_target="tpu_custom_call" | custom-call | tf_op jit(solution)/shard_map/edges/pallas_call | solution.py:517
  12.4 0.7 collective-permute-start.1
  13.1 4.5 %collective-permute-start = (f32[32,128]{1,0:T(8,128)S(1)}, f32[32,128]{1,0:T(8,128)S(1)}, u32[]{:S(2)}, u32[]{:S(2)}) collective-permute-start(f32[32,128]{1,0:T(8,128)S(1)} %get-tuple-element.32), channel_id=1, source_target_pairs={{0,1},{2,3},{1,0},{3,2},{4,5},{6,7},{5,4},{7,6},{8,9},{10,11},{9,8... | collective-permute-start | bytes 49160 | tf_op jit(solution)/shard_map/ppermute | solution.py:458
  17.6 1.9 %collective-permute-done.col_first = f32[32,128]{1,0:T(8,128)S(1)} collective-permute-done((f32[32,128]{1,0:T(8,128)S(1)}, f32[32,128]{1,0:T(8,128)S(1)}, u32[]{:S(2)}, u32[]{:S(2)}) %collective-permute-start) | collective-permute-done | bytes 16416 | tf_op jit(solution)/shard_map/ppermute | solution.py:458
  19.5 3.3 %all-to-all-done.parts = f32[32,24,128]{2,1,0:T(8,128)S(1)} async-done(((f32[32,24,128]{2,1,0:T(8,128)}), f32[32,24,128]{2,1,0:T(8,128)S(1)}, u32[]{:S(2)}, u32[]{:S(2)}) %all-to-all-start) | async-done | bytes 393248 | tf_op jit(solution)/shard_map/all_to_all | solution.py:532
  22.8 1.0 %share_sum.2 = f32[32,16,128]{2,1,0:T(8,128)} custom-call(f32[24,128]{1,0:T(8,128)S(1)} %get-tuple-element.31.weights, f32[32,24,128]{2,1,0:T(8,128)S(1)} %all-to-all-done.parts, bf16[512,256]{1,0:T(8,128)(2,1)S(1)} %copy-done.4, bf16[512,128]{1,0:T(8,128)(2,1)S(1)} %copy-done.5), custom_call_target="tpu_custom_call" | custom-call | tf_op jit(solution)/shard_map/share_sum/pallas_call | solution.py:534
  23.8 3.8 %all-to-all-start.1 = ((f32[32,16,128]{2,1,0:T(8,128)}), f32[32,16,128]{2,1,0:T(8,128)S(1)}, u32[]{:S(2)}, u32[]{:S(2)}) async-start(f32[32,16,128]{2,1,0:T(8,128)} %share_sum.2), calls=%async_computation.1 | async-start | bytes 524288 | tf_op jit(solution)/shard_map/all_to_all | solution.py:545
  27.6 0.3 collective-permute-start.2
  27.9 0.7 collective-permute-start.3
  28.9 8.9 %all-to-all-done.1.shares = f32[32,16,128]{2,1,0:T(8,128)S(1)} async-done(((f32[32,16,128]{2,1,0:T(8,128)}), f32[32,16,128]{2,1,0:T(8,128)S(1)}, u32[]{:S(2)}, u32[]{:S(2)}) %all-to-all-start.1) | async-done | bytes 262176 | tf_op jit(solution)/shard_map/all_to_all | solution.py:545
  37.8 2.9 %inner_nudged.1 = (f32[24,32,128]{2,1,0:T(8,128)S(1)}, f32[16,32,128]{2,1,0:T(8,128)S(1)}, f32[32,24,128]{2,1,0:T(8,128)}) custom-call(f32[32,16,128]{2,1,0:T(8,128)S(1)} %all-to-all-done.1.shares, f32[48,32,128]{2,1,0:T(8,128)S(1)} %bitcast.4, f32[64,128]{1,0:T(8,128)S(1)} %collective-permute-done.2.row_first, ...), custom_call_target="tpu_custom_call" | custom-call | tf_op jit(solution)/shard_map/inner_nudged/pallas_call | solution.py:567
  40.8 3.2 %all-to-all-start.2 = ((f32[32,24,128]{2,1,0:T(8,128)}), f32[32,24,128]{2,1,0:T(8,128)S(1)}, u32[]{:S(2)}, u32[]{:S(2)}) async-start(f32[32,24,128]{2,1,0:T(8,128)} %get-tuple-element.42), calls=%async_computation.2 | async-start | bytes 786432 | tf_op jit(solution)/shard_map/all_to_all | solution.py:532
  44.0 0.9 %copy-done.7 = f32[16,32,128]{2,1,0:T(8,128)S(1)} copy-done((f32[16,32,128]{2,1,0:T(8,128)S(1)}, f32[16,32,128]{2,1,0:T(8,128)}, u32[]{:S(2)}) %copy-start.7) | copy-done | bytes 262168
  44.9 0.8 %copy-done.9 = f32[64,128]{1,0:T(8,128)S(1)} copy-done((f32[64,128]{1,0:T(8,128)S(1)}, f32[64,128]{1,0:T(8,128)}, u32[]{:S(2)}) %copy-start.9) | copy-done | bytes 32792
  45.7 0.8 %copy-done.11 = f32[64,128]{1,0:T(8,128)S(1)} copy-done((f32[64,128]{1,0:T(8,128)S(1)}, f32[64,128]{1,0:T(8,128)}, u32[]{:S(2)}) %copy-start.11) | copy-done | bytes 32792
  46.5 0.7 copy-done.13
  47.2 1.6 %inner_others.1 = (f32[24,32,128]{2,1,0:T(8,128)S(1)}, f32[16,32,128]{2,1,0:T(8,128)S(1)}, f32[64,128]{1,0:T(8,128)S(1)}, f32[64,128]{1,0:T(8,128)S(1)}, f32[32,128]{1,0:T(8,128)S(1)}) custom-call(f32[48,32,128]{2,1,0:T(8,128)S(1)} %bitcast.5, f32[16,32,128]{2,1,0:T(8,128)S(1)} %copy-done.3, f32[16,32,128]{2,1,0:T(8,128)S(1)} %copy-done.1, ...), custom_call_target="tpu_custom_call" | custom-call | tf_op jit(solution)/shard_map/inner_others/pallas_call | solution.py:578
  48.8 0.6 copy-done.18
  49.4 0.6 copy-done.20
  50.0 0.7 collective-permute-start.5
  50.7 4.5 %collective-permute-start.4 = (f32[32,128]{1,0:T(8,128)S(1)}, f32[32,128]{1,0:T(8,128)S(1)}, u32[]{:S(2)}, u32[]{:S(2)}) collective-permute-start(f32[32,128]{1,0:T(8,128)S(1)} %get-tuple-element.45), channel_id=1, source_target_pairs={{0,1},{2,3},{1,0},{3,2},{4,5},{6,7},{5,4},{7,6},{8,9},{10,11},{9,8... | collective-permute-start | bytes 49160 | tf_op jit(solution)/shard_map/ppermute | solution.py:458
  55.2 1.7 %collective-permute-done.4.col_first = f32[32,128]{1,0:T(8,128)S(1)} collective-permute-done((f32[32,128]{1,0:T(8,128)S(1)}, f32[32,128]{1,0:T(8,128)S(1)}, u32[]{:S(2)}, u32[]{:S(2)}) %collective-permute-start.4) | collective-permute-done | bytes 16416 | tf_op jit(solution)/shard_map/ppermute | solution.py:458
  57.0 0.7 copy-done.15
  57.7 1.0 %share_sum.3 = f32[32,16,128]{2,1,0:T(8,128)} custom-call(f32[24,128]{1,0:T(8,128)S(1)} %copy-done.15, f32[32,24,128]{2,1,0:T(8,128)S(1)} %all-to-all-done.2.parts, bf16[512,256]{1,0:T(8,128)(2,1)S(1)} %copy-done.4, bf16[512,128]{1,0:T(8,128)(2,1)S(1)} %copy-done.5), custom_call_target="tpu_custom_call" | custom-call | tf_op jit(solution)/shard_map/share_sum/pallas_call | solution.py:534
  58.7 4.2 %all-to-all-start.3 = ((f32[32,16,128]{2,1,0:T(8,128)}), f32[32,16,128]{2,1,0:T(8,128)S(1)}, u32[]{:S(2)}, u32[]{:S(2)}) async-start(f32[32,16,128]{2,1,0:T(8,128)} %share_sum.3), calls=%async_computation.3 | async-start | bytes 524288 | tf_op jit(solution)/shard_map/all_to_all | solution.py:545
  62.9 0.3 collective-permute-start.6
  63.2 0.7 collective-permute-start.7
  64.2 2.1 %last_others.1 = (f32[48,32,128]{2,1,0:T(8,128)}, f32[16,32,128]{2,1,0:T(8,128)}) custom-call(f32[24,32,128]{2,1,0:T(8,128)S(1)} %get-tuple-element.55.fields, f32[16,32,128]{2,1,0:T(8,128)S(1)} %get-tuple-element.54.plume.rest_0_, f32[16,32,128]{2,1,0:T(8,128)S(1)} %copy-done.1, f32[64,128]{1,0:T(8,128)S(1)} %collective-permute-done.6.row_first, ...), custom_call_target="tpu_custom_call" | custom-call | tf_op jit(solution)/shard_map/last_others/pallas_call | solution.py:547
  66.3 6.8 %all-to-all-done.3.shares = f32[32,16,128]{2,1,0:T(8,128)S(1)} async-done(((f32[32,16,128]{2,1,0:T(8,128)}), f32[32,16,128]{2,1,0:T(8,128)S(1)}, u32[]{:S(2)}, u32[]{:S(2)}) %all-to-all-start.3) | async-done | bytes 262176 | tf_op jit(solution)/shard_map/all_to_all | solution.py:545
  73.1 2.5 %last_nudged.1 = (f32[48,32,128]{2,1,0:T(8,128)}, f32[16,32,128]{2,1,0:T(8,128)}) custom-call(f32[32,16,128]{2,1,0:T(8,128)S(1)} %all-to-all-done.3.shares, f32[24,32,128]{2,1,0:T(8,128)S(1)} %get-tuple-element.43.rest_0_.fields, f32[64,128]{1,0:T(8,128)S(1)} %collective-permute-done.6.row_first, ...), custom_call_target="tpu_custom_call", output_to_operand_aliasing={{0}: (10, {}), {1}: (11, {})} | custom-call | tf_op jit(solution)/shard_map/last_nudged/pallas_call | solution.py:556
  (47 shorter events, 0.8 us)
Async XLA Ops:
  0.6 10.2 %copy-start.22 = (s32[3,8]{1,0:T(4,128)S(1)}, s32[3,8]{1,0:T(4,128)}, u32[]{:S(2)}) copy-start(s32[3,8]{1,0:T(4,128)} %param.14) | copy-start | bytes 292
  0.6 10.3 %copy-start = (f32[3,16,32,128]{3,2,1,0:T(8,128)S(1)}, f32[3,16,32,128]{3,2,1,0:T(8,128)}, u32[]{:S(2)}) copy-start(f32[3,16,32,128]{3,2,1,0:T(8,128)} %param.12) | copy-start | bytes 2359300
  0.7 10.2 %copy-start.3 = (f32[16,32,128]{2,1,0:T(8,128)S(1)}, f32[16,32,128]{2,1,0:T(8,128)}, u32[]{:S(2)}) copy-start(f32[16,32,128]{2,1,0:T(8,128)} %plume.3) | copy-start | bytes 786436
  0.7 10.2 %copy-start.17 = (s32[8]{0:T(128)S(1)}, s32[8]{0:T(128)}, u32[]{:S(2)}) copy-start(s32[8]{0:T(128)} %levels_all.1) | copy-start | bytes 100
  3.5 19.3 %copy-start.4 = (bf16[512,256]{1,0:T(8,128)(2,1)S(1)}, bf16[512,256]{1,0:T(8,128)(2,1)}, u32[]{:S(2)}) copy-start(bf16[512,256]{1,0:T(8,128)(2,1)} %constant.13.clone.x_back) | copy-start | bytes 786436
  3.5 19.3 %copy-start.5 = (bf16[512,128]{1,0:T(8,128)(2,1)S(1)}, bf16[512,128]{1,0:T(8,128)(2,1)}, u32[]{:S(2)}) copy-start(bf16[512,128]{1,0:T(8,128)(2,1)} %constant.14.clone.x_beside) | copy-start | bytes 393220
  3.5 34.4 %copy-start.2 = (bf16[4,192,256]{2,1,0:T(8,128)(2,1)S(1)}, bf16[4,192,256]{2,1,0:T(8,128)(2,1)}, u32[]{:S(2)}) copy-start(bf16[4,192,256]{2,1,0:T(8,128)(2,1)} %constant.12.clone.y_back) | copy-start | bytes 1179652
  3.5 19.3 %all-to-all-start = ((f32[32,24,128]{2,1,0:T(8,128)}), f32[32,24,128]{2,1,0:T(8,128)S(1)}, u32[]{:S(2)}, u32[]{:S(2)}) async-start(f32[32,24,128]{2,1,0:T(8,128)} %first_modes.1), calls=%async_computation | async-start | bytes 786432 | tf_op jit(solution)/shard_map/all_to_all | solution.py:532
  12.4 25.4 %copy-start.16 = (s32[48]{0:T(128)}, s32[48]{0:T(128)S(1)}, u32[]{:S(2)}) copy-start(s32[48]{0:T(128)S(1)} %get-tuple-element.41.order_all) | copy-start | bytes 580
  12.4 28.3 %copy-start.14 = (f32[24,128]{1,0:T(8,128)}, f32[24,128]{1,0:T(8,128)S(1)}, u32[]{:S(2)}) copy-start(f32[24,128]{1,0:T(8,128)S(1)} %get-tuple-element.31.weights) | copy-start | bytes 36868
  12.4 5.2 %collective-permute-start.1 = (f32[32,128]{1,0:T(8,128)S(1)}, f32[32,128]{1,0:T(8,128)S(1)}, u32[]{:S(2)}, u32[]{:S(2)}) collective-permute-start(f32[32,128]{1,0:T(8,128)S(1)} %get-tuple-element.32), channel_id=1, source_target_pairs={{1,2},{2,1},{5,6},{6,5},{9,10},{10,9},{13,14},{14,13},{17,18},{18,... | collective-permute-start | bytes 49160 | tf_op jit(solution)/shard_map/ppermute | solution.py:458
  13.1 6.5 %collective-permute-start = (f32[32,128]{1,0:T(8,128)S(1)}, f32[32,128]{1,0:T(8,128)S(1)}, u32[]{:S(2)}, u32[]{:S(2)}) collective-permute-start(f32[32,128]{1,0:T(8,128)S(1)} %get-tuple-element.32), channel_id=1, source_target_pairs={{0,1},{2,3},{1,0},{3,2},{4,5},{6,7},{5,4},{7,6},{8,9},{10,11},{9,8... | collective-permute-start | bytes 49160 | tf_op jit(solution)/shard_map/ppermute | solution.py:458
  19.5 21.2 %copy-start.12 = (f32[32,128]{1,0:T(8,128)}, f32[32,128]{1,0:T(8,128)S(1)}, u32[]{:S(2)}) copy-start(f32[32,128]{1,0:T(8,128)S(1)} %collective-permute-done.col_first) | copy-start | bytes 49156
  23.8 14.0 %all-to-all-start.1 = ((f32[32,16,128]{2,1,0:T(8,128)}), f32[32,16,128]{2,1,0:T(8,128)S(1)}, u32[]{:S(2)}, u32[]{:S(2)}) async-start(f32[32,16,128]{2,1,0:T(8,128)} %share_sum.2), calls=%async_computation.1 | async-start | bytes 524288 | tf_op jit(solution)/shard_map/all_to_all | solution.py:545
  27.6 1.3 %collective-permute-start.2 = (f32[64,128]{1,0:T(8,128)S(1)}, f32[64,128]{1,0:T(8,128)S(1)}, u32[]{:S(2)}, u32[]{:S(2)}) collective-permute-start(f32[64,128]{1,0:T(8,128)S(1)} %get-tuple-element.37), channel_id=1, source_target_pairs={{0,4},{8,12},{16,20},{24,28},{4,0},{12,8},{20,16},{28,24},{1,5},{9... | collective-permute-start | bytes 98312 | tf_op jit(solution)/shard_map/ppermute | solution.py:458
  27.9 1.0 %collective-permute-start.3 = (f32[64,128]{1,0:T(8,128)S(1)}, f32[64,128]{1,0:T(8,128)S(1)}, u32[]{:S(2)}, u32[]{:S(2)}) collective-permute-start(f32[64,128]{1,0:T(8,128)S(1)} %get-tuple-element.38), channel_id=1, source_target_pairs={{4,8},{12,16},{20,24},{8,4},{16,12},{24,20},{5,9},{13,17},{21,25},... | collective-permute-start | bytes 98312 | tf_op jit(solution)/shard_map/ppermute | solution.py:458
  28.9 11.8 %copy-start.8 = (f32[64,128]{1,0:T(8,128)}, f32[64,128]{1,0:T(8,128)S(1)}, u32[]{:S(2)}) copy-start(f32[64,128]{1,0:T(8,128)S(1)} %collective-permute-done.2.row_first) | copy-start | bytes 98308
  28.9 11.8 %copy-start.10 = (f32[64,128]{1,0:T(8,128)}, f32[64,128]{1,0:T(8,128)S(1)}, u32[]{:S(2)}) copy-start(f32[64,128]{1,0:T(8,128)S(1)} %collective-permute-done.3.row_second) | copy-start | bytes 98308
  37.8 6.1 %copy-start.1 = (f32[16,32,128]{2,1,0:T(8,128)S(1)}, f32[16,32,128]{2,1,0:T(8,128)}, u32[]{:S(2)}) copy-start(f32[16,32,128]{2,1,0:T(8,128)} %rest_1_.3) | copy-start | bytes 786436
  40.8 3.2 %copy-start.6 = (f32[16,32,128]{2,1,0:T(8,128)}, f32[16,32,128]{2,1,0:T(8,128)S(1)}, u32[]{:S(2)}) copy-start(f32[16,32,128]{2,1,0:T(8,128)S(1)} %get-tuple-element.44.rest_1_) | copy-start | bytes 786436
  40.8 16.2 %all-to-all-start.2 = ((f32[32,24,128]{2,1,0:T(8,128)}), f32[32,24,128]{2,1,0:T(8,128)S(1)}, u32[]{:S(2)}, u32[]{:S(2)}) async-start(f32[32,24,128]{2,1,0:T(8,128)} %get-tuple-element.42), calls=%async_computation.2 | async-start | bytes 786432 | tf_op jit(solution)/shard_map/all_to_all | solution.py:532
  44.0 1.0 %copy-start.7 = (f32[16,32,128]{2,1,0:T(8,128)S(1)}, f32[16,32,128]{2,1,0:T(8,128)}, u32[]{:S(2)}) copy-start(f32[16,32,128]{2,1,0:T(8,128)} %copy-done.6) | copy-start | bytes 786436
  44.9 0.8 %copy-start.9 = (f32[64,128]{1,0:T(8,128)S(1)}, f32[64,128]{1,0:T(8,128)}, u32[]{:S(2)}) copy-start(f32[64,128]{1,0:T(8,128)} %copy-done.8) | copy-start | bytes 98308
  45.7 0.8 %copy-start.11 = (f32[64,128]{1,0:T(8,128)S(1)}, f32[64,128]{1,0:T(8,128)}, u32[]{:S(2)}) copy-start(f32[64,128]{1,0:T(8,128)} %copy-done.10) | copy-start | bytes 98308
  46.5 0.7 copy-start.13
  50.0 5.2 %collective-permute-start.5 = (f32[32,128]{1,0:T(8,128)S(1)}, f32[32,128]{1,0:T(8,128)S(1)}, u32[]{:S(2)}, u32[]{:S(2)}) collective-permute-start(f32[32,128]{1,0:T(8,128)S(1)} %get-tuple-element.45), channel_id=1, source_target_pairs={{1,2},{2,1},{5,6},{6,5},{9,10},{10,9},{13,14},{14,13},{17,18},{18,... | collective-permute-start | bytes 49160 | tf_op jit(solution)/shard_map/ppermute | solution.py:458
  50.7 6.3 %collective-permute-start.4 = (f32[32,128]{1,0:T(8,128)S(1)}, f32[32,128]{1,0:T(8,128)S(1)}, u32[]{:S(2)}, u32[]{:S(2)}) collective-permute-start(f32[32,128]{1,0:T(8,128)S(1)} %get-tuple-element.45), channel_id=1, source_target_pairs={{0,1},{2,3},{1,0},{3,2},{4,5},{6,7},{5,4},{7,6},{8,9},{10,11},{9,8... | collective-permute-start | bytes 49160 | tf_op jit(solution)/shard_map/ppermute | solution.py:458
  57.7 5.3 %copy-start.21 = (f32[64,128]{1,0:T(8,128)S(1)}, f32[64,128]{1,0:T(8,128)}, u32[]{:S(2)}) copy-start(f32[64,128]{1,0:T(8,128)} %copy-done.20) | copy-start | bytes 98308
  57.7 5.6 %copy-start.19 = (f32[64,128]{1,0:T(8,128)S(1)}, f32[64,128]{1,0:T(8,128)}, u32[]{:S(2)}) copy-start(f32[64,128]{1,0:T(8,128)} %copy-done.18) | copy-start | bytes 98308
  58.7 14.4 %all-to-all-start.3 = ((f32[32,16,128]{2,1,0:T(8,128)}), f32[32,16,128]{2,1,0:T(8,128)S(1)}, u32[]{:S(2)}, u32[]{:S(2)}) async-start(f32[32,16,128]{2,1,0:T(8,128)} %share_sum.3), calls=%async_computation.3 | async-start | bytes 524288 | tf_op jit(solution)/shard_map/all_to_all | solution.py:545
  62.9 1.3 %collective-permute-start.6 = (f32[64,128]{1,0:T(8,128)S(1)}, f32[64,128]{1,0:T(8,128)S(1)}, u32[]{:S(2)}, u32[]{:S(2)}) collective-permute-start(f32[64,128]{1,0:T(8,128)S(1)} %copy-done.21), channel_id=1, source_target_pairs={{0,4},{8,12},{16,20},{24,28},{4,0},{12,8},{20,16},{28,24},{1,5},{9... | collective-permute-start | bytes 98312 | tf_op jit(solution)/shard_map/ppermute | solution.py:458
  63.2 1.0 %collective-permute-start.7 = (f32[64,128]{1,0:T(8,128)S(1)}, f32[64,128]{1,0:T(8,128)S(1)}, u32[]{:S(2)}, u32[]{:S(2)}) collective-permute-start(f32[64,128]{1,0:T(8,128)S(1)} %copy-done.19), channel_id=1, source_target_pairs={{4,8},{12,16},{20,24},{8,4},{16,12},{24,20},{5,9},{13,17},{21,25},... | collective-permute-start | bytes 98312 | tf_op jit(solution)/shard_map/ppermute | solution.py:458
  (3 other events, 1.9 us)

commit v16 on v15

--- a/solution.py
+++ b/solution.py
@@ -158,7 +158,9 @@
     return lax.rem(lax.axis_index(axis), 2) == 0
 
 
-def edge_kernel(n_gy, period, cuts, levels, fields, plume, first, second, cols, weights, order):
+def edge_kernel(n_gy, period, cuts, levels, fields, plume, y_back_all, first, second, cols, weights,
+                nudged, others, y_back, order, sems):
+    copies = fetch_all(sems, [(y_back_all.at[lax.axis_index("gy")], y_back)])
     level_total = plume.shape[0]
     weights[...] = share_weights(n_gy, period, cuts, weights.shape)
     count = levels.shape[0]
@@ -178,6 +180,15 @@
         order[level_total + chosen[n]] = jnp.int32(n)
     slabs = [fields[f * level_total + l] for f in range(3) for l in chosen]
     emit_edges(slabs + [plume[l] for l in chosen], first, second, cols)
+    kept = level_total - count
+    for c, a in enumerate(slabs):
+        f, n = c // level_total, c % level_total
+        if n < count:
+            nudged[f * count + n] = a
+        else:
+            others[f * kept + n - count] = a
+    for copy in copies:
+        copy.wait()
 
 
 def emit_edges(slabs, first, second, cols):
@@ -357,13 +368,13 @@
     copies = fetch_all(sems, [(order_all, order)] + extra)
     halo = Halo(row_first, row_second, col_first, col_second, west, east)
     updates, update_rows = nudge_updates(
-        shares, spread, spread_edges, y_back[gy], nudged, cells_x)
+        shares, spread, spread_edges, y_back[...], nudged, cells_x)
     copies[0].wait()
     level_at = [order[n] for n in range(level_count)]
     beside = []
     for k in range(nudged):
         f, n = k // level_count, k % level_count
-        a = fields[f * level_total + level_at[n]] if step == 0 else fields[k]
+        a = fields[k]
         before, after = halo.rows(f * level_total + n)
         place(slabs.at[k], a + updates[k][:, :cells_y],
               (before + update_rows[2 * k : 2 * k + 1, :cells_y],
@@ -409,10 +420,15 @@
         fields_all, plume_all, order, slab, west, east, sems, fields_out, plume_out, out_sems = rest
     else:
         (done, winds, fields_out, plume_out, first, second, cols, order, slab, west, east,
-         sems) = rest
+         sems, plume_here, source_here) = rest
     copies = fetch_all(sems, [(order_all, order)])
+    if not last:
+        copies += fetch_all(
+            sems.at[pl.ds(1, 2)], [(plume, plume_here), (source, source_here)])
+        plume, source = plume_here, source_here
     halo = Halo(row_first, row_second, col_first, col_second, west, east)
-    copies[0].wait()
+    for copy in copies:
+        copy.wait()
     level_at = [order[n] for n in range(level_total)]
     kept = level_total - level_count
     sent = []
@@ -423,8 +439,7 @@
         if m < 0:
             parts = wind_weights(winds[n], winds[level_count + n])
         else:
-            given = [fields[f * level_total + l] if step == 0 else fields[f * kept + m]
-                     for f in range(3)]
+            given = [fields[f * kept + m] for f in range(3)]
             parts = wind_weights(given[0], given[1])
             for f in range(3):
                 c = f * level_total + n
@@ -498,7 +513,8 @@
                       vmem(devices * rows, LANES), vmem(devices * rows, LANES),
                       rows_space, rows_space, pltpu.SemaphoreType.DMA((5,))]
     others_scratch = [order_space, vmem(total, cells_x + 2 * PAD, cells_y), rows_space, rows_space,
-                      pltpu.SemaphoreType.DMA((1,))]
+                      pltpu.SemaphoreType.DMA((3,))]
+    ash_space = vmem(level_total, cells_x, cells_y)
 
     def out_scratch(slabs):
         return [vmem(3 * slabs, cells_x, cells_y), vmem(slabs, cells_x, cells_y),
@@ -514,17 +530,21 @@
         compiler_params=limit(8),
         name="first_modes",
     )(*map(in_hbm, (levels, owners, flat, parent_modes, x_fwd, y_fwd)))
-    *edges, weights, order = pl.pallas_call(
+    field_shapes = [f32((3 * count, cells_x, cells_y)), f32((3 * kept, cells_x, cells_y))]
+    *edges, weights, flat_nudged, others, y_back, order = pl.pallas_call(
         functools.partial(edge_kernel, n_gy, period),
         out_shape=edge_shapes
-        + [f32((2 * rows, LANES)), jax.ShapeDtypeStruct(order_shape, jnp.int32)],
-        in_specs=[SMEM, SMEM, VMEM, VMEM],
-        out_specs=[VMEM] * 4 + [SMEM],
+        + [f32((2 * rows, LANES))] + field_shapes
+        + [jax.ShapeDtypeStruct(y_back.shape[1:], y_back.dtype),
+           jax.ShapeDtypeStruct(order_shape, jnp.int32)],
+        in_specs=[SMEM, SMEM, VMEM, VMEM, HBM],
+        out_specs=[VMEM] * 7 + [SMEM],
+        scratch_shapes=[pltpu.SemaphoreType.DMA((1,))],
         compiler_params=limit(8),
         name="edges",
-    )(cuts, levels, flat, plume)
+    )(cuts, levels, flat, plume, in_hbm(y_back))
     order = in_hbm(order)
-    others = flat
+    flat = flat_nudged
     for step in range(STEPS):
         last = step == STEPS - 1
         to_first, to_second, cols = edges
@@ -578,12 +598,12 @@
             others, plume, *edges = pl.pallas_call(
                 functools.partial(others_kernel, step, False, count),
                 out_shape=[f32((3 * kept, cells_x, cells_y)), f32(plume.shape)] + edge_shapes,
-                in_specs=[VMEM] * 7 + [HBM] + [VMEM] * 2,
+                in_specs=[VMEM] + [HBM] * 2 + [VMEM] * 4 + [HBM] + [VMEM] * 2,
                 out_specs=[VMEM] * 5,
-                scratch_shapes=others_scratch,
+                scratch_shapes=others_scratch + [ash_space, ash_space],
                 compiler_params=limit(8),
                 name="inner_others",
-            )(others, plume, source, *halo, order, done, winds)
+            )(others, in_hbm(plume), in_hbm(source), *halo, order, done, winds)
             flat = done
     return flat.reshape(fields.shape), plume
 

time: 76.1 us -> 73.7 us (0.968)
  local copies, waits for them, and re-layouts: 5.26 us -> 0.13 us
  waiting for transfers between devices: 23.2 us -> 25.3 us
  Pallas kernels: 15.3 us -> 17.3 us
  starting transfers between devices: 30.8 us -> 29.7 us
    unnamed x46 -> x16, local copies, waits for them, and re-layouts: 5.18 us -> 0.04 us
    all_to_all x2, waiting for transfers between devices: 3.26 us -> 5.36 us  [local(): parts = lax.all_to_all(modes, AXES, 0, 0, tiled=True)]
    pallas_call x1, Pallas kernels: 1.48 us -> 2.42 us  [local(): pl.pallas_call(functools.partial(edge_kernel, n_gy, period), out_shape=ed...]
  transfers between devices with their start and end apart: 12 -> 12, of which waited for: 7 -> 8; matrix products, arithmetic and copies ran while one was open for 0% -> 0% of each run, Pallas kernels for 7% -> 9%
where the time goes in v16:
time: 73.7 us; the launch traced here: 73.2 us
  starting transfers between devices  29.7 us (40%)
  waiting for transfers between devices  25.3 us (34%)
  Pallas kernels  17.3 us (23%)
  between operations  0.82 us (1%)
    all_to_all x2, waiting for transfers between devices, local(): shares = lax.all_to_all(share, AXES, 0, 0, tiled=True)  15.7 us
    ppermute x8, starting transfers between devices, exchange(): lax.ppermute(data, axis, pairs + [(b, a) for a, b in pairs])  12.3 us
    all_to_all x2, starting transfers between devices, local(): parts = lax.all_to_all(modes, AXES, 0, 0, tiled=True)  9.92 us
    all_to_all x2, starting transfers between devices, local(): shares = lax.all_to_all(share, AXES, 0, 0, tiled=True)  7.46 us
    all_to_all x2, waiting for transfers between devices, local(): parts = lax.all_to_all(modes, AXES, 0, 0, tiled=True)  5.36 us
    ppermute x8, waiting for transfers between devices, exchange(): lax.ppermute(data, axis, pairs + [(b, a) for a, b in pairs])  4.21 us
    pallas_call x1, Pallas kernels, local(): pl.pallas_call(functools.partial(nudged_kernel, n_gy, step, False, count,...  3.33 us
    pallas_call x1, Pallas kernels, local(): pl.pallas_call(functools.partial(first_kernel, n_gy, level_total), out_sh...  2.78 us
  transfers between devices with their start and end apart: 12, of which 8 were waited for; matrix products, arithmetic and copies ran while one was open for 0% of the time, Pallas kernels for 9%

profile of v16, /device:TPU:0, one launch (start us, length us, event | category | flops | bytes accessed | tf_op | source)
XLA Modules:
  0.0 73.2 jit_solution(6362574636189995540)
XLA Ops:
  0.6 0.0 copy-start.2
  0.7 2.8 %first_modes.1 = f32[32,24,128]{2,1,0:T(8,128)} custom-call(s32[8]{0:T(128)} %levels_all.1, s32[2]{0:T(128)} %rest_0_.1, f32[48,32,128]{2,1,0:T(8,128)} %bitcast.2, f32[1,2,24,4096]{3,2,1,0:T(8,128)} %rest_1_.2, bf16[8,384,256]{2,1,0:T(8,128)(2,1)} %constant.10.clone.x_fwd_all.rest_2_, bf16[4,64,384]{2,1,0:T(8,128)(2,1)} %constant.11.clone.y_fwd_all.rest_3_), custom_call_target="tpu_custom_call" | custom-call | tf_op jit(solution)/shard_map/first_modes/pallas_call | solution.py:523
  3.5 0.0 copy-start.3
  3.5 0.0 copy-start.4
  3.5 7.3 %all-to-all-start = ((f32[32,24,128]{2,1,0:T(8,128)}), f32[32,24,128]{2,1,0:T(8,128)S(1)}, u32[]{:S(2)}, u32[]{:S(2)}) async-start(f32[32,24,128]{2,1,0:T(8,128)} %first_modes.1), calls=%async_computation | async-start | bytes 786432 | tf_op jit(solution)/shard_map/all_to_all | solution.py:552
  10.8 0.1 reshape.13.cuts
  10.9 2.4 %edges.1 = (f32[64,128]{1,0:T(8,128)S(1)}, f32[64,128]{1,0:T(8,128)S(1)}, f32[32,128]{1,0:T(8,128)S(1)}, f32[24,128]{1,0:T(8,128)S(1)}, f32[24,32,128]{2,1,0:T(8...) custom-call(s32[24]{0:T(128)S(1)} %reshape.13.cuts, s32[8]{0:T(128)S(1)} %copy-done.6, ...), custom_call_target="tpu_custom_call" | custom-call | tf_op jit(solution)/shard_map/edges/pallas_call | solution.py:534
  13.3 0.7 collective-permute-start.1
  14.0 4.5 %collective-permute-start = (f32[32,128]{1,0:T(8,128)S(1)}, f32[32,128]{1,0:T(8,128)S(1)}, u32[]{:S(2)}, u32[]{:S(2)}) collective-permute-start(f32[32,128]{1,0:T(8,128)S(1)} %get-tuple-element.35), channel_id=1, source_target_pairs={{0,1},{2,3},{1,0},{3,2},{4,5},{6,7},{5,4},{7,6},{8,9},{10,11},{9,8... | collective-permute-start | bytes 49160 | tf_op jit(solution)/shard_map/ppermute | solution.py:473
  18.6 1.7 %collective-permute-done.col_first = f32[32,128]{1,0:T(8,128)S(1)} collective-permute-done((f32[32,128]{1,0:T(8,128)S(1)}, f32[32,128]{1,0:T(8,128)S(1)}, u32[]{:S(2)}, u32[]{:S(2)}) %collective-permute-start) | collective-permute-done | bytes 16416 | tf_op jit(solution)/shard_map/ppermute | solution.py:473
  20.3 2.5 %all-to-all-done.parts = f32[32,24,128]{2,1,0:T(8,128)S(1)} async-done(((f32[32,24,128]{2,1,0:T(8,128)}), f32[32,24,128]{2,1,0:T(8,128)S(1)}, u32[]{:S(2)}, u32[]{:S(2)}) %all-to-all-start) | async-done | bytes 393248 | tf_op jit(solution)/shard_map/all_to_all | solution.py:552
  22.8 1.0 %share_sum.2 = f32[32,16,128]{2,1,0:T(8,128)} custom-call(f32[24,128]{1,0:T(8,128)S(1)} %get-tuple-element.34.weights, f32[32,24,128]{2,1,0:T(8,128)S(1)} %all-to-all-done.parts, bf16[512,256]{1,0:T(8,128)(2,1)S(1)} %copy-done.3, bf16[512,128]{1,0:T(8,128)(2,1)S(1)} %copy-done.4), custom_call_target="tpu_custom_call" | custom-call | tf_op jit(solution)/shard_map/share_sum/pallas_call | solution.py:554
  23.8 3.8 %all-to-all-start.1 = ((f32[32,16,128]{2,1,0:T(8,128)}), f32[32,16,128]{2,1,0:T(8,128)S(1)}, u32[]{:S(2)}, u32[]{:S(2)}) async-start(f32[32,16,128]{2,1,0:T(8,128)} %share_sum.2), calls=%async_computation.1 | async-start | bytes 524288 | tf_op jit(solution)/shard_map/all_to_all | solution.py:565
  27.6 0.3 collective-permute-start.2
  27.9 0.7 collective-permute-start.3
  28.6 0.3 collective-permute-done.2.row_first
  28.9 8.9 %all-to-all-done.1.shares = f32[32,16,128]{2,1,0:T(8,128)S(1)} async-done(((f32[32,16,128]{2,1,0:T(8,128)}), f32[32,16,128]{2,1,0:T(8,128)S(1)}, u32[]{:S(2)}, u32[]{:S(2)}) %all-to-all-start.1) | async-done | bytes 262176 | tf_op jit(solution)/shard_map/all_to_all | solution.py:565
  37.8 3.3 %inner_nudged.1 = (f32[24,32,128]{2,1,0:T(8,128)S(1)}, f32[16,32,128]{2,1,0:T(8,128)S(1)}, f32[32,24,128]{2,1,0:T(8,128)}) custom-call(f32[32,16,128]{2,1,0:T(8,128)S(1)} %all-to-all-done.1.shares, f32[24,32,128]{2,1,0:T(8,128)S(1)} %get-tuple-element.40.fields, f32[64,128]{1,0:T(8,128)S(1)} %collective-permute-done.2.row_first, ...), custom_call_target="tpu_custom_call" | custom-call | tf_op jit(solution)/shard_map/inner_nudged/pallas_call | solution.py:587
  41.2 2.6 %all-to-all-start.2 = ((f32[32,24,128]{2,1,0:T(8,128)}), f32[32,24,128]{2,1,0:T(8,128)S(1)}, u32[]{:S(2)}, u32[]{:S(2)}) async-start(f32[32,24,128]{2,1,0:T(8,128)} %get-tuple-element.47), calls=%async_computation.2 | async-start | bytes 786432 | tf_op jit(solution)/shard_map/all_to_all | solution.py:552
  43.8 2.0 %inner_others.1 = (f32[24,32,128]{2,1,0:T(8,128)S(1)}, f32[16,32,128]{2,1,0:T(8,128)S(1)}, f32[64,128]{1,0:T(8,128)S(1)}, f32[64,128]{1,0:T(8,128)S(1)}, f32[32,128]{1,0:T(8,128)S(1)}) custom-call(f32[24,32,128]{2,1,0:T(8,128)S(1)} %get-tuple-element.48.fields, f32[16,32,128]{2,1,0:T(8,128)} %plume.3, f32[16,32,128]{2,1,0:T(8,128)} %rest_1_.3, ...), custom_call_target="tpu_custom_call" | custom-call | tf_op jit(solution)/shard_map/inner_others/pallas_call | solution.py:598
  45.9 0.7 collective-permute-start.5
  46.5 4.5 %collective-permute-start.4 = (f32[32,128]{1,0:T(8,128)S(1)}, f32[32,128]{1,0:T(8,128)S(1)}, u32[]{:S(2)}, u32[]{:S(2)}) collective-permute-start(f32[32,128]{1,0:T(8,128)S(1)} %get-tuple-element.51), channel_id=1, source_target_pairs={{0,1},{2,3},{1,0},{3,2},{4,5},{6,7},{5,4},{7,6},{8,9},{10,11},{9,8... | collective-permute-start | bytes 49160 | tf_op jit(solution)/shard_map/ppermute | solution.py:473
  51.1 1.9 %collective-permute-done.4.col_first = f32[32,128]{1,0:T(8,128)S(1)} collective-permute-done((f32[32,128]{1,0:T(8,128)S(1)}, f32[32,128]{1,0:T(8,128)S(1)}, u32[]{:S(2)}, u32[]{:S(2)}) %collective-permute-start.4) | collective-permute-done | bytes 16416 | tf_op jit(solution)/shard_map/ppermute | solution.py:473
  52.9 2.8 %all-to-all-done.2.parts = f32[32,24,128]{2,1,0:T(8,128)S(1)} async-done(((f32[32,24,128]{2,1,0:T(8,128)}), f32[32,24,128]{2,1,0:T(8,128)S(1)}, u32[]{:S(2)}, u32[]{:S(2)}) %all-to-all-start.2) | async-done | bytes 393248 | tf_op jit(solution)/shard_map/all_to_all | solution.py:552
  55.8 1.0 %share_sum.3 = f32[32,16,128]{2,1,0:T(8,128)} custom-call(f32[24,128]{1,0:T(8,128)S(1)} %get-tuple-element.34.weights, f32[32,24,128]{2,1,0:T(8,128)S(1)} %all-to-all-done.2.parts, bf16[512,256]{1,0:T(8,128)(2,1)S(1)} %copy-done.3, bf16[512,128]{1,0:T(8,128)(2,1)S(1)} %copy-done.4), custom_call_target="tpu_custom_call" | custom-call | tf_op jit(solution)/shard_map/share_sum/pallas_call | solution.py:554
  56.8 3.7 %all-to-all-start.3 = ((f32[32,16,128]{2,1,0:T(8,128)}), f32[32,16,128]{2,1,0:T(8,128)S(1)}, u32[]{:S(2)}, u32[]{:S(2)}) async-start(f32[32,16,128]{2,1,0:T(8,128)} %share_sum.3), calls=%async_computation.3 | async-start | bytes 524288 | tf_op jit(solution)/shard_map/all_to_all | solution.py:565
  60.5 0.3 collective-permute-start.6
  60.8 0.7 collective-permute-start.7
  61.5 0.3 collective-permute-done.6.row_first
  61.8 2.1 %last_others.1 = (f32[48,32,128]{2,1,0:T(8,128)}, f32[16,32,128]{2,1,0:T(8,128)}) custom-call(f32[24,32,128]{2,1,0:T(8,128)S(1)} %get-tuple-element.61.fields, f32[16,32,128]{2,1,0:T(8,128)S(1)} %get-tuple-element.60.plume.rest_0_, f32[16,32,128]{2,1,0:T(8,128)S(1)} %copy-done.1, f32[64,128]{1,0:T(8,128)S(1)} %collective-permute-done.6.row_first, ...), custom_call_target="tpu_custom_call" | custom-call | tf_op jit(solution)/shard_map/last_others/pallas_call | solution.py:567
  63.9 6.8 %all-to-all-done.3.shares = f32[32,16,128]{2,1,0:T(8,128)S(1)} async-done(((f32[32,16,128]{2,1,0:T(8,128)}), f32[32,16,128]{2,1,0:T(8,128)S(1)}, u32[]{:S(2)}, u32[]{:S(2)}) %all-to-all-start.3) | async-done | bytes 262176 | tf_op jit(solution)/shard_map/all_to_all | solution.py:565
  70.7 2.5 %last_nudged.1 = (f32[48,32,128]{2,1,0:T(8,128)}, f32[16,32,128]{2,1,0:T(8,128)}) custom-call(f32[32,16,128]{2,1,0:T(8,128)S(1)} %all-to-all-done.3.shares, f32[24,32,128]{2,1,0:T(8,128)S(1)} %get-tuple-element.49.rest_0_.fields, f32[64,128]{1,0:T(8,128)S(1)} %collective-permute-done.6.row_first, ...), custom_call_target="tpu_custom_call", output_to_operand_aliasing={{0}: (10, {}), {1}: (11, {})} | custom-call | tf_op jit(solution)/shard_map/last_nudged/pallas_call | solution.py:576
  (17 shorter events, 0.0 us)
Async XLA Ops:
  0.6 10.2 %copy-start.7 = (s32[3,8]{1,0:T(4,128)S(1)}, s32[3,8]{1,0:T(4,128)}, u32[]{:S(2)}) copy-start(s32[3,8]{1,0:T(4,128)} %param.14) | copy-start | bytes 292
  0.6 10.2 %copy-start = (f32[3,16,32,128]{3,2,1,0:T(8,128)S(1)}, f32[3,16,32,128]{3,2,1,0:T(8,128)}, u32[]{:S(2)}) copy-start(f32[3,16,32,128]{3,2,1,0:T(8,128)} %param.12) | copy-start | bytes 2359300
  0.6 10.2 %copy-start.2 = (f32[16,32,128]{2,1,0:T(8,128)S(1)}, f32[16,32,128]{2,1,0:T(8,128)}, u32[]{:S(2)}) copy-start(f32[16,32,128]{2,1,0:T(8,128)} %plume.3) | copy-start | bytes 786436
  0.7 10.2 %copy-start.6 = (s32[8]{0:T(128)S(1)}, s32[8]{0:T(128)}, u32[]{:S(2)}) copy-start(s32[8]{0:T(128)} %levels_all.1) | copy-start | bytes 100
  3.5 19.3 %copy-start.3 = (bf16[512,256]{1,0:T(8,128)(2,1)S(1)}, bf16[512,256]{1,0:T(8,128)(2,1)}, u32[]{:S(2)}) copy-start(bf16[512,256]{1,0:T(8,128)(2,1)} %constant.13.clone.x_back) | copy-start | bytes 786436
  3.5 19.3 %copy-start.4 = (bf16[512,128]{1,0:T(8,128)(2,1)S(1)}, bf16[512,128]{1,0:T(8,128)(2,1)}, u32[]{:S(2)}) copy-start(bf16[512,128]{1,0:T(8,128)(2,1)} %constant.14.clone.x_beside) | copy-start | bytes 393220
  3.5 19.3 %all-to-all-start = ((f32[32,24,128]{2,1,0:T(8,128)}), f32[32,24,128]{2,1,0:T(8,128)S(1)}, u32[]{:S(2)}, u32[]{:S(2)}) async-start(f32[32,24,128]{2,1,0:T(8,128)} %first_modes.1), calls=%async_computation | async-start | bytes 786432 | tf_op jit(solution)/shard_map/all_to_all | solution.py:552
  13.3 24.5 %copy-start.5 = (s32[48]{0:T(128)}, s32[48]{0:T(128)S(1)}, u32[]{:S(2)}) copy-start(s32[48]{0:T(128)S(1)} %get-tuple-element.46.order_all) | copy-start | bytes 580
  13.3 5.2 %collective-permute-start.1 = (f32[32,128]{1,0:T(8,128)S(1)}, f32[32,128]{1,0:T(8,128)S(1)}, u32[]{:S(2)}, u32[]{:S(2)}) collective-permute-start(f32[32,128]{1,0:T(8,128)S(1)} %get-tuple-element.35), channel_id=1, source_target_pairs={{1,2},{2,1},{5,6},{6,5},{9,10},{10,9},{13,14},{14,13},{17,18},{18,... | collective-permute-start | bytes 49160 | tf_op jit(solution)/shard_map/ppermute | solution.py:473
  14.0 6.3 %collective-permute-start = (f32[32,128]{1,0:T(8,128)S(1)}, f32[32,128]{1,0:T(8,128)S(1)}, u32[]{:S(2)}, u32[]{:S(2)}) collective-permute-start(f32[32,128]{1,0:T(8,128)S(1)} %get-tuple-element.35), channel_id=1, source_target_pairs={{0,1},{2,3},{1,0},{3,2},{4,5},{6,7},{5,4},{7,6},{8,9},{10,11},{9,8... | collective-permute-start | bytes 49160 | tf_op jit(solution)/shard_map/ppermute | solution.py:473
  23.8 14.0 %all-to-all-start.1 = ((f32[32,16,128]{2,1,0:T(8,128)}), f32[32,16,128]{2,1,0:T(8,128)S(1)}, u32[]{:S(2)}, u32[]{:S(2)}) async-start(f32[32,16,128]{2,1,0:T(8,128)} %share_sum.2), calls=%async_computation.1 | async-start | bytes 524288 | tf_op jit(solution)/shard_map/all_to_all | solution.py:565
  27.6 1.3 %collective-permute-start.2 = (f32[64,128]{1,0:T(8,128)S(1)}, f32[64,128]{1,0:T(8,128)S(1)}, u32[]{:S(2)}, u32[]{:S(2)}) collective-permute-start(f32[64,128]{1,0:T(8,128)S(1)} %get-tuple-element.41), channel_id=1, source_target_pairs={{0,4},{8,12},{16,20},{24,28},{4,0},{12,8},{20,16},{28,24},{1,5},{9... | collective-permute-start | bytes 98312 | tf_op jit(solution)/shard_map/ppermute | solution.py:473
  27.9 1.0 %collective-permute-start.3 = (f32[64,128]{1,0:T(8,128)S(1)}, f32[64,128]{1,0:T(8,128)S(1)}, u32[]{:S(2)}, u32[]{:S(2)}) collective-permute-start(f32[64,128]{1,0:T(8,128)S(1)} %get-tuple-element.42), channel_id=1, source_target_pairs={{4,8},{12,16},{20,24},{8,4},{16,12},{24,20},{5,9},{13,17},{21,25},... | collective-permute-start | bytes 98312 | tf_op jit(solution)/shard_map/ppermute | solution.py:473
  41.2 14.6 %all-to-all-start.2 = ((f32[32,24,128]{2,1,0:T(8,128)}), f32[32,24,128]{2,1,0:T(8,128)S(1)}, u32[]{:S(2)}, u32[]{:S(2)}) async-start(f32[32,24,128]{2,1,0:T(8,128)} %get-tuple-element.47), calls=%async_computation.2 | async-start | bytes 786432 | tf_op jit(solution)/shard_map/all_to_all | solution.py:552
  43.8 18.0 %copy-start.1 = (f32[16,32,128]{2,1,0:T(8,128)S(1)}, f32[16,32,128]{2,1,0:T(8,128)}, u32[]{:S(2)}) copy-start(f32[16,32,128]{2,1,0:T(8,128)} %rest_1_.3) | copy-start | bytes 786436
  45.9 5.2 %collective-permute-start.5 = (f32[32,128]{1,0:T(8,128)S(1)}, f32[32,128]{1,0:T(8,128)S(1)}, u32[]{:S(2)}, u32[]{:S(2)}) collective-permute-start(f32[32,128]{1,0:T(8,128)S(1)} %get-tuple-element.51), channel_id=1, source_target_pairs={{1,2},{2,1},{5,6},{6,5},{9,10},{10,9},{13,14},{14,13},{17,18},{18,... | collective-permute-start | bytes 49160 | tf_op jit(solution)/shard_map/ppermute | solution.py:473
  46.5 6.4 %collective-permute-start.4 = (f32[32,128]{1,0:T(8,128)S(1)}, f32[32,128]{1,0:T(8,128)S(1)}, u32[]{:S(2)}, u32[]{:S(2)}) collective-permute-start(f32[32,128]{1,0:T(8,128)S(1)} %get-tuple-element.51), channel_id=1, source_target_pairs={{0,1},{2,3},{1,0},{3,2},{4,5},{6,7},{5,4},{7,6},{8,9},{10,11},{9,8... | collective-permute-start | bytes 49160 | tf_op jit(solution)/shard_map/ppermute | solution.py:473
  56.8 13.9 %all-to-all-start.3 = ((f32[32,16,128]{2,1,0:T(8,128)}), f32[32,16,128]{2,1,0:T(8,128)S(1)}, u32[]{:S(2)}, u32[]{:S(2)}) async-start(f32[32,16,128]{2,1,0:T(8,128)} %share_sum.3), calls=%async_computation.3 | async-start | bytes 524288 | tf_op jit(solution)/shard_map/all_to_all | solution.py:565
  60.5 1.3 %collective-permute-start.6 = (f32[64,128]{1,0:T(8,128)S(1)}, f32[64,128]{1,0:T(8,128)S(1)}, u32[]{:S(2)}, u32[]{:S(2)}) collective-permute-start(f32[64,128]{1,0:T(8,128)S(1)} %get-tuple-element.56), channel_id=1, source_target_pairs={{0,4},{8,12},{16,20},{24,28},{4,0},{12,8},{20,16},{28,24},{1,5},{9... | collective-permute-start | bytes 98312 | tf_op jit(solution)/shard_map/ppermute | solution.py:473
  60.8 1.0 %collective-permute-start.7 = (f32[64,128]{1,0:T(8,128)S(1)}, f32[64,128]{1,0:T(8,128)S(1)}, u32[]{:S(2)}, u32[]{:S(2)}) collective-permute-start(f32[64,128]{1,0:T(8,128)S(1)} %get-tuple-element.57), channel_id=1, source_target_pairs={{4,8},{12,16},{20,24},{8,4},{16,12},{24,20},{5,9},{13,17},{21,25},... | collective-permute-start | bytes 98312 | tf_op jit(solution)/shard_map/ppermute | solution.py:473

commit v17 on v16

--- a/solution.py
+++ b/solution.py
@@ -97,7 +97,28 @@
         stacked, table, (((0,), (0,)), ((), ())), preferred_element_type=jnp.float32)
 
 
-def emit_modes(chosen, parent, is_owner, x_fwd, y_fwd, modes, turned, work):
+def halvings(n_gx, n_gy):
+    return [(axis, 1 << b) for axis, count in (("gx", n_gx), ("gy", n_gy))
+            for b in range(count.bit_length() - 1)]
+
+
+def share_places(n_gx, n_gy):
+    places = []
+    for device in range(n_gx * n_gy):
+        index = {"gx": device // n_gy, "gy": device % n_gy}
+        spot = 0
+        for axis, bit in halvings(n_gx, n_gy):
+            spot = 2 * spot + (index[axis] & bit > 0)
+        places.append(spot)
+    return places
+
+
+def bit_of(axis, bit):
+    return lax.rem(lax.axis_index(axis) // bit, 2)
+
+
+def emit_modes(chosen, parent, is_owner, places, split_by, x_fwd, y_fwd, keep, send, modes, turned,
+               work):
     devices, rows = modes.shape[0], modes.shape[1] // 2
     slabs = parent.shape[0]
     groups = slabs // GROUP
@@ -123,8 +144,20 @@
 
     for d in range(devices):
         for p in range(2):
-            modes[d, p * rows : (p + 1) * rows, :] = work[
+            modes[places[d], p * rows : (p + 1) * rows, :] = work[
                 d * rows : (d + 1) * rows, p * LANES : (p + 1) * LANES]
+    count = devices // 2
+    mine = bit_of(*split_by)
+    keep[...] = modes[pl.ds(mine * count, count)]
+    send[...] = modes[pl.ds((1 - mine) * count, count)]
+
+
+def fold_kernel(split_by, kept, received, keep, send):
+    count = keep.shape[0]
+    mine = bit_of(*split_by)
+    for out, start in ((keep, mine * count), (send, (1 - mine) * count)):
+        for i in range(count):
+            out[i] = kept[start + i] + received[start + i]
 
 
 def fetch_all(sems, pairs):
@@ -138,9 +171,9 @@
     return (c // level_count) * level_total + levels[c % level_count]
 
 
-def first_kernel(n_gy, level_total, levels_all, owners_all, fields_all, parent_all, x_fwd_all,
-                 y_fwd_all, modes, levels, owners, fields, sems, parent, x_fwd, y_fwd, turned,
-                 work):
+def first_kernel(n_gy, level_total, places, split_by, levels_all, owners_all, fields_all, parent_all,
+                 x_fwd_all, y_fwd_all, keep, send, levels, owners, fields, sems, parent, x_fwd, y_fwd,
+                 modes, turned, work):
     gx, gy = lax.axis_index("gx"), lax.axis_index("gy")
     copies = fetch_all(sems, [
         (levels_all, levels), (owners_all, owners), (fields_all, fields),
@@ -150,7 +183,8 @@
     level_count = parent.shape[0] // 3
     emit_modes(
         [fields[slab_of(levels, c, level_count, level_total)] for c in range(parent.shape[0])],
-        parent, owners[0] == gx * n_gy + gy, x_fwd[...], y_fwd[...], modes, turned, work,
+        parent, owners[0] == gx * n_gy + gy, places, split_by, x_fwd[...], y_fwd[...], keep, send,
+        modes, turned, work,
     )
 
 
@@ -225,13 +259,9 @@
     return -(-rows // 3)
 
 
-def share_kernel(n_gx, n_gy, weights, parts, x_back, x_beside, out):
-    devices = parts.shape[0]
-    rows = parts.shape[1] // 2
-    total = parts[0]
-    for d in range(1, devices):
-        total = total + parts[d]
-    mismatch = total * weights[...]
+def share_kernel(n_gx, n_gy, weights, kept, received, x_back, x_beside, out):
+    rows = kept.shape[1] // 2
+    mismatch = (kept[0] + received[0]) * weights[...]
     both = jnp.concatenate([mismatch[:rows], mismatch[rows:]], axis=1)
     spare = -rows % 16
     if spare:
@@ -350,7 +380,7 @@
     return updates, update_rows
 
 
-def nudged_kernel(n_gy, step, last, level_count, level_total, shares, fields, row_first, row_second,
+def nudged_kernel(n_gy, step, last, level_count, level_total, places, split_by, shares, fields, row_first, row_second,
                   col_first, col_second, y_back, order_all, *rest):
     gx, gy = lax.axis_index("gx"), lax.axis_index("gy")
     cells_x, cells_y = fields.shape[1:]
@@ -360,9 +390,9 @@
          sems, fields_out, plume_out, out_sems) = rest
         extra = []
     else:
-        (owners_all, parent_all, x_fwd_all, y_fwd_all, fields_out, winds_out, modes,
+        (owners_all, parent_all, x_fwd_all, y_fwd_all, fields_out, winds_out, keep, send,
          order, slabs, spread, spread_edges, west, east, sems,
-         owners, parent, x_fwd, y_fwd, turned, work) = rest
+         owners, parent, x_fwd, y_fwd, modes, turned, work) = rest
         extra = [(owners_all, owners), (x_fwd_all.at[gx], x_fwd), (y_fwd_all.at[gy], y_fwd),
                  (parent_all.at[0, step + 1], parent)]
     copies = fetch_all(sems, [(order_all, order)] + extra)
@@ -409,8 +439,8 @@
         return
     for copy in copies[1:]:
         copy.wait()
-    emit_modes(results, parent, owners[step + 1] == gx * n_gy + gy, x_fwd[...], y_fwd[...], modes,
-               turned, work)
+    emit_modes(results, parent, owners[step + 1] == gx * n_gy + gy, places, split_by, x_fwd[...],
+               y_fwd[...], keep, send, modes, turned, work)
 
 
 def others_kernel(step, last, level_count, fields, plume, source, row_first, row_second, col_first,
@@ -499,7 +529,9 @@
 
     count = levels.shape[0]
     kept = level_total - count
-    mode_shape = f32((devices, 2 * rows, LANES))
+    half_shapes = [f32((devices // 2, 2 * rows, LANES))] * 2
+    steps = halvings(n_gx, n_gy)
+    places = share_places(n_gx, n_gy)
     order_shape = (3 * level_total,)
     edge_shapes = [f32((total, cells_y)), f32((total, cells_y)), f32((cells_x, 2 * total))]
     levels_space = pltpu.SMEM(levels.shape, jnp.int32)
@@ -507,7 +539,7 @@
     order_space = pltpu.SMEM(order_shape, jnp.int32)
     rows_space = vmem(total, cells_y)
     mode_scratch = [vmem(nudged, 4 * KX * KX), table_space(x_fwd),
-                    table_space(y_fwd), vmem(nudged, KX, LANES),
+                    table_space(y_fwd), vmem(devices, 2 * rows, LANES), vmem(nudged, KX, LANES),
                     vmem(devices * rows, 2 * LANES)]
     nudged_scratch = [order_space, vmem(nudged + count, cells_x + 2 * PAD, cells_y),
                       vmem(devices * rows, LANES), vmem(devices * rows, LANES),
@@ -520,11 +552,11 @@
         return [vmem(3 * slabs, cells_x, cells_y), vmem(slabs, cells_x, cells_y),
                 pltpu.SemaphoreType.DMA((4 * slabs,))]
 
-    modes = pl.pallas_call(
-        functools.partial(first_kernel, n_gy, level_total),
-        out_shape=mode_shape,
+    keep, send = pl.pallas_call(
+        functools.partial(first_kernel, n_gy, level_total, places, steps[0]),
+        out_shape=half_shapes,
         in_specs=[HBM] * 6,
-        out_specs=VMEM,
+        out_specs=[VMEM] * 2,
         scratch_shapes=[levels_space, owners_space, vmem(field_rows, cells_x, cells_y),
                         pltpu.SemaphoreType.DMA((6,))] + mode_scratch,
         compiler_params=limit(8),
@@ -548,17 +580,32 @@
     for step in range(STEPS):
         last = step == STEPS - 1
         to_first, to_second, cols = edges
-        col_first, col_second = exchange("gy", cols, cols)
-        parts = lax.all_to_all(modes, AXES, 0, 0, tiled=True)
-        parts, col_first, col_second = lax.optimization_barrier((parts, col_first, col_second))
+        for n, (axis, bit) in enumerate(steps):
+            received = lax.ppermute(
+                send, axis, [(i, i ^ bit) for i in range(lax.axis_size(axis))])
+            if n + 1 < len(steps):
+                half = f32((keep.shape[0] // 2,) + keep.shape[1:])
+                keep, send = pl.pallas_call(
+                    functools.partial(fold_kernel, steps[n + 1]),
+                    out_shape=[half] * 2,
+                    in_specs=[VMEM] * 2,
+                    out_specs=[VMEM] * 2,
+                    compiler_params=limit(4),
+                    name="fold",
+                )(keep, received)
+            if n == 0:
+                send, cols = lax.optimization_barrier((send, cols))
+                col_first, col_second = exchange("gy", cols, cols)
+        received, col_first, col_second = lax.optimization_barrier(
+            (received, col_first, col_second))
         share = pl.pallas_call(
             functools.partial(share_kernel, n_gx, n_gy),
             out_shape=f32((devices, rows + beside_rows(rows), LANES)),
-            in_specs=[VMEM] * 4,
+            in_specs=[VMEM] * 5,
             out_specs=VMEM,
             compiler_params=limit(8),
             name="share_sum",
-        )(weights, parts, x_back, x_beside)
+        )(weights, keep, received, x_back, x_beside)
         share, to_first, to_second = lax.optimization_barrier((share, to_first, to_second))
         row_first, row_second = exchange("gx", to_first, to_second)
         halo = [row_first, row_second, col_first, col_second]
@@ -574,7 +621,7 @@
                 name="last_others",
             )(others, plume, source, *halo, order)
             flat, plume = pl.pallas_call(
-                functools.partial(nudged_kernel, n_gy, step, True, count, level_total),
+                functools.partial(nudged_kernel, n_gy, step, True, count, level_total, None, None),
                 out_shape=[f32((field_rows, cells_x, cells_y)), f32(plume.shape)],
                 in_specs=[VMEM] * 7 + [HBM] + [VMEM] * 2 + [HBM] * 2,
                 out_specs=[HBM] * 2,
@@ -584,12 +631,13 @@
                 name="last_nudged",
             )(shares, flat, *halo, y_back, order, plume, source, *final)
         else:
-            done, winds, modes = pl.pallas_call(
-                functools.partial(nudged_kernel, n_gy, step, False, count, level_total),
-                out_shape=[f32((nudged, cells_x, cells_y)), f32((2 * count, cells_x, cells_y)),
-                           mode_shape],
+            done, winds, keep, send = pl.pallas_call(
+                functools.partial(nudged_kernel, n_gy, step, False, count, level_total, places,
+                                  steps[0]),
+                out_shape=[f32((nudged, cells_x, cells_y)), f32((2 * count, cells_x, cells_y))]
+                + half_shapes,
                 in_specs=[VMEM] * 7 + [HBM] * 5,
-                out_specs=[VMEM] * 3,
+                out_specs=[VMEM] * 4,
                 scratch_shapes=nudged_scratch + [owners_space] + mode_scratch,
                 compiler_params=limit(12),
                 name="inner_nudged",

time: 73.7 us -> 82.6 us (1.12)
  waiting for transfers between devices: 25.3 us -> 37.6 us
  Pallas kernels: 17.3 us -> 15.4 us
  starting transfers between devices: 29.7 us -> 28.2 us
    ppermute x0 -> x10, waiting for transfers between devices: none -> 18.6 us  [local(): lax.ppermute(send, axis, [(i, i ^ bit) for i in range(lax.axis_size(axis))])]
    ppermute x0 -> x10, starting transfers between devices: none -> 11.3 us  [local(): lax.ppermute(send, axis, [(i, i ^ bit) for i in range(lax.axis_size(axis))])]
    all_to_all x2 -> x0, starting transfers between devices: 9.92 us -> none  [local(): parts = lax.all_to_all(modes, AXES, 0, 0, tiled=True)]
    all_to_all x2 -> x0, waiting for transfers between devices: 5.36 us -> none  [local(): parts = lax.all_to_all(modes, AXES, 0, 0, tiled=True)]
    all_to_all x2, starting transfers between devices: 7.46 us -> 5.64 us  [local(): shares = lax.all_to_all(share, AXES, 0, 0, tiled=True)]
    pallas_call x1, Pallas kernels: 3.33 us -> 2.14 us  [local(): pl.pallas_call(functools.partial(nudged_kernel, n_gy, step, False, count,...]
    ppermute x8, starting transfers between devices: 12.3 us -> 11.3 us  [exchange(): lax.ppermute(data, axis, pairs + [(b, a) for a, b in pairs])]
    ppermute x8, waiting for transfers between devices: 4.21 us -> 3.21 us  [exchange(): lax.ppermute(data, axis, pairs + [(b, a) for a, b in pairs])]
  transfers between devices with their start and end apart: 12 -> 20, of which waited for: 8 -> 12; matrix products, arithmetic and copies ran while one was open for 0% -> 0% of each run, Pallas kernels for 9% -> 8%
where the time goes in v17:
time: 82.6 us; the launch traced here: 82.2 us
  waiting for transfers between devices  37.6 us (46%)
  starting transfers between devices  28.2 us (34%)
  Pallas kernels  15.4 us (19%)
  between operations  0.86 us (1%)
    ppermute x10, waiting for transfers between devices, local(): lax.ppermute(send, axis, [(i, i ^ bit) for i in range(lax.axis_size(axis))])  18.6 us
    all_to_all x2, waiting for transfers between devices, local(): shares = lax.all_to_all(share, AXES, 0, 0, tiled=True)  15.7 us
    ppermute x10, starting transfers between devices, local(): lax.ppermute(send, axis, [(i, i ^ bit) for i in range(lax.axis_size(axis))])  11.3 us
    ppermute x8, starting transfers between devices, exchange(): lax.ppermute(data, axis, pairs + [(b, a) for a, b in pairs])  11.3 us
    all_to_all x2, starting transfers between devices, local(): shares = lax.all_to_all(share, AXES, 0, 0, tiled=True)  5.64 us
    ppermute x8, waiting for transfers between devices, exchange(): lax.ppermute(data, axis, pairs + [(b, a) for a, b in pairs])  3.21 us
    pallas_call x1, Pallas kernels, local(): pl.pallas_call(functools.partial(nudged_kernel, n_gy, step, True, count,...  2.5 us
    pallas_call x1, Pallas kernels, local(): pl.pallas_call(functools.partial(edge_kernel, n_gy, period), out_shape=ed...  2.42 us
  transfers between devices with their start and end apart: 20, of which 12 were waited for; matrix products, arithmetic and copies ran while one was open for 0% of the time, Pallas kernels for 8%

profile of v17, /device:TPU:0, one launch (start us, length us, event | category | flops | bytes accessed | tf_op | source)
XLA Modules:
  0.0 82.2 jit_solution(568104478657573199)
XLA Ops:
  0.7 2.1 %first_modes.1 = (f32[16,24,128]{2,1,0:T(8,128)S(1)}, f32[16,24,128]{2,1,0:T(8,128)S(1)}) custom-call(s32[8]{0:T(128)} %levels_all.1, s32[2]{0:T(128)} %rest_0_.1, f32[48,32,128]{2,1,0:T(8,128)} %bitcast.2, f32[1,2,24,4096]{3,2,1,0:T(8,128)} %rest_1_.2, bf16[8,384,256]{2,1,0:T(8,128)(2,1)} %constant.10.clone.x_fwd_all.rest_2_, ...), custom_call_target="tpu_custom_call" | custom-call | tf_op jit(solution)/shard_map/first_modes/pallas_call | solution.py:555
  3.4 2.4 %edges.1 = (f32[64,128]{1,0:T(8,128)S(1)}, f32[64,128]{1,0:T(8,128)S(1)}, f32[32,128]{1,0:T(8,128)S(1)}, f32[24,128]{1,0:T(8,128)S(1)}, f32[24,32,128]{2,1,0:T(8...) custom-call(s32[24]{0:T(128)S(1)} %reshape.13.cuts, s32[8]{0:T(128)S(1)} %copy-done.6, ...), custom_call_target="tpu_custom_call" | custom-call | tf_op jit(solution)/shard_map/edges/pallas_call | solution.py:566
  5.9 2.6 %collective-permute-start.1 = (f32[8,24,128]{2,1,0:T(8,128)S(1)}, f32[8,24,128]{2,1,0:T(8,128)S(1)}, u32[]{:S(2)}, u32[]{:S(2)}) collective-permute-start(f32[8,24,128]{2,1,0:T(8,128)S(1)} %get-tuple-element.63), channel_id=1, source_target_pairs={{0,8},{4,12},{8,0},{12,4},{16,24},{20,28},{24,16},{28,20},{1,9},{5... | collective-permute-start | bytes 294920 | tf_op jit(solution)/shard_map/ppermute | solution.py:584
  8.4 3.4 %collective-permute-done.1.received = f32[8,24,128]{2,1,0:T(8,128)S(1)} collective-permute-done((f32[8,24,128]{2,1,0:T(8,128)S(1)}, f32[8,24,128]{2,1,0:T(8,128)S(1)}, u32[]{:S(2)}, u32[]{:S(2)}) %collective-permute-start.1) | collective-permute-done | bytes 98336 | tf_op jit(solution)/shard_map/ppermute | solution.py:584
  11.9 1.8 %collective-permute-start.2 = (f32[4,24,128]{2,1,0:T(8,128)S(1)}, f32[4,24,128]{2,1,0:T(8,128)S(1)}, u32[]{:S(2)}, u32[]{:S(2)}) collective-permute-start(f32[4,24,128]{2,1,0:T(8,128)S(1)} %get-tuple-element.65), channel_id=1, source_target_pairs={{0,16},{4,20},{8,24},{12,28},{16,0},{20,4},{24,8},{28,12},{1,17},{... | collective-permute-start | bytes 147464 | tf_op jit(solution)/shard_map/ppermute | solution.py:584
  13.7 2.3 %collective-permute-done.2.received = f32[4,24,128]{2,1,0:T(8,128)S(1)} collective-permute-done((f32[4,24,128]{2,1,0:T(8,128)S(1)}, f32[4,24,128]{2,1,0:T(8,128)S(1)}, u32[]{:S(2)}, u32[]{:S(2)}) %collective-permute-start.2) | collective-permute-done | bytes 49184 | tf_op jit(solution)/shard_map/ppermute | solution.py:584
  16.1 1.9 %collective-permute-start.3 = (f32[2,24,128]{2,1,0:T(8,128)S(1)}, f32[2,24,128]{2,1,0:T(8,128)S(1)}, u32[]{:S(2)}, u32[]{:S(2)}) collective-permute-start(f32[2,24,128]{2,1,0:T(8,128)S(1)} %get-tuple-element.67), channel_id=1, source_target_pairs={{0,1},{1,0},{2,3},{3,2},{4,5},{5,4},{6,7},{7,6},{8,9},{9,8},{10,11... | collective-permute-start | bytes 73736 | tf_op jit(solution)/shard_map/ppermute | solution.py:584
  18.0 0.7 collective-permute-start.6
  18.6 4.9 %collective-permute-start.5 = (f32[32,128]{1,0:T(8,128)S(1)}, f32[32,128]{1,0:T(8,128)S(1)}, u32[]{:S(2)}, u32[]{:S(2)}) collective-permute-start(f32[32,128]{1,0:T(8,128)S(1)} %get-tuple-element.70), channel_id=1, source_target_pairs={{0,1},{2,3},{1,0},{3,2},{4,5},{6,7},{5,4},{7,6},{8,9},{10,11},{9,8... | collective-permute-start | bytes 49160 | tf_op jit(solution)/shard_map/ppermute | solution.py:503
  23.6 1.6 %collective-permute-done.5.col_first = f32[32,128]{1,0:T(8,128)S(1)} collective-permute-done((f32[32,128]{1,0:T(8,128)S(1)}, f32[32,128]{1,0:T(8,128)S(1)}, u32[]{:S(2)}, u32[]{:S(2)}) %collective-permute-start.5) | collective-permute-done | bytes 16416 | tf_op jit(solution)/shard_map/ppermute | solution.py:503
  25.3 3.0 %collective-permute-done.4.received = f32[1,24,128]{2,1,0:T(8,128)S(1)} collective-permute-done((f32[1,24,128]{2,1,0:T(8,128)S(1)}, f32[1,24,128]{2,1,0:T(8,128)S(1)}, u32[]{:S(2)}, u32[]{:S(2)}) %collective-permute-start.4) | collective-permute-done | bytes 12320 | tf_op jit(solution)/shard_map/ppermute | solution.py:584
  28.2 1.0 %share_sum.2 = f32[32,16,128]{2,1,0:T(8,128)} custom-call(f32[24,128]{1,0:T(8,128)S(1)} %get-tuple-element.57.weights, f32[1,24,128]{2,1,0:T(8,128)S(1)} %get-tuple-element.68.kept, f32[1,24,128]{2,1,0:T(8,128)S(1)} %collective-permute-done.4.received, bf16[512,256]{1,0:T(8,128)(2,1)S(1)} %copy-done.3, bf16[512,128]{1,0:T(8,128)(2,1)S(1)} %copy-done.4), custom_call_target="tpu_custom_call" | custom-call | tf_op jit(solution)/shard_map/share_sum/pallas_call | solution.py:601
  29.2 2.7 %all-to-all-start = ((f32[32,16,128]{2,1,0:T(8,128)}), f32[32,16,128]{2,1,0:T(8,128)S(1)}, u32[]{:S(2)}, u32[]{:S(2)}) async-start(f32[32,16,128]{2,1,0:T(8,128)} %share_sum.2), calls=%async_computation | async-start | bytes 524288 | tf_op jit(solution)/shard_map/all_to_all | solution.py:612
  32.3 0.7 collective-permute-start.8
  33.2 8.9 %all-to-all-done.shares = f32[32,16,128]{2,1,0:T(8,128)S(1)} async-done(((f32[32,16,128]{2,1,0:T(8,128)}), f32[32,16,128]{2,1,0:T(8,128)S(1)}, u32[]{:S(2)}, u32[]{:S(2)}) %all-to-all-start) | async-done | bytes 262176 | tf_op jit(solution)/shard_map/all_to_all | solution.py:612
  42.2 2.1 %inner_nudged.1 = (f32[24,32,128]{2,1,0:T(8,128)S(1)}, f32[16,32,128]{2,1,0:T(8,128)S(1)}, f32[16,24,128]{2,1,0:T(8,128)S(1)}, f32[16,24,128]{2,1,0:T(8,128)S(1)}) custom-call(f32[32,16,128]{2,1,0:T(8,128)S(1)} %all-to-all-done.shares, f32[24,32,128]{2,1,0:T(8,128)S(1)} %get-tuple-element.75.fields, f32[64,128]{1,0:T(8,128)S(1)} %collective-permute-done.7.row_first, ...), custom_call_target="tpu_custom_call" | custom-call | tf_op jit(solution)/shard_map/inner_nudged/pallas_call | solution.py:634
  44.8 2.0 %inner_others.1 = (f32[24,32,128]{2,1,0:T(8,128)S(1)}, f32[16,32,128]{2,1,0:T(8,128)S(1)}, f32[64,128]{1,0:T(8,128)S(1)}, f32[64,128]{1,0:T(8,128)S(1)}, f32[32,128]{1,0:T(8,128)S(1)}) custom-call(f32[24,32,128]{2,1,0:T(8,128)S(1)} %get-tuple-element.86.fields, f32[16,32,128]{2,1,0:T(8,128)} %plume.3, f32[16,32,128]{2,1,0:T(8,128)} %rest_1_.3, ...), custom_call_target="tpu_custom_call" | custom-call | tf_op jit(solution)/shard_map/inner_others/pallas_call | solution.py:646
  46.9 1.0 %collective-permute-start.10 = (f32[8,24,128]{2,1,0:T(8,128)S(1)}, f32[8,24,128]{2,1,0:T(8,128)S(1)}, u32[]{:S(2)}, u32[]{:S(2)}) collective-permute-start(f32[8,24,128]{2,1,0:T(8,128)S(1)} %get-tuple-element.90), channel_id=1, source_target_pairs={{0,8},{4,12},{8,0},{12,4},{16,24},{20,28},{24,16},{28,20},{1,9},{5... | collective-permute-start | bytes 294920 | tf_op jit(solution)/shard_map/ppermute | solution.py:584
  47.9 3.9 %collective-permute-done.10.received = f32[8,24,128]{2,1,0:T(8,128)S(1)} collective-permute-done((f32[8,24,128]{2,1,0:T(8,128)S(1)}, f32[8,24,128]{2,1,0:T(8,128)S(1)}, u32[]{:S(2)}, u32[]{:S(2)}) %collective-permute-start.10) | collective-permute-done | bytes 98336 | tf_op jit(solution)/shard_map/ppermute | solution.py:584
  51.8 1.1 %collective-permute-start.11 = (f32[4,24,128]{2,1,0:T(8,128)S(1)}, f32[4,24,128]{2,1,0:T(8,128)S(1)}, u32[]{:S(2)}, u32[]{:S(2)}) collective-permute-start(f32[4,24,128]{2,1,0:T(8,128)S(1)} %get-tuple-element.92), channel_id=1, source_target_pairs={{0,16},{4,20},{8,24},{12,28},{16,0},{20,4},{24,8},{28,12},{1,17},{... | collective-permute-start | bytes 147464 | tf_op jit(solution)/shard_map/ppermute | solution.py:584
  52.9 3.0 %collective-permute-done.11.received = f32[4,24,128]{2,1,0:T(8,128)S(1)} collective-permute-done((f32[4,24,128]{2,1,0:T(8,128)S(1)}, f32[4,24,128]{2,1,0:T(8,128)S(1)}, u32[]{:S(2)}, u32[]{:S(2)}) %collective-permute-start.11) | collective-permute-done | bytes 49184 | tf_op jit(solution)/shard_map/ppermute | solution.py:584
  55.9 1.2 %collective-permute-start.12 = (f32[2,24,128]{2,1,0:T(8,128)S(1)}, f32[2,24,128]{2,1,0:T(8,128)S(1)}, u32[]{:S(2)}, u32[]{:S(2)}) collective-permute-start(f32[2,24,128]{2,1,0:T(8,128)S(1)} %get-tuple-element.94), channel_id=1, source_target_pairs={{0,1},{1,0},{2,3},{3,2},{4,5},{5,4},{6,7},{7,6},{8,9},{9,8},{10,11... | collective-permute-start | bytes 73736 | tf_op jit(solution)/shard_map/ppermute | solution.py:584
  57.8 3.1 %collective-permute-start.14 = (f32[32,128]{1,0:T(8,128)S(1)}, f32[32,128]{1,0:T(8,128)S(1)}, u32[]{:S(2)}, u32[]{:S(2)}) collective-permute-start(f32[32,128]{1,0:T(8,128)S(1)} %get-tuple-element.97), channel_id=1, source_target_pairs={{0,1},{2,3},{1,0},{3,2},{4,5},{6,7},{5,4},{7,6},{8,9},{10,11},{9,8... | collective-permute-start | bytes 49160 | tf_op jit(solution)/shard_map/ppermute | solution.py:503
  60.9 0.7 collective-permute-start.13
  61.6 1.0 %collective-permute-done.14.col_first = f32[32,128]{1,0:T(8,128)S(1)} collective-permute-done((f32[32,128]{1,0:T(8,128)S(1)}, f32[32,128]{1,0:T(8,128)S(1)}, u32[]{:S(2)}, u32[]{:S(2)}) %collective-permute-start.14) | collective-permute-done | bytes 16416 | tf_op jit(solution)/shard_map/ppermute | solution.py:503
  62.6 3.0 %collective-permute-done.13.received = f32[1,24,128]{2,1,0:T(8,128)S(1)} collective-permute-done((f32[1,24,128]{2,1,0:T(8,128)S(1)}, f32[1,24,128]{2,1,0:T(8,128)S(1)}, u32[]{:S(2)}, u32[]{:S(2)}) %collective-permute-start.13) | collective-permute-done | bytes 12320 | tf_op jit(solution)/shard_map/ppermute | solution.py:584
  65.5 1.0 %share_sum.3 = f32[32,16,128]{2,1,0:T(8,128)} custom-call(f32[24,128]{1,0:T(8,128)S(1)} %get-tuple-element.57.weights, f32[1,24,128]{2,1,0:T(8,128)S(1)} %get-tuple-element.95.kept, f32[1,24,128]{2,1,0:T(8,128)S(1)} %collective-permute-done.13.received, bf16[512,256]{1,0:T(8,128)(2,1)S(1)} %copy-done.3, bf16[512,128]{1,0:T(8,128)(2,1)S(1)} %copy-done.4), custom_call_target="tpu_custom_call" | custom-call | tf_op jit(solution)/shard_map/share_sum/pallas_call | solution.py:601
  66.6 2.9 %all-to-all-start.1 = ((f32[32,16,128]{2,1,0:T(8,128)}), f32[32,16,128]{2,1,0:T(8,128)S(1)}, u32[]{:S(2)}, u32[]{:S(2)}) async-start(f32[32,16,128]{2,1,0:T(8,128)} %share_sum.3), calls=%async_computation.1 | async-start | bytes 524288 | tf_op jit(solution)/shard_map/all_to_all | solution.py:612
  69.8 0.7 collective-permute-start.17
  70.8 2.1 %last_others.1 = (f32[48,32,128]{2,1,0:T(8,128)}, f32[16,32,128]{2,1,0:T(8,128)}) custom-call(f32[24,32,128]{2,1,0:T(8,128)S(1)} %get-tuple-element.107.fields, f32[16,32,128]{2,1,0:T(8,128)S(1)} %get-tuple-element.106.plume.rest_0_, f32[16,32,128]{2,1,0:T(8,128)S(1)} %copy-done.1, f32[64,128]{1,0:T(8,128)S(1)} %collective-permute-done.16.row_first, ...), custom_call_target="tpu_custom_call" | custom-call | tf_op jit(solution)/shard_map/last_others/pallas_call | solution.py:614
  72.9 6.8 %all-to-all-done.1.shares = f32[32,16,128]{2,1,0:T(8,128)S(1)} async-done(((f32[32,16,128]{2,1,0:T(8,128)}), f32[32,16,128]{2,1,0:T(8,128)S(1)}, u32[]{:S(2)}, u32[]{:S(2)}) %all-to-all-start.1) | async-done | bytes 262176 | tf_op jit(solution)/shard_map/all_to_all | solution.py:612
  79.7 2.5 %last_nudged.1 = (f32[48,32,128]{2,1,0:T(8,128)}, f32[16,32,128]{2,1,0:T(8,128)}) custom-call(f32[32,16,128]{2,1,0:T(8,128)S(1)} %all-to-all-done.1.shares, f32[24,32,128]{2,1,0:T(8,128)S(1)} %get-tuple-element.87.rest_0_.fields, f32[64,128]{1,0:T(8,128)S(1)} %collective-permute-done.16.row_first, ...), custom_call_target="tpu_custom_call", output_to_operand_aliasing={{0}: (10, {}), {1}: (11, {})} | custom-call | tf_op jit(solution)/shard_map/last_nudged/pallas_call | solution.py:623
  (41 shorter events, 3.2 us)
Async XLA Ops:
  0.6 2.7 %copy-start.7 = (s32[3,8]{1,0:T(4,128)S(1)}, s32[3,8]{1,0:T(4,128)}, u32[]{:S(2)}) copy-start(s32[3,8]{1,0:T(4,128)} %param.14) | copy-start | bytes 292
  0.6 2.7 %copy-start = (f32[3,16,32,128]{3,2,1,0:T(8,128)S(1)}, f32[3,16,32,128]{3,2,1,0:T(8,128)}, u32[]{:S(2)}) copy-start(f32[3,16,32,128]{3,2,1,0:T(8,128)} %param.12) | copy-start | bytes 2359300
  0.6 2.7 %copy-start.2 = (f32[16,32,128]{2,1,0:T(8,128)S(1)}, f32[16,32,128]{2,1,0:T(8,128)}, u32[]{:S(2)}) copy-start(f32[16,32,128]{2,1,0:T(8,128)} %plume.3) | copy-start | bytes 786436
  0.7 2.7 %copy-start.6 = (s32[8]{0:T(128)S(1)}, s32[8]{0:T(128)}, u32[]{:S(2)}) copy-start(s32[8]{0:T(128)} %levels_all.1) | copy-start | bytes 100
  2.7 25.5 %copy-start.3 = (bf16[512,256]{1,0:T(8,128)(2,1)S(1)}, bf16[512,256]{1,0:T(8,128)(2,1)}, u32[]{:S(2)}) copy-start(bf16[512,256]{1,0:T(8,128)(2,1)} %constant.13.clone.x_back) | copy-start | bytes 786436
  2.8 25.5 %copy-start.4 = (bf16[512,128]{1,0:T(8,128)(2,1)S(1)}, bf16[512,128]{1,0:T(8,128)(2,1)}, u32[]{:S(2)}) copy-start(bf16[512,128]{1,0:T(8,128)(2,1)} %constant.14.clone.x_beside) | copy-start | bytes 393220
  2.8 3.1 %collective-permute-start = (f32[16,24,128]{2,1,0:T(8,128)S(1)}, f32[16,24,128]{2,1,0:T(8,128)S(1)}, u32[]{:S(2)}, u32[]{:S(2)}) collective-permute-start(f32[16,24,128]{2,1,0:T(8,128)S(1)} %get-tuple-element.59), channel_id=1, source_target_pairs={{0,4},{4,0},{8,12},{12,8},{16,20},{20,16},{24,28},{28,24},{1,5},{5... | collective-permute-start | bytes 589832 | tf_op jit(solution)/shard_map/ppermute | solution.py:584
  5.8 17.7 %copy-start.5 = (s32[48]{0:T(128)}, s32[48]{0:T(128)S(1)}, u32[]{:S(2)}) copy-start(s32[48]{0:T(128)S(1)} %get-tuple-element.81.order_all) | copy-start | bytes 580
  5.9 6.0 %collective-permute-start.1 = (f32[8,24,128]{2,1,0:T(8,128)S(1)}, f32[8,24,128]{2,1,0:T(8,128)S(1)}, u32[]{:S(2)}, u32[]{:S(2)}) collective-permute-start(f32[8,24,128]{2,1,0:T(8,128)S(1)} %get-tuple-element.63), channel_id=1, source_target_pairs={{0,8},{4,12},{8,0},{12,4},{16,24},{20,28},{24,16},{28,20},{1,9},{5... | collective-permute-start | bytes 294920 | tf_op jit(solution)/shard_map/ppermute | solution.py:584
  11.9 4.2 %collective-permute-start.2 = (f32[4,24,128]{2,1,0:T(8,128)S(1)}, f32[4,24,128]{2,1,0:T(8,128)S(1)}, u32[]{:S(2)}, u32[]{:S(2)}) collective-permute-start(f32[4,24,128]{2,1,0:T(8,128)S(1)} %get-tuple-element.65), channel_id=1, source_target_pairs={{0,16},{4,20},{8,24},{12,28},{16,0},{20,4},{24,8},{28,12},{1,17},{... | collective-permute-start | bytes 147464 | tf_op jit(solution)/shard_map/ppermute | solution.py:584
  16.1 7.5 %collective-permute-start.3 = (f32[2,24,128]{2,1,0:T(8,128)S(1)}, f32[2,24,128]{2,1,0:T(8,128)S(1)}, u32[]{:S(2)}, u32[]{:S(2)}) collective-permute-start(f32[2,24,128]{2,1,0:T(8,128)S(1)} %get-tuple-element.67), channel_id=1, source_target_pairs={{0,1},{1,0},{2,3},{3,2},{4,5},{5,4},{6,7},{7,6},{8,9},{9,8},{10,11... | collective-permute-start | bytes 73736 | tf_op jit(solution)/shard_map/ppermute | solution.py:584
  18.0 5.7 %collective-permute-start.6 = (f32[32,128]{1,0:T(8,128)S(1)}, f32[32,128]{1,0:T(8,128)S(1)}, u32[]{:S(2)}, u32[]{:S(2)}) collective-permute-start(f32[32,128]{1,0:T(8,128)S(1)} %get-tuple-element.70), channel_id=1, source_target_pairs={{1,2},{2,1},{5,6},{6,5},{9,10},{10,9},{13,14},{14,13},{17,18},{18,... | collective-permute-start | bytes 49160 | tf_op jit(solution)/shard_map/ppermute | solution.py:503
  18.6 6.6 %collective-permute-start.5 = (f32[32,128]{1,0:T(8,128)S(1)}, f32[32,128]{1,0:T(8,128)S(1)}, u32[]{:S(2)}, u32[]{:S(2)}) collective-permute-start(f32[32,128]{1,0:T(8,128)S(1)} %get-tuple-element.70), channel_id=1, source_target_pairs={{0,1},{2,3},{1,0},{3,2},{4,5},{6,7},{5,4},{7,6},{8,9},{10,11},{9,8... | collective-permute-start | bytes 49160 | tf_op jit(solution)/shard_map/ppermute | solution.py:503
  23.6 4.7 %collective-permute-start.4 = (f32[1,24,128]{2,1,0:T(8,128)S(1)}, f32[1,24,128]{2,1,0:T(8,128)S(1)}, u32[]{:S(2)}, u32[]{:S(2)}) collective-permute-start(f32[1,24,128]{2,1,0:T(8,128)S(1)} %get-tuple-element.69), channel_id=1, source_target_pairs={{0,2},{1,3},{2,0},{3,1},{4,6},{5,7},{6,4},{7,5},{8,10},{9,11},{10,... | collective-permute-start | bytes 36872 | tf_op jit(solution)/shard_map/ppermute | solution.py:584
  29.2 12.9 %all-to-all-start = ((f32[32,16,128]{2,1,0:T(8,128)}), f32[32,16,128]{2,1,0:T(8,128)S(1)}, u32[]{:S(2)}, u32[]{:S(2)}) async-start(f32[32,16,128]{2,1,0:T(8,128)} %share_sum.2), calls=%async_computation | async-start | bytes 524288 | tf_op jit(solution)/shard_map/all_to_all | solution.py:612
  32.0 1.3 %collective-permute-start.7 = (f32[64,128]{1,0:T(8,128)S(1)}, f32[64,128]{1,0:T(8,128)S(1)}, u32[]{:S(2)}, u32[]{:S(2)}) collective-permute-start(f32[64,128]{1,0:T(8,128)S(1)} %get-tuple-element.76), channel_id=1, source_target_pairs={{0,4},{8,12},{16,20},{24,28},{4,0},{12,8},{20,16},{28,24},{1,5},{9... | collective-permute-start | bytes 98312 | tf_op jit(solution)/shard_map/ppermute | solution.py:503
  32.3 1.0 %collective-permute-start.8 = (f32[64,128]{1,0:T(8,128)S(1)}, f32[64,128]{1,0:T(8,128)S(1)}, u32[]{:S(2)}, u32[]{:S(2)}) collective-permute-start(f32[64,128]{1,0:T(8,128)S(1)} %get-tuple-element.77), channel_id=1, source_target_pairs={{4,8},{12,16},{20,24},{8,4},{16,12},{24,20},{5,9},{13,17},{21,25},... | collective-permute-start | bytes 98312 | tf_op jit(solution)/shard_map/ppermute | solution.py:503
  44.3 2.5 %collective-permute-start.9 = (f32[16,24,128]{2,1,0:T(8,128)S(1)}, f32[16,24,128]{2,1,0:T(8,128)S(1)}, u32[]{:S(2)}, u32[]{:S(2)}) collective-permute-start(f32[16,24,128]{2,1,0:T(8,128)S(1)} %get-tuple-element.83), channel_id=1, source_target_pairs={{0,4},{4,0},{8,12},{12,8},{16,20},{20,16},{24,28},{28,24},{1,5},{5... | collective-permute-start | bytes 589832 | tf_op jit(solution)/shard_map/ppermute | solution.py:584
  44.8 26.0 %copy-start.1 = (f32[16,32,128]{2,1,0:T(8,128)S(1)}, f32[16,32,128]{2,1,0:T(8,128)}, u32[]{:S(2)}) copy-start(f32[16,32,128]{2,1,0:T(8,128)} %rest_1_.3) | copy-start | bytes 786436
  46.9 4.9 %collective-permute-start.10 = (f32[8,24,128]{2,1,0:T(8,128)S(1)}, f32[8,24,128]{2,1,0:T(8,128)S(1)}, u32[]{:S(2)}, u32[]{:S(2)}) collective-permute-start(f32[8,24,128]{2,1,0:T(8,128)S(1)} %get-tuple-element.90), channel_id=1, source_target_pairs={{0,8},{4,12},{8,0},{12,4},{16,24},{20,28},{24,16},{28,20},{1,9},{5... | collective-permute-start | bytes 294920 | tf_op jit(solution)/shard_map/ppermute | solution.py:584
  51.8 4.2 %collective-permute-start.11 = (f32[4,24,128]{2,1,0:T(8,128)S(1)}, f32[4,24,128]{2,1,0:T(8,128)S(1)}, u32[]{:S(2)}, u32[]{:S(2)}) collective-permute-start(f32[4,24,128]{2,1,0:T(8,128)S(1)} %get-tuple-element.92), channel_id=1, source_target_pairs={{0,16},{4,20},{8,24},{12,28},{16,0},{20,4},{24,8},{28,12},{1,17},{... | collective-permute-start | bytes 147464 | tf_op jit(solution)/shard_map/ppermute | solution.py:584
  55.9 4.9 %collective-permute-start.12 = (f32[2,24,128]{2,1,0:T(8,128)S(1)}, f32[2,24,128]{2,1,0:T(8,128)S(1)}, u32[]{:S(2)}, u32[]{:S(2)}) collective-permute-start(f32[2,24,128]{2,1,0:T(8,128)S(1)} %get-tuple-element.94), channel_id=1, source_target_pairs={{0,1},{1,0},{2,3},{3,2},{4,5},{5,4},{6,7},{7,6},{8,9},{9,8},{10,11... | collective-permute-start | bytes 73736 | tf_op jit(solution)/shard_map/ppermute | solution.py:584
  57.1 4.5 %collective-permute-start.15 = (f32[32,128]{1,0:T(8,128)S(1)}, f32[32,128]{1,0:T(8,128)S(1)}, u32[]{:S(2)}, u32[]{:S(2)}) collective-permute-start(f32[32,128]{1,0:T(8,128)S(1)} %get-tuple-element.97), channel_id=1, source_target_pairs={{1,2},{2,1},{5,6},{6,5},{9,10},{10,9},{13,14},{14,13},{17,18},{18,... | collective-permute-start | bytes 49160 | tf_op jit(solution)/shard_map/ppermute | solution.py:503
  57.8 4.8 %collective-permute-start.14 = (f32[32,128]{1,0:T(8,128)S(1)}, f32[32,128]{1,0:T(8,128)S(1)}, u32[]{:S(2)}, u32[]{:S(2)}) collective-permute-start(f32[32,128]{1,0:T(8,128)S(1)} %get-tuple-element.97), channel_id=1, source_target_pairs={{0,1},{2,3},{1,0},{3,2},{4,5},{6,7},{5,4},{7,6},{8,9},{10,11},{9,8... | collective-permute-start | bytes 49160 | tf_op jit(solution)/shard_map/ppermute | solution.py:503
  60.9 4.7 %collective-permute-start.13 = (f32[1,24,128]{2,1,0:T(8,128)S(1)}, f32[1,24,128]{2,1,0:T(8,128)S(1)}, u32[]{:S(2)}, u32[]{:S(2)}) collective-permute-start(f32[1,24,128]{2,1,0:T(8,128)S(1)} %get-tuple-element.96), channel_id=1, source_target_pairs={{0,2},{1,3},{2,0},{3,1},{4,6},{5,7},{6,4},{7,5},{8,10},{9,11},{10,... | collective-permute-start | bytes 36872 | tf_op jit(solution)/shard_map/ppermute | solution.py:584
  66.6 13.1 %all-to-all-start.1 = ((f32[32,16,128]{2,1,0:T(8,128)}), f32[32,16,128]{2,1,0:T(8,128)S(1)}, u32[]{:S(2)}, u32[]{:S(2)}) async-start(f32[32,16,128]{2,1,0:T(8,128)} %share_sum.3), calls=%async_computation.1 | async-start | bytes 524288 | tf_op jit(solution)/shard_map/all_to_all | solution.py:612
  69.5 1.3 %collective-permute-start.16 = (f32[64,128]{1,0:T(8,128)S(1)}, f32[64,128]{1,0:T(8,128)S(1)}, u32[]{:S(2)}, u32[]{:S(2)}) collective-permute-start(f32[64,128]{1,0:T(8,128)S(1)} %get-tuple-element.102), channel_id=1, source_target_pairs={{0,4},{8,12},{16,20},{24,28},{4,0},{12,8},{20,16},{28,24},{1,5},{9... | collective-permute-start | bytes 98312 | tf_op jit(solution)/shard_map/ppermute | solution.py:503
  69.8 1.0 %collective-permute-start.17 = (f32[64,128]{1,0:T(8,128)S(1)}, f32[64,128]{1,0:T(8,128)S(1)}, u32[]{:S(2)}, u32[]{:S(2)}) collective-permute-start(f32[64,128]{1,0:T(8,128)S(1)} %get-tuple-element.103), channel_id=1, source_target_pairs={{4,8},{12,16},{20,24},{8,4},{16,12},{24,20},{5,9},{13,17},{21,25},... | collective-permute-start | bytes 98312 | tf_op jit(solution)/shard_map/ppermute | solution.py:503

commit v18 on v16

--- a/solution.py
+++ b/solution.py
@@ -97,7 +97,16 @@
         stacked, table, (((0,), (0,)), ((), ())), preferred_element_type=jnp.float32)
 
 
-def emit_modes(chosen, parent, is_owner, x_fwd, y_fwd, modes, turned, work):
+def core():
+    return lax.rem(lax.axis_index("gx"), 2)
+
+
+def share_places(n_gx, n_gy):
+    return [(d // n_gy % 2 * (n_gx // 2) + d // n_gy // 2) * n_gy + d % n_gy
+            for d in range(n_gx * n_gy)]
+
+
+def emit_modes(chosen, parent, is_owner, places, x_fwd, y_fwd, keep, send, modes, turned, work):
     devices, rows = modes.shape[0], modes.shape[1] // 2
     slabs = parent.shape[0]
     groups = slabs // GROUP
@@ -123,8 +132,16 @@
 
     for d in range(devices):
         for p in range(2):
-            modes[d, p * rows : (p + 1) * rows, :] = work[
+            modes[places[d], p * rows : (p + 1) * rows, :] = work[
                 d * rows : (d + 1) * rows, p * LANES : (p + 1) * LANES]
+    count = devices // 2
+    mine = core()
+    keep[...] = modes[pl.ds(mine * count, count)]
+    send[...] = modes[pl.ds((1 - mine) * count, count)]
+
+
+def add_kernel(kept, received, out):
+    out[...] = kept[...] + received[...]
 
 
 def fetch_all(sems, pairs):
@@ -138,9 +155,9 @@
     return (c // level_count) * level_total + levels[c % level_count]
 
 
-def first_kernel(n_gy, level_total, levels_all, owners_all, fields_all, parent_all, x_fwd_all,
-                 y_fwd_all, modes, levels, owners, fields, sems, parent, x_fwd, y_fwd, turned,
-                 work):
+def first_kernel(n_gy, level_total, places, levels_all, owners_all, fields_all, parent_all,
+                 x_fwd_all, y_fwd_all, keep, send, levels, owners, fields, sems, parent, x_fwd, y_fwd,
+                 modes, turned, work):
     gx, gy = lax.axis_index("gx"), lax.axis_index("gy")
     copies = fetch_all(sems, [
         (levels_all, levels), (owners_all, owners), (fields_all, fields),
@@ -150,7 +167,8 @@
     level_count = parent.shape[0] // 3
     emit_modes(
         [fields[slab_of(levels, c, level_count, level_total)] for c in range(parent.shape[0])],
-        parent, owners[0] == gx * n_gy + gy, x_fwd[...], y_fwd[...], modes, turned, work,
+        parent, owners[0] == gx * n_gy + gy, places, x_fwd[...], y_fwd[...], keep, send,
+        modes, turned, work,
     )
 
 
@@ -226,10 +244,9 @@
 
 
 def share_kernel(n_gx, n_gy, weights, parts, x_back, x_beside, out):
-    devices = parts.shape[0]
     rows = parts.shape[1] // 2
     total = parts[0]
-    for d in range(1, devices):
+    for d in range(1, parts.shape[0]):
         total = total + parts[d]
     mismatch = total * weights[...]
     both = jnp.concatenate([mismatch[:rows], mismatch[rows:]], axis=1)
@@ -350,7 +367,7 @@
     return updates, update_rows
 
 
-def nudged_kernel(n_gy, step, last, level_count, level_total, shares, fields, row_first, row_second,
+def nudged_kernel(n_gy, step, last, level_count, level_total, places, shares, fields, row_first, row_second,
                   col_first, col_second, y_back, order_all, *rest):
     gx, gy = lax.axis_index("gx"), lax.axis_index("gy")
     cells_x, cells_y = fields.shape[1:]
@@ -360,9 +377,9 @@
          sems, fields_out, plume_out, out_sems) = rest
         extra = []
     else:
-        (owners_all, parent_all, x_fwd_all, y_fwd_all, fields_out, winds_out, modes,
+        (owners_all, parent_all, x_fwd_all, y_fwd_all, fields_out, winds_out, keep, send,
          order, slabs, spread, spread_edges, west, east, sems,
-         owners, parent, x_fwd, y_fwd, turned, work) = rest
+         owners, parent, x_fwd, y_fwd, modes, turned, work) = rest
         extra = [(owners_all, owners), (x_fwd_all.at[gx], x_fwd), (y_fwd_all.at[gy], y_fwd),
                  (parent_all.at[0, step + 1], parent)]
     copies = fetch_all(sems, [(order_all, order)] + extra)
@@ -409,8 +426,8 @@
         return
     for copy in copies[1:]:
         copy.wait()
-    emit_modes(results, parent, owners[step + 1] == gx * n_gy + gy, x_fwd[...], y_fwd[...], modes,
-               turned, work)
+    emit_modes(results, parent, owners[step + 1] == gx * n_gy + gy, places, x_fwd[...], y_fwd[...],
+               keep, send, modes, turned, work)
 
 
 def others_kernel(step, last, level_count, fields, plume, source, row_first, row_second, col_first,
@@ -499,7 +516,9 @@
 
     count = levels.shape[0]
     kept = level_total - count
-    mode_shape = f32((devices, 2 * rows, LANES))
+    half_shapes = [f32((devices // 2, 2 * rows, LANES))] * 2
+    places = share_places(n_gx, n_gy)
+    same_core = [[gx * n_gy + gy for gx in range(c, n_gx, 2) for gy in range(n_gy)] for c in range(2)]
     order_shape = (3 * level_total,)
     edge_shapes = [f32((total, cells_y)), f32((total, cells_y)), f32((cells_x, 2 * total))]
     levels_space = pltpu.SMEM(levels.shape, jnp.int32)
@@ -507,7 +526,7 @@
     order_space = pltpu.SMEM(order_shape, jnp.int32)
     rows_space = vmem(total, cells_y)
     mode_scratch = [vmem(nudged, 4 * KX * KX), table_space(x_fwd),
-                    table_space(y_fwd), vmem(nudged, KX, LANES),
+                    table_space(y_fwd), vmem(devices, 2 * rows, LANES), vmem(nudged, KX, LANES),
                     vmem(devices * rows, 2 * LANES)]
     nudged_scratch = [order_space, vmem(nudged + count, cells_x + 2 * PAD, cells_y),
                       vmem(devices * rows, LANES), vmem(devices * rows, LANES),
@@ -520,36 +539,58 @@
         return [vmem(3 * slabs, cells_x, cells_y), vmem(slabs, cells_x, cells_y),
                 pltpu.SemaphoreType.DMA((4 * slabs,))]
 
-    modes = pl.pallas_call(
-        functools.partial(first_kernel, n_gy, level_total),
-        out_shape=mode_shape,
+    keep, send = pl.pallas_call(
+        functools.partial(first_kernel, n_gy, level_total, places),
+        out_shape=half_shapes,
         in_specs=[HBM] * 6,
-        out_specs=VMEM,
+        out_specs=[VMEM] * 2,
         scratch_shapes=[levels_space, owners_space, vmem(field_rows, cells_x, cells_y),
                         pltpu.SemaphoreType.DMA((6,))] + mode_scratch,
         compiler_params=limit(8),
         name="first_modes",
     )(*map(in_hbm, (levels, owners, flat, parent_modes, x_fwd, y_fwd)))
     field_shapes = [f32((3 * count, cells_x, cells_y)), f32((3 * kept, cells_x, cells_y))]
-    *edges, weights, flat_nudged, others, y_back, order = pl.pallas_call(
-        functools.partial(edge_kernel, n_gy, period),
-        out_shape=edge_shapes
-        + [f32((2 * rows, LANES))] + field_shapes
-        + [jax.ShapeDtypeStruct(y_back.shape[1:], y_back.dtype),
-           jax.ShapeDtypeStruct(order_shape, jnp.int32)],
-        in_specs=[SMEM, SMEM, VMEM, VMEM, HBM],
-        out_specs=[VMEM] * 7 + [SMEM],
-        scratch_shapes=[pltpu.SemaphoreType.DMA((1,))],
-        compiler_params=limit(8),
-        name="edges",
-    )(cuts, levels, flat, plume, in_hbm(y_back))
-    order = in_hbm(order)
-    flat = flat_nudged
     for step in range(STEPS):
         last = step == STEPS - 1
+        received = lax.ppermute(send, "gx", [(i, i ^ 1) for i in range(n_gx)])
+        modes = pl.pallas_call(
+            add_kernel,
+            out_shape=half_shapes[0],
+            in_specs=[VMEM] * 2,
+            out_specs=VMEM,
+            compiler_params=limit(4),
+            name="add_cores",
+        )(keep, received)
+        if step == 0:
+            modes, flat = lax.optimization_barrier((modes, flat))
+            *edges, weights, flat_nudged, others, y_back, order = pl.pallas_call(
+                functools.partial(edge_kernel, n_gy, period),
+                out_shape=edge_shapes
+                + [f32((2 * rows, LANES))] + field_shapes
+                + [jax.ShapeDtypeStruct(y_back.shape[1:], y_back.dtype),
+                   jax.ShapeDtypeStruct(order_shape, jnp.int32)],
+                in_specs=[SMEM, SMEM, VMEM, VMEM, HBM],
+                out_specs=[VMEM] * 7 + [SMEM],
+                scratch_shapes=[pltpu.SemaphoreType.DMA((1,))],
+                compiler_params=limit(8),
+                name="edges",
+            )(cuts, levels, flat, plume, in_hbm(y_back))
+            order = in_hbm(order)
+            flat = flat_nudged
+        else:
+            modes, others = lax.optimization_barrier((modes, others))
+            others, plume, *edges = pl.pallas_call(
+                functools.partial(others_kernel, 0, False, count),
+                out_shape=[f32((3 * kept, cells_x, cells_y)), f32(plume.shape)] + edge_shapes,
+                in_specs=[VMEM] + [HBM] * 2 + [VMEM] * 4 + [HBM] + [VMEM] * 2,
+                out_specs=[VMEM] * 5,
+                scratch_shapes=others_scratch + [ash_space, ash_space],
+                compiler_params=limit(8),
+                name="inner_others",
+            )(others, in_hbm(plume), in_hbm(source), *halo, order, flat, winds)
         to_first, to_second, cols = edges
         col_first, col_second = exchange("gy", cols, cols)
-        parts = lax.all_to_all(modes, AXES, 0, 0, tiled=True)
+        parts = lax.all_to_all(modes, AXES, 0, 0, axis_index_groups=same_core, tiled=True)
         parts, col_first, col_second = lax.optimization_barrier((parts, col_first, col_second))
         share = pl.pallas_call(
             functools.partial(share_kernel, n_gx, n_gy),
@@ -574,7 +615,7 @@
                 name="last_others",
             )(others, plume, source, *halo, order)
             flat, plume = pl.pallas_call(
-                functools.partial(nudged_kernel, n_gy, step, True, count, level_total),
+                functools.partial(nudged_kernel, n_gy, step, True, count, level_total, None),
                 out_shape=[f32((field_rows, cells_x, cells_y)), f32(plume.shape)],
                 in_specs=[VMEM] * 7 + [HBM] + [VMEM] * 2 + [HBM] * 2,
                 out_specs=[HBM] * 2,
@@ -584,27 +625,17 @@
                 name="last_nudged",
             )(shares, flat, *halo, y_back, order, plume, source, *final)
         else:
-            done, winds, modes = pl.pallas_call(
-                functools.partial(nudged_kernel, n_gy, step, False, count, level_total),
-                out_shape=[f32((nudged, cells_x, cells_y)), f32((2 * count, cells_x, cells_y)),
-                           mode_shape],
+            flat, winds, keep, send = pl.pallas_call(
+                functools.partial(nudged_kernel, n_gy, step, False, count, level_total, places),
+                out_shape=[f32((nudged, cells_x, cells_y)), f32((2 * count, cells_x, cells_y))]
+                + half_shapes,
                 in_specs=[VMEM] * 7 + [HBM] * 5,
-                out_specs=[VMEM] * 3,
+                out_specs=[VMEM] * 4,
                 scratch_shapes=nudged_scratch + [owners_space] + mode_scratch,
                 compiler_params=limit(12),
                 name="inner_nudged",
             )(shares, flat, *halo, y_back, order,
               *map(in_hbm, (owners, parent_modes, x_fwd, y_fwd)))
-            others, plume, *edges = pl.pallas_call(
-                functools.partial(others_kernel, step, False, count),
-                out_shape=[f32((3 * kept, cells_x, cells_y)), f32(plume.shape)] + edge_shapes,
-                in_specs=[VMEM] + [HBM] * 2 + [VMEM] * 4 + [HBM] + [VMEM] * 2,
-                out_specs=[VMEM] * 5,
-                scratch_shapes=others_scratch + [ash_space, ash_space],
-                compiler_params=limit(8),
-                name="inner_others",
-            )(others, in_hbm(plume), in_hbm(source), *halo, order, done, winds)
-            flat = done
     return flat.reshape(fields.shape), plume
 
 

time: 73.7 us -> 74.1 us (level)
  starting transfers between devices: 29.7 us -> 33.3 us
  waiting for transfers between devices: 25.3 us -> 22.6 us
    all_to_all x2, waiting for transfers between devices: 5.36 us -> 0.68 us  [local(): lax.all_to_all(modes, AXES, 0, 0, axis_index_groups=same_core, tiled=True)]
    ppermute x0 -> x2, waiting for transfers between devices: none -> 2.14 us  [local(): received = lax.ppermute(send, 'gx', [(i, i ^ 1) for i in range(n_gx)])]
    all_to_all x2, starting transfers between devices: 9.92 us -> 11.9 us  [local(): lax.all_to_all(modes, AXES, 0, 0, axis_index_groups=same_core, tiled=True)]
    pallas_call x1, Pallas kernels: 3.33 us -> 2.15 us  [local(): pl.pallas_call(functools.partial(nudged_kernel, n_gy, step, False, count,...]
    ppermute x0 -> x2, starting transfers between devices: none -> 0.98 us  [local(): received = lax.ppermute(send, 'gx', [(i, i ^ 1) for i in range(n_gx)])]
    pallas_call x2 -> x4, Pallas kernels: 4.82 us -> 5.5 us  [the longest x1 2.06 us: local(): pl.pallas_call(functools.partial(first_kernel, n_gy, level_total, places)...]
  transfers between devices with their start and end apart: 12 -> 14, of which waited for: 8 -> 9; matrix products, arithmetic and copies ran while one was open for 0% -> 0% of each run, Pallas kernels for 9% -> 9%
where the time goes in v18:
time: 74.1 us; the launch traced here: 73.5 us
  starting transfers between devices  33.3 us (45%)
  waiting for transfers between devices  22.6 us (30%)
  Pallas kernels  16.7 us (23%)
  between operations  0.82 us (1%)
    all_to_all x2, waiting for transfers between devices, local(): shares = lax.all_to_all(share, AXES, 0, 0, tiled=True)  15.7 us
    ppermute x8, starting transfers between devices, exchange(): lax.ppermute(data, axis, pairs + [(b, a) for a, b in pairs])  12.7 us
    all_to_all x2, starting transfers between devices, local(): lax.all_to_all(modes, AXES, 0, 0, axis_index_groups=same_core, tiled=True)  11.9 us
    all_to_all x2, starting transfers between devices, local(): shares = lax.all_to_all(share, AXES, 0, 0, tiled=True)  7.71 us
    ppermute x8, waiting for transfers between devices, exchange(): lax.ppermute(data, axis, pairs + [(b, a) for a, b in pairs])  4.04 us
    pallas_call x1, Pallas kernels, local(): pl.pallas_call(functools.partial(nudged_kernel, n_gy, step, True, count,...  2.5 us
    pallas_call x1, Pallas kernels, local(): pl.pallas_call(functools.partial(edge_kernel, n_gy, period), out_shape=ed...  2.42 us
    pallas_call x1, Pallas kernels, local(): pl.pallas_call(functools.partial(nudged_kernel, n_gy, step, False, count,...  2.15 us
  transfers between devices with their start and end apart: 14, of which 9 were waited for; matrix products, arithmetic and copies ran while one was open for 0% of the time, Pallas kernels for 9%

profile of v18, /device:TPU:0, one launch (start us, length us, event | category | flops | bytes accessed | tf_op | source)
XLA Modules:
  0.0 73.5 jit_solution(12863019712462720589)
XLA Ops:
  0.7 2.1 %first_modes.1 = (f32[16,24,128]{2,1,0:T(8,128)S(1)}, f32[16,24,128]{2,1,0:T(8,128)S(1)}) custom-call(s32[8]{0:T(128)} %levels.1, s32[2]{0:T(128)} %rest_0_.1, f32[48,32,128]{2,1,0:T(8,128)} %bitcast.2, f32[1,2,24,4096]{3,2,1,0:T(8,128)} %rest_1_.2, bf16[8,384,256]{2,1,0:T(8,128)(2,1)} %constant.10.clone.x_fwd_all.rest_2_, ...), custom_call_target="tpu_custom_call" | custom-call | tf_op jit(solution)/shard_map/first_modes/pallas_call | solution.py:542
  2.8 0.5 collective-permute-start
  3.3 1.1 %collective-permute-done.received = f32[16,24,128]{2,1,0:T(8,128)S(1)} collective-permute-done((f32[16,24,128]{2,1,0:T(8,128)S(1)}, f32[16,24,128]{2,1,0:T(8,128)S(1)}, u32[]{:S(2)}, u32[]{:S(2)}) %collective-permute-start) | collective-permute-done | bytes 196640 | tf_op jit(solution)/shard_map/ppermute | solution.py:555
  4.4 0.7 add_cores.2
  5.0 8.2 %all-to-all-start = ((f32[16,24,128]{2,1,0:T(8,128)}), f32[16,24,128]{2,1,0:T(8,128)S(1)}, u32[]{:S(2)}, u32[]{:S(2)}) async-start(f32[16,24,128]{2,1,0:T(8,128)} %add_cores.2), calls=%async_computation | async-start | bytes 393216 | tf_op jit(solution)/shard_map/all_to_all | solution.py:593
  13.4 2.4 %edges.1 = (f32[64,128]{1,0:T(8,128)S(1)}, f32[64,128]{1,0:T(8,128)S(1)}, f32[32,128]{1,0:T(8,128)S(1)}, f32[24,128]{1,0:T(8,128)S(1)}, f32[24,32,128]{2,1,0:T(8...) custom-call(s32[24]{0:T(128)S(1)} %reshape.13.cuts, s32[8]{0:T(128)S(1)} %copy-done.6, ...), custom_call_target="tpu_custom_call" | custom-call | tf_op jit(solution)/shard_map/edges/pallas_call | solution.py:566
  15.8 0.7 collective-permute-start.2
  16.5 4.7 %collective-permute-start.1 = (f32[32,128]{1,0:T(8,128)S(1)}, f32[32,128]{1,0:T(8,128)S(1)}, u32[]{:S(2)}, u32[]{:S(2)}) collective-permute-start(f32[32,128]{1,0:T(8,128)S(1)} %get-tuple-element.46), channel_id=1, source_target_pairs={{0,1},{2,3},{1,0},{3,2},{4,5},{6,7},{5,4},{7,6},{8,9},{10,11},{9,8... | collective-permute-start | bytes 49160 | tf_op jit(solution)/shard_map/ppermute | solution.py:490
  21.2 1.7 %collective-permute-done.1.col_first = f32[32,128]{1,0:T(8,128)S(1)} collective-permute-done((f32[32,128]{1,0:T(8,128)S(1)}, f32[32,128]{1,0:T(8,128)S(1)}, u32[]{:S(2)}, u32[]{:S(2)}) %collective-permute-start.1) | collective-permute-done | bytes 16416 | tf_op jit(solution)/shard_map/ppermute | solution.py:490
  22.9 1.0 %share_sum.2 = f32[32,16,128]{2,1,0:T(8,128)} custom-call(f32[24,128]{1,0:T(8,128)S(1)} %get-tuple-element.44.weights, f32[16,24,128]{2,1,0:T(8,128)S(1)} %all-to-all-done.parts, bf16[512,256]{1,0:T(8,128)(2,1)S(1)} %copy-done.3, bf16[512,128]{1,0:T(8,128)(2,1)S(1)} %copy-done.4), custom_call_target="tpu_custom_call" | custom-call | tf_op jit(solution)/shard_map/share_sum/pallas_call | solution.py:595
  24.0 4.2 %all-to-all-start.1 = ((f32[32,16,128]{2,1,0:T(8,128)}), f32[32,16,128]{2,1,0:T(8,128)S(1)}, u32[]{:S(2)}, u32[]{:S(2)}) async-start(f32[32,16,128]{2,1,0:T(8,128)} %share_sum.2), calls=%async_computation.1 | async-start | bytes 524288 | tf_op jit(solution)/shard_map/all_to_all | solution.py:606
  28.1 0.3 collective-permute-start.3
  28.5 0.7 collective-permute-start.4
  29.1 0.3 collective-permute-done.3.row_first
  29.4 8.9 %all-to-all-done.1.shares = f32[32,16,128]{2,1,0:T(8,128)S(1)} async-done(((f32[32,16,128]{2,1,0:T(8,128)}), f32[32,16,128]{2,1,0:T(8,128)S(1)}, u32[]{:S(2)}, u32[]{:S(2)}) %all-to-all-start.1) | async-done | bytes 262176 | tf_op jit(solution)/shard_map/all_to_all | solution.py:606
  38.3 2.1 %inner_nudged.1 = (f32[24,32,128]{2,1,0:T(8,128)S(1)}, f32[16,32,128]{2,1,0:T(8,128)S(1)}, f32[16,24,128]{2,1,0:T(8,128)S(1)}, f32[16,24,128]{2,1,0:T(8,128)S(1)}) custom-call(f32[32,16,128]{2,1,0:T(8,128)S(1)} %all-to-all-done.1.shares, f32[24,32,128]{2,1,0:T(8,128)S(1)} %get-tuple-element.51.fields, f32[64,128]{1,0:T(8,128)S(1)} %collective-permute-done.3.row_first, ...), custom_call_target="tpu_custom_call" | custom-call | tf_op jit(solution)/shard_map/inner_nudged/pallas_call | solution.py:628
  40.5 0.5 collective-permute-start.5
  41.0 1.1 %collective-permute-done.5.received = f32[16,24,128]{2,1,0:T(8,128)S(1)} collective-permute-done((f32[16,24,128]{2,1,0:T(8,128)S(1)}, f32[16,24,128]{2,1,0:T(8,128)S(1)}, u32[]{:S(2)}, u32[]{:S(2)}) %collective-permute-start.5) | collective-permute-done | bytes 196640 | tf_op jit(solution)/shard_map/ppermute | solution.py:555
  42.0 0.7 add_cores.3
  42.7 3.7 %all-to-all-start.2 = ((f32[16,24,128]{2,1,0:T(8,128)}), f32[16,24,128]{2,1,0:T(8,128)S(1)}, u32[]{:S(2)}, u32[]{:S(2)}) async-start(f32[16,24,128]{2,1,0:T(8,128)} %add_cores.3), calls=%async_computation.2 | async-start | bytes 393216 | tf_op jit(solution)/shard_map/all_to_all | solution.py:593
  46.5 2.0 %inner_others.1 = (f32[24,32,128]{2,1,0:T(8,128)S(1)}, f32[16,32,128]{2,1,0:T(8,128)S(1)}, f32[64,128]{1,0:T(8,128)S(1)}, f32[64,128]{1,0:T(8,128)S(1)}, f32[32,128]{1,0:T(8,128)S(1)}) custom-call(f32[24,32,128]{2,1,0:T(8,128)S(1)} %get-tuple-element.62.fields, f32[16,32,128]{2,1,0:T(8,128)} %plume.3, f32[16,32,128]{2,1,0:T(8,128)} %rest_1_.3, ...), custom_call_target="tpu_custom_call" | custom-call | tf_op jit(solution)/shard_map/inner_others/pallas_call | solution.py:582
  48.5 0.7 collective-permute-start.7
  49.2 4.7 %collective-permute-start.6 = (f32[32,128]{1,0:T(8,128)S(1)}, f32[32,128]{1,0:T(8,128)S(1)}, u32[]{:S(2)}, u32[]{:S(2)}) collective-permute-start(f32[32,128]{1,0:T(8,128)S(1)} %get-tuple-element.65), channel_id=1, source_target_pairs={{0,1},{2,3},{1,0},{3,2},{4,5},{6,7},{5,4},{7,6},{8,9},{10,11},{9,8... | collective-permute-start | bytes 49160 | tf_op jit(solution)/shard_map/ppermute | solution.py:490
  53.9 1.7 %collective-permute-done.6.col_first = f32[32,128]{1,0:T(8,128)S(1)} collective-permute-done((f32[32,128]{1,0:T(8,128)S(1)}, f32[32,128]{1,0:T(8,128)S(1)}, u32[]{:S(2)}, u32[]{:S(2)}) %collective-permute-start.6) | collective-permute-done | bytes 16416 | tf_op jit(solution)/shard_map/ppermute | solution.py:490
  55.6 0.7 all-to-all-done.2.parts
  56.3 1.0 %share_sum.3 = f32[32,16,128]{2,1,0:T(8,128)} custom-call(f32[24,128]{1,0:T(8,128)S(1)} %get-tuple-element.44.weights, f32[16,24,128]{2,1,0:T(8,128)S(1)} %all-to-all-done.2.parts, bf16[512,256]{1,0:T(8,128)(2,1)S(1)} %copy-done.3, bf16[512,128]{1,0:T(8,128)(2,1)S(1)} %copy-done.4), custom_call_target="tpu_custom_call" | custom-call | tf_op jit(solution)/shard_map/share_sum/pallas_call | solution.py:595
  57.3 3.5 %all-to-all-start.3 = ((f32[32,16,128]{2,1,0:T(8,128)}), f32[32,16,128]{2,1,0:T(8,128)S(1)}, u32[]{:S(2)}, u32[]{:S(2)}) async-start(f32[32,16,128]{2,1,0:T(8,128)} %share_sum.3), calls=%async_computation.3 | async-start | bytes 524288 | tf_op jit(solution)/shard_map/all_to_all | solution.py:606
  60.8 0.3 collective-permute-start.8
  61.1 0.7 collective-permute-start.9
  62.1 2.1 %last_others.1 = (f32[48,32,128]{2,1,0:T(8,128)}, f32[16,32,128]{2,1,0:T(8,128)}) custom-call(f32[24,32,128]{2,1,0:T(8,128)S(1)} %get-tuple-element.75.fields, f32[16,32,128]{2,1,0:T(8,128)S(1)} %get-tuple-element.74.plume.rest_0_, f32[16,32,128]{2,1,0:T(8,128)S(1)} %copy-done.1, f32[64,128]{1,0:T(8,128)S(1)} %collective-permute-done.8.row_first, ...), custom_call_target="tpu_custom_call" | custom-call | tf_op jit(solution)/shard_map/last_others/pallas_call | solution.py:608
  64.2 6.8 %all-to-all-done.3.shares = f32[32,16,128]{2,1,0:T(8,128)S(1)} async-done(((f32[32,16,128]{2,1,0:T(8,128)}), f32[32,16,128]{2,1,0:T(8,128)S(1)}, u32[]{:S(2)}, u32[]{:S(2)}) %all-to-all-start.3) | async-done | bytes 262176 | tf_op jit(solution)/shard_map/all_to_all | solution.py:606
  71.0 2.5 %last_nudged.1 = (f32[48,32,128]{2,1,0:T(8,128)}, f32[16,32,128]{2,1,0:T(8,128)}) custom-call(f32[32,16,128]{2,1,0:T(8,128)S(1)} %all-to-all-done.3.shares, f32[24,32,128]{2,1,0:T(8,128)S(1)} %get-tuple-element.63.rest_0_.fields, f32[64,128]{1,0:T(8,128)S(1)} %collective-permute-done.8.row_first, ...), custom_call_target="tpu_custom_call", output_to_operand_aliasing={{0}: (10, {}), {1}: (11, {})} | custom-call | tf_op jit(solution)/shard_map/last_nudged/pallas_call | solution.py:617
  (23 shorter events, 0.4 us)
Async XLA Ops:
  0.6 12.7 %copy-start.7 = (s32[3,8]{1,0:T(4,128)S(1)}, s32[3,8]{1,0:T(4,128)}, u32[]{:S(2)}) copy-start(s32[3,8]{1,0:T(4,128)} %param.14) | copy-start | bytes 292
  0.6 12.7 %copy-start = (f32[3,16,32,128]{3,2,1,0:T(8,128)S(1)}, f32[3,16,32,128]{3,2,1,0:T(8,128)}, u32[]{:S(2)}) copy-start(f32[3,16,32,128]{3,2,1,0:T(8,128)} %param.12) | copy-start | bytes 2359300
  0.7 12.7 %copy-start.2 = (f32[16,32,128]{2,1,0:T(8,128)S(1)}, f32[16,32,128]{2,1,0:T(8,128)}, u32[]{:S(2)}) copy-start(f32[16,32,128]{2,1,0:T(8,128)} %plume.3) | copy-start | bytes 786436
  0.7 12.7 %copy-start.6 = (s32[8]{0:T(128)S(1)}, s32[8]{0:T(128)}, u32[]{:S(2)}) copy-start(s32[8]{0:T(128)} %levels.1) | copy-start | bytes 100
  2.7 20.2 %copy-start.3 = (bf16[512,256]{1,0:T(8,128)(2,1)S(1)}, bf16[512,256]{1,0:T(8,128)(2,1)}, u32[]{:S(2)}) copy-start(bf16[512,256]{1,0:T(8,128)(2,1)} %constant.13.clone.x_back) | copy-start | bytes 786436
  2.8 20.2 %copy-start.4 = (bf16[512,128]{1,0:T(8,128)(2,1)S(1)}, bf16[512,128]{1,0:T(8,128)(2,1)}, u32[]{:S(2)}) copy-start(bf16[512,128]{1,0:T(8,128)(2,1)} %constant.14.clone.x_beside) | copy-start | bytes 393220
  2.8 1.6 %collective-permute-start = (f32[16,24,128]{2,1,0:T(8,128)S(1)}, f32[16,24,128]{2,1,0:T(8,128)S(1)}, u32[]{:S(2)}, u32[]{:S(2)}) collective-permute-start(f32[16,24,128]{2,1,0:T(8,128)S(1)} %get-tuple-element.42), channel_id=1, source_target_pairs={{0,4},{4,0},{8,12},{12,8},{16,20},{20,16},{24,28},{28,24},{1,5},{5... | collective-permute-start | bytes 589832 | tf_op jit(solution)/shard_map/ppermute | solution.py:555
  5.0 17.9 %all-to-all-start = ((f32[16,24,128]{2,1,0:T(8,128)}), f32[16,24,128]{2,1,0:T(8,128)S(1)}, u32[]{:S(2)}, u32[]{:S(2)}) async-start(f32[16,24,128]{2,1,0:T(8,128)} %add_cores.2), calls=%async_computation | async-start | bytes 393216 | tf_op jit(solution)/shard_map/all_to_all | solution.py:593
  15.8 22.5 %copy-start.5 = (s32[48]{0:T(128)}, s32[48]{0:T(128)S(1)}, u32[]{:S(2)}) copy-start(s32[48]{0:T(128)S(1)} %get-tuple-element.57.order_all) | copy-start | bytes 580
  15.8 5.4 %collective-permute-start.2 = (f32[32,128]{1,0:T(8,128)S(1)}, f32[32,128]{1,0:T(8,128)S(1)}, u32[]{:S(2)}, u32[]{:S(2)}) collective-permute-start(f32[32,128]{1,0:T(8,128)S(1)} %get-tuple-element.46), channel_id=1, source_target_pairs={{1,2},{2,1},{5,6},{6,5},{9,10},{10,9},{13,14},{14,13},{17,18},{18,... | collective-permute-start | bytes 49160 | tf_op jit(solution)/shard_map/ppermute | solution.py:490
  16.5 6.4 %collective-permute-start.1 = (f32[32,128]{1,0:T(8,128)S(1)}, f32[32,128]{1,0:T(8,128)S(1)}, u32[]{:S(2)}, u32[]{:S(2)}) collective-permute-start(f32[32,128]{1,0:T(8,128)S(1)} %get-tuple-element.46), channel_id=1, source_target_pairs={{0,1},{2,3},{1,0},{3,2},{4,5},{6,7},{5,4},{7,6},{8,9},{10,11},{9,8... | collective-permute-start | bytes 49160 | tf_op jit(solution)/shard_map/ppermute | solution.py:490
  24.0 14.4 %all-to-all-start.1 = ((f32[32,16,128]{2,1,0:T(8,128)}), f32[32,16,128]{2,1,0:T(8,128)S(1)}, u32[]{:S(2)}, u32[]{:S(2)}) async-start(f32[32,16,128]{2,1,0:T(8,128)} %share_sum.2), calls=%async_computation.1 | async-start | bytes 524288 | tf_op jit(solution)/shard_map/all_to_all | solution.py:606
  28.1 1.3 %collective-permute-start.3 = (f32[64,128]{1,0:T(8,128)S(1)}, f32[64,128]{1,0:T(8,128)S(1)}, u32[]{:S(2)}, u32[]{:S(2)}) collective-permute-start(f32[64,128]{1,0:T(8,128)S(1)} %get-tuple-element.52), channel_id=1, source_target_pairs={{0,4},{8,12},{16,20},{24,28},{4,0},{12,8},{20,16},{28,24},{1,5},{9... | collective-permute-start | bytes 98312 | tf_op jit(solution)/shard_map/ppermute | solution.py:490
  28.5 1.0 %collective-permute-start.4 = (f32[64,128]{1,0:T(8,128)S(1)}, f32[64,128]{1,0:T(8,128)S(1)}, u32[]{:S(2)}, u32[]{:S(2)}) collective-permute-start(f32[64,128]{1,0:T(8,128)S(1)} %get-tuple-element.53), channel_id=1, source_target_pairs={{4,8},{12,16},{20,24},{8,4},{16,12},{24,20},{5,9},{13,17},{21,25},... | collective-permute-start | bytes 98312 | tf_op jit(solution)/shard_map/ppermute | solution.py:490
  40.5 1.5 %collective-permute-start.5 = (f32[16,24,128]{2,1,0:T(8,128)S(1)}, f32[16,24,128]{2,1,0:T(8,128)S(1)}, u32[]{:S(2)}, u32[]{:S(2)}) collective-permute-start(f32[16,24,128]{2,1,0:T(8,128)S(1)} %get-tuple-element.59), channel_id=1, source_target_pairs={{0,4},{4,0},{8,12},{12,8},{16,20},{20,16},{24,28},{28,24},{1,5},{5... | collective-permute-start | bytes 589832 | tf_op jit(solution)/shard_map/ppermute | solution.py:555
  42.7 13.5 %all-to-all-start.2 = ((f32[16,24,128]{2,1,0:T(8,128)}), f32[16,24,128]{2,1,0:T(8,128)S(1)}, u32[]{:S(2)}, u32[]{:S(2)}) async-start(f32[16,24,128]{2,1,0:T(8,128)} %add_cores.3), calls=%async_computation.2 | async-start | bytes 393216 | tf_op jit(solution)/shard_map/all_to_all | solution.py:593
  46.5 15.7 %copy-start.1 = (f32[16,32,128]{2,1,0:T(8,128)S(1)}, f32[16,32,128]{2,1,0:T(8,128)}, u32[]{:S(2)}) copy-start(f32[16,32,128]{2,1,0:T(8,128)} %rest_1_.3) | copy-start | bytes 786436
  48.5 5.4 %collective-permute-start.7 = (f32[32,128]{1,0:T(8,128)S(1)}, f32[32,128]{1,0:T(8,128)S(1)}, u32[]{:S(2)}, u32[]{:S(2)}) collective-permute-start(f32[32,128]{1,0:T(8,128)S(1)} %get-tuple-element.65), channel_id=1, source_target_pairs={{1,2},{2,1},{5,6},{6,5},{9,10},{10,9},{13,14},{14,13},{17,18},{18,... | collective-permute-start | bytes 49160 | tf_op jit(solution)/shard_map/ppermute | solution.py:490
  49.2 6.4 %collective-permute-start.6 = (f32[32,128]{1,0:T(8,128)S(1)}, f32[32,128]{1,0:T(8,128)S(1)}, u32[]{:S(2)}, u32[]{:S(2)}) collective-permute-start(f32[32,128]{1,0:T(8,128)S(1)} %get-tuple-element.65), channel_id=1, source_target_pairs={{0,1},{2,3},{1,0},{3,2},{4,5},{6,7},{5,4},{7,6},{8,9},{10,11},{9,8... | collective-permute-start | bytes 49160 | tf_op jit(solution)/shard_map/ppermute | solution.py:490
  57.3 13.7 %all-to-all-start.3 = ((f32[32,16,128]{2,1,0:T(8,128)}), f32[32,16,128]{2,1,0:T(8,128)S(1)}, u32[]{:S(2)}, u32[]{:S(2)}) async-start(f32[32,16,128]{2,1,0:T(8,128)} %share_sum.3), calls=%async_computation.3 | async-start | bytes 524288 | tf_op jit(solution)/shard_map/all_to_all | solution.py:606
  60.8 1.3 %collective-permute-start.8 = (f32[64,128]{1,0:T(8,128)S(1)}, f32[64,128]{1,0:T(8,128)S(1)}, u32[]{:S(2)}, u32[]{:S(2)}) collective-permute-start(f32[64,128]{1,0:T(8,128)S(1)} %get-tuple-element.70), channel_id=1, source_target_pairs={{0,4},{8,12},{16,20},{24,28},{4,0},{12,8},{20,16},{28,24},{1,5},{9... | collective-permute-start | bytes 98312 | tf_op jit(solution)/shard_map/ppermute | solution.py:490
  61.1 1.0 %collective-permute-start.9 = (f32[64,128]{1,0:T(8,128)S(1)}, f32[64,128]{1,0:T(8,128)S(1)}, u32[]{:S(2)}, u32[]{:S(2)}) collective-permute-start(f32[64,128]{1,0:T(8,128)S(1)} %get-tuple-element.71), channel_id=1, source_target_pairs={{4,8},{12,16},{20,24},{8,4},{16,12},{24,20},{5,9},{13,17},{21,25},... | collective-permute-start | bytes 98312 | tf_op jit(solution)/shard_map/ppermute | solution.py:490

commit v19 on v18

--- a/solution.py
+++ b/solution.py
@@ -176,10 +176,14 @@
     return lax.rem(lax.axis_index(axis), 2) == 0
 
 
-def edge_kernel(n_gy, period, cuts, levels, fields, plume, y_back_all, first, second, cols, weights,
-                nudged, others, y_back, order, sems):
+def edge_kernel(fields, plume, first, second, cols):
+    slabs = [fields[c] for c in range(fields.shape[0])]
+    emit_edges(slabs + [plume[l] for l in range(plume.shape[0])], first, second, cols)
+
+
+def prepare_kernel(n_gy, period, level_total, cuts, levels, fields, y_back_all, weights, nudged, others,
+                   y_back, order, sems):
     copies = fetch_all(sems, [(y_back_all.at[lax.axis_index("gy")], y_back)])
-    level_total = plume.shape[0]
     weights[...] = share_weights(n_gy, period, cuts, weights.shape)
     count = levels.shape[0]
     for n in range(count):
@@ -197,7 +201,6 @@
     for n in range(level_total):
         order[level_total + chosen[n]] = jnp.int32(n)
     slabs = [fields[f * level_total + l] for f in range(3) for l in chosen]
-    emit_edges(slabs + [plume[l] for l in chosen], first, second, cols)
     kept = level_total - count
     for c, a in enumerate(slabs):
         f, n = c // level_total, c % level_total
@@ -297,7 +300,7 @@
             lane % 2 == 0, pltpu.roll(north, self.last, 1), pltpu.roll(south, 1, 1))
 
     def rows(self, c):
-        return self.west[c : c + 1, :], self.east[c : c + 1, :]
+        return self.west[pl.ds(c, 1), :], self.east[pl.ds(c, 1), :]
 
     def column(self, c):
         return pltpu.roll(self.columns, self.last - 2 * c, 1)
@@ -388,11 +391,12 @@
         shares, spread, spread_edges, y_back[...], nudged, cells_x)
     copies[0].wait()
     level_at = [order[n] for n in range(level_count)]
+    halo_at = level_at if step == 0 else list(range(level_count))
     beside = []
     for k in range(nudged):
         f, n = k // level_count, k % level_count
         a = fields[k]
-        before, after = halo.rows(f * level_total + n)
+        before, after = halo.rows(f * level_total + halo_at[n])
         place(slabs.at[k], a + updates[k][:, :cells_y],
               (before + update_rows[2 * k : 2 * k + 1, :cells_y],
                after + update_rows[2 * k + 1 : 2 * k + 2, :cells_y]))
@@ -405,7 +409,7 @@
         parts = wind_weights(u, v)
         for f in range(3):
             k = f * level_count + n
-            column = halo.column(f * level_total + n) + beside[k]
+            column = halo.column(f * level_total + halo_at[n]) + beside[k]
             results[k] = halo.move(slabs[k], column, parts)
             fields_out[k] = results[k]
         if not last:
@@ -437,12 +441,8 @@
         fields_all, plume_all, order, slab, west, east, sems, fields_out, plume_out, out_sems = rest
     else:
         (done, winds, fields_out, plume_out, first, second, cols, order, slab, west, east,
-         sems, plume_here, source_here) = rest
+         sems) = rest
     copies = fetch_all(sems, [(order_all, order)])
-    if not last:
-        copies += fetch_all(
-            sems.at[pl.ds(1, 2)], [(plume, plume_here), (source, source_here)])
-        plume, source = plume_here, source_here
     halo = Halo(row_first, row_second, col_first, col_second, west, east)
     for copy in copies:
         copy.wait()
@@ -460,13 +460,15 @@
             parts = wind_weights(given[0], given[1])
             for f in range(3):
                 c = f * level_total + n
-                place(slab.at[4 * n + f], given[f], halo.rows(c))
-                results[c] = halo.move(slab[4 * n + f], halo.column(c), parts)
+                beyond = f * level_total + l if step == 0 else c
+                place(slab.at[4 * n + f], given[f], halo.rows(beyond))
+                results[c] = halo.move(slab[4 * n + f], halo.column(beyond), parts)
                 fields_out[f * kept + m] = results[c]
         c = 3 * level_total + n
-        place(slab.at[4 * n + 3], plume[l] if step == 0 else plume[n], halo.rows(c))
+        beyond = 3 * level_total + l if step == 0 else c
+        place(slab.at[4 * n + 3], plume[l] if step == 0 else plume[n], halo.rows(beyond))
         higher = (jnp.minimum(l + 1, level_total - 1) if step == 0 else order[level_total + l + 1])
-        results[c] = (halo.move(slab[4 * n + 3], halo.column(c), settling(parts))
+        results[c] = (halo.move(slab[4 * n + 3], halo.column(beyond), settling(parts))
                       + above(l, level_total) * plume[higher] + source[l])
         plume_out[m if last else n] = results[c]
         if last:
@@ -532,8 +534,7 @@
                       vmem(devices * rows, LANES), vmem(devices * rows, LANES),
                       rows_space, rows_space, pltpu.SemaphoreType.DMA((5,))]
     others_scratch = [order_space, vmem(total, cells_x + 2 * PAD, cells_y), rows_space, rows_space,
-                      pltpu.SemaphoreType.DMA((3,))]
-    ash_space = vmem(level_total, cells_x, cells_y)
+                      pltpu.SemaphoreType.DMA((1,))]
 
     def out_scratch(slabs):
         return [vmem(3 * slabs, cells_x, cells_y), vmem(slabs, cells_x, cells_y),
@@ -549,7 +550,6 @@
         compiler_params=limit(8),
         name="first_modes",
     )(*map(in_hbm, (levels, owners, flat, parent_modes, x_fwd, y_fwd)))
-    field_shapes = [f32((3 * count, cells_x, cells_y)), f32((3 * kept, cells_x, cells_y))]
     for step in range(STEPS):
         last = step == STEPS - 1
         received = lax.ppermute(send, "gx", [(i, i ^ 1) for i in range(n_gx)])
@@ -563,18 +563,26 @@
         )(keep, received)
         if step == 0:
             modes, flat = lax.optimization_barrier((modes, flat))
-            *edges, weights, flat_nudged, others, y_back, order = pl.pallas_call(
-                functools.partial(edge_kernel, n_gy, period),
-                out_shape=edge_shapes
-                + [f32((2 * rows, LANES))] + field_shapes
-                + [jax.ShapeDtypeStruct(y_back.shape[1:], y_back.dtype),
-                   jax.ShapeDtypeStruct(order_shape, jnp.int32)],
-                in_specs=[SMEM, SMEM, VMEM, VMEM, HBM],
-                out_specs=[VMEM] * 7 + [SMEM],
+            edges = pl.pallas_call(
+                edge_kernel,
+                out_shape=edge_shapes,
+                in_specs=[VMEM] * 2,
+                out_specs=[VMEM] * 3,
+                compiler_params=limit(8),
+                name="edges",
+            )(flat, plume)
+            weights, flat_nudged, others, y_back, order = pl.pallas_call(
+                functools.partial(prepare_kernel, n_gy, period, level_total),
+                out_shape=[f32((2 * rows, LANES)), f32((3 * count, cells_x, cells_y)),
+                           f32((3 * kept, cells_x, cells_y)),
+                           jax.ShapeDtypeStruct(y_back.shape[1:], y_back.dtype),
+                           jax.ShapeDtypeStruct(order_shape, jnp.int32)],
+                in_specs=[SMEM, SMEM, VMEM, HBM],
+                out_specs=[VMEM] * 4 + [SMEM],
                 scratch_shapes=[pltpu.SemaphoreType.DMA((1,))],
                 compiler_params=limit(8),
-                name="edges",
-            )(cuts, levels, flat, plume, in_hbm(y_back))
+                name="prepare",
+            )(cuts, levels, flat, in_hbm(y_back))
             order = in_hbm(order)
             flat = flat_nudged
         else:
@@ -582,12 +590,12 @@
             others, plume, *edges = pl.pallas_call(
                 functools.partial(others_kernel, 0, False, count),
                 out_shape=[f32((3 * kept, cells_x, cells_y)), f32(plume.shape)] + edge_shapes,
-                in_specs=[VMEM] + [HBM] * 2 + [VMEM] * 4 + [HBM] + [VMEM] * 2,
+                in_specs=[VMEM] * 7 + [HBM] + [VMEM] * 2,
                 out_specs=[VMEM] * 5,
-                scratch_shapes=others_scratch + [ash_space, ash_space],
+                scratch_shapes=others_scratch,
                 compiler_params=limit(8),
                 name="inner_others",
-            )(others, in_hbm(plume), in_hbm(source), *halo, order, flat, winds)
+            )(others, plume, source, *halo, order, flat, winds)
         to_first, to_second, cols = edges
         col_first, col_second = exchange("gy", cols, cols)
         parts = lax.all_to_all(modes, AXES, 0, 0, axis_index_groups=same_core, tiled=True)

time: 74.1 us -> 72.3 us (0.976)
  starting transfers between devices: 33.3 us -> 30.9 us
    all_to_all x2, waiting for transfers between devices: 0.68 us -> 2.98 us  [local(): lax.all_to_all(modes, AXES, 0, 0, axis_index_groups=same_core, tiled=True)]
    all_to_all x2, starting transfers between devices: 7.71 us -> 5.54 us  [local(): shares = lax.all_to_all(share, AXES, 0, 0, tiled=True)]
    ppermute x8, waiting for transfers between devices: 4.04 us -> 2.46 us  [exchange(): lax.ppermute(data, axis, pairs + [(b, a) for a, b in pairs])]
    pallas_call x1 -> x2, Pallas kernels: 2.42 us -> 2.38 us  [the longest x1 2.05 us: local(): pl.pallas_call(functools.partial(prepare_kernel, n_gy, period, level_tota...]
where the time goes in v19:
time: 72.3 us; the launch traced here: 71.5 us
  starting transfers between devices  30.9 us (43%)
  waiting for transfers between devices  23.3 us (32%)
  Pallas kernels  16.2 us (22%)
  between operations  0.83 us (1%)
    all_to_all x2, waiting for transfers between devices, local(): shares = lax.all_to_all(share, AXES, 0, 0, tiled=True)  15.8 us
    ppermute x8, starting transfers between devices, exchange(): lax.ppermute(data, axis, pairs + [(b, a) for a, b in pairs])  12.5 us
    all_to_all x2, starting transfers between devices, local(): lax.all_to_all(modes, AXES, 0, 0, axis_index_groups=same_core, tiled=True)  11.9 us
    all_to_all x2, starting transfers between devices, local(): shares = lax.all_to_all(share, AXES, 0, 0, tiled=True)  5.54 us
    all_to_all x2, waiting for transfers between devices, local(): lax.all_to_all(modes, AXES, 0, 0, axis_index_groups=same_core, tiled=True)  2.98 us
    pallas_call x1, Pallas kernels, local(): pl.pallas_call(functools.partial(nudged_kernel, n_gy, step, True, count,...  2.5 us
    ppermute x8, waiting for transfers between devices, exchange(): lax.ppermute(data, axis, pairs + [(b, a) for a, b in pairs])  2.46 us
    ppermute x2, waiting for transfers between devices, local(): received = lax.ppermute(send, 'gx', [(i, i ^ 1) for i in range(n_gx)])  2.14 us
  transfers between devices with their start and end apart: 14, of which 9 were waited for; matrix products, arithmetic and copies ran while one was open for 0% of the time, Pallas kernels for 9%

profile of v19, /device:TPU:0, one launch (start us, length us, event | category | flops | bytes accessed | tf_op | source)
XLA Modules:
  0.0 71.5 jit_solution(4123603779867011901)
XLA Ops:
  0.6 2.1 %first_modes.1 = (f32[16,24,128]{2,1,0:T(8,128)S(1)}, f32[16,24,128]{2,1,0:T(8,128)S(1)}) custom-call(s32[8]{0:T(128)} %levels.1, s32[2]{0:T(128)} %rest_0_.1, f32[48,32,128]{2,1,0:T(8,128)} %bitcast.2, f32[1,2,24,4096]{3,2,1,0:T(8,128)} %rest_1_.2, bf16[8,384,256]{2,1,0:T(8,128)(2,1)} %constant.10.clone.x_fwd_all.rest_2_, ...), custom_call_target="tpu_custom_call" | custom-call | tf_op jit(solution)/shard_map/first_modes/pallas_call | solution.py:543
  2.7 0.5 collective-permute-start
  3.3 1.1 %collective-permute-done.received = f32[16,24,128]{2,1,0:T(8,128)S(1)} collective-permute-done((f32[16,24,128]{2,1,0:T(8,128)S(1)}, f32[16,24,128]{2,1,0:T(8,128)S(1)}, u32[]{:S(2)}, u32[]{:S(2)}) %collective-permute-start) | collective-permute-done | bytes 196640 | tf_op jit(solution)/shard_map/ppermute | solution.py:555
  4.3 0.7 add_cores.2
  5.0 8.2 %all-to-all-start = ((f32[16,24,128]{2,1,0:T(8,128)}), f32[16,24,128]{2,1,0:T(8,128)S(1)}, u32[]{:S(2)}, u32[]{:S(2)}) async-start(f32[16,24,128]{2,1,0:T(8,128)} %add_cores.2), calls=%async_computation | async-start | bytes 393216 | tf_op jit(solution)/shard_map/all_to_all | solution.py:601
  13.3 0.3 edges.1
  13.6 0.7 collective-permute-start.2
  14.3 4.7 %collective-permute-start.1 = (f32[32,128]{1,0:T(8,128)S(1)}, f32[32,128]{1,0:T(8,128)S(1)}, u32[]{:S(2)}, u32[]{:S(2)}) collective-permute-start(f32[32,128]{1,0:T(8,128)S(1)} %get-tuple-element.46), channel_id=1, source_target_pairs={{0,1},{2,3},{1,0},{3,2},{4,5},{6,7},{5,4},{7,6},{8,9},{10,11},{9,8... | collective-permute-start | bytes 49160 | tf_op jit(solution)/shard_map/ppermute | solution.py:492
  19.1 2.0 %prepare.1 = (f32[24,128]{1,0:T(8,128)S(1)}, f32[24,32,128]{2,1,0:T(8,128)S(1)}, f32[24,32,128]{2,1,0:T(8,128)S(1)}, bf16[192,256]{1,0:T(8,128)(2,1)S(1)}, s32[48]{0:T(128)S(1)}) custom-call(s32[24]{0:T(128)S(1)} %reshape.13.cuts, s32[8]{0:T(128)S(1)} %copy-done.6, f32[48,32,128]{2,1,0:T(8,128)S(1)} %bitcast.4, bf16[4,192,256]{2,1,0:T(8,128)(2,1)} %constant.12.clone.y_back_all), custom_call_target="tpu_custom_call" | custom-call | tf_op jit(solution)/shard_map/prepare/pallas_call | solution.py:574
  21.2 1.7 %all-to-all-done.parts = f32[16,24,128]{2,1,0:T(8,128)S(1)} async-done(((f32[16,24,128]{2,1,0:T(8,128)}), f32[16,24,128]{2,1,0:T(8,128)S(1)}, u32[]{:S(2)}, u32[]{:S(2)}) %all-to-all-start) | async-done | bytes 196640 | tf_op jit(solution)/shard_map/all_to_all | solution.py:601
  22.9 1.0 %share_sum.2 = f32[32,16,128]{2,1,0:T(8,128)} custom-call(f32[24,128]{1,0:T(8,128)S(1)} %get-tuple-element.44.weights, f32[16,24,128]{2,1,0:T(8,128)S(1)} %all-to-all-done.parts, bf16[512,256]{1,0:T(8,128)(2,1)S(1)} %copy-done.2, bf16[512,128]{1,0:T(8,128)(2,1)S(1)} %copy-done.4), custom_call_target="tpu_custom_call" | custom-call | tf_op jit(solution)/shard_map/share_sum/pallas_call | solution.py:603
  23.9 2.6 %all-to-all-start.1 = ((f32[32,16,128]{2,1,0:T(8,128)}), f32[32,16,128]{2,1,0:T(8,128)S(1)}, u32[]{:S(2)}, u32[]{:S(2)}) async-start(f32[32,16,128]{2,1,0:T(8,128)} %share_sum.2), calls=%async_computation.1 | async-start | bytes 524288 | tf_op jit(solution)/shard_map/all_to_all | solution.py:614
  26.7 0.7 collective-permute-start.4
  27.4 0.4 collective-permute-done.3.row_first
  27.8 8.9 %all-to-all-done.1.shares = f32[32,16,128]{2,1,0:T(8,128)S(1)} async-done(((f32[32,16,128]{2,1,0:T(8,128)}), f32[32,16,128]{2,1,0:T(8,128)S(1)}, u32[]{:S(2)}, u32[]{:S(2)}) %all-to-all-start.1) | async-done | bytes 262176 | tf_op jit(solution)/shard_map/all_to_all | solution.py:614
  36.7 2.1 %inner_nudged.1 = (f32[24,32,128]{2,1,0:T(8,128)S(1)}, f32[16,32,128]{2,1,0:T(8,128)S(1)}, f32[16,24,128]{2,1,0:T(8,128)S(1)}, f32[16,24,128]{2,1,0:T(8,128)S(1)}) custom-call(f32[32,16,128]{2,1,0:T(8,128)S(1)} %all-to-all-done.1.shares, f32[24,32,128]{2,1,0:T(8,128)S(1)} %get-tuple-element.51.fields, f32[64,128]{1,0:T(8,128)S(1)} %collective-permute-done.3.row_first, ...), custom_call_target="tpu_custom_call" | custom-call | tf_op jit(solution)/shard_map/inner_nudged/pallas_call | solution.py:636
  38.9 0.5 collective-permute-start.5
  39.3 1.1 %collective-permute-done.5.received = f32[16,24,128]{2,1,0:T(8,128)S(1)} collective-permute-done((f32[16,24,128]{2,1,0:T(8,128)S(1)}, f32[16,24,128]{2,1,0:T(8,128)S(1)}, u32[]{:S(2)}, u32[]{:S(2)}) %collective-permute-start.5) | collective-permute-done | bytes 196640 | tf_op jit(solution)/shard_map/ppermute | solution.py:555
  40.4 0.7 add_cores.3
  41.1 3.7 %all-to-all-start.2 = ((f32[16,24,128]{2,1,0:T(8,128)}), f32[16,24,128]{2,1,0:T(8,128)S(1)}, u32[]{:S(2)}, u32[]{:S(2)}) async-start(f32[16,24,128]{2,1,0:T(8,128)} %add_cores.3), calls=%async_computation.2 | async-start | bytes 393216 | tf_op jit(solution)/shard_map/all_to_all | solution.py:601
  44.8 1.6 %inner_others.1 = (f32[24,32,128]{2,1,0:T(8,128)S(1)}, f32[16,32,128]{2,1,0:T(8,128)S(1)}, f32[64,128]{1,0:T(8,128)S(1)}, f32[64,128]{1,0:T(8,128)S(1)}, f32[32,128]{1,0:T(8,128)S(1)}) custom-call(f32[24,32,128]{2,1,0:T(8,128)S(1)} %get-tuple-element.62.fields, f32[16,32,128]{2,1,0:T(8,128)S(1)} %copy-done.3, f32[16,32,128]{2,1,0:T(8,128)S(1)} %copy-done.1, ...), custom_call_target="tpu_custom_call" | custom-call | tf_op jit(solution)/shard_map/inner_others/pallas_call | solution.py:590
  46.5 0.7 collective-permute-start.7
  47.1 4.7 %collective-permute-start.6 = (f32[32,128]{1,0:T(8,128)S(1)}, f32[32,128]{1,0:T(8,128)S(1)}, u32[]{:S(2)}, u32[]{:S(2)}) collective-permute-start(f32[32,128]{1,0:T(8,128)S(1)} %get-tuple-element.65), channel_id=1, source_target_pairs={{0,1},{2,3},{1,0},{3,2},{4,5},{6,7},{5,4},{7,6},{8,9},{10,11},{9,8... | collective-permute-start | bytes 49160 | tf_op jit(solution)/shard_map/ppermute | solution.py:492
  51.8 1.7 %collective-permute-done.6.col_first = f32[32,128]{1,0:T(8,128)S(1)} collective-permute-done((f32[32,128]{1,0:T(8,128)S(1)}, f32[32,128]{1,0:T(8,128)S(1)}, u32[]{:S(2)}, u32[]{:S(2)}) %collective-permute-start.6) | collective-permute-done | bytes 16416 | tf_op jit(solution)/shard_map/ppermute | solution.py:492
  53.5 1.2 %all-to-all-done.2.parts = f32[16,24,128]{2,1,0:T(8,128)S(1)} async-done(((f32[16,24,128]{2,1,0:T(8,128)}), f32[16,24,128]{2,1,0:T(8,128)S(1)}, u32[]{:S(2)}, u32[]{:S(2)}) %all-to-all-start.2) | async-done | bytes 196640 | tf_op jit(solution)/shard_map/all_to_all | solution.py:601
  54.8 1.0 %share_sum.3 = f32[32,16,128]{2,1,0:T(8,128)} custom-call(f32[24,128]{1,0:T(8,128)S(1)} %get-tuple-element.44.weights, f32[16,24,128]{2,1,0:T(8,128)S(1)} %all-to-all-done.2.parts, bf16[512,256]{1,0:T(8,128)(2,1)S(1)} %copy-done.2, bf16[512,128]{1,0:T(8,128)(2,1)S(1)} %copy-done.4), custom_call_target="tpu_custom_call" | custom-call | tf_op jit(solution)/shard_map/share_sum/pallas_call | solution.py:603
  55.8 3.0 %all-to-all-start.3 = ((f32[32,16,128]{2,1,0:T(8,128)}), f32[32,16,128]{2,1,0:T(8,128)S(1)}, u32[]{:S(2)}, u32[]{:S(2)}) async-start(f32[32,16,128]{2,1,0:T(8,128)} %share_sum.3), calls=%async_computation.3 | async-start | bytes 524288 | tf_op jit(solution)/shard_map/all_to_all | solution.py:614
  58.7 0.3 collective-permute-start.8
  59.1 0.7 collective-permute-start.9
  60.0 2.1 %last_others.1 = (f32[48,32,128]{2,1,0:T(8,128)}, f32[16,32,128]{2,1,0:T(8,128)}) custom-call(f32[24,32,128]{2,1,0:T(8,128)S(1)} %get-tuple-element.75.fields, f32[16,32,128]{2,1,0:T(8,128)S(1)} %get-tuple-element.74.plume.rest_0_, f32[16,32,128]{2,1,0:T(8,128)S(1)} %copy-done.1, f32[64,128]{1,0:T(8,128)S(1)} %collective-permute-done.8.row_first, ...), custom_call_target="tpu_custom_call" | custom-call | tf_op jit(solution)/shard_map/last_others/pallas_call | solution.py:616
  62.1 6.8 %all-to-all-done.3.shares = f32[32,16,128]{2,1,0:T(8,128)S(1)} async-done(((f32[32,16,128]{2,1,0:T(8,128)}), f32[32,16,128]{2,1,0:T(8,128)S(1)}, u32[]{:S(2)}, u32[]{:S(2)}) %all-to-all-start.3) | async-done | bytes 262176 | tf_op jit(solution)/shard_map/all_to_all | solution.py:614
  68.9 2.5 %last_nudged.1 = (f32[48,32,128]{2,1,0:T(8,128)}, f32[16,32,128]{2,1,0:T(8,128)}) custom-call(f32[32,16,128]{2,1,0:T(8,128)S(1)} %all-to-all-done.3.shares, f32[24,32,128]{2,1,0:T(8,128)S(1)} %get-tuple-element.63.rest_0_.fields, f32[64,128]{1,0:T(8,128)S(1)} %collective-permute-done.8.row_first, ...), custom_call_target="tpu_custom_call", output_to_operand_aliasing={{0}: (10, {}), {1}: (11, {})} | custom-call | tf_op jit(solution)/shard_map/last_nudged/pallas_call | solution.py:625
  (24 shorter events, 0.6 us)
Async XLA Ops:
  0.6 12.6 %copy-start = (f32[3,16,32,128]{3,2,1,0:T(8,128)S(1)}, f32[3,16,32,128]{3,2,1,0:T(8,128)}, u32[]{:S(2)}) copy-start(f32[3,16,32,128]{3,2,1,0:T(8,128)} %param.12) | copy-start | bytes 2359300
  0.6 12.6 %copy-start.3 = (f32[16,32,128]{2,1,0:T(8,128)S(1)}, f32[16,32,128]{2,1,0:T(8,128)}, u32[]{:S(2)}) copy-start(f32[16,32,128]{2,1,0:T(8,128)} %plume.3) | copy-start | bytes 786436
  2.7 16.3 %copy-start.7 = (s32[3,8]{1,0:T(4,128)S(1)}, s32[3,8]{1,0:T(4,128)}, u32[]{:S(2)}) copy-start(s32[3,8]{1,0:T(4,128)} %param.14) | copy-start | bytes 292
  2.7 16.4 %copy-start.6 = (s32[8]{0:T(128)S(1)}, s32[8]{0:T(128)}, u32[]{:S(2)}) copy-start(s32[8]{0:T(128)} %levels.1) | copy-start | bytes 100
  2.7 1.6 %collective-permute-start = (f32[16,24,128]{2,1,0:T(8,128)S(1)}, f32[16,24,128]{2,1,0:T(8,128)S(1)}, u32[]{:S(2)}, u32[]{:S(2)}) collective-permute-start(f32[16,24,128]{2,1,0:T(8,128)S(1)} %get-tuple-element.42), channel_id=1, source_target_pairs={{0,4},{4,0},{8,12},{12,8},{16,20},{20,16},{24,28},{28,24},{1,5},{5... | collective-permute-start | bytes 589832 | tf_op jit(solution)/shard_map/ppermute | solution.py:555
  4.3 18.6 %copy-start.2 = (bf16[512,256]{1,0:T(8,128)(2,1)S(1)}, bf16[512,256]{1,0:T(8,128)(2,1)}, u32[]{:S(2)}) copy-start(bf16[512,256]{1,0:T(8,128)(2,1)} %constant.13.clone.x_back) | copy-start | bytes 786436
  4.3 18.6 %copy-start.4 = (bf16[512,128]{1,0:T(8,128)(2,1)S(1)}, bf16[512,128]{1,0:T(8,128)(2,1)}, u32[]{:S(2)}) copy-start(bf16[512,128]{1,0:T(8,128)(2,1)} %constant.14.clone.x_beside) | copy-start | bytes 393220
  5.0 17.9 %all-to-all-start = ((f32[16,24,128]{2,1,0:T(8,128)}), f32[16,24,128]{2,1,0:T(8,128)S(1)}, u32[]{:S(2)}, u32[]{:S(2)}) async-start(f32[16,24,128]{2,1,0:T(8,128)} %add_cores.2), calls=%async_computation | async-start | bytes 393216 | tf_op jit(solution)/shard_map/all_to_all | solution.py:601
  13.6 7.5 %collective-permute-start.2 = (f32[32,128]{1,0:T(8,128)S(1)}, f32[32,128]{1,0:T(8,128)S(1)}, u32[]{:S(2)}, u32[]{:S(2)}) collective-permute-start(f32[32,128]{1,0:T(8,128)S(1)} %get-tuple-element.46), channel_id=1, source_target_pairs={{1,2},{2,1},{5,6},{6,5},{9,10},{10,9},{13,14},{14,13},{17,18},{18,... | collective-permute-start | bytes 49160 | tf_op jit(solution)/shard_map/ppermute | solution.py:492
  14.3 6.9 %collective-permute-start.1 = (f32[32,128]{1,0:T(8,128)S(1)}, f32[32,128]{1,0:T(8,128)S(1)}, u32[]{:S(2)}, u32[]{:S(2)}) collective-permute-start(f32[32,128]{1,0:T(8,128)S(1)} %get-tuple-element.46), channel_id=1, source_target_pairs={{0,1},{2,3},{1,0},{3,2},{4,5},{6,7},{5,4},{7,6},{8,9},{10,11},{9,8... | collective-permute-start | bytes 49160 | tf_op jit(solution)/shard_map/ppermute | solution.py:492
  21.1 2.8 %copy-start.5 = (s32[48]{0:T(128)}, s32[48]{0:T(128)S(1)}, u32[]{:S(2)}) copy-start(s32[48]{0:T(128)S(1)} %get-tuple-element.57.order_all) | copy-start | bytes 580
  23.9 12.8 %all-to-all-start.1 = ((f32[32,16,128]{2,1,0:T(8,128)}), f32[32,16,128]{2,1,0:T(8,128)S(1)}, u32[]{:S(2)}, u32[]{:S(2)}) async-start(f32[32,16,128]{2,1,0:T(8,128)} %share_sum.2), calls=%async_computation.1 | async-start | bytes 524288 | tf_op jit(solution)/shard_map/all_to_all | solution.py:614
  26.5 1.3 %collective-permute-start.3 = (f32[64,128]{1,0:T(8,128)S(1)}, f32[64,128]{1,0:T(8,128)S(1)}, u32[]{:S(2)}, u32[]{:S(2)}) collective-permute-start(f32[64,128]{1,0:T(8,128)S(1)} %get-tuple-element.52), channel_id=1, source_target_pairs={{0,4},{8,12},{16,20},{24,28},{4,0},{12,8},{20,16},{28,24},{1,5},{9... | collective-permute-start | bytes 98312 | tf_op jit(solution)/shard_map/ppermute | solution.py:492
  26.7 1.1 %collective-permute-start.4 = (f32[64,128]{1,0:T(8,128)S(1)}, f32[64,128]{1,0:T(8,128)S(1)}, u32[]{:S(2)}, u32[]{:S(2)}) collective-permute-start(f32[64,128]{1,0:T(8,128)S(1)} %get-tuple-element.53), channel_id=1, source_target_pairs={{4,8},{12,16},{20,24},{8,4},{16,12},{24,20},{5,9},{13,17},{21,25},... | collective-permute-start | bytes 98312 | tf_op jit(solution)/shard_map/ppermute | solution.py:492
  36.7 8.1 %copy-start.1 = (f32[16,32,128]{2,1,0:T(8,128)S(1)}, f32[16,32,128]{2,1,0:T(8,128)}, u32[]{:S(2)}) copy-start(f32[16,32,128]{2,1,0:T(8,128)} %rest_1_.3) | copy-start | bytes 786436
  38.9 1.5 %collective-permute-start.5 = (f32[16,24,128]{2,1,0:T(8,128)S(1)}, f32[16,24,128]{2,1,0:T(8,128)S(1)}, u32[]{:S(2)}, u32[]{:S(2)}) collective-permute-start(f32[16,24,128]{2,1,0:T(8,128)S(1)} %get-tuple-element.59), channel_id=1, source_target_pairs={{0,4},{4,0},{8,12},{12,8},{16,20},{20,16},{24,28},{28,24},{1,5},{5... | collective-permute-start | bytes 589832 | tf_op jit(solution)/shard_map/ppermute | solution.py:555
  41.1 13.7 %all-to-all-start.2 = ((f32[16,24,128]{2,1,0:T(8,128)}), f32[16,24,128]{2,1,0:T(8,128)S(1)}, u32[]{:S(2)}, u32[]{:S(2)}) async-start(f32[16,24,128]{2,1,0:T(8,128)} %add_cores.3), calls=%async_computation.2 | async-start | bytes 393216 | tf_op jit(solution)/shard_map/all_to_all | solution.py:601
  46.5 5.4 %collective-permute-start.7 = (f32[32,128]{1,0:T(8,128)S(1)}, f32[32,128]{1,0:T(8,128)S(1)}, u32[]{:S(2)}, u32[]{:S(2)}) collective-permute-start(f32[32,128]{1,0:T(8,128)S(1)} %get-tuple-element.65), channel_id=1, source_target_pairs={{1,2},{2,1},{5,6},{6,5},{9,10},{10,9},{13,14},{14,13},{17,18},{18,... | collective-permute-start | bytes 49160 | tf_op jit(solution)/shard_map/ppermute | solution.py:492
  47.1 6.4 %collective-permute-start.6 = (f32[32,128]{1,0:T(8,128)S(1)}, f32[32,128]{1,0:T(8,128)S(1)}, u32[]{:S(2)}, u32[]{:S(2)}) collective-permute-start(f32[32,128]{1,0:T(8,128)S(1)} %get-tuple-element.65), channel_id=1, source_target_pairs={{0,1},{2,3},{1,0},{3,2},{4,5},{6,7},{5,4},{7,6},{8,9},{10,11},{9,8... | collective-permute-start | bytes 49160 | tf_op jit(solution)/shard_map/ppermute | solution.py:492
  55.8 13.2 %all-to-all-start.3 = ((f32[32,16,128]{2,1,0:T(8,128)}), f32[32,16,128]{2,1,0:T(8,128)S(1)}, u32[]{:S(2)}, u32[]{:S(2)}) async-start(f32[32,16,128]{2,1,0:T(8,128)} %share_sum.3), calls=%async_computation.3 | async-start | bytes 524288 | tf_op jit(solution)/shard_map/all_to_all | solution.py:614
  58.7 1.3 %collective-permute-start.8 = (f32[64,128]{1,0:T(8,128)S(1)}, f32[64,128]{1,0:T(8,128)S(1)}, u32[]{:S(2)}, u32[]{:S(2)}) collective-permute-start(f32[64,128]{1,0:T(8,128)S(1)} %get-tuple-element.70), channel_id=1, source_target_pairs={{0,4},{8,12},{16,20},{24,28},{4,0},{12,8},{20,16},{28,24},{1,5},{9... | collective-permute-start | bytes 98312 | tf_op jit(solution)/shard_map/ppermute | solution.py:492
  59.1 1.0 %collective-permute-start.9 = (f32[64,128]{1,0:T(8,128)S(1)}, f32[64,128]{1,0:T(8,128)S(1)}, u32[]{:S(2)}, u32[]{:S(2)}) collective-permute-start(f32[64,128]{1,0:T(8,128)S(1)} %get-tuple-element.71), channel_id=1, source_target_pairs={{4,8},{12,16},{20,24},{8,4},{16,12},{24,20},{5,9},{13,17},{21,25},... | collective-permute-start | bytes 98312 | tf_op jit(solution)/shard_map/ppermute | solution.py:492

commit v20 on v19

--- a/solution.py
+++ b/solution.py
@@ -106,8 +106,8 @@
             for d in range(n_gx * n_gy)]
 
 
-def emit_modes(chosen, parent, is_owner, places, x_fwd, y_fwd, keep, send, modes, turned, work):
-    devices, rows = modes.shape[0], modes.shape[1] // 2
+def emit_modes(chosen, parent, is_owner, places, x_fwd, y_fwd, keep, send, turned, work):
+    devices, rows = len(places), keep.shape[1] // 2
     slabs = parent.shape[0]
     groups = slabs // GROUP
     head, rest = split(jnp.concatenate(chosen, axis=0))
@@ -130,14 +130,15 @@
             for p in range(2):
                 work[span, p * LANES : (p + 1) * LANES] += block[p * 2 * KX : (p + 1) * 2 * KX]
 
-    for d in range(devices):
-        for p in range(2):
-            modes[places[d], p * rows : (p + 1) * rows, :] = work[
-                d * rows : (d + 1) * rows, p * LANES : (p + 1) * LANES]
     count = devices // 2
-    mine = core()
-    keep[...] = modes[pl.ds(mine * count, count)]
-    send[...] = modes[pl.ds((1 - mine) * count, count)]
+    for mine in range(2):
+        @pl.when(core() == mine)
+        def _(mine=mine):
+            for d in range(devices):
+                half = keep if places[d] // count == mine else send
+                for p in range(2):
+                    half[places[d] % count, p * rows : (p + 1) * rows, :] = work[
+                        d * rows : (d + 1) * rows, p * LANES : (p + 1) * LANES]
 
 
 def add_kernel(kept, received, out):
@@ -157,7 +158,7 @@
 
 def first_kernel(n_gy, level_total, places, levels_all, owners_all, fields_all, parent_all,
                  x_fwd_all, y_fwd_all, keep, send, levels, owners, fields, sems, parent, x_fwd, y_fwd,
-                 modes, turned, work):
+                 turned, work):
     gx, gy = lax.axis_index("gx"), lax.axis_index("gy")
     copies = fetch_all(sems, [
         (levels_all, levels), (owners_all, owners), (fields_all, fields),
@@ -168,7 +169,7 @@
     emit_modes(
         [fields[slab_of(levels, c, level_count, level_total)] for c in range(parent.shape[0])],
         parent, owners[0] == gx * n_gy + gy, places, x_fwd[...], y_fwd[...], keep, send,
-        modes, turned, work,
+        turned, work,
     )
 
 
@@ -176,15 +177,14 @@
     return lax.rem(lax.axis_index(axis), 2) == 0
 
 
-def edge_kernel(fields, plume, first, second, cols):
+def edge_kernel(n_gy, period, cuts, fields, plume, first, second, cols, weights):
+    weights[...] = share_weights(n_gy, period, cuts, weights.shape)
     slabs = [fields[c] for c in range(fields.shape[0])]
     emit_edges(slabs + [plume[l] for l in range(plume.shape[0])], first, second, cols)
 
 
-def prepare_kernel(n_gy, period, level_total, cuts, levels, fields, y_back_all, weights, nudged, others,
-                   y_back, order, sems):
+def prepare_kernel(level_total, levels, fields, y_back_all, nudged, others, y_back, order, sems):
     copies = fetch_all(sems, [(y_back_all.at[lax.axis_index("gy")], y_back)])
-    weights[...] = share_weights(n_gy, period, cuts, weights.shape)
     count = levels.shape[0]
     for n in range(count):
         order[n] = levels[n]
@@ -382,7 +382,7 @@
     else:
         (owners_all, parent_all, x_fwd_all, y_fwd_all, fields_out, winds_out, keep, send,
          order, slabs, spread, spread_edges, west, east, sems,
-         owners, parent, x_fwd, y_fwd, modes, turned, work) = rest
+         owners, parent, x_fwd, y_fwd, turned, work) = rest
         extra = [(owners_all, owners), (x_fwd_all.at[gx], x_fwd), (y_fwd_all.at[gy], y_fwd),
                  (parent_all.at[0, step + 1], parent)]
     copies = fetch_all(sems, [(order_all, order)] + extra)
@@ -431,21 +431,17 @@
     for copy in copies[1:]:
         copy.wait()
     emit_modes(results, parent, owners[step + 1] == gx * n_gy + gy, places, x_fwd[...], y_fwd[...],
-               keep, send, modes, turned, work)
+               keep, send, turned, work)
 
 
 def others_kernel(step, last, level_count, fields, plume, source, row_first, row_second, col_first,
-                  col_second, order_all, *rest):
+                  col_second, order, *rest):
     level_total, cells_x, cells_y = plume.shape
     if last:
-        fields_all, plume_all, order, slab, west, east, sems, fields_out, plume_out, out_sems = rest
+        fields_all, plume_all, slab, west, east, fields_out, plume_out, out_sems = rest
     else:
-        (done, winds, fields_out, plume_out, first, second, cols, order, slab, west, east,
-         sems) = rest
-    copies = fetch_all(sems, [(order_all, order)])
+        done, winds, fields_out, plume_out, first, second, cols, slab, west, east = rest
     halo = Halo(row_first, row_second, col_first, col_second, west, east)
-    for copy in copies:
-        copy.wait()
     level_at = [order[n] for n in range(level_total)]
     kept = level_total - level_count
     sent = []
@@ -528,13 +524,12 @@
     order_space = pltpu.SMEM(order_shape, jnp.int32)
     rows_space = vmem(total, cells_y)
     mode_scratch = [vmem(nudged, 4 * KX * KX), table_space(x_fwd),
-                    table_space(y_fwd), vmem(devices, 2 * rows, LANES), vmem(nudged, KX, LANES),
+                    table_space(y_fwd), vmem(nudged, KX, LANES),
                     vmem(devices * rows, 2 * LANES)]
     nudged_scratch = [order_space, vmem(nudged + count, cells_x + 2 * PAD, cells_y),
                       vmem(devices * rows, LANES), vmem(devices * rows, LANES),
                       rows_space, rows_space, pltpu.SemaphoreType.DMA((5,))]
-    others_scratch = [order_space, vmem(total, cells_x + 2 * PAD, cells_y), rows_space, rows_space,
-                      pltpu.SemaphoreType.DMA((1,))]
+    others_scratch = [vmem(total, cells_x + 2 * PAD, cells_y), rows_space, rows_space]
 
     def out_scratch(slabs):
         return [vmem(3 * slabs, cells_x, cells_y), vmem(slabs, cells_x, cells_y),
@@ -563,34 +558,20 @@
         )(keep, received)
         if step == 0:
             modes, flat = lax.optimization_barrier((modes, flat))
-            edges = pl.pallas_call(
-                edge_kernel,
-                out_shape=edge_shapes,
-                in_specs=[VMEM] * 2,
-                out_specs=[VMEM] * 3,
+            *edges, weights = pl.pallas_call(
+                functools.partial(edge_kernel, n_gy, period),
+                out_shape=edge_shapes + [f32((2 * rows, LANES))],
+                in_specs=[SMEM, VMEM, VMEM],
+                out_specs=[VMEM] * 4,
                 compiler_params=limit(8),
                 name="edges",
-            )(flat, plume)
-            weights, flat_nudged, others, y_back, order = pl.pallas_call(
-                functools.partial(prepare_kernel, n_gy, period, level_total),
-                out_shape=[f32((2 * rows, LANES)), f32((3 * count, cells_x, cells_y)),
-                           f32((3 * kept, cells_x, cells_y)),
-                           jax.ShapeDtypeStruct(y_back.shape[1:], y_back.dtype),
-                           jax.ShapeDtypeStruct(order_shape, jnp.int32)],
-                in_specs=[SMEM, SMEM, VMEM, HBM],
-                out_specs=[VMEM] * 4 + [SMEM],
-                scratch_shapes=[pltpu.SemaphoreType.DMA((1,))],
-                compiler_params=limit(8),
-                name="prepare",
-            )(cuts, levels, flat, in_hbm(y_back))
-            order = in_hbm(order)
-            flat = flat_nudged
+            )(cuts, flat, plume)
         else:
             modes, others = lax.optimization_barrier((modes, others))
             others, plume, *edges = pl.pallas_call(
                 functools.partial(others_kernel, 0, False, count),
                 out_shape=[f32((3 * kept, cells_x, cells_y)), f32(plume.shape)] + edge_shapes,
-                in_specs=[VMEM] * 7 + [HBM] + [VMEM] * 2,
+                in_specs=[VMEM] * 7 + [SMEM] + [VMEM] * 2,
                 out_specs=[VMEM] * 5,
                 scratch_shapes=others_scratch,
                 compiler_params=limit(8),
@@ -611,12 +592,25 @@
         share, to_first, to_second = lax.optimization_barrier((share, to_first, to_second))
         row_first, row_second = exchange("gx", to_first, to_second)
         halo = [row_first, row_second, col_first, col_second]
+        if step == 0:
+            share, levels = lax.optimization_barrier((share, levels))
+            flat, others, y_back, order = pl.pallas_call(
+                functools.partial(prepare_kernel, level_total),
+                out_shape=[f32((3 * count, cells_x, cells_y)), f32((3 * kept, cells_x, cells_y)),
+                           jax.ShapeDtypeStruct(y_back.shape[1:], y_back.dtype),
+                           jax.ShapeDtypeStruct(order_shape, jnp.int32)],
+                in_specs=[SMEM, VMEM, HBM],
+                out_specs=[VMEM] * 3 + [SMEM],
+                scratch_shapes=[pltpu.SemaphoreType.DMA((1,))],
+                compiler_params=limit(8),
+                name="prepare",
+            )(levels, flat, in_hbm(y_back))
         shares = lax.all_to_all(share, AXES, 0, 0, tiled=True)
         if last:
             final = pl.pallas_call(
                 functools.partial(others_kernel, step, True, count),
                 out_shape=[f32((field_rows, cells_x, cells_y)), f32(plume.shape)],
-                in_specs=[VMEM] * 7 + [HBM],
+                in_specs=[VMEM] * 7 + [SMEM],
                 out_specs=[HBM] * 2,
                 scratch_shapes=others_scratch + out_scratch(kept),
                 compiler_params=limit(8),
@@ -631,7 +625,7 @@
                 input_output_aliases={10: 0, 11: 1},
                 compiler_params=limit(12),
                 name="last_nudged",
-            )(shares, flat, *halo, y_back, order, plume, source, *final)
+            )(shares, flat, *halo, y_back, in_hbm(order), plume, source, *final)
         else:
             flat, winds, keep, send = pl.pallas_call(
                 functools.partial(nudged_kernel, n_gy, step, False, count, level_total, places),
@@ -642,7 +636,7 @@
                 scratch_shapes=nudged_scratch + [owners_space] + mode_scratch,
                 compiler_params=limit(12),
                 name="inner_nudged",
-            )(shares, flat, *halo, y_back, order,
+            )(shares, flat, *halo, y_back, in_hbm(order),
               *map(in_hbm, (owners, parent_modes, x_fwd, y_fwd)))
     return flat.reshape(fields.shape), plume
 

time: 72.3 us -> 72 us (level)
    all_to_all x2, waiting for transfers between devices: 15.8 us -> 14.1 us  [local(): shares = lax.all_to_all(share, AXES, 0, 0, tiled=True)]
    ppermute x8, waiting for transfers between devices: 2.46 us -> 3.74 us  [exchange(): lax.ppermute(data, axis, pairs + [(b, a) for a, b in pairs])]
where the time goes in v20:
time: 72 us; the launch traced here: 71.4 us
  starting transfers between devices  31.1 us (43%)
  waiting for transfers between devices  22.8 us (32%)
  Pallas kernels  16.5 us (23%)
  between operations  0.85 us (1%)
    all_to_all x2, waiting for transfers between devices, local(): shares = lax.all_to_all(share, AXES, 0, 0, tiled=True)  14.1 us
    ppermute x8, starting transfers between devices, exchange(): lax.ppermute(data, axis, pairs + [(b, a) for a, b in pairs])  12.6 us
    all_to_all x2, starting transfers between devices, local(): lax.all_to_all(modes, AXES, 0, 0, axis_index_groups=same_core, tiled=True)  11.9 us
    all_to_all x2, starting transfers between devices, local(): shares = lax.all_to_all(share, AXES, 0, 0, tiled=True)  5.53 us
    ppermute x8, waiting for transfers between devices, exchange(): lax.ppermute(data, axis, pairs + [(b, a) for a, b in pairs])  3.74 us
    all_to_all x2, waiting for transfers between devices, local(): lax.all_to_all(modes, AXES, 0, 0, axis_index_groups=same_core, tiled=True)  2.86 us
    pallas_call x1, Pallas kernels, local(): pl.pallas_call(functools.partial(nudged_kernel, n_gy, step, True, count,...  2.5 us
    ppermute x2, waiting for transfers between devices, local(): received = lax.ppermute(send, 'gx', [(i, i ^ 1) for i in range(n_gx)])  2.14 us
  transfers between devices with their start and end apart: 14, of which 9 were waited for; matrix products, arithmetic and copies ran while one was open for 0% of the time, Pallas kernels for 9%

profile of v20, /device:TPU:0, one launch (start us, length us, event | category | flops | bytes accessed | tf_op | source)
XLA Modules:
  0.0 71.4 jit_solution(5902956108762762721)
XLA Ops:
  0.7 2.0 %first_modes.1 = (f32[16,24,128]{2,1,0:T(8,128)S(1)}, f32[16,24,128]{2,1,0:T(8,128)S(1)}) custom-call(s32[8]{0:T(128)} %levels, s32[2]{0:T(128)} %rest_0_.1, f32[48,32,128]{2,1,0:T(8,128)} %bitcast.2, f32[1,2,24,4096]{3,2,1,0:T(8,128)} %rest_1_.2, bf16[8,384,256]{2,1,0:T(8,128)(2,1)} %constant.10.clone.x_fwd_all.rest_2_, ...), custom_call_target="tpu_custom_call" | custom-call | tf_op jit(solution)/shard_map/first_modes/pallas_call | solution.py:538
  2.7 0.5 collective-permute-start
  3.2 1.1 %collective-permute-done.received = f32[16,24,128]{2,1,0:T(8,128)S(1)} collective-permute-done((f32[16,24,128]{2,1,0:T(8,128)S(1)}, f32[16,24,128]{2,1,0:T(8,128)S(1)}, u32[]{:S(2)}, u32[]{:S(2)}) %collective-permute-start) | collective-permute-done | bytes 196640 | tf_op jit(solution)/shard_map/ppermute | solution.py:550
  4.3 0.7 add_cores.2
  5.0 8.2 %all-to-all-start = ((f32[16,24,128]{2,1,0:T(8,128)}), f32[16,24,128]{2,1,0:T(8,128)S(1)}, u32[]{:S(2)}, u32[]{:S(2)}) async-start(f32[16,24,128]{2,1,0:T(8,128)} %add_cores.2), calls=%async_computation | async-start | bytes 393216 | tf_op jit(solution)/shard_map/all_to_all | solution.py:582
  13.4 0.9 %edges.1 = (f32[64,128]{1,0:T(8,128)S(1)}, f32[64,128]{1,0:T(8,128)S(1)}, f32[32,128]{1,0:T(8,128)S(1)}, f32[24,128]{1,0:T(8,128)S(1)}) custom-call(s32[24]{0:T(128)S(1)} %reshape.13.cuts, f32[48,32,128]{2,1,0:T(8,128)S(1)} %bitcast.3, f32[16,32,128]{2,1,0:T(8,128)S(1)} %copy-done.3), custom_call_target="tpu_custom_call" | custom-call | tf_op jit(solution)/shard_map/edges/pallas_call | solution.py:561
  14.2 0.7 collective-permute-start.2
  14.9 4.7 %collective-permute-start.1 = (f32[32,128]{1,0:T(8,128)S(1)}, f32[32,128]{1,0:T(8,128)S(1)}, u32[]{:S(2)}, u32[]{:S(2)}) collective-permute-start(f32[32,128]{1,0:T(8,128)S(1)} %get-tuple-element.48), channel_id=1, source_target_pairs={{0,1},{2,3},{1,0},{3,2},{4,5},{6,7},{5,4},{7,6},{8,9},{10,11},{9,8... | collective-permute-start | bytes 49160 | tf_op jit(solution)/shard_map/ppermute | solution.py:488
  19.6 1.7 %collective-permute-done.1.col_first = f32[32,128]{1,0:T(8,128)S(1)} collective-permute-done((f32[32,128]{1,0:T(8,128)S(1)}, f32[32,128]{1,0:T(8,128)S(1)}, u32[]{:S(2)}, u32[]{:S(2)}) %collective-permute-start.1) | collective-permute-done | bytes 16416 | tf_op jit(solution)/shard_map/ppermute | solution.py:488
  21.3 1.6 %all-to-all-done.parts = f32[16,24,128]{2,1,0:T(8,128)S(1)} async-done(((f32[16,24,128]{2,1,0:T(8,128)}), f32[16,24,128]{2,1,0:T(8,128)S(1)}, u32[]{:S(2)}, u32[]{:S(2)}) %all-to-all-start) | async-done | bytes 196640 | tf_op jit(solution)/shard_map/all_to_all | solution.py:582
  22.9 1.0 %share_sum.2 = f32[32,16,128]{2,1,0:T(8,128)} custom-call(f32[24,128]{1,0:T(8,128)S(1)} %get-tuple-element.46.weights, f32[16,24,128]{2,1,0:T(8,128)S(1)} %all-to-all-done.parts, bf16[512,256]{1,0:T(8,128)(2,1)S(1)} %copy-done.2, bf16[512,128]{1,0:T(8,128)(2,1)S(1)} %copy-done.4), custom_call_target="tpu_custom_call" | custom-call | tf_op jit(solution)/shard_map/share_sum/pallas_call | solution.py:584
  23.9 2.6 %all-to-all-start.1 = ((f32[32,16,128]{2,1,0:T(8,128)}), f32[32,16,128]{2,1,0:T(8,128)S(1)}, u32[]{:S(2)}, u32[]{:S(2)}) async-start(f32[32,16,128]{2,1,0:T(8,128)} %share_sum.2), calls=%async_computation.1 | async-start | bytes 524288 | tf_op jit(solution)/shard_map/all_to_all | solution.py:608
  26.9 0.7 collective-permute-start.4
  27.5 2.0 %prepare.1 = (f32[24,32,128]{2,1,0:T(8,128)S(1)}, f32[24,32,128]{2,1,0:T(8,128)S(1)}, bf16[192,256]{1,0:T(8,128)(2,1)S(1)}, s32[48]{0:T(128)S(1)}) custom-call(s32[8]{0:T(128)S(1)} %copy-done.7, f32[48,32,128]{2,1,0:T(8,128)S(1)} %bitcast.4, bf16[4,192,256]{2,1,0:T(8,128)(2,1)} %constant.12.clone.y_back_all), custom_call_target="tpu_custom_call" | custom-call | tf_op jit(solution)/shard_map/prepare/pallas_call | solution.py:597
  29.6 7.1 %all-to-all-done.1.shares = f32[32,16,128]{2,1,0:T(8,128)S(1)} async-done(((f32[32,16,128]{2,1,0:T(8,128)}), f32[32,16,128]{2,1,0:T(8,128)S(1)}, u32[]{:S(2)}, u32[]{:S(2)}) %all-to-all-start.1) | async-done | bytes 262176 | tf_op jit(solution)/shard_map/all_to_all | solution.py:608
  36.8 2.1 %inner_nudged.1 = (f32[24,32,128]{2,1,0:T(8,128)S(1)}, f32[16,32,128]{2,1,0:T(8,128)S(1)}, f32[16,24,128]{2,1,0:T(8,128)S(1)}, f32[16,24,128]{2,1,0:T(8,128)S(1)}) custom-call(f32[32,16,128]{2,1,0:T(8,128)S(1)} %all-to-all-done.1.shares, f32[24,32,128]{2,1,0:T(8,128)S(1)} %get-tuple-element.55.fields, f32[64,128]{1,0:T(8,128)S(1)} %collective-permute-done.3.row_first, ...), custom_call_target="tpu_custom_call" | custom-call | tf_op jit(solution)/shard_map/inner_nudged/pallas_call | solution.py:630
  38.9 0.5 collective-permute-start.5
  39.3 1.1 %collective-permute-done.5.received = f32[16,24,128]{2,1,0:T(8,128)S(1)} collective-permute-done((f32[16,24,128]{2,1,0:T(8,128)S(1)}, f32[16,24,128]{2,1,0:T(8,128)S(1)}, u32[]{:S(2)}, u32[]{:S(2)}) %collective-permute-start.5) | collective-permute-done | bytes 196640 | tf_op jit(solution)/shard_map/ppermute | solution.py:550
  40.4 0.7 add_cores.3
  41.1 3.7 %all-to-all-start.2 = ((f32[16,24,128]{2,1,0:T(8,128)}), f32[16,24,128]{2,1,0:T(8,128)S(1)}, u32[]{:S(2)}, u32[]{:S(2)}) async-start(f32[16,24,128]{2,1,0:T(8,128)} %add_cores.3), calls=%async_computation.2 | async-start | bytes 393216 | tf_op jit(solution)/shard_map/all_to_all | solution.py:582
  44.8 1.5 %inner_others.1 = (f32[24,32,128]{2,1,0:T(8,128)S(1)}, f32[16,32,128]{2,1,0:T(8,128)S(1)}, f32[64,128]{1,0:T(8,128)S(1)}, f32[64,128]{1,0:T(8,128)S(1)}, f32[32,128]{1,0:T(8,128)S(1)}) custom-call(f32[24,32,128]{2,1,0:T(8,128)S(1)} %get-tuple-element.66.fields, f32[16,32,128]{2,1,0:T(8,128)S(1)} %copy-done.3, f32[16,32,128]{2,1,0:T(8,128)S(1)} %copy-done.1, ...), custom_call_target="tpu_custom_call" | custom-call | tf_op jit(solution)/shard_map/inner_others/pallas_call | solution.py:571
  46.4 0.7 collective-permute-start.7
  47.1 4.7 %collective-permute-start.6 = (f32[32,128]{1,0:T(8,128)S(1)}, f32[32,128]{1,0:T(8,128)S(1)}, u32[]{:S(2)}, u32[]{:S(2)}) collective-permute-start(f32[32,128]{1,0:T(8,128)S(1)} %get-tuple-element.69), channel_id=1, source_target_pairs={{0,1},{2,3},{1,0},{3,2},{4,5},{6,7},{5,4},{7,6},{8,9},{10,11},{9,8... | collective-permute-start | bytes 49160 | tf_op jit(solution)/shard_map/ppermute | solution.py:488
  51.8 1.7 %collective-permute-done.6.col_first = f32[32,128]{1,0:T(8,128)S(1)} collective-permute-done((f32[32,128]{1,0:T(8,128)S(1)}, f32[32,128]{1,0:T(8,128)S(1)}, u32[]{:S(2)}, u32[]{:S(2)}) %collective-permute-start.6) | collective-permute-done | bytes 16416 | tf_op jit(solution)/shard_map/ppermute | solution.py:488
  53.5 1.3 %all-to-all-done.2.parts = f32[16,24,128]{2,1,0:T(8,128)S(1)} async-done(((f32[16,24,128]{2,1,0:T(8,128)}), f32[16,24,128]{2,1,0:T(8,128)S(1)}, u32[]{:S(2)}, u32[]{:S(2)}) %all-to-all-start.2) | async-done | bytes 196640 | tf_op jit(solution)/shard_map/all_to_all | solution.py:582
  54.8 1.0 %share_sum.3 = f32[32,16,128]{2,1,0:T(8,128)} custom-call(f32[24,128]{1,0:T(8,128)S(1)} %get-tuple-element.46.weights, f32[16,24,128]{2,1,0:T(8,128)S(1)} %all-to-all-done.2.parts, bf16[512,256]{1,0:T(8,128)(2,1)S(1)} %copy-done.2, bf16[512,128]{1,0:T(8,128)(2,1)S(1)} %copy-done.4), custom_call_target="tpu_custom_call" | custom-call | tf_op jit(solution)/shard_map/share_sum/pallas_call | solution.py:584
  55.8 2.9 %all-to-all-start.3 = ((f32[32,16,128]{2,1,0:T(8,128)}), f32[32,16,128]{2,1,0:T(8,128)S(1)}, u32[]{:S(2)}, u32[]{:S(2)}) async-start(f32[32,16,128]{2,1,0:T(8,128)} %share_sum.3), calls=%async_computation.3 | async-start | bytes 524288 | tf_op jit(solution)/shard_map/all_to_all | solution.py:608
  58.7 0.3 collective-permute-start.8
  59.0 0.7 collective-permute-start.9
  60.0 2.0 %last_others.1 = (f32[48,32,128]{2,1,0:T(8,128)}, f32[16,32,128]{2,1,0:T(8,128)}) custom-call(f32[24,32,128]{2,1,0:T(8,128)S(1)} %get-tuple-element.79.fields, f32[16,32,128]{2,1,0:T(8,128)S(1)} %get-tuple-element.78.plume.rest_0_, f32[16,32,128]{2,1,0:T(8,128)S(1)} %copy-done.1, f32[64,128]{1,0:T(8,128)S(1)} %collective-permute-done.8.row_first, ...), custom_call_target="tpu_custom_call" | custom-call | tf_op jit(solution)/shard_map/last_others/pallas_call | solution.py:610
  62.0 6.9 %all-to-all-done.3.shares = f32[32,16,128]{2,1,0:T(8,128)S(1)} async-done(((f32[32,16,128]{2,1,0:T(8,128)}), f32[32,16,128]{2,1,0:T(8,128)S(1)}, u32[]{:S(2)}, u32[]{:S(2)}) %all-to-all-start.3) | async-done | bytes 262176 | tf_op jit(solution)/shard_map/all_to_all | solution.py:608
  68.9 2.5 %last_nudged.1 = (f32[48,32,128]{2,1,0:T(8,128)}, f32[16,32,128]{2,1,0:T(8,128)}) custom-call(f32[32,16,128]{2,1,0:T(8,128)S(1)} %all-to-all-done.3.shares, f32[24,32,128]{2,1,0:T(8,128)S(1)} %get-tuple-element.67.rest_0_.fields, f32[64,128]{1,0:T(8,128)S(1)} %collective-permute-done.8.row_first, ...), custom_call_target="tpu_custom_call", output_to_operand_aliasing={{0}: (10, {}), {1}: (11, {})} | custom-call | tf_op jit(solution)/shard_map/last_nudged/pallas_call | solution.py:619
  (26 shorter events, 0.7 us)
Async XLA Ops:
  0.6 12.6 %copy-start.8 = (s32[3,8]{1,0:T(4,128)S(1)}, s32[3,8]{1,0:T(4,128)}, u32[]{:S(2)}) copy-start(s32[3,8]{1,0:T(4,128)} %param.14) | copy-start | bytes 292
  0.6 12.7 %copy-start = (f32[3,16,32,128]{3,2,1,0:T(8,128)S(1)}, f32[3,16,32,128]{3,2,1,0:T(8,128)}, u32[]{:S(2)}) copy-start(f32[3,16,32,128]{3,2,1,0:T(8,128)} %param.12) | copy-start | bytes 2359300
  0.7 12.7 %copy-start.3 = (f32[16,32,128]{2,1,0:T(8,128)S(1)}, f32[16,32,128]{2,1,0:T(8,128)}, u32[]{:S(2)}) copy-start(f32[16,32,128]{2,1,0:T(8,128)} %plume.3) | copy-start | bytes 786436
  2.7 20.2 %copy-start.2 = (bf16[512,256]{1,0:T(8,128)(2,1)S(1)}, bf16[512,256]{1,0:T(8,128)(2,1)}, u32[]{:S(2)}) copy-start(bf16[512,256]{1,0:T(8,128)(2,1)} %constant.13.clone.x_back) | copy-start | bytes 786436
  2.7 20.2 %copy-start.4 = (bf16[512,128]{1,0:T(8,128)(2,1)S(1)}, bf16[512,128]{1,0:T(8,128)(2,1)}, u32[]{:S(2)}) copy-start(bf16[512,128]{1,0:T(8,128)(2,1)} %constant.14.clone.x_beside) | copy-start | bytes 393220
  2.7 1.6 %collective-permute-start = (f32[16,24,128]{2,1,0:T(8,128)S(1)}, f32[16,24,128]{2,1,0:T(8,128)S(1)}, u32[]{:S(2)}, u32[]{:S(2)}) collective-permute-start(f32[16,24,128]{2,1,0:T(8,128)S(1)} %get-tuple-element.44), channel_id=1, source_target_pairs={{0,4},{4,0},{8,12},{12,8},{16,20},{20,16},{24,28},{28,24},{1,5},{5... | collective-permute-start | bytes 589832 | tf_op jit(solution)/shard_map/ppermute | solution.py:550
  4.3 23.2 %copy-start.7 = (s32[8]{0:T(128)S(1)}, s32[8]{0:T(128)}, u32[]{:S(2)}) copy-start(s32[8]{0:T(128)} %levels) | copy-start | bytes 100
  5.0 17.9 %all-to-all-start = ((f32[16,24,128]{2,1,0:T(8,128)}), f32[16,24,128]{2,1,0:T(8,128)S(1)}, u32[]{:S(2)}, u32[]{:S(2)}) async-start(f32[16,24,128]{2,1,0:T(8,128)} %add_cores.2), calls=%async_computation | async-start | bytes 393216 | tf_op jit(solution)/shard_map/all_to_all | solution.py:582
  14.2 5.4 %collective-permute-start.2 = (f32[32,128]{1,0:T(8,128)S(1)}, f32[32,128]{1,0:T(8,128)S(1)}, u32[]{:S(2)}, u32[]{:S(2)}) collective-permute-start(f32[32,128]{1,0:T(8,128)S(1)} %get-tuple-element.48), channel_id=1, source_target_pairs={{1,2},{2,1},{5,6},{6,5},{9,10},{10,9},{13,14},{14,13},{17,18},{18,... | collective-permute-start | bytes 49160 | tf_op jit(solution)/shard_map/ppermute | solution.py:488
  14.9 6.4 %collective-permute-start.1 = (f32[32,128]{1,0:T(8,128)S(1)}, f32[32,128]{1,0:T(8,128)S(1)}, u32[]{:S(2)}, u32[]{:S(2)}) collective-permute-start(f32[32,128]{1,0:T(8,128)S(1)} %get-tuple-element.48), channel_id=1, source_target_pairs={{0,1},{2,3},{1,0},{3,2},{4,5},{6,7},{5,4},{7,6},{8,9},{10,11},{9,8... | collective-permute-start | bytes 49160 | tf_op jit(solution)/shard_map/ppermute | solution.py:488
  23.9 12.8 %all-to-all-start.1 = ((f32[32,16,128]{2,1,0:T(8,128)}), f32[32,16,128]{2,1,0:T(8,128)S(1)}, u32[]{:S(2)}, u32[]{:S(2)}) async-start(f32[32,16,128]{2,1,0:T(8,128)} %share_sum.2), calls=%async_computation.1 | async-start | bytes 524288 | tf_op jit(solution)/shard_map/all_to_all | solution.py:608
  26.6 3.1 %collective-permute-start.3 = (f32[64,128]{1,0:T(8,128)S(1)}, f32[64,128]{1,0:T(8,128)S(1)}, u32[]{:S(2)}, u32[]{:S(2)}) collective-permute-start(f32[64,128]{1,0:T(8,128)S(1)} %get-tuple-element.56), channel_id=1, source_target_pairs={{0,4},{8,12},{16,20},{24,28},{4,0},{12,8},{20,16},{28,24},{1,5},{9... | collective-permute-start | bytes 98312 | tf_op jit(solution)/shard_map/ppermute | solution.py:488
  26.9 2.7 %collective-permute-start.4 = (f32[64,128]{1,0:T(8,128)S(1)}, f32[64,128]{1,0:T(8,128)S(1)}, u32[]{:S(2)}, u32[]{:S(2)}) collective-permute-start(f32[64,128]{1,0:T(8,128)S(1)} %get-tuple-element.57), channel_id=1, source_target_pairs={{4,8},{12,16},{20,24},{8,4},{16,12},{24,20},{5,9},{13,17},{21,25},... | collective-permute-start | bytes 98312 | tf_op jit(solution)/shard_map/ppermute | solution.py:488
  29.6 7.2 %copy-start.5 = (s32[48]{0:T(128)}, s32[48]{0:T(128)S(1)}, u32[]{:S(2)}) copy-start(s32[48]{0:T(128)S(1)} %get-tuple-element.61.order_all.order) | copy-start | bytes 580
  36.8 8.1 %copy-start.1 = (f32[16,32,128]{2,1,0:T(8,128)S(1)}, f32[16,32,128]{2,1,0:T(8,128)}, u32[]{:S(2)}) copy-start(f32[16,32,128]{2,1,0:T(8,128)} %rest_1_.3) | copy-start | bytes 786436
  36.8 8.1 %copy-start.6 = (s32[48]{0:T(128)S(1)}, s32[48]{0:T(128)}, u32[]{:S(2)}) copy-start(s32[48]{0:T(128)} %copy-done.5) | copy-start | bytes 580
  38.9 1.5 %collective-permute-start.5 = (f32[16,24,128]{2,1,0:T(8,128)S(1)}, f32[16,24,128]{2,1,0:T(8,128)S(1)}, u32[]{:S(2)}, u32[]{:S(2)}) collective-permute-start(f32[16,24,128]{2,1,0:T(8,128)S(1)} %get-tuple-element.63), channel_id=1, source_target_pairs={{0,4},{4,0},{8,12},{12,8},{16,20},{20,16},{24,28},{28,24},{1,5},{5... | collective-permute-start | bytes 589832 | tf_op jit(solution)/shard_map/ppermute | solution.py:550
  41.1 13.7 %all-to-all-start.2 = ((f32[16,24,128]{2,1,0:T(8,128)}), f32[16,24,128]{2,1,0:T(8,128)S(1)}, u32[]{:S(2)}, u32[]{:S(2)}) async-start(f32[16,24,128]{2,1,0:T(8,128)} %add_cores.3), calls=%async_computation.2 | async-start | bytes 393216 | tf_op jit(solution)/shard_map/all_to_all | solution.py:582
  46.4 5.4 %collective-permute-start.7 = (f32[32,128]{1,0:T(8,128)S(1)}, f32[32,128]{1,0:T(8,128)S(1)}, u32[]{:S(2)}, u32[]{:S(2)}) collective-permute-start(f32[32,128]{1,0:T(8,128)S(1)} %get-tuple-element.69), channel_id=1, source_target_pairs={{1,2},{2,1},{5,6},{6,5},{9,10},{10,9},{13,14},{14,13},{17,18},{18,... | collective-permute-start | bytes 49160 | tf_op jit(solution)/shard_map/ppermute | solution.py:488
  47.1 6.4 %collective-permute-start.6 = (f32[32,128]{1,0:T(8,128)S(1)}, f32[32,128]{1,0:T(8,128)S(1)}, u32[]{:S(2)}, u32[]{:S(2)}) collective-permute-start(f32[32,128]{1,0:T(8,128)S(1)} %get-tuple-element.69), channel_id=1, source_target_pairs={{0,1},{2,3},{1,0},{3,2},{4,5},{6,7},{5,4},{7,6},{8,9},{10,11},{9,8... | collective-permute-start | bytes 49160 | tf_op jit(solution)/shard_map/ppermute | solution.py:488
  55.8 13.1 %all-to-all-start.3 = ((f32[32,16,128]{2,1,0:T(8,128)}), f32[32,16,128]{2,1,0:T(8,128)S(1)}, u32[]{:S(2)}, u32[]{:S(2)}) async-start(f32[32,16,128]{2,1,0:T(8,128)} %share_sum.3), calls=%async_computation.3 | async-start | bytes 524288 | tf_op jit(solution)/shard_map/all_to_all | solution.py:608
  58.7 1.3 %collective-permute-start.8 = (f32[64,128]{1,0:T(8,128)S(1)}, f32[64,128]{1,0:T(8,128)S(1)}, u32[]{:S(2)}, u32[]{:S(2)}) collective-permute-start(f32[64,128]{1,0:T(8,128)S(1)} %get-tuple-element.74), channel_id=1, source_target_pairs={{0,4},{8,12},{16,20},{24,28},{4,0},{12,8},{20,16},{28,24},{1,5},{9... | collective-permute-start | bytes 98312 | tf_op jit(solution)/shard_map/ppermute | solution.py:488
  59.0 1.0 %collective-permute-start.9 = (f32[64,128]{1,0:T(8,128)S(1)}, f32[64,128]{1,0:T(8,128)S(1)}, u32[]{:S(2)}, u32[]{:S(2)}) collective-permute-start(f32[64,128]{1,0:T(8,128)S(1)} %get-tuple-element.75), channel_id=1, source_target_pairs={{4,8},{12,16},{20,24},{8,4},{16,12},{24,20},{5,9},{13,17},{21,25},... | collective-permute-start | bytes 98312 | tf_op jit(solution)/shard_map/ppermute | solution.py:488

commit v21 on v20

--- a/solution.py
+++ b/solution.py
@@ -101,9 +101,19 @@
     return lax.rem(lax.axis_index("gx"), 2)
 
 
+def ranking(n_gx, n_gy):
+    return sorted(range(n_gx * n_gy), key=lambda d: (abs(2 * (d % n_gy) - (n_gy - 1)), d))
+
+
+def core_groups(n_gx, n_gy):
+    return [[d for d in ranking(n_gx, n_gy) if d // n_gy % 2 == c] for c in range(2)]
+
+
 def share_places(n_gx, n_gy):
-    return [(d // n_gy % 2 * (n_gx // 2) + d // n_gy // 2) * n_gy + d % n_gy
-            for d in range(n_gx * n_gy)]
+    places = {}
+    for c, group in enumerate(core_groups(n_gx, n_gy)):
+        places.update({d: c * len(group) + i for i, d in enumerate(group)})
+    return [places[d] for d in range(n_gx * n_gy)]
 
 
 def emit_modes(chosen, parent, is_owner, places, x_fwd, y_fwd, keep, send, turned, work):
@@ -266,6 +276,7 @@
     cells_x = LANES // GROUP
     slot = lax.broadcasted_iota(jnp.int32, (height, LANES), 1) // cells_x
     spot = lax.broadcasted_iota(jnp.int32, (packed, LANES), 1) // width
+    spot_at = {d: i for i, d in enumerate(ranking(n_gx, n_gy))}
     for g in range(n_gx):
         first = g * cells_x // LANES * LANES
         tile = jnp.zeros((height, LANES), jnp.float32)
@@ -279,8 +290,8 @@
             beside = jnp.where(
                 spot == m, pltpu.roll(piece, (m - g) * width % LANES, 1), beside)
         for h in range(n_gy):
-            out[g * n_gy + h, :rows, :] = tile[:rows]
-            out[g * n_gy + h, rows:, :] = beside
+            out[spot_at[g * n_gy + h], :rows, :] = tile[:rows]
+            out[spot_at[g * n_gy + h], rows:, :] = beside
 
 
 class Halo:
@@ -342,14 +353,14 @@
     return jnp.where(l + 1 < level_total, 0.3, 0.0).astype(jnp.float32)
 
 
-def nudge_updates(shares, spread, spread_edges, y_table, nudged, cells_x):
+def nudge_updates(ranks, shares, spread, spread_edges, y_table, nudged, cells_x):
     devices = shares.shape[0]
     rows = spread.shape[0] // devices
     packed = beside_rows(rows)
     width = 2 * GROUP
-    for d in range(devices):
-        spread[d * rows : (d + 1) * rows] = shares[d, :rows, :]
-        edge = shares[d, rows:, :]
+    for i, d in enumerate(ranks):
+        spread[d * rows : (d + 1) * rows] = shares[i, :rows, :]
+        edge = shares[i, rows:, :]
         for m in range(3):
             count = min(packed, rows - m * packed)
             if count > 0:
@@ -370,7 +381,7 @@
     return updates, update_rows
 
 
-def nudged_kernel(n_gy, step, last, level_count, level_total, places, shares, fields, row_first, row_second,
+def nudged_kernel(n_gy, step, last, level_count, level_total, ranks, places, shares, fields, row_first, row_second,
                   col_first, col_second, y_back, order_all, *rest):
     gx, gy = lax.axis_index("gx"), lax.axis_index("gy")
     cells_x, cells_y = fields.shape[1:]
@@ -388,7 +399,7 @@
     copies = fetch_all(sems, [(order_all, order)] + extra)
     halo = Halo(row_first, row_second, col_first, col_second, west, east)
     updates, update_rows = nudge_updates(
-        shares, spread, spread_edges, y_back[...], nudged, cells_x)
+        ranks, shares, spread, spread_edges, y_back[...], nudged, cells_x)
     copies[0].wait()
     level_at = [order[n] for n in range(level_count)]
     halo_at = level_at if step == 0 else list(range(level_count))
@@ -516,7 +527,7 @@
     kept = level_total - count
     half_shapes = [f32((devices // 2, 2 * rows, LANES))] * 2
     places = share_places(n_gx, n_gy)
-    same_core = [[gx * n_gy + gy for gx in range(c, n_gx, 2) for gy in range(n_gy)] for c in range(2)]
+    ranks = ranking(n_gx, n_gy)
     order_shape = (3 * level_total,)
     edge_shapes = [f32((total, cells_y)), f32((total, cells_y)), f32((cells_x, 2 * total))]
     levels_space = pltpu.SMEM(levels.shape, jnp.int32)
@@ -579,7 +590,8 @@
             )(others, plume, source, *halo, order, flat, winds)
         to_first, to_second, cols = edges
         col_first, col_second = exchange("gy", cols, cols)
-        parts = lax.all_to_all(modes, AXES, 0, 0, axis_index_groups=same_core, tiled=True)
+        parts = lax.all_to_all(modes, AXES, 0, 0, axis_index_groups=core_groups(n_gx, n_gy),
+                               tiled=True)
         parts, col_first, col_second = lax.optimization_barrier((parts, col_first, col_second))
         share = pl.pallas_call(
             functools.partial(share_kernel, n_gx, n_gy),
@@ -605,7 +617,7 @@
                 compiler_params=limit(8),
                 name="prepare",
             )(levels, flat, in_hbm(y_back))
-        shares = lax.all_to_all(share, AXES, 0, 0, tiled=True)
+        shares = lax.all_to_all(share, AXES, 0, 0, axis_index_groups=[ranks], tiled=True)
         if last:
             final = pl.pallas_call(
                 functools.partial(others_kernel, step, True, count),
@@ -617,7 +629,7 @@
                 name="last_others",
             )(others, plume, source, *halo, order)
             flat, plume = pl.pallas_call(
-                functools.partial(nudged_kernel, n_gy, step, True, count, level_total, None),
+                functools.partial(nudged_kernel, n_gy, step, True, count, level_total, ranks, None),
                 out_shape=[f32((field_rows, cells_x, cells_y)), f32(plume.shape)],
                 in_specs=[VMEM] * 7 + [HBM] + [VMEM] * 2 + [HBM] * 2,
                 out_specs=[HBM] * 2,
@@ -628,7 +640,7 @@
             )(shares, flat, *halo, y_back, in_hbm(order), plume, source, *final)
         else:
             flat, winds, keep, send = pl.pallas_call(
-                functools.partial(nudged_kernel, n_gy, step, False, count, level_total, places),
+                functools.partial(nudged_kernel, n_gy, step, False, count, level_total, ranks, places),
                 out_shape=[f32((nudged, cells_x, cells_y)), f32((2 * count, cells_x, cells_y))]
                 + half_shapes,
                 in_specs=[VMEM] * 7 + [HBM] * 5,

time: 72 us -> 71.5 us (level)
  starting transfers between devices: 31.1 us -> 29.6 us
  waiting for transfers between devices: 22.8 us -> 23.7 us
    ppermute x8, starting transfers between devices: 12.6 us -> 9.85 us  [exchange(): lax.ppermute(data, axis, pairs + [(b, a) for a, b in pairs])]
    all_to_all x4, starting transfers between devices: 17.5 us -> 19.2 us  [the longest x2 12.1 us: local(): lax.all_to_all(modes, AXES, 0, 0, axis_index_groups=core_groups(n_gx, n_g...]
where the time goes in v21:
time: 71.5 us; the launch traced here: 70.8 us
  starting transfers between devices  29.6 us (41%)
  waiting for transfers between devices  23.7 us (33%)
  Pallas kernels  16.5 us (23%)
  between operations  0.84 us (1%)
    all_to_all x2, waiting for transfers between devices, local(): lax.all_to_all(share, AXES, 0, 0, axis_index_groups=[ranks], tiled=True)  16.1 us
    all_to_all x2, starting transfers between devices, local(): lax.all_to_all(modes, AXES, 0, 0, axis_index_groups=core_groups(n_gx, n_g...  12.1 us
    ppermute x8, starting transfers between devices, exchange(): lax.ppermute(data, axis, pairs + [(b, a) for a, b in pairs])  9.85 us
    all_to_all x2, starting transfers between devices, local(): lax.all_to_all(share, AXES, 0, 0, axis_index_groups=[ranks], tiled=True)  7.07 us
    ppermute x8, waiting for transfers between devices, exchange(): lax.ppermute(data, axis, pairs + [(b, a) for a, b in pairs])  3.74 us
    pallas_call x1, Pallas kernels, local(): pl.pallas_call(functools.partial(nudged_kernel, n_gy, step, True, count,...  2.5 us
    ppermute x2, waiting for transfers between devices, local(): received = lax.ppermute(send, 'gx', [(i, i ^ 1) for i in range(n_gx)])  2.5 us
    pallas_call x1, Pallas kernels, local(): pl.pallas_call(functools.partial(nudged_kernel, n_gy, step, False, count,...  2.11 us
  transfers between devices with their start and end apart: 14, of which 9 were waited for; matrix products, arithmetic and copies ran while one was open for 0% of the time, Pallas kernels for 9%

profile of v21, /device:TPU:0, one launch (start us, length us, event | category | flops | bytes accessed | tf_op | source)
XLA Modules:
  0.0 70.8 jit_solution(5399585157337390044)
XLA Ops:
  0.7 2.0 %first_modes.1 = (f32[16,24,128]{2,1,0:T(8,128)S(1)}, f32[16,24,128]{2,1,0:T(8,128)S(1)}) custom-call(s32[8]{0:T(128)} %levels, s32[2]{0:T(128)} %rest_0_.1, f32[48,32,128]{2,1,0:T(8,128)} %bitcast.2, f32[1,2,24,4096]{3,2,1,0:T(8,128)} %rest_1_.2, bf16[8,384,256]{2,1,0:T(8,128)(2,1)} %constant.10.clone.x_fwd_all.rest_2_, ...), custom_call_target="tpu_custom_call" | custom-call | tf_op jit(solution)/shard_map/first_modes/pallas_call | solution.py:549
  2.7 0.5 collective-permute-start
  3.2 1.1 %collective-permute-done.received = f32[16,24,128]{2,1,0:T(8,128)S(1)} collective-permute-done((f32[16,24,128]{2,1,0:T(8,128)S(1)}, f32[16,24,128]{2,1,0:T(8,128)S(1)}, u32[]{:S(2)}, u32[]{:S(2)}) %collective-permute-start) | collective-permute-done | bytes 196640 | tf_op jit(solution)/shard_map/ppermute | solution.py:561
  4.3 0.7 add_cores.2
  5.0 8.7 %all-to-all-start = ((f32[16,24,128]{2,1,0:T(8,128)}), f32[16,24,128]{2,1,0:T(8,128)S(1)}, u32[]{:S(2)}, u32[]{:S(2)}) async-start(f32[16,24,128]{2,1,0:T(8,128)} %add_cores.2), calls=%async_computation | async-start | bytes 393216 | tf_op jit(solution)/shard_map/all_to_all | solution.py:593
  13.8 0.9 %edges.1 = (f32[64,128]{1,0:T(8,128)S(1)}, f32[64,128]{1,0:T(8,128)S(1)}, f32[32,128]{1,0:T(8,128)S(1)}, f32[24,128]{1,0:T(8,128)S(1)}) custom-call(s32[24]{0:T(128)S(1)} %reshape.13.cuts, f32[48,32,128]{2,1,0:T(8,128)S(1)} %bitcast.3, f32[16,32,128]{2,1,0:T(8,128)S(1)} %copy-done.3), custom_call_target="tpu_custom_call" | custom-call | tf_op jit(solution)/shard_map/edges/pallas_call | solution.py:572
  14.7 0.7 collective-permute-start.2
  15.4 3.3 %collective-permute-start.1 = (f32[32,128]{1,0:T(8,128)S(1)}, f32[32,128]{1,0:T(8,128)S(1)}, u32[]{:S(2)}, u32[]{:S(2)}) collective-permute-start(f32[32,128]{1,0:T(8,128)S(1)} %get-tuple-element.48), channel_id=1, source_target_pairs={{0,1},{2,3},{1,0},{3,2},{4,5},{6,7},{5,4},{7,6},{8,9},{10,11},{9,8... | collective-permute-start | bytes 49160 | tf_op jit(solution)/shard_map/ppermute | solution.py:499
  18.7 1.7 %collective-permute-done.1.col_first = f32[32,128]{1,0:T(8,128)S(1)} collective-permute-done((f32[32,128]{1,0:T(8,128)S(1)}, f32[32,128]{1,0:T(8,128)S(1)}, u32[]{:S(2)}, u32[]{:S(2)}) %collective-permute-start.1) | collective-permute-done | bytes 16416 | tf_op jit(solution)/shard_map/ppermute | solution.py:499
  20.4 0.7 %all-to-all-done.parts = f32[16,24,128]{2,1,0:T(8,128)S(1)} async-done(((f32[16,24,128]{2,1,0:T(8,128)}), f32[16,24,128]{2,1,0:T(8,128)S(1)}, u32[]{:S(2)}, u32[]{:S(2)}) %all-to-all-start) | async-done | bytes 196640 | tf_op jit(solution)/shard_map/all_to_all | solution.py:593
  21.2 1.0 %share_sum.2 = f32[32,16,128]{2,1,0:T(8,128)} custom-call(f32[24,128]{1,0:T(8,128)S(1)} %get-tuple-element.46.weights, f32[16,24,128]{2,1,0:T(8,128)S(1)} %all-to-all-done.parts, bf16[512,256]{1,0:T(8,128)(2,1)S(1)} %copy-done.2, bf16[512,128]{1,0:T(8,128)(2,1)S(1)} %copy-done.4), custom_call_target="tpu_custom_call" | custom-call | tf_op jit(solution)/shard_map/share_sum/pallas_call | solution.py:596
  22.2 3.5 %all-to-all-start.1 = ((f32[32,16,128]{2,1,0:T(8,128)}), f32[32,16,128]{2,1,0:T(8,128)S(1)}, u32[]{:S(2)}, u32[]{:S(2)}) async-start(f32[32,16,128]{2,1,0:T(8,128)} %share_sum.2), calls=%async_computation.1 | async-start | bytes 524288 | tf_op jit(solution)/shard_map/all_to_all | solution.py:620
  25.7 0.3 collective-permute-start.3
  26.0 0.7 collective-permute-start.4
  26.6 2.0 %prepare.1 = (f32[24,32,128]{2,1,0:T(8,128)S(1)}, f32[24,32,128]{2,1,0:T(8,128)S(1)}, bf16[192,256]{1,0:T(8,128)(2,1)S(1)}, s32[48]{0:T(128)S(1)}) custom-call(s32[8]{0:T(128)S(1)} %copy-done.7, f32[48,32,128]{2,1,0:T(8,128)S(1)} %bitcast.4, bf16[4,192,256]{2,1,0:T(8,128)(2,1)} %constant.12.clone.y_back_all), custom_call_target="tpu_custom_call" | custom-call | tf_op jit(solution)/shard_map/prepare/pallas_call | solution.py:609
  28.7 8.1 %all-to-all-done.1.shares = f32[32,16,128]{2,1,0:T(8,128)S(1)} async-done(((f32[32,16,128]{2,1,0:T(8,128)}), f32[32,16,128]{2,1,0:T(8,128)S(1)}, u32[]{:S(2)}, u32[]{:S(2)}) %all-to-all-start.1) | async-done | bytes 262176 | tf_op jit(solution)/shard_map/all_to_all | solution.py:620
  36.9 2.1 %inner_nudged.1 = (f32[24,32,128]{2,1,0:T(8,128)S(1)}, f32[16,32,128]{2,1,0:T(8,128)S(1)}, f32[16,24,128]{2,1,0:T(8,128)S(1)}, f32[16,24,128]{2,1,0:T(8,128)S(1)}) custom-call(f32[32,16,128]{2,1,0:T(8,128)S(1)} %all-to-all-done.1.shares, f32[24,32,128]{2,1,0:T(8,128)S(1)} %get-tuple-element.55.fields, f32[64,128]{1,0:T(8,128)S(1)} %collective-permute-done.3.row_first, ...), custom_call_target="tpu_custom_call" | custom-call | tf_op jit(solution)/shard_map/inner_nudged/pallas_call | solution.py:642
  39.1 1.4 %collective-permute-done.5.received = f32[16,24,128]{2,1,0:T(8,128)S(1)} collective-permute-done((f32[16,24,128]{2,1,0:T(8,128)S(1)}, f32[16,24,128]{2,1,0:T(8,128)S(1)}, u32[]{:S(2)}, u32[]{:S(2)}) %collective-permute-start.5) | collective-permute-done | bytes 196640 | tf_op jit(solution)/shard_map/ppermute | solution.py:561
  40.5 0.7 add_cores.3
  41.2 3.4 %all-to-all-start.2 = ((f32[16,24,128]{2,1,0:T(8,128)}), f32[16,24,128]{2,1,0:T(8,128)S(1)}, u32[]{:S(2)}, u32[]{:S(2)}) async-start(f32[16,24,128]{2,1,0:T(8,128)} %add_cores.3), calls=%async_computation.2 | async-start | bytes 393216 | tf_op jit(solution)/shard_map/all_to_all | solution.py:593
  44.6 1.5 %inner_others.1 = (f32[24,32,128]{2,1,0:T(8,128)S(1)}, f32[16,32,128]{2,1,0:T(8,128)S(1)}, f32[64,128]{1,0:T(8,128)S(1)}, f32[64,128]{1,0:T(8,128)S(1)}, f32[32,128]{1,0:T(8,128)S(1)}) custom-call(f32[24,32,128]{2,1,0:T(8,128)S(1)} %get-tuple-element.66.fields, f32[16,32,128]{2,1,0:T(8,128)S(1)} %copy-done.3, f32[16,32,128]{2,1,0:T(8,128)S(1)} %copy-done.1, ...), custom_call_target="tpu_custom_call" | custom-call | tf_op jit(solution)/shard_map/inner_others/pallas_call | solution.py:582
  46.2 0.7 collective-permute-start.7
  46.9 3.3 %collective-permute-start.6 = (f32[32,128]{1,0:T(8,128)S(1)}, f32[32,128]{1,0:T(8,128)S(1)}, u32[]{:S(2)}, u32[]{:S(2)}) collective-permute-start(f32[32,128]{1,0:T(8,128)S(1)} %get-tuple-element.69), channel_id=1, source_target_pairs={{0,1},{2,3},{1,0},{3,2},{4,5},{6,7},{5,4},{7,6},{8,9},{10,11},{9,8... | collective-permute-start | bytes 49160 | tf_op jit(solution)/shard_map/ppermute | solution.py:499
  50.1 1.7 %collective-permute-done.6.col_first = f32[32,128]{1,0:T(8,128)S(1)} collective-permute-done((f32[32,128]{1,0:T(8,128)S(1)}, f32[32,128]{1,0:T(8,128)S(1)}, u32[]{:S(2)}, u32[]{:S(2)}) %collective-permute-start.6) | collective-permute-done | bytes 16416 | tf_op jit(solution)/shard_map/ppermute | solution.py:499
  51.8 0.6 all-to-all-done.2.parts
  52.5 1.0 %share_sum.3 = f32[32,16,128]{2,1,0:T(8,128)} custom-call(f32[24,128]{1,0:T(8,128)S(1)} %get-tuple-element.46.weights, f32[16,24,128]{2,1,0:T(8,128)S(1)} %all-to-all-done.2.parts, bf16[512,256]{1,0:T(8,128)(2,1)S(1)} %copy-done.2, bf16[512,128]{1,0:T(8,128)(2,1)S(1)} %copy-done.4), custom_call_target="tpu_custom_call" | custom-call | tf_op jit(solution)/shard_map/share_sum/pallas_call | solution.py:596
  53.5 3.6 %all-to-all-start.3 = ((f32[32,16,128]{2,1,0:T(8,128)}), f32[32,16,128]{2,1,0:T(8,128)S(1)}, u32[]{:S(2)}, u32[]{:S(2)}) async-start(f32[32,16,128]{2,1,0:T(8,128)} %share_sum.3), calls=%async_computation.3 | async-start | bytes 524288 | tf_op jit(solution)/shard_map/all_to_all | solution.py:620
  57.1 0.3 collective-permute-start.8
  57.4 0.7 collective-permute-start.9
  58.4 2.0 %last_others.1 = (f32[48,32,128]{2,1,0:T(8,128)}, f32[16,32,128]{2,1,0:T(8,128)}) custom-call(f32[24,32,128]{2,1,0:T(8,128)S(1)} %get-tuple-element.79.fields, f32[16,32,128]{2,1,0:T(8,128)S(1)} %get-tuple-element.78.plume.rest_0_, f32[16,32,128]{2,1,0:T(8,128)S(1)} %copy-done.1, f32[64,128]{1,0:T(8,128)S(1)} %collective-permute-done.8.row_first, ...), custom_call_target="tpu_custom_call" | custom-call | tf_op jit(solution)/shard_map/last_others/pallas_call | solution.py:622
  60.4 7.9 %all-to-all-done.3.shares = f32[32,16,128]{2,1,0:T(8,128)S(1)} async-done(((f32[32,16,128]{2,1,0:T(8,128)}), f32[32,16,128]{2,1,0:T(8,128)S(1)}, u32[]{:S(2)}, u32[]{:S(2)}) %all-to-all-start.3) | async-done | bytes 262176 | tf_op jit(solution)/shard_map/all_to_all | solution.py:620
  68.3 2.5 %last_nudged.1 = (f32[48,32,128]{2,1,0:T(8,128)}, f32[16,32,128]{2,1,0:T(8,128)}) custom-call(f32[32,16,128]{2,1,0:T(8,128)S(1)} %all-to-all-done.3.shares, f32[24,32,128]{2,1,0:T(8,128)S(1)} %get-tuple-element.67.rest_0_.fields, f32[64,128]{1,0:T(8,128)S(1)} %collective-permute-done.8.row_first, ...), custom_call_target="tpu_custom_call", output_to_operand_aliasing={{0}: (10, {}), {1}: (11, {})} | custom-call | tf_op jit(solution)/shard_map/last_nudged/pallas_call | solution.py:631
  (26 shorter events, 0.5 us)
Async XLA Ops:
  0.6 13.1 %copy-start.8 = (s32[3,8]{1,0:T(4,128)S(1)}, s32[3,8]{1,0:T(4,128)}, u32[]{:S(2)}) copy-start(s32[3,8]{1,0:T(4,128)} %param.14) | copy-start | bytes 292
  0.6 13.2 %copy-start = (f32[3,16,32,128]{3,2,1,0:T(8,128)S(1)}, f32[3,16,32,128]{3,2,1,0:T(8,128)}, u32[]{:S(2)}) copy-start(f32[3,16,32,128]{3,2,1,0:T(8,128)} %param.12) | copy-start | bytes 2359300
  0.7 13.2 %copy-start.3 = (f32[16,32,128]{2,1,0:T(8,128)S(1)}, f32[16,32,128]{2,1,0:T(8,128)}, u32[]{:S(2)}) copy-start(f32[16,32,128]{2,1,0:T(8,128)} %plume.3) | copy-start | bytes 786436
  2.7 18.5 %copy-start.2 = (bf16[512,256]{1,0:T(8,128)(2,1)S(1)}, bf16[512,256]{1,0:T(8,128)(2,1)}, u32[]{:S(2)}) copy-start(bf16[512,256]{1,0:T(8,128)(2,1)} %constant.13.clone.x_back) | copy-start | bytes 786436
  2.7 18.4 %copy-start.4 = (bf16[512,128]{1,0:T(8,128)(2,1)S(1)}, bf16[512,128]{1,0:T(8,128)(2,1)}, u32[]{:S(2)}) copy-start(bf16[512,128]{1,0:T(8,128)(2,1)} %constant.14.clone.x_beside) | copy-start | bytes 393220
  2.7 1.6 %collective-permute-start = (f32[16,24,128]{2,1,0:T(8,128)S(1)}, f32[16,24,128]{2,1,0:T(8,128)S(1)}, u32[]{:S(2)}, u32[]{:S(2)}) collective-permute-start(f32[16,24,128]{2,1,0:T(8,128)S(1)} %get-tuple-element.44), channel_id=1, source_target_pairs={{0,4},{4,0},{8,12},{12,8},{16,20},{20,16},{24,28},{28,24},{1,5},{5... | collective-permute-start | bytes 589832 | tf_op jit(solution)/shard_map/ppermute | solution.py:561
  4.3 22.3 %copy-start.7 = (s32[8]{0:T(128)S(1)}, s32[8]{0:T(128)}, u32[]{:S(2)}) copy-start(s32[8]{0:T(128)} %levels) | copy-start | bytes 100
  5.0 16.1 %all-to-all-start = ((f32[16,24,128]{2,1,0:T(8,128)}), f32[16,24,128]{2,1,0:T(8,128)S(1)}, u32[]{:S(2)}, u32[]{:S(2)}) async-start(f32[16,24,128]{2,1,0:T(8,128)} %add_cores.2), calls=%async_computation | async-start | bytes 393216 | tf_op jit(solution)/shard_map/all_to_all | solution.py:593
  14.7 4.0 %collective-permute-start.2 = (f32[32,128]{1,0:T(8,128)S(1)}, f32[32,128]{1,0:T(8,128)S(1)}, u32[]{:S(2)}, u32[]{:S(2)}) collective-permute-start(f32[32,128]{1,0:T(8,128)S(1)} %get-tuple-element.48), channel_id=1, source_target_pairs={{1,2},{2,1},{5,6},{6,5},{9,10},{10,9},{13,14},{14,13},{17,18},{18,... | collective-permute-start | bytes 49160 | tf_op jit(solution)/shard_map/ppermute | solution.py:499
  15.4 5.1 %collective-permute-start.1 = (f32[32,128]{1,0:T(8,128)S(1)}, f32[32,128]{1,0:T(8,128)S(1)}, u32[]{:S(2)}, u32[]{:S(2)}) collective-permute-start(f32[32,128]{1,0:T(8,128)S(1)} %get-tuple-element.48), channel_id=1, source_target_pairs={{0,1},{2,3},{1,0},{3,2},{4,5},{6,7},{5,4},{7,6},{8,9},{10,11},{9,8... | collective-permute-start | bytes 49160 | tf_op jit(solution)/shard_map/ppermute | solution.py:499
  22.2 14.7 %all-to-all-start.1 = ((f32[32,16,128]{2,1,0:T(8,128)}), f32[32,16,128]{2,1,0:T(8,128)S(1)}, u32[]{:S(2)}, u32[]{:S(2)}) async-start(f32[32,16,128]{2,1,0:T(8,128)} %share_sum.2), calls=%async_computation.1 | async-start | bytes 524288 | tf_op jit(solution)/shard_map/all_to_all | solution.py:620
  25.7 3.1 %collective-permute-start.3 = (f32[64,128]{1,0:T(8,128)S(1)}, f32[64,128]{1,0:T(8,128)S(1)}, u32[]{:S(2)}, u32[]{:S(2)}) collective-permute-start(f32[64,128]{1,0:T(8,128)S(1)} %get-tuple-element.56), channel_id=1, source_target_pairs={{0,4},{8,12},{16,20},{24,28},{4,0},{12,8},{20,16},{28,24},{1,5},{9... | collective-permute-start | bytes 98312 | tf_op jit(solution)/shard_map/ppermute | solution.py:499
  26.0 2.7 %collective-permute-start.4 = (f32[64,128]{1,0:T(8,128)S(1)}, f32[64,128]{1,0:T(8,128)S(1)}, u32[]{:S(2)}, u32[]{:S(2)}) collective-permute-start(f32[64,128]{1,0:T(8,128)S(1)} %get-tuple-element.57), channel_id=1, source_target_pairs={{4,8},{12,16},{20,24},{8,4},{16,12},{24,20},{5,9},{13,17},{21,25},... | collective-permute-start | bytes 98312 | tf_op jit(solution)/shard_map/ppermute | solution.py:499
  28.7 8.2 %copy-start.5 = (s32[48]{0:T(128)}, s32[48]{0:T(128)S(1)}, u32[]{:S(2)}) copy-start(s32[48]{0:T(128)S(1)} %get-tuple-element.61.order_all.order) | copy-start | bytes 580
  36.9 7.8 %copy-start.1 = (f32[16,32,128]{2,1,0:T(8,128)S(1)}, f32[16,32,128]{2,1,0:T(8,128)}, u32[]{:S(2)}) copy-start(f32[16,32,128]{2,1,0:T(8,128)} %rest_1_.3) | copy-start | bytes 786436
  36.9 7.8 %copy-start.6 = (s32[48]{0:T(128)S(1)}, s32[48]{0:T(128)}, u32[]{:S(2)}) copy-start(s32[48]{0:T(128)} %copy-done.5) | copy-start | bytes 580
  39.0 1.5 %collective-permute-start.5 = (f32[16,24,128]{2,1,0:T(8,128)S(1)}, f32[16,24,128]{2,1,0:T(8,128)S(1)}, u32[]{:S(2)}, u32[]{:S(2)}) collective-permute-start(f32[16,24,128]{2,1,0:T(8,128)S(1)} %get-tuple-element.63), channel_id=1, source_target_pairs={{0,4},{4,0},{8,12},{12,8},{16,20},{20,16},{24,28},{28,24},{1,5},{5... | collective-permute-start | bytes 589832 | tf_op jit(solution)/shard_map/ppermute | solution.py:561
  41.2 11.3 %all-to-all-start.2 = ((f32[16,24,128]{2,1,0:T(8,128)}), f32[16,24,128]{2,1,0:T(8,128)S(1)}, u32[]{:S(2)}, u32[]{:S(2)}) async-start(f32[16,24,128]{2,1,0:T(8,128)} %add_cores.3), calls=%async_computation.2 | async-start | bytes 393216 | tf_op jit(solution)/shard_map/all_to_all | solution.py:593
  46.2 3.9 %collective-permute-start.7 = (f32[32,128]{1,0:T(8,128)S(1)}, f32[32,128]{1,0:T(8,128)S(1)}, u32[]{:S(2)}, u32[]{:S(2)}) collective-permute-start(f32[32,128]{1,0:T(8,128)S(1)} %get-tuple-element.69), channel_id=1, source_target_pairs={{1,2},{2,1},{5,6},{6,5},{9,10},{10,9},{13,14},{14,13},{17,18},{18,... | collective-permute-start | bytes 49160 | tf_op jit(solution)/shard_map/ppermute | solution.py:499
  46.9 5.0 %collective-permute-start.6 = (f32[32,128]{1,0:T(8,128)S(1)}, f32[32,128]{1,0:T(8,128)S(1)}, u32[]{:S(2)}, u32[]{:S(2)}) collective-permute-start(f32[32,128]{1,0:T(8,128)S(1)} %get-tuple-element.69), channel_id=1, source_target_pairs={{0,1},{2,3},{1,0},{3,2},{4,5},{6,7},{5,4},{7,6},{8,9},{10,11},{9,8... | collective-permute-start | bytes 49160 | tf_op jit(solution)/shard_map/ppermute | solution.py:499
  53.5 14.8 %all-to-all-start.3 = ((f32[32,16,128]{2,1,0:T(8,128)}), f32[32,16,128]{2,1,0:T(8,128)S(1)}, u32[]{:S(2)}, u32[]{:S(2)}) async-start(f32[32,16,128]{2,1,0:T(8,128)} %share_sum.3), calls=%async_computation.3 | async-start | bytes 524288 | tf_op jit(solution)/shard_map/all_to_all | solution.py:620
  57.1 1.3 %collective-permute-start.8 = (f32[64,128]{1,0:T(8,128)S(1)}, f32[64,128]{1,0:T(8,128)S(1)}, u32[]{:S(2)}, u32[]{:S(2)}) collective-permute-start(f32[64,128]{1,0:T(8,128)S(1)} %get-tuple-element.74), channel_id=1, source_target_pairs={{0,4},{8,12},{16,20},{24,28},{4,0},{12,8},{20,16},{28,24},{1,5},{9... | collective-permute-start | bytes 98312 | tf_op jit(solution)/shard_map/ppermute | solution.py:499
  57.4 1.0 %collective-permute-start.9 = (f32[64,128]{1,0:T(8,128)S(1)}, f32[64,128]{1,0:T(8,128)S(1)}, u32[]{:S(2)}, u32[]{:S(2)}) collective-permute-start(f32[64,128]{1,0:T(8,128)S(1)} %get-tuple-element.75), channel_id=1, source_target_pairs={{4,8},{12,16},{20,24},{8,4},{16,12},{24,20},{5,9},{13,17},{21,25},... | collective-permute-start | bytes 98312 | tf_op jit(solution)/shard_map/ppermute | solution.py:499

commit v22 on v21

--- a/solution.py
+++ b/solution.py
@@ -101,12 +101,12 @@
     return lax.rem(lax.axis_index("gx"), 2)
 
 
-def ranking(n_gx, n_gy):
-    return sorted(range(n_gx * n_gy), key=lambda d: (abs(2 * (d % n_gy) - (n_gy - 1)), d))
+def ranking(n_gx, n_gy, sign):
+    return sorted(range(n_gx * n_gy), key=lambda d: (sign * abs(2 * (d % n_gy) - (n_gy - 1)), d))
 
 
 def core_groups(n_gx, n_gy):
-    return [[d for d in ranking(n_gx, n_gy) if d // n_gy % 2 == c] for c in range(2)]
+    return [[d for d in ranking(n_gx, n_gy, 1) if d // n_gy % 2 == c] for c in range(2)]
 
 
 def share_places(n_gx, n_gy):
@@ -276,7 +276,7 @@
     cells_x = LANES // GROUP
     slot = lax.broadcasted_iota(jnp.int32, (height, LANES), 1) // cells_x
     spot = lax.broadcasted_iota(jnp.int32, (packed, LANES), 1) // width
-    spot_at = {d: i for i, d in enumerate(ranking(n_gx, n_gy))}
+    spot_at = {d: i for i, d in enumerate(ranking(n_gx, n_gy, -1))}
     for g in range(n_gx):
         first = g * cells_x // LANES * LANES
         tile = jnp.zeros((height, LANES), jnp.float32)
@@ -527,7 +527,7 @@
     kept = level_total - count
     half_shapes = [f32((devices // 2, 2 * rows, LANES))] * 2
     places = share_places(n_gx, n_gy)
-    ranks = ranking(n_gx, n_gy)
+    ranks = ranking(n_gx, n_gy, -1)
     order_shape = (3 * level_total,)
     edge_shapes = [f32((total, cells_y)), f32((total, cells_y)), f32((cells_x, 2 * total))]
     levels_space = pltpu.SMEM(levels.shape, jnp.int32)

time: 71.5 us -> 71.4 us (level)
  no operation moved by 1% of the time
where the time goes in v22:
time: 71.4 us; the launch traced here: 70.8 us
  starting transfers between devices  29.6 us (41%)
  waiting for transfers between devices  23.7 us (33%)
  Pallas kernels  16.5 us (23%)
  between operations  0.84 us (1%)
    all_to_all x2, waiting for transfers between devices, local(): lax.all_to_all(share, AXES, 0, 0, axis_index_groups=[ranks], tiled=True)  16.1 us
    all_to_all x2, starting transfers between devices, local(): lax.all_to_all(modes, AXES, 0, 0, axis_index_groups=core_groups(n_gx, n_g...  12.1 us
    ppermute x8, starting transfers between devices, exchange(): lax.ppermute(data, axis, pairs + [(b, a) for a, b in pairs])  9.85 us
    all_to_all x2, starting transfers between devices, local(): lax.all_to_all(share, AXES, 0, 0, axis_index_groups=[ranks], tiled=True)  7.07 us
    ppermute x8, waiting for transfers between devices, exchange(): lax.ppermute(data, axis, pairs + [(b, a) for a, b in pairs])  3.74 us
    pallas_call x1, Pallas kernels, local(): pl.pallas_call(functools.partial(nudged_kernel, n_gy, step, True, count,...  2.5 us
    ppermute x2, waiting for transfers between devices, local(): received = lax.ppermute(send, 'gx', [(i, i ^ 1) for i in range(n_gx)])  2.5 us
    pallas_call x1, Pallas kernels, local(): pl.pallas_call(functools.partial(nudged_kernel, n_gy, step, False, count,...  2.11 us
  transfers between devices with their start and end apart: 14, of which 9 were waited for; matrix products, arithmetic and copies ran while one was open for 0% of the time, Pallas kernels for 9%

profile of v22, /device:TPU:0, one launch (start us, length us, event | category | flops | bytes accessed | tf_op | source)
XLA Modules:
  0.0 70.8 jit_solution(5681377289038837404)
XLA Ops:
  0.7 2.0 %first_modes.1 = (f32[16,24,128]{2,1,0:T(8,128)S(1)}, f32[16,24,128]{2,1,0:T(8,128)S(1)}) custom-call(s32[8]{0:T(128)} %levels, s32[2]{0:T(128)} %rest_0_.1, f32[48,32,128]{2,1,0:T(8,128)} %bitcast.2, f32[1,2,24,4096]{3,2,1,0:T(8,128)} %rest_1_.2, bf16[8,384,256]{2,1,0:T(8,128)(2,1)} %constant.10.clone.x_fwd_all.rest_2_, ...), custom_call_target="tpu_custom_call" | custom-call | tf_op jit(solution)/shard_map/first_modes/pallas_call | solution.py:549
  2.7 0.5 collective-permute-start
  3.2 1.1 %collective-permute-done.received = f32[16,24,128]{2,1,0:T(8,128)S(1)} collective-permute-done((f32[16,24,128]{2,1,0:T(8,128)S(1)}, f32[16,24,128]{2,1,0:T(8,128)S(1)}, u32[]{:S(2)}, u32[]{:S(2)}) %collective-permute-start) | collective-permute-done | bytes 196640 | tf_op jit(solution)/shard_map/ppermute | solution.py:561
  4.3 0.7 add_cores.2
  5.0 8.7 %all-to-all-start = ((f32[16,24,128]{2,1,0:T(8,128)}), f32[16,24,128]{2,1,0:T(8,128)S(1)}, u32[]{:S(2)}, u32[]{:S(2)}) async-start(f32[16,24,128]{2,1,0:T(8,128)} %add_cores.2), calls=%async_computation | async-start | bytes 393216 | tf_op jit(solution)/shard_map/all_to_all | solution.py:593
  13.8 0.9 %edges.1 = (f32[64,128]{1,0:T(8,128)S(1)}, f32[64,128]{1,0:T(8,128)S(1)}, f32[32,128]{1,0:T(8,128)S(1)}, f32[24,128]{1,0:T(8,128)S(1)}) custom-call(s32[24]{0:T(128)S(1)} %reshape.13.cuts, f32[48,32,128]{2,1,0:T(8,128)S(1)} %bitcast.3, f32[16,32,128]{2,1,0:T(8,128)S(1)} %copy-done.3), custom_call_target="tpu_custom_call" | custom-call | tf_op jit(solution)/shard_map/edges/pallas_call | solution.py:572
  14.7 0.7 collective-permute-start.2
  15.4 3.3 %collective-permute-start.1 = (f32[32,128]{1,0:T(8,128)S(1)}, f32[32,128]{1,0:T(8,128)S(1)}, u32[]{:S(2)}, u32[]{:S(2)}) collective-permute-start(f32[32,128]{1,0:T(8,128)S(1)} %get-tuple-element.48), channel_id=1, source_target_pairs={{0,1},{2,3},{1,0},{3,2},{4,5},{6,7},{5,4},{7,6},{8,9},{10,11},{9,8... | collective-permute-start | bytes 49160 | tf_op jit(solution)/shard_map/ppermute | solution.py:499
  18.7 1.7 %collective-permute-done.1.col_first = f32[32,128]{1,0:T(8,128)S(1)} collective-permute-done((f32[32,128]{1,0:T(8,128)S(1)}, f32[32,128]{1,0:T(8,128)S(1)}, u32[]{:S(2)}, u32[]{:S(2)}) %collective-permute-start.1) | collective-permute-done | bytes 16416 | tf_op jit(solution)/shard_map/ppermute | solution.py:499
  20.4 0.7 %all-to-all-done.parts = f32[16,24,128]{2,1,0:T(8,128)S(1)} async-done(((f32[16,24,128]{2,1,0:T(8,128)}), f32[16,24,128]{2,1,0:T(8,128)S(1)}, u32[]{:S(2)}, u32[]{:S(2)}) %all-to-all-start) | async-done | bytes 196640 | tf_op jit(solution)/shard_map/all_to_all | solution.py:593
  21.2 1.0 %share_sum.2 = f32[32,16,128]{2,1,0:T(8,128)} custom-call(f32[24,128]{1,0:T(8,128)S(1)} %get-tuple-element.46.weights, f32[16,24,128]{2,1,0:T(8,128)S(1)} %all-to-all-done.parts, bf16[512,256]{1,0:T(8,128)(2,1)S(1)} %copy-done.2, bf16[512,128]{1,0:T(8,128)(2,1)S(1)} %copy-done.4), custom_call_target="tpu_custom_call" | custom-call | tf_op jit(solution)/shard_map/share_sum/pallas_call | solution.py:596
  22.2 3.5 %all-to-all-start.1 = ((f32[32,16,128]{2,1,0:T(8,128)}), f32[32,16,128]{2,1,0:T(8,128)S(1)}, u32[]{:S(2)}, u32[]{:S(2)}) async-start(f32[32,16,128]{2,1,0:T(8,128)} %share_sum.2), calls=%async_computation.1 | async-start | bytes 524288 | tf_op jit(solution)/shard_map/all_to_all | solution.py:620
  25.7 0.3 collective-permute-start.3
  26.0 0.7 collective-permute-start.4
  26.6 2.0 %prepare.1 = (f32[24,32,128]{2,1,0:T(8,128)S(1)}, f32[24,32,128]{2,1,0:T(8,128)S(1)}, bf16[192,256]{1,0:T(8,128)(2,1)S(1)}, s32[48]{0:T(128)S(1)}) custom-call(s32[8]{0:T(128)S(1)} %copy-done.7, f32[48,32,128]{2,1,0:T(8,128)S(1)} %bitcast.4, bf16[4,192,256]{2,1,0:T(8,128)(2,1)} %constant.12.clone.y_back_all), custom_call_target="tpu_custom_call" | custom-call | tf_op jit(solution)/shard_map/prepare/pallas_call | solution.py:609
  28.7 8.1 %all-to-all-done.1.shares = f32[32,16,128]{2,1,0:T(8,128)S(1)} async-done(((f32[32,16,128]{2,1,0:T(8,128)}), f32[32,16,128]{2,1,0:T(8,128)S(1)}, u32[]{:S(2)}, u32[]{:S(2)}) %all-to-all-start.1) | async-done | bytes 262176 | tf_op jit(solution)/shard_map/all_to_all | solution.py:620
  36.9 2.1 %inner_nudged.1 = (f32[24,32,128]{2,1,0:T(8,128)S(1)}, f32[16,32,128]{2,1,0:T(8,128)S(1)}, f32[16,24,128]{2,1,0:T(8,128)S(1)}, f32[16,24,128]{2,1,0:T(8,128)S(1)}) custom-call(f32[32,16,128]{2,1,0:T(8,128)S(1)} %all-to-all-done.1.shares, f32[24,32,128]{2,1,0:T(8,128)S(1)} %get-tuple-element.55.fields, f32[64,128]{1,0:T(8,128)S(1)} %collective-permute-done.3.row_first, ...), custom_call_target="tpu_custom_call" | custom-call | tf_op jit(solution)/shard_map/inner_nudged/pallas_call | solution.py:642
  39.1 1.4 %collective-permute-done.5.received = f32[16,24,128]{2,1,0:T(8,128)S(1)} collective-permute-done((f32[16,24,128]{2,1,0:T(8,128)S(1)}, f32[16,24,128]{2,1,0:T(8,128)S(1)}, u32[]{:S(2)}, u32[]{:S(2)}) %collective-permute-start.5) | collective-permute-done | bytes 196640 | tf_op jit(solution)/shard_map/ppermute | solution.py:561
  40.5 0.7 add_cores.3
  41.2 3.4 %all-to-all-start.2 = ((f32[16,24,128]{2,1,0:T(8,128)}), f32[16,24,128]{2,1,0:T(8,128)S(1)}, u32[]{:S(2)}, u32[]{:S(2)}) async-start(f32[16,24,128]{2,1,0:T(8,128)} %add_cores.3), calls=%async_computation.2 | async-start | bytes 393216 | tf_op jit(solution)/shard_map/all_to_all | solution.py:593
  44.6 1.5 %inner_others.1 = (f32[24,32,128]{2,1,0:T(8,128)S(1)}, f32[16,32,128]{2,1,0:T(8,128)S(1)}, f32[64,128]{1,0:T(8,128)S(1)}, f32[64,128]{1,0:T(8,128)S(1)}, f32[32,128]{1,0:T(8,128)S(1)}) custom-call(f32[24,32,128]{2,1,0:T(8,128)S(1)} %get-tuple-element.66.fields, f32[16,32,128]{2,1,0:T(8,128)S(1)} %copy-done.3, f32[16,32,128]{2,1,0:T(8,128)S(1)} %copy-done.1, ...), custom_call_target="tpu_custom_call" | custom-call | tf_op jit(solution)/shard_map/inner_others/pallas_call | solution.py:582
  46.2 0.7 collective-permute-start.7
  46.9 3.3 %collective-permute-start.6 = (f32[32,128]{1,0:T(8,128)S(1)}, f32[32,128]{1,0:T(8,128)S(1)}, u32[]{:S(2)}, u32[]{:S(2)}) collective-permute-start(f32[32,128]{1,0:T(8,128)S(1)} %get-tuple-element.69), channel_id=1, source_target_pairs={{0,1},{2,3},{1,0},{3,2},{4,5},{6,7},{5,4},{7,6},{8,9},{10,11},{9,8... | collective-permute-start | bytes 49160 | tf_op jit(solution)/shard_map/ppermute | solution.py:499
  50.1 1.7 %collective-permute-done.6.col_first = f32[32,128]{1,0:T(8,128)S(1)} collective-permute-done((f32[32,128]{1,0:T(8,128)S(1)}, f32[32,128]{1,0:T(8,128)S(1)}, u32[]{:S(2)}, u32[]{:S(2)}) %collective-permute-start.6) | collective-permute-done | bytes 16416 | tf_op jit(solution)/shard_map/ppermute | solution.py:499
  51.8 0.6 all-to-all-done.2.parts
  52.5 1.0 %share_sum.3 = f32[32,16,128]{2,1,0:T(8,128)} custom-call(f32[24,128]{1,0:T(8,128)S(1)} %get-tuple-element.46.weights, f32[16,24,128]{2,1,0:T(8,128)S(1)} %all-to-all-done.2.parts, bf16[512,256]{1,0:T(8,128)(2,1)S(1)} %copy-done.2, bf16[512,128]{1,0:T(8,128)(2,1)S(1)} %copy-done.4), custom_call_target="tpu_custom_call" | custom-call | tf_op jit(solution)/shard_map/share_sum/pallas_call | solution.py:596
  53.5 3.6 %all-to-all-start.3 = ((f32[32,16,128]{2,1,0:T(8,128)}), f32[32,16,128]{2,1,0:T(8,128)S(1)}, u32[]{:S(2)}, u32[]{:S(2)}) async-start(f32[32,16,128]{2,1,0:T(8,128)} %share_sum.3), calls=%async_computation.3 | async-start | bytes 524288 | tf_op jit(solution)/shard_map/all_to_all | solution.py:620
  57.1 0.3 collective-permute-start.8
  57.4 0.7 collective-permute-start.9
  58.4 2.0 %last_others.1 = (f32[48,32,128]{2,1,0:T(8,128)}, f32[16,32,128]{2,1,0:T(8,128)}) custom-call(f32[24,32,128]{2,1,0:T(8,128)S(1)} %get-tuple-element.79.fields, f32[16,32,128]{2,1,0:T(8,128)S(1)} %get-tuple-element.78.plume.rest_0_, f32[16,32,128]{2,1,0:T(8,128)S(1)} %copy-done.1, f32[64,128]{1,0:T(8,128)S(1)} %collective-permute-done.8.row_first, ...), custom_call_target="tpu_custom_call" | custom-call | tf_op jit(solution)/shard_map/last_others/pallas_call | solution.py:622
  60.4 7.9 %all-to-all-done.3.shares = f32[32,16,128]{2,1,0:T(8,128)S(1)} async-done(((f32[32,16,128]{2,1,0:T(8,128)}), f32[32,16,128]{2,1,0:T(8,128)S(1)}, u32[]{:S(2)}, u32[]{:S(2)}) %all-to-all-start.3) | async-done | bytes 262176 | tf_op jit(solution)/shard_map/all_to_all | solution.py:620
  68.3 2.5 %last_nudged.1 = (f32[48,32,128]{2,1,0:T(8,128)}, f32[16,32,128]{2,1,0:T(8,128)}) custom-call(f32[32,16,128]{2,1,0:T(8,128)S(1)} %all-to-all-done.3.shares, f32[24,32,128]{2,1,0:T(8,128)S(1)} %get-tuple-element.67.rest_0_.fields, f32[64,128]{1,0:T(8,128)S(1)} %collective-permute-done.8.row_first, ...), custom_call_target="tpu_custom_call", output_to_operand_aliasing={{0}: (10, {}), {1}: (11, {})} | custom-call | tf_op jit(solution)/shard_map/last_nudged/pallas_call | solution.py:631
  (26 shorter events, 0.5 us)
Async XLA Ops:
  0.6 13.1 %copy-start.8 = (s32[3,8]{1,0:T(4,128)S(1)}, s32[3,8]{1,0:T(4,128)}, u32[]{:S(2)}) copy-start(s32[3,8]{1,0:T(4,128)} %param.14) | copy-start | bytes 292
  0.6 13.2 %copy-start = (f32[3,16,32,128]{3,2,1,0:T(8,128)S(1)}, f32[3,16,32,128]{3,2,1,0:T(8,128)}, u32[]{:S(2)}) copy-start(f32[3,16,32,128]{3,2,1,0:T(8,128)} %param.12) | copy-start | bytes 2359300
  0.7 13.2 %copy-start.3 = (f32[16,32,128]{2,1,0:T(8,128)S(1)}, f32[16,32,128]{2,1,0:T(8,128)}, u32[]{:S(2)}) copy-start(f32[16,32,128]{2,1,0:T(8,128)} %plume.3) | copy-start | bytes 786436
  2.7 18.5 %copy-start.2 = (bf16[512,256]{1,0:T(8,128)(2,1)S(1)}, bf16[512,256]{1,0:T(8,128)(2,1)}, u32[]{:S(2)}) copy-start(bf16[512,256]{1,0:T(8,128)(2,1)} %constant.13.clone.x_back) | copy-start | bytes 786436
  2.7 18.4 %copy-start.4 = (bf16[512,128]{1,0:T(8,128)(2,1)S(1)}, bf16[512,128]{1,0:T(8,128)(2,1)}, u32[]{:S(2)}) copy-start(bf16[512,128]{1,0:T(8,128)(2,1)} %constant.14.clone.x_beside) | copy-start | bytes 393220
  2.7 1.6 %collective-permute-start = (f32[16,24,128]{2,1,0:T(8,128)S(1)}, f32[16,24,128]{2,1,0:T(8,128)S(1)}, u32[]{:S(2)}, u32[]{:S(2)}) collective-permute-start(f32[16,24,128]{2,1,0:T(8,128)S(1)} %get-tuple-element.44), channel_id=1, source_target_pairs={{0,4},{4,0},{8,12},{12,8},{16,20},{20,16},{24,28},{28,24},{1,5},{5... | collective-permute-start | bytes 589832 | tf_op jit(solution)/shard_map/ppermute | solution.py:561
  4.3 22.3 %copy-start.7 = (s32[8]{0:T(128)S(1)}, s32[8]{0:T(128)}, u32[]{:S(2)}) copy-start(s32[8]{0:T(128)} %levels) | copy-start | bytes 100
  5.0 16.1 %all-to-all-start = ((f32[16,24,128]{2,1,0:T(8,128)}), f32[16,24,128]{2,1,0:T(8,128)S(1)}, u32[]{:S(2)}, u32[]{:S(2)}) async-start(f32[16,24,128]{2,1,0:T(8,128)} %add_cores.2), calls=%async_computation | async-start | bytes 393216 | tf_op jit(solution)/shard_map/all_to_all | solution.py:593
  14.7 4.0 %collective-permute-start.2 = (f32[32,128]{1,0:T(8,128)S(1)}, f32[32,128]{1,0:T(8,128)S(1)}, u32[]{:S(2)}, u32[]{:S(2)}) collective-permute-start(f32[32,128]{1,0:T(8,128)S(1)} %get-tuple-element.48), channel_id=1, source_target_pairs={{1,2},{2,1},{5,6},{6,5},{9,10},{10,9},{13,14},{14,13},{17,18},{18,... | collective-permute-start | bytes 49160 | tf_op jit(solution)/shard_map/ppermute | solution.py:499
  15.4 5.1 %collective-permute-start.1 = (f32[32,128]{1,0:T(8,128)S(1)}, f32[32,128]{1,0:T(8,128)S(1)}, u32[]{:S(2)}, u32[]{:S(2)}) collective-permute-start(f32[32,128]{1,0:T(8,128)S(1)} %get-tuple-element.48), channel_id=1, source_target_pairs={{0,1},{2,3},{1,0},{3,2},{4,5},{6,7},{5,4},{7,6},{8,9},{10,11},{9,8... | collective-permute-start | bytes 49160 | tf_op jit(solution)/shard_map/ppermute | solution.py:499
  22.2 14.7 %all-to-all-start.1 = ((f32[32,16,128]{2,1,0:T(8,128)}), f32[32,16,128]{2,1,0:T(8,128)S(1)}, u32[]{:S(2)}, u32[]{:S(2)}) async-start(f32[32,16,128]{2,1,0:T(8,128)} %share_sum.2), calls=%async_computation.1 | async-start | bytes 524288 | tf_op jit(solution)/shard_map/all_to_all | solution.py:620
  25.7 3.1 %collective-permute-start.3 = (f32[64,128]{1,0:T(8,128)S(1)}, f32[64,128]{1,0:T(8,128)S(1)}, u32[]{:S(2)}, u32[]{:S(2)}) collective-permute-start(f32[64,128]{1,0:T(8,128)S(1)} %get-tuple-element.56), channel_id=1, source_target_pairs={{0,4},{8,12},{16,20},{24,28},{4,0},{12,8},{20,16},{28,24},{1,5},{9... | collective-permute-start | bytes 98312 | tf_op jit(solution)/shard_map/ppermute | solution.py:499
  26.0 2.7 %collective-permute-start.4 = (f32[64,128]{1,0:T(8,128)S(1)}, f32[64,128]{1,0:T(8,128)S(1)}, u32[]{:S(2)}, u32[]{:S(2)}) collective-permute-start(f32[64,128]{1,0:T(8,128)S(1)} %get-tuple-element.57), channel_id=1, source_target_pairs={{4,8},{12,16},{20,24},{8,4},{16,12},{24,20},{5,9},{13,17},{21,25},... | collective-permute-start | bytes 98312 | tf_op jit(solution)/shard_map/ppermute | solution.py:499
  28.7 8.2 %copy-start.5 = (s32[48]{0:T(128)}, s32[48]{0:T(128)S(1)}, u32[]{:S(2)}) copy-start(s32[48]{0:T(128)S(1)} %get-tuple-element.61.order_all.order) | copy-start | bytes 580
  36.9 7.8 %copy-start.1 = (f32[16,32,128]{2,1,0:T(8,128)S(1)}, f32[16,32,128]{2,1,0:T(8,128)}, u32[]{:S(2)}) copy-start(f32[16,32,128]{2,1,0:T(8,128)} %rest_1_.3) | copy-start | bytes 786436
  36.9 7.8 %copy-start.6 = (s32[48]{0:T(128)S(1)}, s32[48]{0:T(128)}, u32[]{:S(2)}) copy-start(s32[48]{0:T(128)} %copy-done.5) | copy-start | bytes 580
  39.0 1.5 %collective-permute-start.5 = (f32[16,24,128]{2,1,0:T(8,128)S(1)}, f32[16,24,128]{2,1,0:T(8,128)S(1)}, u32[]{:S(2)}, u32[]{:S(2)}) collective-permute-start(f32[16,24,128]{2,1,0:T(8,128)S(1)} %get-tuple-element.63), channel_id=1, source_target_pairs={{0,4},{4,0},{8,12},{12,8},{16,20},{20,16},{24,28},{28,24},{1,5},{5... | collective-permute-start | bytes 589832 | tf_op jit(solution)/shard_map/ppermute | solution.py:561
  41.2 11.3 %all-to-all-start.2 = ((f32[16,24,128]{2,1,0:T(8,128)}), f32[16,24,128]{2,1,0:T(8,128)S(1)}, u32[]{:S(2)}, u32[]{:S(2)}) async-start(f32[16,24,128]{2,1,0:T(8,128)} %add_cores.3), calls=%async_computation.2 | async-start | bytes 393216 | tf_op jit(solution)/shard_map/all_to_all | solution.py:593
  46.2 3.9 %collective-permute-start.7 = (f32[32,128]{1,0:T(8,128)S(1)}, f32[32,128]{1,0:T(8,128)S(1)}, u32[]{:S(2)}, u32[]{:S(2)}) collective-permute-start(f32[32,128]{1,0:T(8,128)S(1)} %get-tuple-element.69), channel_id=1, source_target_pairs={{1,2},{2,1},{5,6},{6,5},{9,10},{10,9},{13,14},{14,13},{17,18},{18,... | collective-permute-start | bytes 49160 | tf_op jit(solution)/shard_map/ppermute | solution.py:499
  46.9 5.0 %collective-permute-start.6 = (f32[32,128]{1,0:T(8,128)S(1)}, f32[32,128]{1,0:T(8,128)S(1)}, u32[]{:S(2)}, u32[]{:S(2)}) collective-permute-start(f32[32,128]{1,0:T(8,128)S(1)} %get-tuple-element.69), channel_id=1, source_target_pairs={{0,1},{2,3},{1,0},{3,2},{4,5},{6,7},{5,4},{7,6},{8,9},{10,11},{9,8... | collective-permute-start | bytes 49160 | tf_op jit(solution)/shard_map/ppermute | solution.py:499
  53.5 14.8 %all-to-all-start.3 = ((f32[32,16,128]{2,1,0:T(8,128)}), f32[32,16,128]{2,1,0:T(8,128)S(1)}, u32[]{:S(2)}, u32[]{:S(2)}) async-start(f32[32,16,128]{2,1,0:T(8,128)} %share_sum.3), calls=%async_computation.3 | async-start | bytes 524288 | tf_op jit(solution)/shard_map/all_to_all | solution.py:620
  57.1 1.3 %collective-permute-start.8 = (f32[64,128]{1,0:T(8,128)S(1)}, f32[64,128]{1,0:T(8,128)S(1)}, u32[]{:S(2)}, u32[]{:S(2)}) collective-permute-start(f32[64,128]{1,0:T(8,128)S(1)} %get-tuple-element.74), channel_id=1, source_target_pairs={{0,4},{8,12},{16,20},{24,28},{4,0},{12,8},{20,16},{28,24},{1,5},{9... | collective-permute-start | bytes 98312 | tf_op jit(solution)/shard_map/ppermute | solution.py:499
  57.4 1.0 %collective-permute-start.9 = (f32[64,128]{1,0:T(8,128)S(1)}, f32[64,128]{1,0:T(8,128)S(1)}, u32[]{:S(2)}, u32[]{:S(2)}) collective-permute-start(f32[64,128]{1,0:T(8,128)S(1)} %get-tuple-element.75), channel_id=1, source_target_pairs={{4,8},{12,16},{20,24},{8,4},{16,12},{24,20},{5,9},{13,17},{21,25},... | collective-permute-start | bytes 98312 | tf_op jit(solution)/shard_map/ppermute | solution.py:499

commit v23 on v21

--- a/solution.py
+++ b/solution.py
@@ -116,7 +116,7 @@
     return [places[d] for d in range(n_gx * n_gy)]
 
 
-def emit_modes(chosen, parent, is_owner, places, x_fwd, y_fwd, keep, send, turned, work):
+def emit_modes(chosen, parent, parent_copy, is_owner, places, x_fwd, y_fwd, keep, send, turned, work):
     devices, rows = len(places), keep.shape[1] // 2
     slabs = parent.shape[0]
     groups = slabs // GROUP
@@ -130,6 +130,8 @@
     if count < devices * rows:
         work[count:] = jnp.zeros((devices * rows - count, 2 * LANES), jnp.float32)
 
+    parent_copy.wait()
+
     @pl.when(is_owner)
     def _():
         for i in range(KX):
@@ -173,12 +175,12 @@
     copies = fetch_all(sems, [
         (levels_all, levels), (owners_all, owners), (fields_all, fields),
         (x_fwd_all.at[gx], x_fwd), (y_fwd_all.at[gy], y_fwd), (parent_all.at[0, 0], parent)])
-    for copy in copies:
+    for copy in copies[:-1]:
         copy.wait()
     level_count = parent.shape[0] // 3
     emit_modes(
         [fields[slab_of(levels, c, level_count, level_total)] for c in range(parent.shape[0])],
-        parent, owners[0] == gx * n_gy + gy, places, x_fwd[...], y_fwd[...], keep, send,
+        parent, copies[-1], owners[0] == gx * n_gy + gy, places, x_fwd[...], y_fwd[...], keep, send,
         turned, work,
     )
 
@@ -439,9 +441,9 @@
         for copy in sent:
             copy.wait()
         return
-    for copy in copies[1:]:
+    for copy in copies[1:-1]:
         copy.wait()
-    emit_modes(results, parent, owners[step + 1] == gx * n_gy + gy, places, x_fwd[...], y_fwd[...],
+    emit_modes(results, parent, copies[-1], owners[step + 1] == gx * n_gy + gy, places, x_fwd[...], y_fwd[...],
                keep, send, turned, work)
 
 
@@ -568,7 +570,6 @@
             name="add_cores",
         )(keep, received)
         if step == 0:
-            modes, flat = lax.optimization_barrier((modes, flat))
             *edges, weights = pl.pallas_call(
                 functools.partial(edge_kernel, n_gy, period),
                 out_shape=edge_shapes + [f32((2 * rows, LANES))],
@@ -578,7 +579,6 @@
                 name="edges",
             )(cuts, flat, plume)
         else:
-            modes, others = lax.optimization_barrier((modes, others))
             others, plume, *edges = pl.pallas_call(
                 functools.partial(others_kernel, 0, False, count),
                 out_shape=[f32((3 * kept, cells_x, cells_y)), f32(plume.shape)] + edge_shapes,

time: 71.5 us -> 71.2 us (level)
  no operation moved by 1% of the time
where the time goes in v23:
time: 71.2 us; the launch traced here: 70.6 us
  starting transfers between devices  29.5 us (41%)
  waiting for transfers between devices  23.8 us (33%)
  Pallas kernels  16.3 us (23%)
  between operations  0.84 us (1%)
    all_to_all x2, waiting for transfers between devices, local(): lax.all_to_all(share, AXES, 0, 0, axis_index_groups=[ranks], tiled=True)  16.1 us
    all_to_all x2, starting transfers between devices, local(): lax.all_to_all(modes, AXES, 0, 0, axis_index_groups=core_groups(n_gx, n_g...  12.1 us
    ppermute x8, starting transfers between devices, exchange(): lax.ppermute(data, axis, pairs + [(b, a) for a, b in pairs])  9.85 us
    all_to_all x2, starting transfers between devices, local(): lax.all_to_all(share, AXES, 0, 0, axis_index_groups=[ranks], tiled=True)  6.91 us
    ppermute x8, waiting for transfers between devices, exchange(): lax.ppermute(data, axis, pairs + [(b, a) for a, b in pairs])  3.74 us
    pallas_call x1, Pallas kernels, local(): pl.pallas_call(functools.partial(nudged_kernel, n_gy, step, True, count,...  2.5 us
    ppermute x2, waiting for transfers between devices, local(): received = lax.ppermute(send, 'gx', [(i, i ^ 1) for i in range(n_gx)])  2.5 us
    pallas_call x1, Pallas kernels, local(): pl.pallas_call(functools.partial(prepare_kernel, level_total), out_shape=...  2.05 us
  transfers between devices with their start and end apart: 14, of which 9 were waited for; matrix products, arithmetic and copies ran while one was open for 0% of the time, Pallas kernels for 9%

profile of v23, /device:TPU:0, one launch (start us, length us, event | category | flops | bytes accessed | tf_op | source)
XLA Modules:
  0.0 70.6 jit_solution(12922451768263640241)
XLA Ops:
  0.7 1.9 %first_modes.1 = (f32[16,24,128]{2,1,0:T(8,128)S(1)}, f32[16,24,128]{2,1,0:T(8,128)S(1)}) custom-call(s32[8]{0:T(128)} %levels, s32[2]{0:T(128)} %rest_0_.1, f32[48,32,128]{2,1,0:T(8,128)} %bitcast.2, f32[1,2,24,4096]{3,2,1,0:T(8,128)} %rest_1_.2, bf16[8,384,256]{2,1,0:T(8,128)(2,1)} %constant.10.clone.x_fwd_all.rest_2_, ...), custom_call_target="tpu_custom_call" | custom-call | tf_op jit(solution)/shard_map/first_modes/pallas_call | solution.py:551
  2.6 0.5 collective-permute-start
  3.1 1.1 %collective-permute-done.received = f32[16,24,128]{2,1,0:T(8,128)S(1)} collective-permute-done((f32[16,24,128]{2,1,0:T(8,128)S(1)}, f32[16,24,128]{2,1,0:T(8,128)S(1)}, u32[]{:S(2)}, u32[]{:S(2)}) %collective-permute-start) | collective-permute-done | bytes 196640 | tf_op jit(solution)/shard_map/ppermute | solution.py:563
  4.2 0.7 add_cores.2
  4.9 8.7 %all-to-all-start = ((f32[16,24,128]{2,1,0:T(8,128)}), f32[16,24,128]{2,1,0:T(8,128)S(1)}, u32[]{:S(2)}, u32[]{:S(2)}) async-start(f32[16,24,128]{2,1,0:T(8,128)} %add_cores.2), calls=%async_computation | async-start | bytes 393216 | tf_op jit(solution)/shard_map/all_to_all | solution.py:593
  13.7 0.9 %edges.1 = (f32[64,128]{1,0:T(8,128)S(1)}, f32[64,128]{1,0:T(8,128)S(1)}, f32[32,128]{1,0:T(8,128)S(1)}, f32[24,128]{1,0:T(8,128)S(1)}) custom-call(s32[24]{0:T(128)S(1)} %reshape.13.cuts, f32[48,32,128]{2,1,0:T(8,128)S(1)} %bitcast.3, f32[16,32,128]{2,1,0:T(8,128)S(1)} %copy-done.3), custom_call_target="tpu_custom_call" | custom-call | tf_op jit(solution)/shard_map/edges/pallas_call | solution.py:573
  14.6 0.7 collective-permute-start.2
  15.2 3.3 %collective-permute-start.1 = (f32[32,128]{1,0:T(8,128)S(1)}, f32[32,128]{1,0:T(8,128)S(1)}, u32[]{:S(2)}, u32[]{:S(2)}) collective-permute-start(f32[32,128]{1,0:T(8,128)S(1)} %get-tuple-element.42), channel_id=1, source_target_pairs={{0,1},{2,3},{1,0},{3,2},{4,5},{6,7},{5,4},{7,6},{8,9},{10,11},{9,8... | collective-permute-start | bytes 49160 | tf_op jit(solution)/shard_map/ppermute | solution.py:501
  18.6 1.7 %collective-permute-done.1.col_first = f32[32,128]{1,0:T(8,128)S(1)} collective-permute-done((f32[32,128]{1,0:T(8,128)S(1)}, f32[32,128]{1,0:T(8,128)S(1)}, u32[]{:S(2)}, u32[]{:S(2)}) %collective-permute-start.1) | collective-permute-done | bytes 16416 | tf_op jit(solution)/shard_map/ppermute | solution.py:501
  20.3 0.9 %all-to-all-done.parts = f32[16,24,128]{2,1,0:T(8,128)S(1)} async-done(((f32[16,24,128]{2,1,0:T(8,128)}), f32[16,24,128]{2,1,0:T(8,128)S(1)}, u32[]{:S(2)}, u32[]{:S(2)}) %all-to-all-start) | async-done | bytes 196640 | tf_op jit(solution)/shard_map/all_to_all | solution.py:593
  21.2 1.0 %share_sum.2 = f32[32,16,128]{2,1,0:T(8,128)} custom-call(f32[24,128]{1,0:T(8,128)S(1)} %get-tuple-element.39.weights, f32[16,24,128]{2,1,0:T(8,128)S(1)} %all-to-all-done.parts, bf16[512,256]{1,0:T(8,128)(2,1)S(1)} %copy-done.2, bf16[512,128]{1,0:T(8,128)(2,1)S(1)} %copy-done.4), custom_call_target="tpu_custom_call" | custom-call | tf_op jit(solution)/shard_map/share_sum/pallas_call | solution.py:596
  22.2 3.3 %all-to-all-start.1 = ((f32[32,16,128]{2,1,0:T(8,128)}), f32[32,16,128]{2,1,0:T(8,128)S(1)}, u32[]{:S(2)}, u32[]{:S(2)}) async-start(f32[32,16,128]{2,1,0:T(8,128)} %share_sum.2), calls=%async_computation.1 | async-start | bytes 524288 | tf_op jit(solution)/shard_map/all_to_all | solution.py:620
  25.5 0.3 collective-permute-start.3
  25.8 0.7 collective-permute-start.4
  26.5 2.0 %prepare.1 = (f32[24,32,128]{2,1,0:T(8,128)S(1)}, f32[24,32,128]{2,1,0:T(8,128)S(1)}, bf16[192,256]{1,0:T(8,128)(2,1)S(1)}, s32[48]{0:T(128)S(1)}) custom-call(s32[8]{0:T(128)S(1)} %copy-done.7, f32[48,32,128]{2,1,0:T(8,128)S(1)} %bitcast.4, bf16[4,192,256]{2,1,0:T(8,128)(2,1)} %constant.12.clone.y_back_all), custom_call_target="tpu_custom_call" | custom-call | tf_op jit(solution)/shard_map/prepare/pallas_call | solution.py:609
  28.6 8.1 %all-to-all-done.1.shares = f32[32,16,128]{2,1,0:T(8,128)S(1)} async-done(((f32[32,16,128]{2,1,0:T(8,128)}), f32[32,16,128]{2,1,0:T(8,128)S(1)}, u32[]{:S(2)}, u32[]{:S(2)}) %all-to-all-start.1) | async-done | bytes 262176 | tf_op jit(solution)/shard_map/all_to_all | solution.py:620
  36.7 2.0 %inner_nudged.1 = (f32[24,32,128]{2,1,0:T(8,128)S(1)}, f32[16,32,128]{2,1,0:T(8,128)S(1)}, f32[16,24,128]{2,1,0:T(8,128)S(1)}, f32[16,24,128]{2,1,0:T(8,128)S(1)}) custom-call(f32[32,16,128]{2,1,0:T(8,128)S(1)} %all-to-all-done.1.shares, f32[24,32,128]{2,1,0:T(8,128)S(1)} %get-tuple-element.49.fields, f32[64,128]{1,0:T(8,128)S(1)} %collective-permute-done.3.row_first, ...), custom_call_target="tpu_custom_call" | custom-call | tf_op jit(solution)/shard_map/inner_nudged/pallas_call | solution.py:642
  38.9 1.4 %collective-permute-done.5.received = f32[16,24,128]{2,1,0:T(8,128)S(1)} collective-permute-done((f32[16,24,128]{2,1,0:T(8,128)S(1)}, f32[16,24,128]{2,1,0:T(8,128)S(1)}, u32[]{:S(2)}, u32[]{:S(2)}) %collective-permute-start.5) | collective-permute-done | bytes 196640 | tf_op jit(solution)/shard_map/ppermute | solution.py:563
  40.3 0.7 add_cores.3
  41.0 3.4 %all-to-all-start.2 = ((f32[16,24,128]{2,1,0:T(8,128)}), f32[16,24,128]{2,1,0:T(8,128)S(1)}, u32[]{:S(2)}, u32[]{:S(2)}) async-start(f32[16,24,128]{2,1,0:T(8,128)} %add_cores.3), calls=%async_computation.2 | async-start | bytes 393216 | tf_op jit(solution)/shard_map/all_to_all | solution.py:593
  44.4 1.5 %inner_others.1 = (f32[24,32,128]{2,1,0:T(8,128)S(1)}, f32[16,32,128]{2,1,0:T(8,128)S(1)}, f32[64,128]{1,0:T(8,128)S(1)}, f32[64,128]{1,0:T(8,128)S(1)}, f32[32,128]{1,0:T(8,128)S(1)}) custom-call(f32[24,32,128]{2,1,0:T(8,128)S(1)} %get-tuple-element.58.fields, f32[16,32,128]{2,1,0:T(8,128)S(1)} %copy-done.3, f32[16,32,128]{2,1,0:T(8,128)S(1)} %copy-done.1, ...), custom_call_target="tpu_custom_call" | custom-call | tf_op jit(solution)/shard_map/inner_others/pallas_call | solution.py:582
  46.0 0.7 collective-permute-start.7
  46.7 3.3 %collective-permute-start.6 = (f32[32,128]{1,0:T(8,128)S(1)}, f32[32,128]{1,0:T(8,128)S(1)}, u32[]{:S(2)}, u32[]{:S(2)}) collective-permute-start(f32[32,128]{1,0:T(8,128)S(1)} %get-tuple-element.61), channel_id=1, source_target_pairs={{0,1},{2,3},{1,0},{3,2},{4,5},{6,7},{5,4},{7,6},{8,9},{10,11},{9,8... | collective-permute-start | bytes 49160 | tf_op jit(solution)/shard_map/ppermute | solution.py:501
  49.9 1.7 %collective-permute-done.6.col_first = f32[32,128]{1,0:T(8,128)S(1)} collective-permute-done((f32[32,128]{1,0:T(8,128)S(1)}, f32[32,128]{1,0:T(8,128)S(1)}, u32[]{:S(2)}, u32[]{:S(2)}) %collective-permute-start.6) | collective-permute-done | bytes 16416 | tf_op jit(solution)/shard_map/ppermute | solution.py:501
  51.6 0.6 all-to-all-done.2.parts
  52.3 1.0 %share_sum.3 = f32[32,16,128]{2,1,0:T(8,128)} custom-call(f32[24,128]{1,0:T(8,128)S(1)} %get-tuple-element.39.weights, f32[16,24,128]{2,1,0:T(8,128)S(1)} %all-to-all-done.2.parts, bf16[512,256]{1,0:T(8,128)(2,1)S(1)} %copy-done.2, bf16[512,128]{1,0:T(8,128)(2,1)S(1)} %copy-done.4), custom_call_target="tpu_custom_call" | custom-call | tf_op jit(solution)/shard_map/share_sum/pallas_call | solution.py:596
  53.3 3.6 %all-to-all-start.3 = ((f32[32,16,128]{2,1,0:T(8,128)}), f32[32,16,128]{2,1,0:T(8,128)S(1)}, u32[]{:S(2)}, u32[]{:S(2)}) async-start(f32[32,16,128]{2,1,0:T(8,128)} %share_sum.3), calls=%async_computation.3 | async-start | bytes 524288 | tf_op jit(solution)/shard_map/all_to_all | solution.py:620
  56.9 0.3 collective-permute-start.8
  57.2 0.7 collective-permute-start.9
  58.2 2.0 %last_others.1 = (f32[48,32,128]{2,1,0:T(8,128)}, f32[16,32,128]{2,1,0:T(8,128)}) custom-call(f32[24,32,128]{2,1,0:T(8,128)S(1)} %get-tuple-element.71.fields, f32[16,32,128]{2,1,0:T(8,128)S(1)} %get-tuple-element.70.plume.rest_0_, f32[16,32,128]{2,1,0:T(8,128)S(1)} %copy-done.1, f32[64,128]{1,0:T(8,128)S(1)} %collective-permute-done.8.row_first, ...), custom_call_target="tpu_custom_call" | custom-call | tf_op jit(solution)/shard_map/last_others/pallas_call | solution.py:622
  60.2 7.9 %all-to-all-done.3.shares = f32[32,16,128]{2,1,0:T(8,128)S(1)} async-done(((f32[32,16,128]{2,1,0:T(8,128)}), f32[32,16,128]{2,1,0:T(8,128)S(1)}, u32[]{:S(2)}, u32[]{:S(2)}) %all-to-all-start.3) | async-done | bytes 262176 | tf_op jit(solution)/shard_map/all_to_all | solution.py:620
  68.1 2.5 %last_nudged.1 = (f32[48,32,128]{2,1,0:T(8,128)}, f32[16,32,128]{2,1,0:T(8,128)}) custom-call(f32[32,16,128]{2,1,0:T(8,128)S(1)} %all-to-all-done.3.shares, f32[24,32,128]{2,1,0:T(8,128)S(1)} %get-tuple-element.59.rest_0_.fields, f32[64,128]{1,0:T(8,128)S(1)} %collective-permute-done.8.row_first, ...), custom_call_target="tpu_custom_call", output_to_operand_aliasing={{0}: (10, {}), {1}: (11, {})} | custom-call | tf_op jit(solution)/shard_map/last_nudged/pallas_call | solution.py:631
  (26 shorter events, 0.5 us)
Async XLA Ops:
  0.6 13.0 %copy-start.8 = (s32[3,8]{1,0:T(4,128)S(1)}, s32[3,8]{1,0:T(4,128)}, u32[]{:S(2)}) copy-start(s32[3,8]{1,0:T(4,128)} %param.14) | copy-start | bytes 292
  0.6 13.0 %copy-start = (f32[3,16,32,128]{3,2,1,0:T(8,128)S(1)}, f32[3,16,32,128]{3,2,1,0:T(8,128)}, u32[]{:S(2)}) copy-start(f32[3,16,32,128]{3,2,1,0:T(8,128)} %param.12) | copy-start | bytes 2359300
  0.7 13.0 %copy-start.3 = (f32[16,32,128]{2,1,0:T(8,128)S(1)}, f32[16,32,128]{2,1,0:T(8,128)}, u32[]{:S(2)}) copy-start(f32[16,32,128]{2,1,0:T(8,128)} %plume.3) | copy-start | bytes 786436
  2.6 18.6 %copy-start.2 = (bf16[512,256]{1,0:T(8,128)(2,1)S(1)}, bf16[512,256]{1,0:T(8,128)(2,1)}, u32[]{:S(2)}) copy-start(bf16[512,256]{1,0:T(8,128)(2,1)} %constant.13.clone.x_back) | copy-start | bytes 786436
  2.6 18.6 %copy-start.4 = (bf16[512,128]{1,0:T(8,128)(2,1)S(1)}, bf16[512,128]{1,0:T(8,128)(2,1)}, u32[]{:S(2)}) copy-start(bf16[512,128]{1,0:T(8,128)(2,1)} %constant.14.clone.x_beside) | copy-start | bytes 393220
  2.6 1.6 %collective-permute-start = (f32[16,24,128]{2,1,0:T(8,128)S(1)}, f32[16,24,128]{2,1,0:T(8,128)S(1)}, u32[]{:S(2)}, u32[]{:S(2)}) collective-permute-start(f32[16,24,128]{2,1,0:T(8,128)S(1)} %get-tuple-element.41), channel_id=1, source_target_pairs={{0,4},{4,0},{8,12},{12,8},{16,20},{20,16},{24,28},{28,24},{1,5},{5... | collective-permute-start | bytes 589832 | tf_op jit(solution)/shard_map/ppermute | solution.py:563
  4.2 22.3 %copy-start.7 = (s32[8]{0:T(128)S(1)}, s32[8]{0:T(128)}, u32[]{:S(2)}) copy-start(s32[8]{0:T(128)} %levels) | copy-start | bytes 100
  4.9 16.3 %all-to-all-start = ((f32[16,24,128]{2,1,0:T(8,128)}), f32[16,24,128]{2,1,0:T(8,128)S(1)}, u32[]{:S(2)}, u32[]{:S(2)}) async-start(f32[16,24,128]{2,1,0:T(8,128)} %add_cores.2), calls=%async_computation | async-start | bytes 393216 | tf_op jit(solution)/shard_map/all_to_all | solution.py:593
  14.6 4.0 %collective-permute-start.2 = (f32[32,128]{1,0:T(8,128)S(1)}, f32[32,128]{1,0:T(8,128)S(1)}, u32[]{:S(2)}, u32[]{:S(2)}) collective-permute-start(f32[32,128]{1,0:T(8,128)S(1)} %get-tuple-element.42), channel_id=1, source_target_pairs={{1,2},{2,1},{5,6},{6,5},{9,10},{10,9},{13,14},{14,13},{17,18},{18,... | collective-permute-start | bytes 49160 | tf_op jit(solution)/shard_map/ppermute | solution.py:501
  15.2 5.1 %collective-permute-start.1 = (f32[32,128]{1,0:T(8,128)S(1)}, f32[32,128]{1,0:T(8,128)S(1)}, u32[]{:S(2)}, u32[]{:S(2)}) collective-permute-start(f32[32,128]{1,0:T(8,128)S(1)} %get-tuple-element.42), channel_id=1, source_target_pairs={{0,1},{2,3},{1,0},{3,2},{4,5},{6,7},{5,4},{7,6},{8,9},{10,11},{9,8... | collective-permute-start | bytes 49160 | tf_op jit(solution)/shard_map/ppermute | solution.py:501
  22.2 14.5 %all-to-all-start.1 = ((f32[32,16,128]{2,1,0:T(8,128)}), f32[32,16,128]{2,1,0:T(8,128)S(1)}, u32[]{:S(2)}, u32[]{:S(2)}) async-start(f32[32,16,128]{2,1,0:T(8,128)} %share_sum.2), calls=%async_computation.1 | async-start | bytes 524288 | tf_op jit(solution)/shard_map/all_to_all | solution.py:620
  25.5 3.1 %collective-permute-start.3 = (f32[64,128]{1,0:T(8,128)S(1)}, f32[64,128]{1,0:T(8,128)S(1)}, u32[]{:S(2)}, u32[]{:S(2)}) collective-permute-start(f32[64,128]{1,0:T(8,128)S(1)} %get-tuple-element.50), channel_id=1, source_target_pairs={{0,4},{8,12},{16,20},{24,28},{4,0},{12,8},{20,16},{28,24},{1,5},{9... | collective-permute-start | bytes 98312 | tf_op jit(solution)/shard_map/ppermute | solution.py:501
  25.8 2.7 %collective-permute-start.4 = (f32[64,128]{1,0:T(8,128)S(1)}, f32[64,128]{1,0:T(8,128)S(1)}, u32[]{:S(2)}, u32[]{:S(2)}) collective-permute-start(f32[64,128]{1,0:T(8,128)S(1)} %get-tuple-element.51), channel_id=1, source_target_pairs={{4,8},{12,16},{20,24},{8,4},{16,12},{24,20},{5,9},{13,17},{21,25},... | collective-permute-start | bytes 98312 | tf_op jit(solution)/shard_map/ppermute | solution.py:501
  28.6 8.2 %copy-start.5 = (s32[48]{0:T(128)}, s32[48]{0:T(128)S(1)}, u32[]{:S(2)}) copy-start(s32[48]{0:T(128)S(1)} %get-tuple-element.55.order_all.order) | copy-start | bytes 580
  36.7 7.7 %copy-start.1 = (f32[16,32,128]{2,1,0:T(8,128)S(1)}, f32[16,32,128]{2,1,0:T(8,128)}, u32[]{:S(2)}) copy-start(f32[16,32,128]{2,1,0:T(8,128)} %rest_1_.3) | copy-start | bytes 786436
  36.7 7.7 %copy-start.6 = (s32[48]{0:T(128)S(1)}, s32[48]{0:T(128)}, u32[]{:S(2)}) copy-start(s32[48]{0:T(128)} %copy-done.5) | copy-start | bytes 580
  38.8 1.5 %collective-permute-start.5 = (f32[16,24,128]{2,1,0:T(8,128)S(1)}, f32[16,24,128]{2,1,0:T(8,128)S(1)}, u32[]{:S(2)}, u32[]{:S(2)}) collective-permute-start(f32[16,24,128]{2,1,0:T(8,128)S(1)} %get-tuple-element.57), channel_id=1, source_target_pairs={{0,4},{4,0},{8,12},{12,8},{16,20},{20,16},{24,28},{28,24},{1,5},{5... | collective-permute-start | bytes 589832 | tf_op jit(solution)/shard_map/ppermute | solution.py:563
  41.0 11.3 %all-to-all-start.2 = ((f32[16,24,128]{2,1,0:T(8,128)}), f32[16,24,128]{2,1,0:T(8,128)S(1)}, u32[]{:S(2)}, u32[]{:S(2)}) async-start(f32[16,24,128]{2,1,0:T(8,128)} %add_cores.3), calls=%async_computation.2 | async-start | bytes 393216 | tf_op jit(solution)/shard_map/all_to_all | solution.py:593
  46.0 3.9 %collective-permute-start.7 = (f32[32,128]{1,0:T(8,128)S(1)}, f32[32,128]{1,0:T(8,128)S(1)}, u32[]{:S(2)}, u32[]{:S(2)}) collective-permute-start(f32[32,128]{1,0:T(8,128)S(1)} %get-tuple-element.61), channel_id=1, source_target_pairs={{1,2},{2,1},{5,6},{6,5},{9,10},{10,9},{13,14},{14,13},{17,18},{18,... | collective-permute-start | bytes 49160 | tf_op jit(solution)/shard_map/ppermute | solution.py:501
  46.7 5.0 %collective-permute-start.6 = (f32[32,128]{1,0:T(8,128)S(1)}, f32[32,128]{1,0:T(8,128)S(1)}, u32[]{:S(2)}, u32[]{:S(2)}) collective-permute-start(f32[32,128]{1,0:T(8,128)S(1)} %get-tuple-element.61), channel_id=1, source_target_pairs={{0,1},{2,3},{1,0},{3,2},{4,5},{6,7},{5,4},{7,6},{8,9},{10,11},{9,8... | collective-permute-start | bytes 49160 | tf_op jit(solution)/shard_map/ppermute | solution.py:501
  53.3 14.8 %all-to-all-start.3 = ((f32[32,16,128]{2,1,0:T(8,128)}), f32[32,16,128]{2,1,0:T(8,128)S(1)}, u32[]{:S(2)}, u32[]{:S(2)}) async-start(f32[32,16,128]{2,1,0:T(8,128)} %share_sum.3), calls=%async_computation.3 | async-start | bytes 524288 | tf_op jit(solution)/shard_map/all_to_all | solution.py:620
  56.9 1.3 %collective-permute-start.8 = (f32[64,128]{1,0:T(8,128)S(1)}, f32[64,128]{1,0:T(8,128)S(1)}, u32[]{:S(2)}, u32[]{:S(2)}) collective-permute-start(f32[64,128]{1,0:T(8,128)S(1)} %get-tuple-element.66), channel_id=1, source_target_pairs={{0,4},{8,12},{16,20},{24,28},{4,0},{12,8},{20,16},{28,24},{1,5},{9... | collective-permute-start | bytes 98312 | tf_op jit(solution)/shard_map/ppermute | solution.py:501
  57.2 1.0 %collective-permute-start.9 = (f32[64,128]{1,0:T(8,128)S(1)}, f32[64,128]{1,0:T(8,128)S(1)}, u32[]{:S(2)}, u32[]{:S(2)}) collective-permute-start(f32[64,128]{1,0:T(8,128)S(1)} %get-tuple-element.67), channel_id=1, source_target_pairs={{4,8},{12,16},{20,24},{8,4},{16,12},{24,20},{5,9},{13,17},{21,25},... | collective-permute-start | bytes 98312 | tf_op jit(solution)/shard_map/ppermute | solution.py:501

commit v24 on v23

--- a/solution.py
+++ b/solution.py
@@ -561,14 +561,6 @@
     for step in range(STEPS):
         last = step == STEPS - 1
         received = lax.ppermute(send, "gx", [(i, i ^ 1) for i in range(n_gx)])
-        modes = pl.pallas_call(
-            add_kernel,
-            out_shape=half_shapes[0],
-            in_specs=[VMEM] * 2,
-            out_specs=VMEM,
-            compiler_params=limit(4),
-            name="add_cores",
-        )(keep, received)
         if step == 0:
             *edges, weights = pl.pallas_call(
                 functools.partial(edge_kernel, n_gy, period),
@@ -588,7 +580,16 @@
                 compiler_params=limit(8),
                 name="inner_others",
             )(others, plume, source, *halo, order, flat, winds)
+        received, *edges = lax.optimization_barrier((received, *edges))
         to_first, to_second, cols = edges
+        modes = pl.pallas_call(
+            add_kernel,
+            out_shape=half_shapes[0],
+            in_specs=[VMEM] * 2,
+            out_specs=VMEM,
+            compiler_params=limit(4),
+            name="add_cores",
+        )(keep, received)
         col_first, col_second = exchange("gy", cols, cols)
         parts = lax.all_to_all(modes, AXES, 0, 0, axis_index_groups=core_groups(n_gx, n_gy),
                                tiled=True)

time: 71.2 us -> 70.2 us (0.986)
  starting transfers between devices: 29.5 us -> 28.1 us
    ppermute x2, waiting for transfers between devices: 2.5 us -> 0.1 us  [local(): received = lax.ppermute(send, 'gx', [(i, i ^ 1) for i in range(n_gx)])]
    all_to_all x2, waiting for transfers between devices: 1.51 us -> 3.68 us  [local(): lax.all_to_all(modes, AXES, 0, 0, axis_index_groups=core_groups(n_gx, n_g...]
    all_to_all x2, starting transfers between devices: 6.91 us -> 5.17 us  [local(): lax.all_to_all(share, AXES, 0, 0, axis_index_groups=[ranks], tiled=True)]
    ppermute x8, waiting for transfers between devices: 3.74 us -> 4.48 us  [exchange(): lax.ppermute(data, axis, pairs + [(b, a) for a, b in pairs])]
  transfers between devices with their start and end apart: 14 -> 14, of which waited for: 9 -> 8; matrix products, arithmetic and copies ran while one was open for 0% -> 0% of each run, Pallas kernels for 9% -> 9%
where the time goes in v24:
time: 70.2 us; the launch traced here: 69.9 us
  starting transfers between devices  28.1 us (40%)
  waiting for transfers between devices  24 us (34%)
  Pallas kernels  16.3 us (23%)
  between operations  0.83 us (1%)
    all_to_all x2, waiting for transfers between devices, local(): lax.all_to_all(share, AXES, 0, 0, axis_index_groups=[ranks], tiled=True)  15.7 us
    all_to_all x2, starting transfers between devices, local(): lax.all_to_all(modes, AXES, 0, 0, axis_index_groups=core_groups(n_gx, n_g...  12.8 us
    ppermute x8, starting transfers between devices, exchange(): lax.ppermute(data, axis, pairs + [(b, a) for a, b in pairs])  9.58 us
    all_to_all x2, starting transfers between devices, local(): lax.all_to_all(share, AXES, 0, 0, axis_index_groups=[ranks], tiled=True)  5.17 us
    ppermute x8, waiting for transfers between devices, exchange(): lax.ppermute(data, axis, pairs + [(b, a) for a, b in pairs])  4.48 us
    all_to_all x2, waiting for transfers between devices, local(): lax.all_to_all(modes, AXES, 0, 0, axis_index_groups=core_groups(n_gx, n_g...  3.68 us
    pallas_call x1, Pallas kernels, local(): pl.pallas_call(functools.partial(nudged_kernel, n_gy, step, True, count,...  2.5 us
    pallas_call x1, Pallas kernels, local(): pl.pallas_call(functools.partial(prepare_kernel, level_total), out_shape=...  2.05 us
  transfers between devices with their start and end apart: 14, of which 8 were waited for; matrix products, arithmetic and copies ran while one was open for 0% of the time, Pallas kernels for 9%

profile of v24, /device:TPU:0, one launch (start us, length us, event | category | flops | bytes accessed | tf_op | source)
XLA Modules:
  0.0 69.9 jit_solution(2203136805432821883)
XLA Ops:
  0.7 1.9 %first_modes.1 = (f32[16,24,128]{2,1,0:T(8,128)S(1)}, f32[16,24,128]{2,1,0:T(8,128)S(1)}) custom-call(s32[8]{0:T(128)} %levels, s32[2]{0:T(128)} %rest_0_.1, f32[48,32,128]{2,1,0:T(8,128)} %bitcast.2, f32[1,2,24,4096]{3,2,1,0:T(8,128)} %rest_1_.2, bf16[8,384,256]{2,1,0:T(8,128)(2,1)} %constant.10.clone.x_fwd_all.rest_2_, ...), custom_call_target="tpu_custom_call" | custom-call | tf_op jit(solution)/shard_map/first_modes/pallas_call | solution.py:551
  2.6 0.5 collective-permute-start
  3.2 0.9 %edges.1 = (f32[64,128]{1,0:T(8,128)S(1)}, f32[64,128]{1,0:T(8,128)S(1)}, f32[32,128]{1,0:T(8,128)S(1)}, f32[24,128]{1,0:T(8,128)S(1)}) custom-call(s32[24]{0:T(128)S(1)} %reshape.13.cuts, f32[48,32,128]{2,1,0:T(8,128)S(1)} %bitcast.3, f32[16,32,128]{2,1,0:T(8,128)S(1)} %copy-done.3), custom_call_target="tpu_custom_call" | custom-call | tf_op jit(solution)/shard_map/edges/pallas_call | solution.py:565
  4.2 0.7 add_cores.2
  4.9 9.2 %all-to-all-start = ((f32[16,24,128]{2,1,0:T(8,128)}), f32[16,24,128]{2,1,0:T(8,128)S(1)}, u32[]{:S(2)}, u32[]{:S(2)}) async-start(f32[16,24,128]{2,1,0:T(8,128)} %add_cores.2), calls=%async_computation | async-start | bytes 393216 | tf_op jit(solution)/shard_map/all_to_all | solution.py:594
  14.0 0.7 collective-permute-start.2
  14.7 3.3 %collective-permute-start.1 = (f32[32,128]{1,0:T(8,128)S(1)}, f32[32,128]{1,0:T(8,128)S(1)}, u32[]{:S(2)}, u32[]{:S(2)}) collective-permute-start(f32[32,128]{1,0:T(8,128)S(1)} %get-tuple-element.54), channel_id=1, source_target_pairs={{0,1},{2,3},{1,0},{3,2},{4,5},{6,7},{5,4},{7,6},{8,9},{10,11},{9,8... | collective-permute-start | bytes 49160 | tf_op jit(solution)/shard_map/ppermute | solution.py:501
  18.0 1.9 %collective-permute-done.1.col_first = f32[32,128]{1,0:T(8,128)S(1)} collective-permute-done((f32[32,128]{1,0:T(8,128)S(1)}, f32[32,128]{1,0:T(8,128)S(1)}, u32[]{:S(2)}, u32[]{:S(2)}) %collective-permute-start.1) | collective-permute-done | bytes 16416 | tf_op jit(solution)/shard_map/ppermute | solution.py:501
  19.9 1.8 %all-to-all-done.parts = f32[16,24,128]{2,1,0:T(8,128)S(1)} async-done(((f32[16,24,128]{2,1,0:T(8,128)}), f32[16,24,128]{2,1,0:T(8,128)S(1)}, u32[]{:S(2)}, u32[]{:S(2)}) %all-to-all-start) | async-done | bytes 196640 | tf_op jit(solution)/shard_map/all_to_all | solution.py:594
  21.7 1.0 %share_sum.2 = f32[32,16,128]{2,1,0:T(8,128)} custom-call(f32[24,128]{1,0:T(8,128)S(1)} %get-tuple-element.47.weights, f32[16,24,128]{2,1,0:T(8,128)S(1)} %all-to-all-done.parts, bf16[512,256]{1,0:T(8,128)(2,1)S(1)} %copy-done.2, bf16[512,128]{1,0:T(8,128)(2,1)S(1)} %copy-done.4), custom_call_target="tpu_custom_call" | custom-call | tf_op jit(solution)/shard_map/share_sum/pallas_call | solution.py:597
  22.7 2.6 %all-to-all-start.1 = ((f32[32,16,128]{2,1,0:T(8,128)}), f32[32,16,128]{2,1,0:T(8,128)S(1)}, u32[]{:S(2)}, u32[]{:S(2)}) async-start(f32[32,16,128]{2,1,0:T(8,128)} %share_sum.2), calls=%async_computation.1 | async-start | bytes 524288 | tf_op jit(solution)/shard_map/all_to_all | solution.py:621
  25.3 0.2 collective-permute-start.3
  25.5 0.7 collective-permute-start.4
  26.2 2.0 %prepare.1 = (f32[24,32,128]{2,1,0:T(8,128)S(1)}, f32[24,32,128]{2,1,0:T(8,128)S(1)}, bf16[192,256]{1,0:T(8,128)(2,1)S(1)}, s32[48]{0:T(128)S(1)}) custom-call(s32[8]{0:T(128)S(1)} %copy-done.7, f32[48,32,128]{2,1,0:T(8,128)S(1)} %bitcast.4, bf16[4,192,256]{2,1,0:T(8,128)(2,1)} %constant.12.clone.y_back_all), custom_call_target="tpu_custom_call" | custom-call | tf_op jit(solution)/shard_map/prepare/pallas_call | solution.py:610
  28.2 0.5 copy-done.5
  28.8 7.8 %all-to-all-done.1.shares = f32[32,16,128]{2,1,0:T(8,128)S(1)} async-done(((f32[32,16,128]{2,1,0:T(8,128)}), f32[32,16,128]{2,1,0:T(8,128)S(1)}, u32[]{:S(2)}, u32[]{:S(2)}) %all-to-all-start.1) | async-done | bytes 262176 | tf_op jit(solution)/shard_map/all_to_all | solution.py:621
  36.5 2.0 %inner_nudged.1 = (f32[24,32,128]{2,1,0:T(8,128)S(1)}, f32[16,32,128]{2,1,0:T(8,128)S(1)}, f32[16,24,128]{2,1,0:T(8,128)S(1)}, f32[16,24,128]{2,1,0:T(8,128)S(1)}) custom-call(f32[32,16,128]{2,1,0:T(8,128)S(1)} %all-to-all-done.1.shares, f32[24,32,128]{2,1,0:T(8,128)S(1)} %get-tuple-element.61.fields, f32[64,128]{1,0:T(8,128)S(1)} %collective-permute-done.3.row_first, ...), custom_call_target="tpu_custom_call" | custom-call | tf_op jit(solution)/shard_map/inner_nudged/pallas_call | solution.py:643
  38.7 1.5 %inner_others.1 = (f32[24,32,128]{2,1,0:T(8,128)S(1)}, f32[16,32,128]{2,1,0:T(8,128)S(1)}, f32[64,128]{1,0:T(8,128)S(1)}, f32[64,128]{1,0:T(8,128)S(1)}, f32[32,128]{1,0:T(8,128)S(1)}) custom-call(f32[24,32,128]{2,1,0:T(8,128)S(1)} %get-tuple-element.70.fields, f32[16,32,128]{2,1,0:T(8,128)S(1)} %copy-done.3, f32[16,32,128]{2,1,0:T(8,128)S(1)} %copy-done.1, ...), custom_call_target="tpu_custom_call" | custom-call | tf_op jit(solution)/shard_map/inner_others/pallas_call | solution.py:574
  40.2 0.7 %add_cores.3 = f32[16,24,128]{2,1,0:T(8,128)} custom-call(f32[16,24,128]{2,1,0:T(8,128)S(1)} %get-tuple-element.68.kept, f32[16,24,128]{2,1,0:T(8,128)S(1)} %collective-permute-done.5.received), custom_call_target="tpu_custom_call" | custom-call | tf_op jit(solution)/shard_map/add_cores/pallas_call | solution.py:585
  40.9 3.6 %all-to-all-start.2 = ((f32[16,24,128]{2,1,0:T(8,128)}), f32[16,24,128]{2,1,0:T(8,128)S(1)}, u32[]{:S(2)}, u32[]{:S(2)}) async-start(f32[16,24,128]{2,1,0:T(8,128)} %add_cores.3), calls=%async_computation.2 | async-start | bytes 393216 | tf_op jit(solution)/shard_map/all_to_all | solution.py:594
  44.6 0.7 collective-permute-start.7
  45.2 3.3 %collective-permute-start.6 = (f32[32,128]{1,0:T(8,128)S(1)}, f32[32,128]{1,0:T(8,128)S(1)}, u32[]{:S(2)}, u32[]{:S(2)}) collective-permute-start(f32[32,128]{1,0:T(8,128)S(1)} %get-tuple-element.77), channel_id=1, source_target_pairs={{0,1},{2,3},{1,0},{3,2},{4,5},{6,7},{5,4},{7,6},{8,9},{10,11},{9,8... | collective-permute-start | bytes 49160 | tf_op jit(solution)/shard_map/ppermute | solution.py:501
  48.5 2.2 %collective-permute-done.6.col_first = f32[32,128]{1,0:T(8,128)S(1)} collective-permute-done((f32[32,128]{1,0:T(8,128)S(1)}, f32[32,128]{1,0:T(8,128)S(1)}, u32[]{:S(2)}, u32[]{:S(2)}) %collective-permute-start.6) | collective-permute-done | bytes 16416 | tf_op jit(solution)/shard_map/ppermute | solution.py:501
  50.7 1.9 %all-to-all-done.2.parts = f32[16,24,128]{2,1,0:T(8,128)S(1)} async-done(((f32[16,24,128]{2,1,0:T(8,128)}), f32[16,24,128]{2,1,0:T(8,128)S(1)}, u32[]{:S(2)}, u32[]{:S(2)}) %all-to-all-start.2) | async-done | bytes 196640 | tf_op jit(solution)/shard_map/all_to_all | solution.py:594
  52.6 1.0 %share_sum.3 = f32[32,16,128]{2,1,0:T(8,128)} custom-call(f32[24,128]{1,0:T(8,128)S(1)} %get-tuple-element.47.weights, f32[16,24,128]{2,1,0:T(8,128)S(1)} %all-to-all-done.2.parts, bf16[512,256]{1,0:T(8,128)(2,1)S(1)} %copy-done.2, bf16[512,128]{1,0:T(8,128)(2,1)S(1)} %copy-done.4), custom_call_target="tpu_custom_call" | custom-call | tf_op jit(solution)/shard_map/share_sum/pallas_call | solution.py:597
  53.6 2.6 %all-to-all-start.3 = ((f32[32,16,128]{2,1,0:T(8,128)}), f32[32,16,128]{2,1,0:T(8,128)S(1)}, u32[]{:S(2)}, u32[]{:S(2)}) async-start(f32[32,16,128]{2,1,0:T(8,128)} %share_sum.3), calls=%async_computation.3 | async-start | bytes 524288 | tf_op jit(solution)/shard_map/all_to_all | solution.py:621
  56.2 0.2 collective-permute-start.8
  56.3 0.7 collective-permute-start.9
  57.0 0.4 collective-permute-done.8.row_first
  57.4 2.0 %last_others.1 = (f32[48,32,128]{2,1,0:T(8,128)}, f32[16,32,128]{2,1,0:T(8,128)}) custom-call(f32[24,32,128]{2,1,0:T(8,128)S(1)} %get-tuple-element.87.fields, f32[16,32,128]{2,1,0:T(8,128)S(1)} %get-tuple-element.86.plume.rest_0_, f32[16,32,128]{2,1,0:T(8,128)S(1)} %copy-done.1, f32[64,128]{1,0:T(8,128)S(1)} %collective-permute-done.8.row_first, ...), custom_call_target="tpu_custom_call" | custom-call | tf_op jit(solution)/shard_map/last_others/pallas_call | solution.py:623
  59.4 7.9 %all-to-all-done.3.shares = f32[32,16,128]{2,1,0:T(8,128)S(1)} async-done(((f32[32,16,128]{2,1,0:T(8,128)}), f32[32,16,128]{2,1,0:T(8,128)S(1)}, u32[]{:S(2)}, u32[]{:S(2)}) %all-to-all-start.3) | async-done | bytes 262176 | tf_op jit(solution)/shard_map/all_to_all | solution.py:621
  67.4 2.5 %last_nudged.1 = (f32[48,32,128]{2,1,0:T(8,128)}, f32[16,32,128]{2,1,0:T(8,128)}) custom-call(f32[32,16,128]{2,1,0:T(8,128)S(1)} %all-to-all-done.3.shares, f32[24,32,128]{2,1,0:T(8,128)S(1)} %get-tuple-element.71.rest_0_.fields, f32[64,128]{1,0:T(8,128)S(1)} %collective-permute-done.8.row_first, ...), custom_call_target="tpu_custom_call", output_to_operand_aliasing={{0}: (10, {}), {1}: (11, {})} | custom-call | tf_op jit(solution)/shard_map/last_nudged/pallas_call | solution.py:632
  (26 shorter events, 0.3 us)
Async XLA Ops:
  0.6 2.5 %copy-start.8 = (s32[3,8]{1,0:T(4,128)S(1)}, s32[3,8]{1,0:T(4,128)}, u32[]{:S(2)}) copy-start(s32[3,8]{1,0:T(4,128)} %param.14) | copy-start | bytes 292
  0.6 2.6 %copy-start = (f32[3,16,32,128]{3,2,1,0:T(8,128)S(1)}, f32[3,16,32,128]{3,2,1,0:T(8,128)}, u32[]{:S(2)}) copy-start(f32[3,16,32,128]{3,2,1,0:T(8,128)} %param.12) | copy-start | bytes 2359300
  0.7 2.5 %copy-start.3 = (f32[16,32,128]{2,1,0:T(8,128)S(1)}, f32[16,32,128]{2,1,0:T(8,128)}, u32[]{:S(2)}) copy-start(f32[16,32,128]{2,1,0:T(8,128)} %plume.3) | copy-start | bytes 786436
  2.6 19.1 %copy-start.2 = (bf16[512,256]{1,0:T(8,128)(2,1)S(1)}, bf16[512,256]{1,0:T(8,128)(2,1)}, u32[]{:S(2)}) copy-start(bf16[512,256]{1,0:T(8,128)(2,1)} %constant.13.clone.x_back) | copy-start | bytes 786436
  2.6 19.1 %copy-start.4 = (bf16[512,128]{1,0:T(8,128)(2,1)S(1)}, bf16[512,128]{1,0:T(8,128)(2,1)}, u32[]{:S(2)}) copy-start(bf16[512,128]{1,0:T(8,128)(2,1)} %constant.14.clone.x_beside) | copy-start | bytes 393220
  2.6 1.6 %collective-permute-start = (f32[16,24,128]{2,1,0:T(8,128)S(1)}, f32[16,24,128]{2,1,0:T(8,128)S(1)}, u32[]{:S(2)}, u32[]{:S(2)}) collective-permute-start(f32[16,24,128]{2,1,0:T(8,128)S(1)} %get-tuple-element.49), channel_id=1, source_target_pairs={{0,4},{4,0},{8,12},{12,8},{16,20},{20,16},{24,28},{28,24},{1,5},{5... | collective-permute-start | bytes 589832 | tf_op jit(solution)/shard_map/ppermute | solution.py:563
  3.2 22.9 %copy-start.7 = (s32[8]{0:T(128)S(1)}, s32[8]{0:T(128)}, u32[]{:S(2)}) copy-start(s32[8]{0:T(128)} %levels) | copy-start | bytes 100
  4.9 16.8 %all-to-all-start = ((f32[16,24,128]{2,1,0:T(8,128)}), f32[16,24,128]{2,1,0:T(8,128)S(1)}, u32[]{:S(2)}, u32[]{:S(2)}) async-start(f32[16,24,128]{2,1,0:T(8,128)} %add_cores.2), calls=%async_computation | async-start | bytes 393216 | tf_op jit(solution)/shard_map/all_to_all | solution.py:594
  14.0 4.0 %collective-permute-start.2 = (f32[32,128]{1,0:T(8,128)S(1)}, f32[32,128]{1,0:T(8,128)S(1)}, u32[]{:S(2)}, u32[]{:S(2)}) collective-permute-start(f32[32,128]{1,0:T(8,128)S(1)} %get-tuple-element.54), channel_id=1, source_target_pairs={{1,2},{2,1},{5,6},{6,5},{9,10},{10,9},{13,14},{14,13},{17,18},{18,... | collective-permute-start | bytes 49160 | tf_op jit(solution)/shard_map/ppermute | solution.py:501
  14.7 5.2 %collective-permute-start.1 = (f32[32,128]{1,0:T(8,128)S(1)}, f32[32,128]{1,0:T(8,128)S(1)}, u32[]{:S(2)}, u32[]{:S(2)}) collective-permute-start(f32[32,128]{1,0:T(8,128)S(1)} %get-tuple-element.54), channel_id=1, source_target_pairs={{0,1},{2,3},{1,0},{3,2},{4,5},{6,7},{5,4},{7,6},{8,9},{10,11},{9,8... | collective-permute-start | bytes 49160 | tf_op jit(solution)/shard_map/ppermute | solution.py:501
  22.7 13.8 %all-to-all-start.1 = ((f32[32,16,128]{2,1,0:T(8,128)}), f32[32,16,128]{2,1,0:T(8,128)S(1)}, u32[]{:S(2)}, u32[]{:S(2)}) async-start(f32[32,16,128]{2,1,0:T(8,128)} %share_sum.2), calls=%async_computation.1 | async-start | bytes 524288 | tf_op jit(solution)/shard_map/all_to_all | solution.py:621
  25.3 3.4 %collective-permute-start.3 = (f32[64,128]{1,0:T(8,128)S(1)}, f32[64,128]{1,0:T(8,128)S(1)}, u32[]{:S(2)}, u32[]{:S(2)}) collective-permute-start(f32[64,128]{1,0:T(8,128)S(1)} %get-tuple-element.62), channel_id=1, source_target_pairs={{0,4},{8,12},{16,20},{24,28},{4,0},{12,8},{20,16},{28,24},{1,5},{9... | collective-permute-start | bytes 98312 | tf_op jit(solution)/shard_map/ppermute | solution.py:501
  25.5 3.3 %collective-permute-start.4 = (f32[64,128]{1,0:T(8,128)S(1)}, f32[64,128]{1,0:T(8,128)S(1)}, u32[]{:S(2)}, u32[]{:S(2)}) collective-permute-start(f32[64,128]{1,0:T(8,128)S(1)} %get-tuple-element.63), channel_id=1, source_target_pairs={{4,8},{12,16},{20,24},{8,4},{16,12},{24,20},{5,9},{13,17},{21,25},... | collective-permute-start | bytes 98312 | tf_op jit(solution)/shard_map/ppermute | solution.py:501
  28.2 0.5 copy-start.5
  36.5 2.1 %copy-start.1 = (f32[16,32,128]{2,1,0:T(8,128)S(1)}, f32[16,32,128]{2,1,0:T(8,128)}, u32[]{:S(2)}) copy-start(f32[16,32,128]{2,1,0:T(8,128)} %rest_1_.3) | copy-start | bytes 786436
  36.5 2.1 %copy-start.6 = (s32[48]{0:T(128)S(1)}, s32[48]{0:T(128)}, u32[]{:S(2)}) copy-start(s32[48]{0:T(128)} %copy-done.5) | copy-start | bytes 580
  38.6 1.7 %collective-permute-start.5 = (f32[16,24,128]{2,1,0:T(8,128)S(1)}, f32[16,24,128]{2,1,0:T(8,128)S(1)}, u32[]{:S(2)}, u32[]{:S(2)}) collective-permute-start(f32[16,24,128]{2,1,0:T(8,128)S(1)} %get-tuple-element.69), channel_id=1, source_target_pairs={{0,4},{4,0},{8,12},{12,8},{16,20},{20,16},{24,28},{28,24},{1,5},{5... | collective-permute-start | bytes 589832 | tf_op jit(solution)/shard_map/ppermute | solution.py:563
  40.9 11.6 %all-to-all-start.2 = ((f32[16,24,128]{2,1,0:T(8,128)}), f32[16,24,128]{2,1,0:T(8,128)S(1)}, u32[]{:S(2)}, u32[]{:S(2)}) async-start(f32[16,24,128]{2,1,0:T(8,128)} %add_cores.3), calls=%async_computation.2 | async-start | bytes 393216 | tf_op jit(solution)/shard_map/all_to_all | solution.py:594
  44.6 4.0 %collective-permute-start.7 = (f32[32,128]{1,0:T(8,128)S(1)}, f32[32,128]{1,0:T(8,128)S(1)}, u32[]{:S(2)}, u32[]{:S(2)}) collective-permute-start(f32[32,128]{1,0:T(8,128)S(1)} %get-tuple-element.77), channel_id=1, source_target_pairs={{1,2},{2,1},{5,6},{6,5},{9,10},{10,9},{13,14},{14,13},{17,18},{18,... | collective-permute-start | bytes 49160 | tf_op jit(solution)/shard_map/ppermute | solution.py:501
  45.2 5.5 %collective-permute-start.6 = (f32[32,128]{1,0:T(8,128)S(1)}, f32[32,128]{1,0:T(8,128)S(1)}, u32[]{:S(2)}, u32[]{:S(2)}) collective-permute-start(f32[32,128]{1,0:T(8,128)S(1)} %get-tuple-element.77), channel_id=1, source_target_pairs={{0,1},{2,3},{1,0},{3,2},{4,5},{6,7},{5,4},{7,6},{8,9},{10,11},{9,8... | collective-permute-start | bytes 49160 | tf_op jit(solution)/shard_map/ppermute | solution.py:501
  53.6 13.8 %all-to-all-start.3 = ((f32[32,16,128]{2,1,0:T(8,128)}), f32[32,16,128]{2,1,0:T(8,128)S(1)}, u32[]{:S(2)}, u32[]{:S(2)}) async-start(f32[32,16,128]{2,1,0:T(8,128)} %share_sum.3), calls=%async_computation.3 | async-start | bytes 524288 | tf_op jit(solution)/shard_map/all_to_all | solution.py:621
  56.2 1.3 %collective-permute-start.8 = (f32[64,128]{1,0:T(8,128)S(1)}, f32[64,128]{1,0:T(8,128)S(1)}, u32[]{:S(2)}, u32[]{:S(2)}) collective-permute-start(f32[64,128]{1,0:T(8,128)S(1)} %get-tuple-element.82), channel_id=1, source_target_pairs={{0,4},{8,12},{16,20},{24,28},{4,0},{12,8},{20,16},{28,24},{1,5},{9... | collective-permute-start | bytes 98312 | tf_op jit(solution)/shard_map/ppermute | solution.py:501
  56.3 1.1 %collective-permute-start.9 = (f32[64,128]{1,0:T(8,128)S(1)}, f32[64,128]{1,0:T(8,128)S(1)}, u32[]{:S(2)}, u32[]{:S(2)}) collective-permute-start(f32[64,128]{1,0:T(8,128)S(1)} %get-tuple-element.83), channel_id=1, source_target_pairs={{4,8},{12,16},{20,24},{8,4},{16,12},{24,20},{5,9},{13,17},{21,25},... | collective-permute-start | bytes 98312 | tf_op jit(solution)/shard_map/ppermute | solution.py:501

commit v25 on v24

--- a/solution.py
+++ b/solution.py
@@ -278,7 +278,6 @@
     cells_x = LANES // GROUP
     slot = lax.broadcasted_iota(jnp.int32, (height, LANES), 1) // cells_x
     spot = lax.broadcasted_iota(jnp.int32, (packed, LANES), 1) // width
-    spot_at = {d: i for i, d in enumerate(ranking(n_gx, n_gy))}
     for g in range(n_gx):
         first = g * cells_x // LANES * LANES
         tile = jnp.zeros((height, LANES), jnp.float32)
@@ -292,8 +291,8 @@
             beside = jnp.where(
                 spot == m, pltpu.roll(piece, (m - g) * width % LANES, 1), beside)
         for h in range(n_gy):
-            out[spot_at[g * n_gy + h], :rows, :] = tile[:rows]
-            out[spot_at[g * n_gy + h], rows:, :] = beside
+            out[g * n_gy + h, :rows, :] = tile[:rows]
+            out[g * n_gy + h, rows:, :] = beside
 
 
 class Halo:
@@ -355,14 +354,14 @@
     return jnp.where(l + 1 < level_total, 0.3, 0.0).astype(jnp.float32)
 
 
-def nudge_updates(ranks, shares, spread, spread_edges, y_table, nudged, cells_x):
+def nudge_updates(shares, spread, spread_edges, y_table, nudged, cells_x):
     devices = shares.shape[0]
     rows = spread.shape[0] // devices
     packed = beside_rows(rows)
     width = 2 * GROUP
-    for i, d in enumerate(ranks):
-        spread[d * rows : (d + 1) * rows] = shares[i, :rows, :]
-        edge = shares[i, rows:, :]
+    for d in range(devices):
+        spread[d * rows : (d + 1) * rows] = shares[d, :rows, :]
+        edge = shares[d, rows:, :]
         for m in range(3):
             count = min(packed, rows - m * packed)
             if count > 0:
@@ -383,7 +382,7 @@
     return updates, update_rows
 
 
-def nudged_kernel(n_gy, step, last, level_count, level_total, ranks, places, shares, fields, row_first, row_second,
+def nudged_kernel(n_gy, step, last, level_count, level_total, places, shares, fields, row_first, row_second,
                   col_first, col_second, y_back, order_all, *rest):
     gx, gy = lax.axis_index("gx"), lax.axis_index("gy")
     cells_x, cells_y = fields.shape[1:]
@@ -401,7 +400,7 @@
     copies = fetch_all(sems, [(order_all, order)] + extra)
     halo = Halo(row_first, row_second, col_first, col_second, west, east)
     updates, update_rows = nudge_updates(
-        ranks, shares, spread, spread_edges, y_back[...], nudged, cells_x)
+        shares, spread, spread_edges, y_back[...], nudged, cells_x)
     copies[0].wait()
     level_at = [order[n] for n in range(level_count)]
     halo_at = level_at if step == 0 else list(range(level_count))
@@ -529,7 +528,6 @@
     kept = level_total - count
     half_shapes = [f32((devices // 2, 2 * rows, LANES))] * 2
     places = share_places(n_gx, n_gy)
-    ranks = ranking(n_gx, n_gy)
     order_shape = (3 * level_total,)
     edge_shapes = [f32((total, cells_y)), f32((total, cells_y)), f32((cells_x, 2 * total))]
     levels_space = pltpu.SMEM(levels.shape, jnp.int32)
@@ -618,7 +616,7 @@
                 compiler_params=limit(8),
                 name="prepare",
             )(levels, flat, in_hbm(y_back))
-        shares = lax.all_to_all(share, AXES, 0, 0, axis_index_groups=[ranks], tiled=True)
+        shares = lax.all_to_all(share, AXES, 0, 0, tiled=True)
         if last:
             final = pl.pallas_call(
                 functools.partial(others_kernel, step, True, count),
@@ -630,7 +628,7 @@
                 name="last_others",
             )(others, plume, source, *halo, order)
             flat, plume = pl.pallas_call(
-                functools.partial(nudged_kernel, n_gy, step, True, count, level_total, ranks, None),
+                functools.partial(nudged_kernel, n_gy, step, True, count, level_total, None),
                 out_shape=[f32((field_rows, cells_x, cells_y)), f32(plume.shape)],
                 in_specs=[VMEM] * 7 + [HBM] + [VMEM] * 2 + [HBM] * 2,
                 out_specs=[HBM] * 2,
@@ -641,7 +639,7 @@
             )(shares, flat, *halo, y_back, in_hbm(order), plume, source, *final)
         else:
             flat, winds, keep, send = pl.pallas_call(
-                functools.partial(nudged_kernel, n_gy, step, False, count, level_total, ranks, places),
+                functools.partial(nudged_kernel, n_gy, step, False, count, level_total, places),
                 out_shape=[f32((nudged, cells_x, cells_y)), f32((2 * count, cells_x, cells_y))]
                 + half_shapes,
                 in_specs=[VMEM] * 7 + [HBM] * 5,

time: 70.2 us -> 68.8 us (0.980)
  waiting for transfers between devices: 24 us -> 21.8 us
    all_to_all x2, waiting for transfers between devices: 15.7 us -> 13.7 us  [local(): shares = lax.all_to_all(share, AXES, 0, 0, tiled=True)]
where the time goes in v25:
time: 68.8 us; the launch traced here: 68.2 us
  starting transfers between devices  28.6 us (42%)
  waiting for transfers between devices  21.8 us (32%)
  Pallas kernels  16.3 us (24%)
  between operations  0.8 us (1%)
    all_to_all x2, waiting for transfers between devices, local(): shares = lax.all_to_all(share, AXES, 0, 0, tiled=True)  13.7 us
    all_to_all x2, starting transfers between devices, local(): lax.all_to_all(modes, AXES, 0, 0, axis_index_groups=core_groups(n_gx, n_g...  12.8 us
    ppermute x8, starting transfers between devices, exchange(): lax.ppermute(data, axis, pairs + [(b, a) for a, b in pairs])  9.68 us
    all_to_all x2, starting transfers between devices, local(): shares = lax.all_to_all(share, AXES, 0, 0, tiled=True)  5.17 us
    ppermute x8, waiting for transfers between devices, exchange(): lax.ppermute(data, axis, pairs + [(b, a) for a, b in pairs])  4.09 us
    all_to_all x2, waiting for transfers between devices, local(): lax.all_to_all(modes, AXES, 0, 0, axis_index_groups=core_groups(n_gx, n_g...  3.94 us
    pallas_call x1, Pallas kernels, local(): pl.pallas_call(functools.partial(nudged_kernel, n_gy, step, True, count,...  2.5 us
    pallas_call x1, Pallas kernels, local(): pl.pallas_call(functools.partial(prepare_kernel, level_total), out_shape=...  2.05 us
  transfers between devices with their start and end apart: 14, of which 8 were waited for; matrix products, arithmetic and copies ran while one was open for 0% of the time, Pallas kernels for 9%

profile of v25, /device:TPU:0, one launch (start us, length us, event | category | flops | bytes accessed | tf_op | source)
XLA Modules:
  0.0 68.2 jit_solution(11995858973267897959)
XLA Ops:
  0.7 1.9 %first_modes.1 = (f32[16,24,128]{2,1,0:T(8,128)S(1)}, f32[16,24,128]{2,1,0:T(8,128)S(1)}) custom-call(s32[8]{0:T(128)} %levels, s32[2]{0:T(128)} %rest_0_.1, f32[48,32,128]{2,1,0:T(8,128)} %bitcast.2, f32[1,2,24,4096]{3,2,1,0:T(8,128)} %rest_1_.2, bf16[8,384,256]{2,1,0:T(8,128)(2,1)} %constant.10.clone.x_fwd_all.rest_2_, ...), custom_call_target="tpu_custom_call" | custom-call | tf_op jit(solution)/shard_map/first_modes/pallas_call | solution.py:549
  2.6 0.5 collective-permute-start
  3.2 0.9 %edges.1 = (f32[64,128]{1,0:T(8,128)S(1)}, f32[64,128]{1,0:T(8,128)S(1)}, f32[32,128]{1,0:T(8,128)S(1)}, f32[24,128]{1,0:T(8,128)S(1)}) custom-call(s32[24]{0:T(128)S(1)} %reshape.13.cuts, f32[48,32,128]{2,1,0:T(8,128)S(1)} %bitcast.3, f32[16,32,128]{2,1,0:T(8,128)S(1)} %copy-done.3), custom_call_target="tpu_custom_call" | custom-call | tf_op jit(solution)/shard_map/edges/pallas_call | solution.py:563
  4.2 0.7 %add_cores.2 = f32[16,24,128]{2,1,0:T(8,128)} custom-call(f32[16,24,128]{2,1,0:T(8,128)S(1)} %get-tuple-element.48.kept, f32[16,24,128]{2,1,0:T(8,128)S(1)} %collective-permute-done.received), custom_call_target="tpu_custom_call" | custom-call | tf_op jit(solution)/shard_map/add_cores/pallas_call | solution.py:583
  4.9 8.7 %all-to-all-start = ((f32[16,24,128]{2,1,0:T(8,128)}), f32[16,24,128]{2,1,0:T(8,128)S(1)}, u32[]{:S(2)}, u32[]{:S(2)}) async-start(f32[16,24,128]{2,1,0:T(8,128)} %add_cores.2), calls=%async_computation | async-start | bytes 393216 | tf_op jit(solution)/shard_map/all_to_all | solution.py:592
  13.6 0.7 collective-permute-start.2
  14.2 3.3 %collective-permute-start.1 = (f32[32,128]{1,0:T(8,128)S(1)}, f32[32,128]{1,0:T(8,128)S(1)}, u32[]{:S(2)}, u32[]{:S(2)}) collective-permute-start(f32[32,128]{1,0:T(8,128)S(1)} %get-tuple-element.54), channel_id=1, source_target_pairs={{0,1},{2,3},{1,0},{3,2},{4,5},{6,7},{5,4},{7,6},{8,9},{10,11},{9,8... | collective-permute-start | bytes 49160 | tf_op jit(solution)/shard_map/ppermute | solution.py:500
  17.6 1.9 %collective-permute-done.1.col_first = f32[32,128]{1,0:T(8,128)S(1)} collective-permute-done((f32[32,128]{1,0:T(8,128)S(1)}, f32[32,128]{1,0:T(8,128)S(1)}, u32[]{:S(2)}, u32[]{:S(2)}) %collective-permute-start.1) | collective-permute-done | bytes 16416 | tf_op jit(solution)/shard_map/ppermute | solution.py:500
  19.4 1.8 %all-to-all-done.parts = f32[16,24,128]{2,1,0:T(8,128)S(1)} async-done(((f32[16,24,128]{2,1,0:T(8,128)}), f32[16,24,128]{2,1,0:T(8,128)S(1)}, u32[]{:S(2)}, u32[]{:S(2)}) %all-to-all-start) | async-done | bytes 196640 | tf_op jit(solution)/shard_map/all_to_all | solution.py:592
  21.2 1.0 %share_sum.2 = f32[32,16,128]{2,1,0:T(8,128)} custom-call(f32[24,128]{1,0:T(8,128)S(1)} %get-tuple-element.47.weights, f32[16,24,128]{2,1,0:T(8,128)S(1)} %all-to-all-done.parts, bf16[512,256]{1,0:T(8,128)(2,1)S(1)} %copy-done.2, bf16[512,128]{1,0:T(8,128)(2,1)S(1)} %copy-done.4), custom_call_target="tpu_custom_call" | custom-call | tf_op jit(solution)/shard_map/share_sum/pallas_call | solution.py:595
  22.3 2.6 %all-to-all-start.1 = ((f32[32,16,128]{2,1,0:T(8,128)}), f32[32,16,128]{2,1,0:T(8,128)S(1)}, u32[]{:S(2)}, u32[]{:S(2)}) async-start(f32[32,16,128]{2,1,0:T(8,128)} %share_sum.2), calls=%async_computation.1 | async-start | bytes 524288 | tf_op jit(solution)/shard_map/all_to_all | solution.py:619
  25.0 0.7 collective-permute-start.4
  25.7 2.0 %prepare.1 = (f32[24,32,128]{2,1,0:T(8,128)S(1)}, f32[24,32,128]{2,1,0:T(8,128)S(1)}, bf16[192,256]{1,0:T(8,128)(2,1)S(1)}, s32[48]{0:T(128)S(1)}) custom-call(s32[8]{0:T(128)S(1)} %copy-done.7, f32[48,32,128]{2,1,0:T(8,128)S(1)} %bitcast.4, bf16[4,192,256]{2,1,0:T(8,128)(2,1)} %constant.12.clone.y_back_all), custom_call_target="tpu_custom_call" | custom-call | tf_op jit(solution)/shard_map/prepare/pallas_call | solution.py:608
  27.8 0.5 copy-done.5
  28.3 6.8 %all-to-all-done.1.shares = f32[32,16,128]{2,1,0:T(8,128)S(1)} async-done(((f32[32,16,128]{2,1,0:T(8,128)}), f32[32,16,128]{2,1,0:T(8,128)S(1)}, u32[]{:S(2)}, u32[]{:S(2)}) %all-to-all-start.1) | async-done | bytes 262176 | tf_op jit(solution)/shard_map/all_to_all | solution.py:619
  35.1 2.0 %inner_nudged.1 = (f32[24,32,128]{2,1,0:T(8,128)S(1)}, f32[16,32,128]{2,1,0:T(8,128)S(1)}, f32[16,24,128]{2,1,0:T(8,128)S(1)}, f32[16,24,128]{2,1,0:T(8,128)S(1)}) custom-call(f32[32,16,128]{2,1,0:T(8,128)S(1)} %all-to-all-done.1.shares, f32[24,32,128]{2,1,0:T(8,128)S(1)} %get-tuple-element.61.fields, f32[64,128]{1,0:T(8,128)S(1)} %collective-permute-done.3.row_first, ...), custom_call_target="tpu_custom_call" | custom-call | tf_op jit(solution)/shard_map/inner_nudged/pallas_call | solution.py:641
  37.1 0.5 collective-permute-start.5
  37.6 1.5 %inner_others.1 = (f32[24,32,128]{2,1,0:T(8,128)S(1)}, f32[16,32,128]{2,1,0:T(8,128)S(1)}, f32[64,128]{1,0:T(8,128)S(1)}, f32[64,128]{1,0:T(8,128)S(1)}, f32[32,128]{1,0:T(8,128)S(1)}) custom-call(f32[24,32,128]{2,1,0:T(8,128)S(1)} %get-tuple-element.70.fields, f32[16,32,128]{2,1,0:T(8,128)S(1)} %copy-done.3, f32[16,32,128]{2,1,0:T(8,128)S(1)} %copy-done.1, ...), custom_call_target="tpu_custom_call" | custom-call | tf_op jit(solution)/shard_map/inner_others/pallas_call | solution.py:572
  39.1 0.7 %add_cores.3 = f32[16,24,128]{2,1,0:T(8,128)} custom-call(f32[16,24,128]{2,1,0:T(8,128)S(1)} %get-tuple-element.68.kept, f32[16,24,128]{2,1,0:T(8,128)S(1)} %collective-permute-done.5.received), custom_call_target="tpu_custom_call" | custom-call | tf_op jit(solution)/shard_map/add_cores/pallas_call | solution.py:583
  39.8 4.1 %all-to-all-start.2 = ((f32[16,24,128]{2,1,0:T(8,128)}), f32[16,24,128]{2,1,0:T(8,128)S(1)}, u32[]{:S(2)}, u32[]{:S(2)}) async-start(f32[16,24,128]{2,1,0:T(8,128)} %add_cores.3), calls=%async_computation.2 | async-start | bytes 393216 | tf_op jit(solution)/shard_map/all_to_all | solution.py:592
  43.9 0.7 collective-permute-start.7
  44.6 3.3 %collective-permute-start.6 = (f32[32,128]{1,0:T(8,128)S(1)}, f32[32,128]{1,0:T(8,128)S(1)}, u32[]{:S(2)}, u32[]{:S(2)}) collective-permute-start(f32[32,128]{1,0:T(8,128)S(1)} %get-tuple-element.77), channel_id=1, source_target_pairs={{0,1},{2,3},{1,0},{3,2},{4,5},{6,7},{5,4},{7,6},{8,9},{10,11},{9,8... | collective-permute-start | bytes 49160 | tf_op jit(solution)/shard_map/ppermute | solution.py:500
  47.9 1.9 %collective-permute-done.6.col_first = f32[32,128]{1,0:T(8,128)S(1)} collective-permute-done((f32[32,128]{1,0:T(8,128)S(1)}, f32[32,128]{1,0:T(8,128)S(1)}, u32[]{:S(2)}, u32[]{:S(2)}) %collective-permute-start.6) | collective-permute-done | bytes 16416 | tf_op jit(solution)/shard_map/ppermute | solution.py:500
  49.8 2.1 %all-to-all-done.2.parts = f32[16,24,128]{2,1,0:T(8,128)S(1)} async-done(((f32[16,24,128]{2,1,0:T(8,128)}), f32[16,24,128]{2,1,0:T(8,128)S(1)}, u32[]{:S(2)}, u32[]{:S(2)}) %all-to-all-start.2) | async-done | bytes 196640 | tf_op jit(solution)/shard_map/all_to_all | solution.py:592
  51.9 1.0 %share_sum.3 = f32[32,16,128]{2,1,0:T(8,128)} custom-call(f32[24,128]{1,0:T(8,128)S(1)} %get-tuple-element.47.weights, f32[16,24,128]{2,1,0:T(8,128)S(1)} %all-to-all-done.2.parts, bf16[512,256]{1,0:T(8,128)(2,1)S(1)} %copy-done.2, bf16[512,128]{1,0:T(8,128)(2,1)S(1)} %copy-done.4), custom_call_target="tpu_custom_call" | custom-call | tf_op jit(solution)/shard_map/share_sum/pallas_call | solution.py:595
  52.9 2.6 %all-to-all-start.3 = ((f32[32,16,128]{2,1,0:T(8,128)}), f32[32,16,128]{2,1,0:T(8,128)S(1)}, u32[]{:S(2)}, u32[]{:S(2)}) async-start(f32[32,16,128]{2,1,0:T(8,128)} %share_sum.3), calls=%async_computation.3 | async-start | bytes 524288 | tf_op jit(solution)/shard_map/all_to_all | solution.py:619
  55.5 0.3 collective-permute-start.8
  55.8 0.7 collective-permute-start.9
  56.4 0.3 collective-permute-done.8.row_first
  56.8 2.0 %last_others.1 = (f32[48,32,128]{2,1,0:T(8,128)}, f32[16,32,128]{2,1,0:T(8,128)}) custom-call(f32[24,32,128]{2,1,0:T(8,128)S(1)} %get-tuple-element.87.fields, f32[16,32,128]{2,1,0:T(8,128)S(1)} %get-tuple-element.86.plume.rest_0_, f32[16,32,128]{2,1,0:T(8,128)S(1)} %copy-done.1, f32[64,128]{1,0:T(8,128)S(1)} %collective-permute-done.8.row_first, ...), custom_call_target="tpu_custom_call" | custom-call | tf_op jit(solution)/shard_map/last_others/pallas_call | solution.py:621
  58.8 6.9 %all-to-all-done.3.shares = f32[32,16,128]{2,1,0:T(8,128)S(1)} async-done(((f32[32,16,128]{2,1,0:T(8,128)}), f32[32,16,128]{2,1,0:T(8,128)S(1)}, u32[]{:S(2)}, u32[]{:S(2)}) %all-to-all-start.3) | async-done | bytes 262176 | tf_op jit(solution)/shard_map/all_to_all | solution.py:619
  65.7 2.5 %last_nudged.1 = (f32[48,32,128]{2,1,0:T(8,128)}, f32[16,32,128]{2,1,0:T(8,128)}) custom-call(f32[32,16,128]{2,1,0:T(8,128)S(1)} %all-to-all-done.3.shares, f32[24,32,128]{2,1,0:T(8,128)S(1)} %get-tuple-element.71.rest_0_.fields, f32[64,128]{1,0:T(8,128)S(1)} %collective-permute-done.8.row_first, ...), custom_call_target="tpu_custom_call", output_to_operand_aliasing={{0}: (10, {}), {1}: (11, {})} | custom-call | tf_op jit(solution)/shard_map/last_nudged/pallas_call | solution.py:630
  (26 shorter events, 0.4 us)
Async XLA Ops:
  0.6 2.5 %copy-start.8 = (s32[3,8]{1,0:T(4,128)S(1)}, s32[3,8]{1,0:T(4,128)}, u32[]{:S(2)}) copy-start(s32[3,8]{1,0:T(4,128)} %param.14) | copy-start | bytes 292
  0.6 2.6 %copy-start = (f32[3,16,32,128]{3,2,1,0:T(8,128)S(1)}, f32[3,16,32,128]{3,2,1,0:T(8,128)}, u32[]{:S(2)}) copy-start(f32[3,16,32,128]{3,2,1,0:T(8,128)} %param.12) | copy-start | bytes 2359300
  0.7 2.5 %copy-start.3 = (f32[16,32,128]{2,1,0:T(8,128)S(1)}, f32[16,32,128]{2,1,0:T(8,128)}, u32[]{:S(2)}) copy-start(f32[16,32,128]{2,1,0:T(8,128)} %plume.3) | copy-start | bytes 786436
  2.6 18.7 %copy-start.2 = (bf16[512,256]{1,0:T(8,128)(2,1)S(1)}, bf16[512,256]{1,0:T(8,128)(2,1)}, u32[]{:S(2)}) copy-start(bf16[512,256]{1,0:T(8,128)(2,1)} %constant.13.clone.x_back) | copy-start | bytes 786436
  2.6 18.7 %copy-start.4 = (bf16[512,128]{1,0:T(8,128)(2,1)S(1)}, bf16[512,128]{1,0:T(8,128)(2,1)}, u32[]{:S(2)}) copy-start(bf16[512,128]{1,0:T(8,128)(2,1)} %constant.14.clone.x_beside) | copy-start | bytes 393220
  2.6 1.6 %collective-permute-start = (f32[16,24,128]{2,1,0:T(8,128)S(1)}, f32[16,24,128]{2,1,0:T(8,128)S(1)}, u32[]{:S(2)}, u32[]{:S(2)}) collective-permute-start(f32[16,24,128]{2,1,0:T(8,128)S(1)} %get-tuple-element.49), channel_id=1, source_target_pairs={{0,4},{4,0},{8,12},{12,8},{16,20},{20,16},{24,28},{28,24},{1,5},{5... | collective-permute-start | bytes 589832 | tf_op jit(solution)/shard_map/ppermute | solution.py:561
  3.2 22.5 %copy-start.7 = (s32[8]{0:T(128)S(1)}, s32[8]{0:T(128)}, u32[]{:S(2)}) copy-start(s32[8]{0:T(128)} %levels) | copy-start | bytes 100
  4.9 16.4 %all-to-all-start = ((f32[16,24,128]{2,1,0:T(8,128)}), f32[16,24,128]{2,1,0:T(8,128)S(1)}, u32[]{:S(2)}, u32[]{:S(2)}) async-start(f32[16,24,128]{2,1,0:T(8,128)} %add_cores.2), calls=%async_computation | async-start | bytes 393216 | tf_op jit(solution)/shard_map/all_to_all | solution.py:592
  13.6 4.0 %collective-permute-start.2 = (f32[32,128]{1,0:T(8,128)S(1)}, f32[32,128]{1,0:T(8,128)S(1)}, u32[]{:S(2)}, u32[]{:S(2)}) collective-permute-start(f32[32,128]{1,0:T(8,128)S(1)} %get-tuple-element.54), channel_id=1, source_target_pairs={{1,2},{2,1},{5,6},{6,5},{9,10},{10,9},{13,14},{14,13},{17,18},{18,... | collective-permute-start | bytes 49160 | tf_op jit(solution)/shard_map/ppermute | solution.py:500
  14.2 5.2 %collective-permute-start.1 = (f32[32,128]{1,0:T(8,128)S(1)}, f32[32,128]{1,0:T(8,128)S(1)}, u32[]{:S(2)}, u32[]{:S(2)}) collective-permute-start(f32[32,128]{1,0:T(8,128)S(1)} %get-tuple-element.54), channel_id=1, source_target_pairs={{0,1},{2,3},{1,0},{3,2},{4,5},{6,7},{5,4},{7,6},{8,9},{10,11},{9,8... | collective-permute-start | bytes 49160 | tf_op jit(solution)/shard_map/ppermute | solution.py:500
  22.3 12.8 %all-to-all-start.1 = ((f32[32,16,128]{2,1,0:T(8,128)}), f32[32,16,128]{2,1,0:T(8,128)S(1)}, u32[]{:S(2)}, u32[]{:S(2)}) async-start(f32[32,16,128]{2,1,0:T(8,128)} %share_sum.2), calls=%async_computation.1 | async-start | bytes 524288 | tf_op jit(solution)/shard_map/all_to_all | solution.py:619
  24.9 3.4 %collective-permute-start.3 = (f32[64,128]{1,0:T(8,128)S(1)}, f32[64,128]{1,0:T(8,128)S(1)}, u32[]{:S(2)}, u32[]{:S(2)}) collective-permute-start(f32[64,128]{1,0:T(8,128)S(1)} %get-tuple-element.62), channel_id=1, source_target_pairs={{0,4},{8,12},{16,20},{24,28},{4,0},{12,8},{20,16},{28,24},{1,5},{9... | collective-permute-start | bytes 98312 | tf_op jit(solution)/shard_map/ppermute | solution.py:500
  25.0 3.3 %collective-permute-start.4 = (f32[64,128]{1,0:T(8,128)S(1)}, f32[64,128]{1,0:T(8,128)S(1)}, u32[]{:S(2)}, u32[]{:S(2)}) collective-permute-start(f32[64,128]{1,0:T(8,128)S(1)} %get-tuple-element.63), channel_id=1, source_target_pairs={{4,8},{12,16},{20,24},{8,4},{16,12},{24,20},{5,9},{13,17},{21,25},... | collective-permute-start | bytes 98312 | tf_op jit(solution)/shard_map/ppermute | solution.py:500
  27.8 0.5 copy-start.5
  35.0 2.5 %copy-start.1 = (f32[16,32,128]{2,1,0:T(8,128)S(1)}, f32[16,32,128]{2,1,0:T(8,128)}, u32[]{:S(2)}) copy-start(f32[16,32,128]{2,1,0:T(8,128)} %rest_1_.3) | copy-start | bytes 786436
  35.1 2.5 %copy-start.6 = (s32[48]{0:T(128)S(1)}, s32[48]{0:T(128)}, u32[]{:S(2)}) copy-start(s32[48]{0:T(128)} %copy-done.5) | copy-start | bytes 580
  37.1 2.0 %collective-permute-start.5 = (f32[16,24,128]{2,1,0:T(8,128)S(1)}, f32[16,24,128]{2,1,0:T(8,128)S(1)}, u32[]{:S(2)}, u32[]{:S(2)}) collective-permute-start(f32[16,24,128]{2,1,0:T(8,128)S(1)} %get-tuple-element.69), channel_id=1, source_target_pairs={{0,4},{4,0},{8,12},{12,8},{16,20},{20,16},{24,28},{28,24},{1,5},{5... | collective-permute-start | bytes 589832 | tf_op jit(solution)/shard_map/ppermute | solution.py:561
  39.8 12.1 %all-to-all-start.2 = ((f32[16,24,128]{2,1,0:T(8,128)}), f32[16,24,128]{2,1,0:T(8,128)S(1)}, u32[]{:S(2)}, u32[]{:S(2)}) async-start(f32[16,24,128]{2,1,0:T(8,128)} %add_cores.3), calls=%async_computation.2 | async-start | bytes 393216 | tf_op jit(solution)/shard_map/all_to_all | solution.py:592
  43.9 4.0 %collective-permute-start.7 = (f32[32,128]{1,0:T(8,128)S(1)}, f32[32,128]{1,0:T(8,128)S(1)}, u32[]{:S(2)}, u32[]{:S(2)}) collective-permute-start(f32[32,128]{1,0:T(8,128)S(1)} %get-tuple-element.77), channel_id=1, source_target_pairs={{1,2},{2,1},{5,6},{6,5},{9,10},{10,9},{13,14},{14,13},{17,18},{18,... | collective-permute-start | bytes 49160 | tf_op jit(solution)/shard_map/ppermute | solution.py:500
  44.6 5.2 %collective-permute-start.6 = (f32[32,128]{1,0:T(8,128)S(1)}, f32[32,128]{1,0:T(8,128)S(1)}, u32[]{:S(2)}, u32[]{:S(2)}) collective-permute-start(f32[32,128]{1,0:T(8,128)S(1)} %get-tuple-element.77), channel_id=1, source_target_pairs={{0,1},{2,3},{1,0},{3,2},{4,5},{6,7},{5,4},{7,6},{8,9},{10,11},{9,8... | collective-permute-start | bytes 49160 | tf_op jit(solution)/shard_map/ppermute | solution.py:500
  52.9 12.8 %all-to-all-start.3 = ((f32[32,16,128]{2,1,0:T(8,128)}), f32[32,16,128]{2,1,0:T(8,128)S(1)}, u32[]{:S(2)}, u32[]{:S(2)}) async-start(f32[32,16,128]{2,1,0:T(8,128)} %share_sum.3), calls=%async_computation.3 | async-start | bytes 524288 | tf_op jit(solution)/shard_map/all_to_all | solution.py:619
  55.5 1.3 %collective-permute-start.8 = (f32[64,128]{1,0:T(8,128)S(1)}, f32[64,128]{1,0:T(8,128)S(1)}, u32[]{:S(2)}, u32[]{:S(2)}) collective-permute-start(f32[64,128]{1,0:T(8,128)S(1)} %get-tuple-element.82), channel_id=1, source_target_pairs={{0,4},{8,12},{16,20},{24,28},{4,0},{12,8},{20,16},{28,24},{1,5},{9... | collective-permute-start | bytes 98312 | tf_op jit(solution)/shard_map/ppermute | solution.py:500
  55.8 1.0 %collective-permute-start.9 = (f32[64,128]{1,0:T(8,128)S(1)}, f32[64,128]{1,0:T(8,128)S(1)}, u32[]{:S(2)}, u32[]{:S(2)}) collective-permute-start(f32[64,128]{1,0:T(8,128)S(1)} %get-tuple-element.83), channel_id=1, source_target_pairs={{4,8},{12,16},{20,24},{8,4},{16,12},{24,20},{5,9},{13,17},{21,25},... | collective-permute-start | bytes 98312 | tf_op jit(solution)/shard_map/ppermute | solution.py:500

commit v26 on v25

--- a/solution.py
+++ b/solution.py
@@ -102,7 +102,7 @@
 
 
 def ranking(n_gx, n_gy):
-    return sorted(range(n_gx * n_gy), key=lambda d: (abs(2 * (d % n_gy) - (n_gy - 1)), d))
+    return sorted(range(n_gx * n_gy), key=lambda d: (-abs(2 * (d % n_gy) - (n_gy - 1)), d))
 
 
 def core_groups(n_gx, n_gy):

time: 68.8 us -> 70.3 us (1.022)
  starting transfers between devices: 28.6 us -> 30.3 us
    ppermute x8, starting transfers between devices: 9.68 us -> 12.4 us  [exchange(): lax.ppermute(data, axis, pairs + [(b, a) for a, b in pairs])]
    all_to_all x2, starting transfers between devices: 12.8 us -> 11.8 us  [local(): lax.all_to_all(modes, AXES, 0, 0, axis_index_groups=core_groups(n_gx, n_g...]
where the time goes in v26:
time: 70.3 us; the launch traced here: 69.7 us
  starting transfers between devices  30.3 us (43%)
  waiting for transfers between devices  21.6 us (31%)
  Pallas kernels  16.3 us (23%)
  between operations  0.82 us (1%)
    all_to_all x2, waiting for transfers between devices, local(): shares = lax.all_to_all(share, AXES, 0, 0, tiled=True)  13.7 us
    ppermute x8, starting transfers between devices, exchange(): lax.ppermute(data, axis, pairs + [(b, a) for a, b in pairs])  12.4 us
    all_to_all x2, starting transfers between devices, local(): lax.all_to_all(modes, AXES, 0, 0, axis_index_groups=core_groups(n_gx, n_g...  11.8 us
    all_to_all x2, starting transfers between devices, local(): shares = lax.all_to_all(share, AXES, 0, 0, tiled=True)  5.17 us
    ppermute x8, waiting for transfers between devices, exchange(): lax.ppermute(data, axis, pairs + [(b, a) for a, b in pairs])  4.28 us
    all_to_all x2, waiting for transfers between devices, local(): lax.all_to_all(modes, AXES, 0, 0, axis_index_groups=core_groups(n_gx, n_g...  3.58 us
    pallas_call x1, Pallas kernels, local(): pl.pallas_call(functools.partial(nudged_kernel, n_gy, step, True, count,...  2.5 us
    pallas_call x1, Pallas kernels, local(): pl.pallas_call(functools.partial(prepare_kernel, level_total), out_shape=...  2.05 us
  transfers between devices with their start and end apart: 14, of which 8 were waited for; matrix products, arithmetic and copies ran while one was open for 0% of the time, Pallas kernels for 9%

profile of v26, /device:TPU:0, one launch (start us, length us, event | category | flops | bytes accessed | tf_op | source)
XLA Modules:
  0.0 69.7 jit_solution(8702649206080676059)
XLA Ops:
  0.7 1.9 %first_modes.1 = (f32[16,24,128]{2,1,0:T(8,128)S(1)}, f32[16,24,128]{2,1,0:T(8,128)S(1)}) custom-call(s32[8]{0:T(128)} %levels, s32[2]{0:T(128)} %rest_0_.1, f32[48,32,128]{2,1,0:T(8,128)} %bitcast.2, f32[1,2,24,4096]{3,2,1,0:T(8,128)} %rest_1_.2, bf16[8,384,256]{2,1,0:T(8,128)(2,1)} %constant.10.clone.x_fwd_all.rest_2_, ...), custom_call_target="tpu_custom_call" | custom-call | tf_op jit(solution)/shard_map/first_modes/pallas_call | solution.py:549
  2.6 0.5 collective-permute-start
  3.2 0.9 %edges.1 = (f32[64,128]{1,0:T(8,128)S(1)}, f32[64,128]{1,0:T(8,128)S(1)}, f32[32,128]{1,0:T(8,128)S(1)}, f32[24,128]{1,0:T(8,128)S(1)}) custom-call(s32[24]{0:T(128)S(1)} %reshape.13.cuts, f32[48,32,128]{2,1,0:T(8,128)S(1)} %bitcast.3, f32[16,32,128]{2,1,0:T(8,128)S(1)} %copy-done.3), custom_call_target="tpu_custom_call" | custom-call | tf_op jit(solution)/shard_map/edges/pallas_call | solution.py:563
  4.2 0.7 add_cores.2
  4.9 8.2 %all-to-all-start = ((f32[16,24,128]{2,1,0:T(8,128)}), f32[16,24,128]{2,1,0:T(8,128)S(1)}, u32[]{:S(2)}, u32[]{:S(2)}) async-start(f32[16,24,128]{2,1,0:T(8,128)} %add_cores.2), calls=%async_computation | async-start | bytes 393216 | tf_op jit(solution)/shard_map/all_to_all | solution.py:592
  13.1 0.7 collective-permute-start.2
  13.8 4.7 %collective-permute-start.1 = (f32[32,128]{1,0:T(8,128)S(1)}, f32[32,128]{1,0:T(8,128)S(1)}, u32[]{:S(2)}, u32[]{:S(2)}) collective-permute-start(f32[32,128]{1,0:T(8,128)S(1)} %get-tuple-element.54), channel_id=1, source_target_pairs={{0,1},{2,3},{1,0},{3,2},{4,5},{6,7},{5,4},{7,6},{8,9},{10,11},{9,8... | collective-permute-start | bytes 49160 | tf_op jit(solution)/shard_map/ppermute | solution.py:500
  18.5 1.8 %collective-permute-done.1.col_first = f32[32,128]{1,0:T(8,128)S(1)} collective-permute-done((f32[32,128]{1,0:T(8,128)S(1)}, f32[32,128]{1,0:T(8,128)S(1)}, u32[]{:S(2)}, u32[]{:S(2)}) %collective-permute-start.1) | collective-permute-done | bytes 16416 | tf_op jit(solution)/shard_map/ppermute | solution.py:500
  20.3 1.8 %all-to-all-done.parts = f32[16,24,128]{2,1,0:T(8,128)S(1)} async-done(((f32[16,24,128]{2,1,0:T(8,128)}), f32[16,24,128]{2,1,0:T(8,128)S(1)}, u32[]{:S(2)}, u32[]{:S(2)}) %all-to-all-start) | async-done | bytes 196640 | tf_op jit(solution)/shard_map/all_to_all | solution.py:592
  22.1 1.0 %share_sum.2 = f32[32,16,128]{2,1,0:T(8,128)} custom-call(f32[24,128]{1,0:T(8,128)S(1)} %get-tuple-element.47.weights, f32[16,24,128]{2,1,0:T(8,128)S(1)} %all-to-all-done.parts, bf16[512,256]{1,0:T(8,128)(2,1)S(1)} %copy-done.2, bf16[512,128]{1,0:T(8,128)(2,1)S(1)} %copy-done.4), custom_call_target="tpu_custom_call" | custom-call | tf_op jit(solution)/shard_map/share_sum/pallas_call | solution.py:595
  23.2 2.6 %all-to-all-start.1 = ((f32[32,16,128]{2,1,0:T(8,128)}), f32[32,16,128]{2,1,0:T(8,128)S(1)}, u32[]{:S(2)}, u32[]{:S(2)}) async-start(f32[32,16,128]{2,1,0:T(8,128)} %share_sum.2), calls=%async_computation.1 | async-start | bytes 524288 | tf_op jit(solution)/shard_map/all_to_all | solution.py:619
  25.9 0.7 collective-permute-start.4
  26.6 2.0 %prepare.1 = (f32[24,32,128]{2,1,0:T(8,128)S(1)}, f32[24,32,128]{2,1,0:T(8,128)S(1)}, bf16[192,256]{1,0:T(8,128)(2,1)S(1)}, s32[48]{0:T(128)S(1)}) custom-call(s32[8]{0:T(128)S(1)} %copy-done.7, f32[48,32,128]{2,1,0:T(8,128)S(1)} %bitcast.4, bf16[4,192,256]{2,1,0:T(8,128)(2,1)} %constant.12.clone.y_back_all), custom_call_target="tpu_custom_call" | custom-call | tf_op jit(solution)/shard_map/prepare/pallas_call | solution.py:608
  28.7 0.5 copy-done.5
  29.2 6.7 %all-to-all-done.1.shares = f32[32,16,128]{2,1,0:T(8,128)S(1)} async-done(((f32[32,16,128]{2,1,0:T(8,128)}), f32[32,16,128]{2,1,0:T(8,128)S(1)}, u32[]{:S(2)}, u32[]{:S(2)}) %all-to-all-start.1) | async-done | bytes 262176 | tf_op jit(solution)/shard_map/all_to_all | solution.py:619
  36.0 2.0 %inner_nudged.1 = (f32[24,32,128]{2,1,0:T(8,128)S(1)}, f32[16,32,128]{2,1,0:T(8,128)S(1)}, f32[16,24,128]{2,1,0:T(8,128)S(1)}, f32[16,24,128]{2,1,0:T(8,128)S(1)}) custom-call(f32[32,16,128]{2,1,0:T(8,128)S(1)} %all-to-all-done.1.shares, f32[24,32,128]{2,1,0:T(8,128)S(1)} %get-tuple-element.61.fields, f32[64,128]{1,0:T(8,128)S(1)} %collective-permute-done.3.row_first, ...), custom_call_target="tpu_custom_call" | custom-call | tf_op jit(solution)/shard_map/inner_nudged/pallas_call | solution.py:641
  38.0 0.5 collective-permute-start.5
  38.5 1.5 %inner_others.1 = (f32[24,32,128]{2,1,0:T(8,128)S(1)}, f32[16,32,128]{2,1,0:T(8,128)S(1)}, f32[64,128]{1,0:T(8,128)S(1)}, f32[64,128]{1,0:T(8,128)S(1)}, f32[32,128]{1,0:T(8,128)S(1)}) custom-call(f32[24,32,128]{2,1,0:T(8,128)S(1)} %get-tuple-element.70.fields, f32[16,32,128]{2,1,0:T(8,128)S(1)} %copy-done.3, f32[16,32,128]{2,1,0:T(8,128)S(1)} %copy-done.1, ...), custom_call_target="tpu_custom_call" | custom-call | tf_op jit(solution)/shard_map/inner_others/pallas_call | solution.py:572
  40.0 0.7 %add_cores.3 = f32[16,24,128]{2,1,0:T(8,128)} custom-call(f32[16,24,128]{2,1,0:T(8,128)S(1)} %get-tuple-element.68.kept, f32[16,24,128]{2,1,0:T(8,128)S(1)} %collective-permute-done.5.received), custom_call_target="tpu_custom_call" | custom-call | tf_op jit(solution)/shard_map/add_cores/pallas_call | solution.py:583
  40.7 3.5 %all-to-all-start.2 = ((f32[16,24,128]{2,1,0:T(8,128)}), f32[16,24,128]{2,1,0:T(8,128)S(1)}, u32[]{:S(2)}, u32[]{:S(2)}) async-start(f32[16,24,128]{2,1,0:T(8,128)} %add_cores.3), calls=%async_computation.2 | async-start | bytes 393216 | tf_op jit(solution)/shard_map/all_to_all | solution.py:592
  44.3 0.7 collective-permute-start.7
  44.9 4.6 %collective-permute-start.6 = (f32[32,128]{1,0:T(8,128)S(1)}, f32[32,128]{1,0:T(8,128)S(1)}, u32[]{:S(2)}, u32[]{:S(2)}) collective-permute-start(f32[32,128]{1,0:T(8,128)S(1)} %get-tuple-element.77), channel_id=1, source_target_pairs={{0,1},{2,3},{1,0},{3,2},{4,5},{6,7},{5,4},{7,6},{8,9},{10,11},{9,8... | collective-permute-start | bytes 49160 | tf_op jit(solution)/shard_map/ppermute | solution.py:500
  49.6 2.1 %collective-permute-done.6.col_first = f32[32,128]{1,0:T(8,128)S(1)} collective-permute-done((f32[32,128]{1,0:T(8,128)S(1)}, f32[32,128]{1,0:T(8,128)S(1)}, u32[]{:S(2)}, u32[]{:S(2)}) %collective-permute-start.6) | collective-permute-done | bytes 16416 | tf_op jit(solution)/shard_map/ppermute | solution.py:500
  51.6 1.8 %all-to-all-done.2.parts = f32[16,24,128]{2,1,0:T(8,128)S(1)} async-done(((f32[16,24,128]{2,1,0:T(8,128)}), f32[16,24,128]{2,1,0:T(8,128)S(1)}, u32[]{:S(2)}, u32[]{:S(2)}) %all-to-all-start.2) | async-done | bytes 196640 | tf_op jit(solution)/shard_map/all_to_all | solution.py:592
  53.4 1.0 %share_sum.3 = f32[32,16,128]{2,1,0:T(8,128)} custom-call(f32[24,128]{1,0:T(8,128)S(1)} %get-tuple-element.47.weights, f32[16,24,128]{2,1,0:T(8,128)S(1)} %all-to-all-done.2.parts, bf16[512,256]{1,0:T(8,128)(2,1)S(1)} %copy-done.2, bf16[512,128]{1,0:T(8,128)(2,1)S(1)} %copy-done.4), custom_call_target="tpu_custom_call" | custom-call | tf_op jit(solution)/shard_map/share_sum/pallas_call | solution.py:595
  54.4 2.6 %all-to-all-start.3 = ((f32[32,16,128]{2,1,0:T(8,128)}), f32[32,16,128]{2,1,0:T(8,128)S(1)}, u32[]{:S(2)}, u32[]{:S(2)}) async-start(f32[32,16,128]{2,1,0:T(8,128)} %share_sum.3), calls=%async_computation.3 | async-start | bytes 524288 | tf_op jit(solution)/shard_map/all_to_all | solution.py:619
  57.0 0.3 collective-permute-start.8
  57.3 0.7 collective-permute-start.9
  57.9 0.4 collective-permute-done.8.row_first
  58.3 2.0 %last_others.1 = (f32[48,32,128]{2,1,0:T(8,128)}, f32[16,32,128]{2,1,0:T(8,128)}) custom-call(f32[24,32,128]{2,1,0:T(8,128)S(1)} %get-tuple-element.87.fields, f32[16,32,128]{2,1,0:T(8,128)S(1)} %get-tuple-element.86.plume.rest_0_, f32[16,32,128]{2,1,0:T(8,128)S(1)} %copy-done.1, f32[64,128]{1,0:T(8,128)S(1)} %collective-permute-done.8.row_first, ...), custom_call_target="tpu_custom_call" | custom-call | tf_op jit(solution)/shard_map/last_others/pallas_call | solution.py:621
  60.3 6.9 %all-to-all-done.3.shares = f32[32,16,128]{2,1,0:T(8,128)S(1)} async-done(((f32[32,16,128]{2,1,0:T(8,128)}), f32[32,16,128]{2,1,0:T(8,128)S(1)}, u32[]{:S(2)}, u32[]{:S(2)}) %all-to-all-start.3) | async-done | bytes 262176 | tf_op jit(solution)/shard_map/all_to_all | solution.py:619
  67.2 2.5 %last_nudged.1 = (f32[48,32,128]{2,1,0:T(8,128)}, f32[16,32,128]{2,1,0:T(8,128)}) custom-call(f32[32,16,128]{2,1,0:T(8,128)S(1)} %all-to-all-done.3.shares, f32[24,32,128]{2,1,0:T(8,128)S(1)} %get-tuple-element.71.rest_0_.fields, f32[64,128]{1,0:T(8,128)S(1)} %collective-permute-done.8.row_first, ...), custom_call_target="tpu_custom_call", output_to_operand_aliasing={{0}: (10, {}), {1}: (11, {})} | custom-call | tf_op jit(solution)/shard_map/last_nudged/pallas_call | solution.py:630
  (26 shorter events, 0.4 us)
Async XLA Ops:
  0.6 2.5 %copy-start.8 = (s32[3,8]{1,0:T(4,128)S(1)}, s32[3,8]{1,0:T(4,128)}, u32[]{:S(2)}) copy-start(s32[3,8]{1,0:T(4,128)} %param.14) | copy-start | bytes 292
  0.6 2.6 %copy-start = (f32[3,16,32,128]{3,2,1,0:T(8,128)S(1)}, f32[3,16,32,128]{3,2,1,0:T(8,128)}, u32[]{:S(2)}) copy-start(f32[3,16,32,128]{3,2,1,0:T(8,128)} %param.12) | copy-start | bytes 2359300
  0.7 2.5 %copy-start.3 = (f32[16,32,128]{2,1,0:T(8,128)S(1)}, f32[16,32,128]{2,1,0:T(8,128)}, u32[]{:S(2)}) copy-start(f32[16,32,128]{2,1,0:T(8,128)} %plume.3) | copy-start | bytes 786436
  2.6 19.6 %copy-start.2 = (bf16[512,256]{1,0:T(8,128)(2,1)S(1)}, bf16[512,256]{1,0:T(8,128)(2,1)}, u32[]{:S(2)}) copy-start(bf16[512,256]{1,0:T(8,128)(2,1)} %constant.13.clone.x_back) | copy-start | bytes 786436
  2.6 19.6 %copy-start.4 = (bf16[512,128]{1,0:T(8,128)(2,1)S(1)}, bf16[512,128]{1,0:T(8,128)(2,1)}, u32[]{:S(2)}) copy-start(bf16[512,128]{1,0:T(8,128)(2,1)} %constant.14.clone.x_beside) | copy-start | bytes 393220
  2.6 1.6 %collective-permute-start = (f32[16,24,128]{2,1,0:T(8,128)S(1)}, f32[16,24,128]{2,1,0:T(8,128)S(1)}, u32[]{:S(2)}, u32[]{:S(2)}) collective-permute-start(f32[16,24,128]{2,1,0:T(8,128)S(1)} %get-tuple-element.49), channel_id=1, source_target_pairs={{0,4},{4,0},{8,12},{12,8},{16,20},{20,16},{24,28},{28,24},{1,5},{5... | collective-permute-start | bytes 589832 | tf_op jit(solution)/shard_map/ppermute | solution.py:561
  3.2 23.4 %copy-start.7 = (s32[8]{0:T(128)S(1)}, s32[8]{0:T(128)}, u32[]{:S(2)}) copy-start(s32[8]{0:T(128)} %levels) | copy-start | bytes 100
  4.9 17.3 %all-to-all-start = ((f32[16,24,128]{2,1,0:T(8,128)}), f32[16,24,128]{2,1,0:T(8,128)S(1)}, u32[]{:S(2)}, u32[]{:S(2)}) async-start(f32[16,24,128]{2,1,0:T(8,128)} %add_cores.2), calls=%async_computation | async-start | bytes 393216 | tf_op jit(solution)/shard_map/all_to_all | solution.py:592
  13.1 5.4 %collective-permute-start.2 = (f32[32,128]{1,0:T(8,128)S(1)}, f32[32,128]{1,0:T(8,128)S(1)}, u32[]{:S(2)}, u32[]{:S(2)}) collective-permute-start(f32[32,128]{1,0:T(8,128)S(1)} %get-tuple-element.54), channel_id=1, source_target_pairs={{1,2},{2,1},{5,6},{6,5},{9,10},{10,9},{13,14},{14,13},{17,18},{18,... | collective-permute-start | bytes 49160 | tf_op jit(solution)/shard_map/ppermute | solution.py:500
  13.8 6.5 %collective-permute-start.1 = (f32[32,128]{1,0:T(8,128)S(1)}, f32[32,128]{1,0:T(8,128)S(1)}, u32[]{:S(2)}, u32[]{:S(2)}) collective-permute-start(f32[32,128]{1,0:T(8,128)S(1)} %get-tuple-element.54), channel_id=1, source_target_pairs={{0,1},{2,3},{1,0},{3,2},{4,5},{6,7},{5,4},{7,6},{8,9},{10,11},{9,8... | collective-permute-start | bytes 49160 | tf_op jit(solution)/shard_map/ppermute | solution.py:500
  23.2 12.8 %all-to-all-start.1 = ((f32[32,16,128]{2,1,0:T(8,128)}), f32[32,16,128]{2,1,0:T(8,128)S(1)}, u32[]{:S(2)}, u32[]{:S(2)}) async-start(f32[32,16,128]{2,1,0:T(8,128)} %share_sum.2), calls=%async_computation.1 | async-start | bytes 524288 | tf_op jit(solution)/shard_map/all_to_all | solution.py:619
  25.8 3.5 %collective-permute-start.3 = (f32[64,128]{1,0:T(8,128)S(1)}, f32[64,128]{1,0:T(8,128)S(1)}, u32[]{:S(2)}, u32[]{:S(2)}) collective-permute-start(f32[64,128]{1,0:T(8,128)S(1)} %get-tuple-element.62), channel_id=1, source_target_pairs={{0,4},{8,12},{16,20},{24,28},{4,0},{12,8},{20,16},{28,24},{1,5},{9... | collective-permute-start | bytes 98312 | tf_op jit(solution)/shard_map/ppermute | solution.py:500
  25.9 3.3 %collective-permute-start.4 = (f32[64,128]{1,0:T(8,128)S(1)}, f32[64,128]{1,0:T(8,128)S(1)}, u32[]{:S(2)}, u32[]{:S(2)}) collective-permute-start(f32[64,128]{1,0:T(8,128)S(1)} %get-tuple-element.63), channel_id=1, source_target_pairs={{4,8},{12,16},{20,24},{8,4},{16,12},{24,20},{5,9},{13,17},{21,25},... | collective-permute-start | bytes 98312 | tf_op jit(solution)/shard_map/ppermute | solution.py:500
  28.7 0.5 copy-start.5
  36.0 2.5 %copy-start.1 = (f32[16,32,128]{2,1,0:T(8,128)S(1)}, f32[16,32,128]{2,1,0:T(8,128)}, u32[]{:S(2)}) copy-start(f32[16,32,128]{2,1,0:T(8,128)} %rest_1_.3) | copy-start | bytes 786436
  36.0 2.5 %copy-start.6 = (s32[48]{0:T(128)S(1)}, s32[48]{0:T(128)}, u32[]{:S(2)}) copy-start(s32[48]{0:T(128)} %copy-done.5) | copy-start | bytes 580
  38.0 2.0 %collective-permute-start.5 = (f32[16,24,128]{2,1,0:T(8,128)S(1)}, f32[16,24,128]{2,1,0:T(8,128)S(1)}, u32[]{:S(2)}, u32[]{:S(2)}) collective-permute-start(f32[16,24,128]{2,1,0:T(8,128)S(1)} %get-tuple-element.69), channel_id=1, source_target_pairs={{0,4},{4,0},{8,12},{12,8},{16,20},{20,16},{24,28},{28,24},{1,5},{5... | collective-permute-start | bytes 589832 | tf_op jit(solution)/shard_map/ppermute | solution.py:561
  40.7 12.7 %all-to-all-start.2 = ((f32[16,24,128]{2,1,0:T(8,128)}), f32[16,24,128]{2,1,0:T(8,128)S(1)}, u32[]{:S(2)}, u32[]{:S(2)}) async-start(f32[16,24,128]{2,1,0:T(8,128)} %add_cores.3), calls=%async_computation.2 | async-start | bytes 393216 | tf_op jit(solution)/shard_map/all_to_all | solution.py:592
  44.3 5.3 %collective-permute-start.7 = (f32[32,128]{1,0:T(8,128)S(1)}, f32[32,128]{1,0:T(8,128)S(1)}, u32[]{:S(2)}, u32[]{:S(2)}) collective-permute-start(f32[32,128]{1,0:T(8,128)S(1)} %get-tuple-element.77), channel_id=1, source_target_pairs={{1,2},{2,1},{5,6},{6,5},{9,10},{10,9},{13,14},{14,13},{17,18},{18,... | collective-permute-start | bytes 49160 | tf_op jit(solution)/shard_map/ppermute | solution.py:500
  44.9 6.7 %collective-permute-start.6 = (f32[32,128]{1,0:T(8,128)S(1)}, f32[32,128]{1,0:T(8,128)S(1)}, u32[]{:S(2)}, u32[]{:S(2)}) collective-permute-start(f32[32,128]{1,0:T(8,128)S(1)} %get-tuple-element.77), channel_id=1, source_target_pairs={{0,1},{2,3},{1,0},{3,2},{4,5},{6,7},{5,4},{7,6},{8,9},{10,11},{9,8... | collective-permute-start | bytes 49160 | tf_op jit(solution)/shard_map/ppermute | solution.py:500
  54.4 12.8 %all-to-all-start.3 = ((f32[32,16,128]{2,1,0:T(8,128)}), f32[32,16,128]{2,1,0:T(8,128)S(1)}, u32[]{:S(2)}, u32[]{:S(2)}) async-start(f32[32,16,128]{2,1,0:T(8,128)} %share_sum.3), calls=%async_computation.3 | async-start | bytes 524288 | tf_op jit(solution)/shard_map/all_to_all | solution.py:619
  57.0 1.3 %collective-permute-start.8 = (f32[64,128]{1,0:T(8,128)S(1)}, f32[64,128]{1,0:T(8,128)S(1)}, u32[]{:S(2)}, u32[]{:S(2)}) collective-permute-start(f32[64,128]{1,0:T(8,128)S(1)} %get-tuple-element.82), channel_id=1, source_target_pairs={{0,4},{8,12},{16,20},{24,28},{4,0},{12,8},{20,16},{28,24},{1,5},{9... | collective-permute-start | bytes 98312 | tf_op jit(solution)/shard_map/ppermute | solution.py:500
  57.3 1.0 %collective-permute-start.9 = (f32[64,128]{1,0:T(8,128)S(1)}, f32[64,128]{1,0:T(8,128)S(1)}, u32[]{:S(2)}, u32[]{:S(2)}) collective-permute-start(f32[64,128]{1,0:T(8,128)S(1)} %get-tuple-element.83), channel_id=1, source_target_pairs={{4,8},{12,16},{20,24},{8,4},{16,12},{24,20},{5,9},{13,17},{21,25},... | collective-permute-start | bytes 98312 | tf_op jit(solution)/shard_map/ppermute | solution.py:500
